TPU v7x, 32 devices: a whole 2x2x4 slice. The times are simulated.
32 devices in a mesh: groups: 2 (over y), expert: 4 (over z), dp: 4 (over x, core).
Axes of the slice: x: 2, y: 2, z: 4, core: 2. Of those that a mesh axis runs over, the one named last changes fastest.
Arguments:
- tokens: bfloat16 [4096, 4096], P(('groups', 'expert'), 'dp'), parts along dimension 0, may hold values from -6 to 6
- router_weight: bfloat16 [4096, 4], P('dp'), may hold values from -0.09375 to 0.09375
- gate_weight: bfloat16 [4, 4096, 1024], P('expert', None, 'dp'), may hold values from -0.09375 to 0.09375
- up_weight: bfloat16 [4, 4096, 1024], P('expert', None, 'dp'), may hold values from -0.09375 to 0.09375
- down_weight: bfloat16 [4, 1024, 4096], P('expert', None, 'dp'), may hold values from -0.1875 to 0.1875
- picks: int32 [8, 512], P('groups'), parts along dimension 0, may hold values from 0 to 2047, as said below
Outputs:
- combined: bfloat16 [4096, 4096], P(('groups', 'expert'), 'dp'), parts along dimension 0
There are 2 independent parts, one for each index of `groups`. A program takes and returns all parts, laid end to end along the dimension named above; an argument that names none is the same for every part. Nothing has to cross between parts.
Inputs may be any that keep to these rules, and one draw needn't show every extreme that they name: Each row of picks holds 512 distinct token indices; at most 256 of a row lie among one index of expert's 512 consecutive tokens, and exactly 256 do in one such block for every row.
All inputs are finite; a program needn't handle non-finite values.
Results may differ from a plain program's by a relative error of at most 0.0059.
Values may be sent and summed in bfloat16 or wider, within the bound.
No kernel may reach another device: no remote copies, remote signals or barrier semaphores. Data moves between devices by JAX's collectives and lax.ppermute only.
A program may use at most 64 MiB of HBM per device.

v0:
```python
import jax
import jax.numpy as jnp
from jax import lax
from jax.sharding import PartitionSpec as P


def scaled_scores(kernel, column_total):
    row_scale = jnp.ones((kernel.shape[0],), jnp.float32)
    column_scale = jnp.ones((kernel.shape[1],), jnp.float32)
    for sweep_index in range(3):
        column_scale = 1.0 / column_total(jnp.sum(kernel * row_scale[:, None], axis=0))
        row_scale = 1.0 / jnp.sum(kernel * column_scale[None, :], axis=1)
    return row_scale[:, None] * kernel * column_scale[None, :]


def run_expert(row_block, gate_weight, up_weight, down_weight):
    piece = lax.all_gather(row_block, "dp", axis=1, tiled=True)
    gate_piece = gate_weight[0]
    up_piece = up_weight[0]
    gate = jnp.dot(piece, gate_piece, preferred_element_type=jnp.float32)
    upward = jnp.dot(piece, up_piece, preferred_element_type=jnp.float32)
    hidden = (jax.nn.silu(gate) * upward).astype(jnp.bfloat16)
    down_piece = down_weight[0]
    result = jnp.dot(
        lax.all_gather(hidden, "dp", axis=1, tiled=True),
        down_piece,
        preferred_element_type=jnp.float32,
    )
    return result.astype(jnp.bfloat16)


def shards(tokens, router_weight, gate_weight, up_weight, down_weight, picks):
    expert_count = lax.axis_size("expert")
    own_expert = lax.axis_index("expert")
    tok_rows, feat_width = tokens.shape
    num_experts, capacity = picks.shape
    slot_depth = 2 * capacity // expert_count
    partial_value = jnp.dot(tokens, router_weight, preferred_element_type=jnp.float32)
    logits = lax.psum(partial_value, "dp")
    scores = scaled_scores(jnp.exp(logits), lambda column: lax.psum(column, "expert"))
    owners = picks // tok_rows
    local_pick = owners == own_expert
    slot_rank = jnp.cumsum(local_pick.astype(jnp.int32), axis=1) - 1
    depth_ids = jnp.arange(slot_depth, dtype=jnp.int32)
    landing = local_pick[:, :, None] & (slot_rank[:, :, None] == depth_ids[None, None, :])
    filled = jnp.any(landing, axis=1).reshape(-1)
    slot_row = jnp.sum(jnp.where(landing, (picks % tok_rows)[:, :, None], 0), axis=1).reshape(-1)
    row_ids = jnp.arange(tok_rows, dtype=jnp.int32)
    selector = (slot_row[:, None] == row_ids[None, :]) & filled[:, None]
    outbound = jnp.dot(selector.astype(jnp.bfloat16), tokens, preferred_element_type=jnp.float32)
    outbound = outbound.astype(jnp.bfloat16).reshape(num_experts, slot_depth, feat_width)
    expert_ids = jnp.repeat(jnp.arange(num_experts, dtype=jnp.int32), slot_depth)
    slot_score = jnp.where(filled, scores[slot_row, expert_ids], 0.0)
    token_total = jnp.sum(jnp.where(selector, slot_score[:, None], 0.0), axis=0)
    slot_weight = jnp.where(
        filled, slot_score / jnp.maximum(token_total[slot_row], 1.0 / num_experts), 0.0
    )
    combine = jnp.where(selector, slot_weight[:, None], 0.0).astype(jnp.bfloat16)
    arrived = lax.all_to_all(outbound, "expert", split_axis=0, concat_axis=0, tiled=True)
    source_count, depth_count, row_width = arrived.shape
    results = run_expert(
        arrived.reshape(source_count * depth_count, row_width), gate_weight, up_weight, down_weight
    )
    results = results.reshape(source_count, depth_count, row_width)
    returned = lax.all_to_all(results, "expert", split_axis=0, concat_axis=0, tiled=True)
    combined = lax.dot_general(
        combine,
        returned.reshape(-1, feat_width),
        (((0,), (0,)), ((), ())),
        preferred_element_type=jnp.float32,
    )
    return combined.astype(jnp.bfloat16)


def solution(mesh):
    return jax.shard_map(
        shards,
        mesh=mesh,
        in_specs=(
            P(("groups", "expert"), "dp"),
            P("dp", None),
            P("expert", None, "dp"),
            P("expert", None, "dp"),
            P("expert", None, "dp"),
            P("groups", None),
        ),
        out_specs=P(("groups", "expert"), "dp"),
        check_vma=False,
    )
```

profile of v0, /device:TPU:0, one launch (start us, length us, event | category | flops | bytes accessed | tf_op | source)
XLA Modules:
  0.0 258.9 jit_solution(9553869404324567037)
XLA Ops:
  6.5 0.9 add_select_fusion
  7.4 0.7 fusion.35
  8.1 1.2 reduce-window.6
  9.4 0.2 slice_reduce_fusion
  9.6 0.2 reduce-window.9
  9.8 0.1 add_bitcast_fusion
  9.8 0.7 fusion.7
  10.6 1.1 select_reduce_fusion.1
  11.7 3.0 %fusion.11 = bf16[1024,1024]{1,0:T(8,128)(2,1)S(1)} fusion(bf16[512,1024]{1,0:T(8,128)(2,1)} %param.6, s32[1024]{0:T(1024)S(1)} %bitcast.53, pred[1024]{0:T(1024)(128)(4,1)S(1)} %and.33), kind=kOutput, calls=%fused_computation.17 | convolution fusion | flops 1075838976 | bytes 3150848 | tf_op jit(solution)/shard_map/dot_general | solution.py:50
  14.8 54.4 %all_to_all.10 = bf16[4,256,1024]{2,1,0:T(8,128)(2,1)} all-to-all(bf16[4,256,1024]{2,1,0:T(8,128)(2,1)S(1)} %bitcast.48), channel_id=1, replica_groups=mesh['groups'=2,'expert'=4,'dp'=4] {'expert'}, dimensions={0} | all-to-all | bytes 4194304 | tf_op jit(solution)/shard_map/all_to_all | solution.py:59
  69.3 57.6 %all-gather.3.cloned.1.call-done = bf16[1024,4096]{1,0:T(8,128)(2,1)} async-done(((bf16[1024,1024]{1,0:T(8,128)(2,1)}), bf16[1024,4096]{1,0:T(8,128)(2,1)}) %all-gather.3.cloned.1.call-update) | async-done | bytes 8388624 | tf_op jit(solution)/shard_map/all_gather | solution.py:17
  126.9 6.5 %fusion.4 = f32[1024,256]{1,0:T(8,128)S(1)} fusion(bf16[1024,4096]{1,0:T(8,128)(2,1)} %all-gather.3.cloned.1.call-done, bf16[1,4096,256]{2,1,0:T(8,128)(2,1)} %param.8), kind=kOutput, calls=%fused_computation.6 | convolution fusion | flops 2147483648 | bytes 11534336 | tf_op jit(solution)/shard_map/dot_general | solution.py:20
  133.4 0.5 copy-done.4
  133.9 3.1 %fusion.20 = bf16[1024,256]{1,0:T(8,128)(2,1)} fusion(bf16[1024,4096]{1,0:T(8,128)(2,1)S(1)} %copy-done.3, bf16[1,4096,256]{2,1,0:T(8,128)(2,1)S(1)} %copy-done.4, f32[1024,256]{1,0:T(8,128)S(1)} %fusion.4), kind=kOutput, calls=%fused_computation.21 | convolution fusion | flops 2149056512 | bytes 12058624 | tf_op jit(solution)/shard_map/dot_general | solution.py:21
  137.0 0.4 fusion.37
  137.4 6.0 %psum.28 = f32[512,4]{0,1:T(4,128)S(1)} all-reduce(f32[512,4]{0,1:T(4,128)S(1)} %fusion.37), channel_id=1, replica_groups=mesh['groups'=2,'expert'=4,'dp'=4] {'dp'}, use_global_device_ids=true, to_apply=%region_4.0 | all-reduce | flops 2048 | bytes 16384 | tf_op jit(solution)/shard_map/psum | solution.py:39
  143.4 0.1 exponential_reduce_fusion
  143.6 11.9 %psum.29 = f32[4]{0:T(128)S(1)} all-reduce(f32[4]{0:T(128)S(1)} %exponential_reduce_fusion), channel_id=1, replica_groups=mesh['groups'=2,'expert'=4,'dp'=4] {'expert'}, use_global_device_ids=true, to_apply=%region_6.0 | all-reduce | flops 4 | bytes 32 | tf_op jit(solution)/shard_map/psum | solution.py:40
  155.4 4.6 %all-gather.5.cloned.1.call-done = bf16[1024,1024]{1,0:T(8,128)(2,1)} async-done(((bf16[1024,256]{1,0:T(8,128)(2,1)}), bf16[1024,1024]{1,0:T(8,128)(2,1)}) %all-gather.5.cloned.1.call-update) | async-done | bytes 2097168 | tf_op jit(solution)/shard_map/all_gather | solution.py:25
  160.0 5.3 %fusion.14 = bf16[1024,1024]{1,0:T(8,128)(2,1)} fusion(bf16[1024,1024]{1,0:T(8,128)(2,1)} %all-gather.5.cloned.1.call-done, bf16[1,1024,1024]{2,1,0:T(8,128)(2,1)S(1)} %copy-done), kind=kOutput, calls=%fused_computation.18 | convolution fusion | flops 2148532224 | bytes 6291456 | tf_op jit(solution)/shard_map/dot_general | solution.py:24
  165.3 4.6 %all-to-all-start.1 = ((bf16[4,256,1024]{2,1,0:T(8,128)(2,1)}), bf16[4,256,1024]{2,1,0:T(8,128)(2,1)}, u32[]{:S(2)}, u32[]{:S(2)}) async-start(bf16[4,256,1024]{2,1,0:T(8,128)(2,1)} %bitcast.47), calls=%async_computation.1 | async-start | bytes 4194304 | tf_op jit(solution)/shard_map/all_to_all | solution.py:65
  169.9 0.1 multiply_reduce_fusion.4
  170.0 0.1 multiply_reduce_fusion.3
  170.1 40.4 %psum.30 = f32[4]{0:T(128)S(1)} all-reduce(f32[4]{0:T(128)S(1)} %multiply_reduce_fusion.3), channel_id=1, replica_groups=mesh['groups'=2,'expert'=4,'dp'=4] {'expert'}, use_global_device_ids=true, to_apply=%region_9.0 | all-reduce | flops 4 | bytes 32 | tf_op jit(solution)/shard_map/psum | solution.py:40
  210.5 0.1 multiply_reduce_fusion.2
  210.6 0.1 multiply_reduce_fusion.1
  210.7 20.3 %psum.31 = f32[4]{0:T(128)S(1)} all-reduce(f32[4]{0:T(128)S(1)} %multiply_reduce_fusion.1), channel_id=1, replica_groups=mesh['groups'=2,'expert'=4,'dp'=4] {'expert'}, use_global_device_ids=true, to_apply=%region_12.13 | all-reduce | flops 4 | bytes 32 | tf_op jit(solution)/shard_map/psum | solution.py:40
  231.0 0.1 multiply_reduce_fusion
  231.2 9.0 %gather_fusion = f32[1024]{0:T(1024)S(1)} fusion(f32[512,4]{0,1:T(4,128)S(1)} %multiply_multiply_fusion, s32[1024]{0:T(1024)S(1)} %bitcast.45), kind=kCustom, calls=%fused_computation | custom fusion | bytes 16384 | tf_op jit(solution)/shard_map/gather | solution.py:53
  240.3 0.8 select_reduce_fusion
  241.1 6.9 %gather_fusion.1 = f32[1024]{0:T(1024)S(1)} fusion(f32[512]{0:T(512)S(1)} %select_reduce_fusion, s32[1024]{0:T(1024)S(1)} %broadcast_clamp_fusion), kind=kCustom, calls=%fused_computation.1 | custom fusion | bytes 12288 | tf_op jit(solution)/shard_map/gather | solution.py:56
  248.1 4.0 %convolution_convert_fusion = bf16[512,1024]{1,0:T(8,128)(2,1)} fusion(bf16[1024,1024]{1,0:T(8,128)(2,1)} %bitcast.8, bf16[1024]{0:T(1024)(128)(2,1)S(1)} %divide_select_fusion, s32[1024]{0:T(1024)S(1)} %bitcast.55, pred[1024]{0:T(1024)(128)(4,1)S(1)} %and.33), kind=kOutput, calls=%fused_computation.19 | convolution fusion | flops 1075838976 | bytes 3152896 | tf_op jit(solution)/shard_map/dot_general | solution.py:66
  (32 shorter events, 0.3 us)
Async XLA Ops:
  6.5 153.5 %copy-start = (bf16[1,1024,1024]{2,1,0:T(8,128)(2,1)S(1)}, bf16[1,1024,1024]{2,1,0:T(8,128)(2,1)}, u32[]{:S(2)}) copy-start(bf16[1,1024,1024]{2,1,0:T(8,128)(2,1)} %param.10) | copy-start | bytes 6291460
  6.5 120.4 %all-gather.3.cloned.1.call-start = ((), (), s32[]{:S(2)}) async-start(), calls=%async_computation.2 | async-start | bytes 10485760 | tf_op jit(solution)/shard_map/all_gather | solution.py:17
  69.2 90.8 %all-gather.5.cloned.1.call-start = ((), (), s32[]{:S(2)}) async-start(), calls=%async_computation.3 | async-start | bytes 2621440 | tf_op jit(solution)/shard_map/all_gather | solution.py:25
  126.9 6.5 %copy-start.3 = (bf16[1024,4096]{1,0:T(8,128)(2,1)S(1)}, bf16[1024,4096]{1,0:T(8,128)(2,1)}, u32[]{:S(2)}) copy-start(bf16[1024,4096]{1,0:T(8,128)(2,1)} %all-gather.3.cloned.1.call-done) | copy-start | bytes 25165828
  126.9 7.0 %copy-start.4 = (bf16[1,4096,256]{2,1,0:T(8,128)(2,1)S(1)}, bf16[1,4096,256]{2,1,0:T(8,128)(2,1)}, u32[]{:S(2)}) copy-start(bf16[1,4096,256]{2,1,0:T(8,128)(2,1)} %param.9) | copy-start | bytes 6291460
  133.9 3.2 %copy-start.1 = (bf16[512,1024]{1,0:T(8,128)(2,1)S(1)}, bf16[512,1024]{1,0:T(8,128)(2,1)}, u32[]{:S(2)}) copy-start(bf16[512,1024]{1,0:T(8,128)(2,1)} %param.6) | copy-start | bytes 3145732
  133.9 3.2 %copy-start.2 = (bf16[1024,4]{0,1:T(4,128)(2,1)S(1)}, bf16[1024,4]{0,1:T(4,128)(2,1)}, u32[]{:S(2)}) copy-start(bf16[1024,4]{0,1:T(4,128)(2,1)} %param.7) | copy-start | bytes 24580
  165.3 82.7 %all-to-all-start.1 = ((bf16[4,256,1024]{2,1,0:T(8,128)(2,1)}), bf16[4,256,1024]{2,1,0:T(8,128)(2,1)}, u32[]{:S(2)}, u32[]{:S(2)}) async-start(bf16[4,256,1024]{2,1,0:T(8,128)(2,1)} %bitcast.47), calls=%async_computation.1 | async-start | bytes 4194304 | tf_op jit(solution)/shard_map/all_to_all | solution.py:65
Sparse Core Ops, SparseCore 0:
  69.4 57.4 all-gather.2
  137.1 22.8 all-gather.4
where the time goes:
time: 259 us
  blocking collectives  133 us (51%)
  waiting for transfers between devices  62.3 us (24%)
  matrix products  22.3 us (9%)
  local copies, waits for them, and re-layouts  16.7 us (6%)
  between operations  13.6 us (5%)
  other arithmetic  6.53 us (3%)
  starting transfers between devices  4.64 us (2%)
    psum x3, blocking collectives, shards(): lax.psum(column, 'expert')  72.5 us
    all_gather x1, waiting for transfers between devices, run_expert(): piece = lax.all_gather(row_block, 'dp', axis=1, tiled=True)  57.6 us
    all_to_all x1, blocking collectives, shards(): lax.all_to_all(outbound, 'expert', split_axis=0, concat_axis=0, tiled=True)  54.4 us
    gather x1, local copies, waits for them, and re-layouts, shards(): slot_score = jnp.where(filled, scores[slot_row, expert_ids], 0.0)  9.03 us
    gather x1, local copies, waits for them, and re-layouts, shards(): token_total[slot_row]  6.88 us
    dot_general x1, matrix products, run_expert(): gate = jnp.dot(piece, gate_piece, preferred_element_type=jnp.float32)  6.46 us
    psum x1, blocking collectives, shards(): logits = lax.psum(partial_value, 'dp')  6.01 us
    dot_general x1, matrix products, run_expert(): jnp.dot(lax.all_gather(hidden, 'dp', axis=1, tiled=True), down_piece, pre...  5.27 us
  transfers between devices with their start and end apart: 3, of which 2 were waited for; matrix products, arithmetic and copies ran while one was open for 7% of the time, Pallas kernels for 0%

commit v1 on v0

v1 whole, which is shorter than its diff:
```python
import functools

import jax
import jax.numpy as jnp
from jax import lax
from jax.experimental import pallas as pl
from jax.experimental.pallas import tpu as pltpu
from jax.sharding import PartitionSpec as P

BATCHES = 2
F32 = jnp.float32
BF16 = jnp.bfloat16
I32 = jnp.int32
VMEM_LIMIT = 48 * 1024 * 1024


def whole(count):
    return [pl.BlockSpec(memory_space=pltpu.VMEM)] * count


def smem():
    return pl.BlockSpec(memory_space=pltpu.SMEM)


def params():
    return pltpu.CompilerParams(vmem_limit_bytes=VMEM_LIMIT)


def dot(a, b):
    return jnp.dot(a, b, preferred_element_type=F32)


def pack_kernel(experts, depth, place_ref, picks_ref, tokens_ref, code_ref, *sends):
    me = place_ref[0]
    rows, width = tokens_ref.shape
    capacity = picks_ref.shape[1]
    strips = rows // 128
    lanes = lax.broadcasted_iota(I32, (128, capacity), 0)
    strip_ids = lax.broadcasted_iota(I32, (8, capacity), 0)
    upper = (lax.broadcasted_iota(I32, (128, 128), 0) < lax.broadcasted_iota(I32, (128, 128), 1)).astype(BF16)
    before = (lax.broadcasted_iota(I32, (8, 8), 1) < lax.broadcasted_iota(I32, (8, 8), 0)).astype(BF16)
    slot_ids = lax.broadcasted_iota(I32, (BATCHES * depth, rows), 0)
    ones = jnp.ones((128, 128), BF16)
    for shift in range(experts):
        expert = lax.rem(me + shift, experts)
        chosen = picks_ref[pl.ds(expert, 1), :]
        local = chosen - me * rows
        start = jnp.sum((local < 0).astype(F32)).astype(I32)
        strip = lax.shift_right_arithmetic(local, 7)
        place = jnp.bitwise_and(local, 127)
        high = (strip == strip_ids).astype(BF16)
        high = jnp.where(strip_ids < strips, high, jnp.zeros_like(high))
        low = (place == lanes).astype(BF16)
        mask = lax.dot_general(high, low, (((1,), (1,)), ((), ())), preferred_element_type=F32)
        mask16 = mask.astype(BF16)
        totals = dot(mask16, ones)
        rank = (dot(mask16, upper) + dot(before, totals.astype(BF16))).astype(I32)
        batch = lax.rem(rank + start, BATCHES)
        slot = batch * depth + lax.div(rank, BATCHES)
        code = jnp.where(mask > 0.5, slot, -1)
        row = jnp.concatenate([code[i : i + 1] for i in range(strips)], axis=1)
        code_ref[pl.ds(shift, 1), :] = row
        selector = (slot_ids == row).astype(F32).astype(BF16)
        packed = dot(selector, tokens_ref[...]).astype(BF16)
        for k in range(BATCHES):
            sends[k * experts + shift][...] = packed[k * depth : (k + 1) * depth]


def pack_rows(place, picks, tokens, experts, depth):
    rows, width = tokens.shape
    out = pl.pallas_call(
        functools.partial(pack_kernel, experts, depth),
        out_shape=[jax.ShapeDtypeStruct((experts, rows), I32)]
        + [jax.ShapeDtypeStruct((depth, width), BF16)] * (BATCHES * experts),
        in_specs=[smem()] + whole(2),
        out_specs=whole(1 + BATCHES * experts),
        compiler_params=params(),
    )(place, picks, tokens)
    code, sends = out[0], out[1:]
    return code, [sends[k * experts : (k + 1) * experts] for k in range(BATCHES)]


def compact_kernel(experts, k, offset_ref, count_ref, *refs):
    blocks, out_ref = refs[:experts], refs[experts]
    depth = blocks[0].shape[0]
    size = out_ref.shape[0]
    row = lax.broadcasted_iota(I32, (size, depth), 0)
    lane = lax.broadcasted_iota(I32, (size, depth), 1)
    parts = [
        ((row - offset_ref[k, i] == lane) & (lane < count_ref[k, i])).astype(F32).astype(BF16)
        for i in range(experts)
    ]
    out_ref[...] = dot(
        jnp.concatenate(parts, axis=1), jnp.concatenate([b[...] for b in blocks], axis=0)
    ).astype(BF16)


def compact(offsets, counts, k, blocks, size):
    experts = len(blocks)
    return pl.pallas_call(
        functools.partial(compact_kernel, experts, k),
        out_shape=jax.ShapeDtypeStruct((size, blocks[0].shape[1]), BF16),
        in_specs=[smem(), smem()] + whole(experts),
        out_specs=whole(1)[0],
        compiler_params=params(),
    )(offsets, counts, *blocks)


def hidden_kernel(parts, order_ref, gate_ref, up_ref, *refs):
    xs, out_ref, gate_sum, up_sum = refs[:parts], refs[parts], refs[parts + 1], refs[parts + 2]
    step = pl.program_id(0)
    for i in range(parts):

        @pl.when(step == i)
        def _():
            gate = dot(xs[i][...], gate_ref[0])
            up = dot(xs[i][...], up_ref[0])
            if i > 0:
                gate = gate + gate_sum[...]
                up = up + up_sum[...]
            if i < parts - 1:
                gate_sum[...] = gate
                up_sum[...] = up
            else:
                out_ref[...] = (gate * jax.nn.sigmoid(gate) * up).astype(BF16)


def hidden_units(order, gate_weight, up_weight, xs):
    parts = len(xs)
    size, width = xs[0].shape
    units = gate_weight.shape[2]
    weight_spec = pl.BlockSpec((1, width, units), lambda i, order: (0, order[i], 0))
    return pl.pallas_call(
        functools.partial(hidden_kernel, parts),
        grid_spec=pltpu.PrefetchScalarGridSpec(
            num_scalar_prefetch=1,
            grid=(parts,),
            in_specs=[weight_spec, weight_spec] + [pl.BlockSpec((size, width), lambda i, order: (0, 0))] * parts,
            out_specs=pl.BlockSpec((size, units), lambda i, order: (0, 0)),
            scratch_shapes=[pltpu.VMEM((size, units), F32)] * 2,
        ),
        out_shape=jax.ShapeDtypeStruct((size, units), BF16),
        compiler_params=params(),
    )(order, gate_weight, up_weight, *xs)


def down_kernel(parts, experts, k, order_ref, offset_ref, count_ref, down_ref, *refs):
    hs, outs = refs[:parts], refs[parts : parts + experts]
    size, units = hs[0].shape
    depth = outs[0].shape[0]
    total = None
    for i in range(parts):
        first = pl.multiple_of(order_ref[i] * units, units)
        term = dot(hs[i][...], down_ref[0, pl.ds(first, units), :])
        total = term if total is None else total + term
    result = total.astype(BF16)
    row = lax.broadcasted_iota(I32, (depth, size), 0)
    lane = lax.broadcasted_iota(I32, (depth, size), 1)
    for i in range(experts):
        pick = ((lane - offset_ref[k, i] == row) & (row < count_ref[k, i])).astype(F32).astype(BF16)
        outs[i][...] = dot(pick, result).astype(BF16)


def down_rows(order, offsets, counts, k, down_weight, hs, experts, depth):
    parts = len(hs)
    width = down_weight.shape[2]
    return pl.pallas_call(
        functools.partial(down_kernel, parts, experts, k),
        out_shape=[jax.ShapeDtypeStruct((depth, width), BF16)] * experts,
        in_specs=[smem()] * 3 + whole(1 + parts),
        out_specs=whole(experts),
        compiler_params=params(),
    )(order, offsets, counts, down_weight, *hs)


def weight_kernel(experts, place_ref, own_ref, logits_ref, code_ref, out_ref, score_ref):
    me = place_ref[0]
    kernel = jnp.exp(logits_ref[...])
    row_scale = jnp.ones((kernel.shape[0], 1, kernel.shape[2]), F32)
    for sweep in range(3):
        column = jnp.sum(jnp.sum(kernel * row_scale, axis=0, keepdims=True), axis=2, keepdims=True)
        column_scale = 1.0 / column
        row_scale = 1.0 / jnp.sum(kernel * column_scale, axis=1, keepdims=True)
    own = jnp.exp(own_ref[...])
    column_scale = column_scale[0]
    own_scale = 1.0 / jnp.sum(own * column_scale, axis=0, keepdims=True)
    score_ref[...] = own_scale * own * column_scale
    picked = []
    for shift in range(experts):
        score = score_ref[pl.ds(lax.rem(me + shift, experts), 1), :]
        picked.append(jnp.where(code_ref[pl.ds(shift, 1), :] >= 0, score, 0.0))
    total = picked[0]
    for one in picked[1:]:
        total = total + one
    total = jnp.maximum(total, 1.0 / experts)
    for shift in range(experts):
        out_ref[pl.ds(shift, 1), :] = picked[shift] / total


def slot_weights(place, own, logits, code):
    experts, rows = own.shape
    return pl.pallas_call(
        functools.partial(weight_kernel, experts),
        out_shape=jax.ShapeDtypeStruct((experts, rows), F32),
        in_specs=[smem()] + whole(3),
        out_specs=whole(1)[0],
        scratch_shapes=[pltpu.VMEM((experts, rows), F32)],
        compiler_params=params(),
    )(place, own, logits, code)


def combine_kernel(experts, k, last, code_ref, weight_ref, *refs):
    blocks = refs[:experts]
    out_ref = refs[-1]
    depth = blocks[0].shape[0]
    rows = code_ref.shape[1]
    slot_ids = lax.broadcasted_iota(I32, (depth, rows), 0) + k * depth
    parts = [
        jnp.where(slot_ids == code_ref[pl.ds(i, 1), :], weight_ref[pl.ds(i, 1), :], 0.0).astype(BF16)
        for i in range(experts)
    ]
    total = lax.dot_general(
        jnp.concatenate(parts, axis=0),
        jnp.concatenate([b[...] for b in blocks], axis=0),
        (((0,), (0,)), ((), ())),
        preferred_element_type=F32,
    )
    if k > 0:
        total = total + refs[experts][...]
    out_ref[...] = total.astype(out_ref.dtype)


def combine(code, weights, k, blocks, so_far):
    experts = len(blocks)
    last = k == BATCHES - 1
    more = [] if so_far is None else [so_far]
    return pl.pallas_call(
        functools.partial(combine_kernel, experts, k, last),
        out_shape=jax.ShapeDtypeStruct((code.shape[1], blocks[0].shape[1]), BF16 if last else F32),
        in_specs=whole(2 + experts + len(more)),
        out_specs=whole(1)[0],
        compiler_params=params(),
    )(code, weights, *blocks, *more)


def shards(tokens, router_weight, gate_weight, up_weight, down_weight, picks):
    experts = lax.axis_size("expert")
    width_parts = lax.axis_size("dp")
    me = lax.axis_index("expert")
    part = lax.axis_index("dp")
    rows = tokens.shape[0]
    capacity = picks.shape[1]
    depth = 2 * capacity // experts // BATCHES
    size = capacity // BATCHES
    place = me.astype(I32).reshape(1)

    def along_expert(x, shift):
        return lax.ppermute(x, "expert", [(i, (i + shift) % experts) for i in range(experts)])

    def swap(x, bit):
        return lax.ppermute(x, "dp", [(i, i ^ bit) for i in range(width_parts)])

    bits = []
    bit = width_parts // 2
    while bit:
        bits.append(bit)
        bit //= 2
    masks = [0]
    for bit in bits:
        masks = masks + [m ^ bit for m in masks]
    order = jnp.stack([part ^ m for m in masks]).astype(I32)

    def all_parts(x):
        held = [x]
        for bit in bits:
            held = held + [swap(h, bit) for h in held]
        return held

    code, sends = pack_rows(place, picks, tokens, experts, depth)
    own_picks = lax.dynamic_slice_in_dim(picks, me, 1, axis=0)
    sources = lax.rem(me - jnp.arange(experts, dtype=I32) + experts, experts)
    start = jnp.sum((own_picks < (sources * rows)[:, None]).astype(I32), axis=1)
    stop = jnp.sum((own_picks < ((sources + 1) * rows)[:, None]).astype(I32), axis=1)
    ids = jnp.arange(BATCHES, dtype=I32)[:, None]
    offsets = (start[None, :] + (BATCHES - 1) - ids) // BATCHES
    counts = (stop[None, :] + (BATCHES - 1) - ids) // BATCHES - offsets

    arrived = [
        [sends[k][0]] + [along_expert(sends[k][shift], shift) for shift in range(1, experts)]
        for k in range(BATCHES)
    ]

    logits = lax.dot_general(
        router_weight, tokens, (((0,), (1,)), ((), ())), preferred_element_type=F32
    )
    for bit in bits:
        logits = logits + swap(logits, bit)
    gathered = jnp.stack([logits] + [along_expert(logits, shift) for shift in range(1, experts)])
    weights = slot_weights(place, logits, gathered, code)

    total = None
    for k in range(BATCHES):
        block = compact(offsets, counts, k, arrived[k], size)
        hidden = hidden_units(order, gate_weight, up_weight, all_parts(block))
        results = down_rows(order, offsets, counts, k, down_weight, all_parts(hidden), experts, depth)
        returned = [results[0]] + [along_expert(results[shift], -shift) for shift in range(1, experts)]
        total = combine(code, weights, k, returned, total)
    return total


def solution(mesh):
    return jax.shard_map(
        shards,
        mesh=mesh,
        in_specs=(
            P(("groups", "expert"), "dp"),
            P("dp", None),
            P("expert", None, "dp"),
            P("expert", None, "dp"),
            P("expert", None, "dp"),
            P("groups", None),
        ),
        out_specs=P(("groups", "expert"), "dp"),
        check_vma=False,
    )
```

time: 259 us -> 159 us (0.61)
  blocking collectives: 133 us -> 0 us
  starting transfers between devices: 4.64 us -> 37.7 us
  waiting for transfers between devices: 62.3 us -> 87.8 us
  matrix products: 22.3 us -> 0.37 us
  Pallas kernels: 0 us -> 21.4 us
  between operations: 13.6 us -> 0.19 us
  other arithmetic: 6.53 us -> 0.34 us
  local copies, waits for them, and re-layouts: 16.7 us -> 11 us
    ppermute x0 -> x29, waiting for transfers between devices: none -> 87.8 us  [the longest x15 64.6 us: along_expert(): lax.ppermute(x, 'expert', [(i, (i + shift) % experts) for i in range(expe...]
    psum x4 -> x0, blocking collectives: 78.5 us -> none  [the longest x3 72.5 us: shards(): lax.psum(column, 'expert')]
    all_gather x2 -> x0, waiting for transfers between devices: 62.2 us -> none  [the longest x1 57.6 us: run_expert(): piece = lax.all_gather(row_block, 'dp', axis=1, tiled=True)]
    all_to_all x1 -> x0, blocking collectives: 54.4 us -> none  [shards(): lax.all_to_all(outbound, 'expert', split_axis=0, concat_axis=0, tiled=True)]
    ppermute x0 -> x29, starting transfers between devices: none -> 37.7 us  [the longest x15 30.8 us: along_expert(): lax.ppermute(x, 'expert', [(i, (i + shift) % experts) for i in range(expe...]
    dot_general x6 -> x1, matrix products: 22.3 us -> 0.37 us  [shards(): lax.dot_general(router_weight, tokens, (((0,), (1,)), ((), ())), preferre...]
    pallas_call x0 -> x10, Pallas kernels: none -> 21.4 us  [the longest x2 9.18 us: hidden_units(): pl.pallas_call(functools.partial(hidden_kernel, parts), grid_spec=pltpu.P...]
    gather x2 -> x0, local copies, waits for them, and re-layouts: 15.9 us -> none  [the longest x1 9.03 us: shards(): slot_score = jnp.where(filled, scores[slot_row, expert_ids], 0.0)]
  transfers between devices with their start and end apart: 3 -> 29, of which waited for: 2 -> 10; matrix products, arithmetic and copies ran while one was open for 7% -> 0% of each run, Pallas kernels for 0% -> 10%
where the time goes in v1:
time: 159 us
  waiting for transfers between devices  87.8 us (55%)
  starting transfers between devices  37.7 us (24%)
  Pallas kernels  21.4 us (13%)
  local copies, waits for them, and re-layouts  11 us (7%)
    ppermute x15, waiting for transfers between devices, along_expert(): lax.ppermute(x, 'expert', [(i, (i + shift) % experts) for i in range(expe...  64.6 us
    ppermute x15, starting transfers between devices, along_expert(): lax.ppermute(x, 'expert', [(i, (i + shift) % experts) for i in range(expe...  30.8 us
    ppermute x14, waiting for transfers between devices, swap(): return lax.ppermute(x, 'dp', [(i, i ^ bit) for i in range(width_parts)])  23.1 us
    unnamed x34, local copies, waits for them, and re-layouts  11 us
    pallas_call x2, Pallas kernels, hidden_units(): pl.pallas_call(functools.partial(hidden_kernel, parts), grid_spec=pltpu.P...  9.18 us
    ppermute x14, starting transfers between devices, swap(): return lax.ppermute(x, 'dp', [(i, i ^ bit) for i in range(width_parts)])  6.85 us
    pallas_call x1, Pallas kernels, pack_rows(): pl.pallas_call(functools.partial(pack_kernel, experts, depth), out_shape=...  3.63 us
    pallas_call x2, Pallas kernels, down_rows(): pl.pallas_call(functools.partial(down_kernel, parts, experts, k), out_sha...  3.38 us
  transfers between devices with their start and end apart: 29, of which 10 were waited for; matrix products, arithmetic and copies ran while one was open for 0% of the time, Pallas kernels for 10%

profile of v1, /device:TPU:0, one launch (start us, length us, event | category | flops | bytes accessed | tf_op | source)
XLA Modules:
  0.0 158.7 jit_solution(3302599034485688539)
XLA Ops:
  0.0 1.2 copy-done.3
  1.9 3.6 %shard_map.64 = (s32[4,512]{1,0:T(4,128)S(1)}, bf16[128,1024]{1,0:T(8,128)(2,1)S(1)}, bf16[128,1024]{1,0:T(8,128)(2,1)}, bf16[128,1024]{1,0:T(8,128)(2,1)}, bf16...) custom-call(s32[1]{0:T(128)} %bitcast.place_ref, ...), custom_call_target="tpu_custom_call" | custom-call | tf_op jit(solution)/shard_map/pallas_call | solution.py:71
  7.0 3.0 %collective-permute-start.5 = (bf16[128,1024]{1,0:T(8,128)(2,1)}, bf16[128,1024]{1,0:T(8,128)(2,1)S(1)}, u32[]{:S(2)}, u32[]{:S(2)}) collective-permute-start(bf16[128,1024]{1,0:T(8,128)(2,1)} %get-tuple-element.24), channel_id=1, source_target_pairs={{0,4},{4,8},{8,12},{12,0},{1,5},{5,9},{9,13},{13,1},{2,6},{6,10},{... | collective-permute-start | bytes 786440 | tf_op jit(solution)/shard_map/ppermute | solution.py:258
  10.0 2.6 %collective-permute-start.6 = (bf16[128,1024]{1,0:T(8,128)(2,1)}, bf16[128,1024]{1,0:T(8,128)(2,1)S(1)}, u32[]{:S(2)}, u32[]{:S(2)}) collective-permute-start(bf16[128,1024]{1,0:T(8,128)(2,1)} %get-tuple-element.25), channel_id=1, source_target_pairs={{0,8},{4,12},{8,0},{12,4},{1,9},{5,13},{9,1},{13,5},{2,10},{6,14},... | collective-permute-start | bytes 786440 | tf_op jit(solution)/shard_map/ppermute | solution.py:258
  12.6 1.9 %collective-permute-start.18 = (bf16[128,1024]{1,0:T(8,128)(2,1)}, bf16[128,1024]{1,0:T(8,128)(2,1)S(1)}, u32[]{:S(2)}, u32[]{:S(2)}) collective-permute-start(bf16[128,1024]{1,0:T(8,128)(2,1)} %get-tuple-element.33), channel_id=1, source_target_pairs={{0,8},{4,12},{8,0},{12,4},{1,9},{5,13},{9,1},{13,5},{2,10},{6,14},... | collective-permute-start | bytes 786440 | tf_op jit(solution)/shard_map/ppermute | solution.py:258
  14.5 1.9 %collective-permute-start.19 = (bf16[128,1024]{1,0:T(8,128)(2,1)}, bf16[128,1024]{1,0:T(8,128)(2,1)}, u32[]{:S(2)}, u32[]{:S(2)}) collective-permute-start(bf16[128,1024]{1,0:T(8,128)(2,1)} %get-tuple-element.34), channel_id=1, source_target_pairs={{0,12},{4,0},{8,4},{12,8},{1,13},{5,1},{9,5},{13,9},{2,14},{6,2},{... | collective-permute-start | bytes 786440 | tf_op jit(solution)/shard_map/ppermute | solution.py:258
  16.7 14.0 %collective-permute-done.17.refs_1_ = bf16[128,1024]{1,0:T(8,128)(2,1)S(1)} collective-permute-done((bf16[128,1024]{1,0:T(8,128)(2,1)}, bf16[128,1024]{1,0:T(8,128)(2,1)S(1)}, u32[]{:S(2)}, u32[]{:S(2)}) %collective-permute-start.17) | collective-permute-done | bytes 262176 | tf_op jit(solution)/shard_map/ppermute | solution.py:258
  31.5 15.3 %collective-permute-done.18.refs_2_ = bf16[128,1024]{1,0:T(8,128)(2,1)S(1)} collective-permute-done((bf16[128,1024]{1,0:T(8,128)(2,1)}, bf16[128,1024]{1,0:T(8,128)(2,1)S(1)}, u32[]{:S(2)}, u32[]{:S(2)}) %collective-permute-start.18) | collective-permute-done | bytes 262176 | tf_op jit(solution)/shard_map/ppermute | solution.py:258
  47.5 0.9 copy-done.10
  50.3 1.4 shard_map.69.refs_0_
  51.7 1.6 collective-permute-start.20
  54.7 2.9 %collective-permute-done.7.refs_3_ = bf16[128,1024]{1,0:T(8,128)(2,1)S(1)} collective-permute-done((bf16[128,1024]{1,0:T(8,128)(2,1)}, bf16[128,1024]{1,0:T(8,128)(2,1)S(1)}, u32[]{:S(2)}, u32[]{:S(2)}) %collective-permute-start.7) | collective-permute-done | bytes 262176 | tf_op jit(solution)/shard_map/ppermute | solution.py:258
  57.7 0.9 copy-done.6
  59.6 1.0 shard_map.66.refs_0_
  60.6 1.6 collective-permute-start.8
  62.1 4.6 %collective-permute-done.20.refs_1_ = bf16[256,1024]{1,0:T(8,128)(2,1)} collective-permute-done((bf16[256,1024]{1,0:T(8,128)(2,1)S(1)}, bf16[256,1024]{1,0:T(8,128)(2,1)}, u32[]{:S(2)}, u32[]{:S(2)}) %collective-permute-start.20) | collective-permute-done | bytes 524320 | tf_op jit(solution)/shard_map/ppermute | solution.py:261
  67.2 9.7 %collective-permute-done.8.refs_1_ = bf16[256,1024]{1,0:T(8,128)(2,1)} collective-permute-done((bf16[256,1024]{1,0:T(8,128)(2,1)S(1)}, bf16[256,1024]{1,0:T(8,128)(2,1)}, u32[]{:S(2)}, u32[]{:S(2)}) %collective-permute-start.8) | collective-permute-done | bytes 524320 | tf_op jit(solution)/shard_map/ppermute | solution.py:261
  77.0 4.6 %shard_map.70.refs_0_ = bf16[256,256]{1,0:T(8,128)(2,1)S(1)} custom-call(s32[4]{0:T(128)S(1)} %pad_add_fusion.order_ref, bf16[1,4096,256]{2,1,0:T(8,128)(2,1)S(1)} %copy-done.1, bf16[1,4096,256]{2,1,0:T(8,128)(2,1)} %up_ref.3, bf16[256,1024]{1,0:T(8,128)(2,1)S(1)} %shard_map.69.refs_0_, bf16[256,1024]{1,0:T(8,128)(2,1)} %collective-permute-done.20.refs_1_, ...), custom_call_target="tpu_custom_call" | custom-call | tf_op jit(solution)/shard_map/pallas_call | solution.py:133
  81.6 1.6 collective-permute-start.23
  83.2 4.6 %shard_map.67.refs_0_ = bf16[256,256]{1,0:T(8,128)(2,1)S(1)} custom-call(s32[4]{0:T(128)S(1)} %pad_add_fusion.order_ref, bf16[1,4096,256]{2,1,0:T(8,128)(2,1)S(1)} %copy-done.1, bf16[1,4096,256]{2,1,0:T(8,128)(2,1)} %up_ref.3, bf16[256,1024]{1,0:T(8,128)(2,1)S(1)} %shard_map.66.refs_0_, bf16[256,1024]{1,0:T(8,128)(2,1)} %collective-permute-done.8.refs_1_, ...), custom_call_target="tpu_custom_call" | custom-call | tf_op jit(solution)/shard_map/pallas_call | solution.py:133
  88.9 4.6 %collective-permute-done.11.refs_1_ = bf16[256,256]{1,0:T(8,128)(2,1)S(1)} collective-permute-done((bf16[256,256]{1,0:T(8,128)(2,1)S(1)}, bf16[256,256]{1,0:T(8,128)(2,1)S(1)}, u32[]{:S(2)}, u32[]{:S(2)}) %collective-permute-start.11) | collective-permute-done | bytes 131104 | tf_op jit(solution)/shard_map/ppermute | solution.py:261
  93.5 1.7 %shard_map.71 = (bf16[128,1024]{1,0:T(8,128)(2,1)S(1)}, bf16[128,1024]{1,0:T(8,128)(2,1)S(1)}, bf16[128,1024]{1,0:T(8,128)(2,1)S(1)}, bf16[128,1024]{1,0:T(8,128)(2,1)S(1)}) custom-call(s32[4]{0:T(128)S(1)} %pad_add_fusion.order_ref, s32[2,4]{1,0:T(2,128)S(1)} %get-tuple-element.42.offset_ref, s32[2,4]{1,0:T(2,128)S(1)} %get-tuple-element.41.count_ref, ...), custom_call_target="tpu_custom_call" | custom-call | tf_op jit(solution)/shard_map/pallas_call | solution.py:167
  95.2 11.9 %collective-permute-start.26 = (bf16[128,1024]{1,0:T(8,128)(2,1)S(1)}, bf16[128,1024]{1,0:T(8,128)(2,1)S(1)}, u32[]{:S(2)}, u32[]{:S(2)}) collective-permute-start(bf16[128,1024]{1,0:T(8,128)(2,1)S(1)} %get-tuple-element.36), channel_id=1, source_target_pairs={{0,12},{4,0},{8,4},{12,8},{1,13},{5,1},{9,5},{13,9},{2,14},{6,2},{... | collective-permute-start | bytes 786440 | tf_op jit(solution)/shard_map/ppermute | solution.py:258
  108.0 3.1 %collective-permute-done = f32[4,512]{1,0:T(4,128)S(1)} collective-permute-done((f32[4,512]{1,0:T(4,128)S(1)}, f32[4,512]{1,0:T(4,128)S(1)}, u32[]{:S(2)}, u32[]{:S(2)}) %collective-permute-start) | collective-permute-done | bytes 8224 | tf_op jit(solution)/shard_map/ppermute | solution.py:261
  111.2 1.2 collective-permute-done.1
  112.4 1.9 %collective-permute-start.2 = (f32[4,512]{1,0:T(4,128)S(1)}, f32[4,512]{1,0:T(4,128)S(1)}, u32[]{:S(2)}, u32[]{:S(2)}) collective-permute-start(f32[4,512]{1,0:T(4,128)S(1)} %add.45.own_ref), channel_id=1, source_target_pairs={{0,4},{4,8},{8,12},{12,0},{1,5},{5,9},{9,13},{13,1},{2,6},{6,10},{... | collective-permute-start | bytes 24584 | tf_op jit(solution)/shard_map/ppermute | solution.py:258
  114.4 2.9 %collective-permute-start.27 = (bf16[128,1024]{1,0:T(8,128)(2,1)S(1)}, bf16[128,1024]{1,0:T(8,128)(2,1)S(1)}, u32[]{:S(2)}, u32[]{:S(2)}) collective-permute-start(bf16[128,1024]{1,0:T(8,128)(2,1)S(1)} %get-tuple-element.37), channel_id=1, source_target_pairs={{0,8},{4,12},{8,0},{12,4},{1,9},{5,13},{9,1},{13,5},{2,10},{6,14},... | collective-permute-start | bytes 786440 | tf_op jit(solution)/shard_map/ppermute | solution.py:258
  117.3 1.7 %shard_map.68 = (bf16[128,1024]{1,0:T(8,128)(2,1)S(1)}, bf16[128,1024]{1,0:T(8,128)(2,1)S(1)}, bf16[128,1024]{1,0:T(8,128)(2,1)S(1)}, bf16[128,1024]{1,0:T(8,128)(2,1)S(1)}) custom-call(s32[4]{0:T(128)S(1)} %pad_add_fusion.order_ref, s32[2,4]{1,0:T(2,128)S(1)} %get-tuple-element.42.offset_ref, s32[2,4]{1,0:T(2,128)S(1)} %get-tuple-element.41.count_ref, ...), custom_call_target="tpu_custom_call" | custom-call | tf_op jit(solution)/shard_map/pallas_call | solution.py:167
  119.1 3.8 %collective-permute-start.14 = (bf16[128,1024]{1,0:T(8,128)(2,1)S(1)}, bf16[128,1024]{1,0:T(8,128)(2,1)S(1)}, u32[]{:S(2)}, u32[]{:S(2)}) collective-permute-start(bf16[128,1024]{1,0:T(8,128)(2,1)S(1)} %get-tuple-element.28), channel_id=1, source_target_pairs={{0,12},{4,0},{8,4},{12,8},{1,13},{5,1},{9,5},{13,9},{2,14},{6,2},{... | collective-permute-start | bytes 786440 | tf_op jit(solution)/shard_map/ppermute | solution.py:258
  123.9 13.0 %collective-permute-done.27.refs_2_ = bf16[128,1024]{1,0:T(8,128)(2,1)S(1)} collective-permute-done((bf16[128,1024]{1,0:T(8,128)(2,1)S(1)}, bf16[128,1024]{1,0:T(8,128)(2,1)S(1)}, u32[]{:S(2)}, u32[]{:S(2)}) %collective-permute-start.27) | collective-permute-done | bytes 262176 | tf_op jit(solution)/shard_map/ppermute | solution.py:258
  137.6 19.4 %collective-permute-done.15.refs_2_ = bf16[128,1024]{1,0:T(8,128)(2,1)S(1)} collective-permute-done((bf16[128,1024]{1,0:T(8,128)(2,1)S(1)}, bf16[128,1024]{1,0:T(8,128)(2,1)S(1)}, u32[]{:S(2)}, u32[]{:S(2)}) %collective-permute-start.15) | collective-permute-done | bytes 262176 | tf_op jit(solution)/shard_map/ppermute | solution.py:258
  157.0 1.7 %shard_map.73 = bf16[512,1024]{1,0:T(8,128)(2,1)} custom-call(s32[4,512]{1,0:T(4,128)S(1)} %get-tuple-element.22.code_ref, f32[4,512]{1,0:T(4,128)S(1)} %shard_map.65.weight_ref, bf16[128,1024]{1,0:T(8,128)(2,1)S(1)} %get-tuple-element.27.refs_0_, bf16[128,1024]{1,0:T(8,128)(2,1)S(1)} %collective-permute-done.14.refs_1_, ...), custom_call_target="tpu_custom_call" | custom-call | tf_op jit(solution)/shard_map/pallas_call | solution.py:237
  (81 shorter events, 12.7 us)
Async XLA Ops:
  0.0 107.1 %copy-start = (bf16[1024,4]{0,1:T(4,128)(2,1)S(1)}, bf16[1024,4]{0,1:T(4,128)(2,1)}, u32[]{:S(2)}) copy-start(bf16[1024,4]{0,1:T(4,128)(2,1)} %param.7) | copy-start | bytes 24580
  1.9 75.0 %copy-start.1 = (bf16[1,4096,256]{2,1,0:T(8,128)(2,1)S(1)}, bf16[1,4096,256]{2,1,0:T(8,128)(2,1)}, u32[]{:S(2)}) copy-start(bf16[1,4096,256]{2,1,0:T(8,128)(2,1)} %gate_ref.3) | copy-start | bytes 6291460
  7.0 46.3 %collective-permute-start.5 = (bf16[128,1024]{1,0:T(8,128)(2,1)}, bf16[128,1024]{1,0:T(8,128)(2,1)S(1)}, u32[]{:S(2)}, u32[]{:S(2)}) collective-permute-start(bf16[128,1024]{1,0:T(8,128)(2,1)} %get-tuple-element.24), channel_id=1, source_target_pairs={{0,4},{4,8},{8,12},{12,0},{1,5},{5,9},{9,13},{13,1},{2,6},{6,10},{... | collective-permute-start | bytes 786440 | tf_op jit(solution)/shard_map/ppermute | solution.py:258
  10.0 44.0 %collective-permute-start.6 = (bf16[128,1024]{1,0:T(8,128)(2,1)}, bf16[128,1024]{1,0:T(8,128)(2,1)S(1)}, u32[]{:S(2)}, u32[]{:S(2)}) collective-permute-start(bf16[128,1024]{1,0:T(8,128)(2,1)} %get-tuple-element.25), channel_id=1, source_target_pairs={{0,8},{4,12},{8,0},{12,4},{1,9},{5,13},{9,1},{13,5},{2,10},{6,14},... | collective-permute-start | bytes 786440 | tf_op jit(solution)/shard_map/ppermute | solution.py:258
  12.6 18.1 %collective-permute-start.17 = (bf16[128,1024]{1,0:T(8,128)(2,1)}, bf16[128,1024]{1,0:T(8,128)(2,1)S(1)}, u32[]{:S(2)}, u32[]{:S(2)}) collective-permute-start(bf16[128,1024]{1,0:T(8,128)(2,1)} %get-tuple-element.32), channel_id=1, source_target_pairs={{0,4},{4,8},{8,12},{12,0},{1,5},{5,9},{9,13},{13,1},{2,6},{6,10},{... | collective-permute-start | bytes 786440 | tf_op jit(solution)/shard_map/ppermute | solution.py:258
  12.6 34.1 %collective-permute-start.18 = (bf16[128,1024]{1,0:T(8,128)(2,1)}, bf16[128,1024]{1,0:T(8,128)(2,1)S(1)}, u32[]{:S(2)}, u32[]{:S(2)}) collective-permute-start(bf16[128,1024]{1,0:T(8,128)(2,1)} %get-tuple-element.33), channel_id=1, source_target_pairs={{0,8},{4,12},{8,0},{12,4},{1,9},{5,13},{9,1},{13,5},{2,10},{6,14},... | collective-permute-start | bytes 786440 | tf_op jit(solution)/shard_map/ppermute | solution.py:258
  14.5 32.9 %collective-permute-start.19 = (bf16[128,1024]{1,0:T(8,128)(2,1)}, bf16[128,1024]{1,0:T(8,128)(2,1)}, u32[]{:S(2)}, u32[]{:S(2)}) collective-permute-start(bf16[128,1024]{1,0:T(8,128)(2,1)} %get-tuple-element.34), channel_id=1, source_target_pairs={{0,12},{4,0},{8,4},{12,8},{1,13},{5,1},{9,5},{13,9},{2,14},{6,2},{... | collective-permute-start | bytes 786440 | tf_op jit(solution)/shard_map/ppermute | solution.py:258
  31.4 26.2 %collective-permute-start.7 = (bf16[128,1024]{1,0:T(8,128)(2,1)}, bf16[128,1024]{1,0:T(8,128)(2,1)S(1)}, u32[]{:S(2)}, u32[]{:S(2)}) collective-permute-start(bf16[128,1024]{1,0:T(8,128)(2,1)} %copy-done.16), channel_id=1, source_target_pairs={{0,12},{4,0},{8,4},{12,8},{1,13},{5,1},{9,5},{13,9},{2,14},{6,2},{... | collective-permute-start | bytes 786440 | tf_op jit(solution)/shard_map/ppermute | solution.py:258
  51.7 15.0 %collective-permute-start.20 = (bf16[256,1024]{1,0:T(8,128)(2,1)S(1)}, bf16[256,1024]{1,0:T(8,128)(2,1)}, u32[]{:S(2)}, u32[]{:S(2)}) collective-permute-start(bf16[256,1024]{1,0:T(8,128)(2,1)S(1)} %shard_map.69.refs_0_), channel_id=1, source_target_pairs={{0,2},{1,3},{2,0},{3,1},{4,6},{5,7},{6,4},{7,5},{8,10},{9,11},{10,... | collective-permute-start | bytes 1572872 | tf_op jit(solution)/shard_map/ppermute | solution.py:261
  60.6 16.3 %collective-permute-start.8 = (bf16[256,1024]{1,0:T(8,128)(2,1)S(1)}, bf16[256,1024]{1,0:T(8,128)(2,1)}, u32[]{:S(2)}, u32[]{:S(2)}) collective-permute-start(bf16[256,1024]{1,0:T(8,128)(2,1)S(1)} %shard_map.66.refs_0_), channel_id=1, source_target_pairs={{0,2},{1,3},{2,0},{3,1},{4,6},{5,7},{6,4},{7,5},{8,10},{9,11},{10,... | collective-permute-start | bytes 1572872 | tf_op jit(solution)/shard_map/ppermute | solution.py:261
  62.1 14.8 %collective-permute-start.21 = (bf16[256,1024]{1,0:T(8,128)(2,1)S(1)}, bf16[256,1024]{1,0:T(8,128)(2,1)}, u32[]{:S(2)}, u32[]{:S(2)}) collective-permute-start(bf16[256,1024]{1,0:T(8,128)(2,1)S(1)} %shard_map.69.refs_0_), channel_id=1, source_target_pairs={{0,1},{1,0},{2,3},{3,2},{4,5},{5,4},{6,7},{7,6},{8,9},{9,8},{10,11... | collective-permute-start | bytes 1572872 | tf_op jit(solution)/shard_map/ppermute | solution.py:261
  66.7 10.3 %collective-permute-start.22 = (bf16[256,1024]{1,0:T(8,128)(2,1)}, bf16[256,1024]{1,0:T(8,128)(2,1)}, u32[]{:S(2)}, u32[]{:S(2)}) collective-permute-start(bf16[256,1024]{1,0:T(8,128)(2,1)} %collective-permute-done.20.refs_1_), channel_id=1, source_target_pairs={{0,1},{1,0},{2,3},{3,2},{4,5},{5,4},{6,7},{7,6},{8,9},{9,8},{10,11... | collective-permute-start | bytes 1572872 | tf_op jit(solution)/shard_map/ppermute | solution.py:261
  66.7 16.4 %collective-permute-start.9 = (bf16[256,1024]{1,0:T(8,128)(2,1)S(1)}, bf16[256,1024]{1,0:T(8,128)(2,1)}, u32[]{:S(2)}, u32[]{:S(2)}) collective-permute-start(bf16[256,1024]{1,0:T(8,128)(2,1)S(1)} %shard_map.66.refs_0_), channel_id=1, source_target_pairs={{0,1},{1,0},{2,3},{3,2},{4,5},{5,4},{6,7},{7,6},{8,9},{9,8},{10,11... | collective-permute-start | bytes 1572872 | tf_op jit(solution)/shard_map/ppermute | solution.py:261
  76.9 6.3 %collective-permute-start.10 = (bf16[256,1024]{1,0:T(8,128)(2,1)}, bf16[256,1024]{1,0:T(8,128)(2,1)}, u32[]{:S(2)}, u32[]{:S(2)}) collective-permute-start(bf16[256,1024]{1,0:T(8,128)(2,1)} %collective-permute-done.8.refs_1_), channel_id=1, source_target_pairs={{0,1},{1,0},{2,3},{3,2},{4,5},{5,4},{6,7},{7,6},{8,9},{9,8},{10,11... | collective-permute-start | bytes 1572872 | tf_op jit(solution)/shard_map/ppermute | solution.py:261
  81.6 6.8 %collective-permute-start.23 = (bf16[256,256]{1,0:T(8,128)(2,1)S(1)}, bf16[256,256]{1,0:T(8,128)(2,1)S(1)}, u32[]{:S(2)}, u32[]{:S(2)}) collective-permute-start(bf16[256,256]{1,0:T(8,128)(2,1)S(1)} %shard_map.70.refs_0_), channel_id=1, source_target_pairs={{0,2},{1,3},{2,0},{3,1},{4,6},{5,7},{6,4},{7,5},{8,10},{9,11},{10,... | collective-permute-start | bytes 393224 | tf_op jit(solution)/shard_map/ppermute | solution.py:261
  87.8 19.3 %copy-start.4 = (bf16[512,1024]{1,0:T(8,128)(2,1)S(1)}, bf16[512,1024]{1,0:T(8,128)(2,1)}, u32[]{:S(2)}) copy-start(bf16[512,1024]{1,0:T(8,128)(2,1)} %tokens_ref.1) | copy-start | bytes 3145732
  87.8 5.7 %collective-permute-start.11 = (bf16[256,256]{1,0:T(8,128)(2,1)S(1)}, bf16[256,256]{1,0:T(8,128)(2,1)S(1)}, u32[]{:S(2)}, u32[]{:S(2)}) collective-permute-start(bf16[256,256]{1,0:T(8,128)(2,1)S(1)} %shard_map.67.refs_0_), channel_id=1, source_target_pairs={{0,2},{1,3},{2,0},{3,1},{4,6},{5,7},{6,4},{7,5},{8,10},{9,11},{10,... | collective-permute-start | bytes 393224 | tf_op jit(solution)/shard_map/ppermute | solution.py:261
  88.4 5.1 %collective-permute-start.24 = (bf16[256,256]{1,0:T(8,128)(2,1)S(1)}, bf16[256,256]{1,0:T(8,128)(2,1)S(1)}, u32[]{:S(2)}, u32[]{:S(2)}) collective-permute-start(bf16[256,256]{1,0:T(8,128)(2,1)S(1)} %shard_map.70.refs_0_), channel_id=1, source_target_pairs={{0,1},{1,0},{2,3},{3,2},{4,5},{5,4},{6,7},{7,6},{8,9},{9,8},{10,11... | collective-permute-start | bytes 393224 | tf_op jit(solution)/shard_map/ppermute | solution.py:261
  88.4 5.1 %collective-permute-start.25 = (bf16[256,256]{1,0:T(8,128)(2,1)S(1)}, bf16[256,256]{1,0:T(8,128)(2,1)S(1)}, u32[]{:S(2)}, u32[]{:S(2)}) collective-permute-start(bf16[256,256]{1,0:T(8,128)(2,1)S(1)} %collective-permute-done.23.refs_1_), channel_id=1, source_target_pairs={{0,1},{1,0},{2,3},{3,2},{4,5},{5,4},{6,7},{7,6},{8,9},{9,8},{10,11... | collective-permute-start | bytes 393224 | tf_op jit(solution)/shard_map/ppermute | solution.py:261
  88.9 23.5 %collective-permute-start.12 = (bf16[256,256]{1,0:T(8,128)(2,1)S(1)}, bf16[256,256]{1,0:T(8,128)(2,1)S(1)}, u32[]{:S(2)}, u32[]{:S(2)}) collective-permute-start(bf16[256,256]{1,0:T(8,128)(2,1)S(1)} %shard_map.67.refs_0_), channel_id=1, source_target_pairs={{0,1},{1,0},{2,3},{3,2},{4,5},{5,4},{6,7},{7,6},{8,9},{9,8},{10,11... | collective-permute-start | bytes 393224 | tf_op jit(solution)/shard_map/ppermute | solution.py:261
  93.5 20.9 %collective-permute-start.13 = (bf16[256,256]{1,0:T(8,128)(2,1)S(1)}, bf16[256,256]{1,0:T(8,128)(2,1)S(1)}, u32[]{:S(2)}, u32[]{:S(2)}) collective-permute-start(bf16[256,256]{1,0:T(8,128)(2,1)S(1)} %collective-permute-done.11.refs_1_), channel_id=1, source_target_pairs={{0,1},{1,0},{2,3},{3,2},{4,5},{5,4},{6,7},{7,6},{8,9},{9,8},{10,11... | collective-permute-start | bytes 393224 | tf_op jit(solution)/shard_map/ppermute | solution.py:261
  95.2 27.7 %collective-permute-start.26 = (bf16[128,1024]{1,0:T(8,128)(2,1)S(1)}, bf16[128,1024]{1,0:T(8,128)(2,1)S(1)}, u32[]{:S(2)}, u32[]{:S(2)}) collective-permute-start(bf16[128,1024]{1,0:T(8,128)(2,1)S(1)} %get-tuple-element.36), channel_id=1, source_target_pairs={{0,12},{4,0},{8,4},{12,8},{1,13},{5,1},{9,5},{13,9},{2,14},{6,2},{... | collective-permute-start | bytes 786440 | tf_op jit(solution)/shard_map/ppermute | solution.py:258
  107.5 3.7 %collective-permute-start = (f32[4,512]{1,0:T(4,128)S(1)}, f32[4,512]{1,0:T(4,128)S(1)}, u32[]{:S(2)}, u32[]{:S(2)}) collective-permute-start(f32[4,512]{1,0:T(4,128)S(1)} %fusion.2), channel_id=1, source_target_pairs={{0,2},{1,3},{2,0},{3,1},{4,6},{5,7},{6,4},{7,5},{8,10},{9,11},{10,... | collective-permute-start | bytes 24584 | tf_op jit(solution)/shard_map/ppermute | solution.py:261
  111.2 1.2 collective-permute-start.1
  112.3 6.7 %collective-permute-start.4 = (f32[4,512]{1,0:T(4,128)S(1)}, f32[4,512]{1,0:T(4,128)S(1)}, u32[]{:S(2)}, u32[]{:S(2)}) collective-permute-start(f32[4,512]{1,0:T(4,128)S(1)} %add.45.own_ref), channel_id=1, source_target_pairs={{0,12},{4,0},{8,4},{12,8},{1,13},{5,1},{9,5},{13,9},{2,14},{6,2},{... | collective-permute-start | bytes 24584 | tf_op jit(solution)/shard_map/ppermute | solution.py:258
  112.4 6.8 %collective-permute-start.3 = (f32[4,512]{1,0:T(4,128)S(1)}, f32[4,512]{1,0:T(4,128)S(1)}, u32[]{:S(2)}, u32[]{:S(2)}) collective-permute-start(f32[4,512]{1,0:T(4,128)S(1)} %add.45.own_ref), channel_id=1, source_target_pairs={{0,8},{4,12},{8,0},{12,4},{1,9},{5,13},{9,1},{13,5},{2,10},{6,14},... | collective-permute-start | bytes 24584 | tf_op jit(solution)/shard_map/ppermute | solution.py:258
  112.4 10.5 %collective-permute-start.2 = (f32[4,512]{1,0:T(4,128)S(1)}, f32[4,512]{1,0:T(4,128)S(1)}, u32[]{:S(2)}, u32[]{:S(2)}) collective-permute-start(f32[4,512]{1,0:T(4,128)S(1)} %add.45.own_ref), channel_id=1, source_target_pairs={{0,4},{4,8},{8,12},{12,0},{1,5},{5,9},{9,13},{13,1},{2,6},{6,10},{... | collective-permute-start | bytes 24584 | tf_op jit(solution)/shard_map/ppermute | solution.py:258
  114.4 22.5 %collective-permute-start.27 = (bf16[128,1024]{1,0:T(8,128)(2,1)S(1)}, bf16[128,1024]{1,0:T(8,128)(2,1)S(1)}, u32[]{:S(2)}, u32[]{:S(2)}) collective-permute-start(bf16[128,1024]{1,0:T(8,128)(2,1)S(1)} %get-tuple-element.37), channel_id=1, source_target_pairs={{0,8},{4,12},{8,0},{12,4},{1,9},{5,13},{9,1},{13,5},{2,10},{6,14},... | collective-permute-start | bytes 786440 | tf_op jit(solution)/shard_map/ppermute | solution.py:258
  119.0 17.9 %collective-permute-start.28 = (bf16[128,1024]{1,0:T(8,128)(2,1)S(1)}, bf16[128,1024]{1,0:T(8,128)(2,1)S(1)}, u32[]{:S(2)}, u32[]{:S(2)}) collective-permute-start(bf16[128,1024]{1,0:T(8,128)(2,1)S(1)} %get-tuple-element.38), channel_id=1, source_target_pairs={{0,4},{4,8},{8,12},{12,0},{1,5},{5,9},{9,13},{13,1},{2,6},{6,10},{... | collective-permute-start | bytes 786440 | tf_op jit(solution)/shard_map/ppermute | solution.py:258
  119.1 18.5 %collective-permute-start.14 = (bf16[128,1024]{1,0:T(8,128)(2,1)S(1)}, bf16[128,1024]{1,0:T(8,128)(2,1)S(1)}, u32[]{:S(2)}, u32[]{:S(2)}) collective-permute-start(bf16[128,1024]{1,0:T(8,128)(2,1)S(1)} %get-tuple-element.28), channel_id=1, source_target_pairs={{0,12},{4,0},{8,4},{12,8},{1,13},{5,1},{9,5},{13,9},{2,14},{6,2},{... | collective-permute-start | bytes 786440 | tf_op jit(solution)/shard_map/ppermute | solution.py:258
  122.9 34.1 %collective-permute-start.15 = (bf16[128,1024]{1,0:T(8,128)(2,1)S(1)}, bf16[128,1024]{1,0:T(8,128)(2,1)S(1)}, u32[]{:S(2)}, u32[]{:S(2)}) collective-permute-start(bf16[128,1024]{1,0:T(8,128)(2,1)S(1)} %get-tuple-element.29), channel_id=1, source_target_pairs={{0,8},{4,12},{8,0},{12,4},{1,9},{5,13},{9,1},{13,5},{2,10},{6,14},... | collective-permute-start | bytes 786440 | tf_op jit(solution)/shard_map/ppermute | solution.py:258
  122.9 34.1 %collective-permute-start.16 = (bf16[128,1024]{1,0:T(8,128)(2,1)S(1)}, bf16[128,1024]{1,0:T(8,128)(2,1)S(1)}, u32[]{:S(2)}, u32[]{:S(2)}) collective-permute-start(bf16[128,1024]{1,0:T(8,128)(2,1)S(1)} %get-tuple-element.30), channel_id=1, source_target_pairs={{0,4},{4,8},{8,12},{12,0},{1,5},{5,9},{9,13},{13,1},{2,6},{6,10},{... | collective-permute-start | bytes 786440 | tf_op jit(solution)/shard_map/ppermute | solution.py:258
  (14 other events, 22.9 us)

commit v2 on v1

v2 whole, which is shorter than its diff:
```python
import functools

import jax
import jax.numpy as jnp
from jax import lax
from jax.experimental import pallas as pl
from jax.experimental.pallas import tpu as pltpu
from jax.sharding import PartitionSpec as P

BATCHES = 2
F32 = jnp.float32
BF16 = jnp.bfloat16
I32 = jnp.int32
VMEM_LIMIT = 24 * 1024 * 1024


def whole(count):
    return [pl.BlockSpec(memory_space=pltpu.VMEM)] * count


def apart(count):
    return [pl.BlockSpec(memory_space=pl.ANY)] * count


def smem():
    return pl.BlockSpec(memory_space=pltpu.SMEM)


def params():
    return pltpu.CompilerParams(vmem_limit_bytes=VMEM_LIMIT)


def dot(a, b):
    return jnp.dot(a, b, preferred_element_type=F32)


def start_all(sources, targets, sems):
    copies = [pltpu.make_async_copy(a, b, sems.at[i]) for i, (a, b) in enumerate(zip(sources, targets))]
    for copy in copies:
        copy.start()
    return copies


def code_kernel(experts, depth, place_ref, picks_ref, router_ref, tokens_ref, code_ref, logits_ref, *refs):
    sends = refs[:experts]
    held, staged, in_sems, out_sems = refs[experts:]
    load = start_all([tokens_ref], [held], in_sems)[0]
    me = place_ref[0]
    rows, width = held.shape
    capacity = picks_ref.shape[1]
    strips = rows // 128
    lanes = lax.broadcasted_iota(I32, (128, capacity), 0)
    strip_ids = lax.broadcasted_iota(I32, (8, capacity), 0)
    upper = (lax.broadcasted_iota(I32, (128, 128), 0) < lax.broadcasted_iota(I32, (128, 128), 1)).astype(BF16)
    before = (lax.broadcasted_iota(I32, (8, 8), 1) < lax.broadcasted_iota(I32, (8, 8), 0)).astype(BF16)
    ones = jnp.ones((128, 128), BF16)
    code_rows = []
    for shift in range(experts):
        expert = lax.rem(me + shift, experts)
        chosen = picks_ref[pl.ds(expert, 1), :]
        local = chosen - me * rows
        start = jnp.sum((local < 0).astype(F32)).astype(I32)
        strip = lax.shift_right_arithmetic(local, 7)
        place = jnp.bitwise_and(local, 127)
        high = (strip == strip_ids).astype(BF16)
        high = jnp.where(strip_ids < strips, high, jnp.zeros_like(high))
        low = (place == lanes).astype(BF16)
        mask = lax.dot_general(high, low, (((1,), (1,)), ((), ())), preferred_element_type=F32)
        mask16 = mask.astype(BF16)
        totals = dot(mask16, ones)
        rank = (dot(mask16, upper) + dot(before, totals.astype(BF16))).astype(I32)
        batch = lax.rem(rank + start, BATCHES)
        slot = batch * depth + lax.div(rank, BATCHES)
        code = jnp.where(mask > 0.5, slot, -1)
        row = jnp.concatenate([code[i : i + 1] for i in range(strips)], axis=1)
        code_ref[pl.ds(shift, 1), :] = row
        code_rows.append(row)
    load.wait()
    logits_ref[...] = lax.dot_general(
        router_ref[...], held[...], (((1,), (1,)), ((), ())), preferred_element_type=F32
    )
    pack(0, depth, code_rows, held, staged, sends, out_sems)


def pack(k, depth, code_rows, held, staged, sends, sems):
    slot_ids = lax.broadcasted_iota(I32, (depth, held.shape[0]), 0) + k * depth
    copies = []
    for shift in list(range(1, len(sends))) + [0]:
        selector = (slot_ids == code_rows[shift]).astype(F32).astype(BF16)
        staged[shift] = dot(selector, held[...]).astype(BF16)
        copy = pltpu.make_async_copy(staged.at[shift], sends[shift], sems.at[shift])
        copy.start()
        copies.append(copy)
    for copy in copies:
        copy.wait()


def first_batch(place, picks, router, tokens, depth):
    rows, width = tokens.shape
    experts = picks.shape[0]
    out = pl.pallas_call(
        functools.partial(code_kernel, experts, depth),
        out_shape=[jax.ShapeDtypeStruct((experts, rows), I32), jax.ShapeDtypeStruct((experts, rows), F32)]
        + [jax.ShapeDtypeStruct((depth, width), BF16)] * experts,
        in_specs=[smem()] + whole(2) + apart(1),
        out_specs=whole(2) + apart(experts),
        scratch_shapes=[
            pltpu.VMEM((rows, width), BF16),
            pltpu.VMEM((experts, depth, width), BF16),
            pltpu.SemaphoreType.DMA((1,)),
            pltpu.SemaphoreType.DMA((experts,)),
        ],
        compiler_params=params(),
    )(place, picks, router, tokens)
    return out[0], out[1], out[2:]


def pack_kernel(experts, depth, k, code_ref, tokens_ref, *refs):
    sends = refs[:experts]
    held, staged, in_sems, out_sems = refs[experts:]
    start_all([tokens_ref], [held], in_sems)[0].wait()
    code_rows = [code_ref[pl.ds(shift, 1), :] for shift in range(experts)]
    pack(k, depth, code_rows, held, staged, sends, out_sems)


def later_batch(code, tokens, k, depth):
    rows, width = tokens.shape
    experts = code.shape[0]
    return pl.pallas_call(
        functools.partial(pack_kernel, experts, depth, k),
        out_shape=[jax.ShapeDtypeStruct((depth, width), BF16)] * experts,
        in_specs=whole(1) + apart(1),
        out_specs=apart(experts),
        scratch_shapes=[
            pltpu.VMEM((rows, width), BF16),
            pltpu.VMEM((experts, depth, width), BF16),
            pltpu.SemaphoreType.DMA((1,)),
            pltpu.SemaphoreType.DMA((experts,)),
        ],
        compiler_params=params(),
    )(code, tokens)


def compact_kernel(experts, k, offset_ref, count_ref, *refs):
    blocks, out_ref = refs[:experts], refs[experts]
    held, sems = refs[experts + 1 :]
    depth = blocks[0].shape[0]
    size = out_ref.shape[0]
    loads = start_all(blocks, [held.at[pl.ds(i * depth, depth)] for i in range(experts)], sems)
    row = lax.broadcasted_iota(I32, (size, depth), 0)
    lane = lax.broadcasted_iota(I32, (size, depth), 1)
    parts = [
        ((row - offset_ref[k, i] == lane) & (lane < count_ref[k, i])).astype(F32).astype(BF16)
        for i in range(experts)
    ]
    selector = jnp.concatenate(parts, axis=1)
    for load in loads:
        load.wait()
    out_ref[...] = dot(selector, held[...]).astype(BF16)


def compact(offsets, counts, k, blocks, size):
    experts = len(blocks)
    depth, width = blocks[0].shape
    return pl.pallas_call(
        functools.partial(compact_kernel, experts, k),
        out_shape=jax.ShapeDtypeStruct((size, width), BF16),
        in_specs=[smem(), smem()] + apart(experts),
        out_specs=whole(1)[0],
        scratch_shapes=[pltpu.VMEM((experts * depth, width), BF16), pltpu.SemaphoreType.DMA((experts,))],
        compiler_params=params(),
    )(offsets, counts, *blocks)


def hidden_kernel(parts, order_ref, gate_ref, up_ref, *refs):
    xs, out_ref = refs[:parts], refs[parts]
    gate_held, up_held, x_held, sems = refs[parts + 1 :]
    width = xs[0].shape[1]
    loads = []
    for i in range(parts):
        first = pl.multiple_of(order_ref[i] * width, width)
        copies = [
            pltpu.make_async_copy(xs[i], x_held.at[i], sems.at[3 * i]),
            pltpu.make_async_copy(gate_ref.at[0, pl.ds(first, width), :], gate_held.at[i], sems.at[3 * i + 1]),
            pltpu.make_async_copy(up_ref.at[0, pl.ds(first, width), :], up_held.at[i], sems.at[3 * i + 2]),
        ]
        for copy in copies:
            copy.start()
        loads.append(copies)
    gate = up = None
    for i in range(parts):
        for copy in loads[i]:
            copy.wait()
        x = x_held[i]
        gate_term = dot(x, gate_held[i])
        up_term = dot(x, up_held[i])
        gate = gate_term if gate is None else gate + gate_term
        up = up_term if up is None else up + up_term
    out_ref[...] = (gate * jax.nn.sigmoid(gate) * up).astype(BF16)


def hidden_units(order, gate_weight, up_weight, xs):
    parts = len(xs)
    size, width = xs[0].shape
    units = gate_weight.shape[2]
    return pl.pallas_call(
        functools.partial(hidden_kernel, parts),
        out_shape=jax.ShapeDtypeStruct((size, units), BF16),
        in_specs=[smem()] + apart(2 + parts),
        out_specs=whole(1)[0],
        scratch_shapes=[
            pltpu.VMEM((parts, width, units), BF16),
            pltpu.VMEM((parts, width, units), BF16),
            pltpu.VMEM((parts, size, width), BF16),
            pltpu.SemaphoreType.DMA((3 * parts,)),
        ],
        compiler_params=params(),
    )(order, gate_weight, up_weight, *xs)


def down_kernel(parts, experts, k, order_ref, offset_ref, count_ref, down_ref, *refs):
    hs, outs = refs[:parts], refs[parts : parts + experts]
    down_held, h_held, staged, in_sems, out_sems = refs[parts + experts :]
    size, units = hs[0].shape
    depth = outs[0].shape[0]
    loads = []
    for i in range(parts):
        first = pl.multiple_of(order_ref[i] * units, units)
        copies = [
            pltpu.make_async_copy(hs[i], h_held.at[i], in_sems.at[2 * i]),
            pltpu.make_async_copy(down_ref.at[0, pl.ds(first, units), :], down_held.at[i], in_sems.at[2 * i + 1]),
        ]
        for copy in copies:
            copy.start()
        loads.append(copies)
    row = lax.broadcasted_iota(I32, (depth, size), 0)
    lane = lax.broadcasted_iota(I32, (depth, size), 1)
    total = None
    for i in range(parts):
        for copy in loads[i]:
            copy.wait()
        term = dot(h_held[i], down_held[i])
        total = term if total is None else total + term
    result = total.astype(BF16)
    copies = []
    for i in list(range(1, experts)) + [0]:
        pick = ((lane - offset_ref[k, i] == row) & (row < count_ref[k, i])).astype(F32).astype(BF16)
        staged[i] = dot(pick, result).astype(BF16)
        copy = pltpu.make_async_copy(staged.at[i], outs[i], out_sems.at[i])
        copy.start()
        copies.append(copy)
    for copy in copies:
        copy.wait()


def down_rows(order, offsets, counts, k, down_weight, hs, experts, depth):
    parts = len(hs)
    size, units = hs[0].shape
    width = down_weight.shape[2]
    return pl.pallas_call(
        functools.partial(down_kernel, parts, experts, k),
        out_shape=[jax.ShapeDtypeStruct((depth, width), BF16)] * experts,
        in_specs=[smem()] * 3 + apart(1 + parts),
        out_specs=apart(experts),
        scratch_shapes=[
            pltpu.VMEM((parts, units, width), BF16),
            pltpu.VMEM((parts, size, units), BF16),
            pltpu.VMEM((experts, depth, width), BF16),
            pltpu.SemaphoreType.DMA((2 * parts,)),
            pltpu.SemaphoreType.DMA((experts,)),
        ],
        compiler_params=params(),
    )(order, offsets, counts, down_weight, *hs)


def weight_kernel(experts, place_ref, own_ref, logits_ref, code_ref, out_ref, score_ref):
    me = place_ref[0]
    kernel = jnp.exp(logits_ref[...])
    row_scale = jnp.ones((kernel.shape[0], 1, kernel.shape[2]), F32)
    for sweep in range(3):
        column = jnp.sum(jnp.sum(kernel * row_scale, axis=0, keepdims=True), axis=2, keepdims=True)
        column_scale = 1.0 / column
        row_scale = 1.0 / jnp.sum(kernel * column_scale, axis=1, keepdims=True)
    own = jnp.exp(own_ref[...])
    column_scale = column_scale[0]
    own_scale = 1.0 / jnp.sum(own * column_scale, axis=0, keepdims=True)
    score_ref[...] = own_scale * own * column_scale
    picked = []
    for shift in range(experts):
        score = score_ref[pl.ds(lax.rem(me + shift, experts), 1), :]
        picked.append(jnp.where(code_ref[pl.ds(shift, 1), :] >= 0, score, 0.0))
    total = picked[0]
    for one in picked[1:]:
        total = total + one
    total = jnp.maximum(total, 1.0 / experts)
    for shift in range(experts):
        out_ref[pl.ds(shift, 1), :] = picked[shift] / total


def slot_weights(place, own, logits, code):
    experts, rows = own.shape
    return pl.pallas_call(
        functools.partial(weight_kernel, experts),
        out_shape=jax.ShapeDtypeStruct((experts, rows), F32),
        in_specs=[smem()] + whole(3),
        out_specs=whole(1)[0],
        scratch_shapes=[pltpu.VMEM((experts, rows), F32)],
        compiler_params=params(),
    )(place, own, logits, code)


def combine_kernel(experts, k, code_ref, weight_ref, *refs):
    count = experts + (k > 0)
    blocks, out_ref = refs[:count], refs[count]
    held, sems = refs[count + 1], refs[count + 2]
    depth = blocks[0].shape[0]
    rows = code_ref.shape[1]
    targets = [held.at[pl.ds(i * depth, depth)] for i in range(experts)]
    if k > 0:
        targets.append(refs[count + 3])
    loads = start_all(blocks, targets, sems)
    slot_ids = lax.broadcasted_iota(I32, (depth, rows), 0) + k * depth
    parts = [
        jnp.where(slot_ids == code_ref[pl.ds(i, 1), :], weight_ref[pl.ds(i, 1), :], 0.0).astype(BF16)
        for i in range(experts)
    ]
    spread = jnp.concatenate(parts, axis=0)
    for load in loads:
        load.wait()
    total = lax.dot_general(spread, held[...], (((0,), (0,)), ((), ())), preferred_element_type=F32)
    if k > 0:
        total = total + refs[count + 3][...]
    out_ref[...] = total.astype(out_ref.dtype)


def combine(code, weights, k, blocks, so_far):
    experts = len(blocks)
    depth, width = blocks[0].shape
    rows = code.shape[1]
    last = k == BATCHES - 1
    more = [] if so_far is None else [so_far]
    return pl.pallas_call(
        functools.partial(combine_kernel, experts, k),
        out_shape=jax.ShapeDtypeStruct((rows, width), BF16 if last else F32),
        in_specs=whole(2) + apart(experts + len(more)),
        out_specs=whole(1)[0],
        scratch_shapes=[
            pltpu.VMEM((experts * depth, width), BF16),
            pltpu.SemaphoreType.DMA((experts + len(more),)),
        ]
        + [pltpu.VMEM((rows, width), F32)] * len(more),
        compiler_params=params(),
    )(code, weights, *blocks, *more)


def after(value, *first):
    return lax.optimization_barrier((value, first))[0]


def shards(tokens, router_weight, gate_weight, up_weight, down_weight, picks):
    experts = lax.axis_size("expert")
    width_parts = lax.axis_size("dp")
    me = lax.axis_index("expert")
    part = lax.axis_index("dp")
    rows = tokens.shape[0]
    capacity = picks.shape[1]
    depth = 2 * capacity // experts // BATCHES
    size = capacity // BATCHES
    place = me.astype(I32).reshape(1)

    def along_expert(x, shift):
        return lax.ppermute(x, "expert", [(i, (i + shift) % experts) for i in range(experts)])

    def swap(x, bit):
        return lax.ppermute(x, "dp", [(i, i ^ bit) for i in range(width_parts)])

    bits = []
    bit = width_parts // 2
    while bit:
        bits.append(bit)
        bit //= 2
    masks = [0]
    for bit in bits:
        masks = masks + [m ^ bit for m in masks]
    order = jnp.stack([part ^ m for m in masks]).astype(I32)

    def all_parts(x):
        held = [x]
        for bit in bits:
            held = held + [swap(h, bit) for h in held]
        return held

    code, logits, sends = first_batch(place, picks, router_weight.T, tokens, depth)
    gathered = jnp.stack([logits] + [along_expert(logits, shift) for shift in range(1, experts)])
    sends = [[sends[0]] + [after(block, logits) for block in sends[1:]]]
    arrived = [[sends[0][0]] + [along_expert(sends[0][shift], shift) for shift in range(1, experts)]]
    for k in range(1, BATCHES):
        blocks = later_batch(code, tokens, k, depth)
        arrived.append(
            [blocks[0]]
            + [along_expert(after(blocks[shift], arrived[k - 1][shift]), shift) for shift in range(1, experts)]
        )
    for bit in bits:
        gathered = gathered + swap(gathered, bit)
    weights = slot_weights(place, gathered[0], gathered, code)

    own_picks = lax.dynamic_slice_in_dim(picks, me, 1, axis=0)
    sources = lax.rem(me - jnp.arange(experts, dtype=I32) + experts, experts)
    start = jnp.sum((own_picks < (sources * rows)[:, None]).astype(I32), axis=1)
    stop = jnp.sum((own_picks < ((sources + 1) * rows)[:, None]).astype(I32), axis=1)
    ids = jnp.arange(BATCHES, dtype=I32)[:, None]
    offsets = (start[None, :] + (BATCHES - 1) - ids) // BATCHES
    counts = (stop[None, :] + (BATCHES - 1) - ids) // BATCHES - offsets
    offsets, counts, order = after((offsets, counts, order), code)

    total = None
    results = []
    for k in range(BATCHES):
        if k == 0:
            blocks = after(arrived[0], weights)
        else:
            blocks = after(arrived[k], results)
        block = compact(offsets, counts, k, blocks, size)
        hidden = hidden_units(order, gate_weight, up_weight, all_parts(block))
        results = down_rows(order, offsets, counts, k, down_weight, all_parts(hidden), experts, depth)
        returned = [results[0]] + [along_expert(results[shift], -shift) for shift in range(1, experts)]
        total = combine(code, weights, k, returned, total)
    return total


def solution(mesh):
    return jax.shard_map(
        shards,
        mesh=mesh,
        in_specs=(
            P(("groups", "expert"), "dp"),
            P("dp", None),
            P("expert", None, "dp"),
            P("expert", None, "dp"),
            P("expert", None, "dp"),
            P("groups", None),
        ),
        out_specs=P(("groups", "expert"), "dp"),
        check_vma=False,
    )
```

time: 159 us -> 156 us (0.981)
  waiting for transfers between devices: 87.8 us -> 101 us
  starting transfers between devices: 37.7 us -> 25.6 us
  local copies, waits for them, and re-layouts: 11 us -> 6.3 us
    ppermute x14, waiting for transfers between devices: 23.1 us -> 35.8 us  [swap(): return lax.ppermute(x, 'dp', [(i, i ^ bit) for i in range(width_parts)])]
    ppermute x15, starting transfers between devices: 30.8 us -> 19.1 us  [along_expert(): lax.ppermute(x, 'expert', [(i, (i + shift) % experts) for i in range(expe...]
    unnamed x34 -> x16, local copies, waits for them, and re-layouts: 11 us -> 5.59 us
    pallas_call x2, Pallas kernels: 3.38 us -> 6.66 us  [down_rows(): pl.pallas_call(functools.partial(down_kernel, parts, experts, k), out_sha...]
    pallas_call x5 -> x6, Pallas kernels: 15.3 us -> 13 us  [the longest x2 5.14 us: hidden_units(): pl.pallas_call(functools.partial(hidden_kernel, parts), out_shape=jax.Sha...]
  transfers between devices with their start and end apart: 29 -> 29, of which waited for: 10 -> 14; matrix products, arithmetic and copies ran while one was open for 0% -> 1% of each run, Pallas kernels for 10% -> 6%
where the time goes in v2:
time: 156 us
  waiting for transfers between devices  101 us (65%)
  starting transfers between devices  25.6 us (16%)
  Pallas kernels  22.3 us (14%)
  local copies, waits for them, and re-layouts  6.3 us (4%)
    ppermute x15, waiting for transfers between devices, along_expert(): lax.ppermute(x, 'expert', [(i, (i + shift) % experts) for i in range(expe...  65.2 us
    ppermute x14, waiting for transfers between devices, swap(): return lax.ppermute(x, 'dp', [(i, i ^ bit) for i in range(width_parts)])  35.8 us
    ppermute x15, starting transfers between devices, along_expert(): lax.ppermute(x, 'expert', [(i, (i + shift) % experts) for i in range(expe...  19.1 us
    pallas_call x2, Pallas kernels, down_rows(): pl.pallas_call(functools.partial(down_kernel, parts, experts, k), out_sha...  6.66 us
    ppermute x14, starting transfers between devices, swap(): return lax.ppermute(x, 'dp', [(i, i ^ bit) for i in range(width_parts)])  6.48 us
    unnamed x16, local copies, waits for them, and re-layouts  5.59 us
    pallas_call x2, Pallas kernels, hidden_units(): pl.pallas_call(functools.partial(hidden_kernel, parts), out_shape=jax.Sha...  5.14 us
    pallas_call x1, Pallas kernels, first_batch(): pl.pallas_call(functools.partial(code_kernel, experts, depth), out_shape=...  3.29 us
  transfers between devices with their start and end apart: 29, of which 14 were waited for; matrix products, arithmetic and copies ran while one was open for 1% of the time, Pallas kernels for 6%

profile of v2, /device:TPU:0, one launch (start us, length us, event | category | flops | bytes accessed | tf_op | source)
XLA Modules:
  0.0 155.8 jit_solution(8384298286845295475)
XLA Ops:
  0.0 1.4 copy-done.4
  2.8 3.3 %shard_map.64 = (s32[4,512]{1,0:T(4,128)S(1)}, f32[4,512]{1,0:T(4,128)S(1)}, bf16[128,1024]{1,0:T(8,128)(2,1)S(1)}, bf16[128,1024]{1,0:T(8,128)(2,1)S(1)}, bf16[...) custom-call(s32[1]{0:T(128)} %bitcast.place_ref, s32[4,512]{1,0:T(4,128)S(1)} %copy-done.6, bf16[4,1024]{1,0:T(4,128)(2,1)S(1)} %bitcast.16, ...), custom_call_target="tpu_custom_call" | custom-call | tf_op jit(solution)/shard_map/pallas_call | solution.py:101
  6.1 5.1 %collective-permute-start.2 = (f32[4,512]{1,0:T(4,128)S(1)}, f32[4,512]{1,0:T(4,128)S(1)}, u32[]{:S(2)}, u32[]{:S(2)}) collective-permute-start(f32[4,512]{1,0:T(4,128)S(1)} %get-tuple-element.41), channel_id=1, source_target_pairs={{0,12},{4,0},{8,4},{12,8},{1,13},{5,1},{9,5},{13,9},{2,14},{6,2},{... | collective-permute-start | bytes 24584 | tf_op jit(solution)/shard_map/ppermute | solution.py:372
  12.2 2.8 %collective-permute-start.9 = (bf16[128,1024]{1,0:T(8,128)(2,1)}, bf16[128,1024]{1,0:T(8,128)(2,1)S(1)}, u32[]{:S(2)}, u32[]{:S(2)}) collective-permute-start(bf16[128,1024]{1,0:T(8,128)(2,1)} %get-tuple-element.56), channel_id=1, source_target_pairs={{0,12},{4,0},{8,4},{12,8},{1,13},{5,1},{9,5},{13,9},{2,14},{6,2},{... | collective-permute-start | bytes 786440 | tf_op jit(solution)/shard_map/ppermute | solution.py:372
  15.0 1.1 collective-permute-start.7
  17.2 1.6 collective-permute-start.3
  18.8 2.4 %collective-permute-done.3 = f32[4,4,512]{2,1,0:T(4,128)S(1)} collective-permute-done((f32[4,4,512]{2,1,0:T(4,128)S(1)}, f32[4,4,512]{2,1,0:T(4,128)S(1)}, u32[]{:S(2)}, u32[]{:S(2)}) %collective-permute-start.3) | collective-permute-done | bytes 32800 | tf_op jit(solution)/shard_map/ppermute | solution.py:375
  21.3 1.1 collective-permute-done.4
  22.9 15.6 %collective-permute-done.7.refs_2_ = bf16[128,1024]{1,0:T(8,128)(2,1)S(1)} collective-permute-done((bf16[128,1024]{1,0:T(8,128)(2,1)}, bf16[128,1024]{1,0:T(8,128)(2,1)S(1)}, u32[]{:S(2)}, u32[]{:S(2)}) %collective-permute-start.7) | collective-permute-done | bytes 262176 | tf_op jit(solution)/shard_map/ppermute | solution.py:372
  38.5 1.2 shard_map.67.refs_0_
  39.6 1.6 collective-permute-start.11
  41.2 10.5 %collective-permute-done.11.refs_1_ = bf16[256,1024]{1,0:T(8,128)(2,1)S(1)} collective-permute-done((bf16[256,1024]{1,0:T(8,128)(2,1)S(1)}, bf16[256,1024]{1,0:T(8,128)(2,1)S(1)}, u32[]{:S(2)}, u32[]{:S(2)}) %collective-permute-start.11) | collective-permute-done | bytes 524320 | tf_op jit(solution)/shard_map/ppermute | solution.py:375
  51.7 1.2 copy-done.5
  52.9 1.5 shard_map.66
  54.4 1.6 %copy-done.1 = bf16[1,4096,256]{2,1,0:T(8,128)(2,1)S(1)} copy-done((bf16[1,4096,256]{2,1,0:T(8,128)(2,1)S(1)}, bf16[1,4096,256]{2,1,0:T(8,128)(2,1)}, u32[]{:S(2)}) %copy-start.1) | copy-done | bytes 2097176
  56.0 2.6 %shard_map.68.refs_0_ = bf16[256,256]{1,0:T(8,128)(2,1)S(1)} custom-call(s32[4]{0:T(128)S(1)} %pad_add_fusion.order_ref, bf16[1,4096,256]{2,1,0:T(8,128)(2,1)S(1)} %copy-done, bf16[1,4096,256]{2,1,0:T(8,128)(2,1)S(1)} %copy-done.1, bf16[256,1024]{1,0:T(8,128)(2,1)S(1)} %shard_map.67.refs_0_, bf16[256,1024]{1,0:T(8,128)(2,1)S(1)} %collective-permute-done.11.refs_1_, ...), custom_call_target="tpu_custom_call" | custom-call | tf_op jit(solution)/shard_map/pallas_call | solution.py:206
  58.6 1.6 collective-permute-start.14
  60.1 2.8 %collective-permute-start.8 = (bf16[128,1024]{1,0:T(8,128)(2,1)S(1)}, bf16[128,1024]{1,0:T(8,128)(2,1)S(1)}, u32[]{:S(2)}, u32[]{:S(2)}) collective-permute-start(bf16[128,1024]{1,0:T(8,128)(2,1)S(1)} %get-tuple-element.53), channel_id=1, source_target_pairs={{0,8},{4,12},{8,0},{12,4},{1,9},{5,13},{9,1},{13,5},{2,10},{6,14},... | collective-permute-start | bytes 786440 | tf_op jit(solution)/shard_map/ppermute | solution.py:372
  62.9 2.0 %collective-permute-start.6 = (bf16[128,1024]{1,0:T(8,128)(2,1)S(1)}, bf16[128,1024]{1,0:T(8,128)(2,1)S(1)}, u32[]{:S(2)}, u32[]{:S(2)}) collective-permute-start(bf16[128,1024]{1,0:T(8,128)(2,1)S(1)} %get-tuple-element.49), channel_id=1, source_target_pairs={{0,4},{4,8},{8,12},{12,0},{1,5},{5,9},{9,13},{13,1},{2,6},{6,10},{... | collective-permute-start | bytes 786440 | tf_op jit(solution)/shard_map/ppermute | solution.py:372
  66.5 3.3 %shard_map.69 = (bf16[128,1024]{1,0:T(8,128)(2,1)S(1)}, bf16[128,1024]{1,0:T(8,128)(2,1)S(1)}, bf16[128,1024]{1,0:T(8,128)(2,1)S(1)}, bf16[128,1024]{1,0:T(8,128)(2,1)S(1)}) custom-call(s32[4]{0:T(128)S(1)} %pad_add_fusion.order_ref, s32[2,4]{1,0:T(2,128)S(1)} %get-tuple-element.43.offset_ref, s32[2,4]{1,0:T(2,128)S(1)} %get-tuple-element.44.count_ref, ...), custom_call_target="tpu_custom_call" | custom-call | tf_op jit(solution)/shard_map/pallas_call | solution.py:260
  69.8 16.6 %collective-permute-done.8.refs_2_ = bf16[128,1024]{1,0:T(8,128)(2,1)S(1)} collective-permute-done((bf16[128,1024]{1,0:T(8,128)(2,1)S(1)}, bf16[128,1024]{1,0:T(8,128)(2,1)S(1)}, u32[]{:S(2)}, u32[]{:S(2)}) %collective-permute-start.8) | collective-permute-done | bytes 262176 | tf_op jit(solution)/shard_map/ppermute | solution.py:372
  86.4 1.2 shard_map.70.refs_0_
  88.2 13.0 %collective-permute-done.17.refs_1_ = bf16[256,1024]{1,0:T(8,128)(2,1)S(1)} collective-permute-done((bf16[256,1024]{1,0:T(8,128)(2,1)S(1)}, bf16[256,1024]{1,0:T(8,128)(2,1)S(1)}, u32[]{:S(2)}, u32[]{:S(2)}) %collective-permute-start.17) | collective-permute-done | bytes 524320 | tf_op jit(solution)/shard_map/ppermute | solution.py:375
  101.2 1.9 %collective-permute-done.19.refs_3_ = bf16[256,1024]{1,0:T(8,128)(2,1)S(1)} collective-permute-done((bf16[256,1024]{1,0:T(8,128)(2,1)S(1)}, bf16[256,1024]{1,0:T(8,128)(2,1)S(1)}, u32[]{:S(2)}, u32[]{:S(2)}) %collective-permute-start.19) | collective-permute-done | bytes 524320 | tf_op jit(solution)/shard_map/ppermute | solution.py:375
  103.1 2.6 %shard_map.71.refs_0_ = bf16[256,256]{1,0:T(8,128)(2,1)S(1)} custom-call(s32[4]{0:T(128)S(1)} %pad_add_fusion.order_ref, bf16[1,4096,256]{2,1,0:T(8,128)(2,1)S(1)} %copy-done, bf16[1,4096,256]{2,1,0:T(8,128)(2,1)S(1)} %copy-done.2, bf16[256,1024]{1,0:T(8,128)(2,1)S(1)} %shard_map.70.refs_0_, bf16[256,1024]{1,0:T(8,128)(2,1)S(1)} %collective-permute-done.17.refs_1_, ...), custom_call_target="tpu_custom_call" | custom-call | tf_op jit(solution)/shard_map/pallas_call | solution.py:206
  106.3 5.0 %collective-permute-done.20.refs_1_ = bf16[256,256]{1,0:T(8,128)(2,1)S(1)} collective-permute-done((bf16[256,256]{1,0:T(8,128)(2,1)S(1)}, bf16[256,256]{1,0:T(8,128)(2,1)S(1)}, u32[]{:S(2)}, u32[]{:S(2)}) %collective-permute-start.20) | collective-permute-done | bytes 131104 | tf_op jit(solution)/shard_map/ppermute | solution.py:375
  112.7 3.3 %shard_map.72 = (bf16[128,1024]{1,0:T(8,128)(2,1)S(1)}, bf16[128,1024]{1,0:T(8,128)(2,1)S(1)}, bf16[128,1024]{1,0:T(8,128)(2,1)S(1)}, bf16[128,1024]{1,0:T(8,128)(2,1)S(1)}) custom-call(s32[4]{0:T(128)S(1)} %pad_add_fusion.order_ref, s32[2,4]{1,0:T(2,128)S(1)} %get-tuple-element.43.offset_ref, s32[2,4]{1,0:T(2,128)S(1)} %get-tuple-element.44.count_ref, ...), custom_call_target="tpu_custom_call" | custom-call | tf_op jit(solution)/shard_map/pallas_call | solution.py:260
  116.0 3.0 %collective-permute-start.23 = (bf16[128,1024]{1,0:T(8,128)(2,1)S(1)}, bf16[128,1024]{1,0:T(8,128)(2,1)S(1)}, u32[]{:S(2)}, u32[]{:S(2)}) collective-permute-start(bf16[128,1024]{1,0:T(8,128)(2,1)S(1)} %get-tuple-element.72), channel_id=1, source_target_pairs={{0,12},{4,0},{8,4},{12,8},{1,13},{5,1},{9,5},{13,9},{2,14},{6,2},{... | collective-permute-start | bytes 786440 | tf_op jit(solution)/shard_map/ppermute | solution.py:372
  119.7 12.5 %collective-permute-done.27.refs_2_ = bf16[128,1024]{1,0:T(8,128)(2,1)S(1)} collective-permute-done((bf16[128,1024]{1,0:T(8,128)(2,1)S(1)}, bf16[128,1024]{1,0:T(8,128)(2,1)S(1)}, u32[]{:S(2)}, u32[]{:S(2)}) %collective-permute-start.27) | collective-permute-done | bytes 262176 | tf_op jit(solution)/shard_map/ppermute | solution.py:372
  133.2 2.5 %collective-permute-done.23.refs_1_ = bf16[128,1024]{1,0:T(8,128)(2,1)S(1)} collective-permute-done((bf16[128,1024]{1,0:T(8,128)(2,1)S(1)}, bf16[128,1024]{1,0:T(8,128)(2,1)S(1)}, u32[]{:S(2)}, u32[]{:S(2)}) %collective-permute-start.23) | collective-permute-done | bytes 262176 | tf_op jit(solution)/shard_map/ppermute | solution.py:372
  135.8 17.9 %collective-permute-done.24.refs_2_ = bf16[128,1024]{1,0:T(8,128)(2,1)S(1)} collective-permute-done((bf16[128,1024]{1,0:T(8,128)(2,1)S(1)}, bf16[128,1024]{1,0:T(8,128)(2,1)S(1)}, u32[]{:S(2)}, u32[]{:S(2)}) %collective-permute-start.24) | collective-permute-done | bytes 262176 | tf_op jit(solution)/shard_map/ppermute | solution.py:372
  153.7 2.1 %shard_map.74 = bf16[512,1024]{1,0:T(8,128)(2,1)} custom-call(s32[4,512]{1,0:T(4,128)S(1)} %get-tuple-element.40.code_ref, f32[4,512]{1,0:T(4,128)S(1)} %shard_map.65.weight_ref, bf16[128,1024]{1,0:T(8,128)(2,1)S(1)} %get-tuple-element.71.refs_0_, bf16[128,1024]{1,0:T(8,128)(2,1)S(1)} %collective-permute-done.23.refs_1_, ...), custom_call_target="tpu_custom_call" | custom-call | tf_op jit(solution)/shard_map/pallas_call | solution.py:342
  (64 shorter events, 9.8 us)
Async XLA Ops:
  0.0 54.4 %copy-start = (bf16[1,4096,256]{2,1,0:T(8,128)(2,1)S(1)}, bf16[1,4096,256]{2,1,0:T(8,128)(2,1)}, u32[]{:S(2)}) copy-start(bf16[1,4096,256]{2,1,0:T(8,128)(2,1)} %gate_ref.3) | copy-start | bytes 6291460
  6.1 11.0 %collective-permute-start.2 = (f32[4,512]{1,0:T(4,128)S(1)}, f32[4,512]{1,0:T(4,128)S(1)}, u32[]{:S(2)}, u32[]{:S(2)}) collective-permute-start(f32[4,512]{1,0:T(4,128)S(1)} %get-tuple-element.41), channel_id=1, source_target_pairs={{0,12},{4,0},{8,4},{12,8},{1,13},{5,1},{9,5},{13,9},{2,14},{6,2},{... | collective-permute-start | bytes 24584 | tf_op jit(solution)/shard_map/ppermute | solution.py:372
  11.2 6.0 %collective-permute-start.1 = (f32[4,512]{1,0:T(4,128)S(1)}, f32[4,512]{1,0:T(4,128)S(1)}, u32[]{:S(2)}, u32[]{:S(2)}) collective-permute-start(f32[4,512]{1,0:T(4,128)S(1)} %get-tuple-element.41), channel_id=1, source_target_pairs={{0,8},{4,12},{8,0},{12,4},{1,9},{5,13},{9,1},{13,5},{2,10},{6,14},... | collective-permute-start | bytes 24584 | tf_op jit(solution)/shard_map/ppermute | solution.py:372
  11.2 6.0 %collective-permute-start = (f32[4,512]{1,0:T(4,128)S(1)}, f32[4,512]{1,0:T(4,128)S(1)}, u32[]{:S(2)}, u32[]{:S(2)}) collective-permute-start(f32[4,512]{1,0:T(4,128)S(1)} %get-tuple-element.41), channel_id=1, source_target_pairs={{0,4},{4,8},{8,12},{12,0},{1,5},{5,9},{9,13},{13,1},{2,6},{6,10},{... | collective-permute-start | bytes 24584 | tf_op jit(solution)/shard_map/ppermute | solution.py:372
  12.2 10.7 %collective-permute-start.9 = (bf16[128,1024]{1,0:T(8,128)(2,1)}, bf16[128,1024]{1,0:T(8,128)(2,1)S(1)}, u32[]{:S(2)}, u32[]{:S(2)}) collective-permute-start(bf16[128,1024]{1,0:T(8,128)(2,1)} %get-tuple-element.56), channel_id=1, source_target_pairs={{0,12},{4,0},{8,4},{12,8},{1,13},{5,1},{9,5},{13,9},{2,14},{6,2},{... | collective-permute-start | bytes 786440 | tf_op jit(solution)/shard_map/ppermute | solution.py:372
  15.0 23.5 %collective-permute-start.7 = (bf16[128,1024]{1,0:T(8,128)(2,1)}, bf16[128,1024]{1,0:T(8,128)(2,1)S(1)}, u32[]{:S(2)}, u32[]{:S(2)}) collective-permute-start(bf16[128,1024]{1,0:T(8,128)(2,1)} %get-tuple-element.52), channel_id=1, source_target_pairs={{0,8},{4,12},{8,0},{12,4},{1,9},{5,13},{9,1},{13,5},{2,10},{6,14},... | collective-permute-start | bytes 786440 | tf_op jit(solution)/shard_map/ppermute | solution.py:372
  17.1 21.4 %collective-permute-start.5 = (bf16[128,1024]{1,0:T(8,128)(2,1)S(1)}, bf16[128,1024]{1,0:T(8,128)(2,1)S(1)}, u32[]{:S(2)}, u32[]{:S(2)}) collective-permute-start(bf16[128,1024]{1,0:T(8,128)(2,1)S(1)} %get-tuple-element.48), channel_id=1, source_target_pairs={{0,4},{4,8},{8,12},{12,0},{1,5},{5,9},{9,13},{13,1},{2,6},{6,10},{... | collective-permute-start | bytes 786440 | tf_op jit(solution)/shard_map/ppermute | solution.py:372
  17.2 4.0 %collective-permute-start.3 = (f32[4,4,512]{2,1,0:T(4,128)S(1)}, f32[4,4,512]{2,1,0:T(4,128)S(1)}, u32[]{:S(2)}, u32[]{:S(2)}) collective-permute-start(f32[4,4,512]{2,1,0:T(4,128)S(1)} %pad_maximum_fusion), channel_id=1, source_target_pairs={{0,2},{1,3},{2,0},{3,1},{4,6},{5,7},{6,4},{7,5},{8,10},{9,11},{10,... | collective-permute-start | bytes 98312 | tf_op jit(solution)/shard_map/ppermute | solution.py:375
  21.2 1.3 collective-permute-start.4
  39.6 12.1 %collective-permute-start.11 = (bf16[256,1024]{1,0:T(8,128)(2,1)S(1)}, bf16[256,1024]{1,0:T(8,128)(2,1)S(1)}, u32[]{:S(2)}, u32[]{:S(2)}) collective-permute-start(bf16[256,1024]{1,0:T(8,128)(2,1)S(1)} %shard_map.67.refs_0_), channel_id=1, source_target_pairs={{0,2},{1,3},{2,0},{3,1},{4,6},{5,7},{6,4},{7,5},{8,10},{9,11},{10,... | collective-permute-start | bytes 1572872 | tf_op jit(solution)/shard_map/ppermute | solution.py:375
  41.2 13.2 %collective-permute-start.12 = (bf16[256,1024]{1,0:T(8,128)(2,1)S(1)}, bf16[256,1024]{1,0:T(8,128)(2,1)S(1)}, u32[]{:S(2)}, u32[]{:S(2)}) collective-permute-start(bf16[256,1024]{1,0:T(8,128)(2,1)S(1)} %shard_map.67.refs_0_), channel_id=1, source_target_pairs={{0,1},{1,0},{2,3},{3,2},{4,5},{5,4},{6,7},{7,6},{8,9},{9,8},{10,11... | collective-permute-start | bytes 1572872 | tf_op jit(solution)/shard_map/ppermute | solution.py:375
  51.7 2.7 %collective-permute-start.13 = (bf16[256,1024]{1,0:T(8,128)(2,1)S(1)}, bf16[256,1024]{1,0:T(8,128)(2,1)S(1)}, u32[]{:S(2)}, u32[]{:S(2)}) collective-permute-start(bf16[256,1024]{1,0:T(8,128)(2,1)S(1)} %collective-permute-done.11.refs_1_), channel_id=1, source_target_pairs={{0,1},{1,0},{2,3},{3,2},{4,5},{5,4},{6,7},{7,6},{8,9},{9,8},{10,11... | collective-permute-start | bytes 1572872 | tf_op jit(solution)/shard_map/ppermute | solution.py:375
  56.0 10.5 %copy-start.3 = (bf16[1,1024,1024]{2,1,0:T(8,128)(2,1)S(1)}, bf16[1,1024,1024]{2,1,0:T(8,128)(2,1)}, u32[]{:S(2)}) copy-start(bf16[1,1024,1024]{2,1,0:T(8,128)(2,1)} %down_ref.3) | copy-start | bytes 6291460
  58.6 44.6 %copy-start.2 = (bf16[1,4096,256]{2,1,0:T(8,128)(2,1)S(1)}, bf16[1,4096,256]{2,1,0:T(8,128)(2,1)}, u32[]{:S(2)}) copy-start(bf16[1,4096,256]{2,1,0:T(8,128)(2,1)} %up_ref.3) | copy-start | bytes 6291460
  58.6 6.4 %collective-permute-start.14 = (bf16[256,256]{1,0:T(8,128)(2,1)S(1)}, bf16[256,256]{1,0:T(8,128)(2,1)S(1)}, u32[]{:S(2)}, u32[]{:S(2)}) collective-permute-start(bf16[256,256]{1,0:T(8,128)(2,1)S(1)} %shard_map.68.refs_0_), channel_id=1, source_target_pairs={{0,2},{1,3},{2,0},{3,1},{4,6},{5,7},{6,4},{7,5},{8,10},{9,11},{10,... | collective-permute-start | bytes 393224 | tf_op jit(solution)/shard_map/ppermute | solution.py:375
  60.1 9.7 %collective-permute-start.10 = (bf16[128,1024]{1,0:T(8,128)(2,1)S(1)}, bf16[128,1024]{1,0:T(8,128)(2,1)S(1)}, u32[]{:S(2)}, u32[]{:S(2)}) collective-permute-start(bf16[128,1024]{1,0:T(8,128)(2,1)S(1)} %get-tuple-element.57), channel_id=1, source_target_pairs={{0,12},{4,0},{8,4},{12,8},{1,13},{5,1},{9,5},{13,9},{2,14},{6,2},{... | collective-permute-start | bytes 786440 | tf_op jit(solution)/shard_map/ppermute | solution.py:372
  60.1 26.3 %collective-permute-start.8 = (bf16[128,1024]{1,0:T(8,128)(2,1)S(1)}, bf16[128,1024]{1,0:T(8,128)(2,1)S(1)}, u32[]{:S(2)}, u32[]{:S(2)}) collective-permute-start(bf16[128,1024]{1,0:T(8,128)(2,1)S(1)} %get-tuple-element.53), channel_id=1, source_target_pairs={{0,8},{4,12},{8,0},{12,4},{1,9},{5,13},{9,1},{13,5},{2,10},{6,14},... | collective-permute-start | bytes 786440 | tf_op jit(solution)/shard_map/ppermute | solution.py:372
  62.9 23.5 %collective-permute-start.6 = (bf16[128,1024]{1,0:T(8,128)(2,1)S(1)}, bf16[128,1024]{1,0:T(8,128)(2,1)S(1)}, u32[]{:S(2)}, u32[]{:S(2)}) collective-permute-start(bf16[128,1024]{1,0:T(8,128)(2,1)S(1)} %get-tuple-element.49), channel_id=1, source_target_pairs={{0,4},{4,8},{8,12},{12,0},{1,5},{5,9},{9,13},{13,1},{2,6},{6,10},{... | collective-permute-start | bytes 786440 | tf_op jit(solution)/shard_map/ppermute | solution.py:372
  64.9 1.3 collective-permute-start.15
  64.9 1.5 collective-permute-start.16
  87.6 13.6 %collective-permute-start.17 = (bf16[256,1024]{1,0:T(8,128)(2,1)S(1)}, bf16[256,1024]{1,0:T(8,128)(2,1)S(1)}, u32[]{:S(2)}, u32[]{:S(2)}) collective-permute-start(bf16[256,1024]{1,0:T(8,128)(2,1)S(1)} %shard_map.70.refs_0_), channel_id=1, source_target_pairs={{0,2},{1,3},{2,0},{3,1},{4,6},{5,7},{6,4},{7,5},{8,10},{9,11},{10,... | collective-permute-start | bytes 1572872 | tf_op jit(solution)/shard_map/ppermute | solution.py:375
  88.2 13.0 %collective-permute-start.18 = (bf16[256,1024]{1,0:T(8,128)(2,1)S(1)}, bf16[256,1024]{1,0:T(8,128)(2,1)S(1)}, u32[]{:S(2)}, u32[]{:S(2)}) collective-permute-start(bf16[256,1024]{1,0:T(8,128)(2,1)S(1)} %shard_map.70.refs_0_), channel_id=1, source_target_pairs={{0,1},{1,0},{2,3},{3,2},{4,5},{5,4},{6,7},{7,6},{8,9},{9,8},{10,11... | collective-permute-start | bytes 1572872 | tf_op jit(solution)/shard_map/ppermute | solution.py:375
  101.2 1.9 %collective-permute-start.19 = (bf16[256,1024]{1,0:T(8,128)(2,1)S(1)}, bf16[256,1024]{1,0:T(8,128)(2,1)S(1)}, u32[]{:S(2)}, u32[]{:S(2)}) collective-permute-start(bf16[256,1024]{1,0:T(8,128)(2,1)S(1)} %collective-permute-done.17.refs_1_), channel_id=1, source_target_pairs={{0,1},{1,0},{2,3},{3,2},{4,5},{5,4},{6,7},{7,6},{8,9},{9,8},{10,11... | collective-permute-start | bytes 1572872 | tf_op jit(solution)/shard_map/ppermute | solution.py:375
  105.7 5.6 %collective-permute-start.20 = (bf16[256,256]{1,0:T(8,128)(2,1)S(1)}, bf16[256,256]{1,0:T(8,128)(2,1)S(1)}, u32[]{:S(2)}, u32[]{:S(2)}) collective-permute-start(bf16[256,256]{1,0:T(8,128)(2,1)S(1)} %shard_map.71.refs_0_), channel_id=1, source_target_pairs={{0,2},{1,3},{2,0},{3,1},{4,6},{5,7},{6,4},{7,5},{8,10},{9,11},{10,... | collective-permute-start | bytes 393224 | tf_op jit(solution)/shard_map/ppermute | solution.py:375
  106.3 13.3 %collective-permute-start.26 = (bf16[128,1024]{1,0:T(8,128)(2,1)S(1)}, bf16[128,1024]{1,0:T(8,128)(2,1)S(1)}, u32[]{:S(2)}, u32[]{:S(2)}) collective-permute-start(bf16[128,1024]{1,0:T(8,128)(2,1)S(1)} %get-tuple-element.64), channel_id=1, source_target_pairs={{0,12},{4,0},{8,4},{12,8},{1,13},{5,1},{9,5},{13,9},{2,14},{6,2},{... | collective-permute-start | bytes 786440 | tf_op jit(solution)/shard_map/ppermute | solution.py:372
  106.3 5.5 %collective-permute-start.21 = (bf16[256,256]{1,0:T(8,128)(2,1)S(1)}, bf16[256,256]{1,0:T(8,128)(2,1)S(1)}, u32[]{:S(2)}, u32[]{:S(2)}) collective-permute-start(bf16[256,256]{1,0:T(8,128)(2,1)S(1)} %shard_map.71.refs_0_), channel_id=1, source_target_pairs={{0,1},{1,0},{2,3},{3,2},{4,5},{5,4},{6,7},{7,6},{8,9},{9,8},{10,11... | collective-permute-start | bytes 393224 | tf_op jit(solution)/shard_map/ppermute | solution.py:375
  111.3 1.3 collective-permute-start.22
  111.3 20.9 %collective-permute-start.27 = (bf16[128,1024]{1,0:T(8,128)(2,1)S(1)}, bf16[128,1024]{1,0:T(8,128)(2,1)S(1)}, u32[]{:S(2)}, u32[]{:S(2)}) collective-permute-start(bf16[128,1024]{1,0:T(8,128)(2,1)S(1)} %get-tuple-element.65), channel_id=1, source_target_pairs={{0,8},{4,12},{8,0},{12,4},{1,9},{5,13},{9,1},{13,5},{2,10},{6,14},... | collective-permute-start | bytes 786440 | tf_op jit(solution)/shard_map/ppermute | solution.py:372
  111.8 20.4 %collective-permute-start.28 = (bf16[128,1024]{1,0:T(8,128)(2,1)S(1)}, bf16[128,1024]{1,0:T(8,128)(2,1)S(1)}, u32[]{:S(2)}, u32[]{:S(2)}) collective-permute-start(bf16[128,1024]{1,0:T(8,128)(2,1)S(1)} %get-tuple-element.66), channel_id=1, source_target_pairs={{0,4},{4,8},{8,12},{12,0},{1,5},{5,9},{9,13},{13,1},{2,6},{6,10},{... | collective-permute-start | bytes 786440 | tf_op jit(solution)/shard_map/ppermute | solution.py:372
  116.0 19.8 %collective-permute-start.23 = (bf16[128,1024]{1,0:T(8,128)(2,1)S(1)}, bf16[128,1024]{1,0:T(8,128)(2,1)S(1)}, u32[]{:S(2)}, u32[]{:S(2)}) collective-permute-start(bf16[128,1024]{1,0:T(8,128)(2,1)S(1)} %get-tuple-element.72), channel_id=1, source_target_pairs={{0,12},{4,0},{8,4},{12,8},{1,13},{5,1},{9,5},{13,9},{2,14},{6,2},{... | collective-permute-start | bytes 786440 | tf_op jit(solution)/shard_map/ppermute | solution.py:372
  119.0 34.6 %collective-permute-start.24 = (bf16[128,1024]{1,0:T(8,128)(2,1)S(1)}, bf16[128,1024]{1,0:T(8,128)(2,1)S(1)}, u32[]{:S(2)}, u32[]{:S(2)}) collective-permute-start(bf16[128,1024]{1,0:T(8,128)(2,1)S(1)} %get-tuple-element.73), channel_id=1, source_target_pairs={{0,8},{4,12},{8,0},{12,4},{1,9},{5,13},{9,1},{13,5},{2,10},{6,14},... | collective-permute-start | bytes 786440 | tf_op jit(solution)/shard_map/ppermute | solution.py:372
  119.7 34.0 %collective-permute-start.25 = (bf16[128,1024]{1,0:T(8,128)(2,1)S(1)}, bf16[128,1024]{1,0:T(8,128)(2,1)S(1)}, u32[]{:S(2)}, u32[]{:S(2)}) collective-permute-start(bf16[128,1024]{1,0:T(8,128)(2,1)S(1)} %get-tuple-element.74), channel_id=1, source_target_pairs={{0,4},{4,8},{8,12},{12,0},{1,5},{5,9},{9,13},{13,1},{2,6},{6,10},{... | collective-permute-start | bytes 786440 | tf_op jit(solution)/shard_map/ppermute | solution.py:372
  (5 other events, 5.6 us)

commit v3 on v2

--- a/solution.py
+++ b/solution.py
@@ -12,6 +12,7 @@
 BF16 = jnp.bfloat16
 I32 = jnp.int32
 VMEM_LIMIT = 24 * 1024 * 1024
+COST = pl.CostEstimate(flops=1024, bytes_accessed=1024, transcendentals=0)
 
 
 def whole(count):
@@ -111,6 +112,7 @@
             pltpu.SemaphoreType.DMA((experts,)),
         ],
         compiler_params=params(),
+        cost_estimate=COST,
     )(place, picks, router, tokens)
     return out[0], out[1], out[2:]
 
@@ -138,6 +140,7 @@
             pltpu.SemaphoreType.DMA((experts,)),
         ],
         compiler_params=params(),
+        cost_estimate=COST,
     )(code, tokens)
 
 
@@ -169,6 +172,7 @@
         out_specs=whole(1)[0],
         scratch_shapes=[pltpu.VMEM((experts * depth, width), BF16), pltpu.SemaphoreType.DMA((experts,))],
         compiler_params=params(),
+        cost_estimate=COST,
     )(offsets, counts, *blocks)
 
 
@@ -215,6 +219,7 @@
             pltpu.SemaphoreType.DMA((3 * parts,)),
         ],
         compiler_params=params(),
+        cost_estimate=COST,
     )(order, gate_weight, up_weight, *xs)
 
 
@@ -270,6 +275,7 @@
             pltpu.SemaphoreType.DMA((experts,)),
         ],
         compiler_params=params(),
+        cost_estimate=COST,
     )(order, offsets, counts, down_weight, *hs)
 
 
@@ -306,6 +312,7 @@
         out_specs=whole(1)[0],
         scratch_shapes=[pltpu.VMEM((experts, rows), F32)],
         compiler_params=params(),
+        cost_estimate=COST,
     )(place, own, logits, code)
 
 
@@ -350,6 +357,7 @@
         ]
         + [pltpu.VMEM((rows, width), F32)] * len(more),
         compiler_params=params(),
+        cost_estimate=COST,
     )(code, weights, *blocks, *more)
 
 
@@ -390,16 +398,12 @@
             held = held + [swap(h, bit) for h in held]
         return held
 
-    code, logits, sends = first_batch(place, picks, router_weight.T, tokens, depth)
+    code, logits, first = first_batch(place, picks, router_weight.T, tokens, depth)
+    later = [later_batch(code, tokens, k, depth) for k in range(1, BATCHES)]
     gathered = jnp.stack([logits] + [along_expert(logits, shift) for shift in range(1, experts)])
-    sends = [[sends[0]] + [after(block, logits) for block in sends[1:]]]
-    arrived = [[sends[0][0]] + [along_expert(sends[0][shift], shift) for shift in range(1, experts)]]
-    for k in range(1, BATCHES):
-        blocks = later_batch(code, tokens, k, depth)
-        arrived.append(
-            [blocks[0]]
-            + [along_expert(after(blocks[shift], arrived[k - 1][shift]), shift) for shift in range(1, experts)]
-        )
+    first = [first[0]] + [after(block, logits) for block in first[1:]]
+    arrived = [[first[0]] + [along_expert(first[shift], shift) for shift in range(1, experts)]]
+    gathered = after(gathered, later)
     for bit in bits:
         gathered = gathered + swap(gathered, bit)
     weights = slot_weights(place, gathered[0], gathered, code)
@@ -413,18 +417,29 @@
     counts = (stop[None, :] + (BATCHES - 1) - ids) // BATCHES - offsets
     offsets, counts, order = after((offsets, counts, order), code)
 
-    total = None
-    results = []
-    for k in range(BATCHES):
-        if k == 0:
-            blocks = after(arrived[0], weights)
-        else:
-            blocks = after(arrived[k], results)
+    def expert_rows(k, blocks):
         block = compact(offsets, counts, k, blocks, size)
         hidden = hidden_units(order, gate_weight, up_weight, all_parts(block))
-        results = down_rows(order, offsets, counts, k, down_weight, all_parts(hidden), experts, depth)
-        returned = [results[0]] + [along_expert(results[shift], -shift) for shift in range(1, experts)]
-        total = combine(code, weights, k, returned, total)
+        return tuple(down_rows(order, offsets, counts, k, down_weight, all_parts(hidden), experts, depth))
+
+    def no_rows(k, blocks):
+        return tuple(jnp.zeros_like(block) for block in blocks)
+
+    waiting = []
+    results = weights
+    for k in range(BATCHES):
+        moving = later[k] if k < BATCHES - 1 else None
+        blocks, moving = after((arrived[k], moving), results, arrived[k])
+        if moving is not None:
+            arrived.append([moving[0]] + [along_expert(moving[shift], shift) for shift in range(1, experts)])
+        results = lax.cond(
+            jnp.sum(counts[k]) > 0, functools.partial(expert_rows, k), functools.partial(no_rows, k), list(blocks)
+        )
+        waiting.append([results[0]] + [along_expert(results[shift], -shift) for shift in range(1, experts)])
+    total = None
+    for k in range(BATCHES):
+        blocks = waiting[k] if k == BATCHES - 1 else after(waiting[k], results)
+        total = combine(code, weights, k, blocks, total)
     return total
 
 

time: 156 us -> 137 us (0.88)
  waiting for transfers between devices: 101 us -> 72 us
  Pallas kernels: 22.3 us -> 27.9 us
  starting transfers between devices: 25.6 us -> 29.4 us
  local copies, waits for them, and re-layouts: 6.3 us -> 4.55 us
    ppermute x15, waiting for transfers between devices: 65.2 us -> 32 us  [along_expert(): lax.ppermute(x, 'expert', [(i, (i + shift) % experts) for i in range(expe...]
    ppermute x14, waiting for transfers between devices: 35.8 us -> 40.1 us  [swap(): return lax.ppermute(x, 'dp', [(i, i ^ bit) for i in range(width_parts)])]
    ppermute x15, starting transfers between devices: 19.1 us -> 21.5 us  [along_expert(): lax.ppermute(x, 'expert', [(i, (i + shift) % experts) for i in range(expe...]
    pallas_call x2, Pallas kernels: 5.14 us -> 7.24 us  [hidden_units(): pl.pallas_call(functools.partial(hidden_kernel, parts), out_shape=jax.Sha...]
    unnamed x16 -> x8, local copies, waits for them, and re-layouts: 5.59 us -> 3.84 us
  transfers between devices with their start and end apart: 29 -> 29, of which waited for: 14 -> 13; matrix products, arithmetic and copies ran while one was open for 1% -> 1% of each run, Pallas kernels for 6% -> 16%
where the time goes in v3:
time: 137 us
  waiting for transfers between devices  72 us (53%)
  starting transfers between devices  29.4 us (21%)
  Pallas kernels  27.9 us (20%)
  local copies, waits for them, and re-layouts  4.55 us (3%)
  between operations  1.49 us (1%)
    ppermute x14, waiting for transfers between devices, swap(): return lax.ppermute(x, 'dp', [(i, i ^ bit) for i in range(width_parts)])  40.1 us
    ppermute x15, waiting for transfers between devices, along_expert(): lax.ppermute(x, 'expert', [(i, (i + shift) % experts) for i in range(expe...  32 us
    ppermute x15, starting transfers between devices, along_expert(): lax.ppermute(x, 'expert', [(i, (i + shift) % experts) for i in range(expe...  21.5 us
    ppermute x14, starting transfers between devices, swap(): return lax.ppermute(x, 'dp', [(i, i ^ bit) for i in range(width_parts)])  7.9 us
    pallas_call x2, Pallas kernels, hidden_units(): pl.pallas_call(functools.partial(hidden_kernel, parts), out_shape=jax.Sha...  7.24 us
    pallas_call x2, Pallas kernels, down_rows(): pl.pallas_call(functools.partial(down_kernel, parts, experts, k), out_sha...  7.15 us
    pallas_call x2, Pallas kernels, combine(): pl.pallas_call(functools.partial(combine_kernel, experts, k), out_shape=j...  4.45 us
    unnamed x8, local copies, waits for them, and re-layouts  3.84 us
  transfers between devices with their start and end apart: 29, of which 13 were waited for; matrix products, arithmetic and copies ran while one was open for 1% of the time, Pallas kernels for 16%

profile of v3, /device:TPU:0, one launch (start us, length us, event | category | flops | bytes accessed | tf_op | source)
XLA Modules:
  0.0 136.5 jit_solution(11239494040000132964)
XLA Ops:
  2.6 3.2 %shard_map.64 = (s32[4,512]{1,0:T(4,128)S(1)}, f32[4,512]{1,0:T(4,128)S(1)}, bf16[128,1024]{1,0:T(8,128)(2,1)S(1)}, bf16[128,1024]{1,0:T(8,128)(2,1)S(1)}, bf16[...) custom-call(s32[1]{0:T(128)} %bitcast.place_ref, s32[4,512]{1,0:T(4,128)S(1)} %copy-done.2, ...), custom_call_target="tpu_custom_call" | custom-call | flops 1024 | bytes 1024 | tf_op jit(solution)/shard_map/pallas_call | solution.py:102
  5.8 5.1 %collective-permute-start.14 = (f32[4,512]{1,0:T(4,128)S(1)}, f32[4,512]{1,0:T(4,128)S(1)}, u32[]{:S(2)}, u32[]{:S(2)}) collective-permute-start(f32[4,512]{1,0:T(4,128)S(1)} %get-tuple-element.107), channel_id=1, source_target_pairs={{0,12},{4,0},{8,4},{12,8},{1,13},{5,1},{9,5},{13,9},{2,14},{6,2},{... | collective-permute-start | bytes 24584 | tf_op jit(solution)/shard_map/ppermute | solution.py:380
  11.9 2.8 %collective-permute-start.19 = (bf16[128,1024]{1,0:T(8,128)(2,1)S(1)}, bf16[128,1024]{1,0:T(8,128)(2,1)S(1)}, u32[]{:S(2)}, u32[]{:S(2)}) collective-permute-start(bf16[128,1024]{1,0:T(8,128)(2,1)S(1)} %get-tuple-element.121), channel_id=1, source_target_pairs={{0,12},{4,0},{8,4},{12,8},{1,13},{5,1},{9,5},{13,9},{2,14},{6,2},{... | collective-permute-start | bytes 786440 | tf_op jit(solution)/shard_map/ppermute | solution.py:380
  18.0 2.1 %shard_map.65 = (bf16[128,1024]{1,0:T(8,128)(2,1)}, bf16[128,1024]{1,0:T(8,128)(2,1)S(1)}, bf16[128,1024]{1,0:T(8,128)(2,1)S(1)}, bf16[128,1024]{1,0:T(8,128)(2,1)S(1)}) custom-call(s32[4,512]{1,0:T(4,128)S(1)} %get-tuple-element.106.code_ref, bf16[512,1024]{1,0:T(8,128)(2,1)S(1)} %copy-done.1), custom_call_target="tpu_custom_call" | custom-call | flops 1024 | bytes 1024 | tf_op jit(solution)/shard_map/pallas_call | solution.py:131
  20.3 1.6 %collective-permute-start.15 = (f32[4,4,512]{2,1,0:T(4,128)S(1)}, f32[4,4,512]{2,1,0:T(4,128)S(1)}, u32[]{:S(2)}, u32[]{:S(2)}) collective-permute-start(f32[4,4,512]{2,1,0:T(4,128)S(1)} %pad_maximum_fusion), channel_id=1, source_target_pairs={{0,2},{1,3},{2,0},{3,1},{4,6},{5,7},{6,4},{7,5},{8,10},{9,11},{10,... | collective-permute-start | bytes 98312 | tf_op jit(solution)/shard_map/ppermute | solution.py:383
  21.9 2.3 %collective-permute-done.15 = f32[4,4,512]{2,1,0:T(4,128)S(1)} collective-permute-done((f32[4,4,512]{2,1,0:T(4,128)S(1)}, f32[4,4,512]{2,1,0:T(4,128)S(1)}, u32[]{:S(2)}, u32[]{:S(2)}) %collective-permute-start.15) | collective-permute-done | bytes 32800 | tf_op jit(solution)/shard_map/ppermute | solution.py:383
  25.9 12.0 %collective-permute-done.18 = bf16[128,1024]{1,0:T(8,128)(2,1)S(1)} collective-permute-done((bf16[128,1024]{1,0:T(8,128)(2,1)S(1)}, bf16[128,1024]{1,0:T(8,128)(2,1)S(1)}, u32[]{:S(2)}, u32[]{:S(2)}) %collective-permute-start.18) | collective-permute-done | bytes 262176 | tf_op jit(solution)/shard_map/ppermute | solution.py:380
  38.0 1.5 %collective-permute-start.21 = (bf16[128,1024]{1,0:T(8,128)(2,1)S(1)}, bf16[128,1024]{1,0:T(8,128)(2,1)}, u32[]{:S(2)}, u32[]{:S(2)}) collective-permute-start(bf16[128,1024]{1,0:T(8,128)(2,1)S(1)} %get-tuple-element.124), channel_id=1, source_target_pairs={{0,8},{4,12},{8,0},{12,4},{1,9},{5,13},{9,1},{13,5},{2,10},{6,14},... | collective-permute-start | bytes 786440 | tf_op jit(solution)/shard_map/ppermute | solution.py:380
  39.5 2.9 %collective-permute-start.22 = (bf16[128,1024]{1,0:T(8,128)(2,1)S(1)}, bf16[128,1024]{1,0:T(8,128)(2,1)}, u32[]{:S(2)}, u32[]{:S(2)}) collective-permute-start(bf16[128,1024]{1,0:T(8,128)(2,1)S(1)} %get-tuple-element.125), channel_id=1, source_target_pairs={{0,12},{4,0},{8,4},{12,8},{1,13},{5,1},{9,5},{13,9},{2,14},{6,2},{... | collective-permute-start | bytes 786440 | tf_op jit(solution)/shard_map/ppermute | solution.py:380
  43.0 29.7 %conditional.2 = ((bf16[128,1024]{1,0:T(8,128)(2,1)}, bf16[128,1024]{1,0:T(8,128)(2,1)}, bf16[128,1024]{1,0:T(8,128)(2,1)}, bf16[128,1024]{1,0:T(8,128)(2,1)})) conditional(s32[]{:T(128)} %convert_element_type.15, () %tuple.36, (s32[2,4]{1,0:T(2,128)S(1)}, s32[2,4]{1,0:T(2,128)S(1)}, bf16[128,1024]{1,0:T(8,128)(2,1)S(1)}, ...), branch_computations={%region_4.5_spmd, %region_5.6_spmd} | conditional | flops 3072 | bytes 16256276 | solution.py:435
  44.2 1.6 %collective-permute-start = (bf16[256,1024]{1,0:T(8,128)(2,1)S(1)}, bf16[256,1024]{1,0:T(8,128)(2,1)S(1)}, u32[]{:S(2)}, u32[]{:S(2)}) collective-permute-start(bf16[256,1024]{1,0:T(8,128)(2,1)S(1)} %branch_1_fun.6.refs_0_), channel_id=1, source_target_pairs={{0,2},{1,3},{2,0},{3,1},{4,6},{5,7},{6,4},{7,5},{8,10},{9,11},{10,... | collective-permute-start | bytes 1572872 | tf_op jit(solution)/shard_map/cond/branch_1_fun/ppermute | solution.py:383
  45.8 10.9 %collective-permute-done.refs_1_ = bf16[256,1024]{1,0:T(8,128)(2,1)S(1)} collective-permute-done((bf16[256,1024]{1,0:T(8,128)(2,1)S(1)}, bf16[256,1024]{1,0:T(8,128)(2,1)S(1)}, u32[]{:S(2)}, u32[]{:S(2)}) %collective-permute-start) | collective-permute-done | bytes 524320 | tf_op jit(solution)/shard_map/cond/branch_1_fun/ppermute | solution.py:383
  56.7 1.9 %collective-permute-done.2.refs_3_ = bf16[256,1024]{1,0:T(8,128)(2,1)S(1)} collective-permute-done((bf16[256,1024]{1,0:T(8,128)(2,1)S(1)}, bf16[256,1024]{1,0:T(8,128)(2,1)S(1)}, u32[]{:S(2)}, u32[]{:S(2)}) %collective-permute-start.2) | collective-permute-done | bytes 524320 | tf_op jit(solution)/shard_map/cond/branch_1_fun/ppermute | solution.py:383
  58.6 3.6 %branch_1_fun.7.refs_0_ = bf16[256,256]{1,0:T(8,128)(2,1)S(1)} custom-call(s32[4]{0:T(128)S(1)} %get-tuple-element.45.order_ref, bf16[1,4096,256]{2,1,0:T(8,128)(2,1)} %get-tuple-element.49.gate_ref, bf16[1,4096,256]{2,1,0:T(8,128)(2,1)} %get-tuple-element.50.up_ref, bf16[256,1024]{1,0:T(8,128)(2,1)S(1)} %branch_1_fun.6.refs_0_, ...), custom_call_target="tpu_custom_call" | custom-call | flops 1024 | bytes 1024 | tf_op jit(solution)/shard_map/cond/branch_1_fun/pallas_call | solution.py:210
  62.2 1.6 %collective-permute-start.3 = (bf16[256,256]{1,0:T(8,128)(2,1)S(1)}, bf16[256,256]{1,0:T(8,128)(2,1)S(1)}, u32[]{:S(2)}, u32[]{:S(2)}) collective-permute-start(bf16[256,256]{1,0:T(8,128)(2,1)S(1)} %branch_1_fun.7.refs_0_), channel_id=1, source_target_pairs={{0,2},{1,3},{2,0},{3,1},{4,6},{5,7},{6,4},{7,5},{8,10},{9,11},{10,... | collective-permute-start | bytes 393224 | tf_op jit(solution)/shard_map/cond/branch_1_fun/ppermute | solution.py:383
  63.8 4.0 %collective-permute-done.3.refs_1_ = bf16[256,256]{1,0:T(8,128)(2,1)S(1)} collective-permute-done((bf16[256,256]{1,0:T(8,128)(2,1)S(1)}, bf16[256,256]{1,0:T(8,128)(2,1)S(1)}, u32[]{:S(2)}, u32[]{:S(2)}) %collective-permute-start.3) | collective-permute-done | bytes 131104 | tf_op jit(solution)/shard_map/cond/branch_1_fun/ppermute | solution.py:383
  69.2 3.6 %branch_1_fun.8 = (bf16[128,1024]{1,0:T(8,128)(2,1)}, bf16[128,1024]{1,0:T(8,128)(2,1)}, bf16[128,1024]{1,0:T(8,128)(2,1)}, bf16[128,1024]{1,0:T(8,128)(2,1)}) custom-call(s32[4]{0:T(128)S(1)} %get-tuple-element.45.order_ref, s32[2,4]{1,0:T(2,128)S(1)} %get-tuple-element.46.offset_ref, s32[2,4]{1,0:T(2,128)S(1)} %get-tuple-element.47.count_ref, ...), custom_call_target="tpu_custom_call" | custom-call | flops 1024 | bytes 1024 | tf_op jit(solution)/shard_map/cond/branch_1_fun/pallas_call | solution.py:265
  75.8 31.6 %conditional.3 = ((bf16[128,1024]{1,0:T(8,128)(2,1)}, bf16[128,1024]{1,0:T(8,128)(2,1)}, bf16[128,1024]{1,0:T(8,128)(2,1)}, bf16[128,1024]{1,0:T(8,128)(2,1)})) conditional(s32[]{:T(128)} %convert_element_type.14, () %tuple.31, (s32[2,4]{1,0:T(2,128)S(1)}, s32[2,4]{1,0:T(2,128)S(1)}, bf16[128,1024]{1,0:T(8,128)(2,1)}, bf16[128,1024]{1,0:T(8,128)(2,1)}, ...), branch_computations={%region_6.7_spmd, %region_7.8_spmd} | conditional | flops 3072 | bytes 16256276 | solution.py:435
  75.8 2.2 %branch_1_fun.9.refs_0_ = bf16[256,1024]{1,0:T(8,128)(2,1)S(1)} custom-call(s32[2,4]{1,0:T(2,128)S(1)} %get-tuple-element.56.offset_ref, s32[2,4]{1,0:T(2,128)S(1)} %get-tuple-element.57.count_ref, bf16[128,1024]{1,0:T(8,128)(2,1)} %get-tuple-element.61.refs_0_, bf16[128,1024]{1,0:T(8,128)(2,1)} %get-tuple-element.62.refs_1_, ...), custom_call_target="tpu_custom_call" | custom-call | flops 1024 | bytes 1024 | tf_op jit(solution)/shard_map/cond/branch_1_fun/pallas_call | solution.py:168
  78.1 1.6 %collective-permute-start.6 = (bf16[256,1024]{1,0:T(8,128)(2,1)S(1)}, bf16[256,1024]{1,0:T(8,128)(2,1)S(1)}, u32[]{:S(2)}, u32[]{:S(2)}) collective-permute-start(bf16[256,1024]{1,0:T(8,128)(2,1)S(1)} %branch_1_fun.9.refs_0_), channel_id=1, source_target_pairs={{0,2},{1,3},{2,0},{3,1},{4,6},{5,7},{6,4},{7,5},{8,10},{9,11},{10,... | collective-permute-start | bytes 1572872 | tf_op jit(solution)/shard_map/cond/branch_1_fun/ppermute | solution.py:383
  79.6 11.7 %collective-permute-done.6.refs_1_ = bf16[256,1024]{1,0:T(8,128)(2,1)S(1)} collective-permute-done((bf16[256,1024]{1,0:T(8,128)(2,1)S(1)}, bf16[256,1024]{1,0:T(8,128)(2,1)S(1)}, u32[]{:S(2)}, u32[]{:S(2)}) %collective-permute-start.6) | collective-permute-done | bytes 524320 | tf_op jit(solution)/shard_map/cond/branch_1_fun/ppermute | solution.py:383
  91.4 1.9 %collective-permute-done.8.refs_3_ = bf16[256,1024]{1,0:T(8,128)(2,1)S(1)} collective-permute-done((bf16[256,1024]{1,0:T(8,128)(2,1)S(1)}, bf16[256,1024]{1,0:T(8,128)(2,1)S(1)}, u32[]{:S(2)}, u32[]{:S(2)}) %collective-permute-start.8) | collective-permute-done | bytes 524320 | tf_op jit(solution)/shard_map/cond/branch_1_fun/ppermute | solution.py:383
  93.3 3.6 %branch_1_fun.10.refs_0_ = bf16[256,256]{1,0:T(8,128)(2,1)S(1)} custom-call(s32[4]{0:T(128)S(1)} %get-tuple-element.55.order_ref, bf16[1,4096,256]{2,1,0:T(8,128)(2,1)} %get-tuple-element.59.gate_ref, bf16[1,4096,256]{2,1,0:T(8,128)(2,1)} %get-tuple-element.60.up_ref, bf16[256,1024]{1,0:T(8,128)(2,1)S(1)} %branch_1_fun.9.refs_0_, ...), custom_call_target="tpu_custom_call" | custom-call | flops 1024 | bytes 1024 | tf_op jit(solution)/shard_map/cond/branch_1_fun/pallas_call | solution.py:210
  96.9 1.6 %collective-permute-start.9 = (bf16[256,256]{1,0:T(8,128)(2,1)S(1)}, bf16[256,256]{1,0:T(8,128)(2,1)S(1)}, u32[]{:S(2)}, u32[]{:S(2)}) collective-permute-start(bf16[256,256]{1,0:T(8,128)(2,1)S(1)} %branch_1_fun.10.refs_0_), channel_id=1, source_target_pairs={{0,2},{1,3},{2,0},{3,1},{4,6},{5,7},{6,4},{7,5},{8,10},{9,11},{10,... | collective-permute-start | bytes 393224 | tf_op jit(solution)/shard_map/cond/branch_1_fun/ppermute | solution.py:383
  98.5 4.0 %collective-permute-done.9.refs_1_ = bf16[256,256]{1,0:T(8,128)(2,1)S(1)} collective-permute-done((bf16[256,256]{1,0:T(8,128)(2,1)S(1)}, bf16[256,256]{1,0:T(8,128)(2,1)S(1)}, u32[]{:S(2)}, u32[]{:S(2)}) %collective-permute-start.9) | collective-permute-done | bytes 131104 | tf_op jit(solution)/shard_map/cond/branch_1_fun/ppermute | solution.py:383
  103.9 3.6 %branch_1_fun.11 = (bf16[128,1024]{1,0:T(8,128)(2,1)}, bf16[128,1024]{1,0:T(8,128)(2,1)}, bf16[128,1024]{1,0:T(8,128)(2,1)}, bf16[128,1024]{1,0:T(8,128)(2,1)}) custom-call(s32[4]{0:T(128)S(1)} %get-tuple-element.55.order_ref, s32[2,4]{1,0:T(2,128)S(1)} %get-tuple-element.56.offset_ref, s32[2,4]{1,0:T(2,128)S(1)} %get-tuple-element.57.count_ref, ...), custom_call_target="tpu_custom_call" | custom-call | flops 1024 | bytes 1024 | tf_op jit(solution)/shard_map/cond/branch_1_fun/pallas_call | solution.py:265
  107.5 2.4 %collective-permute-start.23 = (bf16[128,1024]{1,0:T(8,128)(2,1)}, bf16[128,1024]{1,0:T(8,128)(2,1)S(1)}, u32[]{:S(2)}, u32[]{:S(2)}) collective-permute-start(bf16[128,1024]{1,0:T(8,128)(2,1)} %get-tuple-element.140), channel_id=1, source_target_pairs={{0,12},{4,0},{8,4},{12,8},{1,13},{5,1},{9,5},{13,9},{2,14},{6,2},{... | collective-permute-start | bytes 786440 | tf_op jit(solution)/shard_map/ppermute | solution.py:380
  110.4 1.7 %collective-permute-start.25 = (bf16[128,1024]{1,0:T(8,128)(2,1)}, bf16[128,1024]{1,0:T(8,128)(2,1)S(1)}, u32[]{:S(2)}, u32[]{:S(2)}) collective-permute-start(bf16[128,1024]{1,0:T(8,128)(2,1)} %get-tuple-element.142), channel_id=1, source_target_pairs={{0,4},{4,8},{8,12},{12,0},{1,5},{5,9},{9,13},{13,1},{2,6},{6,10},{... | collective-permute-start | bytes 786440 | tf_op jit(solution)/shard_map/ppermute | solution.py:380
  112.1 1.7 %shard_map.67.refs_4_ = f32[512,1024]{1,0:T(8,128)S(1)} custom-call(s32[4,512]{1,0:T(4,128)S(1)} %get-tuple-element.106.code_ref, f32[4,512]{1,0:T(4,128)S(1)} %shard_map.66.weight_ref, bf16[128,1024]{1,0:T(8,128)(2,1)} %get-tuple-element.143.refs_0_, bf16[128,1024]{1,0:T(8,128)(2,1)S(1)} %collective-permute-done.26.refs_1_, ...), custom_call_target="tpu_custom_call" | custom-call | flops 1024 | bytes 1024 | tf_op jit(solution)/shard_map/pallas_call | solution.py:349
  113.9 3.0 %collective-permute-done.23.refs_1_ = bf16[128,1024]{1,0:T(8,128)(2,1)S(1)} collective-permute-done((bf16[128,1024]{1,0:T(8,128)(2,1)}, bf16[128,1024]{1,0:T(8,128)(2,1)S(1)}, u32[]{:S(2)}, u32[]{:S(2)}) %collective-permute-start.23) | collective-permute-done | bytes 262176 | tf_op jit(solution)/shard_map/ppermute | solution.py:380
  116.9 16.9 %collective-permute-done.24.refs_2_ = bf16[128,1024]{1,0:T(8,128)(2,1)S(1)} collective-permute-done((bf16[128,1024]{1,0:T(8,128)(2,1)}, bf16[128,1024]{1,0:T(8,128)(2,1)S(1)}, u32[]{:S(2)}, u32[]{:S(2)}) %collective-permute-start.24) | collective-permute-done | bytes 262176 | tf_op jit(solution)/shard_map/ppermute | solution.py:380
  133.8 2.7 %shard_map.68 = bf16[512,1024]{1,0:T(8,128)(2,1)} custom-call(s32[4,512]{1,0:T(4,128)S(1)} %get-tuple-element.106.code_ref, f32[4,512]{1,0:T(4,128)S(1)} %shard_map.66.weight_ref, bf16[128,1024]{1,0:T(8,128)(2,1)} %get-tuple-element.139.refs_0_, bf16[128,1024]{1,0:T(8,128)(2,1)S(1)} %collective-permute-done.23.refs_1_, ...), custom_call_target="tpu_custom_call" | custom-call | flops 1024 | bytes 1024 | tf_op jit(solution)/shard_map/pallas_call | solution.py:349
  (63 shorter events, 15.5 us)
Async XLA Ops:
  5.8 14.4 %collective-permute-start.14 = (f32[4,512]{1,0:T(4,128)S(1)}, f32[4,512]{1,0:T(4,128)S(1)}, u32[]{:S(2)}, u32[]{:S(2)}) collective-permute-start(f32[4,512]{1,0:T(4,128)S(1)} %get-tuple-element.107), channel_id=1, source_target_pairs={{0,12},{4,0},{8,4},{12,8},{1,13},{5,1},{9,5},{13,9},{2,14},{6,2},{... | collective-permute-start | bytes 24584 | tf_op jit(solution)/shard_map/ppermute | solution.py:380
  10.9 9.4 %collective-permute-start.13 = (f32[4,512]{1,0:T(4,128)S(1)}, f32[4,512]{1,0:T(4,128)S(1)}, u32[]{:S(2)}, u32[]{:S(2)}) collective-permute-start(f32[4,512]{1,0:T(4,128)S(1)} %get-tuple-element.107), channel_id=1, source_target_pairs={{0,8},{4,12},{8,0},{12,4},{1,9},{5,13},{9,1},{13,5},{2,10},{6,14},... | collective-permute-start | bytes 24584 | tf_op jit(solution)/shard_map/ppermute | solution.py:380
  10.9 9.4 %collective-permute-start.12 = (f32[4,512]{1,0:T(4,128)S(1)}, f32[4,512]{1,0:T(4,128)S(1)}, u32[]{:S(2)}, u32[]{:S(2)}) collective-permute-start(f32[4,512]{1,0:T(4,128)S(1)} %get-tuple-element.107), channel_id=1, source_target_pairs={{0,4},{4,8},{8,12},{12,0},{1,5},{5,9},{9,13},{13,1},{2,6},{6,10},{... | collective-permute-start | bytes 24584 | tf_op jit(solution)/shard_map/ppermute | solution.py:380
  11.9 14.0 %collective-permute-start.19 = (bf16[128,1024]{1,0:T(8,128)(2,1)S(1)}, bf16[128,1024]{1,0:T(8,128)(2,1)S(1)}, u32[]{:S(2)}, u32[]{:S(2)}) collective-permute-start(bf16[128,1024]{1,0:T(8,128)(2,1)S(1)} %get-tuple-element.121), channel_id=1, source_target_pairs={{0,12},{4,0},{8,4},{12,8},{1,13},{5,1},{9,5},{13,9},{2,14},{6,2},{... | collective-permute-start | bytes 786440 | tf_op jit(solution)/shard_map/ppermute | solution.py:380
  14.7 23.3 %collective-permute-start.18 = (bf16[128,1024]{1,0:T(8,128)(2,1)S(1)}, bf16[128,1024]{1,0:T(8,128)(2,1)S(1)}, u32[]{:S(2)}, u32[]{:S(2)}) collective-permute-start(bf16[128,1024]{1,0:T(8,128)(2,1)S(1)} %get-tuple-element.119), channel_id=1, source_target_pairs={{0,8},{4,12},{8,0},{12,4},{1,9},{5,13},{9,1},{13,5},{2,10},{6,14},... | collective-permute-start | bytes 786440 | tf_op jit(solution)/shard_map/ppermute | solution.py:380
  16.8 1.2 copy-start.1
  20.2 17.8 %collective-permute-start.17 = (bf16[128,1024]{1,0:T(8,128)(2,1)S(1)}, bf16[128,1024]{1,0:T(8,128)(2,1)S(1)}, u32[]{:S(2)}, u32[]{:S(2)}) collective-permute-start(bf16[128,1024]{1,0:T(8,128)(2,1)S(1)} %get-tuple-element.117), channel_id=1, source_target_pairs={{0,4},{4,8},{8,12},{12,0},{1,5},{5,9},{9,13},{13,1},{2,6},{6,10},{... | collective-permute-start | bytes 786440 | tf_op jit(solution)/shard_map/ppermute | solution.py:380
  20.3 4.0 %collective-permute-start.15 = (f32[4,4,512]{2,1,0:T(4,128)S(1)}, f32[4,4,512]{2,1,0:T(4,128)S(1)}, u32[]{:S(2)}, u32[]{:S(2)}) collective-permute-start(f32[4,4,512]{2,1,0:T(4,128)S(1)} %pad_maximum_fusion), channel_id=1, source_target_pairs={{0,2},{1,3},{2,0},{3,1},{4,6},{5,7},{6,4},{7,5},{8,10},{9,11},{10,... | collective-permute-start | bytes 98312 | tf_op jit(solution)/shard_map/ppermute | solution.py:383
  24.3 1.3 collective-permute-start.16
  38.0 36.4 %collective-permute-start.20 = (bf16[128,1024]{1,0:T(8,128)(2,1)S(1)}, bf16[128,1024]{1,0:T(8,128)(2,1)}, u32[]{:S(2)}, u32[]{:S(2)}) collective-permute-start(bf16[128,1024]{1,0:T(8,128)(2,1)S(1)} %get-tuple-element.123), channel_id=1, source_target_pairs={{0,4},{4,8},{8,12},{12,0},{1,5},{5,9},{9,13},{13,1},{2,6},{6,10},{... | collective-permute-start | bytes 786440 | tf_op jit(solution)/shard_map/ppermute | solution.py:380
  38.0 37.8 %collective-permute-start.21 = (bf16[128,1024]{1,0:T(8,128)(2,1)S(1)}, bf16[128,1024]{1,0:T(8,128)(2,1)}, u32[]{:S(2)}, u32[]{:S(2)}) collective-permute-start(bf16[128,1024]{1,0:T(8,128)(2,1)S(1)} %get-tuple-element.124), channel_id=1, source_target_pairs={{0,8},{4,12},{8,0},{12,4},{1,9},{5,13},{9,1},{13,5},{2,10},{6,14},... | collective-permute-start | bytes 786440 | tf_op jit(solution)/shard_map/ppermute | solution.py:380
  39.5 36.4 %collective-permute-start.22 = (bf16[128,1024]{1,0:T(8,128)(2,1)S(1)}, bf16[128,1024]{1,0:T(8,128)(2,1)}, u32[]{:S(2)}, u32[]{:S(2)}) collective-permute-start(bf16[128,1024]{1,0:T(8,128)(2,1)S(1)} %get-tuple-element.125), channel_id=1, source_target_pairs={{0,12},{4,0},{8,4},{12,8},{1,13},{5,1},{9,5},{13,9},{2,14},{6,2},{... | collective-permute-start | bytes 786440 | tf_op jit(solution)/shard_map/ppermute | solution.py:380
  44.2 12.5 %collective-permute-start = (bf16[256,1024]{1,0:T(8,128)(2,1)S(1)}, bf16[256,1024]{1,0:T(8,128)(2,1)S(1)}, u32[]{:S(2)}, u32[]{:S(2)}) collective-permute-start(bf16[256,1024]{1,0:T(8,128)(2,1)S(1)} %branch_1_fun.6.refs_0_), channel_id=1, source_target_pairs={{0,2},{1,3},{2,0},{3,1},{4,6},{5,7},{6,4},{7,5},{8,10},{9,11},{10,... | collective-permute-start | bytes 1572872 | tf_op jit(solution)/shard_map/cond/branch_1_fun/ppermute | solution.py:383
  45.8 10.9 %collective-permute-start.1 = (bf16[256,1024]{1,0:T(8,128)(2,1)S(1)}, bf16[256,1024]{1,0:T(8,128)(2,1)S(1)}, u32[]{:S(2)}, u32[]{:S(2)}) collective-permute-start(bf16[256,1024]{1,0:T(8,128)(2,1)S(1)} %branch_1_fun.6.refs_0_), channel_id=1, source_target_pairs={{0,1},{1,0},{2,3},{3,2},{4,5},{5,4},{6,7},{7,6},{8,9},{9,8},{10,11... | collective-permute-start | bytes 1572872 | tf_op jit(solution)/shard_map/cond/branch_1_fun/ppermute | solution.py:383
  56.7 1.9 %collective-permute-start.2 = (bf16[256,1024]{1,0:T(8,128)(2,1)S(1)}, bf16[256,1024]{1,0:T(8,128)(2,1)S(1)}, u32[]{:S(2)}, u32[]{:S(2)}) collective-permute-start(bf16[256,1024]{1,0:T(8,128)(2,1)S(1)} %collective-permute-done.refs_1_), channel_id=1, source_target_pairs={{0,1},{1,0},{2,3},{3,2},{4,5},{5,4},{6,7},{7,6},{8,9},{9,8},{10,11... | collective-permute-start | bytes 1572872 | tf_op jit(solution)/shard_map/cond/branch_1_fun/ppermute | solution.py:383
  58.6 10.6 %copy-start.4 = (bf16[1,1024,1024]{2,1,0:T(8,128)(2,1)S(1)}, bf16[1,1024,1024]{2,1,0:T(8,128)(2,1)}, u32[]{:S(2)}) copy-start(bf16[1,1024,1024]{2,1,0:T(8,128)(2,1)} %get-tuple-element.48.down_ref) | copy-start | bytes 6291460 | tf_op jit(solution)/shard_map/cond
  62.2 5.6 %collective-permute-start.3 = (bf16[256,256]{1,0:T(8,128)(2,1)S(1)}, bf16[256,256]{1,0:T(8,128)(2,1)S(1)}, u32[]{:S(2)}, u32[]{:S(2)}) collective-permute-start(bf16[256,256]{1,0:T(8,128)(2,1)S(1)} %branch_1_fun.7.refs_0_), channel_id=1, source_target_pairs={{0,2},{1,3},{2,0},{3,1},{4,6},{5,7},{6,4},{7,5},{8,10},{9,11},{10,... | collective-permute-start | bytes 393224 | tf_op jit(solution)/shard_map/cond/branch_1_fun/ppermute | solution.py:383
  63.8 4.1 %collective-permute-start.4 = (bf16[256,256]{1,0:T(8,128)(2,1)S(1)}, bf16[256,256]{1,0:T(8,128)(2,1)S(1)}, u32[]{:S(2)}, u32[]{:S(2)}) collective-permute-start(bf16[256,256]{1,0:T(8,128)(2,1)S(1)} %branch_1_fun.7.refs_0_), channel_id=1, source_target_pairs={{0,1},{1,0},{2,3},{3,2},{4,5},{5,4},{6,7},{7,6},{8,9},{9,8},{10,11... | collective-permute-start | bytes 393224 | tf_op jit(solution)/shard_map/cond/branch_1_fun/ppermute | solution.py:383
  67.8 1.3 collective-permute-start.5
  72.8 37.6 %collective-permute-start.26 = (bf16[128,1024]{1,0:T(8,128)(2,1)}, bf16[128,1024]{1,0:T(8,128)(2,1)S(1)}, u32[]{:S(2)}, u32[]{:S(2)}) collective-permute-start(bf16[128,1024]{1,0:T(8,128)(2,1)} %get-tuple-element.132), channel_id=1, source_target_pairs={{0,12},{4,0},{8,4},{12,8},{1,13},{5,1},{9,5},{13,9},{2,14},{6,2},{... | collective-permute-start | bytes 786440 | tf_op jit(solution)/shard_map/ppermute | solution.py:380
  73.8 38.3 %collective-permute-start.27 = (bf16[128,1024]{1,0:T(8,128)(2,1)}, bf16[128,1024]{1,0:T(8,128)(2,1)S(1)}, u32[]{:S(2)}, u32[]{:S(2)}) collective-permute-start(bf16[128,1024]{1,0:T(8,128)(2,1)} %get-tuple-element.133), channel_id=1, source_target_pairs={{0,8},{4,12},{8,0},{12,4},{1,9},{5,13},{9,1},{13,5},{2,10},{6,14},... | collective-permute-start | bytes 786440 | tf_op jit(solution)/shard_map/ppermute | solution.py:380
  74.4 37.7 %collective-permute-start.28 = (bf16[128,1024]{1,0:T(8,128)(2,1)}, bf16[128,1024]{1,0:T(8,128)(2,1)S(1)}, u32[]{:S(2)}, u32[]{:S(2)}) collective-permute-start(bf16[128,1024]{1,0:T(8,128)(2,1)} %get-tuple-element.134), channel_id=1, source_target_pairs={{0,4},{4,8},{8,12},{12,0},{1,5},{5,9},{9,13},{13,1},{2,6},{6,10},{... | collective-permute-start | bytes 786440 | tf_op jit(solution)/shard_map/ppermute | solution.py:380
  78.1 13.3 %collective-permute-start.6 = (bf16[256,1024]{1,0:T(8,128)(2,1)S(1)}, bf16[256,1024]{1,0:T(8,128)(2,1)S(1)}, u32[]{:S(2)}, u32[]{:S(2)}) collective-permute-start(bf16[256,1024]{1,0:T(8,128)(2,1)S(1)} %branch_1_fun.9.refs_0_), channel_id=1, source_target_pairs={{0,2},{1,3},{2,0},{3,1},{4,6},{5,7},{6,4},{7,5},{8,10},{9,11},{10,... | collective-permute-start | bytes 1572872 | tf_op jit(solution)/shard_map/cond/branch_1_fun/ppermute | solution.py:383
  79.6 11.8 %collective-permute-start.7 = (bf16[256,1024]{1,0:T(8,128)(2,1)S(1)}, bf16[256,1024]{1,0:T(8,128)(2,1)S(1)}, u32[]{:S(2)}, u32[]{:S(2)}) collective-permute-start(bf16[256,1024]{1,0:T(8,128)(2,1)S(1)} %branch_1_fun.9.refs_0_), channel_id=1, source_target_pairs={{0,1},{1,0},{2,3},{3,2},{4,5},{5,4},{6,7},{7,6},{8,9},{9,8},{10,11... | collective-permute-start | bytes 1572872 | tf_op jit(solution)/shard_map/cond/branch_1_fun/ppermute | solution.py:383
  91.4 1.9 %collective-permute-start.8 = (bf16[256,1024]{1,0:T(8,128)(2,1)S(1)}, bf16[256,1024]{1,0:T(8,128)(2,1)S(1)}, u32[]{:S(2)}, u32[]{:S(2)}) collective-permute-start(bf16[256,1024]{1,0:T(8,128)(2,1)S(1)} %collective-permute-done.6.refs_1_), channel_id=1, source_target_pairs={{0,1},{1,0},{2,3},{3,2},{4,5},{5,4},{6,7},{7,6},{8,9},{9,8},{10,11... | collective-permute-start | bytes 1572872 | tf_op jit(solution)/shard_map/cond/branch_1_fun/ppermute | solution.py:383
  93.3 10.6 %copy-start.5 = (bf16[1,1024,1024]{2,1,0:T(8,128)(2,1)S(1)}, bf16[1,1024,1024]{2,1,0:T(8,128)(2,1)}, u32[]{:S(2)}) copy-start(bf16[1,1024,1024]{2,1,0:T(8,128)(2,1)} %get-tuple-element.58.down_ref) | copy-start | bytes 6291460 | tf_op jit(solution)/shard_map/cond
  96.9 5.6 %collective-permute-start.9 = (bf16[256,256]{1,0:T(8,128)(2,1)S(1)}, bf16[256,256]{1,0:T(8,128)(2,1)S(1)}, u32[]{:S(2)}, u32[]{:S(2)}) collective-permute-start(bf16[256,256]{1,0:T(8,128)(2,1)S(1)} %branch_1_fun.10.refs_0_), channel_id=1, source_target_pairs={{0,2},{1,3},{2,0},{3,1},{4,6},{5,7},{6,4},{7,5},{8,10},{9,11},{10,... | collective-permute-start | bytes 393224 | tf_op jit(solution)/shard_map/cond/branch_1_fun/ppermute | solution.py:383
  98.5 4.1 %collective-permute-start.10 = (bf16[256,256]{1,0:T(8,128)(2,1)S(1)}, bf16[256,256]{1,0:T(8,128)(2,1)S(1)}, u32[]{:S(2)}, u32[]{:S(2)}) collective-permute-start(bf16[256,256]{1,0:T(8,128)(2,1)S(1)} %branch_1_fun.10.refs_0_), channel_id=1, source_target_pairs={{0,1},{1,0},{2,3},{3,2},{4,5},{5,4},{6,7},{7,6},{8,9},{9,8},{10,11... | collective-permute-start | bytes 393224 | tf_op jit(solution)/shard_map/cond/branch_1_fun/ppermute | solution.py:383
  102.5 1.3 collective-permute-start.11
  107.5 9.4 %collective-permute-start.23 = (bf16[128,1024]{1,0:T(8,128)(2,1)}, bf16[128,1024]{1,0:T(8,128)(2,1)S(1)}, u32[]{:S(2)}, u32[]{:S(2)}) collective-permute-start(bf16[128,1024]{1,0:T(8,128)(2,1)} %get-tuple-element.140), channel_id=1, source_target_pairs={{0,12},{4,0},{8,4},{12,8},{1,13},{5,1},{9,5},{13,9},{2,14},{6,2},{... | collective-permute-start | bytes 786440 | tf_op jit(solution)/shard_map/ppermute | solution.py:380
  109.8 23.9 %collective-permute-start.24 = (bf16[128,1024]{1,0:T(8,128)(2,1)}, bf16[128,1024]{1,0:T(8,128)(2,1)S(1)}, u32[]{:S(2)}, u32[]{:S(2)}) collective-permute-start(bf16[128,1024]{1,0:T(8,128)(2,1)} %get-tuple-element.141), channel_id=1, source_target_pairs={{0,8},{4,12},{8,0},{12,4},{1,9},{5,13},{9,1},{13,5},{2,10},{6,14},... | collective-permute-start | bytes 786440 | tf_op jit(solution)/shard_map/ppermute | solution.py:380
  110.4 23.4 %collective-permute-start.25 = (bf16[128,1024]{1,0:T(8,128)(2,1)}, bf16[128,1024]{1,0:T(8,128)(2,1)S(1)}, u32[]{:S(2)}, u32[]{:S(2)}) collective-permute-start(bf16[128,1024]{1,0:T(8,128)(2,1)} %get-tuple-element.142), channel_id=1, source_target_pairs={{0,4},{4,8},{8,12},{12,0},{1,5},{5,9},{9,13},{13,1},{2,6},{6,10},{... | collective-permute-start | bytes 786440 | tf_op jit(solution)/shard_map/ppermute | solution.py:380
  (3 other events, 2.6 us)

commit v4 on v3

--- a/solution.py
+++ b/solution.py
@@ -27,8 +27,8 @@
     return pl.BlockSpec(memory_space=pltpu.SMEM)
 
 
-def params():
-    return pltpu.CompilerParams(vmem_limit_bytes=VMEM_LIMIT)
+def params(limit=VMEM_LIMIT):
+    return pltpu.CompilerParams(vmem_limit_bytes=limit)
 
 
 def dot(a, b):
@@ -42,10 +42,12 @@
     return copies
 
 
-def code_kernel(experts, depth, place_ref, picks_ref, router_ref, tokens_ref, code_ref, logits_ref, *refs):
+def code_kernel(experts, depth, place_ref, picks_in, router_in, tokens_ref, code_ref, logits_ref, *refs):
     sends = refs[:experts]
-    held, staged, in_sems, out_sems = refs[experts:]
-    load = start_all([tokens_ref], [held], in_sems)[0]
+    picks_ref, router_ref, held, staged, in_sems, out_sems = refs[experts:]
+    picks_load, router_load, load = start_all(
+        [picks_in, router_in, tokens_ref], [picks_ref, router_ref, held], in_sems
+    )
     me = place_ref[0]
     rows, width = held.shape
     capacity = picks_ref.shape[1]
@@ -55,6 +57,7 @@
     upper = (lax.broadcasted_iota(I32, (128, 128), 0) < lax.broadcasted_iota(I32, (128, 128), 1)).astype(BF16)
     before = (lax.broadcasted_iota(I32, (8, 8), 1) < lax.broadcasted_iota(I32, (8, 8), 0)).astype(BF16)
     ones = jnp.ones((128, 128), BF16)
+    picks_load.wait()
     code_rows = []
     for shift in range(experts):
         expert = lax.rem(me + shift, experts)
@@ -76,6 +79,7 @@
         row = jnp.concatenate([code[i : i + 1] for i in range(strips)], axis=1)
         code_ref[pl.ds(shift, 1), :] = row
         code_rows.append(row)
+    router_load.wait()
     load.wait()
     logits_ref[...] = lax.dot_general(
         router_ref[...], held[...], (((1,), (1,)), ((), ())), preferred_element_type=F32
@@ -103,15 +107,17 @@
         functools.partial(code_kernel, experts, depth),
         out_shape=[jax.ShapeDtypeStruct((experts, rows), I32), jax.ShapeDtypeStruct((experts, rows), F32)]
         + [jax.ShapeDtypeStruct((depth, width), BF16)] * experts,
-        in_specs=[smem()] + whole(2) + apart(1),
+        in_specs=[smem()] + apart(3),
         out_specs=whole(2) + apart(experts),
         scratch_shapes=[
+            pltpu.VMEM(picks.shape, I32),
+            pltpu.VMEM(router.shape, BF16),
             pltpu.VMEM((rows, width), BF16),
             pltpu.VMEM((experts, depth, width), BF16),
-            pltpu.SemaphoreType.DMA((1,)),
+            pltpu.SemaphoreType.DMA((3,)),
             pltpu.SemaphoreType.DMA((experts,)),
         ],
-        compiler_params=params(),
+        compiler_params=params(60 * 1024 * 1024),
         cost_estimate=COST,
     )(place, picks, router, tokens)
     return out[0], out[1], out[2:]
@@ -176,13 +182,17 @@
     )(offsets, counts, *blocks)
 
 
-def hidden_kernel(parts, order_ref, gate_ref, up_ref, *refs):
-    xs, out_ref = refs[:parts], refs[parts]
-    gate_held, up_held, x_held, sems = refs[parts + 1 :]
+def gate_up_kernel(parts, places, last, order_ref, gate_ref, up_ref, *refs):
+    xs, refs = refs[:parts], refs[parts:]
+    if last:
+        gate_before, up_before, out_ref, *refs = refs
+    else:
+        gate_out, up_out, *refs = refs
+    gate_held, up_held, x_held, sems = refs
     width = xs[0].shape[1]
     loads = []
     for i in range(parts):
-        first = pl.multiple_of(order_ref[i] * width, width)
+        first = pl.multiple_of(order_ref[places[i]] * width, width)
         copies = [
             pltpu.make_async_copy(xs[i], x_held.at[i], sems.at[3 * i]),
             pltpu.make_async_copy(gate_ref.at[0, pl.ds(first, width), :], gate_held.at[i], sems.at[3 * i + 1]),
@@ -191,7 +201,7 @@
         for copy in copies:
             copy.start()
         loads.append(copies)
-    gate = up = None
+    gate, up = (gate_before[...], up_before[...]) if last else (None, None)
     for i in range(parts):
         for copy in loads[i]:
             copy.wait()
@@ -200,18 +210,24 @@
         up_term = dot(x, up_held[i])
         gate = gate_term if gate is None else gate + gate_term
         up = up_term if up is None else up + up_term
-    out_ref[...] = (gate * jax.nn.sigmoid(gate) * up).astype(BF16)
-
-
-def hidden_units(order, gate_weight, up_weight, xs):
+    if last:
+        out_ref[...] = (gate * jax.nn.sigmoid(gate) * up).astype(BF16)
+    else:
+        gate_out[...] = gate
+        up_out[...] = up
+
+
+def gate_up(order, places, gate_weight, up_weight, xs, before):
     parts = len(xs)
     size, width = xs[0].shape
     units = gate_weight.shape[2]
-    return pl.pallas_call(
-        functools.partial(hidden_kernel, parts),
-        out_shape=jax.ShapeDtypeStruct((size, units), BF16),
-        in_specs=[smem()] + apart(2 + parts),
-        out_specs=whole(1)[0],
+    last = before is not None
+    sums = [jax.ShapeDtypeStruct((size, units), F32)] * 2
+    return pl.pallas_call(
+        functools.partial(gate_up_kernel, parts, places, last),
+        out_shape=jax.ShapeDtypeStruct((size, units), BF16) if last else sums,
+        in_specs=[smem()] + apart(2 + parts) + (whole(2) if last else []),
+        out_specs=whole(1)[0] if last else whole(2),
         scratch_shapes=[
             pltpu.VMEM((parts, width, units), BF16),
             pltpu.VMEM((parts, width, units), BF16),
@@ -220,33 +236,43 @@
         ],
         compiler_params=params(),
         cost_estimate=COST,
-    )(order, gate_weight, up_weight, *xs)
-
-
-def down_kernel(parts, experts, k, order_ref, offset_ref, count_ref, down_ref, *refs):
-    hs, outs = refs[:parts], refs[parts : parts + experts]
-    down_held, h_held, staged, in_sems, out_sems = refs[parts + experts :]
-    size, units = hs[0].shape
-    depth = outs[0].shape[0]
+    )(order, gate_weight, up_weight, *xs, *(before or []))
+
+
+def down_sum(places, order_ref, down_ref, hs, down_held, h_held, sems, total):
+    units = hs[0].shape[1]
     loads = []
-    for i in range(parts):
-        first = pl.multiple_of(order_ref[i] * units, units)
+    for i in range(len(hs)):
+        first = pl.multiple_of(order_ref[places[i]] * units, units)
         copies = [
-            pltpu.make_async_copy(hs[i], h_held.at[i], in_sems.at[2 * i]),
-            pltpu.make_async_copy(down_ref.at[0, pl.ds(first, units), :], down_held.at[i], in_sems.at[2 * i + 1]),
+            pltpu.make_async_copy(hs[i], h_held.at[i], sems.at[2 * i]),
+            pltpu.make_async_copy(down_ref.at[0, pl.ds(first, units), :], down_held.at[i], sems.at[2 * i + 1]),
         ]
         for copy in copies:
             copy.start()
         loads.append(copies)
-    row = lax.broadcasted_iota(I32, (depth, size), 0)
-    lane = lax.broadcasted_iota(I32, (depth, size), 1)
-    total = None
-    for i in range(parts):
+    for i in range(len(hs)):
         for copy in loads[i]:
             copy.wait()
         term = dot(h_held[i], down_held[i])
         total = term if total is None else total + term
+    return total
+
+
+def down_first_kernel(parts, places, order_ref, down_ref, *refs):
+    hs, out_ref = refs[:parts], refs[parts]
+    out_ref[...] = down_sum(places, order_ref, down_ref, hs, *refs[parts + 1 :], None)
+
+
+def down_last_kernel(parts, places, experts, k, order_ref, offset_ref, count_ref, down_ref, *refs):
+    hs, before, outs = refs[:parts], refs[parts], refs[parts + 1 : parts + 1 + experts]
+    down_held, h_held, in_sems, staged, out_sems = refs[parts + 1 + experts :]
+    size = hs[0].shape[0]
+    depth = outs[0].shape[0]
+    total = down_sum(places, order_ref, down_ref, hs, down_held, h_held, in_sems, before[...])
     result = total.astype(BF16)
+    row = lax.broadcasted_iota(I32, (depth, size), 0)
+    lane = lax.broadcasted_iota(I32, (depth, size), 1)
     copies = []
     for i in list(range(1, experts)) + [0]:
         pick = ((lane - offset_ref[k, i] == row) & (row < count_ref[k, i])).astype(F32).astype(BF16)
@@ -258,25 +284,43 @@
         copy.wait()
 
 
-def down_rows(order, offsets, counts, k, down_weight, hs, experts, depth):
+def down_scratch(parts, size, units, width):
+    return [
+        pltpu.VMEM((parts, units, width), BF16),
+        pltpu.VMEM((parts, size, units), BF16),
+        pltpu.SemaphoreType.DMA((2 * parts,)),
+    ]
+
+
+def down_first(order, places, down_weight, hs):
     parts = len(hs)
     size, units = hs[0].shape
     width = down_weight.shape[2]
     return pl.pallas_call(
-        functools.partial(down_kernel, parts, experts, k),
+        functools.partial(down_first_kernel, parts, places),
+        out_shape=jax.ShapeDtypeStruct((size, width), F32),
+        in_specs=[smem()] + apart(1 + parts),
+        out_specs=whole(1)[0],
+        scratch_shapes=down_scratch(parts, size, units, width),
+        compiler_params=params(),
+        cost_estimate=COST,
+    )(order, down_weight, *hs)
+
+
+def down_last(order, places, offsets, counts, k, down_weight, hs, before, experts, depth):
+    parts = len(hs)
+    size, units = hs[0].shape
+    width = down_weight.shape[2]
+    return pl.pallas_call(
+        functools.partial(down_last_kernel, parts, places, experts, k),
         out_shape=[jax.ShapeDtypeStruct((depth, width), BF16)] * experts,
-        in_specs=[smem()] * 3 + apart(1 + parts),
+        in_specs=[smem()] * 3 + apart(1 + parts) + whole(1),
         out_specs=apart(experts),
-        scratch_shapes=[
-            pltpu.VMEM((parts, units, width), BF16),
-            pltpu.VMEM((parts, size, units), BF16),
-            pltpu.VMEM((experts, depth, width), BF16),
-            pltpu.SemaphoreType.DMA((2 * parts,)),
-            pltpu.SemaphoreType.DMA((experts,)),
-        ],
-        compiler_params=params(),
-        cost_estimate=COST,
-    )(order, offsets, counts, down_weight, *hs)
+        scratch_shapes=down_scratch(parts, size, units, width)
+        + [pltpu.VMEM((experts, depth, width), BF16), pltpu.SemaphoreType.DMA((experts,))],
+        compiler_params=params(),
+        cost_estimate=COST,
+    )(order, offsets, counts, down_weight, *hs, before)
 
 
 def weight_kernel(experts, place_ref, own_ref, logits_ref, code_ref, out_ref, score_ref):
@@ -387,27 +431,30 @@
     while bit:
         bits.append(bit)
         bit //= 2
-    masks = [0]
-    for bit in bits:
-        masks = masks + [m ^ bit for m in masks]
+    near = [0]
+    for bit in bits[1:]:
+        near = near + [m ^ bit for m in near]
+    masks = near + [m ^ bits[0] for m in near]
+    places = range(len(masks))
+    near_places, far_places = places[: len(near)], places[len(near) :]
     order = jnp.stack([part ^ m for m in masks]).astype(I32)
 
-    def all_parts(x):
+    def swap_expert(x, bit):
+        return lax.ppermute(x, "expert", [(i, i ^ bit) for i in range(experts)])
+
+    expert_bits = [1 << i for i in range(experts.bit_length() - 1)]
+
+    def spread(x):
         held = [x]
-        for bit in bits:
+        for bit in bits[1:]:
             held = held + [swap(h, bit) for h in held]
         return held
 
+    def both_parts(x):
+        far = swap(x, bits[0])
+        return spread(x), spread(far)
+
     code, logits, first = first_batch(place, picks, router_weight.T, tokens, depth)
-    later = [later_batch(code, tokens, k, depth) for k in range(1, BATCHES)]
-    gathered = jnp.stack([logits] + [along_expert(logits, shift) for shift in range(1, experts)])
-    first = [first[0]] + [after(block, logits) for block in first[1:]]
-    arrived = [[first[0]] + [along_expert(first[shift], shift) for shift in range(1, experts)]]
-    gathered = after(gathered, later)
-    for bit in bits:
-        gathered = gathered + swap(gathered, bit)
-    weights = slot_weights(place, gathered[0], gathered, code)
-
     own_picks = lax.dynamic_slice_in_dim(picks, me, 1, axis=0)
     sources = lax.rem(me - jnp.arange(experts, dtype=I32) + experts, experts)
     start = jnp.sum((own_picks < (sources * rows)[:, None]).astype(I32), axis=1)
@@ -415,31 +462,62 @@
     ids = jnp.arange(BATCHES, dtype=I32)[:, None]
     offsets = (start[None, :] + (BATCHES - 1) - ids) // BATCHES
     counts = (stop[None, :] + (BATCHES - 1) - ids) // BATCHES - offsets
-    offsets, counts, order = after((offsets, counts, order), code)
+
+    present = [jnp.sum(counts[k]) > 0 for k in range(BATCHES)]
+
+    def beside_first(logits):
+        later = [tuple(later_batch(code, tokens, k, depth)) for k in range(1, BATCHES)]
+        for bit in bits:
+            logits = logits + swap(logits, bit)
+        gathered = logits[None]
+        for bit in expert_bits[:-1]:
+            gathered = jnp.concatenate([gathered, swap_expert(gathered, bit)])
+        return later, logits, gathered
+
+    def nothing_first(logits):
+        return jax.tree.map(lambda x: jnp.zeros(x.shape, x.dtype), jax.eval_shape(beside_first, logits))
+
+    arrived = [[first[0]] + [along_expert(first[shift], shift) for shift in range(1, experts)]]
+    later, logits, gathered = lax.cond(present[0], beside_first, nothing_first, logits)
 
     def expert_rows(k, blocks):
         block = compact(offsets, counts, k, blocks, size)
-        hidden = hidden_units(order, gate_weight, up_weight, all_parts(block))
-        return tuple(down_rows(order, offsets, counts, k, down_weight, all_parts(hidden), experts, depth))
+        near, far = both_parts(block)
+        sums = gate_up(order, near_places, gate_weight, up_weight, near, None)
+        hidden = gate_up(order, far_places, gate_weight, up_weight, far, sums)
+        near, far = both_parts(hidden)
+        partial = down_first(order, near_places, down_weight, near)
+        return tuple(
+            down_last(order, far_places, offsets, counts, k, down_weight, far, partial, experts, depth)
+        )
 
     def no_rows(k, blocks):
         return tuple(jnp.zeros_like(block) for block in blocks)
 
     waiting = []
-    results = weights
+    results = gathered
     for k in range(BATCHES):
         moving = later[k] if k < BATCHES - 1 else None
         blocks, moving = after((arrived[k], moving), results, arrived[k])
         if moving is not None:
             arrived.append([moving[0]] + [along_expert(moving[shift], shift) for shift in range(1, experts)])
+        if k == 0:
+            gathered = after(gathered, blocks)
+            gathered = jnp.concatenate([gathered, swap_expert(gathered, expert_bits[-1])])
         results = lax.cond(
-            jnp.sum(counts[k]) > 0, functools.partial(expert_rows, k), functools.partial(no_rows, k), list(blocks)
+            present[k], functools.partial(expert_rows, k), functools.partial(no_rows, k), list(blocks)
         )
+        if moving is not None:
+            results, arrived[k + 1] = lax.optimization_barrier((results, arrived[k + 1]))
+        if k == 0:
+            results = after(results, gathered)
+        else:
+            results, waiting[k - 1] = lax.optimization_barrier((results, waiting[k - 1]))
         waiting.append([results[0]] + [along_expert(results[shift], -shift) for shift in range(1, experts)])
+    weights = slot_weights(place, logits, after(gathered, results), code)
     total = None
     for k in range(BATCHES):
-        blocks = waiting[k] if k == BATCHES - 1 else after(waiting[k], results)
-        total = combine(code, weights, k, blocks, total)
+        total = combine(code, weights, k, waiting[k], total)
     return total
 
 

time: 137 us -> 134 us (0.978)
  waiting for transfers between devices: 72 us -> 64.8 us
  Pallas kernels: 27.9 us -> 31.7 us
  local copies, waits for them, and re-layouts: 4.55 us -> 1.51 us
  starting transfers between devices: 29.4 us -> 31.3 us
    ppermute x15 -> x12, waiting for transfers between devices: 32 us -> 21.4 us  [along_expert(): lax.ppermute(x, 'expert', [(i, (i + shift) % experts) for i in range(expe...]
    ppermute x0 -> x2, waiting for transfers between devices: none -> 8.96 us  [swap_expert(): return lax.ppermute(x, 'expert', [(i, i ^ bit) for i in range(experts)])]
    ppermute x14, waiting for transfers between devices: 40.1 us -> 34.4 us  [swap(): return lax.ppermute(x, 'dp', [(i, i ^ bit) for i in range(width_parts)])]
    unnamed x8 -> x3, local copies, waits for them, and re-layouts: 3.84 us -> 0.01 us
    pallas_call x4 -> x8, Pallas kernels: 14.4 us -> 16.8 us  [the longest x4 8.49 us: gate_up(): pl.pallas_call(functools.partial(gate_up_kernel, parts, places, last), ou...]
    ppermute x15 -> x12, starting transfers between devices: 21.5 us -> 21.8 us  [along_expert(): lax.ppermute(x, 'expert', [(i, (i + shift) % experts) for i in range(expe...]
  transfers between devices with their start and end apart: 29 -> 28, of which waited for: 13 -> 10; matrix products, arithmetic and copies ran while one was open for 1% -> 2% of each run, Pallas kernels for 16% -> 19%
where the time goes in v4:
time: 134 us; the launch traced here: 133 us
  waiting for transfers between devices  64.8 us (48%)
  Pallas kernels  31.7 us (24%)
  starting transfers between devices  31.3 us (23%)
  other arithmetic  2.32 us (2%)
  local copies, waits for them, and re-layouts  1.51 us (1%)
  between operations  1.37 us (1%)
    ppermute x14, waiting for transfers between devices, swap(): return lax.ppermute(x, 'dp', [(i, i ^ bit) for i in range(width_parts)])  34.4 us
    ppermute x12, starting transfers between devices, along_expert(): lax.ppermute(x, 'expert', [(i, (i + shift) % experts) for i in range(expe...  21.8 us
    ppermute x12, waiting for transfers between devices, along_expert(): lax.ppermute(x, 'expert', [(i, (i + shift) % experts) for i in range(expe...  21.4 us
    ppermute x2, waiting for transfers between devices, swap_expert(): return lax.ppermute(x, 'expert', [(i, i ^ bit) for i in range(experts)])  8.96 us
    pallas_call x4, Pallas kernels, gate_up(): pl.pallas_call(functools.partial(gate_up_kernel, parts, places, last), ou...  8.49 us
    ppermute x14, starting transfers between devices, swap(): return lax.ppermute(x, 'dp', [(i, i ^ bit) for i in range(width_parts)])  8.27 us
    pallas_call x2, Pallas kernels, down_last(): pl.pallas_call(functools.partial(down_last_kernel, parts, places, experts...  5.36 us
    pallas_call x2, Pallas kernels, compact(): pl.pallas_call(functools.partial(compact_kernel, experts, k), out_shape=j...  4.27 us
  transfers between devices with their start and end apart: 28, of which 10 were waited for; matrix products, arithmetic and copies ran while one was open for 2% of the time, Pallas kernels for 19%

profile of v4, /device:TPU:0, one launch (start us, length us, event | category | flops | bytes accessed | tf_op | source)
XLA Modules:
  0.0 133.2 jit_solution(15345468939663109899)
XLA Ops:
  0.0 3.9 %shard_map.64 = (s32[4,512]{1,0:T(4,128)S(1)}, f32[4,512]{1,0:T(4,128)S(1)}, bf16[128,1024]{1,0:T(8,128)(2,1)S(1)}, bf16[128,1024]{1,0:T(8,128)(2,1)}, bf16[128,...) custom-call(s32[1]{0:T(128)} %bitcast.1.place_ref, s32[4,512]{1,0:T(4,128)} %picks_in.1, bf16[4,1024]{1,0:T(4,128)(2,1)} %bitcast.8, ...), custom_call_target="tpu_custom_call" | custom-call | flops 1024 | bytes 1024 | tf_op jit(solution)/shard_map/pallas_call | solution.py:106
  3.9 3.1 %collective-permute-start.15 = (bf16[128,1024]{1,0:T(8,128)(2,1)}, bf16[128,1024]{1,0:T(8,128)(2,1)S(1)}, u32[]{:S(2)}, u32[]{:S(2)}) collective-permute-start(bf16[128,1024]{1,0:T(8,128)(2,1)} %get-tuple-element.141), channel_id=1, source_target_pairs={{0,4},{4,8},{8,12},{12,0},{1,5},{5,9},{9,13},{13,1},{2,6},{6,10},{... | collective-permute-start | bytes 786440 | tf_op jit(solution)/shard_map/ppermute | solution.py:424
  7.0 2.6 %collective-permute-start.16 = (bf16[128,1024]{1,0:T(8,128)(2,1)}, bf16[128,1024]{1,0:T(8,128)(2,1)S(1)}, u32[]{:S(2)}, u32[]{:S(2)}) collective-permute-start(bf16[128,1024]{1,0:T(8,128)(2,1)} %get-tuple-element.142), channel_id=1, source_target_pairs={{0,8},{4,12},{8,0},{12,4},{1,9},{5,13},{9,1},{13,5},{2,10},{6,14},... | collective-permute-start | bytes 786440 | tf_op jit(solution)/shard_map/ppermute | solution.py:424
  13.3 14.3 %conditional.3 = (bf16[128,1024]{1,0:T(8,128)(2,1)S(1)}, bf16[128,1024]{1,0:T(8,128)(2,1)}, bf16[128,1024]{1,0:T(8,128)(2,1)}, bf16[128,1024]{1,0:T(8,128)(2,1)}...) conditional(s32[]{:T(128)} %convert_element_type.15, () %tuple.36, (s32[4,512]{1,0:T(4,128)S(1)}, ...), branch_computations={%region_3.4_spmd, %region_4.5_spmd} | conditional | flops 9216 | bytes 1073216 | solution.py:481
  14.8 2.2 %collective-permute-done.12 = f32[4,512]{1,0:T(4,128)S(1)} collective-permute-done((f32[4,512]{1,0:T(4,128)S(1)}, f32[4,512]{1,0:T(4,128)S(1)}, u32[]{:S(2)}, u32[]{:S(2)}) %collective-permute-start.12) | collective-permute-done | bytes 8224 | tf_op jit(solution)/shard_map/cond/branch_1_fun/ppermute | solution.py:427
  19.5 2.6 %branch_1_fun.11 = (bf16[128,1024]{1,0:T(8,128)(2,1)S(1)}, bf16[128,1024]{1,0:T(8,128)(2,1)}, bf16[128,1024]{1,0:T(8,128)(2,1)}, bf16[128,1024]{1,0:T(8,128)(2,1)}) custom-call(s32[4,512]{1,0:T(4,128)S(1)} %get-tuple-element.51.code_ref, bf16[512,1024]{1,0:T(8,128)(2,1)} %get-tuple-element.52.tokens_ref), custom_call_target="tpu_custom_call" | custom-call | flops 1024 | bytes 1024 | tf_op jit(solution)/shard_map/cond/branch_1_fun/pallas_call | solution.py:137
  22.0 4.9 %collective-permute-done.14 = f32[1,4,512]{2,1,0:T(4,128)S(1)} collective-permute-done((f32[1,4,512]{2,1,0:T(4,128)}, f32[1,4,512]{2,1,0:T(4,128)S(1)}, u32[]{:S(2)}, u32[]{:S(2)}) %collective-permute-start.14) | collective-permute-done | bytes 8224 | tf_op jit(solution)/shard_map/cond/branch_1_fun/ppermute | solution.py:443
  27.6 5.4 %collective-permute-start.19 = (bf16[128,1024]{1,0:T(8,128)(2,1)}, bf16[128,1024]{1,0:T(8,128)(2,1)}, u32[]{:S(2)}, u32[]{:S(2)}) collective-permute-start(bf16[128,1024]{1,0:T(8,128)(2,1)} %get-tuple-element.158), channel_id=1, source_target_pairs={{0,4},{4,8},{8,12},{12,0},{1,5},{5,9},{9,13},{13,1},{2,6},{6,10},{... | collective-permute-start | bytes 786440 | tf_op jit(solution)/shard_map/ppermute | solution.py:424
  35.5 30.7 %conditional.4 = ((bf16[128,1024]{1,0:T(8,128)(2,1)S(1)}, bf16[128,1024]{1,0:T(8,128)(2,1)}, bf16[128,1024]{1,0:T(8,128)(2,1)}, bf16[128,1024]{1,0:T(8,128)(2,1)})) conditional(s32[]{:T(128)} %convert_element_type.15, () %tuple.41, (s32[2,4]{1,0:T(2,128)S(1)}, s32[2,4]{1,0:T(2,128)S(1)}, bf16[128,1024]{1,0:T(8,128)(2,1)S(1)}, ...), branch_computations={%region_6.7_spmd, %region_7.8_spmd} | conditional | flops 5120 | bytes 26744168 | solution.py:507
  36.2 2.1 %branch_1_fun.12.refs_0_ = bf16[256,1024]{1,0:T(8,128)(2,1)S(1)} custom-call(s32[2,4]{1,0:T(2,128)S(1)} %get-tuple-element.59.offset_ref, s32[2,4]{1,0:T(2,128)S(1)} %get-tuple-element.60.count_ref, bf16[128,1024]{1,0:T(8,128)(2,1)S(1)} %get-tuple-element.64.refs_0_, bf16[128,1024]{1,0:T(8,128)(2,1)S(1)} %get-tuple-element.65.refs_1_, ...), custom_call_target="tpu_custom_call" | custom-call | flops 1024 | bytes 1024 | tf_op jit(solution)/shard_map/cond/branch_1_fun/pallas_call | solution.py:174
  38.4 1.6 %collective-permute-start = (bf16[256,1024]{1,0:T(8,128)(2,1)S(1)}, bf16[256,1024]{1,0:T(8,128)(2,1)S(1)}, u32[]{:S(2)}, u32[]{:S(2)}) collective-permute-start(bf16[256,1024]{1,0:T(8,128)(2,1)S(1)} %branch_1_fun.12.refs_0_), channel_id=1, source_target_pairs={{0,2},{1,3},{2,0},{3,1},{4,6},{5,7},{6,4},{7,5},{8,10},{9,11},{10,... | collective-permute-start | bytes 1572872 | tf_op jit(solution)/shard_map/cond/branch_1_fun/ppermute | solution.py:427
  39.9 11.8 %collective-permute-done.refs_0_ = bf16[256,1024]{1,0:T(8,128)(2,1)S(1)} collective-permute-done((bf16[256,1024]{1,0:T(8,128)(2,1)S(1)}, bf16[256,1024]{1,0:T(8,128)(2,1)S(1)}, u32[]{:S(2)}, u32[]{:S(2)}) %collective-permute-start) | collective-permute-done | bytes 524320 | tf_op jit(solution)/shard_map/cond/branch_1_fun/ppermute | solution.py:427
  51.7 2.6 %branch_1_fun.13 = (f32[256,256]{1,0:T(8,128)S(1)}, f32[256,256]{1,0:T(8,128)S(1)}) custom-call(s32[4]{0:T(128)S(1)} %get-tuple-element.58.order_ref, bf16[1,4096,256]{2,1,0:T(8,128)(2,1)S(1)} %get-tuple-element.62.gate_ref, bf16[1,4096,256]{2,1,0:T(8,128)(2,1)} %get-tuple-element.63.up_ref, bf16[256,1024]{1,0:T(8,128)(2,1)S(1)} %branch_1_fun.12.refs_0_, ...), custom_call_target="tpu_custom_call" | custom-call | flops 1024 | bytes 1024 | tf_op jit(solution)/shard_map/cond/branch_1_fun/pallas_call | solution.py:226
  54.4 1.6 %branch_1_fun.14.refs_0_ = bf16[256,256]{1,0:T(8,128)(2,1)S(1)} custom-call(s32[4]{0:T(128)S(1)} %get-tuple-element.58.order_ref, bf16[1,4096,256]{2,1,0:T(8,128)(2,1)S(1)} %get-tuple-element.62.gate_ref, bf16[1,4096,256]{2,1,0:T(8,128)(2,1)S(1)} %copy-done.1, bf16[256,1024]{1,0:T(8,128)(2,1)S(1)} %collective-permute-done.refs_0_, ...), custom_call_target="tpu_custom_call" | custom-call | flops 1024 | bytes 1024 | tf_op jit(solution)/shard_map/cond/branch_1_fun/pallas_call | solution.py:226
  56.0 1.6 %collective-permute-start.3 = (bf16[256,256]{1,0:T(8,128)(2,1)S(1)}, bf16[256,256]{1,0:T(8,128)(2,1)S(1)}, u32[]{:S(2)}, u32[]{:S(2)}) collective-permute-start(bf16[256,256]{1,0:T(8,128)(2,1)S(1)} %branch_1_fun.14.refs_0_), channel_id=1, source_target_pairs={{0,2},{1,3},{2,0},{3,1},{4,6},{5,7},{6,4},{7,5},{8,10},{9,11},{10,... | collective-permute-start | bytes 393224 | tf_op jit(solution)/shard_map/cond/branch_1_fun/ppermute | solution.py:427
  57.8 4.2 %collective-permute-done.3.refs_0_ = bf16[256,256]{1,0:T(8,128)(2,1)S(1)} collective-permute-done((bf16[256,256]{1,0:T(8,128)(2,1)S(1)}, bf16[256,256]{1,0:T(8,128)(2,1)S(1)}, u32[]{:S(2)}, u32[]{:S(2)}) %collective-permute-start.3) | collective-permute-done | bytes 131104 | tf_op jit(solution)/shard_map/cond/branch_1_fun/ppermute | solution.py:427
  63.5 2.7 %branch_1_fun.16 = (bf16[128,1024]{1,0:T(8,128)(2,1)S(1)}, bf16[128,1024]{1,0:T(8,128)(2,1)}, bf16[128,1024]{1,0:T(8,128)(2,1)}, bf16[128,1024]{1,0:T(8,128)(2,1)}) custom-call(s32[4]{0:T(128)S(1)} %get-tuple-element.58.order_ref, s32[2,4]{1,0:T(2,128)S(1)} %get-tuple-element.59.offset_ref, s32[2,4]{1,0:T(2,128)S(1)} %get-tuple-element.60.count_ref, ...), custom_call_target="tpu_custom_call" | custom-call | flops 1024 | bytes 1024 | tf_op jit(solution)/shard_map/cond/branch_1_fun/pallas_call | solution.py:314
  66.8 4.1 %collective-permute-done.18 = f32[2,4,512]{2,1,0:T(4,128)S(1)} collective-permute-done((f32[2,4,512]{2,1,0:T(4,128)S(1)}, f32[2,4,512]{2,1,0:T(4,128)S(1)}, u32[]{:S(2)}, u32[]{:S(2)}) %collective-permute-start.18) | collective-permute-done | bytes 16416 | tf_op jit(solution)/shard_map/ppermute | solution.py:443
  70.9 1.8 %collective-permute-start.22 = (bf16[128,1024]{1,0:T(8,128)(2,1)}, bf16[128,1024]{1,0:T(8,128)(2,1)S(1)}, u32[]{:S(2)}, u32[]{:S(2)}) collective-permute-start(bf16[128,1024]{1,0:T(8,128)(2,1)} %get-tuple-element.170), channel_id=1, source_target_pairs={{0,12},{4,0},{8,4},{12,8},{1,13},{5,1},{9,5},{13,9},{2,14},{6,2},{... | collective-permute-start | bytes 786440 | tf_op jit(solution)/shard_map/ppermute | solution.py:424
  74.1 29.1 %conditional.5 = ((bf16[128,1024]{1,0:T(8,128)(2,1)S(1)}, bf16[128,1024]{1,0:T(8,128)(2,1)}, bf16[128,1024]{1,0:T(8,128)(2,1)}, bf16[128,1024]{1,0:T(8,128)(2,1)})) conditional(s32[]{:T(128)} %convert_element_type.16, () %tuple.40, (s32[2,4]{1,0:T(2,128)S(1)}, s32[2,4]{1,0:T(2,128)S(1)}, bf16[128,1024]{1,0:T(8,128)(2,1)S(1)}, ...), branch_computations={%region_8.9_spmd, %region_9.10_spmd} | conditional | flops 5120 | bytes 24646960 | solution.py:507
  74.1 2.2 %branch_1_fun.17.refs_0_ = bf16[256,1024]{1,0:T(8,128)(2,1)S(1)} custom-call(s32[2,4]{1,0:T(2,128)S(1)} %get-tuple-element.71.offset_ref, s32[2,4]{1,0:T(2,128)S(1)} %get-tuple-element.72.count_ref, bf16[128,1024]{1,0:T(8,128)(2,1)S(1)} %get-tuple-element.76.refs_0_, bf16[128,1024]{1,0:T(8,128)(2,1)} %get-tuple-element.77.refs_1_, ...), custom_call_target="tpu_custom_call" | custom-call | flops 1024 | bytes 1024 | tf_op jit(solution)/shard_map/cond/branch_1_fun/pallas_call | solution.py:174
  76.3 1.6 %collective-permute-start.6 = (bf16[256,1024]{1,0:T(8,128)(2,1)S(1)}, bf16[256,1024]{1,0:T(8,128)(2,1)S(1)}, u32[]{:S(2)}, u32[]{:S(2)}) collective-permute-start(bf16[256,1024]{1,0:T(8,128)(2,1)S(1)} %branch_1_fun.17.refs_0_), channel_id=1, source_target_pairs={{0,2},{1,3},{2,0},{3,1},{4,6},{5,7},{6,4},{7,5},{8,10},{9,11},{10,... | collective-permute-start | bytes 1572872 | tf_op jit(solution)/shard_map/cond/branch_1_fun/ppermute | solution.py:427
  77.9 10.9 %collective-permute-done.6.refs_0_ = bf16[256,1024]{1,0:T(8,128)(2,1)S(1)} collective-permute-done((bf16[256,1024]{1,0:T(8,128)(2,1)S(1)}, bf16[256,1024]{1,0:T(8,128)(2,1)S(1)}, u32[]{:S(2)}, u32[]{:S(2)}) %collective-permute-start.6) | collective-permute-done | bytes 524320 | tf_op jit(solution)/shard_map/cond/branch_1_fun/ppermute | solution.py:427
  88.8 2.6 %branch_1_fun.18 = (f32[256,256]{1,0:T(8,128)S(1)}, f32[256,256]{1,0:T(8,128)S(1)}) custom-call(s32[4]{0:T(128)S(1)} %get-tuple-element.70.order_ref, bf16[1,4096,256]{2,1,0:T(8,128)(2,1)S(1)} %get-tuple-element.74.gate_ref, bf16[1,4096,256]{2,1,0:T(8,128)(2,1)} %get-tuple-element.75.up_ref, bf16[256,1024]{1,0:T(8,128)(2,1)S(1)} %branch_1_fun.17.refs_0_, ...), custom_call_target="tpu_custom_call" | custom-call | flops 1024 | bytes 1024 | tf_op jit(solution)/shard_map/cond/branch_1_fun/pallas_call | solution.py:226
  91.5 1.6 %branch_1_fun.19.refs_0_ = bf16[256,256]{1,0:T(8,128)(2,1)S(1)} custom-call(s32[4]{0:T(128)S(1)} %get-tuple-element.70.order_ref, bf16[1,4096,256]{2,1,0:T(8,128)(2,1)S(1)} %get-tuple-element.74.gate_ref, bf16[1,4096,256]{2,1,0:T(8,128)(2,1)S(1)} %copy-done.2, bf16[256,1024]{1,0:T(8,128)(2,1)S(1)} %collective-permute-done.6.refs_0_, ...), custom_call_target="tpu_custom_call" | custom-call | flops 1024 | bytes 1024 | tf_op jit(solution)/shard_map/cond/branch_1_fun/pallas_call | solution.py:226
  93.1 1.6 %collective-permute-start.9 = (bf16[256,256]{1,0:T(8,128)(2,1)S(1)}, bf16[256,256]{1,0:T(8,128)(2,1)S(1)}, u32[]{:S(2)}, u32[]{:S(2)}) collective-permute-start(bf16[256,256]{1,0:T(8,128)(2,1)S(1)} %branch_1_fun.19.refs_0_), channel_id=1, source_target_pairs={{0,2},{1,3},{2,0},{3,1},{4,6},{5,7},{6,4},{7,5},{8,10},{9,11},{10,... | collective-permute-start | bytes 393224 | tf_op jit(solution)/shard_map/cond/branch_1_fun/ppermute | solution.py:427
  94.9 4.2 %collective-permute-done.9.refs_0_ = bf16[256,256]{1,0:T(8,128)(2,1)S(1)} collective-permute-done((bf16[256,256]{1,0:T(8,128)(2,1)S(1)}, bf16[256,256]{1,0:T(8,128)(2,1)S(1)}, u32[]{:S(2)}, u32[]{:S(2)}) %collective-permute-start.9) | collective-permute-done | bytes 131104 | tf_op jit(solution)/shard_map/cond/branch_1_fun/ppermute | solution.py:427
  100.6 2.7 %branch_1_fun.21 = (bf16[128,1024]{1,0:T(8,128)(2,1)S(1)}, bf16[128,1024]{1,0:T(8,128)(2,1)}, bf16[128,1024]{1,0:T(8,128)(2,1)}, bf16[128,1024]{1,0:T(8,128)(2,1)}) custom-call(s32[4]{0:T(128)S(1)} %get-tuple-element.70.order_ref, s32[2,4]{1,0:T(2,128)S(1)} %get-tuple-element.71.offset_ref, s32[2,4]{1,0:T(2,128)S(1)} %get-tuple-element.72.count_ref, ...), custom_call_target="tpu_custom_call" | custom-call | flops 1024 | bytes 1024 | tf_op jit(solution)/shard_map/cond/branch_1_fun/pallas_call | solution.py:314
  103.3 3.2 %collective-permute-start.25 = (bf16[128,1024]{1,0:T(8,128)(2,1)}, bf16[128,1024]{1,0:T(8,128)(2,1)S(1)}, u32[]{:S(2)}, u32[]{:S(2)}) collective-permute-start(bf16[128,1024]{1,0:T(8,128)(2,1)} %get-tuple-element.182), channel_id=1, source_target_pairs={{0,12},{4,0},{8,4},{12,8},{1,13},{5,1},{9,5},{13,9},{2,14},{6,2},{... | collective-permute-start | bytes 786440 | tf_op jit(solution)/shard_map/ppermute | solution.py:424
  109.8 3.8 %collective-permute-done.25.refs_1_ = bf16[128,1024]{1,0:T(8,128)(2,1)S(1)} collective-permute-done((bf16[128,1024]{1,0:T(8,128)(2,1)}, bf16[128,1024]{1,0:T(8,128)(2,1)S(1)}, u32[]{:S(2)}, u32[]{:S(2)}) %collective-permute-start.25) | collective-permute-done | bytes 262176 | tf_op jit(solution)/shard_map/ppermute | solution.py:424
  113.6 17.6 %collective-permute-done.26.refs_2_ = bf16[128,1024]{1,0:T(8,128)(2,1)S(1)} collective-permute-done((bf16[128,1024]{1,0:T(8,128)(2,1)}, bf16[128,1024]{1,0:T(8,128)(2,1)S(1)}, u32[]{:S(2)}, u32[]{:S(2)}) %collective-permute-start.26) | collective-permute-done | bytes 262176 | tf_op jit(solution)/shard_map/ppermute | solution.py:424
  131.1 2.1 %shard_map.67 = bf16[512,1024]{1,0:T(8,128)(2,1)} custom-call(s32[4,512]{1,0:T(4,128)S(1)} %get-tuple-element.136.code_ref, f32[4,512]{1,0:T(4,128)S(1)} %shard_map.65.weight_ref, bf16[128,1024]{1,0:T(8,128)(2,1)S(1)} %get-tuple-element.181.refs_0_, bf16[128,1024]{1,0:T(8,128)(2,1)S(1)} %collective-permute-done.25.refs_1_, ...), custom_call_target="tpu_custom_call" | custom-call | flops 1024 | bytes 1024 | tf_op jit(solution)/shard_map/pallas_call | solution.py:393
  (69 shorter events, 19.1 us)
Async XLA Ops:
  0.0 35.5 %copy-start = (bf16[1,4096,256]{2,1,0:T(8,128)(2,1)S(1)}, bf16[1,4096,256]{2,1,0:T(8,128)(2,1)}, u32[]{:S(2)}) copy-start(bf16[1,4096,256]{2,1,0:T(8,128)(2,1)} %param.14) | copy-start | bytes 6291460
  3.9 23.7 %collective-permute-start.15 = (bf16[128,1024]{1,0:T(8,128)(2,1)}, bf16[128,1024]{1,0:T(8,128)(2,1)S(1)}, u32[]{:S(2)}, u32[]{:S(2)}) collective-permute-start(bf16[128,1024]{1,0:T(8,128)(2,1)} %get-tuple-element.141), channel_id=1, source_target_pairs={{0,4},{4,8},{8,12},{12,0},{1,5},{5,9},{9,13},{13,1},{2,6},{6,10},{... | collective-permute-start | bytes 786440 | tf_op jit(solution)/shard_map/ppermute | solution.py:424
  7.0 20.7 %collective-permute-start.16 = (bf16[128,1024]{1,0:T(8,128)(2,1)}, bf16[128,1024]{1,0:T(8,128)(2,1)S(1)}, u32[]{:S(2)}, u32[]{:S(2)}) collective-permute-start(bf16[128,1024]{1,0:T(8,128)(2,1)} %get-tuple-element.142), channel_id=1, source_target_pairs={{0,8},{4,12},{8,0},{12,4},{1,9},{5,13},{9,1},{13,5},{2,10},{6,14},... | collective-permute-start | bytes 786440 | tf_op jit(solution)/shard_map/ppermute | solution.py:424
  9.6 18.1 %collective-permute-start.17 = (bf16[128,1024]{1,0:T(8,128)(2,1)}, bf16[128,1024]{1,0:T(8,128)(2,1)S(1)}, u32[]{:S(2)}, u32[]{:S(2)}) collective-permute-start(bf16[128,1024]{1,0:T(8,128)(2,1)} %get-tuple-element.143), channel_id=1, source_target_pairs={{0,12},{4,0},{8,4},{12,8},{1,13},{5,1},{9,5},{13,9},{2,14},{6,2},{... | collective-permute-start | bytes 786440 | tf_op jit(solution)/shard_map/ppermute | solution.py:424
  13.3 3.7 %collective-permute-start.12 = (f32[4,512]{1,0:T(4,128)S(1)}, f32[4,512]{1,0:T(4,128)S(1)}, u32[]{:S(2)}, u32[]{:S(2)}) collective-permute-start(f32[4,512]{1,0:T(4,128)S(1)} %get-tuple-element.57), channel_id=1, source_target_pairs={{0,2},{1,3},{2,0},{3,1},{4,6},{5,7},{6,4},{7,5},{8,10},{9,11},{10,... | collective-permute-start | bytes 24584 | tf_op jit(solution)/shard_map/cond/branch_1_fun/ppermute | solution.py:427
  17.0 1.2 collective-permute-start.13
  18.8 8.1 %collective-permute-start.14 = (f32[1,4,512]{2,1,0:T(4,128)}, f32[1,4,512]{2,1,0:T(4,128)S(1)}, u32[]{:S(2)}, u32[]{:S(2)}) collective-permute-start(f32[1,4,512]{2,1,0:T(4,128)} %bitcast), channel_id=1, source_target_pairs={{0,4},{4,0},{8,12},{12,8},{1,5},{5,1},{9,13},{13,9},{2,6},{6,2},{1... | collective-permute-start | bytes 24584 | tf_op jit(solution)/shard_map/cond/branch_1_fun/ppermute | solution.py:443
  27.6 43.3 %collective-permute-start.19 = (bf16[128,1024]{1,0:T(8,128)(2,1)}, bf16[128,1024]{1,0:T(8,128)(2,1)}, u32[]{:S(2)}, u32[]{:S(2)}) collective-permute-start(bf16[128,1024]{1,0:T(8,128)(2,1)} %get-tuple-element.158), channel_id=1, source_target_pairs={{0,4},{4,8},{8,12},{12,0},{1,5},{5,9},{9,13},{13,1},{2,6},{6,10},{... | collective-permute-start | bytes 786440 | tf_op jit(solution)/shard_map/ppermute | solution.py:424
  33.0 37.9 %collective-permute-start.20 = (bf16[128,1024]{1,0:T(8,128)(2,1)}, bf16[128,1024]{1,0:T(8,128)(2,1)}, u32[]{:S(2)}, u32[]{:S(2)}) collective-permute-start(bf16[128,1024]{1,0:T(8,128)(2,1)} %get-tuple-element.159), channel_id=1, source_target_pairs={{0,8},{4,12},{8,0},{12,4},{1,9},{5,13},{9,1},{13,5},{2,10},{6,14},... | collective-permute-start | bytes 786440 | tf_op jit(solution)/shard_map/ppermute | solution.py:424
  34.6 36.3 %collective-permute-start.21 = (bf16[128,1024]{1,0:T(8,128)(2,1)}, bf16[128,1024]{1,0:T(8,128)(2,1)}, u32[]{:S(2)}, u32[]{:S(2)}) collective-permute-start(bf16[128,1024]{1,0:T(8,128)(2,1)} %get-tuple-element.160), channel_id=1, source_target_pairs={{0,12},{4,0},{8,4},{12,8},{1,13},{5,1},{9,5},{13,9},{2,14},{6,2},{... | collective-permute-start | bytes 786440 | tf_op jit(solution)/shard_map/ppermute | solution.py:424
  38.4 13.4 %collective-permute-start = (bf16[256,1024]{1,0:T(8,128)(2,1)S(1)}, bf16[256,1024]{1,0:T(8,128)(2,1)S(1)}, u32[]{:S(2)}, u32[]{:S(2)}) collective-permute-start(bf16[256,1024]{1,0:T(8,128)(2,1)S(1)} %branch_1_fun.12.refs_0_), channel_id=1, source_target_pairs={{0,2},{1,3},{2,0},{3,1},{4,6},{5,7},{6,4},{7,5},{8,10},{9,11},{10,... | collective-permute-start | bytes 1572872 | tf_op jit(solution)/shard_map/cond/branch_1_fun/ppermute | solution.py:427
  39.9 11.8 %collective-permute-start.2 = (bf16[256,1024]{1,0:T(8,128)(2,1)S(1)}, bf16[256,1024]{1,0:T(8,128)(2,1)S(1)}, u32[]{:S(2)}, u32[]{:S(2)}) collective-permute-start(bf16[256,1024]{1,0:T(8,128)(2,1)S(1)} %branch_1_fun.12.refs_0_), channel_id=1, source_target_pairs={{0,1},{1,0},{2,3},{3,2},{4,5},{5,4},{6,7},{7,6},{8,9},{9,8},{10,11... | collective-permute-start | bytes 1572872 | tf_op jit(solution)/shard_map/cond/branch_1_fun/ppermute | solution.py:427
  51.7 2.6 %collective-permute-start.1 = (bf16[256,1024]{1,0:T(8,128)(2,1)S(1)}, bf16[256,1024]{1,0:T(8,128)(2,1)S(1)}, u32[]{:S(2)}, u32[]{:S(2)}) collective-permute-start(bf16[256,1024]{1,0:T(8,128)(2,1)S(1)} %collective-permute-done.refs_0_), channel_id=1, source_target_pairs={{0,1},{1,0},{2,3},{3,2},{4,5},{5,4},{6,7},{7,6},{8,9},{9,8},{10,11... | collective-permute-start | bytes 1572872 | tf_op jit(solution)/shard_map/cond/branch_1_fun/ppermute | solution.py:427
  51.7 2.6 %copy-start.1 = (bf16[1,4096,256]{2,1,0:T(8,128)(2,1)S(1)}, bf16[1,4096,256]{2,1,0:T(8,128)(2,1)}, u32[]{:S(2)}) copy-start(bf16[1,4096,256]{2,1,0:T(8,128)(2,1)} %get-tuple-element.63.up_ref) | copy-start | bytes 6291460 | tf_op jit(solution)/shard_map/cond
  54.4 7.6 %copy-start.3 = (bf16[1,1024,1024]{2,1,0:T(8,128)(2,1)S(1)}, bf16[1,1024,1024]{2,1,0:T(8,128)(2,1)}, u32[]{:S(2)}) copy-start(bf16[1,1024,1024]{2,1,0:T(8,128)(2,1)} %get-tuple-element.61.down_ref) | copy-start | bytes 6291460 | tf_op jit(solution)/shard_map/cond
  56.0 6.0 %collective-permute-start.3 = (bf16[256,256]{1,0:T(8,128)(2,1)S(1)}, bf16[256,256]{1,0:T(8,128)(2,1)S(1)}, u32[]{:S(2)}, u32[]{:S(2)}) collective-permute-start(bf16[256,256]{1,0:T(8,128)(2,1)S(1)} %branch_1_fun.14.refs_0_), channel_id=1, source_target_pairs={{0,2},{1,3},{2,0},{3,1},{4,6},{5,7},{6,4},{7,5},{8,10},{9,11},{10,... | collective-permute-start | bytes 393224 | tf_op jit(solution)/shard_map/cond/branch_1_fun/ppermute | solution.py:427
  57.6 4.4 %collective-permute-start.5 = (bf16[256,256]{1,0:T(8,128)(2,1)S(1)}, bf16[256,256]{1,0:T(8,128)(2,1)S(1)}, u32[]{:S(2)}, u32[]{:S(2)}) collective-permute-start(bf16[256,256]{1,0:T(8,128)(2,1)S(1)} %branch_1_fun.14.refs_0_), channel_id=1, source_target_pairs={{0,1},{1,0},{2,3},{3,2},{4,5},{5,4},{6,7},{7,6},{8,9},{9,8},{10,11... | collective-permute-start | bytes 393224 | tf_op jit(solution)/shard_map/cond/branch_1_fun/ppermute | solution.py:427
  62.0 1.5 %collective-permute-start.4 = (bf16[256,256]{1,0:T(8,128)(2,1)S(1)}, bf16[256,256]{1,0:T(8,128)(2,1)S(1)}, u32[]{:S(2)}, u32[]{:S(2)}) collective-permute-start(bf16[256,256]{1,0:T(8,128)(2,1)S(1)} %collective-permute-done.3.refs_0_), channel_id=1, source_target_pairs={{0,1},{1,0},{2,3},{3,2},{4,5},{5,4},{6,7},{7,6},{8,9},{9,8},{10,11... | collective-permute-start | bytes 393224 | tf_op jit(solution)/shard_map/cond/branch_1_fun/ppermute | solution.py:427
  66.2 4.7 %collective-permute-start.18 = (f32[2,4,512]{2,1,0:T(4,128)S(1)}, f32[2,4,512]{2,1,0:T(4,128)S(1)}, u32[]{:S(2)}, u32[]{:S(2)}) collective-permute-start(f32[2,4,512]{2,1,0:T(4,128)S(1)} %get-tuple-element.152), channel_id=1, source_target_pairs={{0,8},{4,12},{8,0},{12,4},{1,9},{5,13},{9,1},{13,5},{2,10},{6,14},... | collective-permute-start | bytes 49160 | tf_op jit(solution)/shard_map/ppermute | solution.py:443
  70.9 32.4 %collective-permute-start.22 = (bf16[128,1024]{1,0:T(8,128)(2,1)}, bf16[128,1024]{1,0:T(8,128)(2,1)S(1)}, u32[]{:S(2)}, u32[]{:S(2)}) collective-permute-start(bf16[128,1024]{1,0:T(8,128)(2,1)} %get-tuple-element.170), channel_id=1, source_target_pairs={{0,12},{4,0},{8,4},{12,8},{1,13},{5,1},{9,5},{13,9},{2,14},{6,2},{... | collective-permute-start | bytes 786440 | tf_op jit(solution)/shard_map/ppermute | solution.py:424
  72.7 30.6 %collective-permute-start.23 = (bf16[128,1024]{1,0:T(8,128)(2,1)}, bf16[128,1024]{1,0:T(8,128)(2,1)S(1)}, u32[]{:S(2)}, u32[]{:S(2)}) collective-permute-start(bf16[128,1024]{1,0:T(8,128)(2,1)} %get-tuple-element.171), channel_id=1, source_target_pairs={{0,8},{4,12},{8,0},{12,4},{1,9},{5,13},{9,1},{13,5},{2,10},{6,14},... | collective-permute-start | bytes 786440 | tf_op jit(solution)/shard_map/ppermute | solution.py:424
  72.7 30.6 %collective-permute-start.24 = (bf16[128,1024]{1,0:T(8,128)(2,1)}, bf16[128,1024]{1,0:T(8,128)(2,1)S(1)}, u32[]{:S(2)}, u32[]{:S(2)}) collective-permute-start(bf16[128,1024]{1,0:T(8,128)(2,1)} %get-tuple-element.172), channel_id=1, source_target_pairs={{0,4},{4,8},{8,12},{12,0},{1,5},{5,9},{9,13},{13,1},{2,6},{6,10},{... | collective-permute-start | bytes 786440 | tf_op jit(solution)/shard_map/ppermute | solution.py:424
  76.3 12.5 %collective-permute-start.6 = (bf16[256,1024]{1,0:T(8,128)(2,1)S(1)}, bf16[256,1024]{1,0:T(8,128)(2,1)S(1)}, u32[]{:S(2)}, u32[]{:S(2)}) collective-permute-start(bf16[256,1024]{1,0:T(8,128)(2,1)S(1)} %branch_1_fun.17.refs_0_), channel_id=1, source_target_pairs={{0,2},{1,3},{2,0},{3,1},{4,6},{5,7},{6,4},{7,5},{8,10},{9,11},{10,... | collective-permute-start | bytes 1572872 | tf_op jit(solution)/shard_map/cond/branch_1_fun/ppermute | solution.py:427
  77.9 10.9 %collective-permute-start.8 = (bf16[256,1024]{1,0:T(8,128)(2,1)S(1)}, bf16[256,1024]{1,0:T(8,128)(2,1)S(1)}, u32[]{:S(2)}, u32[]{:S(2)}) collective-permute-start(bf16[256,1024]{1,0:T(8,128)(2,1)S(1)} %branch_1_fun.17.refs_0_), channel_id=1, source_target_pairs={{0,1},{1,0},{2,3},{3,2},{4,5},{5,4},{6,7},{7,6},{8,9},{9,8},{10,11... | collective-permute-start | bytes 1572872 | tf_op jit(solution)/shard_map/cond/branch_1_fun/ppermute | solution.py:427
  88.8 2.6 %collective-permute-start.7 = (bf16[256,1024]{1,0:T(8,128)(2,1)S(1)}, bf16[256,1024]{1,0:T(8,128)(2,1)S(1)}, u32[]{:S(2)}, u32[]{:S(2)}) collective-permute-start(bf16[256,1024]{1,0:T(8,128)(2,1)S(1)} %collective-permute-done.6.refs_0_), channel_id=1, source_target_pairs={{0,1},{1,0},{2,3},{3,2},{4,5},{5,4},{6,7},{7,6},{8,9},{9,8},{10,11... | collective-permute-start | bytes 1572872 | tf_op jit(solution)/shard_map/cond/branch_1_fun/ppermute | solution.py:427
  91.4 7.6 %copy-start.4 = (bf16[1,1024,1024]{2,1,0:T(8,128)(2,1)S(1)}, bf16[1,1024,1024]{2,1,0:T(8,128)(2,1)}, u32[]{:S(2)}) copy-start(bf16[1,1024,1024]{2,1,0:T(8,128)(2,1)} %get-tuple-element.73.down_ref) | copy-start | bytes 6291460 | tf_op jit(solution)/shard_map/cond
  93.1 6.0 %collective-permute-start.9 = (bf16[256,256]{1,0:T(8,128)(2,1)S(1)}, bf16[256,256]{1,0:T(8,128)(2,1)S(1)}, u32[]{:S(2)}, u32[]{:S(2)}) collective-permute-start(bf16[256,256]{1,0:T(8,128)(2,1)S(1)} %branch_1_fun.19.refs_0_), channel_id=1, source_target_pairs={{0,2},{1,3},{2,0},{3,1},{4,6},{5,7},{6,4},{7,5},{8,10},{9,11},{10,... | collective-permute-start | bytes 393224 | tf_op jit(solution)/shard_map/cond/branch_1_fun/ppermute | solution.py:427
  94.7 4.4 %collective-permute-start.11 = (bf16[256,256]{1,0:T(8,128)(2,1)S(1)}, bf16[256,256]{1,0:T(8,128)(2,1)S(1)}, u32[]{:S(2)}, u32[]{:S(2)}) collective-permute-start(bf16[256,256]{1,0:T(8,128)(2,1)S(1)} %branch_1_fun.19.refs_0_), channel_id=1, source_target_pairs={{0,1},{1,0},{2,3},{3,2},{4,5},{5,4},{6,7},{7,6},{8,9},{9,8},{10,11... | collective-permute-start | bytes 393224 | tf_op jit(solution)/shard_map/cond/branch_1_fun/ppermute | solution.py:427
  99.1 1.5 %collective-permute-start.10 = (bf16[256,256]{1,0:T(8,128)(2,1)S(1)}, bf16[256,256]{1,0:T(8,128)(2,1)S(1)}, u32[]{:S(2)}, u32[]{:S(2)}) collective-permute-start(bf16[256,256]{1,0:T(8,128)(2,1)S(1)} %collective-permute-done.9.refs_0_), channel_id=1, source_target_pairs={{0,1},{1,0},{2,3},{3,2},{4,5},{5,4},{6,7},{7,6},{8,9},{9,8},{10,11... | collective-permute-start | bytes 393224 | tf_op jit(solution)/shard_map/cond/branch_1_fun/ppermute | solution.py:427
  103.3 10.3 %collective-permute-start.25 = (bf16[128,1024]{1,0:T(8,128)(2,1)}, bf16[128,1024]{1,0:T(8,128)(2,1)S(1)}, u32[]{:S(2)}, u32[]{:S(2)}) collective-permute-start(bf16[128,1024]{1,0:T(8,128)(2,1)} %get-tuple-element.182), channel_id=1, source_target_pairs={{0,12},{4,0},{8,4},{12,8},{1,13},{5,1},{9,5},{13,9},{2,14},{6,2},{... | collective-permute-start | bytes 786440 | tf_op jit(solution)/shard_map/ppermute | solution.py:424
  106.5 24.6 %collective-permute-start.26 = (bf16[128,1024]{1,0:T(8,128)(2,1)}, bf16[128,1024]{1,0:T(8,128)(2,1)S(1)}, u32[]{:S(2)}, u32[]{:S(2)}) collective-permute-start(bf16[128,1024]{1,0:T(8,128)(2,1)} %get-tuple-element.183), channel_id=1, source_target_pairs={{0,8},{4,12},{8,0},{12,4},{1,9},{5,13},{9,1},{13,5},{2,10},{6,14},... | collective-permute-start | bytes 786440 | tf_op jit(solution)/shard_map/ppermute | solution.py:424
  107.4 23.8 %collective-permute-start.27 = (bf16[128,1024]{1,0:T(8,128)(2,1)}, bf16[128,1024]{1,0:T(8,128)(2,1)S(1)}, u32[]{:S(2)}, u32[]{:S(2)}) collective-permute-start(bf16[128,1024]{1,0:T(8,128)(2,1)} %get-tuple-element.184), channel_id=1, source_target_pairs={{0,4},{4,8},{8,12},{12,0},{1,5},{5,9},{9,13},{13,1},{2,6},{6,10},{... | collective-permute-start | bytes 786440 | tf_op jit(solution)/shard_map/ppermute | solution.py:424
  (3 other events, 4.1 us)

commit v5 on v4

--- a/solution.py
+++ b/solution.py
@@ -470,7 +470,7 @@
         for bit in bits:
             logits = logits + swap(logits, bit)
         gathered = logits[None]
-        for bit in expert_bits[:-1]:
+        for bit in expert_bits:
             gathered = jnp.concatenate([gathered, swap_expert(gathered, bit)])
         return later, logits, gathered
 
@@ -480,40 +480,53 @@
     arrived = [[first[0]] + [along_expert(first[shift], shift) for shift in range(1, experts)]]
     later, logits, gathered = lax.cond(present[0], beside_first, nothing_first, logits)
 
-    def expert_rows(k, blocks):
-        block = compact(offsets, counts, k, blocks, size)
-        near, far = both_parts(block)
-        sums = gate_up(order, near_places, gate_weight, up_weight, near, None)
+    def far_half(far, sums):
+        far = spread(far)
         hidden = gate_up(order, far_places, gate_weight, up_weight, far, sums)
-        near, far = both_parts(hidden)
-        partial = down_first(order, near_places, down_weight, near)
+        far = swap(hidden, bits[0])
+        partial = down_first(order, near_places, down_weight, spread(hidden))
+        far, partial = lax.optimization_barrier((far, partial))
+        return spread(far), partial
+
+    def settle(k, far, partial):
         return tuple(
             down_last(order, far_places, offsets, counts, k, down_weight, far, partial, experts, depth)
         )
 
-    def no_rows(k, blocks):
-        return tuple(jnp.zeros_like(block) for block in blocks)
+    def fenced(k, run, *operands):
+        def skip(*operands):
+            return jax.tree.map(lambda x: jnp.zeros(x.shape, x.dtype), jax.eval_shape(run, *operands))
+
+        return lax.cond(present[k], run, skip, *operands)
+
+    def send_back(results):
+        return [results[0]] + [along_expert(results[shift], -shift) for shift in range(1, experts)]
 
     waiting = []
-    results = gathered
+    far = partial = None
+    moved = gathered
     for k in range(BATCHES):
-        moving = later[k] if k < BATCHES - 1 else None
-        blocks, moving = after((arrived[k], moving), results, arrived[k])
-        if moving is not None:
+        blocks = after(arrived[k], moved)
+        if k < BATCHES - 1:
+            moving = after(later[k], blocks)
             arrived.append([moving[0]] + [along_expert(moving[shift], shift) for shift in range(1, experts)])
-        if k == 0:
-            gathered = after(gathered, blocks)
-            gathered = jnp.concatenate([gathered, swap_expert(gathered, expert_bits[-1])])
-        results = lax.cond(
-            present[k], functools.partial(expert_rows, k), functools.partial(no_rows, k), list(blocks)
-        )
-        if moving is not None:
-            results, arrived[k + 1] = lax.optimization_barrier((results, arrived[k + 1]))
-        if k == 0:
-            results = after(results, gathered)
-        else:
-            results, waiting[k - 1] = lax.optimization_barrier((results, waiting[k - 1]))
-        waiting.append([results[0]] + [along_expert(results[shift], -shift) for shift in range(1, experts)])
+        block = fenced(k, lambda *blocks: compact(offsets, counts, k, blocks, size), *blocks)
+        across = swap(block, bits[0])
+        near = spread(block)
+        if k > 0:
+            far, partial = after((far, partial), block)
+            results = fenced(k, functools.partial(settle, k - 1), far, partial)
+            if k > 1:
+                results, waiting[k - 2] = lax.optimization_barrier((results, waiting[k - 2]))
+            waiting.append(send_back(results))
+            near = after(near, results)
+        sums = fenced(k, lambda *near: gate_up(order, near_places, gate_weight, up_weight, near, None), *near)
+        across, sums = lax.optimization_barrier((across, sums))
+        far, partial = fenced(k, far_half, across, sums)
+        moved = partial
+    results = fenced(0, functools.partial(settle, BATCHES - 1), far, partial)
+    results, waiting[-1] = lax.optimization_barrier((results, waiting[-1]))
+    waiting.append(send_back(results))
     weights = slot_weights(place, logits, after(gathered, results), code)
     total = None
     for k in range(BATCHES):

time: 134 us -> 126 us (0.940)
  waiting for transfers between devices: 64.8 us -> 56 us
  Pallas kernels: 31.7 us -> 37.2 us
  starting transfers between devices: 31.3 us -> 26.2 us
    ppermute x14, waiting for transfers between devices: 34.4 us -> 25.1 us  [swap(): return lax.ppermute(x, 'dp', [(i, i ^ bit) for i in range(width_parts)])]
    ppermute x12, starting transfers between devices: 21.8 us -> 16.5 us  [along_expert(): lax.ppermute(x, 'expert', [(i, (i + shift) % experts) for i in range(expe...]
    pallas_call x4, Pallas kernels: 8.49 us -> 12 us  [gate_up(): pl.pallas_call(functools.partial(gate_up_kernel, parts, places, last), ou...]
  transfers between devices with their start and end apart: 28 -> 28, of which waited for: 10 -> 14; matrix products, arithmetic and copies ran while one was open for 2% -> 3% of each run, Pallas kernels for 19% -> 21%
where the time goes in v5:
time: 126 us
  waiting for transfers between devices  56 us (44%)
  Pallas kernels  37.2 us (30%)
  starting transfers between devices  26.2 us (21%)
  other arithmetic  3.05 us (2%)
  local copies, waits for them, and re-layouts  1.51 us (1%)
  between operations  1.49 us (1%)
    ppermute x14, waiting for transfers between devices, swap(): return lax.ppermute(x, 'dp', [(i, i ^ bit) for i in range(width_parts)])  25.1 us
    ppermute x12, waiting for transfers between devices, along_expert(): lax.ppermute(x, 'expert', [(i, (i + shift) % experts) for i in range(expe...  21.3 us
    ppermute x12, starting transfers between devices, along_expert(): lax.ppermute(x, 'expert', [(i, (i + shift) % experts) for i in range(expe...  16.5 us
    pallas_call x4, Pallas kernels, gate_up(): pl.pallas_call(functools.partial(gate_up_kernel, parts, places, last), ou...  12 us
    ppermute x2, waiting for transfers between devices, swap_expert(): return lax.ppermute(x, 'expert', [(i, i ^ bit) for i in range(experts)])  9.55 us
    ppermute x14, starting transfers between devices, swap(): return lax.ppermute(x, 'dp', [(i, i ^ bit) for i in range(width_parts)])  8.35 us
    pallas_call x2, Pallas kernels, down_last(): pl.pallas_call(functools.partial(down_last_kernel, parts, places, experts...  6.6 us
    pallas_call x2, Pallas kernels, compact(): pl.pallas_call(functools.partial(compact_kernel, experts, k), out_shape=j...  4.96 us
  transfers between devices with their start and end apart: 28, of which 14 were waited for; matrix products, arithmetic and copies ran while one was open for 3% of the time, Pallas kernels for 21%

profile of v5, /device:TPU:0, one launch (start us, length us, event | category | flops | bytes accessed | tf_op | source)
XLA Modules:
  0.0 125.5 jit_solution(11002065410512599624)
XLA Ops:
  0.0 3.7 %shard_map.64 = (s32[4,512]{1,0:T(4,128)S(1)}, f32[4,512]{1,0:T(4,128)S(1)}, bf16[128,1024]{1,0:T(8,128)(2,1)S(1)}, bf16[128,1024]{1,0:T(8,128)(2,1)}, bf16[128,...) custom-call(s32[1]{0:T(128)} %bitcast.1.place_ref, s32[4,512]{1,0:T(4,128)} %picks_in.1, bf16[4,1024]{1,0:T(4,128)(2,1)} %bitcast.8, ...), custom_call_target="tpu_custom_call" | custom-call | flops 1024 | bytes 1024 | tf_op jit(solution)/shard_map/pallas_call | solution.py:106
  3.8 3.1 %collective-permute-start.12 = (bf16[128,1024]{1,0:T(8,128)(2,1)}, bf16[128,1024]{1,0:T(8,128)(2,1)S(1)}, u32[]{:S(2)}, u32[]{:S(2)}) collective-permute-start(bf16[128,1024]{1,0:T(8,128)(2,1)} %get-tuple-element.249), channel_id=1, source_target_pairs={{0,4},{4,8},{8,12},{12,0},{1,5},{5,9},{9,13},{13,1},{2,6},{6,10},{... | collective-permute-start | bytes 786440 | tf_op jit(solution)/shard_map/ppermute | solution.py:424
  6.8 2.6 %collective-permute-start.13 = (bf16[128,1024]{1,0:T(8,128)(2,1)}, bf16[128,1024]{1,0:T(8,128)(2,1)S(1)}, u32[]{:S(2)}, u32[]{:S(2)}) collective-permute-start(bf16[128,1024]{1,0:T(8,128)(2,1)} %get-tuple-element.250), channel_id=1, source_target_pairs={{0,8},{4,12},{8,0},{12,4},{1,9},{5,13},{9,1},{13,5},{2,10},{6,14},... | collective-permute-start | bytes 786440 | tf_op jit(solution)/shard_map/ppermute | solution.py:424
  13.2 20.5 %conditional.9 = (bf16[128,1024]{1,0:T(8,128)(2,1)}, bf16[128,1024]{1,0:T(8,128)(2,1)}, bf16[128,1024]{1,0:T(8,128)(2,1)}, bf16[128,1024]{1,0:T(8,128)(2,1)}, f3...) conditional(s32[]{:T(128)} %convert_element_type.10, () %tuple.80, (s32[4,512]{1,0:T(4,128)S(1)}, ...), branch_computations={%region_3.4_spmd, %region_4.5_spmd} | conditional | flops 25600 | bytes 1089600 | solution.py:481
  14.7 2.2 %collective-permute-done.8 = f32[4,512]{1,0:T(4,128)S(1)} collective-permute-done((f32[4,512]{1,0:T(4,128)S(1)}, f32[4,512]{1,0:T(4,128)S(1)}, u32[]{:S(2)}, u32[]{:S(2)}) %collective-permute-start.8) | collective-permute-done | bytes 8224 | tf_op jit(solution)/shard_map/cond/branch_1_fun/ppermute | solution.py:427
  19.4 7.4 %collective-permute-done.10 = f32[1,4,512]{2,1,0:T(4,128)S(1)} collective-permute-done((f32[1,4,512]{2,1,0:T(4,128)}, f32[1,4,512]{2,1,0:T(4,128)S(1)}, u32[]{:S(2)}, u32[]{:S(2)}) %collective-permute-start.10) | collective-permute-done | bytes 8224 | tf_op jit(solution)/shard_map/cond/branch_1_fun/ppermute | solution.py:443
  28.1 2.7 %branch_1_fun.11 = (bf16[128,1024]{1,0:T(8,128)(2,1)}, bf16[128,1024]{1,0:T(8,128)(2,1)}, bf16[128,1024]{1,0:T(8,128)(2,1)}, bf16[128,1024]{1,0:T(8,128)(2,1)}) custom-call(s32[4,512]{1,0:T(4,128)S(1)} %get-tuple-element.116.code_ref, bf16[512,1024]{1,0:T(8,128)(2,1)} %get-tuple-element.118.tokens_ref), custom_call_target="tpu_custom_call" | custom-call | flops 1024 | bytes 1024 | tf_op jit(solution)/shard_map/cond/branch_1_fun/pallas_call | solution.py:137
  30.9 2.1 %collective-permute-done.11 = f32[2,4,512]{2,1,0:T(4,128)S(1)} collective-permute-done((f32[2,4,512]{2,1,0:T(4,128)S(1)}, f32[2,4,512]{2,1,0:T(4,128)S(1)}, u32[]{:S(2)}, u32[]{:S(2)}) %collective-permute-start.11) | collective-permute-done | bytes 16416 | tf_op jit(solution)/shard_map/cond/branch_1_fun/ppermute | solution.py:443
  33.7 2.0 %conditional.10 = (bf16[256,1024]{1,0:T(8,128)(2,1)}) conditional(s32[]{:T(128)} %convert_element_type.10, () %tuple.88, (s32[2,4]{1,0:T(2,128)S(1)}, s32[2,4]{1,0:T(2,128)S(1)}, bf16[128,1024]{1,0:T(8,128)(2,1)S(1)}, bf16[128,1024]{1,0:T(8,128)(2,1)S(1)}, bf16[128,1024]{1,0:T(8,128)(2,1)S(1)}, /*index=5*/bf16[128,1024]{1,0:T(8,128)(2,1)S(1)}) %tuple.89), branch_computations={%region_6.7_spmd, %region_7.8_spmd} | conditional | flops 1024 | bytes 524298 | solution.py:500
  37.4 2.1 %collective-permute-start.16 = (bf16[128,1024]{1,0:T(8,128)(2,1)}, bf16[128,1024]{1,0:T(8,128)(2,1)}, u32[]{:S(2)}, u32[]{:S(2)}) collective-permute-start(bf16[128,1024]{1,0:T(8,128)(2,1)} %get-tuple-element.258), channel_id=1, source_target_pairs={{0,8},{4,12},{8,0},{12,4},{1,9},{5,13},{9,1},{13,5},{2,10},{6,14},... | collective-permute-start | bytes 786440 | tf_op jit(solution)/shard_map/ppermute | solution.py:424
  41.9 3.6 %conditional.11 = ((f32[256,256]{1,0:T(8,128)S(1)}, f32[256,256]{1,0:T(8,128)S(1)})) conditional(s32[]{:T(128)} %convert_element_type.10, () %tuple.90, (s32[4]{0:T(128)S(1)}, bf16[1,4096,256]{2,1,0:T(8,128)(2,1)S(1)}, bf16[1,4096,256]{2,1,0:T(8,128)(2,1)}, bf16[256,1024]{1,0:T(8,128)(2,1)}, bf16[256,1024]{1,0:T(8,128)(2,1)S(1)}) %tuple.137), branch_computations={%region_8.9_spmd, %region_9.10_spmd} | conditional | flops 1024 | bytes 2098212 | solution.py:500
  42.7 2.8 %branch_1_fun.13 = (f32[256,256]{1,0:T(8,128)S(1)}, f32[256,256]{1,0:T(8,128)S(1)}) custom-call(s32[4]{0:T(128)S(1)} %get-tuple-element.130.order_ref, bf16[1,4096,256]{2,1,0:T(8,128)(2,1)S(1)} %get-tuple-element.131.gate_ref, bf16[1,4096,256]{2,1,0:T(8,128)(2,1)} %get-tuple-element.132.up_ref, bf16[256,1024]{1,0:T(8,128)(2,1)} %get-tuple-element.133.refs_0_, ...), custom_call_target="tpu_custom_call" | custom-call | flops 1024 | bytes 1024 | tf_op jit(solution)/shard_map/cond/branch_1_fun/pallas_call | solution.py:226
  45.5 4.8 %collective-permute-done.18 = bf16[256,1024]{1,0:T(8,128)(2,1)S(1)} collective-permute-done((bf16[256,1024]{1,0:T(8,128)(2,1)}, bf16[256,1024]{1,0:T(8,128)(2,1)S(1)}, u32[]{:S(2)}, u32[]{:S(2)}) %collective-permute-start.18) | collective-permute-done | bytes 524320 | tf_op jit(solution)/shard_map/ppermute | solution.py:427
  50.4 12.2 %conditional.12 = (bf16[256,256]{1,0:T(8,128)(2,1)}, bf16[256,256]{1,0:T(8,128)(2,1)}, f32[256,1024]{1,0:T(8,128)S(1)}) conditional(s32[]{:T(128)} %convert_element_type.10, () %tuple.87, (bf16[256,1024]{1,0:T(8,128)(2,1)S(1)}, s32[4]{0:T(128)S(1)}, bf16[1,4096,256]{2,1,0:T(8,128)(2,1)S(1)}, bf16[1,4096,256]{2,1,0:T(8,128)(2,1)}, ...), branch_computations={%region_10.11_spmd, %region_11.12_spmd} | conditional | flops 2048 | bytes 12060884 | solution.py:500
  52.3 2.5 %branch_1_fun.14.refs_0_ = bf16[256,256]{1,0:T(8,128)(2,1)S(1)} custom-call(s32[4]{0:T(128)S(1)} %get-tuple-element.135.order_ref, bf16[1,4096,256]{2,1,0:T(8,128)(2,1)S(1)} %get-tuple-element.136.gate_ref, bf16[1,4096,256]{2,1,0:T(8,128)(2,1)} %get-tuple-element.137.up_ref, bf16[256,1024]{1,0:T(8,128)(2,1)S(1)} %get-tuple-element.138.refs_0_, ...), custom_call_target="tpu_custom_call" | custom-call | flops 1024 | bytes 1024 | tf_op jit(solution)/shard_map/cond/branch_1_fun/pallas_call | solution.py:226
  58.0 2.9 %collective-permute-done.1 = bf16[256,256]{1,0:T(8,128)(2,1)} collective-permute-done((bf16[256,256]{1,0:T(8,128)(2,1)S(1)}, bf16[256,256]{1,0:T(8,128)(2,1)}, u32[]{:S(2)}, u32[]{:S(2)}) %collective-permute-start.1) | collective-permute-done | bytes 131104 | tf_op jit(solution)/shard_map/cond/branch_1_fun/ppermute | solution.py:427
  62.6 3.0 %conditional.13 = (bf16[256,1024]{1,0:T(8,128)(2,1)}) conditional(s32[]{:T(128)} %convert_element_type.22, () %tuple.84, (s32[2,4]{1,0:T(2,128)S(1)}, s32[2,4]{1,0:T(2,128)S(1)}, bf16[128,1024]{1,0:T(8,128)(2,1)}, bf16[128,1024]{1,0:T(8,128)(2,1)}, bf16[128,1024]{1,0:T(8,128)(2,1)}, /*index=5*/bf16[128,1024]{1,0:T(8,128)(2,1)}) %tuple.95), branch_computations={%region_12.13_spmd, %region_13.14_spmd} | conditional | flops 1024 | bytes 524298 | solution.py:500
  62.6 3.0 %branch_1_fun.16 = bf16[256,1024]{1,0:T(8,128)(2,1)} custom-call(s32[2,4]{1,0:T(2,128)S(1)} %get-tuple-element.144.offset_ref, s32[2,4]{1,0:T(2,128)S(1)} %get-tuple-element.145.count_ref, bf16[128,1024]{1,0:T(8,128)(2,1)} %get-tuple-element.146.refs_0_, bf16[128,1024]{1,0:T(8,128)(2,1)} %get-tuple-element.147.refs_1_, ...), custom_call_target="tpu_custom_call" | custom-call | flops 1024 | bytes 1024 | tf_op jit(solution)/shard_map/cond/branch_1_fun/pallas_call | solution.py:174
  67.4 3.4 %conditional.14 = ((bf16[128,1024]{1,0:T(8,128)(2,1)S(1)}, bf16[128,1024]{1,0:T(8,128)(2,1)}, bf16[128,1024]{1,0:T(8,128)(2,1)}, bf16[128,1024]{1,0:T(8,128)(2,1)})) conditional(s32[]{:T(128)} %convert_element_type.22, () %tuple.97, (s32[4]{0:T(128)S(1)}, s32[2,4]{1,0:T(2,128)S(1)}, s32[2,4]{1,0:T(2,128)S(1)}, bf16[1,1024,1024]{2,1,0:T(8,128)(2,1)}, ...), branch_computations={%region_14.15_spmd, %region_15.16_spmd} | conditional | flops 1024 | bytes 1048624 | solution.py:500
  67.4 3.3 %branch_1_fun.17 = (bf16[128,1024]{1,0:T(8,128)(2,1)S(1)}, bf16[128,1024]{1,0:T(8,128)(2,1)}, bf16[128,1024]{1,0:T(8,128)(2,1)}, bf16[128,1024]{1,0:T(8,128)(2,1)}) custom-call(s32[4]{0:T(128)S(1)} %get-tuple-element.150.order_ref, s32[2,4]{1,0:T(2,128)S(1)} %get-tuple-element.151.offset_ref, s32[2,4]{1,0:T(2,128)S(1)} %get-tuple-element.152.count_ref, ...), custom_call_target="tpu_custom_call" | custom-call | flops 1024 | bytes 1024 | tf_op jit(solution)/shard_map/cond/branch_1_fun/pallas_call | solution.py:314
  73.0 3.5 %conditional.15 = ((f32[256,256]{1,0:T(8,128)}, f32[256,256]{1,0:T(8,128)S(1)})) conditional(s32[]{:T(128)} %convert_element_type.22, () %tuple.96, (s32[4]{0:T(128)S(1)}, bf16[1,4096,256]{2,1,0:T(8,128)(2,1)S(1)}, bf16[1,4096,256]{2,1,0:T(8,128)(2,1)}, bf16[256,1024]{1,0:T(8,128)(2,1)}, bf16[256,1024]{1,0:T(8,128)(2,1)}) %tuple.139), branch_computations={%region_16.17_spmd, %region_17.18_spmd} | conditional | flops 1024 | bytes 524320 | solution.py:500
  73.0 3.5 %branch_1_fun.18 = (f32[256,256]{1,0:T(8,128)}, f32[256,256]{1,0:T(8,128)S(1)}) custom-call(s32[4]{0:T(128)S(1)} %get-tuple-element.157.order_ref, bf16[1,4096,256]{2,1,0:T(8,128)(2,1)S(1)} %get-tuple-element.158.gate_ref, bf16[1,4096,256]{2,1,0:T(8,128)(2,1)} %get-tuple-element.159.up_ref, bf16[256,1024]{1,0:T(8,128)(2,1)} %get-tuple-element.160.refs_0_, ...), custom_call_target="tpu_custom_call" | custom-call | flops 1024 | bytes 1024 | tf_op jit(solution)/shard_map/cond/branch_1_fun/pallas_call | solution.py:226
  76.6 3.8 %collective-permute-done.20 = bf16[256,1024]{1,0:T(8,128)(2,1)} collective-permute-done((bf16[256,1024]{1,0:T(8,128)(2,1)}, bf16[256,1024]{1,0:T(8,128)(2,1)}, u32[]{:S(2)}, u32[]{:S(2)}) %collective-permute-start.20) | collective-permute-done | bytes 524320 | tf_op jit(solution)/shard_map/ppermute | solution.py:427
  80.3 13.1 %conditional.16 = (bf16[256,256]{1,0:T(8,128)(2,1)}, bf16[256,256]{1,0:T(8,128)(2,1)}, f32[256,1024]{1,0:T(8,128)S(1)}) conditional(s32[]{:T(128)} %convert_element_type.22, () %tuple.83, (bf16[256,1024]{1,0:T(8,128)(2,1)}, s32[4]{0:T(128)S(1)}, bf16[1,4096,256]{2,1,0:T(8,128)(2,1)S(1)}, bf16[1,4096,256]{2,1,0:T(8,128)(2,1)}, ...), branch_computations={%region_18.19_spmd, %region_19.20_spmd} | conditional | flops 2048 | bytes 12060884 | solution.py:500
  80.4 2.1 %collective-permute-done.4.refs_1_ = bf16[256,1024]{1,0:T(8,128)(2,1)S(1)} collective-permute-done((bf16[256,1024]{1,0:T(8,128)(2,1)}, bf16[256,1024]{1,0:T(8,128)(2,1)S(1)}, u32[]{:S(2)}, u32[]{:S(2)}) %collective-permute-start.4) | collective-permute-done | bytes 524320 | tf_op jit(solution)/shard_map/cond/branch_1_fun/ppermute | solution.py:427
  82.5 3.1 %branch_1_fun.19.refs_0_ = bf16[256,256]{1,0:T(8,128)(2,1)S(1)} custom-call(s32[4]{0:T(128)S(1)} %get-tuple-element.162.order_ref, bf16[1,4096,256]{2,1,0:T(8,128)(2,1)S(1)} %get-tuple-element.163.gate_ref, bf16[1,4096,256]{2,1,0:T(8,128)(2,1)} %get-tuple-element.164.up_ref, bf16[256,1024]{1,0:T(8,128)(2,1)} %get-tuple-element.165.refs_0_, ...), custom_call_target="tpu_custom_call" | custom-call | flops 1024 | bytes 1024 | tf_op jit(solution)/shard_map/cond/branch_1_fun/pallas_call | solution.py:226
  88.8 2.9 %collective-permute-done.5 = bf16[256,256]{1,0:T(8,128)(2,1)} collective-permute-done((bf16[256,256]{1,0:T(8,128)(2,1)S(1)}, bf16[256,256]{1,0:T(8,128)(2,1)}, u32[]{:S(2)}, u32[]{:S(2)}) %collective-permute-start.5) | collective-permute-done | bytes 131104 | tf_op jit(solution)/shard_map/cond/branch_1_fun/ppermute | solution.py:427
  93.4 3.2 %conditional.17 = ((bf16[128,1024]{1,0:T(8,128)(2,1)S(1)}, bf16[128,1024]{1,0:T(8,128)(2,1)}, bf16[128,1024]{1,0:T(8,128)(2,1)}, bf16[128,1024]{1,0:T(8,128)(2,1)S(1)})) conditional(s32[]{:T(128)} %convert_element_type.10, () %tuple.82, (s32[4]{0:T(128)S(1)}, s32[2,4]{1,0:T(2,128)S(1)}, s32[2,4]{1,0:T(2,128)S(1)}, ...), branch_computations={%region_20.21_spmd, %region_21.22_spmd} | conditional | flops 1024 | bytes 1048624 | solution.py:500
  93.4 3.2 %branch_1_fun.21 = (bf16[128,1024]{1,0:T(8,128)(2,1)S(1)}, bf16[128,1024]{1,0:T(8,128)(2,1)}, bf16[128,1024]{1,0:T(8,128)(2,1)}, bf16[128,1024]{1,0:T(8,128)(2,1)S(1)}) custom-call(s32[4]{0:T(128)S(1)} %get-tuple-element.171.order_ref, s32[2,4]{1,0:T(2,128)S(1)} %get-tuple-element.172.offset_ref, s32[2,4]{1,0:T(2,128)S(1)} %get-tuple-element.173.count_ref, ...), custom_call_target="tpu_custom_call" | custom-call | flops 1024 | bytes 1024 | tf_op jit(solution)/shard_map/cond/branch_1_fun/pallas_call | solution.py:314
  102.2 3.2 %collective-permute-done.25.refs_1_ = bf16[128,1024]{1,0:T(8,128)(2,1)S(1)} collective-permute-done((bf16[128,1024]{1,0:T(8,128)(2,1)}, bf16[128,1024]{1,0:T(8,128)(2,1)S(1)}, u32[]{:S(2)}, u32[]{:S(2)}) %collective-permute-start.25) | collective-permute-done | bytes 262176 | tf_op jit(solution)/shard_map/ppermute | solution.py:424
  105.4 18.0 %collective-permute-done.26.refs_2_ = bf16[128,1024]{1,0:T(8,128)(2,1)S(1)} collective-permute-done((bf16[128,1024]{1,0:T(8,128)(2,1)}, bf16[128,1024]{1,0:T(8,128)(2,1)S(1)}, u32[]{:S(2)}, u32[]{:S(2)}) %collective-permute-start.26) | collective-permute-done | bytes 262176 | tf_op jit(solution)/shard_map/ppermute | solution.py:424
  123.4 2.1 %shard_map.67 = bf16[512,1024]{1,0:T(8,128)(2,1)} custom-call(s32[4,512]{1,0:T(4,128)S(1)} %get-tuple-element.240.code_ref, f32[4,512]{1,0:T(4,128)S(1)} %shard_map.65.weight_ref, bf16[128,1024]{1,0:T(8,128)(2,1)S(1)} %get-tuple-element.293.refs_0_, bf16[128,1024]{1,0:T(8,128)(2,1)S(1)} %collective-permute-done.25.refs_1_, ...), custom_call_target="tpu_custom_call" | custom-call | flops 1024 | bytes 1024 | tf_op jit(solution)/shard_map/pallas_call | solution.py:393
  (68 shorter events, 36.5 us)
Async XLA Ops:
  3.8 30.0 %collective-permute-start.12 = (bf16[128,1024]{1,0:T(8,128)(2,1)}, bf16[128,1024]{1,0:T(8,128)(2,1)S(1)}, u32[]{:S(2)}, u32[]{:S(2)}) collective-permute-start(bf16[128,1024]{1,0:T(8,128)(2,1)} %get-tuple-element.249), channel_id=1, source_target_pairs={{0,4},{4,8},{8,12},{12,0},{1,5},{5,9},{9,13},{13,1},{2,6},{6,10},{... | collective-permute-start | bytes 786440 | tf_op jit(solution)/shard_map/ppermute | solution.py:424
  6.8 26.9 %collective-permute-start.13 = (bf16[128,1024]{1,0:T(8,128)(2,1)}, bf16[128,1024]{1,0:T(8,128)(2,1)S(1)}, u32[]{:S(2)}, u32[]{:S(2)}) collective-permute-start(bf16[128,1024]{1,0:T(8,128)(2,1)} %get-tuple-element.250), channel_id=1, source_target_pairs={{0,8},{4,12},{8,0},{12,4},{1,9},{5,13},{9,1},{13,5},{2,10},{6,14},... | collective-permute-start | bytes 786440 | tf_op jit(solution)/shard_map/ppermute | solution.py:424
  9.4 24.3 %collective-permute-start.14 = (bf16[128,1024]{1,0:T(8,128)(2,1)}, bf16[128,1024]{1,0:T(8,128)(2,1)S(1)}, u32[]{:S(2)}, u32[]{:S(2)}) collective-permute-start(bf16[128,1024]{1,0:T(8,128)(2,1)} %get-tuple-element.251), channel_id=1, source_target_pairs={{0,12},{4,0},{8,4},{12,8},{1,13},{5,1},{9,5},{13,9},{2,14},{6,2},{... | collective-permute-start | bytes 786440 | tf_op jit(solution)/shard_map/ppermute | solution.py:424
  13.2 28.7 %copy-start = (bf16[1,4096,256]{2,1,0:T(8,128)(2,1)S(1)}, bf16[1,4096,256]{2,1,0:T(8,128)(2,1)}, u32[]{:S(2)}) copy-start(bf16[1,4096,256]{2,1,0:T(8,128)(2,1)} %param.26) | copy-start | bytes 6291460
  13.2 3.7 %collective-permute-start.8 = (f32[4,512]{1,0:T(4,128)S(1)}, f32[4,512]{1,0:T(4,128)S(1)}, u32[]{:S(2)}, u32[]{:S(2)}) collective-permute-start(f32[4,512]{1,0:T(4,128)S(1)} %get-tuple-element.123), channel_id=1, source_target_pairs={{0,2},{1,3},{2,0},{3,1},{4,6},{5,7},{6,4},{7,5},{8,10},{9,11},{10,... | collective-permute-start | bytes 24584 | tf_op jit(solution)/shard_map/cond/branch_1_fun/ppermute | solution.py:427
  16.9 1.2 collective-permute-start.9
  18.7 8.1 %collective-permute-start.10 = (f32[1,4,512]{2,1,0:T(4,128)}, f32[1,4,512]{2,1,0:T(4,128)S(1)}, u32[]{:S(2)}, u32[]{:S(2)}) collective-permute-start(f32[1,4,512]{2,1,0:T(4,128)} %bitcast), channel_id=1, source_target_pairs={{0,4},{4,0},{8,12},{12,8},{1,5},{5,1},{9,13},{13,9},{2,6},{6,2},{1... | collective-permute-start | bytes 24584 | tf_op jit(solution)/shard_map/cond/branch_1_fun/ppermute | solution.py:443
  27.5 5.5 %collective-permute-start.11 = (f32[2,4,512]{2,1,0:T(4,128)S(1)}, f32[2,4,512]{2,1,0:T(4,128)S(1)}, u32[]{:S(2)}, u32[]{:S(2)}) collective-permute-start(f32[2,4,512]{2,1,0:T(4,128)S(1)} %pad_maximum_fusion.1), channel_id=1, source_target_pairs={{0,8},{4,12},{8,0},{12,4},{1,9},{5,13},{9,1},{13,5},{2,10},{6,14},... | collective-permute-start | bytes 49160 | tf_op jit(solution)/shard_map/cond/branch_1_fun/ppermute | solution.py:443
  35.7 6.2 %collective-permute-start.19 = (bf16[256,1024]{1,0:T(8,128)(2,1)}, bf16[256,1024]{1,0:T(8,128)(2,1)S(1)}, u32[]{:S(2)}, u32[]{:S(2)}) collective-permute-start(bf16[256,1024]{1,0:T(8,128)(2,1)} %get-tuple-element.358), channel_id=1, source_target_pairs={{0,1},{1,0},{2,3},{3,2},{4,5},{5,4},{6,7},{7,6},{8,9},{9,8},{10,11... | collective-permute-start | bytes 1572872 | tf_op jit(solution)/shard_map/ppermute | solution.py:427
  35.8 14.5 %collective-permute-start.18 = (bf16[256,1024]{1,0:T(8,128)(2,1)}, bf16[256,1024]{1,0:T(8,128)(2,1)S(1)}, u32[]{:S(2)}, u32[]{:S(2)}) collective-permute-start(bf16[256,1024]{1,0:T(8,128)(2,1)} %get-tuple-element.358), channel_id=1, source_target_pairs={{0,2},{1,3},{2,0},{3,1},{4,6},{5,7},{6,4},{7,5},{8,10},{9,11},{10,... | collective-permute-start | bytes 1572872 | tf_op jit(solution)/shard_map/ppermute | solution.py:427
  37.4 25.2 %collective-permute-start.15 = (bf16[128,1024]{1,0:T(8,128)(2,1)}, bf16[128,1024]{1,0:T(8,128)(2,1)}, u32[]{:S(2)}, u32[]{:S(2)}) collective-permute-start(bf16[128,1024]{1,0:T(8,128)(2,1)} %get-tuple-element.257), channel_id=1, source_target_pairs={{0,4},{4,8},{8,12},{12,0},{1,5},{5,9},{9,13},{13,1},{2,6},{6,10},{... | collective-permute-start | bytes 786440 | tf_op jit(solution)/shard_map/ppermute | solution.py:424
  37.4 25.2 %collective-permute-start.16 = (bf16[128,1024]{1,0:T(8,128)(2,1)}, bf16[128,1024]{1,0:T(8,128)(2,1)}, u32[]{:S(2)}, u32[]{:S(2)}) collective-permute-start(bf16[128,1024]{1,0:T(8,128)(2,1)} %get-tuple-element.258), channel_id=1, source_target_pairs={{0,8},{4,12},{8,0},{12,4},{1,9},{5,13},{9,1},{13,5},{2,10},{6,14},... | collective-permute-start | bytes 786440 | tf_op jit(solution)/shard_map/ppermute | solution.py:424
  39.5 23.1 %collective-permute-start.17 = (bf16[128,1024]{1,0:T(8,128)(2,1)}, bf16[128,1024]{1,0:T(8,128)(2,1)}, u32[]{:S(2)}, u32[]{:S(2)}) collective-permute-start(bf16[128,1024]{1,0:T(8,128)(2,1)} %get-tuple-element.259), channel_id=1, source_target_pairs={{0,12},{4,0},{8,4},{12,8},{1,13},{5,1},{9,5},{13,9},{2,14},{6,2},{... | collective-permute-start | bytes 786440 | tf_op jit(solution)/shard_map/ppermute | solution.py:424
  41.9 0.8 copy-start.3
  50.4 1.9 %collective-permute-start = (bf16[256,1024]{1,0:T(8,128)(2,1)S(1)}, bf16[256,1024]{1,0:T(8,128)(2,1)S(1)}, u32[]{:S(2)}, u32[]{:S(2)}) collective-permute-start(bf16[256,1024]{1,0:T(8,128)(2,1)S(1)} %get-tuple-element.138.refs_0_), channel_id=1, source_target_pairs={{0,1},{1,0},{2,3},{3,2},{4,5},{5,4},{6,7},{7,6},{8,9},{9,8},{10,11... | collective-permute-start | bytes 1572872 | tf_op jit(solution)/shard_map/cond/branch_1_fun/ppermute | solution.py:427
  52.3 4.2 %copy-start.1 = (bf16[1,1024,1024]{2,1,0:T(8,128)(2,1)S(1)}, bf16[1,1024,1024]{2,1,0:T(8,128)(2,1)}, u32[]{:S(2)}) copy-start(bf16[1,1024,1024]{2,1,0:T(8,128)(2,1)} %get-tuple-element.141.down_ref) | copy-start | bytes 6291460 | tf_op jit(solution)/shard_map/cond
  54.8 1.7 %collective-permute-start.2 = (bf16[256,256]{1,0:T(8,128)(2,1)S(1)}, bf16[256,256]{1,0:T(8,128)(2,1)S(1)}, u32[]{:S(2)}, u32[]{:S(2)}) collective-permute-start(bf16[256,256]{1,0:T(8,128)(2,1)S(1)} %branch_1_fun.14.refs_0_), channel_id=1, source_target_pairs={{0,1},{1,0},{2,3},{3,2},{4,5},{5,4},{6,7},{7,6},{8,9},{9,8},{10,11... | collective-permute-start | bytes 393224 | tf_op jit(solution)/shard_map/cond/branch_1_fun/ppermute | solution.py:427
  55.0 5.9 %collective-permute-start.1 = (bf16[256,256]{1,0:T(8,128)(2,1)S(1)}, bf16[256,256]{1,0:T(8,128)(2,1)}, u32[]{:S(2)}, u32[]{:S(2)}) collective-permute-start(bf16[256,256]{1,0:T(8,128)(2,1)S(1)} %branch_1_fun.14.refs_0_), channel_id=1, source_target_pairs={{0,2},{1,3},{2,0},{3,1},{4,6},{5,7},{6,4},{7,5},{8,10},{9,11},{10,... | collective-permute-start | bytes 393224 | tf_op jit(solution)/shard_map/cond/branch_1_fun/ppermute | solution.py:427
  60.9 1.7 %collective-permute-start.3 = (bf16[256,256]{1,0:T(8,128)(2,1)}, bf16[256,256]{1,0:T(8,128)(2,1)}, u32[]{:S(2)}, u32[]{:S(2)}) collective-permute-start(bf16[256,256]{1,0:T(8,128)(2,1)} %collective-permute-done.1), channel_id=1, source_target_pairs={{0,1},{1,0},{2,3},{3,2},{4,5},{5,4},{6,7},{7,6},{8,9},{9,8},{10,11... | collective-permute-start | bytes 393224 | tf_op jit(solution)/shard_map/cond/branch_1_fun/ppermute | solution.py:427
  65.6 7.4 %collective-permute-start.21 = (bf16[256,1024]{1,0:T(8,128)(2,1)}, bf16[256,1024]{1,0:T(8,128)(2,1)}, u32[]{:S(2)}, u32[]{:S(2)}) collective-permute-start(bf16[256,1024]{1,0:T(8,128)(2,1)} %get-tuple-element.360), channel_id=1, source_target_pairs={{0,1},{1,0},{2,3},{3,2},{4,5},{5,4},{6,7},{7,6},{8,9},{9,8},{10,11... | collective-permute-start | bytes 1572872 | tf_op jit(solution)/shard_map/ppermute | solution.py:427
  65.8 14.5 %collective-permute-start.20 = (bf16[256,1024]{1,0:T(8,128)(2,1)}, bf16[256,1024]{1,0:T(8,128)(2,1)}, u32[]{:S(2)}, u32[]{:S(2)}) collective-permute-start(bf16[256,1024]{1,0:T(8,128)(2,1)} %get-tuple-element.360), channel_id=1, source_target_pairs={{0,2},{1,3},{2,0},{3,1},{4,6},{5,7},{6,4},{7,5},{8,10},{9,11},{10,... | collective-permute-start | bytes 1572872 | tf_op jit(solution)/shard_map/ppermute | solution.py:427
  70.7 25.9 %collective-permute-start.22 = (bf16[128,1024]{1,0:T(8,128)(2,1)}, bf16[128,1024]{1,0:T(8,128)(2,1)S(1)}, u32[]{:S(2)}, u32[]{:S(2)}) collective-permute-start(bf16[128,1024]{1,0:T(8,128)(2,1)} %get-tuple-element.276), channel_id=1, source_target_pairs={{0,12},{4,0},{8,4},{12,8},{1,13},{5,1},{9,5},{13,9},{2,14},{6,2},{... | collective-permute-start | bytes 786440 | tf_op jit(solution)/shard_map/ppermute | solution.py:424
  72.3 24.4 %collective-permute-start.23 = (bf16[128,1024]{1,0:T(8,128)(2,1)}, bf16[128,1024]{1,0:T(8,128)(2,1)S(1)}, u32[]{:S(2)}, u32[]{:S(2)}) collective-permute-start(bf16[128,1024]{1,0:T(8,128)(2,1)} %get-tuple-element.277), channel_id=1, source_target_pairs={{0,8},{4,12},{8,0},{12,4},{1,9},{5,13},{9,1},{13,5},{2,10},{6,14},... | collective-permute-start | bytes 786440 | tf_op jit(solution)/shard_map/ppermute | solution.py:424
  73.0 23.7 %collective-permute-start.24 = (bf16[128,1024]{1,0:T(8,128)(2,1)}, bf16[128,1024]{1,0:T(8,128)(2,1)S(1)}, u32[]{:S(2)}, u32[]{:S(2)}) collective-permute-start(bf16[128,1024]{1,0:T(8,128)(2,1)} %get-tuple-element.278), channel_id=1, source_target_pairs={{0,4},{4,8},{8,12},{12,0},{1,5},{5,9},{9,13},{13,1},{2,6},{6,10},{... | collective-permute-start | bytes 786440 | tf_op jit(solution)/shard_map/ppermute | solution.py:424
  80.3 2.1 %collective-permute-start.4 = (bf16[256,1024]{1,0:T(8,128)(2,1)}, bf16[256,1024]{1,0:T(8,128)(2,1)S(1)}, u32[]{:S(2)}, u32[]{:S(2)}) collective-permute-start(bf16[256,1024]{1,0:T(8,128)(2,1)} %get-tuple-element.165.refs_0_), channel_id=1, source_target_pairs={{0,1},{1,0},{2,3},{3,2},{4,5},{5,4},{6,7},{7,6},{8,9},{9,8},{10,11... | collective-permute-start | bytes 1572872 | tf_op jit(solution)/shard_map/cond/branch_1_fun/ppermute | solution.py:427
  82.5 4.9 %copy-start.2 = (bf16[1,1024,1024]{2,1,0:T(8,128)(2,1)S(1)}, bf16[1,1024,1024]{2,1,0:T(8,128)(2,1)}, u32[]{:S(2)}) copy-start(bf16[1,1024,1024]{2,1,0:T(8,128)(2,1)} %get-tuple-element.168.down_ref) | copy-start | bytes 6291460 | tf_op jit(solution)/shard_map/cond
  85.6 1.7 %collective-permute-start.6 = (bf16[256,256]{1,0:T(8,128)(2,1)S(1)}, bf16[256,256]{1,0:T(8,128)(2,1)S(1)}, u32[]{:S(2)}, u32[]{:S(2)}) collective-permute-start(bf16[256,256]{1,0:T(8,128)(2,1)S(1)} %branch_1_fun.19.refs_0_), channel_id=1, source_target_pairs={{0,1},{1,0},{2,3},{3,2},{4,5},{5,4},{6,7},{7,6},{8,9},{9,8},{10,11... | collective-permute-start | bytes 393224 | tf_op jit(solution)/shard_map/cond/branch_1_fun/ppermute | solution.py:427
  85.8 5.9 %collective-permute-start.5 = (bf16[256,256]{1,0:T(8,128)(2,1)S(1)}, bf16[256,256]{1,0:T(8,128)(2,1)}, u32[]{:S(2)}, u32[]{:S(2)}) collective-permute-start(bf16[256,256]{1,0:T(8,128)(2,1)S(1)} %branch_1_fun.19.refs_0_), channel_id=1, source_target_pairs={{0,2},{1,3},{2,0},{3,1},{4,6},{5,7},{6,4},{7,5},{8,10},{9,11},{10,... | collective-permute-start | bytes 393224 | tf_op jit(solution)/shard_map/cond/branch_1_fun/ppermute | solution.py:427
  91.7 1.7 %collective-permute-start.7 = (bf16[256,256]{1,0:T(8,128)(2,1)}, bf16[256,256]{1,0:T(8,128)(2,1)}, u32[]{:S(2)}, u32[]{:S(2)}) collective-permute-start(bf16[256,256]{1,0:T(8,128)(2,1)} %collective-permute-done.5), channel_id=1, source_target_pairs={{0,1},{1,0},{2,3},{3,2},{4,5},{5,4},{6,7},{7,6},{8,9},{9,8},{10,11... | collective-permute-start | bytes 393224 | tf_op jit(solution)/shard_map/cond/branch_1_fun/ppermute | solution.py:427
  96.7 8.7 %collective-permute-start.25 = (bf16[128,1024]{1,0:T(8,128)(2,1)}, bf16[128,1024]{1,0:T(8,128)(2,1)S(1)}, u32[]{:S(2)}, u32[]{:S(2)}) collective-permute-start(bf16[128,1024]{1,0:T(8,128)(2,1)} %get-tuple-element.294), channel_id=1, source_target_pairs={{0,12},{4,0},{8,4},{12,8},{1,13},{5,1},{9,5},{13,9},{2,14},{6,2},{... | collective-permute-start | bytes 786440 | tf_op jit(solution)/shard_map/ppermute | solution.py:424
  98.3 25.1 %collective-permute-start.26 = (bf16[128,1024]{1,0:T(8,128)(2,1)}, bf16[128,1024]{1,0:T(8,128)(2,1)S(1)}, u32[]{:S(2)}, u32[]{:S(2)}) collective-permute-start(bf16[128,1024]{1,0:T(8,128)(2,1)} %get-tuple-element.295), channel_id=1, source_target_pairs={{0,8},{4,12},{8,0},{12,4},{1,9},{5,13},{9,1},{13,5},{2,10},{6,14},... | collective-permute-start | bytes 786440 | tf_op jit(solution)/shard_map/ppermute | solution.py:424
  100.0 23.4 %collective-permute-start.27 = (bf16[128,1024]{1,0:T(8,128)(2,1)S(1)}, bf16[128,1024]{1,0:T(8,128)(2,1)S(1)}, u32[]{:S(2)}, u32[]{:S(2)}) collective-permute-start(bf16[128,1024]{1,0:T(8,128)(2,1)S(1)} %get-tuple-element.296), channel_id=1, source_target_pairs={{0,4},{4,8},{8,12},{12,0},{1,5},{5,9},{9,13},{13,1},{2,6},{6,10},{... | collective-permute-start | bytes 786440 | tf_op jit(solution)/shard_map/ppermute | solution.py:424

commit v6 on v5

--- a/solution.py
+++ b/solution.py
@@ -11,7 +11,7 @@
 F32 = jnp.float32
 BF16 = jnp.bfloat16
 I32 = jnp.int32
-VMEM_LIMIT = 24 * 1024 * 1024
+VMEM_LIMIT = 16 * 1024 * 1024
 COST = pl.CostEstimate(flops=1024, bytes_accessed=1024, transcendentals=0)
 
 
@@ -188,26 +188,16 @@
         gate_before, up_before, out_ref, *refs = refs
     else:
         gate_out, up_out, *refs = refs
-    gate_held, up_held, x_held, sems = refs
+    x_held, sems = refs
     width = xs[0].shape[1]
-    loads = []
+    loads = start_all(xs, [x_held.at[i] for i in range(parts)], sems)
+    gate, up = (gate_before[...], up_before[...]) if last else (None, None)
     for i in range(parts):
         first = pl.multiple_of(order_ref[places[i]] * width, width)
-        copies = [
-            pltpu.make_async_copy(xs[i], x_held.at[i], sems.at[3 * i]),
-            pltpu.make_async_copy(gate_ref.at[0, pl.ds(first, width), :], gate_held.at[i], sems.at[3 * i + 1]),
-            pltpu.make_async_copy(up_ref.at[0, pl.ds(first, width), :], up_held.at[i], sems.at[3 * i + 2]),
-        ]
-        for copy in copies:
-            copy.start()
-        loads.append(copies)
-    gate, up = (gate_before[...], up_before[...]) if last else (None, None)
-    for i in range(parts):
-        for copy in loads[i]:
-            copy.wait()
+        loads[i].wait()
         x = x_held[i]
-        gate_term = dot(x, gate_held[i])
-        up_term = dot(x, up_held[i])
+        gate_term = dot(x, gate_ref[0, pl.ds(first, width), :])
+        up_term = dot(x, up_ref[0, pl.ds(first, width), :])
         gate = gate_term if gate is None else gate + gate_term
         up = up_term if up is None else up + up_term
     if last:
@@ -226,35 +216,24 @@
     return pl.pallas_call(
         functools.partial(gate_up_kernel, parts, places, last),
         out_shape=jax.ShapeDtypeStruct((size, units), BF16) if last else sums,
-        in_specs=[smem()] + apart(2 + parts) + (whole(2) if last else []),
+        in_specs=[smem()] + whole(2) + apart(parts) + (whole(2) if last else []),
         out_specs=whole(1)[0] if last else whole(2),
         scratch_shapes=[
-            pltpu.VMEM((parts, width, units), BF16),
-            pltpu.VMEM((parts, width, units), BF16),
             pltpu.VMEM((parts, size, width), BF16),
-            pltpu.SemaphoreType.DMA((3 * parts,)),
+            pltpu.SemaphoreType.DMA((parts,)),
         ],
         compiler_params=params(),
         cost_estimate=COST,
     )(order, gate_weight, up_weight, *xs, *(before or []))
 
 
-def down_sum(places, order_ref, down_ref, hs, down_held, h_held, sems, total):
+def down_sum(places, order_ref, down_ref, hs, h_held, sems, total):
     units = hs[0].shape[1]
-    loads = []
+    loads = start_all(hs, [h_held.at[i] for i in range(len(hs))], sems)
     for i in range(len(hs)):
         first = pl.multiple_of(order_ref[places[i]] * units, units)
-        copies = [
-            pltpu.make_async_copy(hs[i], h_held.at[i], sems.at[2 * i]),
-            pltpu.make_async_copy(down_ref.at[0, pl.ds(first, units), :], down_held.at[i], sems.at[2 * i + 1]),
-        ]
-        for copy in copies:
-            copy.start()
-        loads.append(copies)
-    for i in range(len(hs)):
-        for copy in loads[i]:
-            copy.wait()
-        term = dot(h_held[i], down_held[i])
+        loads[i].wait()
+        term = dot(h_held[i], down_ref[0, pl.ds(first, units), :])
         total = term if total is None else total + term
     return total
 
@@ -266,10 +245,10 @@
 
 def down_last_kernel(parts, places, experts, k, order_ref, offset_ref, count_ref, down_ref, *refs):
     hs, before, outs = refs[:parts], refs[parts], refs[parts + 1 : parts + 1 + experts]
-    down_held, h_held, in_sems, staged, out_sems = refs[parts + 1 + experts :]
+    h_held, in_sems, staged, out_sems = refs[parts + 1 + experts :]
     size = hs[0].shape[0]
     depth = outs[0].shape[0]
-    total = down_sum(places, order_ref, down_ref, hs, down_held, h_held, in_sems, before[...])
+    total = down_sum(places, order_ref, down_ref, hs, h_held, in_sems, before[...])
     result = total.astype(BF16)
     row = lax.broadcasted_iota(I32, (depth, size), 0)
     lane = lax.broadcasted_iota(I32, (depth, size), 1)
@@ -284,12 +263,8 @@
         copy.wait()
 
 
-def down_scratch(parts, size, units, width):
-    return [
-        pltpu.VMEM((parts, units, width), BF16),
-        pltpu.VMEM((parts, size, units), BF16),
-        pltpu.SemaphoreType.DMA((2 * parts,)),
-    ]
+def down_scratch(parts, size, units):
+    return [pltpu.VMEM((parts, size, units), BF16), pltpu.SemaphoreType.DMA((parts,))]
 
 
 def down_first(order, places, down_weight, hs):
@@ -299,9 +274,9 @@
     return pl.pallas_call(
         functools.partial(down_first_kernel, parts, places),
         out_shape=jax.ShapeDtypeStruct((size, width), F32),
-        in_specs=[smem()] + apart(1 + parts),
+        in_specs=[smem()] + whole(1) + apart(parts),
         out_specs=whole(1)[0],
-        scratch_shapes=down_scratch(parts, size, units, width),
+        scratch_shapes=down_scratch(parts, size, units),
         compiler_params=params(),
         cost_estimate=COST,
     )(order, down_weight, *hs)
@@ -314,9 +289,9 @@
     return pl.pallas_call(
         functools.partial(down_last_kernel, parts, places, experts, k),
         out_shape=[jax.ShapeDtypeStruct((depth, width), BF16)] * experts,
-        in_specs=[smem()] * 3 + apart(1 + parts) + whole(1),
+        in_specs=[smem()] * 3 + whole(1) + apart(parts) + whole(1),
         out_specs=apart(experts),
-        scratch_shapes=down_scratch(parts, size, units, width)
+        scratch_shapes=down_scratch(parts, size, units)
         + [pltpu.VMEM((experts, depth, width), BF16), pltpu.SemaphoreType.DMA((experts,))],
         compiler_params=params(),
         cost_estimate=COST,
@@ -488,6 +463,13 @@
         far, partial = lax.optimization_barrier((far, partial))
         return spread(far), partial
 
+    def whole_chain(*blocks):
+        block = compact(offsets, counts, 0, blocks, size)
+        across = swap(block, bits[0])
+        sums = gate_up(order, near_places, gate_weight, up_weight, spread(block), None)
+        across, sums = lax.optimization_barrier((across, sums))
+        return far_half(across, sums)
+
     def settle(k, far, partial):
         return tuple(
             down_last(order, far_places, offsets, counts, k, down_weight, far, partial, experts, depth)
@@ -510,16 +492,19 @@
         if k < BATCHES - 1:
             moving = after(later[k], blocks)
             arrived.append([moving[0]] + [along_expert(moving[shift], shift) for shift in range(1, experts)])
+        if k == 0:
+            far, partial = fenced(k, whole_chain, *blocks)
+            moved = partial
+            continue
         block = fenced(k, lambda *blocks: compact(offsets, counts, k, blocks, size), *blocks)
         across = swap(block, bits[0])
         near = spread(block)
-        if k > 0:
-            far, partial = after((far, partial), block)
-            results = fenced(k, functools.partial(settle, k - 1), far, partial)
-            if k > 1:
-                results, waiting[k - 2] = lax.optimization_barrier((results, waiting[k - 2]))
-            waiting.append(send_back(results))
-            near = after(near, results)
+        far, partial = after((far, partial), block)
+        results = fenced(k, functools.partial(settle, k - 1), far, partial)
+        if k > 1:
+            results, waiting[k - 2] = lax.optimization_barrier((results, waiting[k - 2]))
+        waiting.append(send_back(results))
+        near = after(near, results)
         sums = fenced(k, lambda *near: gate_up(order, near_places, gate_weight, up_weight, near, None), *near)
         across, sums = lax.optimization_barrier((across, sums))
         far, partial = fenced(k, far_half, across, sums)

time: 126 us -> 130 us (1.032)
  starting transfers between devices: 26.2 us -> 28.8 us
    ppermute x12, starting transfers between devices: 16.5 us -> 19.1 us  [along_expert(): lax.ppermute(x, 'expert', [(i, (i + shift) % experts) for i in range(expe...]
    ppermute x14, waiting for transfers between devices: 25.1 us -> 27.3 us  [swap(): return lax.ppermute(x, 'dp', [(i, i ^ bit) for i in range(width_parts)])]
    ppermute x12, waiting for transfers between devices: 21.3 us -> 19.6 us  [along_expert(): lax.ppermute(x, 'expert', [(i, (i + shift) % experts) for i in range(expe...]
    pallas_call x2, Pallas kernels: 6.6 us -> 8.16 us  [down_last(): pl.pallas_call(functools.partial(down_last_kernel, parts, places, experts...]
  transfers between devices with their start and end apart: 28 -> 28, of which waited for: 14 -> 15; matrix products, arithmetic and copies ran while one was open for 3% -> 3% of each run, Pallas kernels for 21% -> 23%
where the time goes in v6:
time: 130 us; the launch traced here: 129 us
  waiting for transfers between devices  56.7 us (44%)
  Pallas kernels  38.5 us (30%)
  starting transfers between devices  28.8 us (22%)
  other arithmetic  2.99 us (2%)
  between operations  1.34 us (1%)
    ppermute x14, waiting for transfers between devices, swap(): return lax.ppermute(x, 'dp', [(i, i ^ bit) for i in range(width_parts)])  27.3 us
    ppermute x12, waiting for transfers between devices, along_expert(): lax.ppermute(x, 'expert', [(i, (i + shift) % experts) for i in range(expe...  19.6 us
    ppermute x12, starting transfers between devices, along_expert(): lax.ppermute(x, 'expert', [(i, (i + shift) % experts) for i in range(expe...  19.1 us
    pallas_call x4, Pallas kernels, gate_up(): pl.pallas_call(functools.partial(gate_up_kernel, parts, places, last), ou...  11.9 us
    ppermute x2, waiting for transfers between devices, swap_expert(): return lax.ppermute(x, 'expert', [(i, i ^ bit) for i in range(experts)])  9.82 us
    ppermute x14, starting transfers between devices, swap(): return lax.ppermute(x, 'dp', [(i, i ^ bit) for i in range(width_parts)])  8.36 us
    pallas_call x2, Pallas kernels, down_last(): pl.pallas_call(functools.partial(down_last_kernel, parts, places, experts...  8.16 us
    pallas_call x2, Pallas kernels, compact(): pl.pallas_call(functools.partial(compact_kernel, experts, k), out_shape=j...  4.95 us
  transfers between devices with their start and end apart: 28, of which 15 were waited for; matrix products, arithmetic and copies ran while one was open for 3% of the time, Pallas kernels for 23%

profile of v6, /device:TPU:0, one launch (start us, length us, event | category | flops | bytes accessed | tf_op | source)
XLA Modules:
  0.0 129.2 jit_solution(3649735982614409475)
XLA Ops:
  0.0 4.0 %shard_map.64 = (s32[4,512]{1,0:T(4,128)S(1)}, f32[4,512]{1,0:T(4,128)S(1)}, bf16[128,1024]{1,0:T(8,128)(2,1)}, bf16[128,1024]{1,0:T(8,128)(2,1)}, bf16[128,1024]{1,0:T(8,128)(2,1)}, /*index=5*/bf16[128,1024]{1,0:T(8,128)(2,1)}) custom-call(s32[1]{0:T(128)} %bitcast.1.place_ref, s32[4,512]{1,0:T(4,128)} %picks_in.1, bf16[4,1024]{1,0:T(4,128)(2,1)} %bitcast.8, ...), custom_call_target="tpu_custom_call" | custom-call | flops 1024 | bytes 1024 | tf_op jit(solution)/shard_map/pallas_call | solution.py:106
  4.0 3.1 %collective-permute-start.14 = (bf16[128,1024]{1,0:T(8,128)(2,1)}, bf16[128,1024]{1,0:T(8,128)(2,1)S(1)}, u32[]{:S(2)}, u32[]{:S(2)}) collective-permute-start(bf16[128,1024]{1,0:T(8,128)(2,1)} %get-tuple-element.222), channel_id=1, source_target_pairs={{0,4},{4,8},{8,12},{12,0},{1,5},{5,9},{9,13},{13,1},{2,6},{6,10},{... | collective-permute-start | bytes 786440 | tf_op jit(solution)/shard_map/ppermute | solution.py:399
  7.1 2.6 %collective-permute-start.15 = (bf16[128,1024]{1,0:T(8,128)(2,1)}, bf16[128,1024]{1,0:T(8,128)(2,1)S(1)}, u32[]{:S(2)}, u32[]{:S(2)}) collective-permute-start(bf16[128,1024]{1,0:T(8,128)(2,1)} %get-tuple-element.223), channel_id=1, source_target_pairs={{0,8},{4,12},{8,0},{12,4},{1,9},{5,13},{9,1},{13,5},{2,10},{6,14},... | collective-permute-start | bytes 786440 | tf_op jit(solution)/shard_map/ppermute | solution.py:399
  13.3 20.7 %conditional.7 = (bf16[128,1024]{1,0:T(8,128)(2,1)S(1)}, bf16[128,1024]{1,0:T(8,128)(2,1)}, bf16[128,1024]{1,0:T(8,128)(2,1)}, bf16[128,1024]{1,0:T(8,128)(2,1)}...) conditional(s32[]{:T(128)} %convert_element_type.19, () %tuple.67, (s32[4,512]{1,0:T(4,128)S(1)}, ...), branch_computations={%region_3.4_spmd, %region_4.5_spmd} | conditional | flops 25600 | bytes 1089600 | solution.py:456
  14.9 2.2 %collective-permute-done.10 = f32[4,512]{1,0:T(4,128)S(1)} collective-permute-done((f32[4,512]{1,0:T(4,128)S(1)}, f32[4,512]{1,0:T(4,128)S(1)}, u32[]{:S(2)}, u32[]{:S(2)}) %collective-permute-start.10) | collective-permute-done | bytes 8224 | tf_op jit(solution)/shard_map/cond/branch_1_fun/ppermute | solution.py:402
  19.5 7.5 %collective-permute-done.12 = f32[1,4,512]{2,1,0:T(4,128)S(1)} collective-permute-done((f32[1,4,512]{2,1,0:T(4,128)}, f32[1,4,512]{2,1,0:T(4,128)S(1)}, u32[]{:S(2)}, u32[]{:S(2)}) %collective-permute-start.12) | collective-permute-done | bytes 8224 | tf_op jit(solution)/shard_map/cond/branch_1_fun/ppermute | solution.py:418
  28.4 2.6 %branch_1_fun.11 = (bf16[128,1024]{1,0:T(8,128)(2,1)S(1)}, bf16[128,1024]{1,0:T(8,128)(2,1)}, bf16[128,1024]{1,0:T(8,128)(2,1)}, bf16[128,1024]{1,0:T(8,128)(2,1)}) custom-call(s32[4,512]{1,0:T(4,128)S(1)} %get-tuple-element.98.code_ref, bf16[512,1024]{1,0:T(8,128)(2,1)} %get-tuple-element.99.tokens_ref), custom_call_target="tpu_custom_call" | custom-call | flops 1024 | bytes 1024 | tf_op jit(solution)/shard_map/cond/branch_1_fun/pallas_call | solution.py:137
  31.0 2.3 %collective-permute-done.13 = f32[2,4,512]{2,1,0:T(4,128)S(1)} collective-permute-done((f32[2,4,512]{2,1,0:T(4,128)S(1)}, f32[2,4,512]{2,1,0:T(4,128)S(1)}, u32[]{:S(2)}, u32[]{:S(2)}) %collective-permute-start.13) | collective-permute-done | bytes 16416 | tf_op jit(solution)/shard_map/cond/branch_1_fun/ppermute | solution.py:418
  34.1 2.1 %collective-permute-start.18 = (bf16[128,1024]{1,0:T(8,128)(2,1)}, bf16[128,1024]{1,0:T(8,128)(2,1)}, u32[]{:S(2)}, u32[]{:S(2)}) collective-permute-start(bf16[128,1024]{1,0:T(8,128)(2,1)} %get-tuple-element.231), channel_id=1, source_target_pairs={{0,8},{4,12},{8,0},{12,4},{1,9},{5,13},{9,1},{13,5},{2,10},{6,14},... | collective-permute-start | bytes 786440 | tf_op jit(solution)/shard_map/ppermute | solution.py:399
  38.5 27.6 %conditional.8 = (bf16[256,256]{1,0:T(8,128)(2,1)}, bf16[256,256]{1,0:T(8,128)(2,1)}, f32[256,1024]{1,0:T(8,128)S(1)}) conditional(s32[]{:T(128)} %convert_element_type.19, () %tuple.74, (s32[2,4]{1,0:T(2,128)S(1)}, s32[2,4]{1,0:T(2,128)S(1)}, bf16[128,1024]{1,0:T(8,128)(2,1)}, bf16[128,1024]{1,0:T(8,128)(2,1)S(1)}, bf16[128,1024]{1,0:T(8,128)(2,1)S(1)}, ...), branch_computations={%region_6.7_spmd, %region_7.8_spmd} | conditional | flops 4096 | bytes 24645952 | solution.py:482
  38.5 2.0 %branch_1_fun.12.refs_0_ = bf16[256,1024]{1,0:T(8,128)(2,1)S(1)} custom-call(s32[2,4]{1,0:T(2,128)S(1)} %get-tuple-element.108.offset_ref, s32[2,4]{1,0:T(2,128)S(1)} %get-tuple-element.109.count_ref, bf16[128,1024]{1,0:T(8,128)(2,1)} %get-tuple-element.110.refs_0_, bf16[128,1024]{1,0:T(8,128)(2,1)S(1)} %get-tuple-element.111.refs_1_, ...), custom_call_target="tpu_custom_call" | custom-call | flops 1024 | bytes 1024 | tf_op jit(solution)/shard_map/cond/branch_1_fun/pallas_call | solution.py:174
  42.5 2.6 %branch_1_fun.13 = (f32[256,256]{1,0:T(8,128)S(1)}, f32[256,256]{1,0:T(8,128)S(1)}) custom-call(s32[4]{0:T(128)S(1)} %get-tuple-element.105.order_ref, bf16[1,4096,256]{2,1,0:T(8,128)(2,1)S(1)} %get-tuple-element.106.gate_ref, bf16[1,4096,256]{2,1,0:T(8,128)(2,1)} %get-tuple-element.107.up_ref, bf16[256,1024]{1,0:T(8,128)(2,1)S(1)} %branch_1_fun.12.refs_0_, ...), custom_call_target="tpu_custom_call" | custom-call | flops 1024 | bytes 1024 | tf_op jit(solution)/shard_map/cond/branch_1_fun/pallas_call | solution.py:216
  45.2 9.8 %collective-permute-done.refs_0_ = bf16[256,1024]{1,0:T(8,128)(2,1)S(1)} collective-permute-done((bf16[256,1024]{1,0:T(8,128)(2,1)S(1)}, bf16[256,1024]{1,0:T(8,128)(2,1)S(1)}, u32[]{:S(2)}, u32[]{:S(2)}) %collective-permute-start) | collective-permute-done | bytes 524320 | tf_op jit(solution)/shard_map/cond/branch_1_fun/ppermute | solution.py:402
  55.0 1.9 %collective-permute-done.2.refs_1_ = bf16[256,1024]{1,0:T(8,128)(2,1)S(1)} collective-permute-done((bf16[256,1024]{1,0:T(8,128)(2,1)S(1)}, bf16[256,1024]{1,0:T(8,128)(2,1)S(1)}, u32[]{:S(2)}, u32[]{:S(2)}) %collective-permute-start.2) | collective-permute-done | bytes 524320 | tf_op jit(solution)/shard_map/cond/branch_1_fun/ppermute | solution.py:402
  61.4 3.0 %collective-permute-done.3 = bf16[256,256]{1,0:T(8,128)(2,1)} collective-permute-done((bf16[256,256]{1,0:T(8,128)(2,1)S(1)}, bf16[256,256]{1,0:T(8,128)(2,1)}, u32[]{:S(2)}, u32[]{:S(2)}) %collective-permute-start.3) | collective-permute-done | bytes 131104 | tf_op jit(solution)/shard_map/cond/branch_1_fun/ppermute | solution.py:402
  66.1 3.0 %conditional.9 = (bf16[256,1024]{1,0:T(8,128)(2,1)}) conditional(s32[]{:T(128)} %convert_element_type.20, () %tuple.71, (s32[2,4]{1,0:T(2,128)S(1)}, s32[2,4]{1,0:T(2,128)S(1)}, bf16[128,1024]{1,0:T(8,128)(2,1)S(1)}, bf16[128,1024]{1,0:T(8,128)(2,1)}, bf16[128,1024]{1,0:T(8,128)(2,1)}, /*index=5*/bf16[128,1024]{1,0:T(8,128)(2,1)}) %tuple.77), branch_computations={%region_8.9_spmd, %region_9.10_spmd} | conditional | flops 1024 | bytes 524298 | solution.py:482
  66.1 3.0 %branch_1_fun.16 = bf16[256,1024]{1,0:T(8,128)(2,1)} custom-call(s32[2,4]{1,0:T(2,128)S(1)} %get-tuple-element.122.offset_ref, s32[2,4]{1,0:T(2,128)S(1)} %get-tuple-element.123.count_ref, bf16[128,1024]{1,0:T(8,128)(2,1)S(1)} %get-tuple-element.124.refs_0_, bf16[128,1024]{1,0:T(8,128)(2,1)} %get-tuple-element.125.refs_1_, ...), custom_call_target="tpu_custom_call" | custom-call | flops 1024 | bytes 1024 | tf_op jit(solution)/shard_map/cond/branch_1_fun/pallas_call | solution.py:174
  70.8 4.1 %conditional.10 = ((bf16[128,1024]{1,0:T(8,128)(2,1)S(1)}, bf16[128,1024]{1,0:T(8,128)(2,1)}, bf16[128,1024]{1,0:T(8,128)(2,1)}, bf16[128,1024]{1,0:T(8,128)(2,1)})) conditional(s32[]{:T(128)} %convert_element_type.20, () %tuple.79, (s32[4]{0:T(128)S(1)}, s32[2,4]{1,0:T(2,128)S(1)}, s32[2,4]{1,0:T(2,128)S(1)}, bf16[1,1024,1024]{2,1,0:T(8,128)(2,1)}, ...), branch_computations={%region_10.11_spmd, %region_11.12_spmd} | conditional | flops 1024 | bytes 1048624 | solution.py:482
  70.8 4.1 %branch_1_fun.17 = (bf16[128,1024]{1,0:T(8,128)(2,1)S(1)}, bf16[128,1024]{1,0:T(8,128)(2,1)}, bf16[128,1024]{1,0:T(8,128)(2,1)}, bf16[128,1024]{1,0:T(8,128)(2,1)}) custom-call(s32[4]{0:T(128)S(1)} %get-tuple-element.128.order_ref, s32[2,4]{1,0:T(2,128)S(1)} %get-tuple-element.129.offset_ref, s32[2,4]{1,0:T(2,128)S(1)} %get-tuple-element.130.count_ref, ...), custom_call_target="tpu_custom_call" | custom-call | flops 1024 | bytes 1024 | tf_op jit(solution)/shard_map/cond/branch_1_fun/pallas_call | solution.py:289
  77.1 1.9 %collective-permute-start.24 = (bf16[128,1024]{1,0:T(8,128)(2,1)}, bf16[128,1024]{1,0:T(8,128)(2,1)S(1)}, u32[]{:S(2)}, u32[]{:S(2)}) collective-permute-start(bf16[128,1024]{1,0:T(8,128)(2,1)} %get-tuple-element.246), channel_id=1, source_target_pairs={{0,4},{4,8},{8,12},{12,0},{1,5},{5,9},{9,13},{13,1},{2,6},{6,10},{... | collective-permute-start | bytes 786440 | tf_op jit(solution)/shard_map/ppermute | solution.py:399
  79.1 4.2 %conditional.11 = ((f32[256,256]{1,0:T(8,128)}, f32[256,256]{1,0:T(8,128)S(1)})) conditional(s32[]{:T(128)} %convert_element_type.20, () %tuple.78, (s32[4]{0:T(128)S(1)}, bf16[1,4096,256]{2,1,0:T(8,128)(2,1)S(1)}, bf16[1,4096,256]{2,1,0:T(8,128)(2,1)}, bf16[256,1024]{1,0:T(8,128)(2,1)}, bf16[256,1024]{1,0:T(8,128)(2,1)}) %tuple.114), branch_computations={%region_12.13_spmd, %region_13.14_spmd} | conditional | flops 1024 | bytes 524320 | solution.py:482
  79.1 4.2 %branch_1_fun.18 = (f32[256,256]{1,0:T(8,128)}, f32[256,256]{1,0:T(8,128)S(1)}) custom-call(s32[4]{0:T(128)S(1)} %get-tuple-element.135.order_ref, bf16[1,4096,256]{2,1,0:T(8,128)(2,1)S(1)} %get-tuple-element.136.gate_ref, bf16[1,4096,256]{2,1,0:T(8,128)(2,1)} %get-tuple-element.137.up_ref, bf16[256,1024]{1,0:T(8,128)(2,1)} %get-tuple-element.138.refs_0_, ...), custom_call_target="tpu_custom_call" | custom-call | flops 1024 | bytes 1024 | tf_op jit(solution)/shard_map/cond/branch_1_fun/pallas_call | solution.py:216
  83.8 13.5 %conditional.12 = (bf16[256,256]{1,0:T(8,128)(2,1)}, bf16[256,256]{1,0:T(8,128)(2,1)}, f32[256,1024]{1,0:T(8,128)S(1)}) conditional(s32[]{:T(128)} %convert_element_type.20, () %tuple.70, (bf16[256,1024]{1,0:T(8,128)(2,1)}, s32[4]{0:T(128)S(1)}, bf16[1,4096,256]{2,1,0:T(8,128)(2,1)S(1)}, bf16[1,4096,256]{2,1,0:T(8,128)(2,1)}, ...), branch_computations={%region_14.15_spmd, %region_15.16_spmd} | conditional | flops 2048 | bytes 12060884 | solution.py:482
  83.8 2.1 %collective-permute-done.6.refs_1_ = bf16[256,1024]{1,0:T(8,128)(2,1)S(1)} collective-permute-done((bf16[256,1024]{1,0:T(8,128)(2,1)}, bf16[256,1024]{1,0:T(8,128)(2,1)S(1)}, u32[]{:S(2)}, u32[]{:S(2)}) %collective-permute-start.6) | collective-permute-done | bytes 524320 | tf_op jit(solution)/shard_map/cond/branch_1_fun/ppermute | solution.py:402
  85.9 3.6 %branch_1_fun.19.refs_0_ = bf16[256,256]{1,0:T(8,128)(2,1)S(1)} custom-call(s32[4]{0:T(128)S(1)} %get-tuple-element.140.order_ref, bf16[1,4096,256]{2,1,0:T(8,128)(2,1)S(1)} %get-tuple-element.141.gate_ref, bf16[1,4096,256]{2,1,0:T(8,128)(2,1)} %get-tuple-element.142.up_ref, bf16[256,1024]{1,0:T(8,128)(2,1)} %get-tuple-element.143.refs_0_, ...), custom_call_target="tpu_custom_call" | custom-call | flops 1024 | bytes 1024 | tf_op jit(solution)/shard_map/cond/branch_1_fun/pallas_call | solution.py:216
  92.6 3.0 %collective-permute-done.7 = bf16[256,256]{1,0:T(8,128)(2,1)} collective-permute-done((bf16[256,256]{1,0:T(8,128)(2,1)S(1)}, bf16[256,256]{1,0:T(8,128)(2,1)}, u32[]{:S(2)}, u32[]{:S(2)}) %collective-permute-start.7) | collective-permute-done | bytes 131104 | tf_op jit(solution)/shard_map/cond/branch_1_fun/ppermute | solution.py:402
  97.3 4.0 %conditional.13 = ((bf16[128,1024]{1,0:T(8,128)(2,1)S(1)}, bf16[128,1024]{1,0:T(8,128)(2,1)}, bf16[128,1024]{1,0:T(8,128)(2,1)}, bf16[128,1024]{1,0:T(8,128)(2,1)S(1)})) conditional(s32[]{:T(128)} %convert_element_type.19, () %tuple.69, (s32[4]{0:T(128)S(1)}, s32[2,4]{1,0:T(2,128)S(1)}, s32[2,4]{1,0:T(2,128)S(1)}, ...), branch_computations={%region_16.17_spmd, %region_17.18_spmd} | conditional | flops 1024 | bytes 1048624 | solution.py:482
  97.3 4.0 %branch_1_fun.21 = (bf16[128,1024]{1,0:T(8,128)(2,1)S(1)}, bf16[128,1024]{1,0:T(8,128)(2,1)}, bf16[128,1024]{1,0:T(8,128)(2,1)}, bf16[128,1024]{1,0:T(8,128)(2,1)S(1)}) custom-call(s32[4]{0:T(128)S(1)} %get-tuple-element.149.order_ref, s32[2,4]{1,0:T(2,128)S(1)} %get-tuple-element.150.offset_ref, s32[2,4]{1,0:T(2,128)S(1)} %get-tuple-element.151.count_ref, ...), custom_call_target="tpu_custom_call" | custom-call | flops 1024 | bytes 1024 | tf_op jit(solution)/shard_map/cond/branch_1_fun/pallas_call | solution.py:289
  103.5 1.9 %collective-permute-start.27 = (bf16[128,1024]{1,0:T(8,128)(2,1)S(1)}, bf16[128,1024]{1,0:T(8,128)(2,1)S(1)}, u32[]{:S(2)}, u32[]{:S(2)}) collective-permute-start(bf16[128,1024]{1,0:T(8,128)(2,1)S(1)} %get-tuple-element.264), channel_id=1, source_target_pairs={{0,4},{4,8},{8,12},{12,0},{1,5},{5,9},{9,13},{13,1},{2,6},{6,10},{... | collective-permute-start | bytes 786440 | tf_op jit(solution)/shard_map/ppermute | solution.py:399
  107.6 2.6 %collective-permute-done.25.refs_1_ = bf16[128,1024]{1,0:T(8,128)(2,1)S(1)} collective-permute-done((bf16[128,1024]{1,0:T(8,128)(2,1)}, bf16[128,1024]{1,0:T(8,128)(2,1)S(1)}, u32[]{:S(2)}, u32[]{:S(2)}) %collective-permute-start.25) | collective-permute-done | bytes 262176 | tf_op jit(solution)/shard_map/ppermute | solution.py:399
  110.2 17.0 %collective-permute-done.26.refs_2_ = bf16[128,1024]{1,0:T(8,128)(2,1)S(1)} collective-permute-done((bf16[128,1024]{1,0:T(8,128)(2,1)}, bf16[128,1024]{1,0:T(8,128)(2,1)S(1)}, u32[]{:S(2)}, u32[]{:S(2)}) %collective-permute-start.26) | collective-permute-done | bytes 262176 | tf_op jit(solution)/shard_map/ppermute | solution.py:399
  127.1 2.1 %shard_map.67 = bf16[512,1024]{1,0:T(8,128)(2,1)} custom-call(s32[4,512]{1,0:T(4,128)S(1)} %get-tuple-element.213.code_ref, f32[4,512]{1,0:T(4,128)S(1)} %shard_map.65.weight_ref, bf16[128,1024]{1,0:T(8,128)(2,1)S(1)} %get-tuple-element.261.refs_0_, bf16[128,1024]{1,0:T(8,128)(2,1)S(1)} %collective-permute-done.25.refs_1_, ...), custom_call_target="tpu_custom_call" | custom-call | flops 1024 | bytes 1024 | tf_op jit(solution)/shard_map/pallas_call | solution.py:368
  (66 shorter events, 32.6 us)
Async XLA Ops:
  0.0 38.5 %copy-start = (bf16[1,4096,256]{2,1,0:T(8,128)(2,1)S(1)}, bf16[1,4096,256]{2,1,0:T(8,128)(2,1)}, u32[]{:S(2)}) copy-start(bf16[1,4096,256]{2,1,0:T(8,128)(2,1)} %param.22) | copy-start | bytes 6291460
  4.0 30.0 %collective-permute-start.14 = (bf16[128,1024]{1,0:T(8,128)(2,1)}, bf16[128,1024]{1,0:T(8,128)(2,1)S(1)}, u32[]{:S(2)}, u32[]{:S(2)}) collective-permute-start(bf16[128,1024]{1,0:T(8,128)(2,1)} %get-tuple-element.222), channel_id=1, source_target_pairs={{0,4},{4,8},{8,12},{12,0},{1,5},{5,9},{9,13},{13,1},{2,6},{6,10},{... | collective-permute-start | bytes 786440 | tf_op jit(solution)/shard_map/ppermute | solution.py:399
  7.1 26.9 %collective-permute-start.15 = (bf16[128,1024]{1,0:T(8,128)(2,1)}, bf16[128,1024]{1,0:T(8,128)(2,1)S(1)}, u32[]{:S(2)}, u32[]{:S(2)}) collective-permute-start(bf16[128,1024]{1,0:T(8,128)(2,1)} %get-tuple-element.223), channel_id=1, source_target_pairs={{0,8},{4,12},{8,0},{12,4},{1,9},{5,13},{9,1},{13,5},{2,10},{6,14},... | collective-permute-start | bytes 786440 | tf_op jit(solution)/shard_map/ppermute | solution.py:399
  9.7 24.3 %collective-permute-start.16 = (bf16[128,1024]{1,0:T(8,128)(2,1)}, bf16[128,1024]{1,0:T(8,128)(2,1)S(1)}, u32[]{:S(2)}, u32[]{:S(2)}) collective-permute-start(bf16[128,1024]{1,0:T(8,128)(2,1)} %get-tuple-element.224), channel_id=1, source_target_pairs={{0,12},{4,0},{8,4},{12,8},{1,13},{5,1},{9,5},{13,9},{2,14},{6,2},{... | collective-permute-start | bytes 786440 | tf_op jit(solution)/shard_map/ppermute | solution.py:399
  13.3 3.7 %collective-permute-start.10 = (f32[4,512]{1,0:T(4,128)S(1)}, f32[4,512]{1,0:T(4,128)S(1)}, u32[]{:S(2)}, u32[]{:S(2)}) collective-permute-start(f32[4,512]{1,0:T(4,128)S(1)} %get-tuple-element.104), channel_id=1, source_target_pairs={{0,2},{1,3},{2,0},{3,1},{4,6},{5,7},{6,4},{7,5},{8,10},{9,11},{10,... | collective-permute-start | bytes 24584 | tf_op jit(solution)/shard_map/cond/branch_1_fun/ppermute | solution.py:402
  17.1 1.2 collective-permute-start.11
  18.8 8.2 %collective-permute-start.12 = (f32[1,4,512]{2,1,0:T(4,128)}, f32[1,4,512]{2,1,0:T(4,128)S(1)}, u32[]{:S(2)}, u32[]{:S(2)}) collective-permute-start(f32[1,4,512]{2,1,0:T(4,128)} %bitcast), channel_id=1, source_target_pairs={{0,4},{4,0},{8,12},{12,8},{1,5},{5,1},{9,13},{13,9},{2,6},{6,2},{1... | collective-permute-start | bytes 24584 | tf_op jit(solution)/shard_map/cond/branch_1_fun/ppermute | solution.py:418
  27.8 5.5 %collective-permute-start.13 = (f32[2,4,512]{2,1,0:T(4,128)S(1)}, f32[2,4,512]{2,1,0:T(4,128)S(1)}, u32[]{:S(2)}, u32[]{:S(2)}) collective-permute-start(f32[2,4,512]{2,1,0:T(4,128)S(1)} %pad_maximum_fusion.1), channel_id=1, source_target_pairs={{0,8},{4,12},{8,0},{12,4},{1,9},{5,13},{9,1},{13,5},{2,10},{6,14},... | collective-permute-start | bytes 49160 | tf_op jit(solution)/shard_map/cond/branch_1_fun/ppermute | solution.py:418
  34.0 32.1 %collective-permute-start.17 = (bf16[128,1024]{1,0:T(8,128)(2,1)}, bf16[128,1024]{1,0:T(8,128)(2,1)}, u32[]{:S(2)}, u32[]{:S(2)}) collective-permute-start(bf16[128,1024]{1,0:T(8,128)(2,1)} %get-tuple-element.230), channel_id=1, source_target_pairs={{0,4},{4,8},{8,12},{12,0},{1,5},{5,9},{9,13},{13,1},{2,6},{6,10},{... | collective-permute-start | bytes 786440 | tf_op jit(solution)/shard_map/ppermute | solution.py:399
  34.1 32.0 %collective-permute-start.18 = (bf16[128,1024]{1,0:T(8,128)(2,1)}, bf16[128,1024]{1,0:T(8,128)(2,1)}, u32[]{:S(2)}, u32[]{:S(2)}) collective-permute-start(bf16[128,1024]{1,0:T(8,128)(2,1)} %get-tuple-element.231), channel_id=1, source_target_pairs={{0,8},{4,12},{8,0},{12,4},{1,9},{5,13},{9,1},{13,5},{2,10},{6,14},... | collective-permute-start | bytes 786440 | tf_op jit(solution)/shard_map/ppermute | solution.py:399
  36.2 29.9 %collective-permute-start.19 = (bf16[128,1024]{1,0:T(8,128)(2,1)}, bf16[128,1024]{1,0:T(8,128)(2,1)}, u32[]{:S(2)}, u32[]{:S(2)}) collective-permute-start(bf16[128,1024]{1,0:T(8,128)(2,1)} %get-tuple-element.232), channel_id=1, source_target_pairs={{0,12},{4,0},{8,4},{12,8},{1,13},{5,1},{9,5},{13,9},{2,14},{6,2},{... | collective-permute-start | bytes 786440 | tf_op jit(solution)/shard_map/ppermute | solution.py:399
  40.5 2.0 %collective-permute-start.1 = (bf16[256,1024]{1,0:T(8,128)(2,1)S(1)}, bf16[256,1024]{1,0:T(8,128)(2,1)S(1)}, u32[]{:S(2)}, u32[]{:S(2)}) collective-permute-start(bf16[256,1024]{1,0:T(8,128)(2,1)S(1)} %branch_1_fun.12.refs_0_), channel_id=1, source_target_pairs={{0,1},{1,0},{2,3},{3,2},{4,5},{5,4},{6,7},{7,6},{8,9},{9,8},{10,11... | collective-permute-start | bytes 1572872 | tf_op jit(solution)/shard_map/cond/branch_1_fun/ppermute | solution.py:402
  40.6 14.3 %collective-permute-start = (bf16[256,1024]{1,0:T(8,128)(2,1)S(1)}, bf16[256,1024]{1,0:T(8,128)(2,1)S(1)}, u32[]{:S(2)}, u32[]{:S(2)}) collective-permute-start(bf16[256,1024]{1,0:T(8,128)(2,1)S(1)} %branch_1_fun.12.refs_0_), channel_id=1, source_target_pairs={{0,2},{1,3},{2,0},{3,1},{4,6},{5,7},{6,4},{7,5},{8,10},{9,11},{10,... | collective-permute-start | bytes 1572872 | tf_op jit(solution)/shard_map/cond/branch_1_fun/ppermute | solution.py:402
  42.5 14.4 %copy-start.1 = (bf16[1,4096,256]{2,1,0:T(8,128)(2,1)S(1)}, bf16[1,4096,256]{2,1,0:T(8,128)(2,1)}, u32[]{:S(2)}) copy-start(bf16[1,4096,256]{2,1,0:T(8,128)(2,1)} %get-tuple-element.107.up_ref) | copy-start | bytes 6291460 | tf_op jit(solution)/shard_map/cond
  55.0 5.1 %copy-start.2 = (bf16[1,1024,1024]{2,1,0:T(8,128)(2,1)S(1)}, bf16[1,1024,1024]{2,1,0:T(8,128)(2,1)}, u32[]{:S(2)}) copy-start(bf16[1,1024,1024]{2,1,0:T(8,128)(2,1)} %get-tuple-element.119.down_ref) | copy-start | bytes 6291460 | tf_op jit(solution)/shard_map/cond
  55.0 1.9 %collective-permute-start.2 = (bf16[256,1024]{1,0:T(8,128)(2,1)S(1)}, bf16[256,1024]{1,0:T(8,128)(2,1)S(1)}, u32[]{:S(2)}, u32[]{:S(2)}) collective-permute-start(bf16[256,1024]{1,0:T(8,128)(2,1)S(1)} %collective-permute-done.refs_0_), channel_id=1, source_target_pairs={{0,1},{1,0},{2,3},{3,2},{4,5},{5,4},{6,7},{7,6},{8,9},{9,8},{10,11... | collective-permute-start | bytes 1572872 | tf_op jit(solution)/shard_map/cond/branch_1_fun/ppermute | solution.py:402
  58.3 1.7 %collective-permute-start.4 = (bf16[256,256]{1,0:T(8,128)(2,1)S(1)}, bf16[256,256]{1,0:T(8,128)(2,1)S(1)}, u32[]{:S(2)}, u32[]{:S(2)}) collective-permute-start(bf16[256,256]{1,0:T(8,128)(2,1)S(1)} %branch_1_fun.14.refs_0_), channel_id=1, source_target_pairs={{0,1},{1,0},{2,3},{3,2},{4,5},{5,4},{6,7},{7,6},{8,9},{9,8},{10,11... | collective-permute-start | bytes 393224 | tf_op jit(solution)/shard_map/cond/branch_1_fun/ppermute | solution.py:402
  58.5 5.9 %collective-permute-start.3 = (bf16[256,256]{1,0:T(8,128)(2,1)S(1)}, bf16[256,256]{1,0:T(8,128)(2,1)}, u32[]{:S(2)}, u32[]{:S(2)}) collective-permute-start(bf16[256,256]{1,0:T(8,128)(2,1)S(1)} %branch_1_fun.14.refs_0_), channel_id=1, source_target_pairs={{0,2},{1,3},{2,0},{3,1},{4,6},{5,7},{6,4},{7,5},{8,10},{9,11},{10,... | collective-permute-start | bytes 393224 | tf_op jit(solution)/shard_map/cond/branch_1_fun/ppermute | solution.py:402
  64.4 1.7 %collective-permute-start.5 = (bf16[256,256]{1,0:T(8,128)(2,1)}, bf16[256,256]{1,0:T(8,128)(2,1)}, u32[]{:S(2)}, u32[]{:S(2)}) collective-permute-start(bf16[256,256]{1,0:T(8,128)(2,1)} %collective-permute-done.3), channel_id=1, source_target_pairs={{0,1},{1,0},{2,3},{3,2},{4,5},{5,4},{6,7},{7,6},{8,9},{9,8},{10,11... | collective-permute-start | bytes 393224 | tf_op jit(solution)/shard_map/cond/branch_1_fun/ppermute | solution.py:402
  69.1 10.0 %collective-permute-start.21 = (bf16[256,1024]{1,0:T(8,128)(2,1)}, bf16[256,1024]{1,0:T(8,128)(2,1)}, u32[]{:S(2)}, u32[]{:S(2)}) collective-permute-start(bf16[256,1024]{1,0:T(8,128)(2,1)} %get-tuple-element.322), channel_id=1, source_target_pairs={{0,1},{1,0},{2,3},{3,2},{4,5},{5,4},{6,7},{7,6},{8,9},{9,8},{10,11... | collective-permute-start | bytes 1572872 | tf_op jit(solution)/shard_map/ppermute | solution.py:402
  69.3 14.5 %collective-permute-start.20 = (bf16[256,1024]{1,0:T(8,128)(2,1)}, bf16[256,1024]{1,0:T(8,128)(2,1)}, u32[]{:S(2)}, u32[]{:S(2)}) collective-permute-start(bf16[256,1024]{1,0:T(8,128)(2,1)} %get-tuple-element.322), channel_id=1, source_target_pairs={{0,2},{1,3},{2,0},{3,1},{4,6},{5,7},{6,4},{7,5},{8,10},{9,11},{10,... | collective-permute-start | bytes 1572872 | tf_op jit(solution)/shard_map/ppermute | solution.py:402
  75.0 26.4 %collective-permute-start.22 = (bf16[128,1024]{1,0:T(8,128)(2,1)}, bf16[128,1024]{1,0:T(8,128)(2,1)S(1)}, u32[]{:S(2)}, u32[]{:S(2)}) collective-permute-start(bf16[128,1024]{1,0:T(8,128)(2,1)} %get-tuple-element.244), channel_id=1, source_target_pairs={{0,12},{4,0},{8,4},{12,8},{1,13},{5,1},{9,5},{13,9},{2,14},{6,2},{... | collective-permute-start | bytes 786440 | tf_op jit(solution)/shard_map/ppermute | solution.py:399
  75.7 25.7 %collective-permute-start.23 = (bf16[128,1024]{1,0:T(8,128)(2,1)}, bf16[128,1024]{1,0:T(8,128)(2,1)S(1)}, u32[]{:S(2)}, u32[]{:S(2)}) collective-permute-start(bf16[128,1024]{1,0:T(8,128)(2,1)} %get-tuple-element.245), channel_id=1, source_target_pairs={{0,8},{4,12},{8,0},{12,4},{1,9},{5,13},{9,1},{13,5},{2,10},{6,14},... | collective-permute-start | bytes 786440 | tf_op jit(solution)/shard_map/ppermute | solution.py:399
  77.1 24.3 %collective-permute-start.24 = (bf16[128,1024]{1,0:T(8,128)(2,1)}, bf16[128,1024]{1,0:T(8,128)(2,1)S(1)}, u32[]{:S(2)}, u32[]{:S(2)}) collective-permute-start(bf16[128,1024]{1,0:T(8,128)(2,1)} %get-tuple-element.246), channel_id=1, source_target_pairs={{0,4},{4,8},{8,12},{12,0},{1,5},{5,9},{9,13},{13,1},{2,6},{6,10},{... | collective-permute-start | bytes 786440 | tf_op jit(solution)/shard_map/ppermute | solution.py:399
  83.8 2.1 %collective-permute-start.6 = (bf16[256,1024]{1,0:T(8,128)(2,1)}, bf16[256,1024]{1,0:T(8,128)(2,1)S(1)}, u32[]{:S(2)}, u32[]{:S(2)}) collective-permute-start(bf16[256,1024]{1,0:T(8,128)(2,1)} %get-tuple-element.143.refs_0_), channel_id=1, source_target_pairs={{0,1},{1,0},{2,3},{3,2},{4,5},{5,4},{6,7},{7,6},{8,9},{9,8},{10,11... | collective-permute-start | bytes 1572872 | tf_op jit(solution)/shard_map/cond/branch_1_fun/ppermute | solution.py:402
  85.9 5.3 %copy-start.3 = (bf16[1,1024,1024]{2,1,0:T(8,128)(2,1)S(1)}, bf16[1,1024,1024]{2,1,0:T(8,128)(2,1)}, u32[]{:S(2)}) copy-start(bf16[1,1024,1024]{2,1,0:T(8,128)(2,1)} %get-tuple-element.146.down_ref) | copy-start | bytes 6291460 | tf_op jit(solution)/shard_map/cond
  89.5 1.7 %collective-permute-start.8 = (bf16[256,256]{1,0:T(8,128)(2,1)S(1)}, bf16[256,256]{1,0:T(8,128)(2,1)S(1)}, u32[]{:S(2)}, u32[]{:S(2)}) collective-permute-start(bf16[256,256]{1,0:T(8,128)(2,1)S(1)} %branch_1_fun.19.refs_0_), channel_id=1, source_target_pairs={{0,1},{1,0},{2,3},{3,2},{4,5},{5,4},{6,7},{7,6},{8,9},{9,8},{10,11... | collective-permute-start | bytes 393224 | tf_op jit(solution)/shard_map/cond/branch_1_fun/ppermute | solution.py:402
  89.7 5.9 %collective-permute-start.7 = (bf16[256,256]{1,0:T(8,128)(2,1)S(1)}, bf16[256,256]{1,0:T(8,128)(2,1)}, u32[]{:S(2)}, u32[]{:S(2)}) collective-permute-start(bf16[256,256]{1,0:T(8,128)(2,1)S(1)} %branch_1_fun.19.refs_0_), channel_id=1, source_target_pairs={{0,2},{1,3},{2,0},{3,1},{4,6},{5,7},{6,4},{7,5},{8,10},{9,11},{10,... | collective-permute-start | bytes 393224 | tf_op jit(solution)/shard_map/cond/branch_1_fun/ppermute | solution.py:402
  95.6 1.7 %collective-permute-start.9 = (bf16[256,256]{1,0:T(8,128)(2,1)}, bf16[256,256]{1,0:T(8,128)(2,1)}, u32[]{:S(2)}, u32[]{:S(2)}) collective-permute-start(bf16[256,256]{1,0:T(8,128)(2,1)} %collective-permute-done.7), channel_id=1, source_target_pairs={{0,1},{1,0},{2,3},{3,2},{4,5},{5,4},{6,7},{7,6},{8,9},{9,8},{10,11... | collective-permute-start | bytes 393224 | tf_op jit(solution)/shard_map/cond/branch_1_fun/ppermute | solution.py:402
  101.4 8.8 %collective-permute-start.25 = (bf16[128,1024]{1,0:T(8,128)(2,1)}, bf16[128,1024]{1,0:T(8,128)(2,1)S(1)}, u32[]{:S(2)}, u32[]{:S(2)}) collective-permute-start(bf16[128,1024]{1,0:T(8,128)(2,1)} %get-tuple-element.262), channel_id=1, source_target_pairs={{0,12},{4,0},{8,4},{12,8},{1,13},{5,1},{9,5},{13,9},{2,14},{6,2},{... | collective-permute-start | bytes 786440 | tf_op jit(solution)/shard_map/ppermute | solution.py:399
  102.9 24.2 %collective-permute-start.26 = (bf16[128,1024]{1,0:T(8,128)(2,1)}, bf16[128,1024]{1,0:T(8,128)(2,1)S(1)}, u32[]{:S(2)}, u32[]{:S(2)}) collective-permute-start(bf16[128,1024]{1,0:T(8,128)(2,1)} %get-tuple-element.263), channel_id=1, source_target_pairs={{0,8},{4,12},{8,0},{12,4},{1,9},{5,13},{9,1},{13,5},{2,10},{6,14},... | collective-permute-start | bytes 786440 | tf_op jit(solution)/shard_map/ppermute | solution.py:399
  103.5 23.6 %collective-permute-start.27 = (bf16[128,1024]{1,0:T(8,128)(2,1)S(1)}, bf16[128,1024]{1,0:T(8,128)(2,1)S(1)}, u32[]{:S(2)}, u32[]{:S(2)}) collective-permute-start(bf16[128,1024]{1,0:T(8,128)(2,1)S(1)} %get-tuple-element.264), channel_id=1, source_target_pairs={{0,4},{4,8},{8,12},{12,0},{1,5},{5,9},{9,13},{13,1},{2,6},{6,10},{... | collective-permute-start | bytes 786440 | tf_op jit(solution)/shard_map/ppermute | solution.py:399

commit v7 on v6

--- a/solution.py
+++ b/solution.py
@@ -182,49 +182,79 @@
     )(offsets, counts, *blocks)
 
 
-def gate_up_kernel(parts, places, last, order_ref, gate_ref, up_ref, *refs):
+def gate_up_near_kernel(parts, near, far, order_ref, gate_ref, up_ref, *refs):
     xs, refs = refs[:parts], refs[parts:]
-    if last:
-        gate_before, up_before, out_ref, *refs = refs
-    else:
-        gate_out, up_out, *refs = refs
-    x_held, sems = refs
+    gate_out, up_out, gate_far, up_far, gate_held, up_held, x_held, sems = refs
     width = xs[0].shape[1]
-    loads = start_all(xs, [x_held.at[i] for i in range(parts)], sems)
-    gate, up = (gate_before[...], up_before[...]) if last else (None, None)
+
+    def fetch(i, place, gate_to, up_to, base):
+        first = pl.multiple_of(order_ref[place] * width, width)
+        return start_all(
+            [gate_ref.at[0, pl.ds(first, width), :], up_ref.at[0, pl.ds(first, width), :]],
+            [gate_to.at[i], up_to.at[i]],
+            sems.at[pl.ds(base, 2)],
+        )
+
+    x_loads = start_all(xs, [x_held.at[i] for i in range(parts)], sems.at[pl.ds(0, parts)])
+    loads = [fetch(i, near[i], gate_held, up_held, parts + 2 * i) for i in range(parts)]
+    late = [fetch(i, far[i], gate_far, up_far, 3 * parts + 2 * i) for i in range(len(far))]
+    gate = up = None
     for i in range(parts):
-        first = pl.multiple_of(order_ref[places[i]] * width, width)
-        loads[i].wait()
+        for copy in [x_loads[i]] + loads[i]:
+            copy.wait()
         x = x_held[i]
-        gate_term = dot(x, gate_ref[0, pl.ds(first, width), :])
-        up_term = dot(x, up_ref[0, pl.ds(first, width), :])
+        gate_term = dot(x, gate_held[i])
+        up_term = dot(x, up_held[i])
         gate = gate_term if gate is None else gate + gate_term
         up = up_term if up is None else up + up_term
-    if last:
-        out_ref[...] = (gate * jax.nn.sigmoid(gate) * up).astype(BF16)
-    else:
-        gate_out[...] = gate
-        up_out[...] = up
-
-
-def gate_up(order, places, gate_weight, up_weight, xs, before):
+    gate_out[...] = gate
+    up_out[...] = up
+    for copies in late:
+        for copy in copies:
+            copy.wait()
+
+
+def gate_up_near(order, near, far, gate_weight, up_weight, xs):
     parts = len(xs)
     size, width = xs[0].shape
     units = gate_weight.shape[2]
-    last = before is not None
-    sums = [jax.ShapeDtypeStruct((size, units), F32)] * 2
-    return pl.pallas_call(
-        functools.partial(gate_up_kernel, parts, places, last),
-        out_shape=jax.ShapeDtypeStruct((size, units), BF16) if last else sums,
-        in_specs=[smem()] + whole(2) + apart(parts) + (whole(2) if last else []),
-        out_specs=whole(1)[0] if last else whole(2),
+    held = jax.ShapeDtypeStruct((len(far), width, units), BF16)
+    return pl.pallas_call(
+        functools.partial(gate_up_near_kernel, parts, near, far),
+        out_shape=[jax.ShapeDtypeStruct((size, units), F32)] * 2 + [held] * 2,
+        in_specs=[smem()] + apart(2 + parts),
+        out_specs=whole(4),
         scratch_shapes=[
+            pltpu.VMEM((parts, width, units), BF16),
+            pltpu.VMEM((parts, width, units), BF16),
             pltpu.VMEM((parts, size, width), BF16),
-            pltpu.SemaphoreType.DMA((parts,)),
+            pltpu.SemaphoreType.DMA((3 * parts + 2 * len(far),)),
         ],
         compiler_params=params(),
         cost_estimate=COST,
-    )(order, gate_weight, up_weight, *xs, *(before or []))
+    )(order, gate_weight, up_weight, *xs)
+
+
+def gate_up_far_kernel(parts, gate_before, up_before, gate_ref, up_ref, *refs):
+    xs, out_ref = refs[:parts], refs[parts]
+    gate, up = gate_before[...], up_before[...]
+    for i in range(parts):
+        x = xs[i][...]
+        gate = gate + dot(x, gate_ref[i])
+        up = up + dot(x, up_ref[i])
+    out_ref[...] = (gate * jax.nn.sigmoid(gate) * up).astype(BF16)
+
+
+def gate_up_far(xs, before):
+    size, units = before[0].shape
+    return pl.pallas_call(
+        functools.partial(gate_up_far_kernel, len(xs)),
+        out_shape=jax.ShapeDtypeStruct((size, units), BF16),
+        in_specs=whole(4 + len(xs)),
+        out_specs=whole(1)[0],
+        compiler_params=params(),
+        cost_estimate=COST,
+    )(*before, *xs)
 
 
 def down_sum(places, order_ref, down_ref, hs, h_held, sems, total):
@@ -457,18 +487,11 @@
 
     def far_half(far, sums):
         far = spread(far)
-        hidden = gate_up(order, far_places, gate_weight, up_weight, far, sums)
+        hidden = gate_up_far(far, sums)
         far = swap(hidden, bits[0])
         partial = down_first(order, near_places, down_weight, spread(hidden))
         far, partial = lax.optimization_barrier((far, partial))
         return spread(far), partial
-
-    def whole_chain(*blocks):
-        block = compact(offsets, counts, 0, blocks, size)
-        across = swap(block, bits[0])
-        sums = gate_up(order, near_places, gate_weight, up_weight, spread(block), None)
-        across, sums = lax.optimization_barrier((across, sums))
-        return far_half(across, sums)
 
     def settle(k, far, partial):
         return tuple(
@@ -492,24 +515,21 @@
         if k < BATCHES - 1:
             moving = after(later[k], blocks)
             arrived.append([moving[0]] + [along_expert(moving[shift], shift) for shift in range(1, experts)])
-        if k == 0:
-            far, partial = fenced(k, whole_chain, *blocks)
-            moved = partial
-            continue
-        block = fenced(k, lambda *blocks: compact(offsets, counts, k, blocks, size), *blocks)
+        block = compact(offsets, counts, k, blocks, size)
         across = swap(block, bits[0])
         near = spread(block)
-        far, partial = after((far, partial), block)
-        results = fenced(k, functools.partial(settle, k - 1), far, partial)
-        if k > 1:
-            results, waiting[k - 2] = lax.optimization_barrier((results, waiting[k - 2]))
-        waiting.append(send_back(results))
-        near = after(near, results)
-        sums = fenced(k, lambda *near: gate_up(order, near_places, gate_weight, up_weight, near, None), *near)
+        if k > 0:
+            far, partial = after((far, partial), block)
+            results = settle(k - 1, far, partial)
+            if k > 1:
+                results, waiting[k - 2] = lax.optimization_barrier((results, waiting[k - 2]))
+            waiting.append(send_back(results))
+            near = after(near, results)
+        sums = gate_up_near(order, near_places, far_places, gate_weight, up_weight, near)
         across, sums = lax.optimization_barrier((across, sums))
         far, partial = fenced(k, far_half, across, sums)
         moved = partial
-    results = fenced(0, functools.partial(settle, BATCHES - 1), far, partial)
+    results = settle(BATCHES - 1, far, partial)
     results, waiting[-1] = lax.optimization_barrier((results, waiting[-1]))
     waiting.append(send_back(results))
     weights = slot_weights(place, logits, after(gathered, results), code)

time: 130 us -> 125 us (0.962)
  Pallas kernels: 38.5 us -> 32.9 us
  local copies, waits for them, and re-layouts: 0.72 us -> 5.55 us
  starting transfers between devices: 28.8 us -> 26.3 us
  waiting for transfers between devices: 56.7 us -> 55.4 us
    unnamed x2 -> x18, local copies, waits for them, and re-layouts: 0.01 us -> 4.85 us
    pallas_call x4, Pallas kernels: 11.9 us -> 7.18 us  [the longest x2 3.65 us: gate_up_near(): pl.pallas_call(functools.partial(gate_up_near_kernel, parts, near, far),...]
    ppermute x14, waiting for transfers between devices: 27.3 us -> 24.1 us  [swap(): return lax.ppermute(x, 'dp', [(i, i ^ bit) for i in range(width_parts)])]
    ppermute x12, starting transfers between devices: 19.1 us -> 16.6 us  [along_expert(): lax.ppermute(x, 'expert', [(i, (i + shift) % experts) for i in range(expe...]
    ppermute x12, waiting for transfers between devices: 19.6 us -> 21.5 us  [along_expert(): lax.ppermute(x, 'expert', [(i, (i + shift) % experts) for i in range(expe...]
    pallas_call x2, Pallas kernels: 4.95 us -> 3.26 us  [compact(): pl.pallas_call(functools.partial(compact_kernel, experts, k), out_shape=j...]
  transfers between devices with their start and end apart: 28 -> 28, of which waited for: 15 -> 15; matrix products, arithmetic and copies ran while one was open for 3% -> 3% of each run, Pallas kernels for 23% -> 19%
where the time goes in v7:
time: 125 us
  waiting for transfers between devices  55.4 us (44%)
  Pallas kernels  32.9 us (26%)
  starting transfers between devices  26.3 us (21%)
  local copies, waits for them, and re-layouts  5.55 us (4%)
  other arithmetic  2.98 us (2%)
  between operations  1.41 us (1%)
    ppermute x14, waiting for transfers between devices, swap(): return lax.ppermute(x, 'dp', [(i, i ^ bit) for i in range(width_parts)])  24.1 us
    ppermute x12, waiting for transfers between devices, along_expert(): lax.ppermute(x, 'expert', [(i, (i + shift) % experts) for i in range(expe...  21.5 us
    ppermute x12, starting transfers between devices, along_expert(): lax.ppermute(x, 'expert', [(i, (i + shift) % experts) for i in range(expe...  16.6 us
    ppermute x2, waiting for transfers between devices, swap_expert(): return lax.ppermute(x, 'expert', [(i, i ^ bit) for i in range(experts)])  9.76 us
    ppermute x14, starting transfers between devices, swap(): return lax.ppermute(x, 'dp', [(i, i ^ bit) for i in range(width_parts)])  8.36 us
    pallas_call x2, Pallas kernels, down_last(): pl.pallas_call(functools.partial(down_last_kernel, parts, places, experts...  8.14 us
    unnamed x18, local copies, waits for them, and re-layouts  4.85 us
    pallas_call x2, Pallas kernels, combine(): pl.pallas_call(functools.partial(combine_kernel, experts, k), out_shape=j...  3.97 us
  transfers between devices with their start and end apart: 28, of which 15 were waited for; matrix products, arithmetic and copies ran while one was open for 3% of the time, Pallas kernels for 19%

profile of v7, /device:TPU:0, one launch (start us, length us, event | category | flops | bytes accessed | tf_op | source)
XLA Modules:
  0.0 124.6 jit_solution(13977485962573549752)
XLA Ops:
  0.0 3.9 %shard_map.64 = (s32[4,512]{1,0:T(4,128)S(1)}, f32[4,512]{1,0:T(4,128)S(1)}, bf16[128,1024]{1,0:T(8,128)(2,1)}, bf16[128,1024]{1,0:T(8,128)(2,1)}, bf16[128,1024]{1,0:T(8,128)(2,1)}, /*index=5*/bf16[128,1024]{1,0:T(8,128)(2,1)}) custom-call(s32[1]{0:T(128)} %bitcast.1.place_ref, s32[4,512]{1,0:T(4,128)} %picks_in.1, bf16[4,1024]{1,0:T(4,128)(2,1)} %bitcast.8, ...), custom_call_target="tpu_custom_call" | custom-call | flops 1024 | bytes 1024 | tf_op jit(solution)/shard_map/pallas_call | solution.py:106
  3.9 3.1 %collective-permute-start.12 = (bf16[128,1024]{1,0:T(8,128)(2,1)}, bf16[128,1024]{1,0:T(8,128)(2,1)S(1)}, u32[]{:S(2)}, u32[]{:S(2)}) collective-permute-start(bf16[128,1024]{1,0:T(8,128)(2,1)} %get-tuple-element.143), channel_id=1, source_target_pairs={{0,4},{4,8},{8,12},{12,0},{1,5},{5,9},{9,13},{13,1},{2,6},{6,10},{... | collective-permute-start | bytes 786440 | tf_op jit(solution)/shard_map/ppermute | solution.py:429
  7.0 2.6 %collective-permute-start.13 = (bf16[128,1024]{1,0:T(8,128)(2,1)}, bf16[128,1024]{1,0:T(8,128)(2,1)S(1)}, u32[]{:S(2)}, u32[]{:S(2)}) collective-permute-start(bf16[128,1024]{1,0:T(8,128)(2,1)} %get-tuple-element.144), channel_id=1, source_target_pairs={{0,8},{4,12},{8,0},{12,4},{1,9},{5,13},{9,1},{13,5},{2,10},{6,14},... | collective-permute-start | bytes 786440 | tf_op jit(solution)/shard_map/ppermute | solution.py:429
  13.2 20.7 %conditional.3 = (bf16[128,1024]{1,0:T(8,128)(2,1)}, bf16[128,1024]{1,0:T(8,128)(2,1)}, bf16[128,1024]{1,0:T(8,128)(2,1)}, bf16[128,1024]{1,0:T(8,128)(2,1)}, f3...) conditional(s32[]{:T(128)} %convert_element_type.15, () %tuple.40, (s32[4,512]{1,0:T(4,128)S(1)}, ...), branch_computations={%region_3.4_spmd, %region_4.5_spmd} | conditional | flops 25600 | bytes 1089600 | solution.py:486
  14.7 2.2 %collective-permute-done.8 = f32[4,512]{1,0:T(4,128)S(1)} collective-permute-done((f32[4,512]{1,0:T(4,128)S(1)}, f32[4,512]{1,0:T(4,128)S(1)}, u32[]{:S(2)}, u32[]{:S(2)}) %collective-permute-start.8) | collective-permute-done | bytes 8224 | tf_op jit(solution)/shard_map/cond/branch_1_fun/ppermute | solution.py:432
  19.4 7.6 %collective-permute-done.10 = f32[1,4,512]{2,1,0:T(4,128)S(1)} collective-permute-done((f32[1,4,512]{2,1,0:T(4,128)}, f32[1,4,512]{2,1,0:T(4,128)S(1)}, u32[]{:S(2)}, u32[]{:S(2)}) %collective-permute-start.10) | collective-permute-done | bytes 8224 | tf_op jit(solution)/shard_map/cond/branch_1_fun/ppermute | solution.py:448
  28.3 2.7 %branch_1_fun.5 = (bf16[128,1024]{1,0:T(8,128)(2,1)}, bf16[128,1024]{1,0:T(8,128)(2,1)}, bf16[128,1024]{1,0:T(8,128)(2,1)}, bf16[128,1024]{1,0:T(8,128)(2,1)}) custom-call(s32[4,512]{1,0:T(4,128)S(1)} %get-tuple-element.39.code_ref, bf16[512,1024]{1,0:T(8,128)(2,1)} %get-tuple-element.40.tokens_ref), custom_call_target="tpu_custom_call" | custom-call | flops 1024 | bytes 1024 | tf_op jit(solution)/shard_map/cond/branch_1_fun/pallas_call | solution.py:137
  31.0 2.2 %collective-permute-done.11 = f32[2,4,512]{2,1,0:T(4,128)S(1)} collective-permute-done((f32[2,4,512]{2,1,0:T(4,128)S(1)}, f32[2,4,512]{2,1,0:T(4,128)S(1)}, u32[]{:S(2)}, u32[]{:S(2)}) %collective-permute-start.11) | collective-permute-done | bytes 16416 | tf_op jit(solution)/shard_map/cond/branch_1_fun/ppermute | solution.py:448
  38.4 2.1 %collective-permute-start.16 = (bf16[128,1024]{1,0:T(8,128)(2,1)}, bf16[128,1024]{1,0:T(8,128)(2,1)}, u32[]{:S(2)}, u32[]{:S(2)}) collective-permute-start(bf16[128,1024]{1,0:T(8,128)(2,1)} %get-tuple-element.152), channel_id=1, source_target_pairs={{0,8},{4,12},{8,0},{12,4},{1,9},{5,13},{9,1},{13,5},{2,10},{6,14},... | collective-permute-start | bytes 786440 | tf_op jit(solution)/shard_map/ppermute | solution.py:429
  40.5 1.7 %collective-permute-start.17 = (bf16[128,1024]{1,0:T(8,128)(2,1)}, bf16[128,1024]{1,0:T(8,128)(2,1)}, u32[]{:S(2)}, u32[]{:S(2)}) collective-permute-start(bf16[128,1024]{1,0:T(8,128)(2,1)} %get-tuple-element.153), channel_id=1, source_target_pairs={{0,12},{4,0},{8,4},{12,8},{1,13},{5,1},{9,5},{13,9},{2,14},{6,2},{... | collective-permute-start | bytes 786440 | tf_op jit(solution)/shard_map/ppermute | solution.py:429
  43.9 1.8 %shard_map.66 = (f32[256,256]{1,0:T(8,128)S(1)}, f32[256,256]{1,0:T(8,128)S(1)}, bf16[2,1024,256]{2,1,0:T(8,128)(2,1)S(1)}, bf16[2,1024,256]{2,1,0:T(8,128)(2,1)S(1)}) custom-call(s32[4]{0:T(128)S(1)} %pad_add_fusion.order_ref, bf16[1,4096,256]{2,1,0:T(8,128)(2,1)S(1)} %copy-done, bf16[1,4096,256]{2,1,0:T(8,128)(2,1)S(1)} %copy-done.1, ...), custom_call_target="tpu_custom_call" | custom-call | flops 1024 | bytes 1024 | tf_op jit(solution)/shard_map/pallas_call | solution.py:222
  45.7 5.5 %collective-permute-done.18 = bf16[256,1024]{1,0:T(8,128)(2,1)} collective-permute-done((bf16[256,1024]{1,0:T(8,128)(2,1)S(1)}, bf16[256,1024]{1,0:T(8,128)(2,1)}, u32[]{:S(2)}, u32[]{:S(2)}) %collective-permute-start.18) | collective-permute-done | bytes 524320 | tf_op jit(solution)/shard_map/ppermute | solution.py:432
  51.3 11.7 %conditional.4 = (bf16[256,256]{1,0:T(8,128)(2,1)}, bf16[256,256]{1,0:T(8,128)(2,1)}, f32[256,1024]{1,0:T(8,128)S(1)}) conditional(s32[]{:T(128)} %convert_element_type.15, () %tuple.45, (bf16[256,1024]{1,0:T(8,128)(2,1)}, f32[256,256]{1,0:T(8,128)S(1)}, f32[256,256]{1,0:T(8,128)S(1)}, bf16[2,1024,256]{2,1,0:T(8,128)(2,1)S(1)}, ...), branch_computations={%region_6.7_spmd, %region_7.8_spmd} | conditional | flops 2048 | bytes 3672248 | solution.py:505
  51.3 2.1 %collective-permute-done.refs_1_ = bf16[256,1024]{1,0:T(8,128)(2,1)S(1)} collective-permute-done((bf16[256,1024]{1,0:T(8,128)(2,1)}, bf16[256,1024]{1,0:T(8,128)(2,1)S(1)}, u32[]{:S(2)}, u32[]{:S(2)}) %collective-permute-start) | collective-permute-done | bytes 524320 | tf_op jit(solution)/shard_map/cond/branch_1_fun/ppermute | solution.py:432
  53.4 1.8 %branch_1_fun.6.refs_0_ = bf16[256,256]{1,0:T(8,128)(2,1)S(1)} custom-call(f32[256,256]{1,0:T(8,128)S(1)} %get-tuple-element.46.gate_before, f32[256,256]{1,0:T(8,128)S(1)} %get-tuple-element.47.up_before, bf16[2,1024,256]{2,1,0:T(8,128)(2,1)S(1)} %get-tuple-element.48.gate_ref, bf16[2,1024,256]{2,1,0:T(8,128)(2,1)S(1)} %get-tuple-element.49.up_ref, ...), custom_call_target="tpu_custom_call" | custom-call | flops 1024 | bytes 1024 | tf_op jit(solution)/shard_map/cond/branch_1_fun/pallas_call | solution.py:250
  58.3 3.0 %collective-permute-done.1 = bf16[256,256]{1,0:T(8,128)(2,1)} collective-permute-done((bf16[256,256]{1,0:T(8,128)(2,1)S(1)}, bf16[256,256]{1,0:T(8,128)(2,1)}, u32[]{:S(2)}, u32[]{:S(2)}) %collective-permute-start.1) | collective-permute-done | bytes 131104 | tf_op jit(solution)/shard_map/cond/branch_1_fun/ppermute | solution.py:432
  61.2 1.7 %collective-permute-done.3 = bf16[256,256]{1,0:T(8,128)(2,1)} collective-permute-done((bf16[256,256]{1,0:T(8,128)(2,1)}, bf16[256,256]{1,0:T(8,128)(2,1)}, u32[]{:S(2)}, u32[]{:S(2)}) %collective-permute-start.3) | collective-permute-done | bytes 131104 | tf_op jit(solution)/shard_map/cond/branch_1_fun/ppermute | solution.py:432
  62.9 2.1 %shard_map.67.refs_0_ = bf16[256,1024]{1,0:T(8,128)(2,1)S(1)} custom-call(s32[2,4]{1,0:T(2,128)S(1)} %get-tuple-element.208.offset_ref, s32[2,4]{1,0:T(2,128)S(1)} %get-tuple-element.209.count_ref, bf16[128,1024]{1,0:T(8,128)(2,1)S(1)} %copy-done.8, bf16[128,1024]{1,0:T(8,128)(2,1)S(1)} %collective-permute-done.15.refs_1_, ...), custom_call_target="tpu_custom_call" | custom-call | flops 1024 | bytes 1024 | tf_op jit(solution)/shard_map/pallas_call | solution.py:174
  66.8 4.1 %shard_map.68 = (bf16[128,1024]{1,0:T(8,128)(2,1)S(1)}, bf16[128,1024]{1,0:T(8,128)(2,1)}, bf16[128,1024]{1,0:T(8,128)(2,1)}, bf16[128,1024]{1,0:T(8,128)(2,1)}) custom-call(s32[4]{0:T(128)S(1)} %pad_add_fusion.order_ref, s32[2,4]{1,0:T(2,128)S(1)} %get-tuple-element.208.offset_ref, s32[2,4]{1,0:T(2,128)S(1)} %get-tuple-element.209.count_ref, ...), custom_call_target="tpu_custom_call" | custom-call | flops 1024 | bytes 1024 | tf_op jit(solution)/shard_map/pallas_call | solution.py:319
  76.0 1.8 %shard_map.69 = (f32[256,256]{1,0:T(8,128)S(1)}, f32[256,256]{1,0:T(8,128)S(1)}, bf16[2,1024,256]{2,1,0:T(8,128)(2,1)S(1)}, bf16[2,1024,256]{2,1,0:T(8,128)(2,1)S(1)}) custom-call(s32[4]{0:T(128)S(1)} %pad_add_fusion.order_ref, bf16[1,4096,256]{2,1,0:T(8,128)(2,1)S(1)} %copy-done, bf16[1,4096,256]{2,1,0:T(8,128)(2,1)S(1)} %copy-done.2, ...), custom_call_target="tpu_custom_call" | custom-call | flops 1024 | bytes 1024 | tf_op jit(solution)/shard_map/pallas_call | solution.py:222
  77.9 1.7 %collective-permute-done.20 = bf16[256,1024]{1,0:T(8,128)(2,1)} collective-permute-done((bf16[256,1024]{1,0:T(8,128)(2,1)S(1)}, bf16[256,1024]{1,0:T(8,128)(2,1)}, u32[]{:S(2)}, u32[]{:S(2)}) %collective-permute-start.20) | collective-permute-done | bytes 524320 | tf_op jit(solution)/shard_map/ppermute | solution.py:432
  79.6 11.7 %conditional.5 = (bf16[256,256]{1,0:T(8,128)(2,1)}, bf16[256,256]{1,0:T(8,128)(2,1)}, f32[256,1024]{1,0:T(8,128)S(1)}) conditional(s32[]{:T(128)} %convert_element_type.16, () %tuple.42, (bf16[256,1024]{1,0:T(8,128)(2,1)}, f32[256,256]{1,0:T(8,128)S(1)}, f32[256,256]{1,0:T(8,128)S(1)}, bf16[2,1024,256]{2,1,0:T(8,128)(2,1)S(1)}, ...), branch_computations={%region_8.9_spmd, %region_9.10_spmd} | conditional | flops 2048 | bytes 3672248 | solution.py:505
  79.6 2.1 %collective-permute-done.4.refs_1_ = bf16[256,1024]{1,0:T(8,128)(2,1)S(1)} collective-permute-done((bf16[256,1024]{1,0:T(8,128)(2,1)}, bf16[256,1024]{1,0:T(8,128)(2,1)S(1)}, u32[]{:S(2)}, u32[]{:S(2)}) %collective-permute-start.4) | collective-permute-done | bytes 524320 | tf_op jit(solution)/shard_map/cond/branch_1_fun/ppermute | solution.py:432
  81.7 1.8 %branch_1_fun.8.refs_0_ = bf16[256,256]{1,0:T(8,128)(2,1)S(1)} custom-call(f32[256,256]{1,0:T(8,128)S(1)} %get-tuple-element.55.gate_before, f32[256,256]{1,0:T(8,128)S(1)} %get-tuple-element.56.up_before, bf16[2,1024,256]{2,1,0:T(8,128)(2,1)S(1)} %get-tuple-element.57.gate_ref, bf16[2,1024,256]{2,1,0:T(8,128)(2,1)S(1)} %get-tuple-element.58.up_ref, ...), custom_call_target="tpu_custom_call" | custom-call | flops 1024 | bytes 1024 | tf_op jit(solution)/shard_map/cond/branch_1_fun/pallas_call | solution.py:250
  86.6 3.0 %collective-permute-done.5 = bf16[256,256]{1,0:T(8,128)(2,1)} collective-permute-done((bf16[256,256]{1,0:T(8,128)(2,1)S(1)}, bf16[256,256]{1,0:T(8,128)(2,1)}, u32[]{:S(2)}, u32[]{:S(2)}) %collective-permute-start.5) | collective-permute-done | bytes 131104 | tf_op jit(solution)/shard_map/cond/branch_1_fun/ppermute | solution.py:432
  91.2 4.0 %shard_map.70 = (bf16[128,1024]{1,0:T(8,128)(2,1)S(1)}, bf16[128,1024]{1,0:T(8,128)(2,1)S(1)}, bf16[128,1024]{1,0:T(8,128)(2,1)S(1)}, bf16[128,1024]{1,0:T(8,128)(2,1)S(1)}) custom-call(s32[4]{0:T(128)S(1)} %pad_add_fusion.order_ref, s32[2,4]{1,0:T(2,128)S(1)} %get-tuple-element.208.offset_ref, s32[2,4]{1,0:T(2,128)S(1)} %get-tuple-element.209.count_ref, ...), custom_call_target="tpu_custom_call" | custom-call | flops 1024 | bytes 1024 | tf_op jit(solution)/shard_map/pallas_call | solution.py:319
  95.3 2.1 %collective-permute-done.23.refs_2_ = bf16[128,1024]{1,0:T(8,128)(2,1)} collective-permute-done((bf16[128,1024]{1,0:T(8,128)(2,1)}, bf16[128,1024]{1,0:T(8,128)(2,1)}, u32[]{:S(2)}, u32[]{:S(2)}) %collective-permute-start.23) | collective-permute-done | bytes 262176 | tf_op jit(solution)/shard_map/ppermute | solution.py:429
  97.6 1.7 %collective-permute-start.26 = (bf16[128,1024]{1,0:T(8,128)(2,1)S(1)}, bf16[128,1024]{1,0:T(8,128)(2,1)S(1)}, u32[]{:S(2)}, u32[]{:S(2)}) collective-permute-start(bf16[128,1024]{1,0:T(8,128)(2,1)S(1)} %get-tuple-element.197), channel_id=1, source_target_pairs={{0,8},{4,12},{8,0},{12,4},{1,9},{5,13},{9,1},{13,5},{2,10},{6,14},... | collective-permute-start | bytes 786440 | tf_op jit(solution)/shard_map/ppermute | solution.py:429
  101.2 1.9 %shard_map.72.refs_4_ = f32[512,1024]{1,0:T(8,128)S(1)} custom-call(s32[4,512]{1,0:T(4,128)S(1)} %get-tuple-element.134.code_ref, f32[4,512]{1,0:T(4,128)S(1)} %shard_map.71.weight_ref, bf16[128,1024]{1,0:T(8,128)(2,1)S(1)} %get-tuple-element.200.refs_0_, bf16[128,1024]{1,0:T(8,128)(2,1)} %collective-permute-done.22.refs_1_, ...), custom_call_target="tpu_custom_call" | custom-call | flops 1024 | bytes 1024 | tf_op jit(solution)/shard_map/pallas_call | solution.py:398
  103.1 1.8 %collective-permute-done.25.refs_1_ = bf16[128,1024]{1,0:T(8,128)(2,1)S(1)} collective-permute-done((bf16[128,1024]{1,0:T(8,128)(2,1)S(1)}, bf16[128,1024]{1,0:T(8,128)(2,1)S(1)}, u32[]{:S(2)}, u32[]{:S(2)}) %collective-permute-start.25) | collective-permute-done | bytes 262176 | tf_op jit(solution)/shard_map/ppermute | solution.py:429
  104.9 17.6 %collective-permute-done.26.refs_2_ = bf16[128,1024]{1,0:T(8,128)(2,1)S(1)} collective-permute-done((bf16[128,1024]{1,0:T(8,128)(2,1)S(1)}, bf16[128,1024]{1,0:T(8,128)(2,1)S(1)}, u32[]{:S(2)}, u32[]{:S(2)}) %collective-permute-start.26) | collective-permute-done | bytes 262176 | tf_op jit(solution)/shard_map/ppermute | solution.py:429
  122.5 2.1 %shard_map.73 = bf16[512,1024]{1,0:T(8,128)(2,1)} custom-call(s32[4,512]{1,0:T(4,128)S(1)} %get-tuple-element.134.code_ref, f32[4,512]{1,0:T(4,128)S(1)} %shard_map.71.weight_ref, bf16[128,1024]{1,0:T(8,128)(2,1)S(1)} %get-tuple-element.195.refs_0_, bf16[128,1024]{1,0:T(8,128)(2,1)S(1)} %collective-permute-done.25.refs_1_, ...), custom_call_target="tpu_custom_call" | custom-call | flops 1024 | bytes 1024 | tf_op jit(solution)/shard_map/pallas_call | solution.py:398
  (72 shorter events, 31.5 us)
Async XLA Ops:
  3.9 30.7 %copy-start.3 = (bf16[128,1024]{1,0:T(8,128)(2,1)S(1)}, bf16[128,1024]{1,0:T(8,128)(2,1)}, u32[]{:S(2)}) copy-start(bf16[128,1024]{1,0:T(8,128)(2,1)} %get-tuple-element.146.refs_0_) | copy-start | bytes 786436
  3.9 38.4 %copy-start = (bf16[1,4096,256]{2,1,0:T(8,128)(2,1)S(1)}, bf16[1,4096,256]{2,1,0:T(8,128)(2,1)}, u32[]{:S(2)}) copy-start(bf16[1,4096,256]{2,1,0:T(8,128)(2,1)} %gate_ref.3) | copy-start | bytes 6291460
  3.9 30.0 %collective-permute-start.12 = (bf16[128,1024]{1,0:T(8,128)(2,1)}, bf16[128,1024]{1,0:T(8,128)(2,1)S(1)}, u32[]{:S(2)}, u32[]{:S(2)}) collective-permute-start(bf16[128,1024]{1,0:T(8,128)(2,1)} %get-tuple-element.143), channel_id=1, source_target_pairs={{0,4},{4,8},{8,12},{12,0},{1,5},{5,9},{9,13},{13,1},{2,6},{6,10},{... | collective-permute-start | bytes 786440 | tf_op jit(solution)/shard_map/ppermute | solution.py:429
  7.0 26.9 %collective-permute-start.13 = (bf16[128,1024]{1,0:T(8,128)(2,1)}, bf16[128,1024]{1,0:T(8,128)(2,1)S(1)}, u32[]{:S(2)}, u32[]{:S(2)}) collective-permute-start(bf16[128,1024]{1,0:T(8,128)(2,1)} %get-tuple-element.144), channel_id=1, source_target_pairs={{0,8},{4,12},{8,0},{12,4},{1,9},{5,13},{9,1},{13,5},{2,10},{6,14},... | collective-permute-start | bytes 786440 | tf_op jit(solution)/shard_map/ppermute | solution.py:429
  9.6 24.3 %collective-permute-start.14 = (bf16[128,1024]{1,0:T(8,128)(2,1)}, bf16[128,1024]{1,0:T(8,128)(2,1)S(1)}, u32[]{:S(2)}, u32[]{:S(2)}) collective-permute-start(bf16[128,1024]{1,0:T(8,128)(2,1)} %get-tuple-element.145), channel_id=1, source_target_pairs={{0,12},{4,0},{8,4},{12,8},{1,13},{5,1},{9,5},{13,9},{2,14},{6,2},{... | collective-permute-start | bytes 786440 | tf_op jit(solution)/shard_map/ppermute | solution.py:429
  13.2 3.7 %collective-permute-start.8 = (f32[4,512]{1,0:T(4,128)S(1)}, f32[4,512]{1,0:T(4,128)S(1)}, u32[]{:S(2)}, u32[]{:S(2)}) collective-permute-start(f32[4,512]{1,0:T(4,128)S(1)} %get-tuple-element.45), channel_id=1, source_target_pairs={{0,2},{1,3},{2,0},{3,1},{4,6},{5,7},{6,4},{7,5},{8,10},{9,11},{10,... | collective-permute-start | bytes 24584 | tf_op jit(solution)/shard_map/cond/branch_1_fun/ppermute | solution.py:432
  16.9 1.2 collective-permute-start.9
  18.7 8.2 %collective-permute-start.10 = (f32[1,4,512]{2,1,0:T(4,128)}, f32[1,4,512]{2,1,0:T(4,128)S(1)}, u32[]{:S(2)}, u32[]{:S(2)}) collective-permute-start(f32[1,4,512]{2,1,0:T(4,128)} %bitcast), channel_id=1, source_target_pairs={{0,4},{4,0},{8,12},{12,8},{1,5},{5,1},{9,13},{13,9},{2,6},{6,2},{1... | collective-permute-start | bytes 24584 | tf_op jit(solution)/shard_map/cond/branch_1_fun/ppermute | solution.py:448
  27.6 5.5 %collective-permute-start.11 = (f32[2,4,512]{2,1,0:T(4,128)S(1)}, f32[2,4,512]{2,1,0:T(4,128)S(1)}, u32[]{:S(2)}, u32[]{:S(2)}) collective-permute-start(f32[2,4,512]{2,1,0:T(4,128)S(1)} %pad_maximum_fusion.1), channel_id=1, source_target_pairs={{0,8},{4,12},{8,0},{12,4},{1,9},{5,13},{9,1},{13,5},{2,10},{6,14},... | collective-permute-start | bytes 49160 | tf_op jit(solution)/shard_map/cond/branch_1_fun/ppermute | solution.py:448
  36.7 5.5 %collective-permute-start.19 = (bf16[256,1024]{1,0:T(8,128)(2,1)S(1)}, bf16[256,1024]{1,0:T(8,128)(2,1)S(1)}, u32[]{:S(2)}, u32[]{:S(2)}) collective-permute-start(bf16[256,1024]{1,0:T(8,128)(2,1)S(1)} %shard_map.65.refs_0_), channel_id=1, source_target_pairs={{0,1},{1,0},{2,3},{3,2},{4,5},{5,4},{6,7},{7,6},{8,9},{9,8},{10,11... | collective-permute-start | bytes 1572872 | tf_op jit(solution)/shard_map/ppermute | solution.py:432
  36.8 14.4 %collective-permute-start.18 = (bf16[256,1024]{1,0:T(8,128)(2,1)S(1)}, bf16[256,1024]{1,0:T(8,128)(2,1)}, u32[]{:S(2)}, u32[]{:S(2)}) collective-permute-start(bf16[256,1024]{1,0:T(8,128)(2,1)S(1)} %shard_map.65.refs_0_), channel_id=1, source_target_pairs={{0,2},{1,3},{2,0},{3,1},{4,6},{5,7},{6,4},{7,5},{8,10},{9,11},{10,... | collective-permute-start | bytes 1572872 | tf_op jit(solution)/shard_map/ppermute | solution.py:432
  38.4 24.6 %collective-permute-start.15 = (bf16[128,1024]{1,0:T(8,128)(2,1)}, bf16[128,1024]{1,0:T(8,128)(2,1)S(1)}, u32[]{:S(2)}, u32[]{:S(2)}) collective-permute-start(bf16[128,1024]{1,0:T(8,128)(2,1)} %get-tuple-element.151), channel_id=1, source_target_pairs={{0,4},{4,8},{8,12},{12,0},{1,5},{5,9},{9,13},{13,1},{2,6},{6,10},{... | collective-permute-start | bytes 786440 | tf_op jit(solution)/shard_map/ppermute | solution.py:429
  38.4 24.6 %collective-permute-start.16 = (bf16[128,1024]{1,0:T(8,128)(2,1)}, bf16[128,1024]{1,0:T(8,128)(2,1)}, u32[]{:S(2)}, u32[]{:S(2)}) collective-permute-start(bf16[128,1024]{1,0:T(8,128)(2,1)} %get-tuple-element.152), channel_id=1, source_target_pairs={{0,8},{4,12},{8,0},{12,4},{1,9},{5,13},{9,1},{13,5},{2,10},{6,14},... | collective-permute-start | bytes 786440 | tf_op jit(solution)/shard_map/ppermute | solution.py:429
  40.5 22.5 %collective-permute-start.17 = (bf16[128,1024]{1,0:T(8,128)(2,1)}, bf16[128,1024]{1,0:T(8,128)(2,1)}, u32[]{:S(2)}, u32[]{:S(2)}) collective-permute-start(bf16[128,1024]{1,0:T(8,128)(2,1)} %get-tuple-element.153), channel_id=1, source_target_pairs={{0,12},{4,0},{8,4},{12,8},{1,13},{5,1},{9,5},{13,9},{2,14},{6,2},{... | collective-permute-start | bytes 786440 | tf_op jit(solution)/shard_map/ppermute | solution.py:429
  43.9 7.4 %copy-start.6 = (bf16[1,1024,1024]{2,1,0:T(8,128)(2,1)S(1)}, bf16[1,1024,1024]{2,1,0:T(8,128)(2,1)}, u32[]{:S(2)}) copy-start(bf16[1,1024,1024]{2,1,0:T(8,128)(2,1)} %down_ref.3) | copy-start | bytes 6291460
  51.3 11.7 %copy-start.8 = (bf16[128,1024]{1,0:T(8,128)(2,1)S(1)}, bf16[128,1024]{1,0:T(8,128)(2,1)}, u32[]{:S(2)}) copy-start(bf16[128,1024]{1,0:T(8,128)(2,1)} %get-tuple-element.164.refs_0_) | copy-start | bytes 786436
  51.3 2.1 %collective-permute-start = (bf16[256,1024]{1,0:T(8,128)(2,1)}, bf16[256,1024]{1,0:T(8,128)(2,1)S(1)}, u32[]{:S(2)}, u32[]{:S(2)}) collective-permute-start(bf16[256,1024]{1,0:T(8,128)(2,1)} %get-tuple-element.50.refs_0_), channel_id=1, source_target_pairs={{0,1},{1,0},{2,3},{3,2},{4,5},{5,4},{6,7},{7,6},{8,9},{9,8},{10,11... | collective-permute-start | bytes 1572872 | tf_op jit(solution)/shard_map/cond/branch_1_fun/ppermute | solution.py:432
  55.1 1.7 %collective-permute-start.2 = (bf16[256,256]{1,0:T(8,128)(2,1)S(1)}, bf16[256,256]{1,0:T(8,128)(2,1)S(1)}, u32[]{:S(2)}, u32[]{:S(2)}) collective-permute-start(bf16[256,256]{1,0:T(8,128)(2,1)S(1)} %branch_1_fun.6.refs_0_), channel_id=1, source_target_pairs={{0,1},{1,0},{2,3},{3,2},{4,5},{5,4},{6,7},{7,6},{8,9},{9,8},{10,11... | collective-permute-start | bytes 393224 | tf_op jit(solution)/shard_map/cond/branch_1_fun/ppermute | solution.py:432
  55.4 5.9 %collective-permute-start.1 = (bf16[256,256]{1,0:T(8,128)(2,1)S(1)}, bf16[256,256]{1,0:T(8,128)(2,1)}, u32[]{:S(2)}, u32[]{:S(2)}) collective-permute-start(bf16[256,256]{1,0:T(8,128)(2,1)S(1)} %branch_1_fun.6.refs_0_), channel_id=1, source_target_pairs={{0,2},{1,3},{2,0},{3,1},{4,6},{5,7},{6,4},{7,5},{8,10},{9,11},{10,... | collective-permute-start | bytes 393224 | tf_op jit(solution)/shard_map/cond/branch_1_fun/ppermute | solution.py:432
  61.2 1.7 %collective-permute-start.3 = (bf16[256,256]{1,0:T(8,128)(2,1)}, bf16[256,256]{1,0:T(8,128)(2,1)}, u32[]{:S(2)}, u32[]{:S(2)}) collective-permute-start(bf16[256,256]{1,0:T(8,128)(2,1)} %collective-permute-done.1), channel_id=1, source_target_pairs={{0,1},{1,0},{2,3},{3,2},{4,5},{5,4},{6,7},{7,6},{8,9},{9,8},{10,11... | collective-permute-start | bytes 393224 | tf_op jit(solution)/shard_map/cond/branch_1_fun/ppermute | solution.py:432
  65.1 9.4 %collective-permute-start.21 = (bf16[256,1024]{1,0:T(8,128)(2,1)S(1)}, bf16[256,1024]{1,0:T(8,128)(2,1)S(1)}, u32[]{:S(2)}, u32[]{:S(2)}) collective-permute-start(bf16[256,1024]{1,0:T(8,128)(2,1)S(1)} %shard_map.67.refs_0_), channel_id=1, source_target_pairs={{0,1},{1,0},{2,3},{3,2},{4,5},{5,4},{6,7},{7,6},{8,9},{9,8},{10,11... | collective-permute-start | bytes 1572872 | tf_op jit(solution)/shard_map/ppermute | solution.py:432
  65.3 14.3 %collective-permute-start.20 = (bf16[256,1024]{1,0:T(8,128)(2,1)S(1)}, bf16[256,1024]{1,0:T(8,128)(2,1)}, u32[]{:S(2)}, u32[]{:S(2)}) collective-permute-start(bf16[256,1024]{1,0:T(8,128)(2,1)S(1)} %shard_map.67.refs_0_), channel_id=1, source_target_pairs={{0,2},{1,3},{2,0},{3,1},{4,6},{5,7},{6,4},{7,5},{8,10},{9,11},{10,... | collective-permute-start | bytes 1572872 | tf_op jit(solution)/shard_map/ppermute | solution.py:432
  70.9 24.4 %collective-permute-start.22 = (bf16[128,1024]{1,0:T(8,128)(2,1)}, bf16[128,1024]{1,0:T(8,128)(2,1)}, u32[]{:S(2)}, u32[]{:S(2)}) collective-permute-start(bf16[128,1024]{1,0:T(8,128)(2,1)} %get-tuple-element.174), channel_id=1, source_target_pairs={{0,12},{4,0},{8,4},{12,8},{1,13},{5,1},{9,5},{13,9},{2,14},{6,2},{... | collective-permute-start | bytes 786440 | tf_op jit(solution)/shard_map/ppermute | solution.py:429
  72.5 24.9 %collective-permute-start.23 = (bf16[128,1024]{1,0:T(8,128)(2,1)}, bf16[128,1024]{1,0:T(8,128)(2,1)}, u32[]{:S(2)}, u32[]{:S(2)}) collective-permute-start(bf16[128,1024]{1,0:T(8,128)(2,1)} %get-tuple-element.175), channel_id=1, source_target_pairs={{0,8},{4,12},{8,0},{12,4},{1,9},{5,13},{9,1},{13,5},{2,10},{6,14},... | collective-permute-start | bytes 786440 | tf_op jit(solution)/shard_map/ppermute | solution.py:429
  73.9 23.5 %collective-permute-start.24 = (bf16[128,1024]{1,0:T(8,128)(2,1)}, bf16[128,1024]{1,0:T(8,128)(2,1)}, u32[]{:S(2)}, u32[]{:S(2)}) collective-permute-start(bf16[128,1024]{1,0:T(8,128)(2,1)} %get-tuple-element.176), channel_id=1, source_target_pairs={{0,4},{4,8},{8,12},{12,0},{1,5},{5,9},{9,13},{13,1},{2,6},{6,10},{... | collective-permute-start | bytes 786440 | tf_op jit(solution)/shard_map/ppermute | solution.py:429
  79.6 2.1 %collective-permute-start.4 = (bf16[256,1024]{1,0:T(8,128)(2,1)}, bf16[256,1024]{1,0:T(8,128)(2,1)S(1)}, u32[]{:S(2)}, u32[]{:S(2)}) collective-permute-start(bf16[256,1024]{1,0:T(8,128)(2,1)} %get-tuple-element.59.refs_0_), channel_id=1, source_target_pairs={{0,1},{1,0},{2,3},{3,2},{4,5},{5,4},{6,7},{7,6},{8,9},{9,8},{10,11... | collective-permute-start | bytes 1572872 | tf_op jit(solution)/shard_map/cond/branch_1_fun/ppermute | solution.py:432
  83.5 1.7 %collective-permute-start.6 = (bf16[256,256]{1,0:T(8,128)(2,1)S(1)}, bf16[256,256]{1,0:T(8,128)(2,1)S(1)}, u32[]{:S(2)}, u32[]{:S(2)}) collective-permute-start(bf16[256,256]{1,0:T(8,128)(2,1)S(1)} %branch_1_fun.8.refs_0_), channel_id=1, source_target_pairs={{0,1},{1,0},{2,3},{3,2},{4,5},{5,4},{6,7},{7,6},{8,9},{9,8},{10,11... | collective-permute-start | bytes 393224 | tf_op jit(solution)/shard_map/cond/branch_1_fun/ppermute | solution.py:432
  83.7 5.9 %collective-permute-start.5 = (bf16[256,256]{1,0:T(8,128)(2,1)S(1)}, bf16[256,256]{1,0:T(8,128)(2,1)}, u32[]{:S(2)}, u32[]{:S(2)}) collective-permute-start(bf16[256,256]{1,0:T(8,128)(2,1)S(1)} %branch_1_fun.8.refs_0_), channel_id=1, source_target_pairs={{0,2},{1,3},{2,0},{3,1},{4,6},{5,7},{6,4},{7,5},{8,10},{9,11},{10,... | collective-permute-start | bytes 393224 | tf_op jit(solution)/shard_map/cond/branch_1_fun/ppermute | solution.py:432
  89.5 1.7 %collective-permute-start.7 = (bf16[256,256]{1,0:T(8,128)(2,1)}, bf16[256,256]{1,0:T(8,128)(2,1)}, u32[]{:S(2)}, u32[]{:S(2)}) collective-permute-start(bf16[256,256]{1,0:T(8,128)(2,1)} %collective-permute-done.5), channel_id=1, source_target_pairs={{0,1},{1,0},{2,3},{3,2},{4,5},{5,4},{6,7},{7,6},{8,9},{9,8},{10,11... | collective-permute-start | bytes 393224 | tf_op jit(solution)/shard_map/cond/branch_1_fun/ppermute | solution.py:432
  97.4 7.5 %collective-permute-start.25 = (bf16[128,1024]{1,0:T(8,128)(2,1)S(1)}, bf16[128,1024]{1,0:T(8,128)(2,1)S(1)}, u32[]{:S(2)}, u32[]{:S(2)}) collective-permute-start(bf16[128,1024]{1,0:T(8,128)(2,1)S(1)} %get-tuple-element.196), channel_id=1, source_target_pairs={{0,12},{4,0},{8,4},{12,8},{1,13},{5,1},{9,5},{13,9},{2,14},{6,2},{... | collective-permute-start | bytes 786440 | tf_op jit(solution)/shard_map/ppermute | solution.py:429
  97.6 24.9 %collective-permute-start.26 = (bf16[128,1024]{1,0:T(8,128)(2,1)S(1)}, bf16[128,1024]{1,0:T(8,128)(2,1)S(1)}, u32[]{:S(2)}, u32[]{:S(2)}) collective-permute-start(bf16[128,1024]{1,0:T(8,128)(2,1)S(1)} %get-tuple-element.197), channel_id=1, source_target_pairs={{0,8},{4,12},{8,0},{12,4},{1,9},{5,13},{9,1},{13,5},{2,10},{6,14},... | collective-permute-start | bytes 786440 | tf_op jit(solution)/shard_map/ppermute | solution.py:429
  99.3 23.2 %collective-permute-start.27 = (bf16[128,1024]{1,0:T(8,128)(2,1)S(1)}, bf16[128,1024]{1,0:T(8,128)(2,1)S(1)}, u32[]{:S(2)}, u32[]{:S(2)}) collective-permute-start(bf16[128,1024]{1,0:T(8,128)(2,1)S(1)} %get-tuple-element.198), channel_id=1, source_target_pairs={{0,4},{4,8},{8,12},{12,0},{1,5},{5,9},{9,13},{13,1},{2,6},{6,10},{... | collective-permute-start | bytes 786440 | tf_op jit(solution)/shard_map/ppermute | solution.py:429
  (5 other events, 8.4 us)

commit v8 on v7

--- a/solution.py
+++ b/solution.py
@@ -257,75 +257,86 @@
     )(*before, *xs)
 
 
-def down_sum(places, order_ref, down_ref, hs, h_held, sems, total):
+def down_first_kernel(parts, near, far, order_ref, down_ref, *refs):
+    hs, (out_ref, far_ref, down_held, h_held, sems) = refs[:parts], refs[parts:]
     units = hs[0].shape[1]
-    loads = start_all(hs, [h_held.at[i] for i in range(len(hs))], sems)
-    for i in range(len(hs)):
-        first = pl.multiple_of(order_ref[places[i]] * units, units)
+
+    def fetch(i, place, target, sem):
+        first = pl.multiple_of(order_ref[place] * units, units)
+        copy = pltpu.make_async_copy(down_ref.at[0, pl.ds(first, units), :], target.at[i], sems.at[sem])
+        copy.start()
+        return copy
+
+    h_loads = start_all(hs, [h_held.at[i] for i in range(parts)], sems.at[pl.ds(0, parts)])
+    loads = [fetch(i, near[i], down_held, parts + i) for i in range(parts)]
+    late = [fetch(i, far[i], far_ref, 2 * parts + i) for i in range(len(far))]
+    total = None
+    for i in range(parts):
+        h_loads[i].wait()
         loads[i].wait()
-        term = dot(h_held[i], down_ref[0, pl.ds(first, units), :])
+        term = dot(h_held[i], down_held[i])
         total = term if total is None else total + term
-    return total
-
-
-def down_first_kernel(parts, places, order_ref, down_ref, *refs):
-    hs, out_ref = refs[:parts], refs[parts]
-    out_ref[...] = down_sum(places, order_ref, down_ref, hs, *refs[parts + 1 :], None)
-
-
-def down_last_kernel(parts, places, experts, k, order_ref, offset_ref, count_ref, down_ref, *refs):
-    hs, before, outs = refs[:parts], refs[parts], refs[parts + 1 : parts + 1 + experts]
-    h_held, in_sems, staged, out_sems = refs[parts + 1 + experts :]
-    size = hs[0].shape[0]
-    depth = outs[0].shape[0]
-    total = down_sum(places, order_ref, down_ref, hs, h_held, in_sems, before[...])
-    result = total.astype(BF16)
-    row = lax.broadcasted_iota(I32, (depth, size), 0)
-    lane = lax.broadcasted_iota(I32, (depth, size), 1)
-    copies = []
-    for i in list(range(1, experts)) + [0]:
-        pick = ((lane - offset_ref[k, i] == row) & (row < count_ref[k, i])).astype(F32).astype(BF16)
-        staged[i] = dot(pick, result).astype(BF16)
-        copy = pltpu.make_async_copy(staged.at[i], outs[i], out_sems.at[i])
-        copy.start()
-        copies.append(copy)
-    for copy in copies:
+    out_ref[...] = total
+    for copy in late:
         copy.wait()
 
 
-def down_scratch(parts, size, units):
-    return [pltpu.VMEM((parts, size, units), BF16), pltpu.SemaphoreType.DMA((parts,))]
-
-
-def down_first(order, places, down_weight, hs):
+def down_first(order, near, far, down_weight, hs):
     parts = len(hs)
     size, units = hs[0].shape
     width = down_weight.shape[2]
     return pl.pallas_call(
-        functools.partial(down_first_kernel, parts, places),
-        out_shape=jax.ShapeDtypeStruct((size, width), F32),
-        in_specs=[smem()] + whole(1) + apart(parts),
-        out_specs=whole(1)[0],
-        scratch_shapes=down_scratch(parts, size, units),
+        functools.partial(down_first_kernel, parts, near, far),
+        out_shape=[
+            jax.ShapeDtypeStruct((size, width), F32),
+            jax.ShapeDtypeStruct((len(far), units, width), BF16),
+        ],
+        in_specs=[smem()] + apart(1 + parts),
+        out_specs=whole(2),
+        scratch_shapes=[
+            pltpu.VMEM((parts, units, width), BF16),
+            pltpu.VMEM((parts, size, units), BF16),
+            pltpu.SemaphoreType.DMA((2 * parts + len(far),)),
+        ],
         compiler_params=params(),
         cost_estimate=COST,
     )(order, down_weight, *hs)
 
 
-def down_last(order, places, offsets, counts, k, down_weight, hs, before, experts, depth):
+def down_last_kernel(parts, experts, k, offset_ref, count_ref, before_ref, down_ref, *refs):
+    hs, outs = refs[:parts], refs[parts : parts + experts]
+    h_held, sems = refs[parts + experts :]
+    loads = start_all(hs, [h_held.at[i] for i in range(parts)], sems)
+    size = hs[0].shape[0]
+    depth = outs[0].shape[0]
+    row = lax.broadcasted_iota(I32, (depth, size), 0)
+    lane = lax.broadcasted_iota(I32, (depth, size), 1)
+    picks = [
+        ((lane - offset_ref[k, i] == row) & (row < count_ref[k, i])).astype(F32).astype(BF16)
+        for i in range(experts)
+    ]
+    total = before_ref[...]
+    for i in range(parts):
+        loads[i].wait()
+        total = total + dot(h_held[i], down_ref[i])
+    result = total.astype(BF16)
+    for i in range(experts):
+        outs[i][...] = dot(picks[i], result).astype(BF16)
+
+
+def down_last(offsets, counts, k, hs, before, experts, depth):
     parts = len(hs)
     size, units = hs[0].shape
-    width = down_weight.shape[2]
-    return pl.pallas_call(
-        functools.partial(down_last_kernel, parts, places, experts, k),
+    width = before[0].shape[1]
+    return pl.pallas_call(
+        functools.partial(down_last_kernel, parts, experts, k),
         out_shape=[jax.ShapeDtypeStruct((depth, width), BF16)] * experts,
-        in_specs=[smem()] * 3 + whole(1) + apart(parts) + whole(1),
-        out_specs=apart(experts),
-        scratch_shapes=down_scratch(parts, size, units)
-        + [pltpu.VMEM((experts, depth, width), BF16), pltpu.SemaphoreType.DMA((experts,))],
-        compiler_params=params(),
-        cost_estimate=COST,
-    )(order, offsets, counts, down_weight, *hs, before)
+        in_specs=[smem()] * 2 + whole(2) + apart(parts),
+        out_specs=whole(experts),
+        scratch_shapes=[pltpu.VMEM((parts, size, units), BF16), pltpu.SemaphoreType.DMA((parts,))],
+        compiler_params=params(),
+        cost_estimate=COST,
+    )(offsets, counts, *before, *hs)
 
 
 def weight_kernel(experts, place_ref, own_ref, logits_ref, code_ref, out_ref, score_ref):
@@ -475,7 +486,7 @@
         for bit in bits:
             logits = logits + swap(logits, bit)
         gathered = logits[None]
-        for bit in expert_bits:
+        for bit in expert_bits[:-1]:
             gathered = jnp.concatenate([gathered, swap_expert(gathered, bit)])
         return later, logits, gathered
 
@@ -489,13 +500,13 @@
         far = spread(far)
         hidden = gate_up_far(far, sums)
         far = swap(hidden, bits[0])
-        partial = down_first(order, near_places, down_weight, spread(hidden))
+        partial = down_first(order, near_places, far_places, down_weight, spread(hidden))
         far, partial = lax.optimization_barrier((far, partial))
         return spread(far), partial
 
     def settle(k, far, partial):
         return tuple(
-            down_last(order, far_places, offsets, counts, k, down_weight, far, partial, experts, depth)
+            down_last(offsets, counts, k, far, partial, experts, depth)
         )
 
     def fenced(k, run, *operands):
@@ -532,7 +543,9 @@
     results = settle(BATCHES - 1, far, partial)
     results, waiting[-1] = lax.optimization_barrier((results, waiting[-1]))
     waiting.append(send_back(results))
-    weights = slot_weights(place, logits, after(gathered, results), code)
+    gathered = after(gathered, results)
+    gathered = jnp.concatenate([gathered, swap_expert(gathered, expert_bits[-1])])
+    weights = slot_weights(place, logits, gathered, code)
     total = None
     for k in range(BATCHES):
         total = combine(code, weights, k, waiting[k], total)

time: 125 us -> 124 us (level)
  starting transfers between devices: 26.3 us -> 35.4 us
  waiting for transfers between devices: 55.4 us -> 48.7 us
  Pallas kernels: 32.9 us -> 30.6 us
    ppermute x12, waiting for transfers between devices: 21.5 us -> 5.21 us  [along_expert(): lax.ppermute(x, 'expert', [(i, (i + shift) % experts) for i in range(expe...]
    ppermute x2, waiting for transfers between devices: 9.76 us -> 25 us  [swap_expert(): return lax.ppermute(x, 'expert', [(i, i ^ bit) for i in range(experts)])]
    ppermute x12, starting transfers between devices: 16.6 us -> 25.5 us  [along_expert(): lax.ppermute(x, 'expert', [(i, (i + shift) % experts) for i in range(expe...]
    ppermute x14, waiting for transfers between devices: 24.1 us -> 18.5 us  [swap(): return lax.ppermute(x, 'dp', [(i, i ^ bit) for i in range(width_parts)])]
    pallas_call x4, Pallas kernels: 10.9 us -> 8.64 us  [the longest x2 5.48 us: down_last(): pl.pallas_call(functools.partial(down_last_kernel, parts, experts, k), ou...]
    unnamed x18 -> x14, local copies, waits for them, and re-layouts: 4.85 us -> 4.14 us
  transfers between devices with their start and end apart: 28 -> 28, of which waited for: 15 -> 14; matrix products, arithmetic and copies ran while one was open for 3% -> 2% of each run, Pallas kernels for 19% -> 17%
where the time goes in v8:
time: 124 us; the launch traced here: 123 us
  waiting for transfers between devices  48.7 us (39%)
  starting transfers between devices  35.4 us (29%)
  Pallas kernels  30.6 us (25%)
  local copies, waits for them, and re-layouts  4.84 us (4%)
  other arithmetic  2.28 us (2%)
  between operations  1.43 us (1%)
    ppermute x12, starting transfers between devices, along_expert(): lax.ppermute(x, 'expert', [(i, (i + shift) % experts) for i in range(expe...  25.5 us
    ppermute x2, waiting for transfers between devices, swap_expert(): return lax.ppermute(x, 'expert', [(i, i ^ bit) for i in range(experts)])  25 us
    ppermute x14, waiting for transfers between devices, swap(): return lax.ppermute(x, 'dp', [(i, i ^ bit) for i in range(width_parts)])  18.5 us
    ppermute x14, starting transfers between devices, swap(): return lax.ppermute(x, 'dp', [(i, i ^ bit) for i in range(width_parts)])  7.93 us
    pallas_call x2, Pallas kernels, down_last(): pl.pallas_call(functools.partial(down_last_kernel, parts, experts, k), ou...  5.48 us
    ppermute x12, waiting for transfers between devices, along_expert(): lax.ppermute(x, 'expert', [(i, (i + shift) % experts) for i in range(expe...  5.21 us
    unnamed x14, local copies, waits for them, and re-layouts  4.14 us
    pallas_call x2, Pallas kernels, combine(): pl.pallas_call(functools.partial(combine_kernel, experts, k), out_shape=j...  3.98 us
  transfers between devices with their start and end apart: 28, of which 14 were waited for; matrix products, arithmetic and copies ran while one was open for 2% of the time, Pallas kernels for 17%

profile of v8, /device:TPU:0, one launch (start us, length us, event | category | flops | bytes accessed | tf_op | source)
XLA Modules:
  0.0 123.4 jit_solution(14286276994027385802)
XLA Ops:
  0.0 3.9 %shard_map.64 = (s32[4,512]{1,0:T(4,128)S(1)}, f32[4,512]{1,0:T(4,128)S(1)}, bf16[128,1024]{1,0:T(8,128)(2,1)}, bf16[128,1024]{1,0:T(8,128)(2,1)}, bf16[128,1024]{1,0:T(8,128)(2,1)}, /*index=5*/bf16[128,1024]{1,0:T(8,128)(2,1)}) custom-call(s32[1]{0:T(128)} %bitcast.1.place_ref, s32[4,512]{1,0:T(4,128)} %picks_in.1, bf16[4,1024]{1,0:T(4,128)(2,1)} %bitcast.8, ...), custom_call_target="tpu_custom_call" | custom-call | flops 1024 | bytes 1024 | tf_op jit(solution)/shard_map/pallas_call | solution.py:106
  3.9 3.1 %collective-permute-start.11 = (bf16[128,1024]{1,0:T(8,128)(2,1)}, bf16[128,1024]{1,0:T(8,128)(2,1)S(1)}, u32[]{:S(2)}, u32[]{:S(2)}) collective-permute-start(bf16[128,1024]{1,0:T(8,128)(2,1)} %get-tuple-element.152), channel_id=1, source_target_pairs={{0,4},{4,8},{8,12},{12,0},{1,5},{5,9},{9,13},{13,1},{2,6},{6,10},{... | collective-permute-start | bytes 786440 | tf_op jit(solution)/shard_map/ppermute | solution.py:440
  7.0 2.6 %collective-permute-start.12 = (bf16[128,1024]{1,0:T(8,128)(2,1)}, bf16[128,1024]{1,0:T(8,128)(2,1)S(1)}, u32[]{:S(2)}, u32[]{:S(2)}) collective-permute-start(bf16[128,1024]{1,0:T(8,128)(2,1)} %get-tuple-element.153), channel_id=1, source_target_pairs={{0,8},{4,12},{8,0},{12,4},{1,9},{5,13},{9,1},{13,5},{2,10},{6,14},... | collective-permute-start | bytes 786440 | tf_op jit(solution)/shard_map/ppermute | solution.py:440
  13.2 14.5 %conditional.3 = (bf16[128,1024]{1,0:T(8,128)(2,1)}, bf16[128,1024]{1,0:T(8,128)(2,1)}, bf16[128,1024]{1,0:T(8,128)(2,1)}, bf16[128,1024]{1,0:T(8,128)(2,1)}, f3...) conditional(s32[]{:T(128)} %convert_element_type.15, () %tuple.40, (s32[4,512]{1,0:T(4,128)S(1)}, ...), branch_computations={%region_3.4_spmd, %region_4.5_spmd} | conditional | flops 9216 | bytes 1073216 | solution.py:497
  14.7 2.2 %collective-permute-done.8 = f32[4,512]{1,0:T(4,128)S(1)} collective-permute-done((f32[4,512]{1,0:T(4,128)S(1)}, f32[4,512]{1,0:T(4,128)S(1)}, u32[]{:S(2)}, u32[]{:S(2)}) %collective-permute-start.8) | collective-permute-done | bytes 8224 | tf_op jit(solution)/shard_map/cond/branch_1_fun/ppermute | solution.py:443
  19.4 2.7 %branch_1_fun.5 = (bf16[128,1024]{1,0:T(8,128)(2,1)}, bf16[128,1024]{1,0:T(8,128)(2,1)}, bf16[128,1024]{1,0:T(8,128)(2,1)}, bf16[128,1024]{1,0:T(8,128)(2,1)}) custom-call(s32[4,512]{1,0:T(4,128)S(1)} %get-tuple-element.39.code_ref, bf16[512,1024]{1,0:T(8,128)(2,1)} %get-tuple-element.40.tokens_ref), custom_call_target="tpu_custom_call" | custom-call | flops 1024 | bytes 1024 | tf_op jit(solution)/shard_map/cond/branch_1_fun/pallas_call | solution.py:137
  22.0 4.9 %collective-permute-done.10 = f32[1,4,512]{2,1,0:T(4,128)S(1)} collective-permute-done((f32[1,4,512]{2,1,0:T(4,128)}, f32[1,4,512]{2,1,0:T(4,128)S(1)}, u32[]{:S(2)}, u32[]{:S(2)}) %collective-permute-start.10) | collective-permute-done | bytes 8224 | tf_op jit(solution)/shard_map/cond/branch_1_fun/ppermute | solution.py:459
  31.4 5.4 %collective-permute-start.14 = (bf16[128,1024]{1,0:T(8,128)(2,1)}, bf16[128,1024]{1,0:T(8,128)(2,1)S(1)}, u32[]{:S(2)}, u32[]{:S(2)}) collective-permute-start(bf16[128,1024]{1,0:T(8,128)(2,1)} %get-tuple-element.160), channel_id=1, source_target_pairs={{0,4},{4,8},{8,12},{12,0},{1,5},{5,9},{9,13},{13,1},{2,6},{6,10},{... | collective-permute-start | bytes 786440 | tf_op jit(solution)/shard_map/ppermute | solution.py:440
  39.2 1.6 %copy-done.1 = bf16[1,4096,256]{2,1,0:T(8,128)(2,1)S(1)} copy-done((bf16[1,4096,256]{2,1,0:T(8,128)(2,1)S(1)}, bf16[1,4096,256]{2,1,0:T(8,128)(2,1)}, u32[]{:S(2)}) %copy-start.1) | copy-done | bytes 2097176
  40.8 1.8 %shard_map.66 = (f32[256,256]{1,0:T(8,128)S(1)}, f32[256,256]{1,0:T(8,128)S(1)}, bf16[2,1024,256]{2,1,0:T(8,128)(2,1)S(1)}, bf16[2,1024,256]{2,1,0:T(8,128)(2,1)S(1)}) custom-call(s32[4]{0:T(128)S(1)} %pad_add_fusion.order_ref, bf16[1,4096,256]{2,1,0:T(8,128)(2,1)S(1)} %copy-done, bf16[1,4096,256]{2,1,0:T(8,128)(2,1)S(1)} %copy-done.1, ...), custom_call_target="tpu_custom_call" | custom-call | flops 1024 | bytes 1024 | tf_op jit(solution)/shard_map/pallas_call | solution.py:222
  42.6 1.6 %collective-permute-done.17 = bf16[256,1024]{1,0:T(8,128)(2,1)} collective-permute-done((bf16[256,1024]{1,0:T(8,128)(2,1)S(1)}, bf16[256,1024]{1,0:T(8,128)(2,1)}, u32[]{:S(2)}, u32[]{:S(2)}) %collective-permute-start.17) | collective-permute-done | bytes 524320 | tf_op jit(solution)/shard_map/ppermute | solution.py:443
  44.3 11.7 %conditional.4 = (bf16[256,256]{1,0:T(8,128)(2,1)}, bf16[256,256]{1,0:T(8,128)(2,1)}, f32[256,1024]{1,0:T(8,128)S(1)}, bf16[2,256,1024]{2,1,0:T(8,128)(2,1)S(1)}) conditional(s32[]{:T(128)} %convert_element_type.15, () %tuple.45, (bf16[256,1024]{1,0:T(8,128)(2,1)}, f32[256,256]{1,0:T(8,128)S(1)}, f32[256,256]{1,0:T(8,128)S(1)}, ...), branch_computations={%region_6.7_spmd, %region_7.8_spmd} | conditional | flops 2048 | bytes 3672256 | solution.py:516
  44.3 2.1 %collective-permute-done.refs_1_ = bf16[256,1024]{1,0:T(8,128)(2,1)S(1)} collective-permute-done((bf16[256,1024]{1,0:T(8,128)(2,1)}, bf16[256,1024]{1,0:T(8,128)(2,1)S(1)}, u32[]{:S(2)}, u32[]{:S(2)}) %collective-permute-start) | collective-permute-done | bytes 524320 | tf_op jit(solution)/shard_map/cond/branch_1_fun/ppermute | solution.py:443
  46.4 1.8 %branch_1_fun.6.refs_0_ = bf16[256,256]{1,0:T(8,128)(2,1)S(1)} custom-call(f32[256,256]{1,0:T(8,128)S(1)} %get-tuple-element.46.gate_before, f32[256,256]{1,0:T(8,128)S(1)} %get-tuple-element.47.up_before, bf16[2,1024,256]{2,1,0:T(8,128)(2,1)S(1)} %get-tuple-element.48.gate_ref, bf16[2,1024,256]{2,1,0:T(8,128)(2,1)S(1)} %get-tuple-element.49.up_ref, ...), custom_call_target="tpu_custom_call" | custom-call | flops 1024 | bytes 1024 | tf_op jit(solution)/shard_map/cond/branch_1_fun/pallas_call | solution.py:250
  51.5 2.8 %collective-permute-done.1 = bf16[256,256]{1,0:T(8,128)(2,1)} collective-permute-done((bf16[256,256]{1,0:T(8,128)(2,1)S(1)}, bf16[256,256]{1,0:T(8,128)(2,1)}, u32[]{:S(2)}, u32[]{:S(2)}) %collective-permute-start.1) | collective-permute-done | bytes 131104 | tf_op jit(solution)/shard_map/cond/branch_1_fun/ppermute | solution.py:443
  54.3 1.7 %collective-permute-done.3 = bf16[256,256]{1,0:T(8,128)(2,1)} collective-permute-done((bf16[256,256]{1,0:T(8,128)(2,1)}, bf16[256,256]{1,0:T(8,128)(2,1)}, u32[]{:S(2)}, u32[]{:S(2)}) %collective-permute-start.3) | collective-permute-done | bytes 131104 | tf_op jit(solution)/shard_map/cond/branch_1_fun/ppermute | solution.py:443
  56.1 2.1 %shard_map.67.refs_0_ = bf16[256,1024]{1,0:T(8,128)(2,1)S(1)} custom-call(s32[2,4]{1,0:T(2,128)S(1)} %get-tuple-element.220.offset_ref, s32[2,4]{1,0:T(2,128)S(1)} %get-tuple-element.221.count_ref, bf16[128,1024]{1,0:T(8,128)(2,1)S(1)} %copy-done.6, bf16[128,1024]{1,0:T(8,128)(2,1)S(1)} %collective-permute-done.14.refs_1_, ...), custom_call_target="tpu_custom_call" | custom-call | flops 1024 | bytes 1024 | tf_op jit(solution)/shard_map/pallas_call | solution.py:174
  59.8 3.1 %shard_map.68 = (bf16[128,1024]{1,0:T(8,128)(2,1)S(1)}, bf16[128,1024]{1,0:T(8,128)(2,1)}, bf16[128,1024]{1,0:T(8,128)(2,1)}, bf16[128,1024]{1,0:T(8,128)(2,1)}) custom-call(s32[2,4]{1,0:T(2,128)S(1)} %get-tuple-element.220.offset_ref, s32[2,4]{1,0:T(2,128)S(1)} %get-tuple-element.221.count_ref, f32[256,1024]{1,0:T(8,128)S(1)} %get-tuple-element.180.before_ref, ...), custom_call_target="tpu_custom_call" | custom-call | flops 1024 | bytes 1024 | tf_op jit(solution)/shard_map/pallas_call | solution.py:331
  62.9 6.4 %collective-permute-start.21 = (bf16[128,1024]{1,0:T(8,128)(2,1)}, bf16[128,1024]{1,0:T(8,128)(2,1)}, u32[]{:S(2)}, u32[]{:S(2)}) collective-permute-start(bf16[128,1024]{1,0:T(8,128)(2,1)} %get-tuple-element.185), channel_id=1, source_target_pairs={{0,12},{4,0},{8,4},{12,8},{1,13},{5,1},{9,5},{13,9},{2,14},{6,2},{... | collective-permute-start | bytes 786440 | tf_op jit(solution)/shard_map/ppermute | solution.py:440
  70.6 1.6 %copy-done.2 = bf16[1,4096,256]{2,1,0:T(8,128)(2,1)S(1)} copy-done((bf16[1,4096,256]{2,1,0:T(8,128)(2,1)S(1)}, bf16[1,4096,256]{2,1,0:T(8,128)(2,1)}, u32[]{:S(2)}) %copy-start.2) | copy-done | bytes 2097176
  72.2 1.8 %shard_map.69 = (f32[256,256]{1,0:T(8,128)S(1)}, f32[256,256]{1,0:T(8,128)S(1)}, bf16[2,1024,256]{2,1,0:T(8,128)(2,1)S(1)}, bf16[2,1024,256]{2,1,0:T(8,128)(2,1)S(1)}) custom-call(s32[4]{0:T(128)S(1)} %pad_add_fusion.order_ref, bf16[1,4096,256]{2,1,0:T(8,128)(2,1)S(1)} %copy-done, bf16[1,4096,256]{2,1,0:T(8,128)(2,1)S(1)} %copy-done.2, ...), custom_call_target="tpu_custom_call" | custom-call | flops 1024 | bytes 1024 | tf_op jit(solution)/shard_map/pallas_call | solution.py:222
  74.0 11.8 %conditional.5 = (bf16[256,256]{1,0:T(8,128)(2,1)}, bf16[256,256]{1,0:T(8,128)(2,1)}, f32[256,1024]{1,0:T(8,128)S(1)}, bf16[2,256,1024]{2,1,0:T(8,128)(2,1)S(1)}) conditional(s32[]{:T(128)} %convert_element_type.16, () %tuple.42, (bf16[256,1024]{1,0:T(8,128)(2,1)}, f32[256,256]{1,0:T(8,128)S(1)}, f32[256,256]{1,0:T(8,128)S(1)}, ...), branch_computations={%region_8.9_spmd, %region_9.10_spmd} | conditional | flops 2048 | bytes 3672256 | solution.py:516
  74.1 2.1 %collective-permute-done.4.refs_1_ = bf16[256,1024]{1,0:T(8,128)(2,1)S(1)} collective-permute-done((bf16[256,1024]{1,0:T(8,128)(2,1)}, bf16[256,1024]{1,0:T(8,128)(2,1)S(1)}, u32[]{:S(2)}, u32[]{:S(2)}) %collective-permute-start.4) | collective-permute-done | bytes 524320 | tf_op jit(solution)/shard_map/cond/branch_1_fun/ppermute | solution.py:443
  76.2 1.8 %branch_1_fun.8.refs_0_ = bf16[256,256]{1,0:T(8,128)(2,1)S(1)} custom-call(f32[256,256]{1,0:T(8,128)S(1)} %get-tuple-element.58.gate_before, f32[256,256]{1,0:T(8,128)S(1)} %get-tuple-element.59.up_before, bf16[2,1024,256]{2,1,0:T(8,128)(2,1)S(1)} %get-tuple-element.60.gate_ref, bf16[2,1024,256]{2,1,0:T(8,128)(2,1)S(1)} %get-tuple-element.61.up_ref, ...), custom_call_target="tpu_custom_call" | custom-call | flops 1024 | bytes 1024 | tf_op jit(solution)/shard_map/cond/branch_1_fun/pallas_call | solution.py:250
  81.0 3.1 %collective-permute-done.5 = bf16[256,256]{1,0:T(8,128)(2,1)} collective-permute-done((bf16[256,256]{1,0:T(8,128)(2,1)S(1)}, bf16[256,256]{1,0:T(8,128)(2,1)}, u32[]{:S(2)}, u32[]{:S(2)}) %collective-permute-start.5) | collective-permute-done | bytes 131104 | tf_op jit(solution)/shard_map/cond/branch_1_fun/ppermute | solution.py:443
  84.1 1.7 %collective-permute-done.7 = bf16[256,256]{1,0:T(8,128)(2,1)} collective-permute-done((bf16[256,256]{1,0:T(8,128)(2,1)}, bf16[256,256]{1,0:T(8,128)(2,1)}, u32[]{:S(2)}, u32[]{:S(2)}) %collective-permute-start.7) | collective-permute-done | bytes 131104 | tf_op jit(solution)/shard_map/cond/branch_1_fun/ppermute | solution.py:443
  85.8 2.4 %shard_map.70 = (bf16[128,1024]{1,0:T(8,128)(2,1)S(1)}, bf16[128,1024]{1,0:T(8,128)(2,1)S(1)}, bf16[128,1024]{1,0:T(8,128)(2,1)S(1)}, bf16[128,1024]{1,0:T(8,128)(2,1)S(1)}) custom-call(s32[2,4]{1,0:T(2,128)S(1)} %get-tuple-element.220.offset_ref, s32[2,4]{1,0:T(2,128)S(1)} %get-tuple-element.221.count_ref, f32[256,1024]{1,0:T(8,128)S(1)} %get-tuple-element.199.before_ref, ...), custom_call_target="tpu_custom_call" | custom-call | flops 1024 | bytes 1024 | tf_op jit(solution)/shard_map/pallas_call | solution.py:331
  88.2 5.1 %collective-permute-done.22.refs_2_ = bf16[128,1024]{1,0:T(8,128)(2,1)} collective-permute-done((bf16[128,1024]{1,0:T(8,128)(2,1)}, bf16[128,1024]{1,0:T(8,128)(2,1)}, u32[]{:S(2)}, u32[]{:S(2)}) %collective-permute-start.22) | collective-permute-done | bytes 262176 | tf_op jit(solution)/shard_map/ppermute | solution.py:440
  94.9 2.0 %collective-permute-start.27 = (bf16[128,1024]{1,0:T(8,128)(2,1)S(1)}, bf16[128,1024]{1,0:T(8,128)(2,1)S(1)}, u32[]{:S(2)}, u32[]{:S(2)}) collective-permute-start(bf16[128,1024]{1,0:T(8,128)(2,1)S(1)} %get-tuple-element.210), channel_id=1, source_target_pairs={{0,4},{4,8},{8,12},{12,0},{1,5},{5,9},{9,13},{13,1},{2,6},{6,10},{... | collective-permute-start | bytes 786440 | tf_op jit(solution)/shard_map/ppermute | solution.py:440
  98.2 20.1 %collective-permute-done.24 = f32[2,4,512]{2,1,0:T(4,128)S(1)} collective-permute-done((f32[2,4,512]{2,1,0:T(4,128)S(1)}, f32[2,4,512]{2,1,0:T(4,128)S(1)}, u32[]{:S(2)}, u32[]{:S(2)}) %collective-permute-start.24) | collective-permute-done | bytes 16416 | tf_op jit(solution)/shard_map/ppermute | solution.py:459
  119.4 1.9 %shard_map.72.refs_4_ = f32[512,1024]{1,0:T(8,128)S(1)} custom-call(s32[4,512]{1,0:T(4,128)S(1)} %get-tuple-element.143.code_ref, f32[4,512]{1,0:T(4,128)S(1)} %shard_map.71.weight_ref, bf16[128,1024]{1,0:T(8,128)(2,1)S(1)} %get-tuple-element.212.refs_0_, bf16[128,1024]{1,0:T(8,128)(2,1)} %collective-permute-done.21.refs_1_, ...), custom_call_target="tpu_custom_call" | custom-call | flops 1024 | bytes 1024 | tf_op jit(solution)/shard_map/pallas_call | solution.py:409
  121.3 2.1 %shard_map.73 = bf16[512,1024]{1,0:T(8,128)(2,1)} custom-call(s32[4,512]{1,0:T(4,128)S(1)} %get-tuple-element.143.code_ref, f32[4,512]{1,0:T(4,128)S(1)} %shard_map.71.weight_ref, bf16[128,1024]{1,0:T(8,128)(2,1)S(1)} %get-tuple-element.207.refs_0_, bf16[128,1024]{1,0:T(8,128)(2,1)S(1)} %collective-permute-done.25.refs_1_, ...), custom_call_target="tpu_custom_call" | custom-call | flops 1024 | bytes 1024 | tf_op jit(solution)/shard_map/pallas_call | solution.py:409
  (68 shorter events, 26.6 us)
Async XLA Ops:
  3.9 35.3 %copy-start = (bf16[1,4096,256]{2,1,0:T(8,128)(2,1)S(1)}, bf16[1,4096,256]{2,1,0:T(8,128)(2,1)}, u32[]{:S(2)}) copy-start(bf16[1,4096,256]{2,1,0:T(8,128)(2,1)} %gate_ref.3) | copy-start | bytes 6291460
  3.9 23.7 %collective-permute-start.11 = (bf16[128,1024]{1,0:T(8,128)(2,1)}, bf16[128,1024]{1,0:T(8,128)(2,1)S(1)}, u32[]{:S(2)}, u32[]{:S(2)}) collective-permute-start(bf16[128,1024]{1,0:T(8,128)(2,1)} %get-tuple-element.152), channel_id=1, source_target_pairs={{0,4},{4,8},{8,12},{12,0},{1,5},{5,9},{9,13},{13,1},{2,6},{6,10},{... | collective-permute-start | bytes 786440 | tf_op jit(solution)/shard_map/ppermute | solution.py:440
  7.0 20.7 %collective-permute-start.12 = (bf16[128,1024]{1,0:T(8,128)(2,1)}, bf16[128,1024]{1,0:T(8,128)(2,1)S(1)}, u32[]{:S(2)}, u32[]{:S(2)}) collective-permute-start(bf16[128,1024]{1,0:T(8,128)(2,1)} %get-tuple-element.153), channel_id=1, source_target_pairs={{0,8},{4,12},{8,0},{12,4},{1,9},{5,13},{9,1},{13,5},{2,10},{6,14},... | collective-permute-start | bytes 786440 | tf_op jit(solution)/shard_map/ppermute | solution.py:440
  9.6 18.1 %collective-permute-start.13 = (bf16[128,1024]{1,0:T(8,128)(2,1)}, bf16[128,1024]{1,0:T(8,128)(2,1)S(1)}, u32[]{:S(2)}, u32[]{:S(2)}) collective-permute-start(bf16[128,1024]{1,0:T(8,128)(2,1)} %get-tuple-element.154), channel_id=1, source_target_pairs={{0,12},{4,0},{8,4},{12,8},{1,13},{5,1},{9,5},{13,9},{2,14},{6,2},{... | collective-permute-start | bytes 786440 | tf_op jit(solution)/shard_map/ppermute | solution.py:440
  13.2 3.7 %collective-permute-start.8 = (f32[4,512]{1,0:T(4,128)S(1)}, f32[4,512]{1,0:T(4,128)S(1)}, u32[]{:S(2)}, u32[]{:S(2)}) collective-permute-start(f32[4,512]{1,0:T(4,128)S(1)} %get-tuple-element.45), channel_id=1, source_target_pairs={{0,2},{1,3},{2,0},{3,1},{4,6},{5,7},{6,4},{7,5},{8,10},{9,11},{10,... | collective-permute-start | bytes 24584 | tf_op jit(solution)/shard_map/cond/branch_1_fun/ppermute | solution.py:443
  16.9 1.2 collective-permute-start.9
  18.7 8.2 %collective-permute-start.10 = (f32[1,4,512]{2,1,0:T(4,128)}, f32[1,4,512]{2,1,0:T(4,128)S(1)}, u32[]{:S(2)}, u32[]{:S(2)}) collective-permute-start(f32[1,4,512]{2,1,0:T(4,128)} %bitcast), channel_id=1, source_target_pairs={{0,4},{4,0},{8,12},{12,8},{1,5},{5,1},{9,13},{13,9},{2,6},{6,2},{1... | collective-permute-start | bytes 24584 | tf_op jit(solution)/shard_map/cond/branch_1_fun/ppermute | solution.py:459
  29.8 9.5 %collective-permute-start.18 = (bf16[256,1024]{1,0:T(8,128)(2,1)S(1)}, bf16[256,1024]{1,0:T(8,128)(2,1)S(1)}, u32[]{:S(2)}, u32[]{:S(2)}) collective-permute-start(bf16[256,1024]{1,0:T(8,128)(2,1)S(1)} %shard_map.65.refs_0_), channel_id=1, source_target_pairs={{0,1},{1,0},{2,3},{3,2},{4,5},{5,4},{6,7},{7,6},{8,9},{9,8},{10,11... | collective-permute-start | bytes 1572872 | tf_op jit(solution)/shard_map/ppermute | solution.py:443
  29.8 14.4 %collective-permute-start.17 = (bf16[256,1024]{1,0:T(8,128)(2,1)S(1)}, bf16[256,1024]{1,0:T(8,128)(2,1)}, u32[]{:S(2)}, u32[]{:S(2)}) collective-permute-start(bf16[256,1024]{1,0:T(8,128)(2,1)S(1)} %shard_map.65.refs_0_), channel_id=1, source_target_pairs={{0,2},{1,3},{2,0},{3,1},{4,6},{5,7},{6,4},{7,5},{8,10},{9,11},{10,... | collective-permute-start | bytes 1572872 | tf_op jit(solution)/shard_map/ppermute | solution.py:443
  31.4 24.5 %collective-permute-start.14 = (bf16[128,1024]{1,0:T(8,128)(2,1)}, bf16[128,1024]{1,0:T(8,128)(2,1)S(1)}, u32[]{:S(2)}, u32[]{:S(2)}) collective-permute-start(bf16[128,1024]{1,0:T(8,128)(2,1)} %get-tuple-element.160), channel_id=1, source_target_pairs={{0,4},{4,8},{8,12},{12,0},{1,5},{5,9},{9,13},{13,1},{2,6},{6,10},{... | collective-permute-start | bytes 786440 | tf_op jit(solution)/shard_map/ppermute | solution.py:440
  36.8 19.3 %collective-permute-start.15 = (bf16[128,1024]{1,0:T(8,128)(2,1)}, bf16[128,1024]{1,0:T(8,128)(2,1)}, u32[]{:S(2)}, u32[]{:S(2)}) collective-permute-start(bf16[128,1024]{1,0:T(8,128)(2,1)} %get-tuple-element.161), channel_id=1, source_target_pairs={{0,8},{4,12},{8,0},{12,4},{1,9},{5,13},{9,1},{13,5},{2,10},{6,14},... | collective-permute-start | bytes 786440 | tf_op jit(solution)/shard_map/ppermute | solution.py:440
  38.3 17.8 %collective-permute-start.16 = (bf16[128,1024]{1,0:T(8,128)(2,1)}, bf16[128,1024]{1,0:T(8,128)(2,1)}, u32[]{:S(2)}, u32[]{:S(2)}) collective-permute-start(bf16[128,1024]{1,0:T(8,128)(2,1)} %get-tuple-element.162), channel_id=1, source_target_pairs={{0,12},{4,0},{8,4},{12,8},{1,13},{5,1},{9,5},{13,9},{2,14},{6,2},{... | collective-permute-start | bytes 786440 | tf_op jit(solution)/shard_map/ppermute | solution.py:440
  40.8 3.5 %copy-start.4 = (bf16[1,1024,1024]{2,1,0:T(8,128)(2,1)S(1)}, bf16[1,1024,1024]{2,1,0:T(8,128)(2,1)}, u32[]{:S(2)}) copy-start(bf16[1,1024,1024]{2,1,0:T(8,128)(2,1)} %param.16) | copy-start | bytes 6291460
  44.3 11.8 %copy-start.6 = (bf16[128,1024]{1,0:T(8,128)(2,1)S(1)}, bf16[128,1024]{1,0:T(8,128)(2,1)}, u32[]{:S(2)}) copy-start(bf16[128,1024]{1,0:T(8,128)(2,1)} %get-tuple-element.174.refs_0_) | copy-start | bytes 786436
  44.3 2.1 %collective-permute-start = (bf16[256,1024]{1,0:T(8,128)(2,1)}, bf16[256,1024]{1,0:T(8,128)(2,1)S(1)}, u32[]{:S(2)}, u32[]{:S(2)}) collective-permute-start(bf16[256,1024]{1,0:T(8,128)(2,1)} %get-tuple-element.50.refs_0_), channel_id=1, source_target_pairs={{0,1},{1,0},{2,3},{3,2},{4,5},{5,4},{6,7},{7,6},{8,9},{9,8},{10,11... | collective-permute-start | bytes 1572872 | tf_op jit(solution)/shard_map/cond/branch_1_fun/ppermute | solution.py:443
  48.2 1.7 %collective-permute-start.2 = (bf16[256,256]{1,0:T(8,128)(2,1)S(1)}, bf16[256,256]{1,0:T(8,128)(2,1)S(1)}, u32[]{:S(2)}, u32[]{:S(2)}) collective-permute-start(bf16[256,256]{1,0:T(8,128)(2,1)S(1)} %branch_1_fun.6.refs_0_), channel_id=1, source_target_pairs={{0,1},{1,0},{2,3},{3,2},{4,5},{5,4},{6,7},{7,6},{8,9},{9,8},{10,11... | collective-permute-start | bytes 393224 | tf_op jit(solution)/shard_map/cond/branch_1_fun/ppermute | solution.py:443
  48.4 5.9 %collective-permute-start.1 = (bf16[256,256]{1,0:T(8,128)(2,1)S(1)}, bf16[256,256]{1,0:T(8,128)(2,1)}, u32[]{:S(2)}, u32[]{:S(2)}) collective-permute-start(bf16[256,256]{1,0:T(8,128)(2,1)S(1)} %branch_1_fun.6.refs_0_), channel_id=1, source_target_pairs={{0,2},{1,3},{2,0},{3,1},{4,6},{5,7},{6,4},{7,5},{8,10},{9,11},{10,... | collective-permute-start | bytes 393224 | tf_op jit(solution)/shard_map/cond/branch_1_fun/ppermute | solution.py:443
  54.3 1.7 %collective-permute-start.3 = (bf16[256,256]{1,0:T(8,128)(2,1)}, bf16[256,256]{1,0:T(8,128)(2,1)}, u32[]{:S(2)}, u32[]{:S(2)}) collective-permute-start(bf16[256,256]{1,0:T(8,128)(2,1)} %collective-permute-done.1), channel_id=1, source_target_pairs={{0,1},{1,0},{2,3},{3,2},{4,5},{5,4},{6,7},{7,6},{8,9},{9,8},{10,11... | collective-permute-start | bytes 393224 | tf_op jit(solution)/shard_map/cond/branch_1_fun/ppermute | solution.py:443
  58.2 12.4 %collective-permute-start.20 = (bf16[256,1024]{1,0:T(8,128)(2,1)S(1)}, bf16[256,1024]{1,0:T(8,128)(2,1)S(1)}, u32[]{:S(2)}, u32[]{:S(2)}) collective-permute-start(bf16[256,1024]{1,0:T(8,128)(2,1)S(1)} %shard_map.67.refs_0_), channel_id=1, source_target_pairs={{0,1},{1,0},{2,3},{3,2},{4,5},{5,4},{6,7},{7,6},{8,9},{9,8},{10,11... | collective-permute-start | bytes 1572872 | tf_op jit(solution)/shard_map/ppermute | solution.py:443
  58.3 15.7 %collective-permute-start.19 = (bf16[256,1024]{1,0:T(8,128)(2,1)S(1)}, bf16[256,1024]{1,0:T(8,128)(2,1)}, u32[]{:S(2)}, u32[]{:S(2)}) collective-permute-start(bf16[256,1024]{1,0:T(8,128)(2,1)S(1)} %shard_map.67.refs_0_), channel_id=1, source_target_pairs={{0,2},{1,3},{2,0},{3,1},{4,6},{5,7},{6,4},{7,5},{8,10},{9,11},{10,... | collective-permute-start | bytes 1572872 | tf_op jit(solution)/shard_map/ppermute | solution.py:443
  62.9 25.2 %collective-permute-start.21 = (bf16[128,1024]{1,0:T(8,128)(2,1)}, bf16[128,1024]{1,0:T(8,128)(2,1)}, u32[]{:S(2)}, u32[]{:S(2)}) collective-permute-start(bf16[128,1024]{1,0:T(8,128)(2,1)} %get-tuple-element.185), channel_id=1, source_target_pairs={{0,12},{4,0},{8,4},{12,8},{1,13},{5,1},{9,5},{13,9},{2,14},{6,2},{... | collective-permute-start | bytes 786440 | tf_op jit(solution)/shard_map/ppermute | solution.py:440
  69.3 23.9 %collective-permute-start.22 = (bf16[128,1024]{1,0:T(8,128)(2,1)}, bf16[128,1024]{1,0:T(8,128)(2,1)}, u32[]{:S(2)}, u32[]{:S(2)}) collective-permute-start(bf16[128,1024]{1,0:T(8,128)(2,1)} %get-tuple-element.186), channel_id=1, source_target_pairs={{0,8},{4,12},{8,0},{12,4},{1,9},{5,13},{9,1},{13,5},{2,10},{6,14},... | collective-permute-start | bytes 786440 | tf_op jit(solution)/shard_map/ppermute | solution.py:440
  69.8 23.4 %collective-permute-start.23 = (bf16[128,1024]{1,0:T(8,128)(2,1)}, bf16[128,1024]{1,0:T(8,128)(2,1)}, u32[]{:S(2)}, u32[]{:S(2)}) collective-permute-start(bf16[128,1024]{1,0:T(8,128)(2,1)} %get-tuple-element.187), channel_id=1, source_target_pairs={{0,4},{4,8},{8,12},{12,0},{1,5},{5,9},{9,13},{13,1},{2,6},{6,10},{... | collective-permute-start | bytes 786440 | tf_op jit(solution)/shard_map/ppermute | solution.py:440
  72.2 1.8 %copy-start.5 = (bf16[1,1024,1024]{2,1,0:T(8,128)(2,1)S(1)}, bf16[1,1024,1024]{2,1,0:T(8,128)(2,1)}, u32[]{:S(2)}) copy-start(bf16[1,1024,1024]{2,1,0:T(8,128)(2,1)} %param.16) | copy-start | bytes 6291460
  74.0 2.2 %collective-permute-start.4 = (bf16[256,1024]{1,0:T(8,128)(2,1)}, bf16[256,1024]{1,0:T(8,128)(2,1)S(1)}, u32[]{:S(2)}, u32[]{:S(2)}) collective-permute-start(bf16[256,1024]{1,0:T(8,128)(2,1)} %get-tuple-element.62.refs_0_), channel_id=1, source_target_pairs={{0,1},{1,0},{2,3},{3,2},{4,5},{5,4},{6,7},{7,6},{8,9},{9,8},{10,11... | collective-permute-start | bytes 1572872 | tf_op jit(solution)/shard_map/cond/branch_1_fun/ppermute | solution.py:443
  78.0 1.4 %collective-permute-start.6 = (bf16[256,256]{1,0:T(8,128)(2,1)S(1)}, bf16[256,256]{1,0:T(8,128)(2,1)S(1)}, u32[]{:S(2)}, u32[]{:S(2)}) collective-permute-start(bf16[256,256]{1,0:T(8,128)(2,1)S(1)} %branch_1_fun.8.refs_0_), channel_id=1, source_target_pairs={{0,1},{1,0},{2,3},{3,2},{4,5},{5,4},{6,7},{7,6},{8,9},{9,8},{10,11... | collective-permute-start | bytes 393224 | tf_op jit(solution)/shard_map/cond/branch_1_fun/ppermute | solution.py:443
  78.2 5.9 %collective-permute-start.5 = (bf16[256,256]{1,0:T(8,128)(2,1)S(1)}, bf16[256,256]{1,0:T(8,128)(2,1)}, u32[]{:S(2)}, u32[]{:S(2)}) collective-permute-start(bf16[256,256]{1,0:T(8,128)(2,1)S(1)} %branch_1_fun.8.refs_0_), channel_id=1, source_target_pairs={{0,2},{1,3},{2,0},{3,1},{4,6},{5,7},{6,4},{7,5},{8,10},{9,11},{10,... | collective-permute-start | bytes 393224 | tf_op jit(solution)/shard_map/cond/branch_1_fun/ppermute | solution.py:443
  84.1 1.7 %collective-permute-start.7 = (bf16[256,256]{1,0:T(8,128)(2,1)}, bf16[256,256]{1,0:T(8,128)(2,1)}, u32[]{:S(2)}, u32[]{:S(2)}) collective-permute-start(bf16[256,256]{1,0:T(8,128)(2,1)} %collective-permute-done.5), channel_id=1, source_target_pairs={{0,1},{1,0},{2,3},{3,2},{4,5},{5,4},{6,7},{7,6},{8,9},{9,8},{10,11... | collective-permute-start | bytes 393224 | tf_op jit(solution)/shard_map/cond/branch_1_fun/ppermute | solution.py:443
  93.2 28.0 %collective-permute-start.25 = (bf16[128,1024]{1,0:T(8,128)(2,1)S(1)}, bf16[128,1024]{1,0:T(8,128)(2,1)S(1)}, u32[]{:S(2)}, u32[]{:S(2)}) collective-permute-start(bf16[128,1024]{1,0:T(8,128)(2,1)S(1)} %get-tuple-element.208), channel_id=1, source_target_pairs={{0,12},{4,0},{8,4},{12,8},{1,13},{5,1},{9,5},{13,9},{2,14},{6,2},{... | collective-permute-start | bytes 786440 | tf_op jit(solution)/shard_map/ppermute | solution.py:440
  93.7 27.6 %collective-permute-start.26 = (bf16[128,1024]{1,0:T(8,128)(2,1)S(1)}, bf16[128,1024]{1,0:T(8,128)(2,1)S(1)}, u32[]{:S(2)}, u32[]{:S(2)}) collective-permute-start(bf16[128,1024]{1,0:T(8,128)(2,1)S(1)} %get-tuple-element.209), channel_id=1, source_target_pairs={{0,8},{4,12},{8,0},{12,4},{1,9},{5,13},{9,1},{13,5},{2,10},{6,14},... | collective-permute-start | bytes 786440 | tf_op jit(solution)/shard_map/ppermute | solution.py:440
  94.9 26.4 %collective-permute-start.27 = (bf16[128,1024]{1,0:T(8,128)(2,1)S(1)}, bf16[128,1024]{1,0:T(8,128)(2,1)S(1)}, u32[]{:S(2)}, u32[]{:S(2)}) collective-permute-start(bf16[128,1024]{1,0:T(8,128)(2,1)S(1)} %get-tuple-element.210), channel_id=1, source_target_pairs={{0,4},{4,8},{8,12},{12,0},{1,5},{5,9},{9,13},{13,1},{2,6},{6,10},{... | collective-permute-start | bytes 786440 | tf_op jit(solution)/shard_map/ppermute | solution.py:440
  96.9 21.4 %collective-permute-start.24 = (f32[2,4,512]{2,1,0:T(4,128)S(1)}, f32[2,4,512]{2,1,0:T(4,128)S(1)}, u32[]{:S(2)}, u32[]{:S(2)}) collective-permute-start(f32[2,4,512]{2,1,0:T(4,128)S(1)} %get-tuple-element.211), channel_id=1, source_target_pairs={{0,8},{4,12},{8,0},{12,4},{1,9},{5,13},{9,1},{13,5},{2,10},{6,14},... | collective-permute-start | bytes 49160 | tf_op jit(solution)/shard_map/ppermute | solution.py:459
  (3 other events, 4.1 us)

commit v9 on v8

--- a/solution.py
+++ b/solution.py
@@ -42,48 +42,46 @@
     return copies
 
 
-def code_kernel(experts, depth, place_ref, picks_in, router_in, tokens_ref, code_ref, logits_ref, *refs):
+def code_kernel(experts, depth, place_ref, picks_in, tokens_ref, code_ref, *refs):
     sends = refs[:experts]
-    picks_ref, router_ref, held, staged, in_sems, out_sems = refs[experts:]
-    picks_load, router_load, load = start_all(
-        [picks_in, router_in, tokens_ref], [picks_ref, router_ref, held], in_sems
-    )
+    picks_ref, held, staged, in_sems, out_sems = refs[experts:]
+    picks_load, load = start_all([picks_in, tokens_ref], [picks_ref, held], in_sems)
     me = place_ref[0]
     rows, width = held.shape
     capacity = picks_ref.shape[1]
     strips = rows // 128
     lanes = lax.broadcasted_iota(I32, (128, capacity), 0)
     strip_ids = lax.broadcasted_iota(I32, (8, capacity), 0)
+    total = 8 * experts
+    row_ids = lax.broadcasted_iota(I32, (total, total), 0)
+    lane_ids = lax.broadcasted_iota(I32, (total, total), 1)
+    same = lax.shift_right_logical(row_ids, 3) == lax.shift_right_logical(lane_ids, 3)
+    before = (same & (lane_ids < row_ids)).astype(F32).astype(BF16)
     upper = (lax.broadcasted_iota(I32, (128, 128), 0) < lax.broadcasted_iota(I32, (128, 128), 1)).astype(BF16)
-    before = (lax.broadcasted_iota(I32, (8, 8), 1) < lax.broadcasted_iota(I32, (8, 8), 0)).astype(BF16)
     ones = jnp.ones((128, 128), BF16)
     picks_load.wait()
+    masks, starts = [], []
+    for shift in range(experts):
+        local = picks_ref[pl.ds(lax.rem(me + shift, experts), 1), :] - me * rows
+        starts.append(jnp.broadcast_to(jnp.sum((local < 0).astype(F32), axis=1, keepdims=True), (8, 128)))
+        strip = lax.shift_right_arithmetic(local, 7)
+        place = jnp.bitwise_and(local, 127)
+        high = ((strip == strip_ids) & (strip_ids < strips)).astype(F32).astype(BF16)
+        low = (place == lanes).astype(F32).astype(BF16)
+        masks.append(lax.dot_general(high, low, (((1,), (1,)), ((), ())), preferred_element_type=F32))
+    mask = jnp.concatenate(masks, axis=0)
+    start = jnp.concatenate(starts, axis=0).astype(I32)
+    mask16 = mask.astype(BF16)
+    totals = dot(mask16, ones)
+    rank = (dot(mask16, upper) + dot(before, totals.astype(BF16))).astype(I32)
+    slot = lax.rem(rank + start, BATCHES) * depth + lax.div(rank, BATCHES)
+    code = jnp.where(mask > 0.5, slot, -1)
     code_rows = []
     for shift in range(experts):
-        expert = lax.rem(me + shift, experts)
-        chosen = picks_ref[pl.ds(expert, 1), :]
-        local = chosen - me * rows
-        start = jnp.sum((local < 0).astype(F32)).astype(I32)
-        strip = lax.shift_right_arithmetic(local, 7)
-        place = jnp.bitwise_and(local, 127)
-        high = (strip == strip_ids).astype(BF16)
-        high = jnp.where(strip_ids < strips, high, jnp.zeros_like(high))
-        low = (place == lanes).astype(BF16)
-        mask = lax.dot_general(high, low, (((1,), (1,)), ((), ())), preferred_element_type=F32)
-        mask16 = mask.astype(BF16)
-        totals = dot(mask16, ones)
-        rank = (dot(mask16, upper) + dot(before, totals.astype(BF16))).astype(I32)
-        batch = lax.rem(rank + start, BATCHES)
-        slot = batch * depth + lax.div(rank, BATCHES)
-        code = jnp.where(mask > 0.5, slot, -1)
-        row = jnp.concatenate([code[i : i + 1] for i in range(strips)], axis=1)
+        row = jnp.concatenate([code[8 * shift + i : 8 * shift + i + 1] for i in range(strips)], axis=1)
         code_ref[pl.ds(shift, 1), :] = row
         code_rows.append(row)
-    router_load.wait()
     load.wait()
-    logits_ref[...] = lax.dot_general(
-        router_ref[...], held[...], (((1,), (1,)), ((), ())), preferred_element_type=F32
-    )
     pack(0, depth, code_rows, held, staged, sends, out_sems)
 
 
@@ -100,27 +98,43 @@
         copy.wait()
 
 
-def first_batch(place, picks, router, tokens, depth):
+def first_batch(place, picks, tokens, depth):
     rows, width = tokens.shape
     experts = picks.shape[0]
     out = pl.pallas_call(
         functools.partial(code_kernel, experts, depth),
-        out_shape=[jax.ShapeDtypeStruct((experts, rows), I32), jax.ShapeDtypeStruct((experts, rows), F32)]
+        out_shape=[jax.ShapeDtypeStruct((experts, rows), I32)]
         + [jax.ShapeDtypeStruct((depth, width), BF16)] * experts,
-        in_specs=[smem()] + apart(3),
-        out_specs=whole(2) + apart(experts),
+        in_specs=[smem()] + apart(2),
+        out_specs=whole(1) + apart(experts),
         scratch_shapes=[
             pltpu.VMEM(picks.shape, I32),
-            pltpu.VMEM(router.shape, BF16),
             pltpu.VMEM((rows, width), BF16),
             pltpu.VMEM((experts, depth, width), BF16),
-            pltpu.SemaphoreType.DMA((3,)),
+            pltpu.SemaphoreType.DMA((2,)),
             pltpu.SemaphoreType.DMA((experts,)),
         ],
         compiler_params=params(60 * 1024 * 1024),
         cost_estimate=COST,
-    )(place, picks, router, tokens)
-    return out[0], out[1], out[2:]
+    )(place, picks, tokens)
+    return out[0], out[1:]
+
+
+def logits_kernel(router_ref, tokens_ref, out_ref):
+    out_ref[...] = lax.dot_general(
+        router_ref[...], tokens_ref[...], (((1,), (1,)), ((), ())), preferred_element_type=F32
+    )
+
+
+def partial_logits(router, tokens):
+    return pl.pallas_call(
+        logits_kernel,
+        out_shape=jax.ShapeDtypeStruct((router.shape[0], tokens.shape[0]), F32),
+        in_specs=whole(2),
+        out_specs=whole(1)[0],
+        compiler_params=params(),
+        cost_estimate=COST,
+    )(router, tokens)
 
 
 def pack_kernel(experts, depth, k, code_ref, tokens_ref, *refs):
@@ -377,14 +391,11 @@
 
 
 def combine_kernel(experts, k, code_ref, weight_ref, *refs):
-    count = experts + (k > 0)
-    blocks, out_ref = refs[:count], refs[count]
-    held, sems = refs[count + 1], refs[count + 2]
+    before, refs = refs[: k > 0], refs[k > 0 :]
+    blocks, (out_ref, held, sems) = refs[:experts], refs[experts:]
     depth = blocks[0].shape[0]
     rows = code_ref.shape[1]
     targets = [held.at[pl.ds(i * depth, depth)] for i in range(experts)]
-    if k > 0:
-        targets.append(refs[count + 3])
     loads = start_all(blocks, targets, sems)
     slot_ids = lax.broadcasted_iota(I32, (depth, rows), 0) + k * depth
     parts = [
@@ -396,7 +407,7 @@
         load.wait()
     total = lax.dot_general(spread, held[...], (((0,), (0,)), ((), ())), preferred_element_type=F32)
     if k > 0:
-        total = total + refs[count + 3][...]
+        total = total + before[0][...]
     out_ref[...] = total.astype(out_ref.dtype)
 
 
@@ -409,16 +420,12 @@
     return pl.pallas_call(
         functools.partial(combine_kernel, experts, k),
         out_shape=jax.ShapeDtypeStruct((rows, width), BF16 if last else F32),
-        in_specs=whole(2) + apart(experts + len(more)),
+        in_specs=whole(2 + len(more)) + apart(experts),
         out_specs=whole(1)[0],
-        scratch_shapes=[
-            pltpu.VMEM((experts * depth, width), BF16),
-            pltpu.SemaphoreType.DMA((experts + len(more),)),
-        ]
-        + [pltpu.VMEM((rows, width), F32)] * len(more),
-        compiler_params=params(),
-        cost_estimate=COST,
-    )(code, weights, *blocks, *more)
+        scratch_shapes=[pltpu.VMEM((experts * depth, width), BF16), pltpu.SemaphoreType.DMA((experts,))],
+        compiler_params=params(),
+        cost_estimate=COST,
+    )(code, weights, *more, *blocks)
 
 
 def after(value, *first):
@@ -470,7 +477,7 @@
         far = swap(x, bits[0])
         return spread(x), spread(far)
 
-    code, logits, first = first_batch(place, picks, router_weight.T, tokens, depth)
+    code, first = first_batch(place, picks, tokens, depth)
     own_picks = lax.dynamic_slice_in_dim(picks, me, 1, axis=0)
     sources = lax.rem(me - jnp.arange(experts, dtype=I32) + experts, experts)
     start = jnp.sum((own_picks < (sources * rows)[:, None]).astype(I32), axis=1)
@@ -481,7 +488,8 @@
 
     present = [jnp.sum(counts[k]) > 0 for k in range(BATCHES)]
 
-    def beside_first(logits):
+    def beside_first(router):
+        logits = partial_logits(router, tokens)
         later = [tuple(later_batch(code, tokens, k, depth)) for k in range(1, BATCHES)]
         for bit in bits:
             logits = logits + swap(logits, bit)
@@ -490,11 +498,11 @@
             gathered = jnp.concatenate([gathered, swap_expert(gathered, bit)])
         return later, logits, gathered
 
-    def nothing_first(logits):
-        return jax.tree.map(lambda x: jnp.zeros(x.shape, x.dtype), jax.eval_shape(beside_first, logits))
+    def nothing_first(router):
+        return jax.tree.map(lambda x: jnp.zeros(x.shape, x.dtype), jax.eval_shape(beside_first, router))
 
     arrived = [[first[0]] + [along_expert(first[shift], shift) for shift in range(1, experts)]]
-    later, logits, gathered = lax.cond(present[0], beside_first, nothing_first, logits)
+    later, logits, gathered = lax.cond(present[0], beside_first, nothing_first, router_weight.T)
 
     def far_half(far, sums):
         far = spread(far)
@@ -529,9 +537,14 @@
         block = compact(offsets, counts, k, blocks, size)
         across = swap(block, bits[0])
         near = spread(block)
+        if k == 1:
+            gathered = after(gathered, blocks)
+            gathered = jnp.concatenate([gathered, swap_expert(gathered, expert_bits[-1])])
         if k > 0:
             far, partial = after((far, partial), block)
             results = settle(k - 1, far, partial)
+            if k == 1:
+                results, gathered = lax.optimization_barrier((results, gathered))
             if k > 1:
                 results, waiting[k - 2] = lax.optimization_barrier((results, waiting[k - 2]))
             waiting.append(send_back(results))
@@ -543,8 +556,6 @@
     results = settle(BATCHES - 1, far, partial)
     results, waiting[-1] = lax.optimization_barrier((results, waiting[-1]))
     waiting.append(send_back(results))
-    gathered = after(gathered, results)
-    gathered = jnp.concatenate([gathered, swap_expert(gathered, expert_bits[-1])])
     weights = slot_weights(place, logits, gathered, code)
     total = None
     for k in range(BATCHES):

time: 124 us -> 121 us (0.976)
  waiting for transfers between devices: 48.7 us -> 44 us
    ppermute x2, waiting for transfers between devices: 25 us -> 3.14 us  [swap_expert(): return lax.ppermute(x, 'expert', [(i, i ^ bit) for i in range(experts)])]
    ppermute x12, waiting for transfers between devices: 5.21 us -> 22.3 us  [along_expert(): lax.ppermute(x, 'expert', [(i, (i + shift) % experts) for i in range(expe...]
    ppermute x12, starting transfers between devices: 25.5 us -> 22.3 us  [along_expert(): lax.ppermute(x, 'expert', [(i, (i + shift) % experts) for i in range(expe...]
    ppermute x2, starting transfers between devices: 1.94 us -> 5.08 us  [swap_expert(): return lax.ppermute(x, 'expert', [(i, i ^ bit) for i in range(experts)])]
    pallas_call x0 -> x1, Pallas kernels: none -> 1.76 us  [partial_logits(): pl.pallas_call(logits_kernel, out_shape=jax.ShapeDtypeStruct((router.shap...]
    unnamed x14 -> x18, local copies, waits for them, and re-layouts: 4.14 us -> 4.84 us
  transfers between devices with their start and end apart: 28 -> 28, of which waited for: 14 -> 15; matrix products, arithmetic and copies ran while one was open for 2% -> 3% of each run, Pallas kernels for 17% -> 19%
where the time goes in v9:
time: 121 us; the launch traced here: 120 us
  waiting for transfers between devices  44 us (36%)
  starting transfers between devices  35.3 us (29%)
  Pallas kernels  31.1 us (26%)
  local copies, waits for them, and re-layouts  5.54 us (5%)
  other arithmetic  2.35 us (2%)
  between operations  1.55 us (1%)
    ppermute x12, starting transfers between devices, along_expert(): lax.ppermute(x, 'expert', [(i, (i + shift) % experts) for i in range(expe...  22.3 us
    ppermute x12, waiting for transfers between devices, along_expert(): lax.ppermute(x, 'expert', [(i, (i + shift) % experts) for i in range(expe...  22.3 us
    ppermute x14, waiting for transfers between devices, swap(): return lax.ppermute(x, 'dp', [(i, i ^ bit) for i in range(width_parts)])  18.5 us
    ppermute x14, starting transfers between devices, swap(): return lax.ppermute(x, 'dp', [(i, i ^ bit) for i in range(width_parts)])  7.91 us
    pallas_call x2, Pallas kernels, down_last(): pl.pallas_call(functools.partial(down_last_kernel, parts, experts, k), ou...  5.47 us
    ppermute x2, starting transfers between devices, swap_expert(): return lax.ppermute(x, 'expert', [(i, i ^ bit) for i in range(experts)])  5.08 us
    unnamed x18, local copies, waits for them, and re-layouts  4.84 us
    pallas_call x2, Pallas kernels, combine(): pl.pallas_call(functools.partial(combine_kernel, experts, k), out_shape=j...  3.82 us
  transfers between devices with their start and end apart: 28, of which 15 were waited for; matrix products, arithmetic and copies ran while one was open for 3% of the time, Pallas kernels for 19%

profile of v9, /device:TPU:0, one launch (start us, length us, event | category | flops | bytes accessed | tf_op | source)
XLA Modules:
  0.0 120.0 jit_solution(1785608502655283875)
XLA Ops:
  0.0 2.7 %shard_map.64 = (s32[4,512]{1,0:T(4,128)S(1)}, bf16[128,1024]{1,0:T(8,128)(2,1)}, bf16[128,1024]{1,0:T(8,128)(2,1)}, bf16[128,1024]{1,0:T(8,128)(2,1)}, bf16[128,1024]{1,0:T(8,128)(2,1)}) custom-call(s32[1]{0:T(128)} %bitcast.1.place_ref, s32[4,512]{1,0:T(4,128)} %picks_in.1, bf16[512,1024]{1,0:T(8,128)(2,1)} %tokens_ref.1), custom_call_target="tpu_custom_call" | custom-call | flops 1024 | bytes 1024 | tf_op jit(solution)/shard_map/pallas_call | solution.py:104
  2.7 3.1 %collective-permute-start.11 = (bf16[128,1024]{1,0:T(8,128)(2,1)}, bf16[128,1024]{1,0:T(8,128)(2,1)S(1)}, u32[]{:S(2)}, u32[]{:S(2)}) collective-permute-start(bf16[128,1024]{1,0:T(8,128)(2,1)} %get-tuple-element.150), channel_id=1, source_target_pairs={{0,4},{4,8},{8,12},{12,0},{1,5},{5,9},{9,13},{13,1},{2,6},{6,10},{... | collective-permute-start | bytes 786440 | tf_op jit(solution)/shard_map/ppermute | solution.py:447
  5.8 2.6 %collective-permute-start.12 = (bf16[128,1024]{1,0:T(8,128)(2,1)}, bf16[128,1024]{1,0:T(8,128)(2,1)S(1)}, u32[]{:S(2)}, u32[]{:S(2)}) collective-permute-start(bf16[128,1024]{1,0:T(8,128)(2,1)} %get-tuple-element.151), channel_id=1, source_target_pairs={{0,8},{4,12},{8,0},{12,4},{1,9},{5,13},{9,1},{13,5},{2,10},{6,14},... | collective-permute-start | bytes 786440 | tf_op jit(solution)/shard_map/ppermute | solution.py:447
  12.1 14.4 %conditional.3 = (bf16[128,1024]{1,0:T(8,128)(2,1)}, bf16[128,1024]{1,0:T(8,128)(2,1)}, bf16[128,1024]{1,0:T(8,128)(2,1)}, bf16[128,1024]{1,0:T(8,128)(2,1)}, f3...) conditional(s32[]{:T(128)} %convert_element_type.15, () %tuple.41, (s32[4,512]{1,0:T(4,128)S(1)}, ...), branch_computations={%region_3.4_spmd, %region_4.5_spmd} | conditional | flops 10240 | bytes 1073216 | solution.py:505
  12.1 1.8 %branch_1_fun.7 = f32[4,512]{1,0:T(4,128)S(1)} custom-call(bf16[4,1024]{1,0:T(4,128)(2,1)} %get-tuple-element.45.router_ref, bf16[512,1024]{1,0:T(8,128)(2,1)} %get-tuple-element.40.tokens_ref), custom_call_target="tpu_custom_call" | custom-call | flops 1024 | bytes 1024 | tf_op jit(solution)/shard_map/cond/branch_1_fun/pallas_call | solution.py:130
  15.4 2.2 %collective-permute-done.8 = f32[4,512]{1,0:T(4,128)S(1)} collective-permute-done((f32[4,512]{1,0:T(4,128)S(1)}, f32[4,512]{1,0:T(4,128)S(1)}, u32[]{:S(2)}, u32[]{:S(2)}) %collective-permute-start.8) | collective-permute-done | bytes 8224 | tf_op jit(solution)/shard_map/cond/branch_1_fun/ppermute | solution.py:450
  20.0 2.7 %branch_1_fun.6 = (bf16[128,1024]{1,0:T(8,128)(2,1)}, bf16[128,1024]{1,0:T(8,128)(2,1)}, bf16[128,1024]{1,0:T(8,128)(2,1)}, bf16[128,1024]{1,0:T(8,128)(2,1)}) custom-call(s32[4,512]{1,0:T(4,128)S(1)} %get-tuple-element.39.code_ref, bf16[512,1024]{1,0:T(8,128)(2,1)} %get-tuple-element.40.tokens_ref), custom_call_target="tpu_custom_call" | custom-call | flops 1024 | bytes 1024 | tf_op jit(solution)/shard_map/cond/branch_1_fun/pallas_call | solution.py:151
  22.7 3.1 %collective-permute-done.10 = f32[1,4,512]{2,1,0:T(4,128)S(1)} collective-permute-done((f32[1,4,512]{2,1,0:T(4,128)}, f32[1,4,512]{2,1,0:T(4,128)S(1)}, u32[]{:S(2)}, u32[]{:S(2)}) %collective-permute-start.10) | collective-permute-done | bytes 8224 | tf_op jit(solution)/shard_map/cond/branch_1_fun/ppermute | solution.py:466
  31.0 5.3 %collective-permute-start.16 = (bf16[128,1024]{1,0:T(8,128)(2,1)}, bf16[128,1024]{1,0:T(8,128)(2,1)S(1)}, u32[]{:S(2)}, u32[]{:S(2)}) collective-permute-start(bf16[128,1024]{1,0:T(8,128)(2,1)} %get-tuple-element.176), channel_id=1, source_target_pairs={{0,4},{4,8},{8,12},{12,0},{1,5},{5,9},{9,13},{13,1},{2,6},{6,10},{... | collective-permute-start | bytes 786440 | tf_op jit(solution)/shard_map/ppermute | solution.py:447
  40.4 1.8 %shard_map.66 = (f32[256,256]{1,0:T(8,128)S(1)}, f32[256,256]{1,0:T(8,128)S(1)}, bf16[2,1024,256]{2,1,0:T(8,128)(2,1)S(1)}, bf16[2,1024,256]{2,1,0:T(8,128)(2,1)S(1)}) custom-call(s32[4]{0:T(128)S(1)} %pad_add_fusion.order_ref, bf16[1,4096,256]{2,1,0:T(8,128)(2,1)S(1)} %copy-done, bf16[1,4096,256]{2,1,0:T(8,128)(2,1)S(1)} %copy-done.1, ...), custom_call_target="tpu_custom_call" | custom-call | flops 1024 | bytes 1024 | tf_op jit(solution)/shard_map/pallas_call | solution.py:236
  42.2 1.7 %collective-permute-done.14 = bf16[256,1024]{1,0:T(8,128)(2,1)} collective-permute-done((bf16[256,1024]{1,0:T(8,128)(2,1)S(1)}, bf16[256,1024]{1,0:T(8,128)(2,1)}, u32[]{:S(2)}, u32[]{:S(2)}) %collective-permute-start.14) | collective-permute-done | bytes 524320 | tf_op jit(solution)/shard_map/ppermute | solution.py:450
  43.9 11.7 %conditional.4 = (bf16[256,256]{1,0:T(8,128)(2,1)}, bf16[256,256]{1,0:T(8,128)(2,1)}, f32[256,1024]{1,0:T(8,128)S(1)}, bf16[2,256,1024]{2,1,0:T(8,128)(2,1)S(1)}) conditional(s32[]{:T(128)} %convert_element_type.15, () %tuple.43, (bf16[256,1024]{1,0:T(8,128)(2,1)}, f32[256,256]{1,0:T(8,128)S(1)}, f32[256,256]{1,0:T(8,128)S(1)}, ...), branch_computations={%region_5.6_spmd, %region_6.7_spmd} | conditional | flops 2048 | bytes 3672256 | solution.py:524
  43.9 2.1 %collective-permute-done.refs_1_ = bf16[256,1024]{1,0:T(8,128)(2,1)S(1)} collective-permute-done((bf16[256,1024]{1,0:T(8,128)(2,1)}, bf16[256,1024]{1,0:T(8,128)(2,1)S(1)}, u32[]{:S(2)}, u32[]{:S(2)}) %collective-permute-start) | collective-permute-done | bytes 524320 | tf_op jit(solution)/shard_map/cond/branch_1_fun/ppermute | solution.py:450
  46.0 1.8 %branch_1_fun.8.refs_0_ = bf16[256,256]{1,0:T(8,128)(2,1)S(1)} custom-call(f32[256,256]{1,0:T(8,128)S(1)} %get-tuple-element.46.gate_before, f32[256,256]{1,0:T(8,128)S(1)} %get-tuple-element.47.up_before, bf16[2,1024,256]{2,1,0:T(8,128)(2,1)S(1)} %get-tuple-element.48.gate_ref, bf16[2,1024,256]{2,1,0:T(8,128)(2,1)S(1)} %get-tuple-element.49.up_ref, ...), custom_call_target="tpu_custom_call" | custom-call | flops 1024 | bytes 1024 | tf_op jit(solution)/shard_map/cond/branch_1_fun/pallas_call | solution.py:264
  51.1 2.8 %collective-permute-done.1 = bf16[256,256]{1,0:T(8,128)(2,1)} collective-permute-done((bf16[256,256]{1,0:T(8,128)(2,1)S(1)}, bf16[256,256]{1,0:T(8,128)(2,1)}, u32[]{:S(2)}, u32[]{:S(2)}) %collective-permute-start.1) | collective-permute-done | bytes 131104 | tf_op jit(solution)/shard_map/cond/branch_1_fun/ppermute | solution.py:450
  53.9 1.7 %collective-permute-done.3 = bf16[256,256]{1,0:T(8,128)(2,1)} collective-permute-done((bf16[256,256]{1,0:T(8,128)(2,1)}, bf16[256,256]{1,0:T(8,128)(2,1)}, u32[]{:S(2)}, u32[]{:S(2)}) %collective-permute-start.3) | collective-permute-done | bytes 131104 | tf_op jit(solution)/shard_map/cond/branch_1_fun/ppermute | solution.py:450
  55.7 2.1 %shard_map.67.refs_0_ = bf16[256,1024]{1,0:T(8,128)(2,1)S(1)} custom-call(s32[2,4]{1,0:T(2,128)S(1)} %get-tuple-element.228.offset_ref, s32[2,4]{1,0:T(2,128)S(1)} %get-tuple-element.229.count_ref, bf16[128,1024]{1,0:T(8,128)(2,1)S(1)} %copy-done.8, bf16[128,1024]{1,0:T(8,128)(2,1)S(1)} %collective-permute-done.16.refs_1_, ...), custom_call_target="tpu_custom_call" | custom-call | flops 1024 | bytes 1024 | tf_op jit(solution)/shard_map/pallas_call | solution.py:188
  59.4 4.4 %collective-permute-start.19 = (f32[2,4,512]{2,1,0:T(4,128)S(1)}, f32[2,4,512]{2,1,0:T(4,128)S(1)}, u32[]{:S(2)}, u32[]{:S(2)}) collective-permute-start(f32[2,4,512]{2,1,0:T(4,128)S(1)} %get-tuple-element.191), channel_id=1, source_target_pairs={{0,8},{4,12},{8,0},{12,4},{1,9},{5,13},{9,1},{13,5},{2,10},{6,14},... | collective-permute-start | bytes 49160 | tf_op jit(solution)/shard_map/ppermute | solution.py:466
  63.8 3.1 %shard_map.68 = (bf16[128,1024]{1,0:T(8,128)(2,1)S(1)}, bf16[128,1024]{1,0:T(8,128)(2,1)}, bf16[128,1024]{1,0:T(8,128)(2,1)}, bf16[128,1024]{1,0:T(8,128)(2,1)}) custom-call(s32[2,4]{1,0:T(2,128)S(1)} %get-tuple-element.228.offset_ref, s32[2,4]{1,0:T(2,128)S(1)} %get-tuple-element.229.count_ref, f32[256,1024]{1,0:T(8,128)S(1)} %get-tuple-element.183.before_ref, ...), custom_call_target="tpu_custom_call" | custom-call | flops 1024 | bytes 1024 | tf_op jit(solution)/shard_map/pallas_call | solution.py:345
  66.9 3.5 %collective-permute-start.22 = (bf16[128,1024]{1,0:T(8,128)(2,1)}, bf16[128,1024]{1,0:T(8,128)(2,1)}, u32[]{:S(2)}, u32[]{:S(2)}) collective-permute-start(bf16[128,1024]{1,0:T(8,128)(2,1)} %get-tuple-element.194), channel_id=1, source_target_pairs={{0,12},{4,0},{8,4},{12,8},{1,13},{5,1},{9,5},{13,9},{2,14},{6,2},{... | collective-permute-start | bytes 786440 | tf_op jit(solution)/shard_map/ppermute | solution.py:447
  73.4 1.8 %shard_map.70 = (f32[256,256]{1,0:T(8,128)S(1)}, f32[256,256]{1,0:T(8,128)S(1)}, bf16[2,1024,256]{2,1,0:T(8,128)(2,1)S(1)}, bf16[2,1024,256]{2,1,0:T(8,128)(2,1)S(1)}) custom-call(s32[4]{0:T(128)S(1)} %pad_add_fusion.order_ref, bf16[1,4096,256]{2,1,0:T(8,128)(2,1)S(1)} %copy-done, bf16[1,4096,256]{2,1,0:T(8,128)(2,1)S(1)} %copy-done.2, ...), custom_call_target="tpu_custom_call" | custom-call | flops 1024 | bytes 1024 | tf_op jit(solution)/shard_map/pallas_call | solution.py:236
  75.2 11.8 %conditional.5 = (bf16[256,256]{1,0:T(8,128)(2,1)}, bf16[256,256]{1,0:T(8,128)(2,1)}, f32[256,1024]{1,0:T(8,128)S(1)}, bf16[2,256,1024]{2,1,0:T(8,128)(2,1)S(1)}) conditional(s32[]{:T(128)} %convert_element_type.16, () %tuple.52, (bf16[256,1024]{1,0:T(8,128)(2,1)}, f32[256,256]{1,0:T(8,128)S(1)}, f32[256,256]{1,0:T(8,128)S(1)}, ...), branch_computations={%region_8.9_spmd, %region_9.10_spmd} | conditional | flops 2048 | bytes 3672256 | solution.py:524
  75.3 2.1 %collective-permute-done.4.refs_1_ = bf16[256,1024]{1,0:T(8,128)(2,1)S(1)} collective-permute-done((bf16[256,1024]{1,0:T(8,128)(2,1)}, bf16[256,1024]{1,0:T(8,128)(2,1)S(1)}, u32[]{:S(2)}, u32[]{:S(2)}) %collective-permute-start.4) | collective-permute-done | bytes 524320 | tf_op jit(solution)/shard_map/cond/branch_1_fun/ppermute | solution.py:450
  77.5 1.8 %branch_1_fun.10.refs_0_ = bf16[256,256]{1,0:T(8,128)(2,1)S(1)} custom-call(f32[256,256]{1,0:T(8,128)S(1)} %get-tuple-element.58.gate_before, f32[256,256]{1,0:T(8,128)S(1)} %get-tuple-element.59.up_before, bf16[2,1024,256]{2,1,0:T(8,128)(2,1)S(1)} %get-tuple-element.60.gate_ref, bf16[2,1024,256]{2,1,0:T(8,128)(2,1)S(1)} %get-tuple-element.61.up_ref, ...), custom_call_target="tpu_custom_call" | custom-call | flops 1024 | bytes 1024 | tf_op jit(solution)/shard_map/cond/branch_1_fun/pallas_call | solution.py:264
  82.2 3.1 %collective-permute-done.5 = bf16[256,256]{1,0:T(8,128)(2,1)} collective-permute-done((bf16[256,256]{1,0:T(8,128)(2,1)S(1)}, bf16[256,256]{1,0:T(8,128)(2,1)}, u32[]{:S(2)}, u32[]{:S(2)}) %collective-permute-start.5) | collective-permute-done | bytes 131104 | tf_op jit(solution)/shard_map/cond/branch_1_fun/ppermute | solution.py:450
  85.3 1.7 %collective-permute-done.7 = bf16[256,256]{1,0:T(8,128)(2,1)} collective-permute-done((bf16[256,256]{1,0:T(8,128)(2,1)}, bf16[256,256]{1,0:T(8,128)(2,1)}, u32[]{:S(2)}, u32[]{:S(2)}) %collective-permute-start.7) | collective-permute-done | bytes 131104 | tf_op jit(solution)/shard_map/cond/branch_1_fun/ppermute | solution.py:450
  87.0 2.4 %shard_map.71 = (bf16[128,1024]{1,0:T(8,128)(2,1)S(1)}, bf16[128,1024]{1,0:T(8,128)(2,1)S(1)}, bf16[128,1024]{1,0:T(8,128)(2,1)S(1)}, bf16[128,1024]{1,0:T(8,128)(2,1)S(1)}) custom-call(s32[2,4]{1,0:T(2,128)S(1)} %get-tuple-element.228.offset_ref, s32[2,4]{1,0:T(2,128)S(1)} %get-tuple-element.229.count_ref, f32[256,1024]{1,0:T(8,128)S(1)} %get-tuple-element.208.before_ref, ...), custom_call_target="tpu_custom_call" | custom-call | flops 1024 | bytes 1024 | tf_op jit(solution)/shard_map/pallas_call | solution.py:345
  89.4 4.7 %collective-permute-done.23.refs_2_ = bf16[128,1024]{1,0:T(8,128)(2,1)} collective-permute-done((bf16[128,1024]{1,0:T(8,128)(2,1)}, bf16[128,1024]{1,0:T(8,128)(2,1)}, u32[]{:S(2)}, u32[]{:S(2)}) %collective-permute-start.23) | collective-permute-done | bytes 262176 | tf_op jit(solution)/shard_map/ppermute | solution.py:447
  95.6 2.0 %collective-permute-start.27 = (bf16[128,1024]{1,0:T(8,128)(2,1)S(1)}, bf16[128,1024]{1,0:T(8,128)(2,1)S(1)}, u32[]{:S(2)}, u32[]{:S(2)}) collective-permute-start(bf16[128,1024]{1,0:T(8,128)(2,1)S(1)} %get-tuple-element.223), channel_id=1, source_target_pairs={{0,4},{4,8},{8,12},{12,0},{1,5},{5,9},{9,13},{13,1},{2,6},{6,10},{... | collective-permute-start | bytes 786440 | tf_op jit(solution)/shard_map/ppermute | solution.py:447
  98.7 1.9 %shard_map.72.refs_0_ = f32[512,1024]{1,0:T(8,128)S(1)} custom-call(s32[4,512]{1,0:T(4,128)S(1)} %get-tuple-element.147.code_ref, f32[4,512]{1,0:T(4,128)S(1)} %shard_map.69.weight_ref, bf16[128,1024]{1,0:T(8,128)(2,1)S(1)} %get-tuple-element.216.refs_0_, bf16[128,1024]{1,0:T(8,128)(2,1)} %collective-permute-done.22.refs_1_, ...), custom_call_target="tpu_custom_call" | custom-call | flops 1024 | bytes 1024 | tf_op jit(solution)/shard_map/pallas_call | solution.py:420
  102.1 16.0 %collective-permute-done.26.refs_3_ = bf16[128,1024]{1,0:T(8,128)(2,1)S(1)} collective-permute-done((bf16[128,1024]{1,0:T(8,128)(2,1)S(1)}, bf16[128,1024]{1,0:T(8,128)(2,1)S(1)}, u32[]{:S(2)}, u32[]{:S(2)}) %collective-permute-start.26) | collective-permute-done | bytes 262176 | tf_op jit(solution)/shard_map/ppermute | solution.py:447
  118.0 1.9 %shard_map.73 = bf16[512,1024]{1,0:T(8,128)(2,1)} custom-call(s32[4,512]{1,0:T(4,128)S(1)} %get-tuple-element.147.code_ref, f32[4,512]{1,0:T(4,128)S(1)} %shard_map.69.weight_ref, f32[512,1024]{1,0:T(8,128)S(1)} %shard_map.72.refs_0_, bf16[128,1024]{1,0:T(8,128)(2,1)S(1)} %get-tuple-element.220.refs_1_, ...), custom_call_target="tpu_custom_call" | custom-call | flops 1024 | bytes 1024 | tf_op jit(solution)/shard_map/pallas_call | solution.py:420
  (73 shorter events, 30.5 us)
Async XLA Ops:
  2.7 24.5 %copy-start.3 = (bf16[128,1024]{1,0:T(8,128)(2,1)S(1)}, bf16[128,1024]{1,0:T(8,128)(2,1)}, u32[]{:S(2)}) copy-start(bf16[128,1024]{1,0:T(8,128)(2,1)} %get-tuple-element.154.refs_0_) | copy-start | bytes 786436
  2.7 23.8 %collective-permute-start.11 = (bf16[128,1024]{1,0:T(8,128)(2,1)}, bf16[128,1024]{1,0:T(8,128)(2,1)S(1)}, u32[]{:S(2)}, u32[]{:S(2)}) collective-permute-start(bf16[128,1024]{1,0:T(8,128)(2,1)} %get-tuple-element.150), channel_id=1, source_target_pairs={{0,4},{4,8},{8,12},{12,0},{1,5},{5,9},{9,13},{13,1},{2,6},{6,10},{... | collective-permute-start | bytes 786440 | tf_op jit(solution)/shard_map/ppermute | solution.py:447
  5.8 20.7 %collective-permute-start.12 = (bf16[128,1024]{1,0:T(8,128)(2,1)}, bf16[128,1024]{1,0:T(8,128)(2,1)S(1)}, u32[]{:S(2)}, u32[]{:S(2)}) collective-permute-start(bf16[128,1024]{1,0:T(8,128)(2,1)} %get-tuple-element.151), channel_id=1, source_target_pairs={{0,8},{4,12},{8,0},{12,4},{1,9},{5,13},{9,1},{13,5},{2,10},{6,14},... | collective-permute-start | bytes 786440 | tf_op jit(solution)/shard_map/ppermute | solution.py:447
  8.4 18.1 %collective-permute-start.13 = (bf16[128,1024]{1,0:T(8,128)(2,1)}, bf16[128,1024]{1,0:T(8,128)(2,1)S(1)}, u32[]{:S(2)}, u32[]{:S(2)}) collective-permute-start(bf16[128,1024]{1,0:T(8,128)(2,1)} %get-tuple-element.152), channel_id=1, source_target_pairs={{0,12},{4,0},{8,4},{12,8},{1,13},{5,1},{9,5},{13,9},{2,14},{6,2},{... | collective-permute-start | bytes 786440 | tf_op jit(solution)/shard_map/ppermute | solution.py:447
  12.1 26.7 %copy-start = (bf16[1,4096,256]{2,1,0:T(8,128)(2,1)S(1)}, bf16[1,4096,256]{2,1,0:T(8,128)(2,1)}, u32[]{:S(2)}) copy-start(bf16[1,4096,256]{2,1,0:T(8,128)(2,1)} %gate_ref.3) | copy-start | bytes 6291460
  13.9 3.7 %collective-permute-start.8 = (f32[4,512]{1,0:T(4,128)S(1)}, f32[4,512]{1,0:T(4,128)S(1)}, u32[]{:S(2)}, u32[]{:S(2)}) collective-permute-start(f32[4,512]{1,0:T(4,128)S(1)} %branch_1_fun.7), channel_id=1, source_target_pairs={{0,2},{1,3},{2,0},{3,1},{4,6},{5,7},{6,4},{7,5},{8,10},{9,11},{10,... | collective-permute-start | bytes 24584 | tf_op jit(solution)/shard_map/cond/branch_1_fun/ppermute | solution.py:450
  17.5 1.2 collective-permute-start.9
  19.3 6.5 %collective-permute-start.10 = (f32[1,4,512]{2,1,0:T(4,128)}, f32[1,4,512]{2,1,0:T(4,128)S(1)}, u32[]{:S(2)}, u32[]{:S(2)}) collective-permute-start(f32[1,4,512]{2,1,0:T(4,128)} %bitcast), channel_id=1, source_target_pairs={{0,4},{4,0},{8,12},{12,8},{1,5},{5,1},{9,13},{13,9},{2,6},{6,2},{1... | collective-permute-start | bytes 24584 | tf_op jit(solution)/shard_map/cond/branch_1_fun/ppermute | solution.py:466
  29.4 9.4 %collective-permute-start.15 = (bf16[256,1024]{1,0:T(8,128)(2,1)S(1)}, bf16[256,1024]{1,0:T(8,128)(2,1)S(1)}, u32[]{:S(2)}, u32[]{:S(2)}) collective-permute-start(bf16[256,1024]{1,0:T(8,128)(2,1)S(1)} %shard_map.65.refs_0_), channel_id=1, source_target_pairs={{0,1},{1,0},{2,3},{3,2},{4,5},{5,4},{6,7},{7,6},{8,9},{9,8},{10,11... | collective-permute-start | bytes 1572872 | tf_op jit(solution)/shard_map/ppermute | solution.py:450
  29.4 14.4 %collective-permute-start.14 = (bf16[256,1024]{1,0:T(8,128)(2,1)S(1)}, bf16[256,1024]{1,0:T(8,128)(2,1)}, u32[]{:S(2)}, u32[]{:S(2)}) collective-permute-start(bf16[256,1024]{1,0:T(8,128)(2,1)S(1)} %shard_map.65.refs_0_), channel_id=1, source_target_pairs={{0,2},{1,3},{2,0},{3,1},{4,6},{5,7},{6,4},{7,5},{8,10},{9,11},{10,... | collective-permute-start | bytes 1572872 | tf_op jit(solution)/shard_map/ppermute | solution.py:450
  31.0 24.6 %collective-permute-start.16 = (bf16[128,1024]{1,0:T(8,128)(2,1)}, bf16[128,1024]{1,0:T(8,128)(2,1)S(1)}, u32[]{:S(2)}, u32[]{:S(2)}) collective-permute-start(bf16[128,1024]{1,0:T(8,128)(2,1)} %get-tuple-element.176), channel_id=1, source_target_pairs={{0,4},{4,8},{8,12},{12,0},{1,5},{5,9},{9,13},{13,1},{2,6},{6,10},{... | collective-permute-start | bytes 786440 | tf_op jit(solution)/shard_map/ppermute | solution.py:447
  36.3 19.3 %collective-permute-start.17 = (bf16[128,1024]{1,0:T(8,128)(2,1)}, bf16[128,1024]{1,0:T(8,128)(2,1)}, u32[]{:S(2)}, u32[]{:S(2)}) collective-permute-start(bf16[128,1024]{1,0:T(8,128)(2,1)} %get-tuple-element.177), channel_id=1, source_target_pairs={{0,8},{4,12},{8,0},{12,4},{1,9},{5,13},{9,1},{13,5},{2,10},{6,14},... | collective-permute-start | bytes 786440 | tf_op jit(solution)/shard_map/ppermute | solution.py:447
  37.9 17.8 %collective-permute-start.18 = (bf16[128,1024]{1,0:T(8,128)(2,1)}, bf16[128,1024]{1,0:T(8,128)(2,1)}, u32[]{:S(2)}, u32[]{:S(2)}) collective-permute-start(bf16[128,1024]{1,0:T(8,128)(2,1)} %get-tuple-element.178), channel_id=1, source_target_pairs={{0,12},{4,0},{8,4},{12,8},{1,13},{5,1},{9,5},{13,9},{2,14},{6,2},{... | collective-permute-start | bytes 786440 | tf_op jit(solution)/shard_map/ppermute | solution.py:447
  40.4 3.5 %copy-start.6 = (bf16[1,1024,1024]{2,1,0:T(8,128)(2,1)S(1)}, bf16[1,1024,1024]{2,1,0:T(8,128)(2,1)}, u32[]{:S(2)}) copy-start(bf16[1,1024,1024]{2,1,0:T(8,128)(2,1)} %param.16) | copy-start | bytes 6291460
  43.9 11.8 %copy-start.8 = (bf16[128,1024]{1,0:T(8,128)(2,1)S(1)}, bf16[128,1024]{1,0:T(8,128)(2,1)}, u32[]{:S(2)}) copy-start(bf16[128,1024]{1,0:T(8,128)(2,1)} %get-tuple-element.179.refs_0_) | copy-start | bytes 786436
  43.9 2.1 %collective-permute-start = (bf16[256,1024]{1,0:T(8,128)(2,1)}, bf16[256,1024]{1,0:T(8,128)(2,1)S(1)}, u32[]{:S(2)}, u32[]{:S(2)}) collective-permute-start(bf16[256,1024]{1,0:T(8,128)(2,1)} %get-tuple-element.50.refs_0_), channel_id=1, source_target_pairs={{0,1},{1,0},{2,3},{3,2},{4,5},{5,4},{6,7},{7,6},{8,9},{9,8},{10,11... | collective-permute-start | bytes 1572872 | tf_op jit(solution)/shard_map/cond/branch_1_fun/ppermute | solution.py:450
  47.8 1.7 %collective-permute-start.2 = (bf16[256,256]{1,0:T(8,128)(2,1)S(1)}, bf16[256,256]{1,0:T(8,128)(2,1)S(1)}, u32[]{:S(2)}, u32[]{:S(2)}) collective-permute-start(bf16[256,256]{1,0:T(8,128)(2,1)S(1)} %branch_1_fun.8.refs_0_), channel_id=1, source_target_pairs={{0,1},{1,0},{2,3},{3,2},{4,5},{5,4},{6,7},{7,6},{8,9},{9,8},{10,11... | collective-permute-start | bytes 393224 | tf_op jit(solution)/shard_map/cond/branch_1_fun/ppermute | solution.py:450
  48.0 5.9 %collective-permute-start.1 = (bf16[256,256]{1,0:T(8,128)(2,1)S(1)}, bf16[256,256]{1,0:T(8,128)(2,1)}, u32[]{:S(2)}, u32[]{:S(2)}) collective-permute-start(bf16[256,256]{1,0:T(8,128)(2,1)S(1)} %branch_1_fun.8.refs_0_), channel_id=1, source_target_pairs={{0,2},{1,3},{2,0},{3,1},{4,6},{5,7},{6,4},{7,5},{8,10},{9,11},{10,... | collective-permute-start | bytes 393224 | tf_op jit(solution)/shard_map/cond/branch_1_fun/ppermute | solution.py:450
  53.9 1.7 %collective-permute-start.3 = (bf16[256,256]{1,0:T(8,128)(2,1)}, bf16[256,256]{1,0:T(8,128)(2,1)}, u32[]{:S(2)}, u32[]{:S(2)}) collective-permute-start(bf16[256,256]{1,0:T(8,128)(2,1)} %collective-permute-done.1), channel_id=1, source_target_pairs={{0,1},{1,0},{2,3},{3,2},{4,5},{5,4},{6,7},{7,6},{8,9},{9,8},{10,11... | collective-permute-start | bytes 393224 | tf_op jit(solution)/shard_map/cond/branch_1_fun/ppermute | solution.py:450
  57.8 14.0 %collective-permute-start.21 = (bf16[256,1024]{1,0:T(8,128)(2,1)S(1)}, bf16[256,1024]{1,0:T(8,128)(2,1)S(1)}, u32[]{:S(2)}, u32[]{:S(2)}) collective-permute-start(bf16[256,1024]{1,0:T(8,128)(2,1)S(1)} %shard_map.67.refs_0_), channel_id=1, source_target_pairs={{0,1},{1,0},{2,3},{3,2},{4,5},{5,4},{6,7},{7,6},{8,9},{9,8},{10,11... | collective-permute-start | bytes 1572872 | tf_op jit(solution)/shard_map/ppermute | solution.py:450
  57.9 17.3 %collective-permute-start.20 = (bf16[256,1024]{1,0:T(8,128)(2,1)S(1)}, bf16[256,1024]{1,0:T(8,128)(2,1)}, u32[]{:S(2)}, u32[]{:S(2)}) collective-permute-start(bf16[256,1024]{1,0:T(8,128)(2,1)S(1)} %shard_map.67.refs_0_), channel_id=1, source_target_pairs={{0,2},{1,3},{2,0},{3,1},{4,6},{5,7},{6,4},{7,5},{8,10},{9,11},{10,... | collective-permute-start | bytes 1572872 | tf_op jit(solution)/shard_map/ppermute | solution.py:450
  59.4 7.5 %collective-permute-start.19 = (f32[2,4,512]{2,1,0:T(4,128)S(1)}, f32[2,4,512]{2,1,0:T(4,128)S(1)}, u32[]{:S(2)}, u32[]{:S(2)}) collective-permute-start(f32[2,4,512]{2,1,0:T(4,128)S(1)} %get-tuple-element.191), channel_id=1, source_target_pairs={{0,8},{4,12},{8,0},{12,4},{1,9},{5,13},{9,1},{13,5},{2,10},{6,14},... | collective-permute-start | bytes 49160 | tf_op jit(solution)/shard_map/ppermute | solution.py:466
  66.9 22.4 %collective-permute-start.22 = (bf16[128,1024]{1,0:T(8,128)(2,1)}, bf16[128,1024]{1,0:T(8,128)(2,1)}, u32[]{:S(2)}, u32[]{:S(2)}) collective-permute-start(bf16[128,1024]{1,0:T(8,128)(2,1)} %get-tuple-element.194), channel_id=1, source_target_pairs={{0,12},{4,0},{8,4},{12,8},{1,13},{5,1},{9,5},{13,9},{2,14},{6,2},{... | collective-permute-start | bytes 786440 | tf_op jit(solution)/shard_map/ppermute | solution.py:447
  70.4 23.7 %collective-permute-start.23 = (bf16[128,1024]{1,0:T(8,128)(2,1)}, bf16[128,1024]{1,0:T(8,128)(2,1)}, u32[]{:S(2)}, u32[]{:S(2)}) collective-permute-start(bf16[128,1024]{1,0:T(8,128)(2,1)} %get-tuple-element.195), channel_id=1, source_target_pairs={{0,8},{4,12},{8,0},{12,4},{1,9},{5,13},{9,1},{13,5},{2,10},{6,14},... | collective-permute-start | bytes 786440 | tf_op jit(solution)/shard_map/ppermute | solution.py:447
  71.0 23.1 %collective-permute-start.24 = (bf16[128,1024]{1,0:T(8,128)(2,1)}, bf16[128,1024]{1,0:T(8,128)(2,1)}, u32[]{:S(2)}, u32[]{:S(2)}) collective-permute-start(bf16[128,1024]{1,0:T(8,128)(2,1)} %get-tuple-element.196), channel_id=1, source_target_pairs={{0,4},{4,8},{8,12},{12,0},{1,5},{5,9},{9,13},{13,1},{2,6},{6,10},{... | collective-permute-start | bytes 786440 | tf_op jit(solution)/shard_map/ppermute | solution.py:447
  75.3 2.2 %collective-permute-start.4 = (bf16[256,1024]{1,0:T(8,128)(2,1)}, bf16[256,1024]{1,0:T(8,128)(2,1)S(1)}, u32[]{:S(2)}, u32[]{:S(2)}) collective-permute-start(bf16[256,1024]{1,0:T(8,128)(2,1)} %get-tuple-element.62.refs_0_), channel_id=1, source_target_pairs={{0,1},{1,0},{2,3},{3,2},{4,5},{5,4},{6,7},{7,6},{8,9},{9,8},{10,11... | collective-permute-start | bytes 1572872 | tf_op jit(solution)/shard_map/cond/branch_1_fun/ppermute | solution.py:450
  79.2 1.4 %collective-permute-start.6 = (bf16[256,256]{1,0:T(8,128)(2,1)S(1)}, bf16[256,256]{1,0:T(8,128)(2,1)S(1)}, u32[]{:S(2)}, u32[]{:S(2)}) collective-permute-start(bf16[256,256]{1,0:T(8,128)(2,1)S(1)} %branch_1_fun.10.refs_0_), channel_id=1, source_target_pairs={{0,1},{1,0},{2,3},{3,2},{4,5},{5,4},{6,7},{7,6},{8,9},{9,8},{10,11... | collective-permute-start | bytes 393224 | tf_op jit(solution)/shard_map/cond/branch_1_fun/ppermute | solution.py:450
  79.4 5.9 %collective-permute-start.5 = (bf16[256,256]{1,0:T(8,128)(2,1)S(1)}, bf16[256,256]{1,0:T(8,128)(2,1)}, u32[]{:S(2)}, u32[]{:S(2)}) collective-permute-start(bf16[256,256]{1,0:T(8,128)(2,1)S(1)} %branch_1_fun.10.refs_0_), channel_id=1, source_target_pairs={{0,2},{1,3},{2,0},{3,1},{4,6},{5,7},{6,4},{7,5},{8,10},{9,11},{10,... | collective-permute-start | bytes 393224 | tf_op jit(solution)/shard_map/cond/branch_1_fun/ppermute | solution.py:450
  85.3 1.7 %collective-permute-start.7 = (bf16[256,256]{1,0:T(8,128)(2,1)}, bf16[256,256]{1,0:T(8,128)(2,1)}, u32[]{:S(2)}, u32[]{:S(2)}) collective-permute-start(bf16[256,256]{1,0:T(8,128)(2,1)} %collective-permute-done.5), channel_id=1, source_target_pairs={{0,1},{1,0},{2,3},{3,2},{4,5},{5,4},{6,7},{7,6},{8,9},{9,8},{10,11... | collective-permute-start | bytes 393224 | tf_op jit(solution)/shard_map/cond/branch_1_fun/ppermute | solution.py:450
  94.1 8.0 %collective-permute-start.25 = (bf16[128,1024]{1,0:T(8,128)(2,1)S(1)}, bf16[128,1024]{1,0:T(8,128)(2,1)S(1)}, u32[]{:S(2)}, u32[]{:S(2)}) collective-permute-start(bf16[128,1024]{1,0:T(8,128)(2,1)S(1)} %get-tuple-element.221), channel_id=1, source_target_pairs={{0,12},{4,0},{8,4},{12,8},{1,13},{5,1},{9,5},{13,9},{2,14},{6,2},{... | collective-permute-start | bytes 786440 | tf_op jit(solution)/shard_map/ppermute | solution.py:447
  94.1 23.9 %collective-permute-start.26 = (bf16[128,1024]{1,0:T(8,128)(2,1)S(1)}, bf16[128,1024]{1,0:T(8,128)(2,1)S(1)}, u32[]{:S(2)}, u32[]{:S(2)}) collective-permute-start(bf16[128,1024]{1,0:T(8,128)(2,1)S(1)} %get-tuple-element.222), channel_id=1, source_target_pairs={{0,8},{4,12},{8,0},{12,4},{1,9},{5,13},{9,1},{13,5},{2,10},{6,14},... | collective-permute-start | bytes 786440 | tf_op jit(solution)/shard_map/ppermute | solution.py:447
  95.6 22.5 %collective-permute-start.27 = (bf16[128,1024]{1,0:T(8,128)(2,1)S(1)}, bf16[128,1024]{1,0:T(8,128)(2,1)S(1)}, u32[]{:S(2)}, u32[]{:S(2)}) collective-permute-start(bf16[128,1024]{1,0:T(8,128)(2,1)S(1)} %get-tuple-element.223), channel_id=1, source_target_pairs={{0,4},{4,8},{8,12},{12,0},{1,5},{5,9},{9,13},{13,1},{2,6},{6,10},{... | collective-permute-start | bytes 786440 | tf_op jit(solution)/shard_map/ppermute | solution.py:447
  (5 other events, 6.7 us)

commit v10 on v9

--- a/solution.py
+++ b/solution.py
@@ -317,9 +317,9 @@
     )(order, down_weight, *hs)
 
 
-def down_last_kernel(parts, experts, k, offset_ref, count_ref, before_ref, down_ref, *refs):
+def down_last_kernel(parts, experts, k, direct, offset_ref, count_ref, before_ref, down_ref, *refs):
     hs, outs = refs[:parts], refs[parts : parts + experts]
-    h_held, sems = refs[parts + experts :]
+    h_held, sems, *staged = refs[parts + experts :]
     loads = start_all(hs, [h_held.at[i] for i in range(parts)], sems)
     size = hs[0].shape[0]
     depth = outs[0].shape[0]
@@ -334,20 +334,32 @@
         loads[i].wait()
         total = total + dot(h_held[i], down_ref[i])
     result = total.astype(BF16)
-    for i in range(experts):
-        outs[i][...] = dot(picks[i], result).astype(BF16)
-
-
-def down_last(offsets, counts, k, hs, before, experts, depth):
+    if direct:
+        for i in range(experts):
+            outs[i][...] = dot(picks[i], result).astype(BF16)
+        return
+    staged_ref, out_sems = staged
+    copies = []
+    for i in list(range(1, experts)) + [0]:
+        staged_ref[i] = dot(picks[i], result).astype(BF16)
+        copy = pltpu.make_async_copy(staged_ref.at[i], outs[i], out_sems.at[i])
+        copy.start()
+        copies.append(copy)
+    for copy in copies:
+        copy.wait()
+
+
+def down_last(offsets, counts, k, hs, before, experts, depth, direct):
     parts = len(hs)
     size, units = hs[0].shape
     width = before[0].shape[1]
     return pl.pallas_call(
-        functools.partial(down_last_kernel, parts, experts, k),
+        functools.partial(down_last_kernel, parts, experts, k, direct),
         out_shape=[jax.ShapeDtypeStruct((depth, width), BF16)] * experts,
         in_specs=[smem()] * 2 + whole(2) + apart(parts),
-        out_specs=whole(experts),
-        scratch_shapes=[pltpu.VMEM((parts, size, units), BF16), pltpu.SemaphoreType.DMA((parts,))],
+        out_specs=whole(experts) if direct else apart(experts),
+        scratch_shapes=[pltpu.VMEM((parts, size, units), BF16), pltpu.SemaphoreType.DMA((parts,))]
+        + ([] if direct else [pltpu.VMEM((experts, depth, width), BF16), pltpu.SemaphoreType.DMA((experts,))]),
         compiler_params=params(),
         cost_estimate=COST,
     )(offsets, counts, *before, *hs)
@@ -514,7 +526,7 @@
 
     def settle(k, far, partial):
         return tuple(
-            down_last(offsets, counts, k, far, partial, experts, depth)
+            down_last(offsets, counts, k, far, partial, experts, depth, k == BATCHES - 1)
         )
 
     def fenced(k, run, *operands):
@@ -534,27 +546,28 @@
         if k < BATCHES - 1:
             moving = after(later[k], blocks)
             arrived.append([moving[0]] + [along_expert(moving[shift], shift) for shift in range(1, experts)])
-        block = compact(offsets, counts, k, blocks, size)
+        if k == 0:
+            block = fenced(k, lambda *blocks: compact(offsets, counts, 0, blocks, size), *blocks)
+        else:
+            block = compact(offsets, counts, k, blocks, size)
         across = swap(block, bits[0])
         near = spread(block)
-        if k == 1:
-            gathered = after(gathered, blocks)
-            gathered = jnp.concatenate([gathered, swap_expert(gathered, expert_bits[-1])])
         if k > 0:
             far, partial = after((far, partial), block)
             results = settle(k - 1, far, partial)
-            if k == 1:
-                results, gathered = lax.optimization_barrier((results, gathered))
             if k > 1:
                 results, waiting[k - 2] = lax.optimization_barrier((results, waiting[k - 2]))
             waiting.append(send_back(results))
             near = after(near, results)
         sums = gate_up_near(order, near_places, far_places, gate_weight, up_weight, near)
         across, sums = lax.optimization_barrier((across, sums))
+        if k == BATCHES - 1:
+            gathered = after(gathered, sums)
+            gathered = jnp.concatenate([gathered, swap_expert(gathered, expert_bits[-1])])
         far, partial = fenced(k, far_half, across, sums)
         moved = partial
     results = settle(BATCHES - 1, far, partial)
-    results, waiting[-1] = lax.optimization_barrier((results, waiting[-1]))
+    results, gathered, waiting[-1] = lax.optimization_barrier((results, gathered, waiting[-1]))
     waiting.append(send_back(results))
     weights = slot_weights(place, logits, gathered, code)
     total = None

time: 121 us -> 120 us (level)
  waiting for transfers between devices: 44 us -> 41.6 us
  starting transfers between devices: 35.3 us -> 37.3 us
  local copies, waits for them, and re-layouts: 5.54 us -> 3.89 us
  Pallas kernels: 31.1 us -> 32.4 us
    ppermute x12, waiting for transfers between devices: 22.3 us -> 18.1 us  [along_expert(): lax.ppermute(x, 'expert', [(i, (i + shift) % experts) for i in range(expe...]
    ppermute x12, starting transfers between devices: 22.3 us -> 25.5 us  [along_expert(): lax.ppermute(x, 'expert', [(i, (i + shift) % experts) for i in range(expe...]
    ppermute x2, waiting for transfers between devices: 3.14 us -> 5.12 us  [swap_expert(): return lax.ppermute(x, 'expert', [(i, i ^ bit) for i in range(experts)])]
    unnamed x18 -> x10, local copies, waits for them, and re-layouts: 4.84 us -> 3.19 us
  transfers between devices with their start and end apart: 28 -> 28, of which waited for: 15 -> 14; matrix products, arithmetic and copies ran while one was open for 3% -> 3% of each run, Pallas kernels for 19% -> 20%
where the time goes in v10:
time: 120 us; the launch traced here: 119 us
  waiting for transfers between devices  41.6 us (35%)
  starting transfers between devices  37.3 us (31%)
  Pallas kernels  32.4 us (27%)
  local copies, waits for them, and re-layouts  3.89 us (3%)
  other arithmetic  2.3 us (2%)
  between operations  1.5 us (1%)
    ppermute x12, starting transfers between devices, along_expert(): lax.ppermute(x, 'expert', [(i, (i + shift) % experts) for i in range(expe...  25.5 us
    ppermute x14, waiting for transfers between devices, swap(): return lax.ppermute(x, 'dp', [(i, i ^ bit) for i in range(width_parts)])  18.4 us
    ppermute x12, waiting for transfers between devices, along_expert(): lax.ppermute(x, 'expert', [(i, (i + shift) % experts) for i in range(expe...  18.1 us
    ppermute x14, starting transfers between devices, swap(): return lax.ppermute(x, 'dp', [(i, i ^ bit) for i in range(width_parts)])  7.67 us
    pallas_call x2, Pallas kernels, down_last(): pl.pallas_call(functools.partial(down_last_kernel, parts, experts, k, dir...  5.47 us
    ppermute x2, waiting for transfers between devices, swap_expert(): return lax.ppermute(x, 'expert', [(i, i ^ bit) for i in range(experts)])  5.12 us
    pallas_call x2, Pallas kernels, gate_up_near(): pl.pallas_call(functools.partial(gate_up_near_kernel, parts, near, far),...  4.4 us
    ppermute x2, starting transfers between devices, swap_expert(): return lax.ppermute(x, 'expert', [(i, i ^ bit) for i in range(experts)])  4.13 us
  transfers between devices with their start and end apart: 28, of which 14 were waited for; matrix products, arithmetic and copies ran while one was open for 3% of the time, Pallas kernels for 20%

profile of v10, /device:TPU:0, one launch (start us, length us, event | category | flops | bytes accessed | tf_op | source)
XLA Modules:
  0.0 119.1 jit_solution(5755617448442851463)
XLA Ops:
  0.0 2.6 %shard_map.64 = (s32[4,512]{1,0:T(4,128)S(1)}, bf16[128,1024]{1,0:T(8,128)(2,1)S(1)}, bf16[128,1024]{1,0:T(8,128)(2,1)}, bf16[128,1024]{1,0:T(8,128)(2,1)}, bf16[128,1024]{1,0:T(8,128)(2,1)}) custom-call(s32[1]{0:T(128)} %bitcast.1.place_ref, s32[4,512]{1,0:T(4,128)} %picks_in.1, bf16[512,1024]{1,0:T(8,128)(2,1)} %tokens_ref.1), custom_call_target="tpu_custom_call" | custom-call | flops 1024 | bytes 1024 | tf_op jit(solution)/shard_map/pallas_call | solution.py:104
  2.6 3.1 %collective-permute-start.11 = (bf16[128,1024]{1,0:T(8,128)(2,1)}, bf16[128,1024]{1,0:T(8,128)(2,1)S(1)}, u32[]{:S(2)}, u32[]{:S(2)}) collective-permute-start(bf16[128,1024]{1,0:T(8,128)(2,1)} %get-tuple-element.171), channel_id=1, source_target_pairs={{0,4},{4,8},{8,12},{12,0},{1,5},{5,9},{9,13},{13,1},{2,6},{6,10},{... | collective-permute-start | bytes 786440 | tf_op jit(solution)/shard_map/ppermute | solution.py:459
  5.7 2.6 %collective-permute-start.12 = (bf16[128,1024]{1,0:T(8,128)(2,1)}, bf16[128,1024]{1,0:T(8,128)(2,1)S(1)}, u32[]{:S(2)}, u32[]{:S(2)}) collective-permute-start(bf16[128,1024]{1,0:T(8,128)(2,1)} %get-tuple-element.172), channel_id=1, source_target_pairs={{0,8},{4,12},{8,0},{12,4},{1,9},{5,13},{9,1},{13,5},{2,10},{6,14},... | collective-permute-start | bytes 786440 | tf_op jit(solution)/shard_map/ppermute | solution.py:459
  11.9 14.5 %conditional.4 = (bf16[128,1024]{1,0:T(8,128)(2,1)}, bf16[128,1024]{1,0:T(8,128)(2,1)}, bf16[128,1024]{1,0:T(8,128)(2,1)}, bf16[128,1024]{1,0:T(8,128)(2,1)}, f3...) conditional(s32[]{:T(128)} %convert_element_type.16, () %tuple.46, (s32[4,512]{1,0:T(4,128)S(1)}, ...), branch_computations={%region_3.4_spmd, %region_4.5_spmd} | conditional | flops 10240 | bytes 1073216 | solution.py:517
  11.9 1.8 %branch_1_fun.8 = f32[4,512]{1,0:T(4,128)S(1)} custom-call(bf16[4,1024]{1,0:T(4,128)(2,1)} %get-tuple-element.60.router_ref, bf16[512,1024]{1,0:T(8,128)(2,1)} %get-tuple-element.55.tokens_ref), custom_call_target="tpu_custom_call" | custom-call | flops 1024 | bytes 1024 | tf_op jit(solution)/shard_map/cond/branch_1_fun/pallas_call | solution.py:130
  15.2 2.2 %collective-permute-done.8 = f32[4,512]{1,0:T(4,128)S(1)} collective-permute-done((f32[4,512]{1,0:T(4,128)S(1)}, f32[4,512]{1,0:T(4,128)S(1)}, u32[]{:S(2)}, u32[]{:S(2)}) %collective-permute-start.8) | collective-permute-done | bytes 8224 | tf_op jit(solution)/shard_map/cond/branch_1_fun/ppermute | solution.py:462
  19.8 2.7 %branch_1_fun.7 = (bf16[128,1024]{1,0:T(8,128)(2,1)}, bf16[128,1024]{1,0:T(8,128)(2,1)}, bf16[128,1024]{1,0:T(8,128)(2,1)}, bf16[128,1024]{1,0:T(8,128)(2,1)}) custom-call(s32[4,512]{1,0:T(4,128)S(1)} %get-tuple-element.54.code_ref, bf16[512,1024]{1,0:T(8,128)(2,1)} %get-tuple-element.55.tokens_ref), custom_call_target="tpu_custom_call" | custom-call | flops 1024 | bytes 1024 | tf_op jit(solution)/shard_map/cond/branch_1_fun/pallas_call | solution.py:151
  22.5 3.2 %collective-permute-done.10 = f32[1,4,512]{2,1,0:T(4,128)S(1)} collective-permute-done((f32[1,4,512]{2,1,0:T(4,128)}, f32[1,4,512]{2,1,0:T(4,128)S(1)}, u32[]{:S(2)}, u32[]{:S(2)}) %collective-permute-start.10) | collective-permute-done | bytes 8224 | tf_op jit(solution)/shard_map/cond/branch_1_fun/ppermute | solution.py:478
  26.4 2.0 %conditional.5 = (bf16[256,1024]{1,0:T(8,128)(2,1)}) conditional(s32[]{:T(128)} %convert_element_type.16, () %tuple.52, (s32[2,4]{1,0:T(2,128)S(1)}, s32[2,4]{1,0:T(2,128)S(1)}, bf16[128,1024]{1,0:T(8,128)(2,1)S(1)}, bf16[128,1024]{1,0:T(8,128)(2,1)S(1)}, bf16[128,1024]{1,0:T(8,128)(2,1)S(1)}, /*index=5*/bf16[128,1024]{1,0:T(8,128)(2,1)S(1)}) %tuple.53), branch_computations={%region_6.7_spmd, %region_7.8_spmd} | conditional | flops 1024 | bytes 524298 | solution.py:536
  26.4 1.9 %branch_1_fun.9 = bf16[256,1024]{1,0:T(8,128)(2,1)} custom-call(s32[2,4]{1,0:T(2,128)S(1)} %get-tuple-element.61.offset_ref, s32[2,4]{1,0:T(2,128)S(1)} %get-tuple-element.62.count_ref, bf16[128,1024]{1,0:T(8,128)(2,1)S(1)} %get-tuple-element.63.refs_0_, bf16[128,1024]{1,0:T(8,128)(2,1)S(1)} %get-tuple-element.64.refs_1_, ...), custom_call_target="tpu_custom_call" | custom-call | flops 1024 | bytes 1024 | tf_op jit(solution)/shard_map/cond/branch_1_fun/pallas_call | solution.py:188
  30.0 5.3 %collective-permute-start.14 = (bf16[128,1024]{1,0:T(8,128)(2,1)}, bf16[128,1024]{1,0:T(8,128)(2,1)S(1)}, u32[]{:S(2)}, u32[]{:S(2)}) collective-permute-start(bf16[128,1024]{1,0:T(8,128)(2,1)} %get-tuple-element.180), channel_id=1, source_target_pairs={{0,4},{4,8},{8,12},{12,0},{1,5},{5,9},{9,13},{13,1},{2,6},{6,10},{... | collective-permute-start | bytes 786440 | tf_op jit(solution)/shard_map/ppermute | solution.py:459
  39.3 2.6 %shard_map.65 = (f32[256,256]{1,0:T(8,128)S(1)}, f32[256,256]{1,0:T(8,128)S(1)}, bf16[2,1024,256]{2,1,0:T(8,128)(2,1)S(1)}, bf16[2,1024,256]{2,1,0:T(8,128)(2,1)S(1)}) custom-call(s32[4]{0:T(128)S(1)} %pad_add_fusion.order_ref, bf16[1,4096,256]{2,1,0:T(8,128)(2,1)S(1)} %copy-done, bf16[1,4096,256]{2,1,0:T(8,128)(2,1)S(1)} %copy-done.1, ...), custom_call_target="tpu_custom_call" | custom-call | flops 1024 | bytes 1024 | tf_op jit(solution)/shard_map/pallas_call | solution.py:236
  43.1 11.7 %conditional.6 = (bf16[256,256]{1,0:T(8,128)(2,1)}, bf16[256,256]{1,0:T(8,128)(2,1)}, f32[256,1024]{1,0:T(8,128)S(1)}, bf16[2,256,1024]{2,1,0:T(8,128)(2,1)S(1)}) conditional(s32[]{:T(128)} %convert_element_type.16, () %tuple.51, (bf16[256,1024]{1,0:T(8,128)(2,1)}, f32[256,256]{1,0:T(8,128)S(1)}, f32[256,256]{1,0:T(8,128)S(1)}, ...), branch_computations={%region_8.9_spmd, %region_9.10_spmd} | conditional | flops 2048 | bytes 3672256 | solution.py:536
  43.1 2.1 %collective-permute-done.refs_1_ = bf16[256,1024]{1,0:T(8,128)(2,1)S(1)} collective-permute-done((bf16[256,1024]{1,0:T(8,128)(2,1)}, bf16[256,1024]{1,0:T(8,128)(2,1)S(1)}, u32[]{:S(2)}, u32[]{:S(2)}) %collective-permute-start) | collective-permute-done | bytes 524320 | tf_op jit(solution)/shard_map/cond/branch_1_fun/ppermute | solution.py:462
  45.2 1.8 %branch_1_fun.10.refs_0_ = bf16[256,256]{1,0:T(8,128)(2,1)S(1)} custom-call(f32[256,256]{1,0:T(8,128)S(1)} %get-tuple-element.67.gate_before, f32[256,256]{1,0:T(8,128)S(1)} %get-tuple-element.68.up_before, bf16[2,1024,256]{2,1,0:T(8,128)(2,1)S(1)} %get-tuple-element.69.gate_ref, bf16[2,1024,256]{2,1,0:T(8,128)(2,1)S(1)} %get-tuple-element.70.up_ref, ...), custom_call_target="tpu_custom_call" | custom-call | flops 1024 | bytes 1024 | tf_op jit(solution)/shard_map/cond/branch_1_fun/pallas_call | solution.py:264
  50.3 2.8 %collective-permute-done.1 = bf16[256,256]{1,0:T(8,128)(2,1)} collective-permute-done((bf16[256,256]{1,0:T(8,128)(2,1)S(1)}, bf16[256,256]{1,0:T(8,128)(2,1)}, u32[]{:S(2)}, u32[]{:S(2)}) %collective-permute-start.1) | collective-permute-done | bytes 131104 | tf_op jit(solution)/shard_map/cond/branch_1_fun/ppermute | solution.py:462
  54.8 2.0 %shard_map.66.refs_0_ = bf16[256,1024]{1,0:T(8,128)(2,1)S(1)} custom-call(s32[2,4]{1,0:T(2,128)S(1)} %get-tuple-element.241.offset_ref, s32[2,4]{1,0:T(2,128)S(1)} %get-tuple-element.242.count_ref, bf16[128,1024]{1,0:T(8,128)(2,1)} %get-tuple-element.194.refs_0_, bf16[128,1024]{1,0:T(8,128)(2,1)S(1)} %collective-permute-done.14.refs_1_, ...), custom_call_target="tpu_custom_call" | custom-call | flops 1024 | bytes 1024 | tf_op jit(solution)/shard_map/pallas_call | solution.py:188
  58.5 3.1 %shard_map.67 = (bf16[128,1024]{1,0:T(8,128)(2,1)S(1)}, bf16[128,1024]{1,0:T(8,128)(2,1)}, bf16[128,1024]{1,0:T(8,128)(2,1)}, bf16[128,1024]{1,0:T(8,128)(2,1)}) custom-call(s32[2,4]{1,0:T(2,128)S(1)} %get-tuple-element.241.offset_ref, s32[2,4]{1,0:T(2,128)S(1)} %get-tuple-element.242.count_ref, f32[256,1024]{1,0:T(8,128)S(1)} %get-tuple-element.200.before_ref, ...), custom_call_target="tpu_custom_call" | custom-call | flops 1024 | bytes 1024 | tf_op jit(solution)/shard_map/pallas_call | solution.py:356
  61.6 6.4 %collective-permute-start.22 = (bf16[128,1024]{1,0:T(8,128)(2,1)}, bf16[128,1024]{1,0:T(8,128)(2,1)}, u32[]{:S(2)}, u32[]{:S(2)}) collective-permute-start(bf16[128,1024]{1,0:T(8,128)(2,1)} %get-tuple-element.205), channel_id=1, source_target_pairs={{0,12},{4,0},{8,4},{12,8},{1,13},{5,1},{9,5},{13,9},{2,14},{6,2},{... | collective-permute-start | bytes 786440 | tf_op jit(solution)/shard_map/ppermute | solution.py:459
  70.8 1.8 %shard_map.68 = (f32[256,256]{1,0:T(8,128)S(1)}, f32[256,256]{1,0:T(8,128)S(1)}, bf16[2,1024,256]{2,1,0:T(8,128)(2,1)S(1)}, bf16[2,1024,256]{2,1,0:T(8,128)(2,1)S(1)}) custom-call(s32[4]{0:T(128)S(1)} %pad_add_fusion.order_ref, bf16[1,4096,256]{2,1,0:T(8,128)(2,1)S(1)} %copy-done, bf16[1,4096,256]{2,1,0:T(8,128)(2,1)S(1)} %copy-done.2, ...), custom_call_target="tpu_custom_call" | custom-call | flops 1024 | bytes 1024 | tf_op jit(solution)/shard_map/pallas_call | solution.py:236
  72.7 11.7 %conditional.7 = (bf16[256,256]{1,0:T(8,128)(2,1)}, bf16[256,256]{1,0:T(8,128)(2,1)}, f32[256,1024]{1,0:T(8,128)S(1)}, bf16[2,256,1024]{2,1,0:T(8,128)(2,1)S(1)}) conditional(s32[]{:T(128)} %convert_element_type.17, () %tuple.48, (bf16[256,1024]{1,0:T(8,128)(2,1)}, f32[256,256]{1,0:T(8,128)S(1)}, f32[256,256]{1,0:T(8,128)S(1)}, ...), branch_computations={%region_10.11_spmd, %region_11.12_spmd} | conditional | flops 2048 | bytes 3672256 | solution.py:536
  72.8 2.1 %collective-permute-done.4.refs_1_ = bf16[256,1024]{1,0:T(8,128)(2,1)S(1)} collective-permute-done((bf16[256,1024]{1,0:T(8,128)(2,1)}, bf16[256,1024]{1,0:T(8,128)(2,1)S(1)}, u32[]{:S(2)}, u32[]{:S(2)}) %collective-permute-start.4) | collective-permute-done | bytes 524320 | tf_op jit(solution)/shard_map/cond/branch_1_fun/ppermute | solution.py:462
  74.9 1.8 %branch_1_fun.12.refs_0_ = bf16[256,256]{1,0:T(8,128)(2,1)S(1)} custom-call(f32[256,256]{1,0:T(8,128)S(1)} %get-tuple-element.79.gate_before, f32[256,256]{1,0:T(8,128)S(1)} %get-tuple-element.80.up_before, bf16[2,1024,256]{2,1,0:T(8,128)(2,1)S(1)} %get-tuple-element.81.gate_ref, bf16[2,1024,256]{2,1,0:T(8,128)(2,1)S(1)} %get-tuple-element.82.up_ref, ...), custom_call_target="tpu_custom_call" | custom-call | flops 1024 | bytes 1024 | tf_op jit(solution)/shard_map/cond/branch_1_fun/pallas_call | solution.py:264
  79.7 3.1 %collective-permute-done.5 = bf16[256,256]{1,0:T(8,128)(2,1)} collective-permute-done((bf16[256,256]{1,0:T(8,128)(2,1)S(1)}, bf16[256,256]{1,0:T(8,128)(2,1)}, u32[]{:S(2)}, u32[]{:S(2)}) %collective-permute-start.5) | collective-permute-done | bytes 131104 | tf_op jit(solution)/shard_map/cond/branch_1_fun/ppermute | solution.py:462
  84.4 3.4 %collective-permute-start.21 = (f32[2,4,512]{2,1,0:T(4,128)S(1)}, f32[2,4,512]{2,1,0:T(4,128)S(1)}, u32[]{:S(2)}, u32[]{:S(2)}) collective-permute-start(f32[2,4,512]{2,1,0:T(4,128)S(1)} %get-tuple-element.227), channel_id=1, source_target_pairs={{0,8},{4,12},{8,0},{12,4},{1,9},{5,13},{9,1},{13,5},{2,10},{6,14},... | collective-permute-start | bytes 49160 | tf_op jit(solution)/shard_map/ppermute | solution.py:478
  87.9 2.4 %shard_map.69 = (bf16[128,1024]{1,0:T(8,128)(2,1)S(1)}, bf16[128,1024]{1,0:T(8,128)(2,1)S(1)}, bf16[128,1024]{1,0:T(8,128)(2,1)S(1)}, bf16[128,1024]{1,0:T(8,128)(2,1)S(1)}) custom-call(s32[2,4]{1,0:T(2,128)S(1)} %get-tuple-element.241.offset_ref, s32[2,4]{1,0:T(2,128)S(1)} %get-tuple-element.242.count_ref, f32[256,1024]{1,0:T(8,128)S(1)} %get-tuple-element.219.before_ref, ...), custom_call_target="tpu_custom_call" | custom-call | flops 1024 | bytes 1024 | tf_op jit(solution)/shard_map/pallas_call | solution.py:356
  90.3 2.0 %collective-permute-done.21 = f32[2,4,512]{2,1,0:T(4,128)S(1)} collective-permute-done((f32[2,4,512]{2,1,0:T(4,128)S(1)}, f32[2,4,512]{2,1,0:T(4,128)S(1)}, u32[]{:S(2)}, u32[]{:S(2)}) %collective-permute-start.21) | collective-permute-done | bytes 16416 | tf_op jit(solution)/shard_map/ppermute | solution.py:478
  92.3 2.8 %collective-permute-start.25 = (bf16[128,1024]{1,0:T(8,128)(2,1)S(1)}, bf16[128,1024]{1,0:T(8,128)(2,1)S(1)}, u32[]{:S(2)}, u32[]{:S(2)}) collective-permute-start(bf16[128,1024]{1,0:T(8,128)(2,1)S(1)} %get-tuple-element.234), channel_id=1, source_target_pairs={{0,12},{4,0},{8,4},{12,8},{1,13},{5,1},{9,5},{13,9},{2,14},{6,2},{... | collective-permute-start | bytes 786440 | tf_op jit(solution)/shard_map/ppermute | solution.py:459
  97.1 1.9 %shard_map.71.refs_0_ = f32[512,1024]{1,0:T(8,128)S(1)} custom-call(s32[4,512]{1,0:T(4,128)S(1)} %get-tuple-element.164.code_ref, f32[4,512]{1,0:T(4,128)S(1)} %shard_map.70.weight_ref, bf16[128,1024]{1,0:T(8,128)(2,1)S(1)} %get-tuple-element.229.refs_0_, bf16[128,1024]{1,0:T(8,128)(2,1)} %collective-permute-done.22.refs_1_, ...), custom_call_target="tpu_custom_call" | custom-call | flops 1024 | bytes 1024 | tf_op jit(solution)/shard_map/pallas_call | solution.py:432
  99.1 2.9 %collective-permute-done.25.refs_2_ = bf16[128,1024]{1,0:T(8,128)(2,1)S(1)} collective-permute-done((bf16[128,1024]{1,0:T(8,128)(2,1)S(1)}, bf16[128,1024]{1,0:T(8,128)(2,1)S(1)}, u32[]{:S(2)}, u32[]{:S(2)}) %collective-permute-start.25) | collective-permute-done | bytes 262176 | tf_op jit(solution)/shard_map/ppermute | solution.py:459
  101.9 15.2 %collective-permute-done.26.refs_3_ = bf16[128,1024]{1,0:T(8,128)(2,1)S(1)} collective-permute-done((bf16[128,1024]{1,0:T(8,128)(2,1)S(1)}, bf16[128,1024]{1,0:T(8,128)(2,1)S(1)}, u32[]{:S(2)}, u32[]{:S(2)}) %collective-permute-start.26) | collective-permute-done | bytes 262176 | tf_op jit(solution)/shard_map/ppermute | solution.py:459
  117.2 1.9 %shard_map.72 = bf16[512,1024]{1,0:T(8,128)(2,1)} custom-call(s32[4,512]{1,0:T(4,128)S(1)} %get-tuple-element.164.code_ref, f32[4,512]{1,0:T(4,128)S(1)} %shard_map.70.weight_ref, f32[512,1024]{1,0:T(8,128)S(1)} %shard_map.71.refs_0_, bf16[128,1024]{1,0:T(8,128)(2,1)S(1)} %get-tuple-element.233.refs_1_, ...), custom_call_target="tpu_custom_call" | custom-call | flops 1024 | bytes 1024 | tf_op jit(solution)/shard_map/pallas_call | solution.py:432
  (66 shorter events, 30.2 us)
Async XLA Ops:
  2.6 23.8 %collective-permute-start.11 = (bf16[128,1024]{1,0:T(8,128)(2,1)}, bf16[128,1024]{1,0:T(8,128)(2,1)S(1)}, u32[]{:S(2)}, u32[]{:S(2)}) collective-permute-start(bf16[128,1024]{1,0:T(8,128)(2,1)} %get-tuple-element.171), channel_id=1, source_target_pairs={{0,4},{4,8},{8,12},{12,0},{1,5},{5,9},{9,13},{13,1},{2,6},{6,10},{... | collective-permute-start | bytes 786440 | tf_op jit(solution)/shard_map/ppermute | solution.py:459
  5.7 20.7 %collective-permute-start.12 = (bf16[128,1024]{1,0:T(8,128)(2,1)}, bf16[128,1024]{1,0:T(8,128)(2,1)S(1)}, u32[]{:S(2)}, u32[]{:S(2)}) collective-permute-start(bf16[128,1024]{1,0:T(8,128)(2,1)} %get-tuple-element.172), channel_id=1, source_target_pairs={{0,8},{4,12},{8,0},{12,4},{1,9},{5,13},{9,1},{13,5},{2,10},{6,14},... | collective-permute-start | bytes 786440 | tf_op jit(solution)/shard_map/ppermute | solution.py:459
  8.3 18.1 %collective-permute-start.13 = (bf16[128,1024]{1,0:T(8,128)(2,1)}, bf16[128,1024]{1,0:T(8,128)(2,1)S(1)}, u32[]{:S(2)}, u32[]{:S(2)}) collective-permute-start(bf16[128,1024]{1,0:T(8,128)(2,1)} %get-tuple-element.173), channel_id=1, source_target_pairs={{0,12},{4,0},{8,4},{12,8},{1,13},{5,1},{9,5},{13,9},{2,14},{6,2},{... | collective-permute-start | bytes 786440 | tf_op jit(solution)/shard_map/ppermute | solution.py:459
  11.9 25.9 %copy-start = (bf16[1,4096,256]{2,1,0:T(8,128)(2,1)S(1)}, bf16[1,4096,256]{2,1,0:T(8,128)(2,1)}, u32[]{:S(2)}) copy-start(bf16[1,4096,256]{2,1,0:T(8,128)(2,1)} %gate_ref.3) | copy-start | bytes 6291460
  13.7 3.7 %collective-permute-start.8 = (f32[4,512]{1,0:T(4,128)S(1)}, f32[4,512]{1,0:T(4,128)S(1)}, u32[]{:S(2)}, u32[]{:S(2)}) collective-permute-start(f32[4,512]{1,0:T(4,128)S(1)} %branch_1_fun.8), channel_id=1, source_target_pairs={{0,2},{1,3},{2,0},{3,1},{4,6},{5,7},{6,4},{7,5},{8,10},{9,11},{10,... | collective-permute-start | bytes 24584 | tf_op jit(solution)/shard_map/cond/branch_1_fun/ppermute | solution.py:462
  17.3 1.2 collective-permute-start.9
  19.1 6.5 %collective-permute-start.10 = (f32[1,4,512]{2,1,0:T(4,128)}, f32[1,4,512]{2,1,0:T(4,128)S(1)}, u32[]{:S(2)}, u32[]{:S(2)}) collective-permute-start(f32[1,4,512]{2,1,0:T(4,128)} %bitcast), channel_id=1, source_target_pairs={{0,4},{4,0},{8,12},{12,8},{1,5},{5,1},{9,13},{13,9},{2,6},{6,2},{1... | collective-permute-start | bytes 24584 | tf_op jit(solution)/shard_map/cond/branch_1_fun/ppermute | solution.py:478
  28.4 9.4 %collective-permute-start.18 = (bf16[256,1024]{1,0:T(8,128)(2,1)}, bf16[256,1024]{1,0:T(8,128)(2,1)S(1)}, u32[]{:S(2)}, u32[]{:S(2)}) collective-permute-start(bf16[256,1024]{1,0:T(8,128)(2,1)} %get-tuple-element.273.refs_0_), channel_id=1, source_target_pairs={{0,1},{1,0},{2,3},{3,2},{4,5},{5,4},{6,7},{7,6},{8,9},{9,8},{10,11... | collective-permute-start | bytes 1572872 | tf_op jit(solution)/shard_map/ppermute | solution.py:462
  28.4 14.7 %collective-permute-start.17 = (bf16[256,1024]{1,0:T(8,128)(2,1)}, bf16[256,1024]{1,0:T(8,128)(2,1)}, u32[]{:S(2)}, u32[]{:S(2)}) collective-permute-start(bf16[256,1024]{1,0:T(8,128)(2,1)} %get-tuple-element.273.refs_0_), channel_id=1, source_target_pairs={{0,2},{1,3},{2,0},{3,1},{4,6},{5,7},{6,4},{7,5},{8,10},{9,11},{10,... | collective-permute-start | bytes 1572872 | tf_op jit(solution)/shard_map/ppermute | solution.py:462
  30.0 24.8 %collective-permute-start.14 = (bf16[128,1024]{1,0:T(8,128)(2,1)}, bf16[128,1024]{1,0:T(8,128)(2,1)S(1)}, u32[]{:S(2)}, u32[]{:S(2)}) collective-permute-start(bf16[128,1024]{1,0:T(8,128)(2,1)} %get-tuple-element.180), channel_id=1, source_target_pairs={{0,4},{4,8},{8,12},{12,0},{1,5},{5,9},{9,13},{13,1},{2,6},{6,10},{... | collective-permute-start | bytes 786440 | tf_op jit(solution)/shard_map/ppermute | solution.py:459
  35.3 19.5 %collective-permute-start.15 = (bf16[128,1024]{1,0:T(8,128)(2,1)}, bf16[128,1024]{1,0:T(8,128)(2,1)S(1)}, u32[]{:S(2)}, u32[]{:S(2)}) collective-permute-start(bf16[128,1024]{1,0:T(8,128)(2,1)} %get-tuple-element.181), channel_id=1, source_target_pairs={{0,8},{4,12},{8,0},{12,4},{1,9},{5,13},{9,1},{13,5},{2,10},{6,14},... | collective-permute-start | bytes 786440 | tf_op jit(solution)/shard_map/ppermute | solution.py:459
  36.9 17.9 %collective-permute-start.16 = (bf16[128,1024]{1,0:T(8,128)(2,1)}, bf16[128,1024]{1,0:T(8,128)(2,1)S(1)}, u32[]{:S(2)}, u32[]{:S(2)}) collective-permute-start(bf16[128,1024]{1,0:T(8,128)(2,1)} %get-tuple-element.182), channel_id=1, source_target_pairs={{0,12},{4,0},{8,4},{12,8},{1,13},{5,1},{9,5},{13,9},{2,14},{6,2},{... | collective-permute-start | bytes 786440 | tf_op jit(solution)/shard_map/ppermute | solution.py:459
  39.3 3.8 %copy-start.3 = (bf16[1,1024,1024]{2,1,0:T(8,128)(2,1)S(1)}, bf16[1,1024,1024]{2,1,0:T(8,128)(2,1)}, u32[]{:S(2)}) copy-start(bf16[1,1024,1024]{2,1,0:T(8,128)(2,1)} %param.18) | copy-start | bytes 6291460
  43.1 2.1 %collective-permute-start = (bf16[256,1024]{1,0:T(8,128)(2,1)}, bf16[256,1024]{1,0:T(8,128)(2,1)S(1)}, u32[]{:S(2)}, u32[]{:S(2)}) collective-permute-start(bf16[256,1024]{1,0:T(8,128)(2,1)} %get-tuple-element.71.refs_0_), channel_id=1, source_target_pairs={{0,1},{1,0},{2,3},{3,2},{4,5},{5,4},{6,7},{7,6},{8,9},{9,8},{10,11... | collective-permute-start | bytes 1572872 | tf_op jit(solution)/shard_map/cond/branch_1_fun/ppermute | solution.py:462
  47.0 1.7 %collective-permute-start.2 = (bf16[256,256]{1,0:T(8,128)(2,1)S(1)}, bf16[256,256]{1,0:T(8,128)(2,1)S(1)}, u32[]{:S(2)}, u32[]{:S(2)}) collective-permute-start(bf16[256,256]{1,0:T(8,128)(2,1)S(1)} %branch_1_fun.10.refs_0_), channel_id=1, source_target_pairs={{0,1},{1,0},{2,3},{3,2},{4,5},{5,4},{6,7},{7,6},{8,9},{9,8},{10,11... | collective-permute-start | bytes 393224 | tf_op jit(solution)/shard_map/cond/branch_1_fun/ppermute | solution.py:462
  47.2 5.9 %collective-permute-start.1 = (bf16[256,256]{1,0:T(8,128)(2,1)S(1)}, bf16[256,256]{1,0:T(8,128)(2,1)}, u32[]{:S(2)}, u32[]{:S(2)}) collective-permute-start(bf16[256,256]{1,0:T(8,128)(2,1)S(1)} %branch_1_fun.10.refs_0_), channel_id=1, source_target_pairs={{0,2},{1,3},{2,0},{3,1},{4,6},{5,7},{6,4},{7,5},{8,10},{9,11},{10,... | collective-permute-start | bytes 393224 | tf_op jit(solution)/shard_map/cond/branch_1_fun/ppermute | solution.py:462
  53.1 1.7 %collective-permute-start.3 = (bf16[256,256]{1,0:T(8,128)(2,1)}, bf16[256,256]{1,0:T(8,128)(2,1)}, u32[]{:S(2)}, u32[]{:S(2)}) collective-permute-start(bf16[256,256]{1,0:T(8,128)(2,1)} %collective-permute-done.1), channel_id=1, source_target_pairs={{0,1},{1,0},{2,3},{3,2},{4,5},{5,4},{6,7},{7,6},{8,9},{9,8},{10,11... | collective-permute-start | bytes 393224 | tf_op jit(solution)/shard_map/cond/branch_1_fun/ppermute | solution.py:462
  56.8 12.5 %collective-permute-start.20 = (bf16[256,1024]{1,0:T(8,128)(2,1)S(1)}, bf16[256,1024]{1,0:T(8,128)(2,1)S(1)}, u32[]{:S(2)}, u32[]{:S(2)}) collective-permute-start(bf16[256,1024]{1,0:T(8,128)(2,1)S(1)} %shard_map.66.refs_0_), channel_id=1, source_target_pairs={{0,1},{1,0},{2,3},{3,2},{4,5},{5,4},{6,7},{7,6},{8,9},{9,8},{10,11... | collective-permute-start | bytes 1572872 | tf_op jit(solution)/shard_map/ppermute | solution.py:462
  57.0 15.7 %collective-permute-start.19 = (bf16[256,1024]{1,0:T(8,128)(2,1)S(1)}, bf16[256,1024]{1,0:T(8,128)(2,1)}, u32[]{:S(2)}, u32[]{:S(2)}) collective-permute-start(bf16[256,1024]{1,0:T(8,128)(2,1)S(1)} %shard_map.66.refs_0_), channel_id=1, source_target_pairs={{0,2},{1,3},{2,0},{3,1},{4,6},{5,7},{6,4},{7,5},{8,10},{9,11},{10,... | collective-permute-start | bytes 1572872 | tf_op jit(solution)/shard_map/ppermute | solution.py:462
  61.6 30.7 %collective-permute-start.22 = (bf16[128,1024]{1,0:T(8,128)(2,1)}, bf16[128,1024]{1,0:T(8,128)(2,1)}, u32[]{:S(2)}, u32[]{:S(2)}) collective-permute-start(bf16[128,1024]{1,0:T(8,128)(2,1)} %get-tuple-element.205), channel_id=1, source_target_pairs={{0,12},{4,0},{8,4},{12,8},{1,13},{5,1},{9,5},{13,9},{2,14},{6,2},{... | collective-permute-start | bytes 786440 | tf_op jit(solution)/shard_map/ppermute | solution.py:459
  68.0 24.3 %collective-permute-start.23 = (bf16[128,1024]{1,0:T(8,128)(2,1)}, bf16[128,1024]{1,0:T(8,128)(2,1)}, u32[]{:S(2)}, u32[]{:S(2)}) collective-permute-start(bf16[128,1024]{1,0:T(8,128)(2,1)} %get-tuple-element.206), channel_id=1, source_target_pairs={{0,8},{4,12},{8,0},{12,4},{1,9},{5,13},{9,1},{13,5},{2,10},{6,14},... | collective-permute-start | bytes 786440 | tf_op jit(solution)/shard_map/ppermute | solution.py:459
  68.4 23.9 %collective-permute-start.24 = (bf16[128,1024]{1,0:T(8,128)(2,1)}, bf16[128,1024]{1,0:T(8,128)(2,1)}, u32[]{:S(2)}, u32[]{:S(2)}) collective-permute-start(bf16[128,1024]{1,0:T(8,128)(2,1)} %get-tuple-element.207), channel_id=1, source_target_pairs={{0,4},{4,8},{8,12},{12,0},{1,5},{5,9},{9,13},{13,1},{2,6},{6,10},{... | collective-permute-start | bytes 786440 | tf_op jit(solution)/shard_map/ppermute | solution.py:459
  69.3 1.6 %copy-start.2 = (bf16[1,4096,256]{2,1,0:T(8,128)(2,1)S(1)}, bf16[1,4096,256]{2,1,0:T(8,128)(2,1)}, u32[]{:S(2)}) copy-start(bf16[1,4096,256]{2,1,0:T(8,128)(2,1)} %up_ref.3) | copy-start | bytes 6291460
  70.8 1.8 %copy-start.4 = (bf16[1,1024,1024]{2,1,0:T(8,128)(2,1)S(1)}, bf16[1,1024,1024]{2,1,0:T(8,128)(2,1)}, u32[]{:S(2)}) copy-start(bf16[1,1024,1024]{2,1,0:T(8,128)(2,1)} %param.18) | copy-start | bytes 6291460
  72.7 2.2 %collective-permute-start.4 = (bf16[256,1024]{1,0:T(8,128)(2,1)}, bf16[256,1024]{1,0:T(8,128)(2,1)S(1)}, u32[]{:S(2)}, u32[]{:S(2)}) collective-permute-start(bf16[256,1024]{1,0:T(8,128)(2,1)} %get-tuple-element.83.refs_0_), channel_id=1, source_target_pairs={{0,1},{1,0},{2,3},{3,2},{4,5},{5,4},{6,7},{7,6},{8,9},{9,8},{10,11... | collective-permute-start | bytes 1572872 | tf_op jit(solution)/shard_map/cond/branch_1_fun/ppermute | solution.py:462
  76.7 1.4 %collective-permute-start.6 = (bf16[256,256]{1,0:T(8,128)(2,1)S(1)}, bf16[256,256]{1,0:T(8,128)(2,1)S(1)}, u32[]{:S(2)}, u32[]{:S(2)}) collective-permute-start(bf16[256,256]{1,0:T(8,128)(2,1)S(1)} %branch_1_fun.12.refs_0_), channel_id=1, source_target_pairs={{0,1},{1,0},{2,3},{3,2},{4,5},{5,4},{6,7},{7,6},{8,9},{9,8},{10,11... | collective-permute-start | bytes 393224 | tf_op jit(solution)/shard_map/cond/branch_1_fun/ppermute | solution.py:462
  76.9 5.9 %collective-permute-start.5 = (bf16[256,256]{1,0:T(8,128)(2,1)S(1)}, bf16[256,256]{1,0:T(8,128)(2,1)}, u32[]{:S(2)}, u32[]{:S(2)}) collective-permute-start(bf16[256,256]{1,0:T(8,128)(2,1)S(1)} %branch_1_fun.12.refs_0_), channel_id=1, source_target_pairs={{0,2},{1,3},{2,0},{3,1},{4,6},{5,7},{6,4},{7,5},{8,10},{9,11},{10,... | collective-permute-start | bytes 393224 | tf_op jit(solution)/shard_map/cond/branch_1_fun/ppermute | solution.py:462
  82.8 1.7 %collective-permute-start.7 = (bf16[256,256]{1,0:T(8,128)(2,1)}, bf16[256,256]{1,0:T(8,128)(2,1)}, u32[]{:S(2)}, u32[]{:S(2)}) collective-permute-start(bf16[256,256]{1,0:T(8,128)(2,1)} %collective-permute-done.5), channel_id=1, source_target_pairs={{0,1},{1,0},{2,3},{3,2},{4,5},{5,4},{6,7},{7,6},{8,9},{9,8},{10,11... | collective-permute-start | bytes 393224 | tf_op jit(solution)/shard_map/cond/branch_1_fun/ppermute | solution.py:462
  84.4 7.8 %collective-permute-start.21 = (f32[2,4,512]{2,1,0:T(4,128)S(1)}, f32[2,4,512]{2,1,0:T(4,128)S(1)}, u32[]{:S(2)}, u32[]{:S(2)}) collective-permute-start(f32[2,4,512]{2,1,0:T(4,128)S(1)} %get-tuple-element.227), channel_id=1, source_target_pairs={{0,8},{4,12},{8,0},{12,4},{1,9},{5,13},{9,1},{13,5},{2,10},{6,14},... | collective-permute-start | bytes 49160 | tf_op jit(solution)/shard_map/ppermute | solution.py:478
  92.3 9.6 %collective-permute-start.25 = (bf16[128,1024]{1,0:T(8,128)(2,1)S(1)}, bf16[128,1024]{1,0:T(8,128)(2,1)S(1)}, u32[]{:S(2)}, u32[]{:S(2)}) collective-permute-start(bf16[128,1024]{1,0:T(8,128)(2,1)S(1)} %get-tuple-element.234), channel_id=1, source_target_pairs={{0,12},{4,0},{8,4},{12,8},{1,13},{5,1},{9,5},{13,9},{2,14},{6,2},{... | collective-permute-start | bytes 786440 | tf_op jit(solution)/shard_map/ppermute | solution.py:459
  95.1 22.0 %collective-permute-start.26 = (bf16[128,1024]{1,0:T(8,128)(2,1)S(1)}, bf16[128,1024]{1,0:T(8,128)(2,1)S(1)}, u32[]{:S(2)}, u32[]{:S(2)}) collective-permute-start(bf16[128,1024]{1,0:T(8,128)(2,1)S(1)} %get-tuple-element.235), channel_id=1, source_target_pairs={{0,8},{4,12},{8,0},{12,4},{1,9},{5,13},{9,1},{13,5},{2,10},{6,14},... | collective-permute-start | bytes 786440 | tf_op jit(solution)/shard_map/ppermute | solution.py:459
  95.1 22.0 %collective-permute-start.27 = (bf16[128,1024]{1,0:T(8,128)(2,1)S(1)}, bf16[128,1024]{1,0:T(8,128)(2,1)S(1)}, u32[]{:S(2)}, u32[]{:S(2)}) collective-permute-start(bf16[128,1024]{1,0:T(8,128)(2,1)S(1)} %get-tuple-element.236), channel_id=1, source_target_pairs={{0,4},{4,8},{8,12},{12,0},{1,5},{5,9},{9,13},{13,1},{2,6},{6,10},{... | collective-permute-start | bytes 786440 | tf_op jit(solution)/shard_map/ppermute | solution.py:459
  (1 other events, 1.6 us)

commit v11 on v10

--- a/solution.py
+++ b/solution.py
@@ -29,6 +29,10 @@
 
 def params(limit=VMEM_LIMIT):
     return pltpu.CompilerParams(vmem_limit_bytes=limit)
+
+
+def partner(place, experts):
+    return -place % experts
 
 
 def dot(a, b):
@@ -62,7 +66,7 @@
     picks_load.wait()
     masks, starts = [], []
     for shift in range(experts):
-        local = picks_ref[pl.ds(lax.rem(me + shift, experts), 1), :] - me * rows
+        local = picks_ref[pl.ds(jnp.bitwise_xor(me, partner(shift, experts)), 1), :] - me * rows
         starts.append(jnp.broadcast_to(jnp.sum((local < 0).astype(F32), axis=1, keepdims=True), (8, 128)))
         strip = lax.shift_right_arithmetic(local, 7)
         place = jnp.bitwise_and(local, 127)
@@ -379,7 +383,7 @@
     score_ref[...] = own_scale * own * column_scale
     picked = []
     for shift in range(experts):
-        score = score_ref[pl.ds(lax.rem(me + shift, experts), 1), :]
+        score = score_ref[pl.ds(jnp.bitwise_xor(me, partner(shift, experts)), 1), :]
         picked.append(jnp.where(code_ref[pl.ds(shift, 1), :] >= 0, score, 0.0))
     total = picked[0]
     for one in picked[1:]:
@@ -456,7 +460,7 @@
     place = me.astype(I32).reshape(1)
 
     def along_expert(x, shift):
-        return lax.ppermute(x, "expert", [(i, (i + shift) % experts) for i in range(experts)])
+        return lax.ppermute(x, "expert", [(i, i ^ shift) for i in range(experts)])
 
     def swap(x, bit):
         return lax.ppermute(x, "dp", [(i, i ^ bit) for i in range(width_parts)])
@@ -474,8 +478,8 @@
     near_places, far_places = places[: len(near)], places[len(near) :]
     order = jnp.stack([part ^ m for m in masks]).astype(I32)
 
-    def swap_expert(x, bit):
-        return lax.ppermute(x, "expert", [(i, i ^ bit) for i in range(experts)])
+    def exchange(blocks):
+        return [blocks[0]] + [along_expert(blocks[i], partner(i, experts)) for i in range(1, experts)]
 
     expert_bits = [1 << i for i in range(experts.bit_length() - 1)]
 
@@ -491,7 +495,7 @@
 
     code, first = first_batch(place, picks, tokens, depth)
     own_picks = lax.dynamic_slice_in_dim(picks, me, 1, axis=0)
-    sources = lax.rem(me - jnp.arange(experts, dtype=I32) + experts, experts)
+    sources = jnp.bitwise_xor(me, jnp.array([partner(i, experts) for i in range(experts)], I32))
     start = jnp.sum((own_picks < (sources * rows)[:, None]).astype(I32), axis=1)
     stop = jnp.sum((own_picks < ((sources + 1) * rows)[:, None]).astype(I32), axis=1)
     ids = jnp.arange(BATCHES, dtype=I32)[:, None]
@@ -507,13 +511,13 @@
             logits = logits + swap(logits, bit)
         gathered = logits[None]
         for bit in expert_bits[:-1]:
-            gathered = jnp.concatenate([gathered, swap_expert(gathered, bit)])
+            gathered = jnp.concatenate([gathered, along_expert(gathered, bit)])
         return later, logits, gathered
 
     def nothing_first(router):
         return jax.tree.map(lambda x: jnp.zeros(x.shape, x.dtype), jax.eval_shape(beside_first, router))
 
-    arrived = [[first[0]] + [along_expert(first[shift], shift) for shift in range(1, experts)]]
+    arrived = [exchange(first)]
     later, logits, gathered = lax.cond(present[0], beside_first, nothing_first, router_weight.T)
 
     def far_half(far, sums):
@@ -535,9 +539,6 @@
 
         return lax.cond(present[k], run, skip, *operands)
 
-    def send_back(results):
-        return [results[0]] + [along_expert(results[shift], -shift) for shift in range(1, experts)]
-
     waiting = []
     far = partial = None
     moved = gathered
@@ -545,7 +546,7 @@
         blocks = after(arrived[k], moved)
         if k < BATCHES - 1:
             moving = after(later[k], blocks)
-            arrived.append([moving[0]] + [along_expert(moving[shift], shift) for shift in range(1, experts)])
+            arrived.append(exchange(moving))
         if k == 0:
             block = fenced(k, lambda *blocks: compact(offsets, counts, 0, blocks, size), *blocks)
         else:
@@ -557,18 +558,18 @@
             results = settle(k - 1, far, partial)
             if k > 1:
                 results, waiting[k - 2] = lax.optimization_barrier((results, waiting[k - 2]))
-            waiting.append(send_back(results))
+            waiting.append(exchange(results))
             near = after(near, results)
         sums = gate_up_near(order, near_places, far_places, gate_weight, up_weight, near)
         across, sums = lax.optimization_barrier((across, sums))
         if k == BATCHES - 1:
             gathered = after(gathered, sums)
-            gathered = jnp.concatenate([gathered, swap_expert(gathered, expert_bits[-1])])
+            gathered = jnp.concatenate([gathered, along_expert(gathered, expert_bits[-1])])
         far, partial = fenced(k, far_half, across, sums)
         moved = partial
     results = settle(BATCHES - 1, far, partial)
     results, gathered, waiting[-1] = lax.optimization_barrier((results, gathered, waiting[-1]))
-    waiting.append(send_back(results))
+    waiting.append(exchange(results))
     weights = slot_weights(place, logits, gathered, code)
     total = None
     for k in range(BATCHES):

time: 120 us -> 119 us (level)
  starting transfers between devices: 37.3 us -> 28.9 us
  waiting for transfers between devices: 41.6 us -> 49 us
    ppermute x14, starting transfers between devices: 29.6 us -> 20.4 us  [along_expert(): return lax.ppermute(x, 'expert', [(i, i ^ shift) for i in range(experts)])]
    ppermute x14, waiting for transfers between devices: 23.2 us -> 27 us  [along_expert(): return lax.ppermute(x, 'expert', [(i, i ^ shift) for i in range(experts)])]
    ppermute x14, waiting for transfers between devices: 18.4 us -> 22 us  [swap(): return lax.ppermute(x, 'dp', [(i, i ^ bit) for i in range(width_parts)])]
  transfers between devices with their start and end apart: 28 -> 28, of which waited for: 14 -> 15; matrix products, arithmetic and copies ran while one was open for 3% -> 3% of each run, Pallas kernels for 20% -> 20%
where the time goes in v11:
time: 119 us
  waiting for transfers between devices  49 us (41%)
  Pallas kernels  32.4 us (27%)
  starting transfers between devices  28.9 us (24%)
  local copies, waits for them, and re-layouts  3.89 us (3%)
  other arithmetic  2.95 us (2%)
  between operations  1.6 us (1%)
    ppermute x14, waiting for transfers between devices, along_expert(): return lax.ppermute(x, 'expert', [(i, i ^ shift) for i in range(experts)])  27 us
    ppermute x14, waiting for transfers between devices, swap(): return lax.ppermute(x, 'dp', [(i, i ^ bit) for i in range(width_parts)])  22 us
    ppermute x14, starting transfers between devices, along_expert(): return lax.ppermute(x, 'expert', [(i, i ^ shift) for i in range(experts)])  20.4 us
    ppermute x14, starting transfers between devices, swap(): return lax.ppermute(x, 'dp', [(i, i ^ bit) for i in range(width_parts)])  8.41 us
    pallas_call x2, Pallas kernels, down_last(): pl.pallas_call(functools.partial(down_last_kernel, parts, experts, k, dir...  5.48 us
    pallas_call x2, Pallas kernels, gate_up_near(): pl.pallas_call(functools.partial(gate_up_near_kernel, parts, near, far),...  4.4 us
    pallas_call x2, Pallas kernels, compact(): pl.pallas_call(functools.partial(compact_kernel, experts, k), out_shape=j...  3.94 us
    pallas_call x2, Pallas kernels, combine(): pl.pallas_call(functools.partial(combine_kernel, experts, k), out_shape=j...  3.83 us
  transfers between devices with their start and end apart: 28, of which 15 were waited for; matrix products, arithmetic and copies ran while one was open for 3% of the time, Pallas kernels for 20%

profile of v11, /device:TPU:0, one launch (start us, length us, event | category | flops | bytes accessed | tf_op | source)
XLA Modules:
  0.0 118.8 jit_solution(7852177701685402609)
XLA Ops:
  0.0 2.6 %shard_map.73 = (s32[4,512]{1,0:T(4,128)S(1)}, bf16[128,1024]{1,0:T(8,128)(2,1)S(1)}, bf16[128,1024]{1,0:T(8,128)(2,1)}, bf16[128,1024]{1,0:T(8,128)(2,1)}, bf16[128,1024]{1,0:T(8,128)(2,1)}) custom-call(s32[1]{0:T(128)} %bitcast.1.place_ref, s32[4,512]{1,0:T(4,128)} %picks_in.1, bf16[512,1024]{1,0:T(8,128)(2,1)} %tokens_ref.1), custom_call_target="tpu_custom_call" | custom-call | flops 1024 | bytes 1024 | tf_op jit(solution)/shard_map/pallas_call | solution.py:108
  2.6 5.1 %collective-permute-start.11 = (bf16[128,1024]{1,0:T(8,128)(2,1)}, bf16[128,1024]{1,0:T(8,128)(2,1)S(1)}, u32[]{:S(2)}, u32[]{:S(2)}) collective-permute-start(bf16[128,1024]{1,0:T(8,128)(2,1)} %get-tuple-element.171), channel_id=1, source_target_pairs={{0,12},{4,8},{8,4},{12,0},{1,13},{5,9},{9,5},{13,1},{2,14},{6,10},... | collective-permute-start | bytes 786440 | tf_op jit(solution)/shard_map/ppermute | solution.py:463
  11.3 14.4 %conditional.4 = (bf16[128,1024]{1,0:T(8,128)(2,1)}, bf16[128,1024]{1,0:T(8,128)(2,1)}, bf16[128,1024]{1,0:T(8,128)(2,1)}, bf16[128,1024]{1,0:T(8,128)(2,1)}, f3...) conditional(s32[]{:T(128)} %convert_element_type.16, () %tuple.46, (s32[4,512]{1,0:T(4,128)S(1)}, ...), branch_computations={%region_3.4_spmd, %region_4.5_spmd} | conditional | flops 10240 | bytes 1073216 | solution.py:521
  14.7 2.0 %collective-permute-done.8 = f32[4,512]{1,0:T(4,128)S(1)} collective-permute-done((f32[4,512]{1,0:T(4,128)S(1)}, f32[4,512]{1,0:T(4,128)S(1)}, u32[]{:S(2)}, u32[]{:S(2)}) %collective-permute-start.8) | collective-permute-done | bytes 8224 | tf_op jit(solution)/shard_map/cond/branch_1_fun/ppermute | solution.py:466
  19.9 2.7 %branch_1_fun.7 = (bf16[128,1024]{1,0:T(8,128)(2,1)}, bf16[128,1024]{1,0:T(8,128)(2,1)}, bf16[128,1024]{1,0:T(8,128)(2,1)}, bf16[128,1024]{1,0:T(8,128)(2,1)}) custom-call(s32[4,512]{1,0:T(4,128)S(1)} %get-tuple-element.54.code_ref, bf16[512,1024]{1,0:T(8,128)(2,1)} %get-tuple-element.55.tokens_ref), custom_call_target="tpu_custom_call" | custom-call | flops 1024 | bytes 1024 | tf_op jit(solution)/shard_map/cond/branch_1_fun/pallas_call | solution.py:155
  22.6 2.4 %collective-permute-done.10 = f32[1,4,512]{2,1,0:T(4,128)S(1)} collective-permute-done((f32[1,4,512]{2,1,0:T(4,128)}, f32[1,4,512]{2,1,0:T(4,128)S(1)}, u32[]{:S(2)}, u32[]{:S(2)}) %collective-permute-start.10) | collective-permute-done | bytes 8224 | tf_op jit(solution)/shard_map/cond/branch_1_fun/ppermute | solution.py:463
  25.7 4.5 %collective-permute-done.12 = bf16[128,1024]{1,0:T(8,128)(2,1)S(1)} collective-permute-done((bf16[128,1024]{1,0:T(8,128)(2,1)}, bf16[128,1024]{1,0:T(8,128)(2,1)S(1)}, u32[]{:S(2)}, u32[]{:S(2)}) %collective-permute-start.12) | collective-permute-done | bytes 262176 | tf_op jit(solution)/shard_map/ppermute | solution.py:463
  30.2 1.9 %conditional.5 = (bf16[256,1024]{1,0:T(8,128)(2,1)}) conditional(s32[]{:T(128)} %convert_element_type.16, () %tuple.52, (s32[2,4]{1,0:T(2,128)S(1)}, s32[2,4]{1,0:T(2,128)S(1)}, bf16[128,1024]{1,0:T(8,128)(2,1)S(1)}, bf16[128,1024]{1,0:T(8,128)(2,1)S(1)}, bf16[128,1024]{1,0:T(8,128)(2,1)S(1)}, /*index=5*/bf16[128,1024]{1,0:T(8,128)(2,1)S(1)}) %tuple.53), branch_computations={%region_6.7_spmd, %region_7.8_spmd} | conditional | flops 1024 | bytes 524298 | solution.py:540
  30.2 1.9 %branch_1_fun.9 = bf16[256,1024]{1,0:T(8,128)(2,1)} custom-call(s32[2,4]{1,0:T(2,128)S(1)} %get-tuple-element.61.offset_ref, s32[2,4]{1,0:T(2,128)S(1)} %get-tuple-element.62.count_ref, bf16[128,1024]{1,0:T(8,128)(2,1)S(1)} %get-tuple-element.63.refs_0_, bf16[128,1024]{1,0:T(8,128)(2,1)S(1)} %get-tuple-element.64.refs_1_, ...), custom_call_target="tpu_custom_call" | custom-call | flops 1024 | bytes 1024 | tf_op jit(solution)/shard_map/cond/branch_1_fun/pallas_call | solution.py:192
  33.8 2.5 %collective-permute-start.14 = (bf16[128,1024]{1,0:T(8,128)(2,1)}, bf16[128,1024]{1,0:T(8,128)(2,1)S(1)}, u32[]{:S(2)}, u32[]{:S(2)}) collective-permute-start(bf16[128,1024]{1,0:T(8,128)(2,1)} %get-tuple-element.180), channel_id=1, source_target_pairs={{0,12},{4,8},{8,4},{12,0},{1,13},{5,9},{9,5},{13,1},{2,14},{6,10},... | collective-permute-start | bytes 786440 | tf_op jit(solution)/shard_map/ppermute | solution.py:463
  36.3 1.9 %collective-permute-start.16 = (bf16[128,1024]{1,0:T(8,128)(2,1)}, bf16[128,1024]{1,0:T(8,128)(2,1)S(1)}, u32[]{:S(2)}, u32[]{:S(2)}) collective-permute-start(bf16[128,1024]{1,0:T(8,128)(2,1)} %get-tuple-element.182), channel_id=1, source_target_pairs={{0,4},{4,0},{8,12},{12,8},{1,5},{5,1},{9,13},{13,9},{2,6},{6,2},{1... | collective-permute-start | bytes 786440 | tf_op jit(solution)/shard_map/ppermute | solution.py:463
  39.9 2.6 %shard_map.74 = (f32[256,256]{1,0:T(8,128)S(1)}, f32[256,256]{1,0:T(8,128)S(1)}, bf16[2,1024,256]{2,1,0:T(8,128)(2,1)S(1)}, bf16[2,1024,256]{2,1,0:T(8,128)(2,1)S(1)}) custom-call(s32[4]{0:T(128)S(1)} %pad_add_fusion.order_ref, bf16[1,4096,256]{2,1,0:T(8,128)(2,1)S(1)} %copy-done, bf16[1,4096,256]{2,1,0:T(8,128)(2,1)S(1)} %copy-done.1, ...), custom_call_target="tpu_custom_call" | custom-call | flops 1024 | bytes 1024 | tf_op jit(solution)/shard_map/pallas_call | solution.py:240
  42.5 4.4 %collective-permute-done.17 = bf16[256,1024]{1,0:T(8,128)(2,1)} collective-permute-done((bf16[256,1024]{1,0:T(8,128)(2,1)}, bf16[256,1024]{1,0:T(8,128)(2,1)}, u32[]{:S(2)}, u32[]{:S(2)}) %collective-permute-start.17) | collective-permute-done | bytes 524320 | tf_op jit(solution)/shard_map/ppermute | solution.py:466
  46.9 11.7 %conditional.6 = (bf16[256,256]{1,0:T(8,128)(2,1)}, bf16[256,256]{1,0:T(8,128)(2,1)}, f32[256,1024]{1,0:T(8,128)S(1)}, bf16[2,256,1024]{2,1,0:T(8,128)(2,1)S(1)}) conditional(s32[]{:T(128)} %convert_element_type.16, () %tuple.51, (bf16[256,1024]{1,0:T(8,128)(2,1)}, f32[256,256]{1,0:T(8,128)S(1)}, f32[256,256]{1,0:T(8,128)S(1)}, ...), branch_computations={%region_8.9_spmd, %region_9.10_spmd} | conditional | flops 2048 | bytes 3672256 | solution.py:540
  46.9 2.1 %collective-permute-done.refs_1_ = bf16[256,1024]{1,0:T(8,128)(2,1)S(1)} collective-permute-done((bf16[256,1024]{1,0:T(8,128)(2,1)}, bf16[256,1024]{1,0:T(8,128)(2,1)S(1)}, u32[]{:S(2)}, u32[]{:S(2)}) %collective-permute-start) | collective-permute-done | bytes 524320 | tf_op jit(solution)/shard_map/cond/branch_1_fun/ppermute | solution.py:466
  54.1 2.8 %collective-permute-done.1 = bf16[256,256]{1,0:T(8,128)(2,1)} collective-permute-done((bf16[256,256]{1,0:T(8,128)(2,1)S(1)}, bf16[256,256]{1,0:T(8,128)(2,1)}, u32[]{:S(2)}, u32[]{:S(2)}) %collective-permute-start.1) | collective-permute-done | bytes 131104 | tf_op jit(solution)/shard_map/cond/branch_1_fun/ppermute | solution.py:466
  58.6 2.0 %shard_map.75.refs_0_ = bf16[256,1024]{1,0:T(8,128)(2,1)S(1)} custom-call(s32[2,4]{1,0:T(2,128)S(1)} %get-tuple-element.241.offset_ref, s32[2,4]{1,0:T(2,128)S(1)} %get-tuple-element.242.count_ref, bf16[128,1024]{1,0:T(8,128)(2,1)} %get-tuple-element.194.refs_0_, bf16[128,1024]{1,0:T(8,128)(2,1)S(1)} %collective-permute-done.14.refs_1_, ...), custom_call_target="tpu_custom_call" | custom-call | flops 1024 | bytes 1024 | tf_op jit(solution)/shard_map/pallas_call | solution.py:192
  62.3 3.1 %shard_map.76 = (bf16[128,1024]{1,0:T(8,128)(2,1)S(1)}, bf16[128,1024]{1,0:T(8,128)(2,1)}, bf16[128,1024]{1,0:T(8,128)(2,1)}, bf16[128,1024]{1,0:T(8,128)(2,1)}) custom-call(s32[2,4]{1,0:T(2,128)S(1)} %get-tuple-element.241.offset_ref, s32[2,4]{1,0:T(2,128)S(1)} %get-tuple-element.242.count_ref, f32[256,1024]{1,0:T(8,128)S(1)} %get-tuple-element.200.before_ref, ...), custom_call_target="tpu_custom_call" | custom-call | flops 1024 | bytes 1024 | tf_op jit(solution)/shard_map/pallas_call | solution.py:360
  65.4 2.6 %collective-permute-start.22 = (bf16[128,1024]{1,0:T(8,128)(2,1)}, bf16[128,1024]{1,0:T(8,128)(2,1)}, u32[]{:S(2)}, u32[]{:S(2)}) collective-permute-start(bf16[128,1024]{1,0:T(8,128)(2,1)} %get-tuple-element.205), channel_id=1, source_target_pairs={{0,12},{4,8},{8,4},{12,0},{1,13},{5,9},{9,5},{13,1},{2,14},{6,10},... | collective-permute-start | bytes 786440 | tf_op jit(solution)/shard_map/ppermute | solution.py:463
  68.0 1.9 %collective-permute-start.24 = (bf16[128,1024]{1,0:T(8,128)(2,1)}, bf16[128,1024]{1,0:T(8,128)(2,1)}, u32[]{:S(2)}, u32[]{:S(2)}) collective-permute-start(bf16[128,1024]{1,0:T(8,128)(2,1)} %get-tuple-element.207), channel_id=1, source_target_pairs={{0,4},{4,0},{8,12},{12,8},{1,5},{5,1},{9,13},{13,9},{2,6},{6,2},{1... | collective-permute-start | bytes 786440 | tf_op jit(solution)/shard_map/ppermute | solution.py:463
  72.1 1.8 %shard_map.77 = (f32[256,256]{1,0:T(8,128)S(1)}, f32[256,256]{1,0:T(8,128)S(1)}, bf16[2,1024,256]{2,1,0:T(8,128)(2,1)S(1)}, bf16[2,1024,256]{2,1,0:T(8,128)(2,1)S(1)}) custom-call(s32[4]{0:T(128)S(1)} %pad_add_fusion.order_ref, bf16[1,4096,256]{2,1,0:T(8,128)(2,1)S(1)} %copy-done, bf16[1,4096,256]{2,1,0:T(8,128)(2,1)S(1)} %copy-done.2, ...), custom_call_target="tpu_custom_call" | custom-call | flops 1024 | bytes 1024 | tf_op jit(solution)/shard_map/pallas_call | solution.py:240
  75.1 11.7 %conditional.7 = (bf16[256,256]{1,0:T(8,128)(2,1)}, bf16[256,256]{1,0:T(8,128)(2,1)}, f32[256,1024]{1,0:T(8,128)S(1)}, bf16[2,256,1024]{2,1,0:T(8,128)(2,1)S(1)}) conditional(s32[]{:T(128)} %convert_element_type.17, () %tuple.48, (bf16[256,1024]{1,0:T(8,128)(2,1)}, f32[256,256]{1,0:T(8,128)S(1)}, f32[256,256]{1,0:T(8,128)S(1)}, ...), branch_computations={%region_10.11_spmd, %region_11.12_spmd} | conditional | flops 2048 | bytes 3672256 | solution.py:540
  75.1 2.1 %collective-permute-done.4.refs_1_ = bf16[256,1024]{1,0:T(8,128)(2,1)S(1)} collective-permute-done((bf16[256,1024]{1,0:T(8,128)(2,1)}, bf16[256,1024]{1,0:T(8,128)(2,1)S(1)}, u32[]{:S(2)}, u32[]{:S(2)}) %collective-permute-start.4) | collective-permute-done | bytes 524320 | tf_op jit(solution)/shard_map/cond/branch_1_fun/ppermute | solution.py:466
  82.3 2.8 %collective-permute-done.5 = bf16[256,256]{1,0:T(8,128)(2,1)} collective-permute-done((bf16[256,256]{1,0:T(8,128)(2,1)S(1)}, bf16[256,256]{1,0:T(8,128)(2,1)}, u32[]{:S(2)}, u32[]{:S(2)}) %collective-permute-start.5) | collective-permute-done | bytes 131104 | tf_op jit(solution)/shard_map/cond/branch_1_fun/ppermute | solution.py:466
  86.8 2.4 %shard_map.78 = (bf16[128,1024]{1,0:T(8,128)(2,1)S(1)}, bf16[128,1024]{1,0:T(8,128)(2,1)S(1)}, bf16[128,1024]{1,0:T(8,128)(2,1)S(1)}, bf16[128,1024]{1,0:T(8,128)(2,1)S(1)}) custom-call(s32[2,4]{1,0:T(2,128)S(1)} %get-tuple-element.241.offset_ref, s32[2,4]{1,0:T(2,128)S(1)} %get-tuple-element.242.count_ref, f32[256,1024]{1,0:T(8,128)S(1)} %get-tuple-element.219.before_ref, ...), custom_call_target="tpu_custom_call" | custom-call | flops 1024 | bytes 1024 | tf_op jit(solution)/shard_map/pallas_call | solution.py:360
  89.2 2.2 %collective-permute-done.21 = f32[2,4,512]{2,1,0:T(4,128)S(1)} collective-permute-done((f32[2,4,512]{2,1,0:T(4,128)S(1)}, f32[2,4,512]{2,1,0:T(4,128)S(1)}, u32[]{:S(2)}, u32[]{:S(2)}) %collective-permute-start.21) | collective-permute-done | bytes 16416 | tf_op jit(solution)/shard_map/ppermute | solution.py:463
  91.5 2.5 %collective-permute-start.25 = (bf16[128,1024]{1,0:T(8,128)(2,1)S(1)}, bf16[128,1024]{1,0:T(8,128)(2,1)S(1)}, u32[]{:S(2)}, u32[]{:S(2)}) collective-permute-start(bf16[128,1024]{1,0:T(8,128)(2,1)S(1)} %get-tuple-element.234), channel_id=1, source_target_pairs={{0,12},{4,8},{8,4},{12,0},{1,13},{5,9},{9,5},{13,1},{2,14},{6,10},... | collective-permute-start | bytes 786440 | tf_op jit(solution)/shard_map/ppermute | solution.py:463
  94.0 1.9 %collective-permute-start.27 = (bf16[128,1024]{1,0:T(8,128)(2,1)S(1)}, bf16[128,1024]{1,0:T(8,128)(2,1)S(1)}, u32[]{:S(2)}, u32[]{:S(2)}) collective-permute-start(bf16[128,1024]{1,0:T(8,128)(2,1)S(1)} %get-tuple-element.236), channel_id=1, source_target_pairs={{0,4},{4,0},{8,12},{12,8},{1,5},{5,1},{9,13},{13,9},{2,6},{6,2},{1... | collective-permute-start | bytes 786440 | tf_op jit(solution)/shard_map/ppermute | solution.py:463
  97.0 1.9 %shard_map.80.refs_0_ = f32[512,1024]{1,0:T(8,128)S(1)} custom-call(s32[4,512]{1,0:T(4,128)S(1)} %get-tuple-element.164.code_ref, f32[4,512]{1,0:T(4,128)S(1)} %shard_map.79.weight_ref, bf16[128,1024]{1,0:T(8,128)(2,1)S(1)} %get-tuple-element.229.refs_0_, bf16[128,1024]{1,0:T(8,128)(2,1)} %collective-permute-done.22.refs_1_, ...), custom_call_target="tpu_custom_call" | custom-call | flops 1024 | bytes 1024 | tf_op jit(solution)/shard_map/pallas_call | solution.py:436
  98.9 3.8 %collective-permute-done.25.refs_2_ = bf16[128,1024]{1,0:T(8,128)(2,1)S(1)} collective-permute-done((bf16[128,1024]{1,0:T(8,128)(2,1)S(1)}, bf16[128,1024]{1,0:T(8,128)(2,1)S(1)}, u32[]{:S(2)}, u32[]{:S(2)}) %collective-permute-start.25) | collective-permute-done | bytes 262176 | tf_op jit(solution)/shard_map/ppermute | solution.py:463
  102.7 14.0 %collective-permute-done.26.refs_3_ = bf16[128,1024]{1,0:T(8,128)(2,1)S(1)} collective-permute-done((bf16[128,1024]{1,0:T(8,128)(2,1)S(1)}, bf16[128,1024]{1,0:T(8,128)(2,1)S(1)}, u32[]{:S(2)}, u32[]{:S(2)}) %collective-permute-start.26) | collective-permute-done | bytes 262176 | tf_op jit(solution)/shard_map/ppermute | solution.py:463
  116.7 1.9 %shard_map.81 = bf16[512,1024]{1,0:T(8,128)(2,1)} custom-call(s32[4,512]{1,0:T(4,128)S(1)} %get-tuple-element.164.code_ref, f32[4,512]{1,0:T(4,128)S(1)} %shard_map.79.weight_ref, f32[512,1024]{1,0:T(8,128)S(1)} %shard_map.80.refs_0_, bf16[128,1024]{1,0:T(8,128)(2,1)S(1)} %get-tuple-element.233.refs_1_, ...), custom_call_target="tpu_custom_call" | custom-call | flops 1024 | bytes 1024 | tf_op jit(solution)/shard_map/pallas_call | solution.py:436
  (65 shorter events, 32.5 us)
Async XLA Ops:
  2.6 23.1 %collective-permute-start.11 = (bf16[128,1024]{1,0:T(8,128)(2,1)}, bf16[128,1024]{1,0:T(8,128)(2,1)S(1)}, u32[]{:S(2)}, u32[]{:S(2)}) collective-permute-start(bf16[128,1024]{1,0:T(8,128)(2,1)} %get-tuple-element.171), channel_id=1, source_target_pairs={{0,12},{4,8},{8,4},{12,0},{1,13},{5,9},{9,5},{13,1},{2,14},{6,10},... | collective-permute-start | bytes 786440 | tf_op jit(solution)/shard_map/ppermute | solution.py:463
  7.7 22.5 %collective-permute-start.12 = (bf16[128,1024]{1,0:T(8,128)(2,1)}, bf16[128,1024]{1,0:T(8,128)(2,1)S(1)}, u32[]{:S(2)}, u32[]{:S(2)}) collective-permute-start(bf16[128,1024]{1,0:T(8,128)(2,1)} %get-tuple-element.172), channel_id=1, source_target_pairs={{0,8},{4,12},{8,0},{12,4},{1,9},{5,13},{9,1},{13,5},{2,10},{6,14},... | collective-permute-start | bytes 786440 | tf_op jit(solution)/shard_map/ppermute | solution.py:463
  7.7 22.5 %collective-permute-start.13 = (bf16[128,1024]{1,0:T(8,128)(2,1)}, bf16[128,1024]{1,0:T(8,128)(2,1)S(1)}, u32[]{:S(2)}, u32[]{:S(2)}) collective-permute-start(bf16[128,1024]{1,0:T(8,128)(2,1)} %get-tuple-element.173), channel_id=1, source_target_pairs={{0,4},{4,0},{8,12},{12,8},{1,5},{5,1},{9,13},{13,9},{2,6},{6,2},{1... | collective-permute-start | bytes 786440 | tf_op jit(solution)/shard_map/ppermute | solution.py:463
  11.2 27.0 %copy-start = (bf16[1,4096,256]{2,1,0:T(8,128)(2,1)S(1)}, bf16[1,4096,256]{2,1,0:T(8,128)(2,1)}, u32[]{:S(2)}) copy-start(bf16[1,4096,256]{2,1,0:T(8,128)(2,1)} %gate_ref.3) | copy-start | bytes 6291460
  13.0 3.7 %collective-permute-start.8 = (f32[4,512]{1,0:T(4,128)S(1)}, f32[4,512]{1,0:T(4,128)S(1)}, u32[]{:S(2)}, u32[]{:S(2)}) collective-permute-start(f32[4,512]{1,0:T(4,128)S(1)} %branch_1_fun.8), channel_id=1, source_target_pairs={{0,2},{1,3},{2,0},{3,1},{4,6},{5,7},{6,4},{7,5},{8,10},{9,11},{10,... | collective-permute-start | bytes 24584 | tf_op jit(solution)/shard_map/cond/branch_1_fun/ppermute | solution.py:466
  16.7 1.2 collective-permute-start.9
  18.5 6.5 %collective-permute-start.10 = (f32[1,4,512]{2,1,0:T(4,128)}, f32[1,4,512]{2,1,0:T(4,128)S(1)}, u32[]{:S(2)}, u32[]{:S(2)}) collective-permute-start(f32[1,4,512]{2,1,0:T(4,128)} %bitcast), channel_id=1, source_target_pairs={{0,4},{4,0},{8,12},{12,8},{1,5},{5,1},{9,13},{13,9},{2,6},{6,2},{1... | collective-permute-start | bytes 24584 | tf_op jit(solution)/shard_map/cond/branch_1_fun/ppermute | solution.py:463
  32.2 6.1 %collective-permute-start.18 = (bf16[256,1024]{1,0:T(8,128)(2,1)}, bf16[256,1024]{1,0:T(8,128)(2,1)S(1)}, u32[]{:S(2)}, u32[]{:S(2)}) collective-permute-start(bf16[256,1024]{1,0:T(8,128)(2,1)} %get-tuple-element.275.refs_0_), channel_id=1, source_target_pairs={{0,1},{1,0},{2,3},{3,2},{4,5},{5,4},{6,7},{7,6},{8,9},{9,8},{10,11... | collective-permute-start | bytes 1572872 | tf_op jit(solution)/shard_map/ppermute | solution.py:466
  32.3 14.7 %collective-permute-start.17 = (bf16[256,1024]{1,0:T(8,128)(2,1)}, bf16[256,1024]{1,0:T(8,128)(2,1)}, u32[]{:S(2)}, u32[]{:S(2)}) collective-permute-start(bf16[256,1024]{1,0:T(8,128)(2,1)} %get-tuple-element.275.refs_0_), channel_id=1, source_target_pairs={{0,2},{1,3},{2,0},{3,1},{4,6},{5,7},{6,4},{7,5},{8,10},{9,11},{10,... | collective-permute-start | bytes 1572872 | tf_op jit(solution)/shard_map/ppermute | solution.py:466
  33.8 24.8 %collective-permute-start.14 = (bf16[128,1024]{1,0:T(8,128)(2,1)}, bf16[128,1024]{1,0:T(8,128)(2,1)S(1)}, u32[]{:S(2)}, u32[]{:S(2)}) collective-permute-start(bf16[128,1024]{1,0:T(8,128)(2,1)} %get-tuple-element.180), channel_id=1, source_target_pairs={{0,12},{4,8},{8,4},{12,0},{1,13},{5,9},{9,5},{13,1},{2,14},{6,10},... | collective-permute-start | bytes 786440 | tf_op jit(solution)/shard_map/ppermute | solution.py:463
  36.3 22.3 %collective-permute-start.15 = (bf16[128,1024]{1,0:T(8,128)(2,1)}, bf16[128,1024]{1,0:T(8,128)(2,1)S(1)}, u32[]{:S(2)}, u32[]{:S(2)}) collective-permute-start(bf16[128,1024]{1,0:T(8,128)(2,1)} %get-tuple-element.181), channel_id=1, source_target_pairs={{0,8},{4,12},{8,0},{12,4},{1,9},{5,13},{9,1},{13,5},{2,10},{6,14},... | collective-permute-start | bytes 786440 | tf_op jit(solution)/shard_map/ppermute | solution.py:463
  36.3 22.3 %collective-permute-start.16 = (bf16[128,1024]{1,0:T(8,128)(2,1)}, bf16[128,1024]{1,0:T(8,128)(2,1)S(1)}, u32[]{:S(2)}, u32[]{:S(2)}) collective-permute-start(bf16[128,1024]{1,0:T(8,128)(2,1)} %get-tuple-element.182), channel_id=1, source_target_pairs={{0,4},{4,0},{8,12},{12,8},{1,5},{5,1},{9,13},{13,9},{2,6},{6,2},{1... | collective-permute-start | bytes 786440 | tf_op jit(solution)/shard_map/ppermute | solution.py:463
  38.3 1.6 %copy-start.1 = (bf16[1,4096,256]{2,1,0:T(8,128)(2,1)S(1)}, bf16[1,4096,256]{2,1,0:T(8,128)(2,1)}, u32[]{:S(2)}) copy-start(bf16[1,4096,256]{2,1,0:T(8,128)(2,1)} %up_ref.3) | copy-start | bytes 6291460
  39.9 7.0 %copy-start.3 = (bf16[1,1024,1024]{2,1,0:T(8,128)(2,1)S(1)}, bf16[1,1024,1024]{2,1,0:T(8,128)(2,1)}, u32[]{:S(2)}) copy-start(bf16[1,1024,1024]{2,1,0:T(8,128)(2,1)} %param.19) | copy-start | bytes 6291460
  46.9 2.1 %collective-permute-start = (bf16[256,1024]{1,0:T(8,128)(2,1)}, bf16[256,1024]{1,0:T(8,128)(2,1)S(1)}, u32[]{:S(2)}, u32[]{:S(2)}) collective-permute-start(bf16[256,1024]{1,0:T(8,128)(2,1)} %get-tuple-element.71.refs_0_), channel_id=1, source_target_pairs={{0,1},{1,0},{2,3},{3,2},{4,5},{5,4},{6,7},{7,6},{8,9},{9,8},{10,11... | collective-permute-start | bytes 1572872 | tf_op jit(solution)/shard_map/cond/branch_1_fun/ppermute | solution.py:466
  50.8 1.7 %collective-permute-start.2 = (bf16[256,256]{1,0:T(8,128)(2,1)S(1)}, bf16[256,256]{1,0:T(8,128)(2,1)S(1)}, u32[]{:S(2)}, u32[]{:S(2)}) collective-permute-start(bf16[256,256]{1,0:T(8,128)(2,1)S(1)} %branch_1_fun.10.refs_0_), channel_id=1, source_target_pairs={{0,1},{1,0},{2,3},{3,2},{4,5},{5,4},{6,7},{7,6},{8,9},{9,8},{10,11... | collective-permute-start | bytes 393224 | tf_op jit(solution)/shard_map/cond/branch_1_fun/ppermute | solution.py:466
  51.0 5.9 %collective-permute-start.1 = (bf16[256,256]{1,0:T(8,128)(2,1)S(1)}, bf16[256,256]{1,0:T(8,128)(2,1)}, u32[]{:S(2)}, u32[]{:S(2)}) collective-permute-start(bf16[256,256]{1,0:T(8,128)(2,1)S(1)} %branch_1_fun.10.refs_0_), channel_id=1, source_target_pairs={{0,2},{1,3},{2,0},{3,1},{4,6},{5,7},{6,4},{7,5},{8,10},{9,11},{10,... | collective-permute-start | bytes 393224 | tf_op jit(solution)/shard_map/cond/branch_1_fun/ppermute | solution.py:466
  56.9 1.7 %collective-permute-start.3 = (bf16[256,256]{1,0:T(8,128)(2,1)}, bf16[256,256]{1,0:T(8,128)(2,1)}, u32[]{:S(2)}, u32[]{:S(2)}) collective-permute-start(bf16[256,256]{1,0:T(8,128)(2,1)} %collective-permute-done.1), channel_id=1, source_target_pairs={{0,1},{1,0},{2,3},{3,2},{4,5},{5,4},{6,7},{7,6},{8,9},{9,8},{10,11... | collective-permute-start | bytes 393224 | tf_op jit(solution)/shard_map/cond/branch_1_fun/ppermute | solution.py:466
  60.6 9.9 %collective-permute-start.20 = (bf16[256,1024]{1,0:T(8,128)(2,1)S(1)}, bf16[256,1024]{1,0:T(8,128)(2,1)S(1)}, u32[]{:S(2)}, u32[]{:S(2)}) collective-permute-start(bf16[256,1024]{1,0:T(8,128)(2,1)S(1)} %shard_map.75.refs_0_), channel_id=1, source_target_pairs={{0,1},{1,0},{2,3},{3,2},{4,5},{5,4},{6,7},{7,6},{8,9},{9,8},{10,11... | collective-permute-start | bytes 1572872 | tf_op jit(solution)/shard_map/ppermute | solution.py:466
  60.8 14.3 %collective-permute-start.19 = (bf16[256,1024]{1,0:T(8,128)(2,1)S(1)}, bf16[256,1024]{1,0:T(8,128)(2,1)}, u32[]{:S(2)}, u32[]{:S(2)}) collective-permute-start(bf16[256,1024]{1,0:T(8,128)(2,1)S(1)} %shard_map.75.refs_0_), channel_id=1, source_target_pairs={{0,2},{1,3},{2,0},{3,1},{4,6},{5,7},{6,4},{7,5},{8,10},{9,11},{10,... | collective-permute-start | bytes 1572872 | tf_op jit(solution)/shard_map/ppermute | solution.py:466
  65.4 26.0 %collective-permute-start.22 = (bf16[128,1024]{1,0:T(8,128)(2,1)}, bf16[128,1024]{1,0:T(8,128)(2,1)}, u32[]{:S(2)}, u32[]{:S(2)}) collective-permute-start(bf16[128,1024]{1,0:T(8,128)(2,1)} %get-tuple-element.205), channel_id=1, source_target_pairs={{0,12},{4,8},{8,4},{12,0},{1,13},{5,9},{9,5},{13,1},{2,14},{6,10},... | collective-permute-start | bytes 786440 | tf_op jit(solution)/shard_map/ppermute | solution.py:463
  68.0 23.5 %collective-permute-start.23 = (bf16[128,1024]{1,0:T(8,128)(2,1)}, bf16[128,1024]{1,0:T(8,128)(2,1)}, u32[]{:S(2)}, u32[]{:S(2)}) collective-permute-start(bf16[128,1024]{1,0:T(8,128)(2,1)} %get-tuple-element.206), channel_id=1, source_target_pairs={{0,8},{4,12},{8,0},{12,4},{1,9},{5,13},{9,1},{13,5},{2,10},{6,14},... | collective-permute-start | bytes 786440 | tf_op jit(solution)/shard_map/ppermute | solution.py:463
  68.0 23.5 %collective-permute-start.24 = (bf16[128,1024]{1,0:T(8,128)(2,1)}, bf16[128,1024]{1,0:T(8,128)(2,1)}, u32[]{:S(2)}, u32[]{:S(2)}) collective-permute-start(bf16[128,1024]{1,0:T(8,128)(2,1)} %get-tuple-element.207), channel_id=1, source_target_pairs={{0,4},{4,0},{8,12},{12,8},{1,5},{5,1},{9,13},{13,9},{2,6},{6,2},{1... | collective-permute-start | bytes 786440 | tf_op jit(solution)/shard_map/ppermute | solution.py:463
  72.1 3.0 %copy-start.4 = (bf16[1,1024,1024]{2,1,0:T(8,128)(2,1)S(1)}, bf16[1,1024,1024]{2,1,0:T(8,128)(2,1)}, u32[]{:S(2)}) copy-start(bf16[1,1024,1024]{2,1,0:T(8,128)(2,1)} %param.19) | copy-start | bytes 6291460
  75.1 2.1 %collective-permute-start.4 = (bf16[256,1024]{1,0:T(8,128)(2,1)}, bf16[256,1024]{1,0:T(8,128)(2,1)S(1)}, u32[]{:S(2)}, u32[]{:S(2)}) collective-permute-start(bf16[256,1024]{1,0:T(8,128)(2,1)} %get-tuple-element.83.refs_0_), channel_id=1, source_target_pairs={{0,1},{1,0},{2,3},{3,2},{4,5},{5,4},{6,7},{7,6},{8,9},{9,8},{10,11... | collective-permute-start | bytes 1572872 | tf_op jit(solution)/shard_map/cond/branch_1_fun/ppermute | solution.py:466
  79.0 1.7 %collective-permute-start.6 = (bf16[256,256]{1,0:T(8,128)(2,1)S(1)}, bf16[256,256]{1,0:T(8,128)(2,1)S(1)}, u32[]{:S(2)}, u32[]{:S(2)}) collective-permute-start(bf16[256,256]{1,0:T(8,128)(2,1)S(1)} %branch_1_fun.12.refs_0_), channel_id=1, source_target_pairs={{0,1},{1,0},{2,3},{3,2},{4,5},{5,4},{6,7},{7,6},{8,9},{9,8},{10,11... | collective-permute-start | bytes 393224 | tf_op jit(solution)/shard_map/cond/branch_1_fun/ppermute | solution.py:466
  79.2 5.9 %collective-permute-start.5 = (bf16[256,256]{1,0:T(8,128)(2,1)S(1)}, bf16[256,256]{1,0:T(8,128)(2,1)}, u32[]{:S(2)}, u32[]{:S(2)}) collective-permute-start(bf16[256,256]{1,0:T(8,128)(2,1)S(1)} %branch_1_fun.12.refs_0_), channel_id=1, source_target_pairs={{0,2},{1,3},{2,0},{3,1},{4,6},{5,7},{6,4},{7,5},{8,10},{9,11},{10,... | collective-permute-start | bytes 393224 | tf_op jit(solution)/shard_map/cond/branch_1_fun/ppermute | solution.py:466
  85.1 1.7 %collective-permute-start.7 = (bf16[256,256]{1,0:T(8,128)(2,1)}, bf16[256,256]{1,0:T(8,128)(2,1)}, u32[]{:S(2)}, u32[]{:S(2)}) collective-permute-start(bf16[256,256]{1,0:T(8,128)(2,1)} %collective-permute-done.5), channel_id=1, source_target_pairs={{0,1},{1,0},{2,3},{3,2},{4,5},{5,4},{6,7},{7,6},{8,9},{9,8},{10,11... | collective-permute-start | bytes 393224 | tf_op jit(solution)/shard_map/cond/branch_1_fun/ppermute | solution.py:466
  86.8 4.6 %collective-permute-start.21 = (f32[2,4,512]{2,1,0:T(4,128)S(1)}, f32[2,4,512]{2,1,0:T(4,128)S(1)}, u32[]{:S(2)}, u32[]{:S(2)}) collective-permute-start(f32[2,4,512]{2,1,0:T(4,128)S(1)} %get-tuple-element.227), channel_id=1, source_target_pairs={{0,8},{4,12},{8,0},{12,4},{1,9},{5,13},{9,1},{13,5},{2,10},{6,14},... | collective-permute-start | bytes 49160 | tf_op jit(solution)/shard_map/ppermute | solution.py:463
  91.5 11.2 %collective-permute-start.25 = (bf16[128,1024]{1,0:T(8,128)(2,1)S(1)}, bf16[128,1024]{1,0:T(8,128)(2,1)S(1)}, u32[]{:S(2)}, u32[]{:S(2)}) collective-permute-start(bf16[128,1024]{1,0:T(8,128)(2,1)S(1)} %get-tuple-element.234), channel_id=1, source_target_pairs={{0,12},{4,8},{8,4},{12,0},{1,13},{5,9},{9,5},{13,1},{2,14},{6,10},... | collective-permute-start | bytes 786440 | tf_op jit(solution)/shard_map/ppermute | solution.py:463
  94.0 22.7 %collective-permute-start.26 = (bf16[128,1024]{1,0:T(8,128)(2,1)S(1)}, bf16[128,1024]{1,0:T(8,128)(2,1)S(1)}, u32[]{:S(2)}, u32[]{:S(2)}) collective-permute-start(bf16[128,1024]{1,0:T(8,128)(2,1)S(1)} %get-tuple-element.235), channel_id=1, source_target_pairs={{0,8},{4,12},{8,0},{12,4},{1,9},{5,13},{9,1},{13,5},{2,10},{6,14},... | collective-permute-start | bytes 786440 | tf_op jit(solution)/shard_map/ppermute | solution.py:463
  94.0 22.7 %collective-permute-start.27 = (bf16[128,1024]{1,0:T(8,128)(2,1)S(1)}, bf16[128,1024]{1,0:T(8,128)(2,1)S(1)}, u32[]{:S(2)}, u32[]{:S(2)}) collective-permute-start(bf16[128,1024]{1,0:T(8,128)(2,1)S(1)} %get-tuple-element.236), channel_id=1, source_target_pairs={{0,4},{4,0},{8,12},{12,8},{1,5},{5,1},{9,13},{13,9},{2,6},{6,2},{1... | collective-permute-start | bytes 786440 | tf_op jit(solution)/shard_map/ppermute | solution.py:463
  (1 other events, 1.6 us)

commit v12 on v11

--- a/solution.py
+++ b/solution.py
@@ -505,20 +505,19 @@
     present = [jnp.sum(counts[k]) > 0 for k in range(BATCHES)]
 
     def beside_first(router):
-        logits = partial_logits(router, tokens)
+        gathered = partial_logits(router, tokens)[None]
+        for bit in expert_bits:
+            gathered = jnp.concatenate([gathered, along_expert(gathered, bit)])
         later = [tuple(later_batch(code, tokens, k, depth)) for k in range(1, BATCHES)]
         for bit in bits:
-            logits = logits + swap(logits, bit)
-        gathered = logits[None]
-        for bit in expert_bits[:-1]:
-            gathered = jnp.concatenate([gathered, along_expert(gathered, bit)])
-        return later, logits, gathered
+            gathered = gathered + swap(gathered, bit)
+        return later, gathered
 
     def nothing_first(router):
         return jax.tree.map(lambda x: jnp.zeros(x.shape, x.dtype), jax.eval_shape(beside_first, router))
 
     arrived = [exchange(first)]
-    later, logits, gathered = lax.cond(present[0], beside_first, nothing_first, router_weight.T)
+    later, gathered = lax.cond(present[0], beside_first, nothing_first, router_weight.T)
 
     def far_half(far, sums):
         far = spread(far)
@@ -562,15 +561,12 @@
             near = after(near, results)
         sums = gate_up_near(order, near_places, far_places, gate_weight, up_weight, near)
         across, sums = lax.optimization_barrier((across, sums))
-        if k == BATCHES - 1:
-            gathered = after(gathered, sums)
-            gathered = jnp.concatenate([gathered, along_expert(gathered, expert_bits[-1])])
         far, partial = fenced(k, far_half, across, sums)
         moved = partial
     results = settle(BATCHES - 1, far, partial)
     results, gathered, waiting[-1] = lax.optimization_barrier((results, gathered, waiting[-1]))
     waiting.append(exchange(results))
-    weights = slot_weights(place, logits, gathered, code)
+    weights = slot_weights(place, gathered[0], gathered, code)
     total = None
     for k in range(BATCHES):
         total = combine(code, weights, k, waiting[k], total)

time: 119 us -> 125 us (1.050)
  waiting for transfers between devices: 49 us -> 57.3 us
  other arithmetic: 2.95 us -> 1.68 us
    ppermute x14, waiting for transfers between devices: 27 us -> 34.4 us  [along_expert(): return lax.ppermute(x, 'expert', [(i, i ^ shift) for i in range(experts)])]
    ppermute x14, starting transfers between devices: 8.41 us -> 6.77 us  [swap(): return lax.ppermute(x, 'dp', [(i, i ^ bit) for i in range(width_parts)])]
  transfers between devices with their start and end apart: 28 -> 28, of which waited for: 15 -> 16; matrix products, arithmetic and copies ran while one was open for 3% -> 2% of each run, Pallas kernels for 20% -> 19%
where the time goes in v12:
time: 125 us
  waiting for transfers between devices  57.3 us (46%)
  Pallas kernels  31.7 us (25%)
  starting transfers between devices  28.5 us (23%)
  local copies, waits for them, and re-layouts  3.89 us (3%)
  other arithmetic  1.68 us (1%)
  between operations  1.6 us (1%)
    ppermute x14, waiting for transfers between devices, along_expert(): return lax.ppermute(x, 'expert', [(i, i ^ shift) for i in range(experts)])  34.4 us
    ppermute x14, waiting for transfers between devices, swap(): return lax.ppermute(x, 'dp', [(i, i ^ bit) for i in range(width_parts)])  22.9 us
    ppermute x14, starting transfers between devices, along_expert(): return lax.ppermute(x, 'expert', [(i, i ^ shift) for i in range(experts)])  21.7 us
    ppermute x14, starting transfers between devices, swap(): return lax.ppermute(x, 'dp', [(i, i ^ bit) for i in range(width_parts)])  6.77 us
    pallas_call x2, Pallas kernels, down_last(): pl.pallas_call(functools.partial(down_last_kernel, parts, experts, k, dir...  5.48 us
    pallas_call x2, Pallas kernels, gate_up_near(): pl.pallas_call(functools.partial(gate_up_near_kernel, parts, near, far),...  4.4 us
    pallas_call x2, Pallas kernels, compact(): pl.pallas_call(functools.partial(compact_kernel, experts, k), out_shape=j...  3.94 us
    pallas_call x2, Pallas kernels, combine(): pl.pallas_call(functools.partial(combine_kernel, experts, k), out_shape=j...  3.83 us
  transfers between devices with their start and end apart: 28, of which 16 were waited for; matrix products, arithmetic and copies ran while one was open for 2% of the time, Pallas kernels for 19%

profile of v12, /device:TPU:0, one launch (start us, length us, event | category | flops | bytes accessed | tf_op | source)
XLA Modules:
  0.0 124.8 jit_solution(8039560276667844434)
XLA Ops:
  0.0 2.6 %shard_map.73 = (s32[4,512]{1,0:T(4,128)S(1)}, bf16[128,1024]{1,0:T(8,128)(2,1)S(1)}, bf16[128,1024]{1,0:T(8,128)(2,1)}, bf16[128,1024]{1,0:T(8,128)(2,1)}, bf16[128,1024]{1,0:T(8,128)(2,1)}) custom-call(s32[1]{0:T(128)} %bitcast.1.place_ref, s32[4,512]{1,0:T(4,128)} %picks_in.1, bf16[512,1024]{1,0:T(8,128)(2,1)} %tokens_ref.1), custom_call_target="tpu_custom_call" | custom-call | flops 1024 | bytes 1024 | tf_op jit(solution)/shard_map/pallas_call | solution.py:108
  2.6 5.1 %collective-permute-start.12 = (bf16[128,1024]{1,0:T(8,128)(2,1)}, bf16[128,1024]{1,0:T(8,128)(2,1)S(1)}, u32[]{:S(2)}, u32[]{:S(2)}) collective-permute-start(bf16[128,1024]{1,0:T(8,128)(2,1)} %get-tuple-element.168), channel_id=1, source_target_pairs={{0,12},{4,8},{8,4},{12,0},{1,13},{5,9},{9,5},{13,1},{2,14},{6,10},... | collective-permute-start | bytes 786440 | tf_op jit(solution)/shard_map/ppermute | solution.py:463
  11.3 26.3 %conditional.4 = (bf16[128,1024]{1,0:T(8,128)(2,1)}, bf16[128,1024]{1,0:T(8,128)(2,1)}, bf16[128,1024]{1,0:T(8,128)(2,1)}, bf16[128,1024]{1,0:T(8,128)(2,1)}, f32[4,4,512]{2,1,0:T(4,128)S(1)}) conditional(s32[]{:T(128)} %convert_element_type.17, () %tuple.46, (s32[4,512]{1,0:T(4,128)S(1)}, bf16[512,1024]{1,0:T(8,128)(2,1)}, ...), branch_computations={%region_4.5_spmd, %region_5.6_spmd} | conditional | flops 55296 | bytes 1081396 | solution.py:520
  11.3 1.8 %branch_1_fun.8 = f32[4,512]{1,0:T(4,128)S(1)} custom-call(bf16[4,1024]{1,0:T(4,128)(2,1)} %get-tuple-element.60.router_ref, bf16[512,1024]{1,0:T(8,128)(2,1)} %get-tuple-element.55.tokens_ref), custom_call_target="tpu_custom_call" | custom-call | flops 1024 | bytes 1024 | tf_op jit(solution)/shard_map/cond/branch_1_fun/pallas_call | solution.py:134
  14.4 10.6 %collective-permute-done.8 = f32[1,4,512]{2,1,0:T(4,128)S(1)} collective-permute-done((f32[1,4,512]{2,1,0:T(4,128)S(1)}, f32[1,4,512]{2,1,0:T(4,128)S(1)}, u32[]{:S(2)}, u32[]{:S(2)}) %collective-permute-start.8) | collective-permute-done | bytes 8224 | tf_op jit(solution)/shard_map/cond/branch_1_fun/ppermute | solution.py:463
  26.3 4.5 %collective-permute-done.9 = f32[2,4,512]{2,1,0:T(4,128)S(1)} collective-permute-done((f32[2,4,512]{2,1,0:T(4,128)S(1)}, f32[2,4,512]{2,1,0:T(4,128)S(1)}, u32[]{:S(2)}, u32[]{:S(2)}) %collective-permute-start.9) | collective-permute-done | bytes 16416 | tf_op jit(solution)/shard_map/cond/branch_1_fun/ppermute | solution.py:463
  32.3 2.4 %collective-permute-done.10 = f32[4,4,512]{2,1,0:T(4,128)S(1)} collective-permute-done((f32[4,4,512]{2,1,0:T(4,128)S(1)}, f32[4,4,512]{2,1,0:T(4,128)S(1)}, u32[]{:S(2)}, u32[]{:S(2)}) %collective-permute-start.10) | collective-permute-done | bytes 32800 | tf_op jit(solution)/shard_map/cond/branch_1_fun/ppermute | solution.py:466
  34.8 2.7 %branch_1_fun.7 = (bf16[128,1024]{1,0:T(8,128)(2,1)}, bf16[128,1024]{1,0:T(8,128)(2,1)}, bf16[128,1024]{1,0:T(8,128)(2,1)}, bf16[128,1024]{1,0:T(8,128)(2,1)}) custom-call(s32[4,512]{1,0:T(4,128)S(1)} %get-tuple-element.54.code_ref, bf16[512,1024]{1,0:T(8,128)(2,1)} %get-tuple-element.55.tokens_ref), custom_call_target="tpu_custom_call" | custom-call | flops 1024 | bytes 1024 | tf_op jit(solution)/shard_map/cond/branch_1_fun/pallas_call | solution.py:155
  37.6 2.0 %conditional.5 = (bf16[256,1024]{1,0:T(8,128)(2,1)}) conditional(s32[]{:T(128)} %convert_element_type.17, () %tuple.51, (s32[2,4]{1,0:T(2,128)S(1)}, s32[2,4]{1,0:T(2,128)S(1)}, bf16[128,1024]{1,0:T(8,128)(2,1)S(1)}, bf16[128,1024]{1,0:T(8,128)(2,1)S(1)}, bf16[128,1024]{1,0:T(8,128)(2,1)S(1)}, /*index=5*/bf16[128,1024]{1,0:T(8,128)(2,1)S(1)}) %tuple.52), branch_computations={%region_6.7_spmd, %region_7.8_spmd} | conditional | flops 1024 | bytes 524298 | solution.py:539
  37.6 1.9 %branch_1_fun.9 = bf16[256,1024]{1,0:T(8,128)(2,1)} custom-call(s32[2,4]{1,0:T(2,128)S(1)} %get-tuple-element.61.offset_ref, s32[2,4]{1,0:T(2,128)S(1)} %get-tuple-element.62.count_ref, bf16[128,1024]{1,0:T(8,128)(2,1)S(1)} %get-tuple-element.63.refs_0_, bf16[128,1024]{1,0:T(8,128)(2,1)S(1)} %get-tuple-element.64.refs_1_, ...), custom_call_target="tpu_custom_call" | custom-call | flops 1024 | bytes 1024 | tf_op jit(solution)/shard_map/cond/branch_1_fun/pallas_call | solution.py:192
  41.6 2.6 %collective-permute-start.15 = (bf16[128,1024]{1,0:T(8,128)(2,1)}, bf16[128,1024]{1,0:T(8,128)(2,1)S(1)}, u32[]{:S(2)}, u32[]{:S(2)}) collective-permute-start(bf16[128,1024]{1,0:T(8,128)(2,1)} %get-tuple-element.177), channel_id=1, source_target_pairs={{0,12},{4,8},{8,4},{12,0},{1,13},{5,9},{9,5},{13,1},{2,14},{6,10},... | collective-permute-start | bytes 786440 | tf_op jit(solution)/shard_map/ppermute | solution.py:463
  47.7 2.6 %shard_map.74 = (f32[256,256]{1,0:T(8,128)S(1)}, f32[256,256]{1,0:T(8,128)S(1)}, bf16[2,1024,256]{2,1,0:T(8,128)(2,1)S(1)}, bf16[2,1024,256]{2,1,0:T(8,128)(2,1)S(1)}) custom-call(s32[4]{0:T(128)S(1)} %pad_add_fusion.order_ref, bf16[1,4096,256]{2,1,0:T(8,128)(2,1)S(1)} %copy-done, bf16[1,4096,256]{2,1,0:T(8,128)(2,1)S(1)} %copy-done.1, ...), custom_call_target="tpu_custom_call" | custom-call | flops 1024 | bytes 1024 | tf_op jit(solution)/shard_map/pallas_call | solution.py:240
  50.3 4.1 %collective-permute-done.18 = bf16[256,1024]{1,0:T(8,128)(2,1)} collective-permute-done((bf16[256,1024]{1,0:T(8,128)(2,1)}, bf16[256,1024]{1,0:T(8,128)(2,1)}, u32[]{:S(2)}, u32[]{:S(2)}) %collective-permute-start.18) | collective-permute-done | bytes 524320 | tf_op jit(solution)/shard_map/ppermute | solution.py:466
  54.4 11.7 %conditional.6 = (bf16[256,256]{1,0:T(8,128)(2,1)}, bf16[256,256]{1,0:T(8,128)(2,1)}, f32[256,1024]{1,0:T(8,128)S(1)}, bf16[2,256,1024]{2,1,0:T(8,128)(2,1)S(1)}) conditional(s32[]{:T(128)} %convert_element_type.17, () %tuple.50, (bf16[256,1024]{1,0:T(8,128)(2,1)}, f32[256,256]{1,0:T(8,128)S(1)}, f32[256,256]{1,0:T(8,128)S(1)}, ...), branch_computations={%region_8.9_spmd, %region_9.10_spmd} | conditional | flops 2048 | bytes 3672256 | solution.py:539
  54.4 2.1 %collective-permute-done.refs_1_ = bf16[256,1024]{1,0:T(8,128)(2,1)S(1)} collective-permute-done((bf16[256,1024]{1,0:T(8,128)(2,1)}, bf16[256,1024]{1,0:T(8,128)(2,1)S(1)}, u32[]{:S(2)}, u32[]{:S(2)}) %collective-permute-start) | collective-permute-done | bytes 524320 | tf_op jit(solution)/shard_map/cond/branch_1_fun/ppermute | solution.py:466
  61.6 2.8 %collective-permute-done.1 = bf16[256,256]{1,0:T(8,128)(2,1)} collective-permute-done((bf16[256,256]{1,0:T(8,128)(2,1)S(1)}, bf16[256,256]{1,0:T(8,128)(2,1)}, u32[]{:S(2)}, u32[]{:S(2)}) %collective-permute-start.1) | collective-permute-done | bytes 131104 | tf_op jit(solution)/shard_map/cond/branch_1_fun/ppermute | solution.py:466
  67.5 2.0 %shard_map.75.refs_0_ = bf16[256,1024]{1,0:T(8,128)(2,1)S(1)} custom-call(s32[2,4]{1,0:T(2,128)S(1)} %get-tuple-element.238.offset_ref, s32[2,4]{1,0:T(2,128)S(1)} %get-tuple-element.237.count_ref, bf16[128,1024]{1,0:T(8,128)(2,1)} %get-tuple-element.191.refs_0_, bf16[128,1024]{1,0:T(8,128)(2,1)S(1)} %collective-permute-done.15.refs_1_, ...), custom_call_target="tpu_custom_call" | custom-call | flops 1024 | bytes 1024 | tf_op jit(solution)/shard_map/pallas_call | solution.py:192
  70.2 3.1 %shard_map.76 = (bf16[128,1024]{1,0:T(8,128)(2,1)S(1)}, bf16[128,1024]{1,0:T(8,128)(2,1)}, bf16[128,1024]{1,0:T(8,128)(2,1)}, bf16[128,1024]{1,0:T(8,128)(2,1)}) custom-call(s32[2,4]{1,0:T(2,128)S(1)} %get-tuple-element.238.offset_ref, s32[2,4]{1,0:T(2,128)S(1)} %get-tuple-element.237.count_ref, f32[256,1024]{1,0:T(8,128)S(1)} %get-tuple-element.197.before_ref, ...), custom_call_target="tpu_custom_call" | custom-call | flops 1024 | bytes 1024 | tf_op jit(solution)/shard_map/pallas_call | solution.py:360
  73.3 2.3 %collective-permute-start.22 = (bf16[128,1024]{1,0:T(8,128)(2,1)}, bf16[128,1024]{1,0:T(8,128)(2,1)}, u32[]{:S(2)}, u32[]{:S(2)}) collective-permute-start(bf16[128,1024]{1,0:T(8,128)(2,1)} %get-tuple-element.202), channel_id=1, source_target_pairs={{0,12},{4,8},{8,4},{12,0},{1,13},{5,9},{9,5},{13,1},{2,14},{6,10},... | collective-permute-start | bytes 786440 | tf_op jit(solution)/shard_map/ppermute | solution.py:463
  75.8 2.0 %collective-permute-start.24 = (bf16[128,1024]{1,0:T(8,128)(2,1)}, bf16[128,1024]{1,0:T(8,128)(2,1)}, u32[]{:S(2)}, u32[]{:S(2)}) collective-permute-start(bf16[128,1024]{1,0:T(8,128)(2,1)} %get-tuple-element.204), channel_id=1, source_target_pairs={{0,4},{4,0},{8,12},{12,8},{1,5},{5,1},{9,13},{13,9},{2,6},{6,2},{1... | collective-permute-start | bytes 786440 | tf_op jit(solution)/shard_map/ppermute | solution.py:463
  80.0 1.8 %shard_map.77 = (f32[256,256]{1,0:T(8,128)S(1)}, f32[256,256]{1,0:T(8,128)S(1)}, bf16[2,1024,256]{2,1,0:T(8,128)(2,1)S(1)}, bf16[2,1024,256]{2,1,0:T(8,128)(2,1)S(1)}) custom-call(s32[4]{0:T(128)S(1)} %pad_add_fusion.order_ref, bf16[1,4096,256]{2,1,0:T(8,128)(2,1)S(1)} %copy-done, bf16[1,4096,256]{2,1,0:T(8,128)(2,1)S(1)} %copy-done.2, ...), custom_call_target="tpu_custom_call" | custom-call | flops 1024 | bytes 1024 | tf_op jit(solution)/shard_map/pallas_call | solution.py:240
  81.8 2.2 %collective-permute-done.20 = bf16[256,1024]{1,0:T(8,128)(2,1)} collective-permute-done((bf16[256,1024]{1,0:T(8,128)(2,1)S(1)}, bf16[256,1024]{1,0:T(8,128)(2,1)}, u32[]{:S(2)}, u32[]{:S(2)}) %collective-permute-start.20) | collective-permute-done | bytes 524320 | tf_op jit(solution)/shard_map/ppermute | solution.py:466
  84.0 11.7 %conditional.7 = (bf16[256,256]{1,0:T(8,128)(2,1)}, bf16[256,256]{1,0:T(8,128)(2,1)}, f32[256,1024]{1,0:T(8,128)S(1)}, bf16[2,256,1024]{2,1,0:T(8,128)(2,1)S(1)}) conditional(s32[]{:T(128)} %convert_element_type.16, () %tuple.45, (bf16[256,1024]{1,0:T(8,128)(2,1)}, f32[256,256]{1,0:T(8,128)S(1)}, f32[256,256]{1,0:T(8,128)S(1)}, ...), branch_computations={%region_10.11_spmd, %region_11.12_spmd} | conditional | flops 2048 | bytes 3672256 | solution.py:539
  84.1 2.1 %collective-permute-done.4.refs_1_ = bf16[256,1024]{1,0:T(8,128)(2,1)S(1)} collective-permute-done((bf16[256,1024]{1,0:T(8,128)(2,1)}, bf16[256,1024]{1,0:T(8,128)(2,1)S(1)}, u32[]{:S(2)}, u32[]{:S(2)}) %collective-permute-start.4) | collective-permute-done | bytes 524320 | tf_op jit(solution)/shard_map/cond/branch_1_fun/ppermute | solution.py:466
  86.2 1.8 %branch_1_fun.12.refs_0_ = bf16[256,256]{1,0:T(8,128)(2,1)S(1)} custom-call(f32[256,256]{1,0:T(8,128)S(1)} %get-tuple-element.79.gate_before, f32[256,256]{1,0:T(8,128)S(1)} %get-tuple-element.80.up_before, bf16[2,1024,256]{2,1,0:T(8,128)(2,1)S(1)} %get-tuple-element.81.gate_ref, bf16[2,1024,256]{2,1,0:T(8,128)(2,1)S(1)} %get-tuple-element.82.up_ref, ...), custom_call_target="tpu_custom_call" | custom-call | flops 1024 | bytes 1024 | tf_op jit(solution)/shard_map/cond/branch_1_fun/pallas_call | solution.py:268
  90.9 3.1 %collective-permute-done.5 = bf16[256,256]{1,0:T(8,128)(2,1)} collective-permute-done((bf16[256,256]{1,0:T(8,128)(2,1)S(1)}, bf16[256,256]{1,0:T(8,128)(2,1)}, u32[]{:S(2)}, u32[]{:S(2)}) %collective-permute-start.5) | collective-permute-done | bytes 131104 | tf_op jit(solution)/shard_map/cond/branch_1_fun/ppermute | solution.py:466
  95.7 2.4 %shard_map.78 = (bf16[128,1024]{1,0:T(8,128)(2,1)S(1)}, bf16[128,1024]{1,0:T(8,128)(2,1)S(1)}, bf16[128,1024]{1,0:T(8,128)(2,1)S(1)}, bf16[128,1024]{1,0:T(8,128)(2,1)S(1)}) custom-call(s32[2,4]{1,0:T(2,128)S(1)} %get-tuple-element.238.offset_ref, s32[2,4]{1,0:T(2,128)S(1)} %get-tuple-element.237.count_ref, f32[256,1024]{1,0:T(8,128)S(1)} %get-tuple-element.216.before_ref, ...), custom_call_target="tpu_custom_call" | custom-call | flops 1024 | bytes 1024 | tf_op jit(solution)/shard_map/pallas_call | solution.py:360
  100.4 3.2 %collective-permute-start.27 = (bf16[128,1024]{1,0:T(8,128)(2,1)S(1)}, bf16[128,1024]{1,0:T(8,128)(2,1)S(1)}, u32[]{:S(2)}, u32[]{:S(2)}) collective-permute-start(bf16[128,1024]{1,0:T(8,128)(2,1)S(1)} %get-tuple-element.232), channel_id=1, source_target_pairs={{0,4},{4,0},{8,12},{12,8},{1,5},{5,1},{9,13},{13,9},{2,6},{6,2},{1... | collective-permute-start | bytes 786440 | tf_op jit(solution)/shard_map/ppermute | solution.py:463
  103.9 1.9 %shard_map.80.refs_0_ = f32[512,1024]{1,0:T(8,128)S(1)} custom-call(s32[4,512]{1,0:T(4,128)S(1)} %get-tuple-element.162.code_ref, f32[4,512]{1,0:T(4,128)S(1)} %shard_map.79.weight_ref, bf16[128,1024]{1,0:T(8,128)(2,1)S(1)} %get-tuple-element.225.refs_0_, bf16[128,1024]{1,0:T(8,128)(2,1)} %collective-permute-done.22.refs_1_, ...), custom_call_target="tpu_custom_call" | custom-call | flops 1024 | bytes 1024 | tf_op jit(solution)/shard_map/pallas_call | solution.py:436
  105.9 4.5 %collective-permute-done.25.refs_2_ = bf16[128,1024]{1,0:T(8,128)(2,1)S(1)} collective-permute-done((bf16[128,1024]{1,0:T(8,128)(2,1)S(1)}, bf16[128,1024]{1,0:T(8,128)(2,1)S(1)}, u32[]{:S(2)}, u32[]{:S(2)}) %collective-permute-start.25) | collective-permute-done | bytes 262176 | tf_op jit(solution)/shard_map/ppermute | solution.py:463
  110.3 12.4 %collective-permute-done.26.refs_3_ = bf16[128,1024]{1,0:T(8,128)(2,1)S(1)} collective-permute-done((bf16[128,1024]{1,0:T(8,128)(2,1)S(1)}, bf16[128,1024]{1,0:T(8,128)(2,1)S(1)}, u32[]{:S(2)}, u32[]{:S(2)}) %collective-permute-start.26) | collective-permute-done | bytes 262176 | tf_op jit(solution)/shard_map/ppermute | solution.py:463
  122.7 1.9 %shard_map.81 = bf16[512,1024]{1,0:T(8,128)(2,1)} custom-call(s32[4,512]{1,0:T(4,128)S(1)} %get-tuple-element.162.code_ref, f32[4,512]{1,0:T(4,128)S(1)} %shard_map.79.weight_ref, f32[512,1024]{1,0:T(8,128)S(1)} %shard_map.80.refs_0_, bf16[128,1024]{1,0:T(8,128)(2,1)S(1)} %get-tuple-element.229.refs_1_, ...), custom_call_target="tpu_custom_call" | custom-call | flops 1024 | bytes 1024 | tf_op jit(solution)/shard_map/pallas_call | solution.py:436
  (66 shorter events, 30.7 us)
Async XLA Ops:
  2.6 35.0 %collective-permute-start.12 = (bf16[128,1024]{1,0:T(8,128)(2,1)}, bf16[128,1024]{1,0:T(8,128)(2,1)S(1)}, u32[]{:S(2)}, u32[]{:S(2)}) collective-permute-start(bf16[128,1024]{1,0:T(8,128)(2,1)} %get-tuple-element.168), channel_id=1, source_target_pairs={{0,12},{4,8},{8,4},{12,0},{1,13},{5,9},{9,5},{13,1},{2,14},{6,10},... | collective-permute-start | bytes 786440 | tf_op jit(solution)/shard_map/ppermute | solution.py:463
  7.7 29.9 %collective-permute-start.13 = (bf16[128,1024]{1,0:T(8,128)(2,1)}, bf16[128,1024]{1,0:T(8,128)(2,1)S(1)}, u32[]{:S(2)}, u32[]{:S(2)}) collective-permute-start(bf16[128,1024]{1,0:T(8,128)(2,1)} %get-tuple-element.169), channel_id=1, source_target_pairs={{0,8},{4,12},{8,0},{12,4},{1,9},{5,13},{9,1},{13,5},{2,10},{6,14},... | collective-permute-start | bytes 786440 | tf_op jit(solution)/shard_map/ppermute | solution.py:463
  7.7 29.9 %collective-permute-start.14 = (bf16[128,1024]{1,0:T(8,128)(2,1)}, bf16[128,1024]{1,0:T(8,128)(2,1)S(1)}, u32[]{:S(2)}, u32[]{:S(2)}) collective-permute-start(bf16[128,1024]{1,0:T(8,128)(2,1)} %get-tuple-element.170), channel_id=1, source_target_pairs={{0,4},{4,0},{8,12},{12,8},{1,5},{5,1},{9,13},{13,9},{2,6},{6,2},{1... | collective-permute-start | bytes 786440 | tf_op jit(solution)/shard_map/ppermute | solution.py:463
  11.2 34.9 %copy-start = (bf16[1,4096,256]{2,1,0:T(8,128)(2,1)S(1)}, bf16[1,4096,256]{2,1,0:T(8,128)(2,1)}, u32[]{:S(2)}) copy-start(bf16[1,4096,256]{2,1,0:T(8,128)(2,1)} %gate_ref.3) | copy-start | bytes 6291460
  13.0 12.0 %collective-permute-start.8 = (f32[1,4,512]{2,1,0:T(4,128)S(1)}, f32[1,4,512]{2,1,0:T(4,128)S(1)}, u32[]{:S(2)}, u32[]{:S(2)}) collective-permute-start(f32[1,4,512]{2,1,0:T(4,128)S(1)} %bitcast.10), channel_id=1, source_target_pairs={{0,4},{4,0},{8,12},{12,8},{1,5},{5,1},{9,13},{13,9},{2,6},{6,2},{1... | collective-permute-start | bytes 24584 | tf_op jit(solution)/shard_map/cond/branch_1_fun/ppermute | solution.py:463
  25.0 5.8 %collective-permute-start.9 = (f32[2,4,512]{2,1,0:T(4,128)S(1)}, f32[2,4,512]{2,1,0:T(4,128)S(1)}, u32[]{:S(2)}, u32[]{:S(2)}) collective-permute-start(f32[2,4,512]{2,1,0:T(4,128)S(1)} %pad_maximum_fusion.1), channel_id=1, source_target_pairs={{0,8},{4,12},{8,0},{12,4},{1,9},{5,13},{9,1},{13,5},{2,10},{6,14},... | collective-permute-start | bytes 49160 | tf_op jit(solution)/shard_map/cond/branch_1_fun/ppermute | solution.py:463
  30.8 4.0 %collective-permute-start.10 = (f32[4,4,512]{2,1,0:T(4,128)S(1)}, f32[4,4,512]{2,1,0:T(4,128)S(1)}, u32[]{:S(2)}, u32[]{:S(2)}) collective-permute-start(f32[4,4,512]{2,1,0:T(4,128)S(1)} %pad_maximum_fusion), channel_id=1, source_target_pairs={{0,2},{1,3},{2,0},{3,1},{4,6},{5,7},{6,4},{7,5},{8,10},{9,11},{10,... | collective-permute-start | bytes 98312 | tf_op jit(solution)/shard_map/cond/branch_1_fun/ppermute | solution.py:466
  34.8 2.8 %collective-permute-start.11 = (f32[4,4,512]{2,1,0:T(4,128)S(1)}, f32[4,4,512]{2,1,0:T(4,128)S(1)}, u32[]{:S(2)}, u32[]{:S(2)}) collective-permute-start(f32[4,4,512]{2,1,0:T(4,128)S(1)} %fusion), channel_id=1, source_target_pairs={{0,1},{1,0},{2,3},{3,2},{4,5},{5,4},{6,7},{7,6},{8,9},{9,8},{10,11... | collective-permute-start | bytes 98312 | tf_op jit(solution)/shard_map/cond/branch_1_fun/ppermute | solution.py:466
  39.6 6.5 %collective-permute-start.19 = (bf16[256,1024]{1,0:T(8,128)(2,1)}, bf16[256,1024]{1,0:T(8,128)(2,1)S(1)}, u32[]{:S(2)}, u32[]{:S(2)}) collective-permute-start(bf16[256,1024]{1,0:T(8,128)(2,1)} %get-tuple-element.269.refs_0_), channel_id=1, source_target_pairs={{0,1},{1,0},{2,3},{3,2},{4,5},{5,4},{6,7},{7,6},{8,9},{9,8},{10,11... | collective-permute-start | bytes 1572872 | tf_op jit(solution)/shard_map/ppermute | solution.py:466
  40.2 14.2 %collective-permute-start.18 = (bf16[256,1024]{1,0:T(8,128)(2,1)}, bf16[256,1024]{1,0:T(8,128)(2,1)}, u32[]{:S(2)}, u32[]{:S(2)}) collective-permute-start(bf16[256,1024]{1,0:T(8,128)(2,1)} %get-tuple-element.269.refs_0_), channel_id=1, source_target_pairs={{0,2},{1,3},{2,0},{3,1},{4,6},{5,7},{6,4},{7,5},{8,10},{9,11},{10,... | collective-permute-start | bytes 1572872 | tf_op jit(solution)/shard_map/ppermute | solution.py:466
  41.6 24.4 %collective-permute-start.15 = (bf16[128,1024]{1,0:T(8,128)(2,1)}, bf16[128,1024]{1,0:T(8,128)(2,1)S(1)}, u32[]{:S(2)}, u32[]{:S(2)}) collective-permute-start(bf16[128,1024]{1,0:T(8,128)(2,1)} %get-tuple-element.177), channel_id=1, source_target_pairs={{0,12},{4,8},{8,4},{12,0},{1,13},{5,9},{9,5},{13,1},{2,14},{6,10},... | collective-permute-start | bytes 786440 | tf_op jit(solution)/shard_map/ppermute | solution.py:463
  44.3 23.2 %collective-permute-start.16 = (bf16[128,1024]{1,0:T(8,128)(2,1)}, bf16[128,1024]{1,0:T(8,128)(2,1)S(1)}, u32[]{:S(2)}, u32[]{:S(2)}) collective-permute-start(bf16[128,1024]{1,0:T(8,128)(2,1)} %get-tuple-element.178), channel_id=1, source_target_pairs={{0,8},{4,12},{8,0},{12,4},{1,9},{5,13},{9,1},{13,5},{2,10},{6,14},... | collective-permute-start | bytes 786440 | tf_op jit(solution)/shard_map/ppermute | solution.py:463
  44.5 23.0 %collective-permute-start.17 = (bf16[128,1024]{1,0:T(8,128)(2,1)}, bf16[128,1024]{1,0:T(8,128)(2,1)S(1)}, u32[]{:S(2)}, u32[]{:S(2)}) collective-permute-start(bf16[128,1024]{1,0:T(8,128)(2,1)} %get-tuple-element.179), channel_id=1, source_target_pairs={{0,4},{4,0},{8,12},{12,8},{1,5},{5,1},{9,13},{13,9},{2,6},{6,2},{1... | collective-permute-start | bytes 786440 | tf_op jit(solution)/shard_map/ppermute | solution.py:463
  46.1 1.6 %copy-start.1 = (bf16[1,4096,256]{2,1,0:T(8,128)(2,1)S(1)}, bf16[1,4096,256]{2,1,0:T(8,128)(2,1)}, u32[]{:S(2)}) copy-start(bf16[1,4096,256]{2,1,0:T(8,128)(2,1)} %up_ref.3) | copy-start | bytes 6291460
  47.7 6.7 %copy-start.3 = (bf16[1,1024,1024]{2,1,0:T(8,128)(2,1)S(1)}, bf16[1,1024,1024]{2,1,0:T(8,128)(2,1)}, u32[]{:S(2)}) copy-start(bf16[1,1024,1024]{2,1,0:T(8,128)(2,1)} %param.19) | copy-start | bytes 6291460
  54.4 2.1 %collective-permute-start = (bf16[256,1024]{1,0:T(8,128)(2,1)}, bf16[256,1024]{1,0:T(8,128)(2,1)S(1)}, u32[]{:S(2)}, u32[]{:S(2)}) collective-permute-start(bf16[256,1024]{1,0:T(8,128)(2,1)} %get-tuple-element.71.refs_0_), channel_id=1, source_target_pairs={{0,1},{1,0},{2,3},{3,2},{4,5},{5,4},{6,7},{7,6},{8,9},{9,8},{10,11... | collective-permute-start | bytes 1572872 | tf_op jit(solution)/shard_map/cond/branch_1_fun/ppermute | solution.py:466
  58.3 1.7 %collective-permute-start.2 = (bf16[256,256]{1,0:T(8,128)(2,1)S(1)}, bf16[256,256]{1,0:T(8,128)(2,1)S(1)}, u32[]{:S(2)}, u32[]{:S(2)}) collective-permute-start(bf16[256,256]{1,0:T(8,128)(2,1)S(1)} %branch_1_fun.10.refs_0_), channel_id=1, source_target_pairs={{0,1},{1,0},{2,3},{3,2},{4,5},{5,4},{6,7},{7,6},{8,9},{9,8},{10,11... | collective-permute-start | bytes 393224 | tf_op jit(solution)/shard_map/cond/branch_1_fun/ppermute | solution.py:466
  58.5 5.9 %collective-permute-start.1 = (bf16[256,256]{1,0:T(8,128)(2,1)S(1)}, bf16[256,256]{1,0:T(8,128)(2,1)}, u32[]{:S(2)}, u32[]{:S(2)}) collective-permute-start(bf16[256,256]{1,0:T(8,128)(2,1)S(1)} %branch_1_fun.10.refs_0_), channel_id=1, source_target_pairs={{0,2},{1,3},{2,0},{3,1},{4,6},{5,7},{6,4},{7,5},{8,10},{9,11},{10,... | collective-permute-start | bytes 393224 | tf_op jit(solution)/shard_map/cond/branch_1_fun/ppermute | solution.py:466
  64.3 1.7 %collective-permute-start.3 = (bf16[256,256]{1,0:T(8,128)(2,1)}, bf16[256,256]{1,0:T(8,128)(2,1)}, u32[]{:S(2)}, u32[]{:S(2)}) collective-permute-start(bf16[256,256]{1,0:T(8,128)(2,1)} %collective-permute-done.1), channel_id=1, source_target_pairs={{0,1},{1,0},{2,3},{3,2},{4,5},{5,4},{6,7},{7,6},{8,9},{9,8},{10,11... | collective-permute-start | bytes 393224 | tf_op jit(solution)/shard_map/cond/branch_1_fun/ppermute | solution.py:466
  69.5 8.9 %collective-permute-start.21 = (bf16[256,1024]{1,0:T(8,128)(2,1)S(1)}, bf16[256,1024]{1,0:T(8,128)(2,1)S(1)}, u32[]{:S(2)}, u32[]{:S(2)}) collective-permute-start(bf16[256,1024]{1,0:T(8,128)(2,1)S(1)} %shard_map.75.refs_0_), channel_id=1, source_target_pairs={{0,1},{1,0},{2,3},{3,2},{4,5},{5,4},{6,7},{7,6},{8,9},{9,8},{10,11... | collective-permute-start | bytes 1572872 | tf_op jit(solution)/shard_map/ppermute | solution.py:466
  69.6 14.4 %collective-permute-start.20 = (bf16[256,1024]{1,0:T(8,128)(2,1)S(1)}, bf16[256,1024]{1,0:T(8,128)(2,1)}, u32[]{:S(2)}, u32[]{:S(2)}) collective-permute-start(bf16[256,1024]{1,0:T(8,128)(2,1)S(1)} %shard_map.75.refs_0_), channel_id=1, source_target_pairs={{0,2},{1,3},{2,0},{3,1},{4,6},{5,7},{6,4},{7,5},{8,10},{9,11},{10,... | collective-permute-start | bytes 1572872 | tf_op jit(solution)/shard_map/ppermute | solution.py:466
  73.3 24.8 %collective-permute-start.22 = (bf16[128,1024]{1,0:T(8,128)(2,1)}, bf16[128,1024]{1,0:T(8,128)(2,1)}, u32[]{:S(2)}, u32[]{:S(2)}) collective-permute-start(bf16[128,1024]{1,0:T(8,128)(2,1)} %get-tuple-element.202), channel_id=1, source_target_pairs={{0,12},{4,8},{8,4},{12,0},{1,13},{5,9},{9,5},{13,1},{2,14},{6,10},... | collective-permute-start | bytes 786440 | tf_op jit(solution)/shard_map/ppermute | solution.py:463
  75.6 23.6 %collective-permute-start.23 = (bf16[128,1024]{1,0:T(8,128)(2,1)}, bf16[128,1024]{1,0:T(8,128)(2,1)}, u32[]{:S(2)}, u32[]{:S(2)}) collective-permute-start(bf16[128,1024]{1,0:T(8,128)(2,1)} %get-tuple-element.203), channel_id=1, source_target_pairs={{0,8},{4,12},{8,0},{12,4},{1,9},{5,13},{9,1},{13,5},{2,10},{6,14},... | collective-permute-start | bytes 786440 | tf_op jit(solution)/shard_map/ppermute | solution.py:463
  75.8 23.4 %collective-permute-start.24 = (bf16[128,1024]{1,0:T(8,128)(2,1)}, bf16[128,1024]{1,0:T(8,128)(2,1)}, u32[]{:S(2)}, u32[]{:S(2)}) collective-permute-start(bf16[128,1024]{1,0:T(8,128)(2,1)} %get-tuple-element.204), channel_id=1, source_target_pairs={{0,4},{4,0},{8,12},{12,8},{1,5},{5,1},{9,13},{13,9},{2,6},{6,2},{1... | collective-permute-start | bytes 786440 | tf_op jit(solution)/shard_map/ppermute | solution.py:463
  80.0 4.0 %copy-start.4 = (bf16[1,1024,1024]{2,1,0:T(8,128)(2,1)S(1)}, bf16[1,1024,1024]{2,1,0:T(8,128)(2,1)}, u32[]{:S(2)}) copy-start(bf16[1,1024,1024]{2,1,0:T(8,128)(2,1)} %param.19) | copy-start | bytes 6291460
  84.0 2.1 %collective-permute-start.4 = (bf16[256,1024]{1,0:T(8,128)(2,1)}, bf16[256,1024]{1,0:T(8,128)(2,1)S(1)}, u32[]{:S(2)}, u32[]{:S(2)}) collective-permute-start(bf16[256,1024]{1,0:T(8,128)(2,1)} %get-tuple-element.83.refs_0_), channel_id=1, source_target_pairs={{0,1},{1,0},{2,3},{3,2},{4,5},{5,4},{6,7},{7,6},{8,9},{9,8},{10,11... | collective-permute-start | bytes 1572872 | tf_op jit(solution)/shard_map/cond/branch_1_fun/ppermute | solution.py:466
  87.9 1.4 %collective-permute-start.6 = (bf16[256,256]{1,0:T(8,128)(2,1)S(1)}, bf16[256,256]{1,0:T(8,128)(2,1)S(1)}, u32[]{:S(2)}, u32[]{:S(2)}) collective-permute-start(bf16[256,256]{1,0:T(8,128)(2,1)S(1)} %branch_1_fun.12.refs_0_), channel_id=1, source_target_pairs={{0,1},{1,0},{2,3},{3,2},{4,5},{5,4},{6,7},{7,6},{8,9},{9,8},{10,11... | collective-permute-start | bytes 393224 | tf_op jit(solution)/shard_map/cond/branch_1_fun/ppermute | solution.py:466
  88.1 5.9 %collective-permute-start.5 = (bf16[256,256]{1,0:T(8,128)(2,1)S(1)}, bf16[256,256]{1,0:T(8,128)(2,1)}, u32[]{:S(2)}, u32[]{:S(2)}) collective-permute-start(bf16[256,256]{1,0:T(8,128)(2,1)S(1)} %branch_1_fun.12.refs_0_), channel_id=1, source_target_pairs={{0,2},{1,3},{2,0},{3,1},{4,6},{5,7},{6,4},{7,5},{8,10},{9,11},{10,... | collective-permute-start | bytes 393224 | tf_op jit(solution)/shard_map/cond/branch_1_fun/ppermute | solution.py:466
  94.0 1.7 %collective-permute-start.7 = (bf16[256,256]{1,0:T(8,128)(2,1)}, bf16[256,256]{1,0:T(8,128)(2,1)}, u32[]{:S(2)}, u32[]{:S(2)}) collective-permute-start(bf16[256,256]{1,0:T(8,128)(2,1)} %collective-permute-done.5), channel_id=1, source_target_pairs={{0,1},{1,0},{2,3},{3,2},{4,5},{5,4},{6,7},{7,6},{8,9},{9,8},{10,11... | collective-permute-start | bytes 393224 | tf_op jit(solution)/shard_map/cond/branch_1_fun/ppermute | solution.py:466
  99.2 11.1 %collective-permute-start.25 = (bf16[128,1024]{1,0:T(8,128)(2,1)S(1)}, bf16[128,1024]{1,0:T(8,128)(2,1)S(1)}, u32[]{:S(2)}, u32[]{:S(2)}) collective-permute-start(bf16[128,1024]{1,0:T(8,128)(2,1)S(1)} %get-tuple-element.230), channel_id=1, source_target_pairs={{0,12},{4,8},{8,4},{12,0},{1,13},{5,9},{9,5},{13,1},{2,14},{6,10},... | collective-permute-start | bytes 786440 | tf_op jit(solution)/shard_map/ppermute | solution.py:463
  100.4 22.3 %collective-permute-start.26 = (bf16[128,1024]{1,0:T(8,128)(2,1)S(1)}, bf16[128,1024]{1,0:T(8,128)(2,1)S(1)}, u32[]{:S(2)}, u32[]{:S(2)}) collective-permute-start(bf16[128,1024]{1,0:T(8,128)(2,1)S(1)} %get-tuple-element.231), channel_id=1, source_target_pairs={{0,8},{4,12},{8,0},{12,4},{1,9},{5,13},{9,1},{13,5},{2,10},{6,14},... | collective-permute-start | bytes 786440 | tf_op jit(solution)/shard_map/ppermute | solution.py:463
  100.4 22.3 %collective-permute-start.27 = (bf16[128,1024]{1,0:T(8,128)(2,1)S(1)}, bf16[128,1024]{1,0:T(8,128)(2,1)S(1)}, u32[]{:S(2)}, u32[]{:S(2)}) collective-permute-start(bf16[128,1024]{1,0:T(8,128)(2,1)S(1)} %get-tuple-element.232), channel_id=1, source_target_pairs={{0,4},{4,0},{8,12},{12,8},{1,5},{5,1},{9,13},{13,9},{2,6},{6,2},{1... | collective-permute-start | bytes 786440 | tf_op jit(solution)/shard_map/ppermute | solution.py:463
  (1 other events, 1.6 us)

commit v13 on v11

--- a/solution.py
+++ b/solution.py
@@ -544,15 +544,17 @@
     moved = gathered
     for k in range(BATCHES):
         blocks = after(arrived[k], moved)
-        if k < BATCHES - 1:
-            moving = after(later[k], blocks)
-            arrived.append(exchange(moving))
         if k == 0:
             block = fenced(k, lambda *blocks: compact(offsets, counts, 0, blocks, size), *blocks)
         else:
             block = compact(offsets, counts, k, blocks, size)
         across = swap(block, bits[0])
         near = spread(block)
+        if k == 0:
+            gathered = after(gathered, block)
+            gathered = jnp.concatenate([gathered, along_expert(gathered, expert_bits[-1])])
+        if k < BATCHES - 1:
+            arrived.append(exchange(after(later[k], blocks, gathered)))
         if k > 0:
             far, partial = after((far, partial), block)
             results = settle(k - 1, far, partial)
@@ -562,9 +564,6 @@
             near = after(near, results)
         sums = gate_up_near(order, near_places, far_places, gate_weight, up_weight, near)
         across, sums = lax.optimization_barrier((across, sums))
-        if k == BATCHES - 1:
-            gathered = after(gathered, sums)
-            gathered = jnp.concatenate([gathered, along_expert(gathered, expert_bits[-1])])
         far, partial = fenced(k, far_half, across, sums)
         moved = partial
     results = settle(BATCHES - 1, far, partial)

time: 119 us -> 119 us (level)
  starting transfers between devices: 28.9 us -> 26.6 us
  waiting for transfers between devices: 49 us -> 51 us
    ppermute x14, waiting for transfers between devices: 27 us -> 31.2 us  [along_expert(): return lax.ppermute(x, 'expert', [(i, i ^ shift) for i in range(experts)])]
    ppermute x14, starting transfers between devices: 8.41 us -> 6.19 us  [swap(): return lax.ppermute(x, 'dp', [(i, i ^ bit) for i in range(width_parts)])]
    ppermute x14, waiting for transfers between devices: 22 us -> 19.8 us  [swap(): return lax.ppermute(x, 'dp', [(i, i ^ bit) for i in range(width_parts)])]
    unnamed x10 -> x11, local copies, waits for them, and re-layouts: 3.19 us -> 3.19 us
  transfers between devices with their start and end apart: 28 -> 28, of which waited for: 15 -> 16; matrix products, arithmetic and copies ran while one was open for 3% -> 3% of each run, Pallas kernels for 20% -> 20%
where the time goes in v13:
time: 119 us
  waiting for transfers between devices  51 us (43%)
  Pallas kernels  32.4 us (27%)
  starting transfers between devices  26.6 us (22%)
  local copies, waits for them, and re-layouts  3.9 us (3%)
  other arithmetic  2.94 us (2%)
  between operations  1.61 us (1%)
    ppermute x14, waiting for transfers between devices, along_expert(): return lax.ppermute(x, 'expert', [(i, i ^ shift) for i in range(experts)])  31.2 us
    ppermute x14, starting transfers between devices, along_expert(): return lax.ppermute(x, 'expert', [(i, i ^ shift) for i in range(experts)])  20.4 us
    ppermute x14, waiting for transfers between devices, swap(): return lax.ppermute(x, 'dp', [(i, i ^ bit) for i in range(width_parts)])  19.8 us
    ppermute x14, starting transfers between devices, swap(): return lax.ppermute(x, 'dp', [(i, i ^ bit) for i in range(width_parts)])  6.19 us
    pallas_call x2, Pallas kernels, down_last(): pl.pallas_call(functools.partial(down_last_kernel, parts, experts, k, dir...  5.47 us
    pallas_call x2, Pallas kernels, gate_up_near(): pl.pallas_call(functools.partial(gate_up_near_kernel, parts, near, far),...  4.4 us
    pallas_call x2, Pallas kernels, compact(): pl.pallas_call(functools.partial(compact_kernel, experts, k), out_shape=j...  3.94 us
    pallas_call x2, Pallas kernels, combine(): pl.pallas_call(functools.partial(combine_kernel, experts, k), out_shape=j...  3.83 us
  transfers between devices with their start and end apart: 28, of which 16 were waited for; matrix products, arithmetic and copies ran while one was open for 3% of the time, Pallas kernels for 20%

profile of v13, /device:TPU:0, one launch (start us, length us, event | category | flops | bytes accessed | tf_op | source)
XLA Modules:
  0.0 118.6 jit_solution(7767300001822516466)
XLA Ops:
  0.0 2.6 %shard_map.73 = (s32[4,512]{1,0:T(4,128)S(1)}, bf16[128,1024]{1,0:T(8,128)(2,1)S(1)}, bf16[128,1024]{1,0:T(8,128)(2,1)}, bf16[128,1024]{1,0:T(8,128)(2,1)}, bf16[128,1024]{1,0:T(8,128)(2,1)}) custom-call(s32[1]{0:T(128)} %bitcast.1.place_ref, s32[4,512]{1,0:T(4,128)} %picks_in.1, bf16[512,1024]{1,0:T(8,128)(2,1)} %tokens_ref.1), custom_call_target="tpu_custom_call" | custom-call | flops 1024 | bytes 1024 | tf_op jit(solution)/shard_map/pallas_call | solution.py:108
  2.6 5.1 %collective-permute-start.11 = (bf16[128,1024]{1,0:T(8,128)(2,1)}, bf16[128,1024]{1,0:T(8,128)(2,1)S(1)}, u32[]{:S(2)}, u32[]{:S(2)}) collective-permute-start(bf16[128,1024]{1,0:T(8,128)(2,1)} %get-tuple-element.171), channel_id=1, source_target_pairs={{0,12},{4,8},{8,4},{12,0},{1,13},{5,9},{9,5},{13,1},{2,14},{6,10},... | collective-permute-start | bytes 786440 | tf_op jit(solution)/shard_map/ppermute | solution.py:463
  11.3 14.4 %conditional.4 = (bf16[128,1024]{1,0:T(8,128)(2,1)}, bf16[128,1024]{1,0:T(8,128)(2,1)}, bf16[128,1024]{1,0:T(8,128)(2,1)}, bf16[128,1024]{1,0:T(8,128)(2,1)}, f3...) conditional(s32[]{:T(128)} %convert_element_type.16, () %tuple.46, (s32[4,512]{1,0:T(4,128)S(1)}, ...), branch_computations={%region_3.4_spmd, %region_4.5_spmd} | conditional | flops 10240 | bytes 1073216 | solution.py:521
  11.3 1.8 %branch_1_fun.8 = f32[4,512]{1,0:T(4,128)S(1)} custom-call(bf16[4,1024]{1,0:T(4,128)(2,1)} %get-tuple-element.60.router_ref, bf16[512,1024]{1,0:T(8,128)(2,1)} %get-tuple-element.55.tokens_ref), custom_call_target="tpu_custom_call" | custom-call | flops 1024 | bytes 1024 | tf_op jit(solution)/shard_map/cond/branch_1_fun/pallas_call | solution.py:134
  14.7 2.0 %collective-permute-done.8 = f32[4,512]{1,0:T(4,128)S(1)} collective-permute-done((f32[4,512]{1,0:T(4,128)S(1)}, f32[4,512]{1,0:T(4,128)S(1)}, u32[]{:S(2)}, u32[]{:S(2)}) %collective-permute-start.8) | collective-permute-done | bytes 8224 | tf_op jit(solution)/shard_map/cond/branch_1_fun/ppermute | solution.py:466
  19.9 2.7 %branch_1_fun.7 = (bf16[128,1024]{1,0:T(8,128)(2,1)}, bf16[128,1024]{1,0:T(8,128)(2,1)}, bf16[128,1024]{1,0:T(8,128)(2,1)}, bf16[128,1024]{1,0:T(8,128)(2,1)}) custom-call(s32[4,512]{1,0:T(4,128)S(1)} %get-tuple-element.54.code_ref, bf16[512,1024]{1,0:T(8,128)(2,1)} %get-tuple-element.55.tokens_ref), custom_call_target="tpu_custom_call" | custom-call | flops 1024 | bytes 1024 | tf_op jit(solution)/shard_map/cond/branch_1_fun/pallas_call | solution.py:155
  22.6 2.4 %collective-permute-done.10 = f32[1,4,512]{2,1,0:T(4,128)S(1)} collective-permute-done((f32[1,4,512]{2,1,0:T(4,128)}, f32[1,4,512]{2,1,0:T(4,128)S(1)}, u32[]{:S(2)}, u32[]{:S(2)}) %collective-permute-start.10) | collective-permute-done | bytes 8224 | tf_op jit(solution)/shard_map/cond/branch_1_fun/ppermute | solution.py:463
  25.7 4.5 %collective-permute-done.12 = bf16[128,1024]{1,0:T(8,128)(2,1)S(1)} collective-permute-done((bf16[128,1024]{1,0:T(8,128)(2,1)}, bf16[128,1024]{1,0:T(8,128)(2,1)S(1)}, u32[]{:S(2)}, u32[]{:S(2)}) %collective-permute-start.12) | collective-permute-done | bytes 262176 | tf_op jit(solution)/shard_map/ppermute | solution.py:463
  30.2 1.9 %conditional.5 = (bf16[256,1024]{1,0:T(8,128)(2,1)}) conditional(s32[]{:T(128)} %convert_element_type.16, () %tuple.50, (s32[2,4]{1,0:T(2,128)S(1)}, s32[2,4]{1,0:T(2,128)S(1)}, bf16[128,1024]{1,0:T(8,128)(2,1)S(1)}, bf16[128,1024]{1,0:T(8,128)(2,1)S(1)}, bf16[128,1024]{1,0:T(8,128)(2,1)S(1)}, /*index=5*/bf16[128,1024]{1,0:T(8,128)(2,1)S(1)}) %tuple.51), branch_computations={%region_6.7_spmd, %region_7.8_spmd} | conditional | flops 1024 | bytes 524298 | solution.py:540
  30.2 1.9 %branch_1_fun.9 = bf16[256,1024]{1,0:T(8,128)(2,1)} custom-call(s32[2,4]{1,0:T(2,128)S(1)} %get-tuple-element.61.offset_ref, s32[2,4]{1,0:T(2,128)S(1)} %get-tuple-element.62.count_ref, bf16[128,1024]{1,0:T(8,128)(2,1)S(1)} %get-tuple-element.63.refs_0_, bf16[128,1024]{1,0:T(8,128)(2,1)S(1)} %get-tuple-element.64.refs_1_, ...), custom_call_target="tpu_custom_call" | custom-call | flops 1024 | bytes 1024 | tf_op jit(solution)/shard_map/cond/branch_1_fun/pallas_call | solution.py:192
  33.8 4.6 %collective-permute-done.14 = f32[2,4,512]{2,1,0:T(4,128)S(1)} collective-permute-done((f32[2,4,512]{2,1,0:T(4,128)S(1)}, f32[2,4,512]{2,1,0:T(4,128)S(1)}, u32[]{:S(2)}, u32[]{:S(2)}) %collective-permute-start.14) | collective-permute-done | bytes 16416 | tf_op jit(solution)/shard_map/ppermute | solution.py:463
  38.5 2.5 %collective-permute-start.15 = (bf16[128,1024]{1,0:T(8,128)(2,1)}, bf16[128,1024]{1,0:T(8,128)(2,1)S(1)}, u32[]{:S(2)}, u32[]{:S(2)}) collective-permute-start(bf16[128,1024]{1,0:T(8,128)(2,1)} %get-tuple-element.181), channel_id=1, source_target_pairs={{0,12},{4,8},{8,4},{12,0},{1,13},{5,9},{9,5},{13,1},{2,14},{6,10},... | collective-permute-start | bytes 786440 | tf_op jit(solution)/shard_map/ppermute | solution.py:463
  40.9 1.9 %collective-permute-start.17 = (bf16[128,1024]{1,0:T(8,128)(2,1)}, bf16[128,1024]{1,0:T(8,128)(2,1)S(1)}, u32[]{:S(2)}, u32[]{:S(2)}) collective-permute-start(bf16[128,1024]{1,0:T(8,128)(2,1)} %get-tuple-element.183), channel_id=1, source_target_pairs={{0,4},{4,0},{8,12},{12,8},{1,5},{5,1},{9,13},{13,9},{2,6},{6,2},{1... | collective-permute-start | bytes 786440 | tf_op jit(solution)/shard_map/ppermute | solution.py:463
  44.5 2.6 %shard_map.74 = (f32[256,256]{1,0:T(8,128)S(1)}, f32[256,256]{1,0:T(8,128)S(1)}, bf16[2,1024,256]{2,1,0:T(8,128)(2,1)S(1)}, bf16[2,1024,256]{2,1,0:T(8,128)(2,1)S(1)}) custom-call(s32[4]{0:T(128)S(1)} %pad_add_fusion.order_ref, bf16[1,4096,256]{2,1,0:T(8,128)(2,1)S(1)} %copy-done, bf16[1,4096,256]{2,1,0:T(8,128)(2,1)S(1)} %copy-done.1, ...), custom_call_target="tpu_custom_call" | custom-call | flops 1024 | bytes 1024 | tf_op jit(solution)/shard_map/pallas_call | solution.py:240
  47.1 11.7 %conditional.6 = (bf16[256,256]{1,0:T(8,128)(2,1)}, bf16[256,256]{1,0:T(8,128)(2,1)}, f32[256,1024]{1,0:T(8,128)S(1)}, bf16[2,256,1024]{2,1,0:T(8,128)(2,1)S(1)}) conditional(s32[]{:T(128)} %convert_element_type.16, () %tuple.54, (bf16[256,1024]{1,0:T(8,128)(2,1)}, f32[256,256]{1,0:T(8,128)S(1)}, f32[256,256]{1,0:T(8,128)S(1)}, ...), branch_computations={%region_8.9_spmd, %region_9.10_spmd} | conditional | flops 2048 | bytes 3672256 | solution.py:540
  47.2 2.1 %collective-permute-done.refs_1_ = bf16[256,1024]{1,0:T(8,128)(2,1)S(1)} collective-permute-done((bf16[256,1024]{1,0:T(8,128)(2,1)}, bf16[256,1024]{1,0:T(8,128)(2,1)S(1)}, u32[]{:S(2)}, u32[]{:S(2)}) %collective-permute-start) | collective-permute-done | bytes 524320 | tf_op jit(solution)/shard_map/cond/branch_1_fun/ppermute | solution.py:466
  54.1 3.1 %collective-permute-done.1 = bf16[256,256]{1,0:T(8,128)(2,1)} collective-permute-done((bf16[256,256]{1,0:T(8,128)(2,1)S(1)}, bf16[256,256]{1,0:T(8,128)(2,1)}, u32[]{:S(2)}, u32[]{:S(2)}) %collective-permute-start.1) | collective-permute-done | bytes 131104 | tf_op jit(solution)/shard_map/cond/branch_1_fun/ppermute | solution.py:466
  58.9 3.7 %collective-permute-done.16.refs_2_ = bf16[128,1024]{1,0:T(8,128)(2,1)S(1)} collective-permute-done((bf16[128,1024]{1,0:T(8,128)(2,1)}, bf16[128,1024]{1,0:T(8,128)(2,1)S(1)}, u32[]{:S(2)}, u32[]{:S(2)}) %collective-permute-start.16) | collective-permute-done | bytes 262176 | tf_op jit(solution)/shard_map/ppermute | solution.py:463
  62.6 2.0 %shard_map.75.refs_0_ = bf16[256,1024]{1,0:T(8,128)(2,1)S(1)} custom-call(s32[2,4]{1,0:T(2,128)S(1)} %get-tuple-element.241.offset_ref, s32[2,4]{1,0:T(2,128)S(1)} %get-tuple-element.242.count_ref, bf16[128,1024]{1,0:T(8,128)(2,1)} %get-tuple-element.195.refs_0_, bf16[128,1024]{1,0:T(8,128)(2,1)S(1)} %collective-permute-done.15.refs_1_, ...), custom_call_target="tpu_custom_call" | custom-call | flops 1024 | bytes 1024 | tf_op jit(solution)/shard_map/pallas_call | solution.py:192
  65.3 3.1 %shard_map.76 = (bf16[128,1024]{1,0:T(8,128)(2,1)S(1)}, bf16[128,1024]{1,0:T(8,128)(2,1)}, bf16[128,1024]{1,0:T(8,128)(2,1)}, bf16[128,1024]{1,0:T(8,128)(2,1)}) custom-call(s32[2,4]{1,0:T(2,128)S(1)} %get-tuple-element.241.offset_ref, s32[2,4]{1,0:T(2,128)S(1)} %get-tuple-element.242.count_ref, f32[256,1024]{1,0:T(8,128)S(1)} %get-tuple-element.201.before_ref, ...), custom_call_target="tpu_custom_call" | custom-call | flops 1024 | bytes 1024 | tf_op jit(solution)/shard_map/pallas_call | solution.py:360
  69.8 3.0 %collective-permute-start.24 = (bf16[128,1024]{1,0:T(8,128)(2,1)}, bf16[128,1024]{1,0:T(8,128)(2,1)}, u32[]{:S(2)}, u32[]{:S(2)}) collective-permute-start(bf16[128,1024]{1,0:T(8,128)(2,1)} %get-tuple-element.208), channel_id=1, source_target_pairs={{0,4},{4,0},{8,12},{12,8},{1,5},{5,1},{9,13},{13,9},{2,6},{6,2},{1... | collective-permute-start | bytes 786440 | tf_op jit(solution)/shard_map/ppermute | solution.py:463
  75.1 1.8 %shard_map.77 = (f32[256,256]{1,0:T(8,128)S(1)}, f32[256,256]{1,0:T(8,128)S(1)}, bf16[2,1024,256]{2,1,0:T(8,128)(2,1)S(1)}, bf16[2,1024,256]{2,1,0:T(8,128)(2,1)S(1)}) custom-call(s32[4]{0:T(128)S(1)} %pad_add_fusion.order_ref, bf16[1,4096,256]{2,1,0:T(8,128)(2,1)S(1)} %copy-done, bf16[1,4096,256]{2,1,0:T(8,128)(2,1)S(1)} %copy-done.2, ...), custom_call_target="tpu_custom_call" | custom-call | flops 1024 | bytes 1024 | tf_op jit(solution)/shard_map/pallas_call | solution.py:240
  76.9 2.2 %collective-permute-done.20 = bf16[256,1024]{1,0:T(8,128)(2,1)} collective-permute-done((bf16[256,1024]{1,0:T(8,128)(2,1)S(1)}, bf16[256,1024]{1,0:T(8,128)(2,1)}, u32[]{:S(2)}, u32[]{:S(2)}) %collective-permute-start.20) | collective-permute-done | bytes 524320 | tf_op jit(solution)/shard_map/ppermute | solution.py:466
  79.1 11.7 %conditional.7 = (bf16[256,256]{1,0:T(8,128)(2,1)}, bf16[256,256]{1,0:T(8,128)(2,1)}, f32[256,1024]{1,0:T(8,128)S(1)}, bf16[2,256,1024]{2,1,0:T(8,128)(2,1)S(1)}) conditional(s32[]{:T(128)} %convert_element_type.17, () %tuple.48, (bf16[256,1024]{1,0:T(8,128)(2,1)}, f32[256,256]{1,0:T(8,128)S(1)}, f32[256,256]{1,0:T(8,128)S(1)}, ...), branch_computations={%region_10.11_spmd, %region_11.12_spmd} | conditional | flops 2048 | bytes 3672256 | solution.py:540
  79.1 2.1 %collective-permute-done.4.refs_1_ = bf16[256,1024]{1,0:T(8,128)(2,1)S(1)} collective-permute-done((bf16[256,1024]{1,0:T(8,128)(2,1)}, bf16[256,1024]{1,0:T(8,128)(2,1)S(1)}, u32[]{:S(2)}, u32[]{:S(2)}) %collective-permute-start.4) | collective-permute-done | bytes 524320 | tf_op jit(solution)/shard_map/cond/branch_1_fun/ppermute | solution.py:466
  86.0 3.1 %collective-permute-done.5 = bf16[256,256]{1,0:T(8,128)(2,1)} collective-permute-done((bf16[256,256]{1,0:T(8,128)(2,1)S(1)}, bf16[256,256]{1,0:T(8,128)(2,1)}, u32[]{:S(2)}, u32[]{:S(2)}) %collective-permute-start.5) | collective-permute-done | bytes 131104 | tf_op jit(solution)/shard_map/cond/branch_1_fun/ppermute | solution.py:466
  90.8 2.4 %shard_map.78 = (bf16[128,1024]{1,0:T(8,128)(2,1)S(1)}, bf16[128,1024]{1,0:T(8,128)(2,1)S(1)}, bf16[128,1024]{1,0:T(8,128)(2,1)S(1)}, bf16[128,1024]{1,0:T(8,128)(2,1)S(1)}) custom-call(s32[2,4]{1,0:T(2,128)S(1)} %get-tuple-element.241.offset_ref, s32[2,4]{1,0:T(2,128)S(1)} %get-tuple-element.242.count_ref, f32[256,1024]{1,0:T(8,128)S(1)} %get-tuple-element.220.before_ref, ...), custom_call_target="tpu_custom_call" | custom-call | flops 1024 | bytes 1024 | tf_op jit(solution)/shard_map/pallas_call | solution.py:360
  94.6 3.0 %collective-permute-start.27 = (bf16[128,1024]{1,0:T(8,128)(2,1)S(1)}, bf16[128,1024]{1,0:T(8,128)(2,1)S(1)}, u32[]{:S(2)}, u32[]{:S(2)}) collective-permute-start(bf16[128,1024]{1,0:T(8,128)(2,1)S(1)} %get-tuple-element.236), channel_id=1, source_target_pairs={{0,4},{4,0},{8,12},{12,8},{1,5},{5,1},{9,13},{13,9},{2,6},{6,2},{1... | collective-permute-start | bytes 786440 | tf_op jit(solution)/shard_map/ppermute | solution.py:463
  98.7 1.9 %shard_map.80.refs_0_ = f32[512,1024]{1,0:T(8,128)S(1)} custom-call(s32[4,512]{1,0:T(4,128)S(1)} %get-tuple-element.164.code_ref, f32[4,512]{1,0:T(4,128)S(1)} %shard_map.79.weight_ref, bf16[128,1024]{1,0:T(8,128)(2,1)S(1)} %get-tuple-element.229.refs_0_, bf16[128,1024]{1,0:T(8,128)(2,1)} %collective-permute-done.22.refs_1_, ...), custom_call_target="tpu_custom_call" | custom-call | flops 1024 | bytes 1024 | tf_op jit(solution)/shard_map/pallas_call | solution.py:436
  100.6 3.7 %collective-permute-done.25.refs_2_ = bf16[128,1024]{1,0:T(8,128)(2,1)S(1)} collective-permute-done((bf16[128,1024]{1,0:T(8,128)(2,1)S(1)}, bf16[128,1024]{1,0:T(8,128)(2,1)S(1)}, u32[]{:S(2)}, u32[]{:S(2)}) %collective-permute-start.25) | collective-permute-done | bytes 262176 | tf_op jit(solution)/shard_map/ppermute | solution.py:463
  104.4 12.2 %collective-permute-done.26.refs_3_ = bf16[128,1024]{1,0:T(8,128)(2,1)S(1)} collective-permute-done((bf16[128,1024]{1,0:T(8,128)(2,1)S(1)}, bf16[128,1024]{1,0:T(8,128)(2,1)S(1)}, u32[]{:S(2)}, u32[]{:S(2)}) %collective-permute-start.26) | collective-permute-done | bytes 262176 | tf_op jit(solution)/shard_map/ppermute | solution.py:463
  116.6 1.9 %shard_map.81 = bf16[512,1024]{1,0:T(8,128)(2,1)} custom-call(s32[4,512]{1,0:T(4,128)S(1)} %get-tuple-element.164.code_ref, f32[4,512]{1,0:T(4,128)S(1)} %shard_map.79.weight_ref, f32[512,1024]{1,0:T(8,128)S(1)} %shard_map.80.refs_0_, bf16[128,1024]{1,0:T(8,128)(2,1)S(1)} %get-tuple-element.233.refs_1_, ...), custom_call_target="tpu_custom_call" | custom-call | flops 1024 | bytes 1024 | tf_op jit(solution)/shard_map/pallas_call | solution.py:436
  (66 shorter events, 30.9 us)
Async XLA Ops:
  2.6 23.1 %collective-permute-start.11 = (bf16[128,1024]{1,0:T(8,128)(2,1)}, bf16[128,1024]{1,0:T(8,128)(2,1)S(1)}, u32[]{:S(2)}, u32[]{:S(2)}) collective-permute-start(bf16[128,1024]{1,0:T(8,128)(2,1)} %get-tuple-element.171), channel_id=1, source_target_pairs={{0,12},{4,8},{8,4},{12,0},{1,13},{5,9},{9,5},{13,1},{2,14},{6,10},... | collective-permute-start | bytes 786440 | tf_op jit(solution)/shard_map/ppermute | solution.py:463
  7.7 22.5 %collective-permute-start.12 = (bf16[128,1024]{1,0:T(8,128)(2,1)}, bf16[128,1024]{1,0:T(8,128)(2,1)S(1)}, u32[]{:S(2)}, u32[]{:S(2)}) collective-permute-start(bf16[128,1024]{1,0:T(8,128)(2,1)} %get-tuple-element.172), channel_id=1, source_target_pairs={{0,8},{4,12},{8,0},{12,4},{1,9},{5,13},{9,1},{13,5},{2,10},{6,14},... | collective-permute-start | bytes 786440 | tf_op jit(solution)/shard_map/ppermute | solution.py:463
  7.7 22.5 %collective-permute-start.13 = (bf16[128,1024]{1,0:T(8,128)(2,1)}, bf16[128,1024]{1,0:T(8,128)(2,1)S(1)}, u32[]{:S(2)}, u32[]{:S(2)}) collective-permute-start(bf16[128,1024]{1,0:T(8,128)(2,1)} %get-tuple-element.173), channel_id=1, source_target_pairs={{0,4},{4,0},{8,12},{12,8},{1,5},{5,1},{9,13},{13,9},{2,6},{6,2},{1... | collective-permute-start | bytes 786440 | tf_op jit(solution)/shard_map/ppermute | solution.py:463
  11.2 31.7 %copy-start = (bf16[1,4096,256]{2,1,0:T(8,128)(2,1)S(1)}, bf16[1,4096,256]{2,1,0:T(8,128)(2,1)}, u32[]{:S(2)}) copy-start(bf16[1,4096,256]{2,1,0:T(8,128)(2,1)} %gate_ref.3) | copy-start | bytes 6291460
  13.0 3.7 %collective-permute-start.8 = (f32[4,512]{1,0:T(4,128)S(1)}, f32[4,512]{1,0:T(4,128)S(1)}, u32[]{:S(2)}, u32[]{:S(2)}) collective-permute-start(f32[4,512]{1,0:T(4,128)S(1)} %branch_1_fun.8), channel_id=1, source_target_pairs={{0,2},{1,3},{2,0},{3,1},{4,6},{5,7},{6,4},{7,5},{8,10},{9,11},{10,... | collective-permute-start | bytes 24584 | tf_op jit(solution)/shard_map/cond/branch_1_fun/ppermute | solution.py:466
  16.7 1.2 collective-permute-start.9
  18.5 6.5 %collective-permute-start.10 = (f32[1,4,512]{2,1,0:T(4,128)}, f32[1,4,512]{2,1,0:T(4,128)S(1)}, u32[]{:S(2)}, u32[]{:S(2)}) collective-permute-start(f32[1,4,512]{2,1,0:T(4,128)} %bitcast), channel_id=1, source_target_pairs={{0,4},{4,0},{8,12},{12,8},{1,5},{5,1},{9,13},{13,9},{2,6},{6,2},{1... | collective-permute-start | bytes 24584 | tf_op jit(solution)/shard_map/cond/branch_1_fun/ppermute | solution.py:463
  32.2 10.7 %collective-permute-start.19 = (bf16[256,1024]{1,0:T(8,128)(2,1)}, bf16[256,1024]{1,0:T(8,128)(2,1)S(1)}, u32[]{:S(2)}, u32[]{:S(2)}) collective-permute-start(bf16[256,1024]{1,0:T(8,128)(2,1)} %get-tuple-element.275.refs_0_), channel_id=1, source_target_pairs={{0,1},{1,0},{2,3},{3,2},{4,5},{5,4},{6,7},{7,6},{8,9},{9,8},{10,11... | collective-permute-start | bytes 1572872 | tf_op jit(solution)/shard_map/ppermute | solution.py:466
  32.3 14.9 %collective-permute-start.18 = (bf16[256,1024]{1,0:T(8,128)(2,1)}, bf16[256,1024]{1,0:T(8,128)(2,1)}, u32[]{:S(2)}, u32[]{:S(2)}) collective-permute-start(bf16[256,1024]{1,0:T(8,128)(2,1)} %get-tuple-element.275.refs_0_), channel_id=1, source_target_pairs={{0,2},{1,3},{2,0},{3,1},{4,6},{5,7},{6,4},{7,5},{8,10},{9,11},{10,... | collective-permute-start | bytes 1572872 | tf_op jit(solution)/shard_map/ppermute | solution.py:466
  33.8 4.6 %collective-permute-start.14 = (f32[2,4,512]{2,1,0:T(4,128)S(1)}, f32[2,4,512]{2,1,0:T(4,128)S(1)}, u32[]{:S(2)}, u32[]{:S(2)}) collective-permute-start(f32[2,4,512]{2,1,0:T(4,128)S(1)} %get-tuple-element.179), channel_id=1, source_target_pairs={{0,8},{4,12},{8,0},{12,4},{1,9},{5,13},{9,1},{13,5},{2,10},{6,14},... | collective-permute-start | bytes 49160 | tf_op jit(solution)/shard_map/ppermute | solution.py:463
  38.5 20.4 %collective-permute-start.15 = (bf16[128,1024]{1,0:T(8,128)(2,1)}, bf16[128,1024]{1,0:T(8,128)(2,1)S(1)}, u32[]{:S(2)}, u32[]{:S(2)}) collective-permute-start(bf16[128,1024]{1,0:T(8,128)(2,1)} %get-tuple-element.181), channel_id=1, source_target_pairs={{0,12},{4,8},{8,4},{12,0},{1,13},{5,9},{9,5},{13,1},{2,14},{6,10},... | collective-permute-start | bytes 786440 | tf_op jit(solution)/shard_map/ppermute | solution.py:463
  40.9 21.6 %collective-permute-start.16 = (bf16[128,1024]{1,0:T(8,128)(2,1)}, bf16[128,1024]{1,0:T(8,128)(2,1)S(1)}, u32[]{:S(2)}, u32[]{:S(2)}) collective-permute-start(bf16[128,1024]{1,0:T(8,128)(2,1)} %get-tuple-element.182), channel_id=1, source_target_pairs={{0,8},{4,12},{8,0},{12,4},{1,9},{5,13},{9,1},{13,5},{2,10},{6,14},... | collective-permute-start | bytes 786440 | tf_op jit(solution)/shard_map/ppermute | solution.py:463
  40.9 21.6 %collective-permute-start.17 = (bf16[128,1024]{1,0:T(8,128)(2,1)}, bf16[128,1024]{1,0:T(8,128)(2,1)S(1)}, u32[]{:S(2)}, u32[]{:S(2)}) collective-permute-start(bf16[128,1024]{1,0:T(8,128)(2,1)} %get-tuple-element.183), channel_id=1, source_target_pairs={{0,4},{4,0},{8,12},{12,8},{1,5},{5,1},{9,13},{13,9},{2,6},{6,2},{1... | collective-permute-start | bytes 786440 | tf_op jit(solution)/shard_map/ppermute | solution.py:463
  42.9 1.6 %copy-start.1 = (bf16[1,4096,256]{2,1,0:T(8,128)(2,1)S(1)}, bf16[1,4096,256]{2,1,0:T(8,128)(2,1)}, u32[]{:S(2)}) copy-start(bf16[1,4096,256]{2,1,0:T(8,128)(2,1)} %up_ref.3) | copy-start | bytes 6291460
  44.5 2.6 %copy-start.3 = (bf16[1,1024,1024]{2,1,0:T(8,128)(2,1)S(1)}, bf16[1,1024,1024]{2,1,0:T(8,128)(2,1)}, u32[]{:S(2)}) copy-start(bf16[1,1024,1024]{2,1,0:T(8,128)(2,1)} %param.19) | copy-start | bytes 6291460
  47.2 2.2 %collective-permute-start = (bf16[256,1024]{1,0:T(8,128)(2,1)}, bf16[256,1024]{1,0:T(8,128)(2,1)S(1)}, u32[]{:S(2)}, u32[]{:S(2)}) collective-permute-start(bf16[256,1024]{1,0:T(8,128)(2,1)} %get-tuple-element.71.refs_0_), channel_id=1, source_target_pairs={{0,1},{1,0},{2,3},{3,2},{4,5},{5,4},{6,7},{7,6},{8,9},{9,8},{10,11... | collective-permute-start | bytes 1572872 | tf_op jit(solution)/shard_map/cond/branch_1_fun/ppermute | solution.py:466
  51.1 1.4 %collective-permute-start.2 = (bf16[256,256]{1,0:T(8,128)(2,1)S(1)}, bf16[256,256]{1,0:T(8,128)(2,1)S(1)}, u32[]{:S(2)}, u32[]{:S(2)}) collective-permute-start(bf16[256,256]{1,0:T(8,128)(2,1)S(1)} %branch_1_fun.10.refs_0_), channel_id=1, source_target_pairs={{0,1},{1,0},{2,3},{3,2},{4,5},{5,4},{6,7},{7,6},{8,9},{9,8},{10,11... | collective-permute-start | bytes 393224 | tf_op jit(solution)/shard_map/cond/branch_1_fun/ppermute | solution.py:466
  51.3 5.9 %collective-permute-start.1 = (bf16[256,256]{1,0:T(8,128)(2,1)S(1)}, bf16[256,256]{1,0:T(8,128)(2,1)}, u32[]{:S(2)}, u32[]{:S(2)}) collective-permute-start(bf16[256,256]{1,0:T(8,128)(2,1)S(1)} %branch_1_fun.10.refs_0_), channel_id=1, source_target_pairs={{0,2},{1,3},{2,0},{3,1},{4,6},{5,7},{6,4},{7,5},{8,10},{9,11},{10,... | collective-permute-start | bytes 393224 | tf_op jit(solution)/shard_map/cond/branch_1_fun/ppermute | solution.py:466
  57.2 1.7 %collective-permute-start.3 = (bf16[256,256]{1,0:T(8,128)(2,1)}, bf16[256,256]{1,0:T(8,128)(2,1)}, u32[]{:S(2)}, u32[]{:S(2)}) collective-permute-start(bf16[256,256]{1,0:T(8,128)(2,1)} %collective-permute-done.1), channel_id=1, source_target_pairs={{0,1},{1,0},{2,3},{3,2},{4,5},{5,4},{6,7},{7,6},{8,9},{9,8},{10,11... | collective-permute-start | bytes 393224 | tf_op jit(solution)/shard_map/cond/branch_1_fun/ppermute | solution.py:466
  64.6 8.9 %collective-permute-start.21 = (bf16[256,1024]{1,0:T(8,128)(2,1)S(1)}, bf16[256,1024]{1,0:T(8,128)(2,1)S(1)}, u32[]{:S(2)}, u32[]{:S(2)}) collective-permute-start(bf16[256,1024]{1,0:T(8,128)(2,1)S(1)} %shard_map.75.refs_0_), channel_id=1, source_target_pairs={{0,1},{1,0},{2,3},{3,2},{4,5},{5,4},{6,7},{7,6},{8,9},{9,8},{10,11... | collective-permute-start | bytes 1572872 | tf_op jit(solution)/shard_map/ppermute | solution.py:466
  64.7 14.4 %collective-permute-start.20 = (bf16[256,1024]{1,0:T(8,128)(2,1)S(1)}, bf16[256,1024]{1,0:T(8,128)(2,1)}, u32[]{:S(2)}, u32[]{:S(2)}) collective-permute-start(bf16[256,1024]{1,0:T(8,128)(2,1)S(1)} %shard_map.75.refs_0_), channel_id=1, source_target_pairs={{0,2},{1,3},{2,0},{3,1},{4,6},{5,7},{6,4},{7,5},{8,10},{9,11},{10,... | collective-permute-start | bytes 1572872 | tf_op jit(solution)/shard_map/ppermute | solution.py:466
  68.4 24.8 %collective-permute-start.22 = (bf16[128,1024]{1,0:T(8,128)(2,1)}, bf16[128,1024]{1,0:T(8,128)(2,1)}, u32[]{:S(2)}, u32[]{:S(2)}) collective-permute-start(bf16[128,1024]{1,0:T(8,128)(2,1)} %get-tuple-element.206), channel_id=1, source_target_pairs={{0,12},{4,8},{8,4},{12,0},{1,13},{5,9},{9,5},{13,1},{2,14},{6,10},... | collective-permute-start | bytes 786440 | tf_op jit(solution)/shard_map/ppermute | solution.py:463
  69.8 23.4 %collective-permute-start.23 = (bf16[128,1024]{1,0:T(8,128)(2,1)}, bf16[128,1024]{1,0:T(8,128)(2,1)}, u32[]{:S(2)}, u32[]{:S(2)}) collective-permute-start(bf16[128,1024]{1,0:T(8,128)(2,1)} %get-tuple-element.207), channel_id=1, source_target_pairs={{0,8},{4,12},{8,0},{12,4},{1,9},{5,13},{9,1},{13,5},{2,10},{6,14},... | collective-permute-start | bytes 786440 | tf_op jit(solution)/shard_map/ppermute | solution.py:463
  69.8 23.4 %collective-permute-start.24 = (bf16[128,1024]{1,0:T(8,128)(2,1)}, bf16[128,1024]{1,0:T(8,128)(2,1)}, u32[]{:S(2)}, u32[]{:S(2)}) collective-permute-start(bf16[128,1024]{1,0:T(8,128)(2,1)} %get-tuple-element.208), channel_id=1, source_target_pairs={{0,4},{4,0},{8,12},{12,8},{1,5},{5,1},{9,13},{13,9},{2,6},{6,2},{1... | collective-permute-start | bytes 786440 | tf_op jit(solution)/shard_map/ppermute | solution.py:463
  75.1 4.0 %copy-start.4 = (bf16[1,1024,1024]{2,1,0:T(8,128)(2,1)S(1)}, bf16[1,1024,1024]{2,1,0:T(8,128)(2,1)}, u32[]{:S(2)}) copy-start(bf16[1,1024,1024]{2,1,0:T(8,128)(2,1)} %param.19) | copy-start | bytes 6291460
  79.1 2.1 %collective-permute-start.4 = (bf16[256,1024]{1,0:T(8,128)(2,1)}, bf16[256,1024]{1,0:T(8,128)(2,1)S(1)}, u32[]{:S(2)}, u32[]{:S(2)}) collective-permute-start(bf16[256,1024]{1,0:T(8,128)(2,1)} %get-tuple-element.83.refs_0_), channel_id=1, source_target_pairs={{0,1},{1,0},{2,3},{3,2},{4,5},{5,4},{6,7},{7,6},{8,9},{9,8},{10,11... | collective-permute-start | bytes 1572872 | tf_op jit(solution)/shard_map/cond/branch_1_fun/ppermute | solution.py:466
  83.0 1.4 %collective-permute-start.6 = (bf16[256,256]{1,0:T(8,128)(2,1)S(1)}, bf16[256,256]{1,0:T(8,128)(2,1)S(1)}, u32[]{:S(2)}, u32[]{:S(2)}) collective-permute-start(bf16[256,256]{1,0:T(8,128)(2,1)S(1)} %branch_1_fun.12.refs_0_), channel_id=1, source_target_pairs={{0,1},{1,0},{2,3},{3,2},{4,5},{5,4},{6,7},{7,6},{8,9},{9,8},{10,11... | collective-permute-start | bytes 393224 | tf_op jit(solution)/shard_map/cond/branch_1_fun/ppermute | solution.py:466
  83.2 5.9 %collective-permute-start.5 = (bf16[256,256]{1,0:T(8,128)(2,1)S(1)}, bf16[256,256]{1,0:T(8,128)(2,1)}, u32[]{:S(2)}, u32[]{:S(2)}) collective-permute-start(bf16[256,256]{1,0:T(8,128)(2,1)S(1)} %branch_1_fun.12.refs_0_), channel_id=1, source_target_pairs={{0,2},{1,3},{2,0},{3,1},{4,6},{5,7},{6,4},{7,5},{8,10},{9,11},{10,... | collective-permute-start | bytes 393224 | tf_op jit(solution)/shard_map/cond/branch_1_fun/ppermute | solution.py:466
  89.1 1.7 %collective-permute-start.7 = (bf16[256,256]{1,0:T(8,128)(2,1)}, bf16[256,256]{1,0:T(8,128)(2,1)}, u32[]{:S(2)}, u32[]{:S(2)}) collective-permute-start(bf16[256,256]{1,0:T(8,128)(2,1)} %collective-permute-done.5), channel_id=1, source_target_pairs={{0,1},{1,0},{2,3},{3,2},{4,5},{5,4},{6,7},{7,6},{8,9},{9,8},{10,11... | collective-permute-start | bytes 393224 | tf_op jit(solution)/shard_map/cond/branch_1_fun/ppermute | solution.py:466
  93.2 11.2 %collective-permute-start.25 = (bf16[128,1024]{1,0:T(8,128)(2,1)S(1)}, bf16[128,1024]{1,0:T(8,128)(2,1)S(1)}, u32[]{:S(2)}, u32[]{:S(2)}) collective-permute-start(bf16[128,1024]{1,0:T(8,128)(2,1)S(1)} %get-tuple-element.234), channel_id=1, source_target_pairs={{0,12},{4,8},{8,4},{12,0},{1,13},{5,9},{9,5},{13,1},{2,14},{6,10},... | collective-permute-start | bytes 786440 | tf_op jit(solution)/shard_map/ppermute | solution.py:463
  94.6 21.9 %collective-permute-start.26 = (bf16[128,1024]{1,0:T(8,128)(2,1)S(1)}, bf16[128,1024]{1,0:T(8,128)(2,1)S(1)}, u32[]{:S(2)}, u32[]{:S(2)}) collective-permute-start(bf16[128,1024]{1,0:T(8,128)(2,1)S(1)} %get-tuple-element.235), channel_id=1, source_target_pairs={{0,8},{4,12},{8,0},{12,4},{1,9},{5,13},{9,1},{13,5},{2,10},{6,14},... | collective-permute-start | bytes 786440 | tf_op jit(solution)/shard_map/ppermute | solution.py:463
  94.6 21.9 %collective-permute-start.27 = (bf16[128,1024]{1,0:T(8,128)(2,1)S(1)}, bf16[128,1024]{1,0:T(8,128)(2,1)S(1)}, u32[]{:S(2)}, u32[]{:S(2)}) collective-permute-start(bf16[128,1024]{1,0:T(8,128)(2,1)S(1)} %get-tuple-element.236), channel_id=1, source_target_pairs={{0,4},{4,0},{8,12},{12,8},{1,5},{5,1},{9,13},{13,9},{2,6},{6,2},{1... | collective-permute-start | bytes 786440 | tf_op jit(solution)/shard_map/ppermute | solution.py:463
  (1 other events, 1.6 us)

commit v14 on v13

--- a/solution.py
+++ b/solution.py
@@ -510,7 +510,9 @@
         for bit in bits:
             logits = logits + swap(logits, bit)
         gathered = logits[None]
-        for bit in expert_bits[:-1]:
+        for bit in expert_bits:
+            if bit == expert_bits[-1]:
+                gathered, later = lax.optimization_barrier((gathered, later))
             gathered = jnp.concatenate([gathered, along_expert(gathered, bit)])
         return later, logits, gathered
 
@@ -550,11 +552,8 @@
             block = compact(offsets, counts, k, blocks, size)
         across = swap(block, bits[0])
         near = spread(block)
-        if k == 0:
-            gathered = after(gathered, block)
-            gathered = jnp.concatenate([gathered, along_expert(gathered, expert_bits[-1])])
         if k < BATCHES - 1:
-            arrived.append(exchange(after(later[k], blocks, gathered)))
+            arrived.append(exchange(after(later[k], blocks)))
         if k > 0:
             far, partial = after((far, partial), block)
             results = settle(k - 1, far, partial)

time: 119 us -> 119 us (level)
  starting transfers between devices: 26.6 us -> 28.1 us
  waiting for transfers between devices: 51 us -> 49.6 us
    ppermute x14, waiting for transfers between devices: 31.2 us -> 25.6 us  [along_expert(): return lax.ppermute(x, 'expert', [(i, i ^ shift) for i in range(experts)])]
    ppermute x14, waiting for transfers between devices: 19.8 us -> 24 us  [swap(): return lax.ppermute(x, 'dp', [(i, i ^ bit) for i in range(width_parts)])]
    ppermute x14, starting transfers between devices: 20.4 us -> 21.7 us  [along_expert(): return lax.ppermute(x, 'expert', [(i, i ^ shift) for i in range(experts)])]
    unnamed x11 -> x10, local copies, waits for them, and re-layouts: 3.19 us -> 3.19 us
  transfers between devices with their start and end apart: 28 -> 28, of which waited for: 16 -> 17; matrix products, arithmetic and copies ran while one was open for 3% -> 3% of each run, Pallas kernels for 20% -> 20%
where the time goes in v14:
time: 119 us
  waiting for transfers between devices  49.6 us (42%)
  Pallas kernels  32.4 us (27%)
  starting transfers between devices  28.1 us (24%)
  local copies, waits for them, and re-layouts  3.89 us (3%)
  other arithmetic  2.95 us (2%)
  between operations  1.6 us (1%)
    ppermute x14, waiting for transfers between devices, along_expert(): return lax.ppermute(x, 'expert', [(i, i ^ shift) for i in range(experts)])  25.6 us
    ppermute x14, waiting for transfers between devices, swap(): return lax.ppermute(x, 'dp', [(i, i ^ bit) for i in range(width_parts)])  24 us
    ppermute x14, starting transfers between devices, along_expert(): return lax.ppermute(x, 'expert', [(i, i ^ shift) for i in range(experts)])  21.7 us
    ppermute x14, starting transfers between devices, swap(): return lax.ppermute(x, 'dp', [(i, i ^ bit) for i in range(width_parts)])  6.42 us
    pallas_call x2, Pallas kernels, down_last(): pl.pallas_call(functools.partial(down_last_kernel, parts, experts, k, dir...  5.48 us
    pallas_call x2, Pallas kernels, gate_up_near(): pl.pallas_call(functools.partial(gate_up_near_kernel, parts, near, far),...  4.4 us
    pallas_call x2, Pallas kernels, compact(): pl.pallas_call(functools.partial(compact_kernel, experts, k), out_shape=j...  3.94 us
    pallas_call x2, Pallas kernels, combine(): pl.pallas_call(functools.partial(combine_kernel, experts, k), out_shape=j...  3.83 us
  transfers between devices with their start and end apart: 28, of which 17 were waited for; matrix products, arithmetic and copies ran while one was open for 3% of the time, Pallas kernels for 20%

profile of v14, /device:TPU:0, one launch (start us, length us, event | category | flops | bytes accessed | tf_op | source)
XLA Modules:
  0.0 118.6 jit_solution(14116313628473613429)
XLA Ops:
  0.0 2.6 %shard_map.73 = (s32[4,512]{1,0:T(4,128)S(1)}, bf16[128,1024]{1,0:T(8,128)(2,1)S(1)}, bf16[128,1024]{1,0:T(8,128)(2,1)}, bf16[128,1024]{1,0:T(8,128)(2,1)}, bf16[128,1024]{1,0:T(8,128)(2,1)}) custom-call(s32[1]{0:T(128)} %bitcast.1.place_ref, s32[4,512]{1,0:T(4,128)} %picks_in.1, bf16[512,1024]{1,0:T(8,128)(2,1)} %tokens_ref.1), custom_call_target="tpu_custom_call" | custom-call | flops 1024 | bytes 1024 | tf_op jit(solution)/shard_map/pallas_call | solution.py:108
  2.6 5.1 %collective-permute-start.12 = (bf16[128,1024]{1,0:T(8,128)(2,1)}, bf16[128,1024]{1,0:T(8,128)(2,1)S(1)}, u32[]{:S(2)}, u32[]{:S(2)}) collective-permute-start(bf16[128,1024]{1,0:T(8,128)(2,1)} %get-tuple-element.175), channel_id=1, source_target_pairs={{0,12},{4,8},{8,4},{12,0},{1,13},{5,9},{9,5},{13,1},{2,14},{6,10},... | collective-permute-start | bytes 786440 | tf_op jit(solution)/shard_map/ppermute | solution.py:463
  11.3 19.5 %conditional.4 = (bf16[128,1024]{1,0:T(8,128)(2,1)}, bf16[128,1024]{1,0:T(8,128)(2,1)}, bf16[128,1024]{1,0:T(8,128)(2,1)}, bf16[128,1024]{1,0:T(8,128)(2,1)}, f3...) conditional(s32[]{:T(128)} %convert_element_type.16, () %tuple.46, (bf16[4,1024]{1,0:T(4,128)(2,1)}, ...), branch_computations={%region_3.4_spmd, %region_4.5_spmd} | conditional | flops 18432 | bytes 1089600 | solution.py:523
  11.3 1.8 %branch_1_fun.7 = f32[4,512]{1,0:T(4,128)S(1)} custom-call(bf16[4,1024]{1,0:T(4,128)(2,1)} %get-tuple-element.54.router_ref, bf16[512,1024]{1,0:T(8,128)(2,1)} %get-tuple-element.55.tokens_ref), custom_call_target="tpu_custom_call" | custom-call | flops 1024 | bytes 1024 | tf_op jit(solution)/shard_map/cond/branch_1_fun/pallas_call | solution.py:134
  14.7 2.0 %collective-permute-done.8 = f32[4,512]{1,0:T(4,128)S(1)} collective-permute-done((f32[4,512]{1,0:T(4,128)S(1)}, f32[4,512]{1,0:T(4,128)S(1)}, u32[]{:S(2)}, u32[]{:S(2)}) %collective-permute-start.8) | collective-permute-done | bytes 8224 | tf_op jit(solution)/shard_map/cond/branch_1_fun/ppermute | solution.py:466
  19.9 2.7 %branch_1_fun.8 = (bf16[128,1024]{1,0:T(8,128)(2,1)}, bf16[128,1024]{1,0:T(8,128)(2,1)}, bf16[128,1024]{1,0:T(8,128)(2,1)}, bf16[128,1024]{1,0:T(8,128)(2,1)}) custom-call(s32[4,512]{1,0:T(4,128)S(1)} %get-tuple-element.56.code_ref, bf16[512,1024]{1,0:T(8,128)(2,1)} %get-tuple-element.55.tokens_ref), custom_call_target="tpu_custom_call" | custom-call | flops 1024 | bytes 1024 | tf_op jit(solution)/shard_map/cond/branch_1_fun/pallas_call | solution.py:155
  22.6 2.4 %collective-permute-done.10 = f32[1,4,512]{2,1,0:T(4,128)S(1)} collective-permute-done((f32[1,4,512]{2,1,0:T(4,128)}, f32[1,4,512]{2,1,0:T(4,128)S(1)}, u32[]{:S(2)}, u32[]{:S(2)}) %collective-permute-start.10) | collective-permute-done | bytes 8224 | tf_op jit(solution)/shard_map/cond/branch_1_fun/ppermute | solution.py:463
  27.0 3.8 %collective-permute-done.11 = f32[2,4,512]{2,1,0:T(4,128)S(1)} collective-permute-done((f32[2,4,512]{2,1,0:T(4,128)S(1)}, f32[2,4,512]{2,1,0:T(4,128)S(1)}, u32[]{:S(2)}, u32[]{:S(2)}) %collective-permute-start.11) | collective-permute-done | bytes 16416 | tf_op jit(solution)/shard_map/cond/branch_1_fun/ppermute | solution.py:463
  30.8 2.0 %conditional.5 = (bf16[256,1024]{1,0:T(8,128)(2,1)}) conditional(s32[]{:T(128)} %convert_element_type.16, () %tuple.52, (s32[2,4]{1,0:T(2,128)S(1)}, s32[2,4]{1,0:T(2,128)S(1)}, bf16[128,1024]{1,0:T(8,128)(2,1)S(1)}, bf16[128,1024]{1,0:T(8,128)(2,1)S(1)}, bf16[128,1024]{1,0:T(8,128)(2,1)S(1)}, /*index=5*/bf16[128,1024]{1,0:T(8,128)(2,1)S(1)}) %tuple.53), branch_computations={%region_6.7_spmd, %region_7.8_spmd} | conditional | flops 1024 | bytes 524298 | solution.py:542
  30.8 1.9 %branch_1_fun.9 = bf16[256,1024]{1,0:T(8,128)(2,1)} custom-call(s32[2,4]{1,0:T(2,128)S(1)} %get-tuple-element.66.offset_ref, s32[2,4]{1,0:T(2,128)S(1)} %get-tuple-element.67.count_ref, bf16[128,1024]{1,0:T(8,128)(2,1)S(1)} %get-tuple-element.68.refs_0_, bf16[128,1024]{1,0:T(8,128)(2,1)S(1)} %get-tuple-element.69.refs_1_, ...), custom_call_target="tpu_custom_call" | custom-call | flops 1024 | bytes 1024 | tf_op jit(solution)/shard_map/cond/branch_1_fun/pallas_call | solution.py:192
  34.4 2.7 %collective-permute-start.15 = (bf16[128,1024]{1,0:T(8,128)(2,1)}, bf16[128,1024]{1,0:T(8,128)(2,1)S(1)}, u32[]{:S(2)}, u32[]{:S(2)}) collective-permute-start(bf16[128,1024]{1,0:T(8,128)(2,1)} %get-tuple-element.184), channel_id=1, source_target_pairs={{0,12},{4,8},{8,4},{12,0},{1,13},{5,9},{9,5},{13,1},{2,14},{6,10},... | collective-permute-start | bytes 786440 | tf_op jit(solution)/shard_map/ppermute | solution.py:463
  40.5 2.6 %shard_map.74 = (f32[256,256]{1,0:T(8,128)S(1)}, f32[256,256]{1,0:T(8,128)S(1)}, bf16[2,1024,256]{2,1,0:T(8,128)(2,1)S(1)}, bf16[2,1024,256]{2,1,0:T(8,128)(2,1)S(1)}) custom-call(s32[4]{0:T(128)S(1)} %pad_add_fusion.order_ref, bf16[1,4096,256]{2,1,0:T(8,128)(2,1)S(1)} %copy-done, bf16[1,4096,256]{2,1,0:T(8,128)(2,1)S(1)} %copy-done.1, ...), custom_call_target="tpu_custom_call" | custom-call | flops 1024 | bytes 1024 | tf_op jit(solution)/shard_map/pallas_call | solution.py:240
  43.1 4.4 %collective-permute-done.18 = bf16[256,1024]{1,0:T(8,128)(2,1)} collective-permute-done((bf16[256,1024]{1,0:T(8,128)(2,1)}, bf16[256,1024]{1,0:T(8,128)(2,1)}, u32[]{:S(2)}, u32[]{:S(2)}) %collective-permute-start.18) | collective-permute-done | bytes 524320 | tf_op jit(solution)/shard_map/ppermute | solution.py:466
  47.5 11.7 %conditional.6 = (bf16[256,256]{1,0:T(8,128)(2,1)}, bf16[256,256]{1,0:T(8,128)(2,1)}, f32[256,1024]{1,0:T(8,128)S(1)}, bf16[2,256,1024]{2,1,0:T(8,128)(2,1)S(1)}) conditional(s32[]{:T(128)} %convert_element_type.16, () %tuple.51, (bf16[256,1024]{1,0:T(8,128)(2,1)}, f32[256,256]{1,0:T(8,128)S(1)}, f32[256,256]{1,0:T(8,128)S(1)}, ...), branch_computations={%region_8.9_spmd, %region_9.10_spmd} | conditional | flops 2048 | bytes 3672256 | solution.py:542
  47.5 2.1 %collective-permute-done.refs_1_ = bf16[256,1024]{1,0:T(8,128)(2,1)S(1)} collective-permute-done((bf16[256,1024]{1,0:T(8,128)(2,1)}, bf16[256,1024]{1,0:T(8,128)(2,1)S(1)}, u32[]{:S(2)}, u32[]{:S(2)}) %collective-permute-start) | collective-permute-done | bytes 524320 | tf_op jit(solution)/shard_map/cond/branch_1_fun/ppermute | solution.py:466
  49.6 1.8 %branch_1_fun.10.refs_0_ = bf16[256,256]{1,0:T(8,128)(2,1)S(1)} custom-call(f32[256,256]{1,0:T(8,128)S(1)} %get-tuple-element.72.gate_before, f32[256,256]{1,0:T(8,128)S(1)} %get-tuple-element.73.up_before, bf16[2,1024,256]{2,1,0:T(8,128)(2,1)S(1)} %get-tuple-element.74.gate_ref, bf16[2,1024,256]{2,1,0:T(8,128)(2,1)S(1)} %get-tuple-element.75.up_ref, ...), custom_call_target="tpu_custom_call" | custom-call | flops 1024 | bytes 1024 | tf_op jit(solution)/shard_map/cond/branch_1_fun/pallas_call | solution.py:268
  54.7 2.8 %collective-permute-done.1 = bf16[256,256]{1,0:T(8,128)(2,1)} collective-permute-done((bf16[256,256]{1,0:T(8,128)(2,1)S(1)}, bf16[256,256]{1,0:T(8,128)(2,1)}, u32[]{:S(2)}, u32[]{:S(2)}) %collective-permute-start.1) | collective-permute-done | bytes 131104 | tf_op jit(solution)/shard_map/cond/branch_1_fun/ppermute | solution.py:466
  59.2 2.2 %collective-permute-done.16.refs_2_ = bf16[128,1024]{1,0:T(8,128)(2,1)S(1)} collective-permute-done((bf16[128,1024]{1,0:T(8,128)(2,1)}, bf16[128,1024]{1,0:T(8,128)(2,1)S(1)}, u32[]{:S(2)}, u32[]{:S(2)}) %collective-permute-start.16) | collective-permute-done | bytes 262176 | tf_op jit(solution)/shard_map/ppermute | solution.py:463
  61.3 2.0 %shard_map.75.refs_0_ = bf16[256,1024]{1,0:T(8,128)(2,1)S(1)} custom-call(s32[2,4]{1,0:T(2,128)S(1)} %get-tuple-element.244.offset_ref, s32[2,4]{1,0:T(2,128)S(1)} %get-tuple-element.245.count_ref, bf16[128,1024]{1,0:T(8,128)(2,1)} %get-tuple-element.198.refs_0_, bf16[128,1024]{1,0:T(8,128)(2,1)S(1)} %collective-permute-done.15.refs_1_, ...), custom_call_target="tpu_custom_call" | custom-call | flops 1024 | bytes 1024 | tf_op jit(solution)/shard_map/pallas_call | solution.py:192
  64.0 3.1 %shard_map.76 = (bf16[128,1024]{1,0:T(8,128)(2,1)S(1)}, bf16[128,1024]{1,0:T(8,128)(2,1)}, bf16[128,1024]{1,0:T(8,128)(2,1)}, bf16[128,1024]{1,0:T(8,128)(2,1)}) custom-call(s32[2,4]{1,0:T(2,128)S(1)} %get-tuple-element.244.offset_ref, s32[2,4]{1,0:T(2,128)S(1)} %get-tuple-element.245.count_ref, f32[256,1024]{1,0:T(8,128)S(1)} %get-tuple-element.204.before_ref, ...), custom_call_target="tpu_custom_call" | custom-call | flops 1024 | bytes 1024 | tf_op jit(solution)/shard_map/pallas_call | solution.py:360
  69.6 2.0 %collective-permute-start.24 = (bf16[128,1024]{1,0:T(8,128)(2,1)}, bf16[128,1024]{1,0:T(8,128)(2,1)}, u32[]{:S(2)}, u32[]{:S(2)}) collective-permute-start(bf16[128,1024]{1,0:T(8,128)(2,1)} %get-tuple-element.211), channel_id=1, source_target_pairs={{0,4},{4,0},{8,12},{12,8},{1,5},{5,1},{9,13},{13,9},{2,6},{6,2},{1... | collective-permute-start | bytes 786440 | tf_op jit(solution)/shard_map/ppermute | solution.py:463
  73.8 1.8 %shard_map.77 = (f32[256,256]{1,0:T(8,128)S(1)}, f32[256,256]{1,0:T(8,128)S(1)}, bf16[2,1024,256]{2,1,0:T(8,128)(2,1)S(1)}, bf16[2,1024,256]{2,1,0:T(8,128)(2,1)S(1)}) custom-call(s32[4]{0:T(128)S(1)} %pad_add_fusion.order_ref, bf16[1,4096,256]{2,1,0:T(8,128)(2,1)S(1)} %copy-done, bf16[1,4096,256]{2,1,0:T(8,128)(2,1)S(1)} %copy-done.2, ...), custom_call_target="tpu_custom_call" | custom-call | flops 1024 | bytes 1024 | tf_op jit(solution)/shard_map/pallas_call | solution.py:240
  75.7 2.2 %collective-permute-done.20 = bf16[256,1024]{1,0:T(8,128)(2,1)} collective-permute-done((bf16[256,1024]{1,0:T(8,128)(2,1)S(1)}, bf16[256,1024]{1,0:T(8,128)(2,1)}, u32[]{:S(2)}, u32[]{:S(2)}) %collective-permute-start.20) | collective-permute-done | bytes 524320 | tf_op jit(solution)/shard_map/ppermute | solution.py:466
  77.9 11.7 %conditional.7 = (bf16[256,256]{1,0:T(8,128)(2,1)}, bf16[256,256]{1,0:T(8,128)(2,1)}, f32[256,1024]{1,0:T(8,128)S(1)}, bf16[2,256,1024]{2,1,0:T(8,128)(2,1)S(1)}) conditional(s32[]{:T(128)} %convert_element_type.17, () %tuple.48, (bf16[256,1024]{1,0:T(8,128)(2,1)}, f32[256,256]{1,0:T(8,128)S(1)}, f32[256,256]{1,0:T(8,128)S(1)}, ...), branch_computations={%region_10.11_spmd, %region_11.12_spmd} | conditional | flops 2048 | bytes 3672256 | solution.py:542
  77.9 2.1 %collective-permute-done.4.refs_1_ = bf16[256,1024]{1,0:T(8,128)(2,1)S(1)} collective-permute-done((bf16[256,1024]{1,0:T(8,128)(2,1)}, bf16[256,1024]{1,0:T(8,128)(2,1)S(1)}, u32[]{:S(2)}, u32[]{:S(2)}) %collective-permute-start.4) | collective-permute-done | bytes 524320 | tf_op jit(solution)/shard_map/cond/branch_1_fun/ppermute | solution.py:466
  84.8 3.1 %collective-permute-done.5 = bf16[256,256]{1,0:T(8,128)(2,1)} collective-permute-done((bf16[256,256]{1,0:T(8,128)(2,1)S(1)}, bf16[256,256]{1,0:T(8,128)(2,1)}, u32[]{:S(2)}, u32[]{:S(2)}) %collective-permute-start.5) | collective-permute-done | bytes 131104 | tf_op jit(solution)/shard_map/cond/branch_1_fun/ppermute | solution.py:466
  89.5 2.4 %shard_map.78 = (bf16[128,1024]{1,0:T(8,128)(2,1)S(1)}, bf16[128,1024]{1,0:T(8,128)(2,1)S(1)}, bf16[128,1024]{1,0:T(8,128)(2,1)S(1)}, bf16[128,1024]{1,0:T(8,128)(2,1)S(1)}) custom-call(s32[2,4]{1,0:T(2,128)S(1)} %get-tuple-element.244.offset_ref, s32[2,4]{1,0:T(2,128)S(1)} %get-tuple-element.245.count_ref, f32[256,1024]{1,0:T(8,128)S(1)} %get-tuple-element.223.before_ref, ...), custom_call_target="tpu_custom_call" | custom-call | flops 1024 | bytes 1024 | tf_op jit(solution)/shard_map/pallas_call | solution.py:360
  94.2 3.2 %collective-permute-start.27 = (bf16[128,1024]{1,0:T(8,128)(2,1)S(1)}, bf16[128,1024]{1,0:T(8,128)(2,1)S(1)}, u32[]{:S(2)}, u32[]{:S(2)}) collective-permute-start(bf16[128,1024]{1,0:T(8,128)(2,1)S(1)} %get-tuple-element.239), channel_id=1, source_target_pairs={{0,4},{4,0},{8,12},{12,8},{1,5},{5,1},{9,13},{13,9},{2,6},{6,2},{1... | collective-permute-start | bytes 786440 | tf_op jit(solution)/shard_map/ppermute | solution.py:463
  98.5 1.9 %shard_map.80.refs_0_ = f32[512,1024]{1,0:T(8,128)S(1)} custom-call(s32[4,512]{1,0:T(4,128)S(1)} %get-tuple-element.168.code_ref, f32[4,512]{1,0:T(4,128)S(1)} %shard_map.79.weight_ref, bf16[128,1024]{1,0:T(8,128)(2,1)S(1)} %get-tuple-element.232.refs_0_, bf16[128,1024]{1,0:T(8,128)(2,1)} %collective-permute-done.22.refs_1_, ...), custom_call_target="tpu_custom_call" | custom-call | flops 1024 | bytes 1024 | tf_op jit(solution)/shard_map/pallas_call | solution.py:436
  100.4 3.8 %collective-permute-done.25.refs_2_ = bf16[128,1024]{1,0:T(8,128)(2,1)S(1)} collective-permute-done((bf16[128,1024]{1,0:T(8,128)(2,1)S(1)}, bf16[128,1024]{1,0:T(8,128)(2,1)S(1)}, u32[]{:S(2)}, u32[]{:S(2)}) %collective-permute-start.25) | collective-permute-done | bytes 262176 | tf_op jit(solution)/shard_map/ppermute | solution.py:463
  104.2 12.4 %collective-permute-done.26.refs_3_ = bf16[128,1024]{1,0:T(8,128)(2,1)S(1)} collective-permute-done((bf16[128,1024]{1,0:T(8,128)(2,1)S(1)}, bf16[128,1024]{1,0:T(8,128)(2,1)S(1)}, u32[]{:S(2)}, u32[]{:S(2)}) %collective-permute-start.26) | collective-permute-done | bytes 262176 | tf_op jit(solution)/shard_map/ppermute | solution.py:463
  116.5 1.9 %shard_map.81 = bf16[512,1024]{1,0:T(8,128)(2,1)} custom-call(s32[4,512]{1,0:T(4,128)S(1)} %get-tuple-element.168.code_ref, f32[4,512]{1,0:T(4,128)S(1)} %shard_map.79.weight_ref, f32[512,1024]{1,0:T(8,128)S(1)} %shard_map.80.refs_0_, bf16[128,1024]{1,0:T(8,128)(2,1)S(1)} %get-tuple-element.236.refs_1_, ...), custom_call_target="tpu_custom_call" | custom-call | flops 1024 | bytes 1024 | tf_op jit(solution)/shard_map/pallas_call | solution.py:436
  (65 shorter events, 34.2 us)
Async XLA Ops:
  2.6 28.2 %collective-permute-start.12 = (bf16[128,1024]{1,0:T(8,128)(2,1)}, bf16[128,1024]{1,0:T(8,128)(2,1)S(1)}, u32[]{:S(2)}, u32[]{:S(2)}) collective-permute-start(bf16[128,1024]{1,0:T(8,128)(2,1)} %get-tuple-element.175), channel_id=1, source_target_pairs={{0,12},{4,8},{8,4},{12,0},{1,13},{5,9},{9,5},{13,1},{2,14},{6,10},... | collective-permute-start | bytes 786440 | tf_op jit(solution)/shard_map/ppermute | solution.py:463
  7.7 23.1 %collective-permute-start.13 = (bf16[128,1024]{1,0:T(8,128)(2,1)}, bf16[128,1024]{1,0:T(8,128)(2,1)S(1)}, u32[]{:S(2)}, u32[]{:S(2)}) collective-permute-start(bf16[128,1024]{1,0:T(8,128)(2,1)} %get-tuple-element.176), channel_id=1, source_target_pairs={{0,8},{4,12},{8,0},{12,4},{1,9},{5,13},{9,1},{13,5},{2,10},{6,14},... | collective-permute-start | bytes 786440 | tf_op jit(solution)/shard_map/ppermute | solution.py:463
  7.7 23.1 %collective-permute-start.14 = (bf16[128,1024]{1,0:T(8,128)(2,1)}, bf16[128,1024]{1,0:T(8,128)(2,1)S(1)}, u32[]{:S(2)}, u32[]{:S(2)}) collective-permute-start(bf16[128,1024]{1,0:T(8,128)(2,1)} %get-tuple-element.177), channel_id=1, source_target_pairs={{0,4},{4,0},{8,12},{12,8},{1,5},{5,1},{9,13},{13,9},{2,6},{6,2},{1... | collective-permute-start | bytes 786440 | tf_op jit(solution)/shard_map/ppermute | solution.py:463
  11.2 27.6 %copy-start = (bf16[1,4096,256]{2,1,0:T(8,128)(2,1)S(1)}, bf16[1,4096,256]{2,1,0:T(8,128)(2,1)}, u32[]{:S(2)}) copy-start(bf16[1,4096,256]{2,1,0:T(8,128)(2,1)} %gate_ref.3) | copy-start | bytes 6291460
  13.0 3.7 %collective-permute-start.8 = (f32[4,512]{1,0:T(4,128)S(1)}, f32[4,512]{1,0:T(4,128)S(1)}, u32[]{:S(2)}, u32[]{:S(2)}) collective-permute-start(f32[4,512]{1,0:T(4,128)S(1)} %branch_1_fun.7), channel_id=1, source_target_pairs={{0,2},{1,3},{2,0},{3,1},{4,6},{5,7},{6,4},{7,5},{8,10},{9,11},{10,... | collective-permute-start | bytes 24584 | tf_op jit(solution)/shard_map/cond/branch_1_fun/ppermute | solution.py:466
  16.7 1.2 collective-permute-start.9
  18.5 6.5 %collective-permute-start.10 = (f32[1,4,512]{2,1,0:T(4,128)}, f32[1,4,512]{2,1,0:T(4,128)S(1)}, u32[]{:S(2)}, u32[]{:S(2)}) collective-permute-start(f32[1,4,512]{2,1,0:T(4,128)} %bitcast), channel_id=1, source_target_pairs={{0,4},{4,0},{8,12},{12,8},{1,5},{5,1},{9,13},{13,9},{2,6},{6,2},{1... | collective-permute-start | bytes 24584 | tf_op jit(solution)/shard_map/cond/branch_1_fun/ppermute | solution.py:463
  25.7 5.1 %collective-permute-start.11 = (f32[2,4,512]{2,1,0:T(4,128)S(1)}, f32[2,4,512]{2,1,0:T(4,128)S(1)}, u32[]{:S(2)}, u32[]{:S(2)}) collective-permute-start(f32[2,4,512]{2,1,0:T(4,128)S(1)} %pad_maximum_fusion.1), channel_id=1, source_target_pairs={{0,8},{4,12},{8,0},{12,4},{1,9},{5,13},{9,1},{13,5},{2,10},{6,14},... | collective-permute-start | bytes 49160 | tf_op jit(solution)/shard_map/cond/branch_1_fun/ppermute | solution.py:463
  32.8 6.1 %collective-permute-start.19 = (bf16[256,1024]{1,0:T(8,128)(2,1)}, bf16[256,1024]{1,0:T(8,128)(2,1)S(1)}, u32[]{:S(2)}, u32[]{:S(2)}) collective-permute-start(bf16[256,1024]{1,0:T(8,128)(2,1)} %get-tuple-element.278.refs_0_), channel_id=1, source_target_pairs={{0,1},{1,0},{2,3},{3,2},{4,5},{5,4},{6,7},{7,6},{8,9},{9,8},{10,11... | collective-permute-start | bytes 1572872 | tf_op jit(solution)/shard_map/ppermute | solution.py:466
  32.9 14.7 %collective-permute-start.18 = (bf16[256,1024]{1,0:T(8,128)(2,1)}, bf16[256,1024]{1,0:T(8,128)(2,1)}, u32[]{:S(2)}, u32[]{:S(2)}) collective-permute-start(bf16[256,1024]{1,0:T(8,128)(2,1)} %get-tuple-element.278.refs_0_), channel_id=1, source_target_pairs={{0,2},{1,3},{2,0},{3,1},{4,6},{5,7},{6,4},{7,5},{8,10},{9,11},{10,... | collective-permute-start | bytes 1572872 | tf_op jit(solution)/shard_map/ppermute | solution.py:466
  34.4 24.8 %collective-permute-start.15 = (bf16[128,1024]{1,0:T(8,128)(2,1)}, bf16[128,1024]{1,0:T(8,128)(2,1)S(1)}, u32[]{:S(2)}, u32[]{:S(2)}) collective-permute-start(bf16[128,1024]{1,0:T(8,128)(2,1)} %get-tuple-element.184), channel_id=1, source_target_pairs={{0,12},{4,8},{8,4},{12,0},{1,13},{5,9},{9,5},{13,1},{2,14},{6,10},... | collective-permute-start | bytes 786440 | tf_op jit(solution)/shard_map/ppermute | solution.py:463
  37.1 24.3 %collective-permute-start.16 = (bf16[128,1024]{1,0:T(8,128)(2,1)}, bf16[128,1024]{1,0:T(8,128)(2,1)S(1)}, u32[]{:S(2)}, u32[]{:S(2)}) collective-permute-start(bf16[128,1024]{1,0:T(8,128)(2,1)} %get-tuple-element.185), channel_id=1, source_target_pairs={{0,8},{4,12},{8,0},{12,4},{1,9},{5,13},{9,1},{13,5},{2,10},{6,14},... | collective-permute-start | bytes 786440 | tf_op jit(solution)/shard_map/ppermute | solution.py:463
  37.9 23.4 %collective-permute-start.17 = (bf16[128,1024]{1,0:T(8,128)(2,1)}, bf16[128,1024]{1,0:T(8,128)(2,1)S(1)}, u32[]{:S(2)}, u32[]{:S(2)}) collective-permute-start(bf16[128,1024]{1,0:T(8,128)(2,1)} %get-tuple-element.186), channel_id=1, source_target_pairs={{0,4},{4,0},{8,12},{12,8},{1,5},{5,1},{9,13},{13,9},{2,6},{6,2},{1... | collective-permute-start | bytes 786440 | tf_op jit(solution)/shard_map/ppermute | solution.py:463
  38.9 1.6 %copy-start.1 = (bf16[1,4096,256]{2,1,0:T(8,128)(2,1)S(1)}, bf16[1,4096,256]{2,1,0:T(8,128)(2,1)}, u32[]{:S(2)}) copy-start(bf16[1,4096,256]{2,1,0:T(8,128)(2,1)} %up_ref.3) | copy-start | bytes 6291460
  40.5 7.0 %copy-start.3 = (bf16[1,1024,1024]{2,1,0:T(8,128)(2,1)S(1)}, bf16[1,1024,1024]{2,1,0:T(8,128)(2,1)}, u32[]{:S(2)}) copy-start(bf16[1,1024,1024]{2,1,0:T(8,128)(2,1)} %param.19) | copy-start | bytes 6291460
  47.5 2.1 %collective-permute-start = (bf16[256,1024]{1,0:T(8,128)(2,1)}, bf16[256,1024]{1,0:T(8,128)(2,1)S(1)}, u32[]{:S(2)}, u32[]{:S(2)}) collective-permute-start(bf16[256,1024]{1,0:T(8,128)(2,1)} %get-tuple-element.76.refs_0_), channel_id=1, source_target_pairs={{0,1},{1,0},{2,3},{3,2},{4,5},{5,4},{6,7},{7,6},{8,9},{9,8},{10,11... | collective-permute-start | bytes 1572872 | tf_op jit(solution)/shard_map/cond/branch_1_fun/ppermute | solution.py:466
  51.4 1.7 %collective-permute-start.2 = (bf16[256,256]{1,0:T(8,128)(2,1)S(1)}, bf16[256,256]{1,0:T(8,128)(2,1)S(1)}, u32[]{:S(2)}, u32[]{:S(2)}) collective-permute-start(bf16[256,256]{1,0:T(8,128)(2,1)S(1)} %branch_1_fun.10.refs_0_), channel_id=1, source_target_pairs={{0,1},{1,0},{2,3},{3,2},{4,5},{5,4},{6,7},{7,6},{8,9},{9,8},{10,11... | collective-permute-start | bytes 393224 | tf_op jit(solution)/shard_map/cond/branch_1_fun/ppermute | solution.py:466
  51.6 5.9 %collective-permute-start.1 = (bf16[256,256]{1,0:T(8,128)(2,1)S(1)}, bf16[256,256]{1,0:T(8,128)(2,1)}, u32[]{:S(2)}, u32[]{:S(2)}) collective-permute-start(bf16[256,256]{1,0:T(8,128)(2,1)S(1)} %branch_1_fun.10.refs_0_), channel_id=1, source_target_pairs={{0,2},{1,3},{2,0},{3,1},{4,6},{5,7},{6,4},{7,5},{8,10},{9,11},{10,... | collective-permute-start | bytes 393224 | tf_op jit(solution)/shard_map/cond/branch_1_fun/ppermute | solution.py:466
  57.5 1.7 %collective-permute-start.3 = (bf16[256,256]{1,0:T(8,128)(2,1)}, bf16[256,256]{1,0:T(8,128)(2,1)}, u32[]{:S(2)}, u32[]{:S(2)}) collective-permute-start(bf16[256,256]{1,0:T(8,128)(2,1)} %collective-permute-done.1), channel_id=1, source_target_pairs={{0,1},{1,0},{2,3},{3,2},{4,5},{5,4},{6,7},{7,6},{8,9},{9,8},{10,11... | collective-permute-start | bytes 393224 | tf_op jit(solution)/shard_map/cond/branch_1_fun/ppermute | solution.py:466
  63.3 8.9 %collective-permute-start.21 = (bf16[256,1024]{1,0:T(8,128)(2,1)S(1)}, bf16[256,1024]{1,0:T(8,128)(2,1)S(1)}, u32[]{:S(2)}, u32[]{:S(2)}) collective-permute-start(bf16[256,1024]{1,0:T(8,128)(2,1)S(1)} %shard_map.75.refs_0_), channel_id=1, source_target_pairs={{0,1},{1,0},{2,3},{3,2},{4,5},{5,4},{6,7},{7,6},{8,9},{9,8},{10,11... | collective-permute-start | bytes 1572872 | tf_op jit(solution)/shard_map/ppermute | solution.py:466
  63.4 14.4 %collective-permute-start.20 = (bf16[256,1024]{1,0:T(8,128)(2,1)S(1)}, bf16[256,1024]{1,0:T(8,128)(2,1)}, u32[]{:S(2)}, u32[]{:S(2)}) collective-permute-start(bf16[256,1024]{1,0:T(8,128)(2,1)S(1)} %shard_map.75.refs_0_), channel_id=1, source_target_pairs={{0,2},{1,3},{2,0},{3,1},{4,6},{5,7},{6,4},{7,5},{8,10},{9,11},{10,... | collective-permute-start | bytes 1572872 | tf_op jit(solution)/shard_map/ppermute | solution.py:466
  67.1 24.8 %collective-permute-start.22 = (bf16[128,1024]{1,0:T(8,128)(2,1)}, bf16[128,1024]{1,0:T(8,128)(2,1)}, u32[]{:S(2)}, u32[]{:S(2)}) collective-permute-start(bf16[128,1024]{1,0:T(8,128)(2,1)} %get-tuple-element.209), channel_id=1, source_target_pairs={{0,12},{4,8},{8,4},{12,0},{1,13},{5,9},{9,5},{13,1},{2,14},{6,10},... | collective-permute-start | bytes 786440 | tf_op jit(solution)/shard_map/ppermute | solution.py:463
  68.7 24.3 %collective-permute-start.23 = (bf16[128,1024]{1,0:T(8,128)(2,1)}, bf16[128,1024]{1,0:T(8,128)(2,1)}, u32[]{:S(2)}, u32[]{:S(2)}) collective-permute-start(bf16[128,1024]{1,0:T(8,128)(2,1)} %get-tuple-element.210), channel_id=1, source_target_pairs={{0,8},{4,12},{8,0},{12,4},{1,9},{5,13},{9,1},{13,5},{2,10},{6,14},... | collective-permute-start | bytes 786440 | tf_op jit(solution)/shard_map/ppermute | solution.py:463
  69.6 23.4 %collective-permute-start.24 = (bf16[128,1024]{1,0:T(8,128)(2,1)}, bf16[128,1024]{1,0:T(8,128)(2,1)}, u32[]{:S(2)}, u32[]{:S(2)}) collective-permute-start(bf16[128,1024]{1,0:T(8,128)(2,1)} %get-tuple-element.211), channel_id=1, source_target_pairs={{0,4},{4,0},{8,12},{12,8},{1,5},{5,1},{9,13},{13,9},{2,6},{6,2},{1... | collective-permute-start | bytes 786440 | tf_op jit(solution)/shard_map/ppermute | solution.py:463
  73.8 4.0 %copy-start.4 = (bf16[1,1024,1024]{2,1,0:T(8,128)(2,1)S(1)}, bf16[1,1024,1024]{2,1,0:T(8,128)(2,1)}, u32[]{:S(2)}) copy-start(bf16[1,1024,1024]{2,1,0:T(8,128)(2,1)} %param.19) | copy-start | bytes 6291460
  77.9 2.1 %collective-permute-start.4 = (bf16[256,1024]{1,0:T(8,128)(2,1)}, bf16[256,1024]{1,0:T(8,128)(2,1)S(1)}, u32[]{:S(2)}, u32[]{:S(2)}) collective-permute-start(bf16[256,1024]{1,0:T(8,128)(2,1)} %get-tuple-element.88.refs_0_), channel_id=1, source_target_pairs={{0,1},{1,0},{2,3},{3,2},{4,5},{5,4},{6,7},{7,6},{8,9},{9,8},{10,11... | collective-permute-start | bytes 1572872 | tf_op jit(solution)/shard_map/cond/branch_1_fun/ppermute | solution.py:466
  81.8 1.4 %collective-permute-start.6 = (bf16[256,256]{1,0:T(8,128)(2,1)S(1)}, bf16[256,256]{1,0:T(8,128)(2,1)S(1)}, u32[]{:S(2)}, u32[]{:S(2)}) collective-permute-start(bf16[256,256]{1,0:T(8,128)(2,1)S(1)} %branch_1_fun.12.refs_0_), channel_id=1, source_target_pairs={{0,1},{1,0},{2,3},{3,2},{4,5},{5,4},{6,7},{7,6},{8,9},{9,8},{10,11... | collective-permute-start | bytes 393224 | tf_op jit(solution)/shard_map/cond/branch_1_fun/ppermute | solution.py:466
  82.0 5.9 %collective-permute-start.5 = (bf16[256,256]{1,0:T(8,128)(2,1)S(1)}, bf16[256,256]{1,0:T(8,128)(2,1)}, u32[]{:S(2)}, u32[]{:S(2)}) collective-permute-start(bf16[256,256]{1,0:T(8,128)(2,1)S(1)} %branch_1_fun.12.refs_0_), channel_id=1, source_target_pairs={{0,2},{1,3},{2,0},{3,1},{4,6},{5,7},{6,4},{7,5},{8,10},{9,11},{10,... | collective-permute-start | bytes 393224 | tf_op jit(solution)/shard_map/cond/branch_1_fun/ppermute | solution.py:466
  87.8 1.7 %collective-permute-start.7 = (bf16[256,256]{1,0:T(8,128)(2,1)}, bf16[256,256]{1,0:T(8,128)(2,1)}, u32[]{:S(2)}, u32[]{:S(2)}) collective-permute-start(bf16[256,256]{1,0:T(8,128)(2,1)} %collective-permute-done.5), channel_id=1, source_target_pairs={{0,1},{1,0},{2,3},{3,2},{4,5},{5,4},{6,7},{7,6},{8,9},{9,8},{10,11... | collective-permute-start | bytes 393224 | tf_op jit(solution)/shard_map/cond/branch_1_fun/ppermute | solution.py:466
  93.0 11.1 %collective-permute-start.25 = (bf16[128,1024]{1,0:T(8,128)(2,1)S(1)}, bf16[128,1024]{1,0:T(8,128)(2,1)S(1)}, u32[]{:S(2)}, u32[]{:S(2)}) collective-permute-start(bf16[128,1024]{1,0:T(8,128)(2,1)S(1)} %get-tuple-element.237), channel_id=1, source_target_pairs={{0,12},{4,8},{8,4},{12,0},{1,13},{5,9},{9,5},{13,1},{2,14},{6,10},... | collective-permute-start | bytes 786440 | tf_op jit(solution)/shard_map/ppermute | solution.py:463
  94.2 22.3 %collective-permute-start.26 = (bf16[128,1024]{1,0:T(8,128)(2,1)S(1)}, bf16[128,1024]{1,0:T(8,128)(2,1)S(1)}, u32[]{:S(2)}, u32[]{:S(2)}) collective-permute-start(bf16[128,1024]{1,0:T(8,128)(2,1)S(1)} %get-tuple-element.238), channel_id=1, source_target_pairs={{0,8},{4,12},{8,0},{12,4},{1,9},{5,13},{9,1},{13,5},{2,10},{6,14},... | collective-permute-start | bytes 786440 | tf_op jit(solution)/shard_map/ppermute | solution.py:463
  94.2 22.3 %collective-permute-start.27 = (bf16[128,1024]{1,0:T(8,128)(2,1)S(1)}, bf16[128,1024]{1,0:T(8,128)(2,1)S(1)}, u32[]{:S(2)}, u32[]{:S(2)}) collective-permute-start(bf16[128,1024]{1,0:T(8,128)(2,1)S(1)} %get-tuple-element.239), channel_id=1, source_target_pairs={{0,4},{4,0},{8,12},{12,8},{1,5},{5,1},{9,13},{13,9},{2,6},{6,2},{1... | collective-permute-start | bytes 786440 | tf_op jit(solution)/shard_map/ppermute | solution.py:463
  (1 other events, 1.6 us)

commit v15 on v11

--- a/solution.py
+++ b/solution.py
@@ -253,23 +253,28 @@
     )(order, gate_weight, up_weight, *xs)
 
 
-def gate_up_far_kernel(parts, gate_before, up_before, gate_ref, up_ref, *refs):
-    xs, out_ref = refs[:parts], refs[parts]
+def gate_up_far_kernel(parts, first, last, gate_before, up_before, gate_ref, up_ref, *refs):
+    xs, outs = refs[:parts], refs[parts:]
     gate, up = gate_before[...], up_before[...]
     for i in range(parts):
         x = xs[i][...]
-        gate = gate + dot(x, gate_ref[i])
-        up = up + dot(x, up_ref[i])
-    out_ref[...] = (gate * jax.nn.sigmoid(gate) * up).astype(BF16)
-
-
-def gate_up_far(xs, before):
-    size, units = before[0].shape
-    return pl.pallas_call(
-        functools.partial(gate_up_far_kernel, len(xs)),
-        out_shape=jax.ShapeDtypeStruct((size, units), BF16),
+        gate = gate + dot(x, gate_ref[first + i])
+        up = up + dot(x, up_ref[first + i])
+    if last:
+        outs[0][...] = (gate * jax.nn.sigmoid(gate) * up).astype(BF16)
+    else:
+        outs[0][...] = gate
+        outs[1][...] = up
+
+
+def gate_up_far(xs, before, first, last):
+    shape = before[0].shape
+    sums = [jax.ShapeDtypeStruct(shape, F32)] * 2
+    return pl.pallas_call(
+        functools.partial(gate_up_far_kernel, len(xs), first, last),
+        out_shape=[jax.ShapeDtypeStruct(shape, BF16)] if last else sums,
         in_specs=whole(4 + len(xs)),
-        out_specs=whole(1)[0],
+        out_specs=whole(1 if last else 2),
         compiler_params=params(),
         cost_estimate=COST,
     )(*before, *xs)
@@ -522,7 +527,10 @@
 
     def far_half(far, sums):
         far = spread(far)
-        hidden = gate_up_far(far, sums)
+        gate, up, *weights = sums
+        sums = gate_up_far(far[:1], (gate, up, *weights), 0, False)
+        far, sums = lax.optimization_barrier((far[1:], sums))
+        hidden = gate_up_far(far, (*sums, *weights), 1, True)[0]
         far = swap(hidden, bits[0])
         partial = down_first(order, near_places, far_places, down_weight, spread(hidden))
         far, partial = lax.optimization_barrier((far, partial))
@@ -568,7 +576,8 @@
         far, partial = fenced(k, far_half, across, sums)
         moved = partial
     results = settle(BATCHES - 1, far, partial)
-    results, gathered, waiting[-1] = lax.optimization_barrier((results, gathered, waiting[-1]))
+    results, waiting[-1] = lax.optimization_barrier((list(results), waiting[-1]))
+    results[-1], gathered = lax.optimization_barrier((results[-1], gathered))
     waiting.append(exchange(results))
     weights = slot_weights(place, logits, gathered, code)
     total = None

time: 119 us -> 117 us (0.983)
  starting transfers between devices: 28.9 us -> 26.9 us
    ppermute x14, starting transfers between devices: 8.41 us -> 6.43 us  [swap(): return lax.ppermute(x, 'dp', [(i, i ^ bit) for i in range(width_parts)])]
    pallas_call x2 -> x4, Pallas kernels: 3.51 us -> 3.84 us  [gate_up_far(): pl.pallas_call(functools.partial(gate_up_far_kernel, len(xs), first, last...]
  transfers between devices with their start and end apart: 28 -> 28, of which waited for: 15 -> 17; matrix products, arithmetic and copies ran while one was open for 3% -> 3% of each run, Pallas kernels for 20% -> 21%
where the time goes in v15:
time: 117 us; the launch traced here: 116 us
  waiting for transfers between devices  48.2 us (41%)
  Pallas kernels  32.7 us (28%)
  starting transfers between devices  26.9 us (23%)
  local copies, waits for them, and re-layouts  3.89 us (3%)
  other arithmetic  2.93 us (3%)
  between operations  1.53 us (1%)
    ppermute x14, waiting for transfers between devices, along_expert(): return lax.ppermute(x, 'expert', [(i, i ^ shift) for i in range(experts)])  27.1 us
    ppermute x14, waiting for transfers between devices, swap(): return lax.ppermute(x, 'dp', [(i, i ^ bit) for i in range(width_parts)])  21 us
    ppermute x14, starting transfers between devices, along_expert(): return lax.ppermute(x, 'expert', [(i, i ^ shift) for i in range(experts)])  20.4 us
    ppermute x14, starting transfers between devices, swap(): return lax.ppermute(x, 'dp', [(i, i ^ bit) for i in range(width_parts)])  6.43 us
    pallas_call x2, Pallas kernels, down_last(): pl.pallas_call(functools.partial(down_last_kernel, parts, experts, k, dir...  5.47 us
    pallas_call x2, Pallas kernels, gate_up_near(): pl.pallas_call(functools.partial(gate_up_near_kernel, parts, near, far),...  4.4 us
    pallas_call x2, Pallas kernels, compact(): pl.pallas_call(functools.partial(compact_kernel, experts, k), out_shape=j...  3.94 us
    pallas_call x4, Pallas kernels, gate_up_far(): pl.pallas_call(functools.partial(gate_up_far_kernel, len(xs), first, last...  3.84 us
  transfers between devices with their start and end apart: 28, of which 17 were waited for; matrix products, arithmetic and copies ran while one was open for 3% of the time, Pallas kernels for 21%

profile of v15, /device:TPU:0, one launch (start us, length us, event | category | flops | bytes accessed | tf_op | source)
XLA Modules:
  0.0 116.2 jit_solution(13440648510974081020)
XLA Ops:
  0.0 2.6 %shard_map.73 = (s32[4,512]{1,0:T(4,128)S(1)}, bf16[128,1024]{1,0:T(8,128)(2,1)S(1)}, bf16[128,1024]{1,0:T(8,128)(2,1)}, bf16[128,1024]{1,0:T(8,128)(2,1)}, bf16[128,1024]{1,0:T(8,128)(2,1)}) custom-call(s32[1]{0:T(128)} %bitcast.1.place_ref, s32[4,512]{1,0:T(4,128)} %picks_in.1, bf16[512,1024]{1,0:T(8,128)(2,1)} %tokens_ref.1), custom_call_target="tpu_custom_call" | custom-call | flops 1024 | bytes 1024 | tf_op jit(solution)/shard_map/pallas_call | solution.py:108
  2.6 5.1 %collective-permute-start.11 = (bf16[128,1024]{1,0:T(8,128)(2,1)}, bf16[128,1024]{1,0:T(8,128)(2,1)S(1)}, u32[]{:S(2)}, u32[]{:S(2)}) collective-permute-start(bf16[128,1024]{1,0:T(8,128)(2,1)} %get-tuple-element.182), channel_id=1, source_target_pairs={{0,12},{4,8},{8,4},{12,0},{1,13},{5,9},{9,5},{13,1},{2,14},{6,10},... | collective-permute-start | bytes 786440 | tf_op jit(solution)/shard_map/ppermute | solution.py:468
  11.2 14.5 %conditional.4 = (bf16[128,1024]{1,0:T(8,128)(2,1)}, bf16[128,1024]{1,0:T(8,128)(2,1)}, bf16[128,1024]{1,0:T(8,128)(2,1)}, bf16[128,1024]{1,0:T(8,128)(2,1)}, f3...) conditional(s32[]{:T(128)} %convert_element_type.16, () %tuple.49, (s32[4,512]{1,0:T(4,128)S(1)}, ...), branch_computations={%region_3.4_spmd, %region_4.5_spmd} | conditional | flops 10240 | bytes 1073216 | solution.py:526
  11.2 1.8 %branch_1_fun.10 = f32[4,512]{1,0:T(4,128)S(1)} custom-call(bf16[4,1024]{1,0:T(4,128)(2,1)} %get-tuple-element.60.router_ref, bf16[512,1024]{1,0:T(8,128)(2,1)} %get-tuple-element.55.tokens_ref), custom_call_target="tpu_custom_call" | custom-call | flops 1024 | bytes 1024 | tf_op jit(solution)/shard_map/cond/branch_1_fun/pallas_call | solution.py:134
  14.6 2.0 %collective-permute-done.8 = f32[4,512]{1,0:T(4,128)S(1)} collective-permute-done((f32[4,512]{1,0:T(4,128)S(1)}, f32[4,512]{1,0:T(4,128)S(1)}, u32[]{:S(2)}, u32[]{:S(2)}) %collective-permute-start.8) | collective-permute-done | bytes 8224 | tf_op jit(solution)/shard_map/cond/branch_1_fun/ppermute | solution.py:471
  19.8 2.7 %branch_1_fun.9 = (bf16[128,1024]{1,0:T(8,128)(2,1)}, bf16[128,1024]{1,0:T(8,128)(2,1)}, bf16[128,1024]{1,0:T(8,128)(2,1)}, bf16[128,1024]{1,0:T(8,128)(2,1)}) custom-call(s32[4,512]{1,0:T(4,128)S(1)} %get-tuple-element.54.code_ref, bf16[512,1024]{1,0:T(8,128)(2,1)} %get-tuple-element.55.tokens_ref), custom_call_target="tpu_custom_call" | custom-call | flops 1024 | bytes 1024 | tf_op jit(solution)/shard_map/cond/branch_1_fun/pallas_call | solution.py:155
  22.5 2.5 %collective-permute-done.10 = f32[1,4,512]{2,1,0:T(4,128)S(1)} collective-permute-done((f32[1,4,512]{2,1,0:T(4,128)}, f32[1,4,512]{2,1,0:T(4,128)S(1)}, u32[]{:S(2)}, u32[]{:S(2)}) %collective-permute-start.10) | collective-permute-done | bytes 8224 | tf_op jit(solution)/shard_map/cond/branch_1_fun/ppermute | solution.py:468
  25.7 4.5 %collective-permute-done.12 = bf16[128,1024]{1,0:T(8,128)(2,1)S(1)} collective-permute-done((bf16[128,1024]{1,0:T(8,128)(2,1)}, bf16[128,1024]{1,0:T(8,128)(2,1)S(1)}, u32[]{:S(2)}, u32[]{:S(2)}) %collective-permute-start.12) | collective-permute-done | bytes 262176 | tf_op jit(solution)/shard_map/ppermute | solution.py:468
  30.2 1.9 %conditional.5 = (bf16[256,1024]{1,0:T(8,128)(2,1)}) conditional(s32[]{:T(128)} %convert_element_type.16, () %tuple.55, (s32[2,4]{1,0:T(2,128)S(1)}, s32[2,4]{1,0:T(2,128)S(1)}, bf16[128,1024]{1,0:T(8,128)(2,1)S(1)}, bf16[128,1024]{1,0:T(8,128)(2,1)S(1)}, bf16[128,1024]{1,0:T(8,128)(2,1)S(1)}, /*index=5*/bf16[128,1024]{1,0:T(8,128)(2,1)S(1)}) %tuple.56), branch_computations={%region_6.7_spmd, %region_7.8_spmd} | conditional | flops 1024 | bytes 524298 | solution.py:548
  30.2 1.9 %branch_1_fun.11 = bf16[256,1024]{1,0:T(8,128)(2,1)} custom-call(s32[2,4]{1,0:T(2,128)S(1)} %get-tuple-element.61.offset_ref, s32[2,4]{1,0:T(2,128)S(1)} %get-tuple-element.62.count_ref, bf16[128,1024]{1,0:T(8,128)(2,1)S(1)} %get-tuple-element.63.refs_0_, bf16[128,1024]{1,0:T(8,128)(2,1)S(1)} %get-tuple-element.64.refs_1_, ...), custom_call_target="tpu_custom_call" | custom-call | flops 1024 | bytes 1024 | tf_op jit(solution)/shard_map/cond/branch_1_fun/pallas_call | solution.py:192
  33.8 2.5 %collective-permute-start.14 = (bf16[128,1024]{1,0:T(8,128)(2,1)}, bf16[128,1024]{1,0:T(8,128)(2,1)S(1)}, u32[]{:S(2)}, u32[]{:S(2)}) collective-permute-start(bf16[128,1024]{1,0:T(8,128)(2,1)} %get-tuple-element.191), channel_id=1, source_target_pairs={{0,12},{4,8},{8,4},{12,0},{1,13},{5,9},{9,5},{13,1},{2,14},{6,10},... | collective-permute-start | bytes 786440 | tf_op jit(solution)/shard_map/ppermute | solution.py:468
  36.3 1.9 %collective-permute-start.16 = (bf16[128,1024]{1,0:T(8,128)(2,1)}, bf16[128,1024]{1,0:T(8,128)(2,1)S(1)}, u32[]{:S(2)}, u32[]{:S(2)}) collective-permute-start(bf16[128,1024]{1,0:T(8,128)(2,1)} %get-tuple-element.193), channel_id=1, source_target_pairs={{0,4},{4,0},{8,12},{12,8},{1,5},{5,1},{9,13},{13,9},{2,6},{6,2},{1... | collective-permute-start | bytes 786440 | tf_op jit(solution)/shard_map/ppermute | solution.py:468
  39.9 2.6 %shard_map.74 = (f32[256,256]{1,0:T(8,128)S(1)}, f32[256,256]{1,0:T(8,128)S(1)}, bf16[2,1024,256]{2,1,0:T(8,128)(2,1)S(1)}, bf16[2,1024,256]{2,1,0:T(8,128)(2,1)S(1)}) custom-call(s32[4]{0:T(128)S(1)} %pad_add_fusion.order_ref, bf16[1,4096,256]{2,1,0:T(8,128)(2,1)S(1)} %copy-done, bf16[1,4096,256]{2,1,0:T(8,128)(2,1)S(1)} %copy-done.1, ...), custom_call_target="tpu_custom_call" | custom-call | flops 1024 | bytes 1024 | tf_op jit(solution)/shard_map/pallas_call | solution.py:240
  42.5 4.4 %collective-permute-done.17 = bf16[256,1024]{1,0:T(8,128)(2,1)} collective-permute-done((bf16[256,1024]{1,0:T(8,128)(2,1)}, bf16[256,1024]{1,0:T(8,128)(2,1)}, u32[]{:S(2)}, u32[]{:S(2)}) %collective-permute-start.17) | collective-permute-done | bytes 524320 | tf_op jit(solution)/shard_map/ppermute | solution.py:471
  46.9 10.3 %conditional.6 = (bf16[256,256]{1,0:T(8,128)(2,1)}, bf16[256,256]{1,0:T(8,128)(2,1)}, f32[256,1024]{1,0:T(8,128)S(1)}, bf16[2,256,1024]{2,1,0:T(8,128)(2,1)S(1)}) conditional(s32[]{:T(128)} %convert_element_type.16, () %tuple.54, (bf16[256,1024]{1,0:T(8,128)(2,1)}, f32[256,256]{1,0:T(8,128)S(1)}, f32[256,256]{1,0:T(8,128)S(1)}, ...), branch_computations={%region_8.9_spmd, %region_9.10_spmd} | conditional | flops 3072 | bytes 3673280 | solution.py:548
  52.8 2.8 %collective-permute-done.1 = bf16[256,256]{1,0:T(8,128)(2,1)} collective-permute-done((bf16[256,256]{1,0:T(8,128)(2,1)S(1)}, bf16[256,256]{1,0:T(8,128)(2,1)}, u32[]{:S(2)}, u32[]{:S(2)}) %collective-permute-start.1) | collective-permute-done | bytes 131104 | tf_op jit(solution)/shard_map/cond/branch_1_fun/ppermute | solution.py:471
  55.6 1.7 %collective-permute-done.3 = bf16[256,256]{1,0:T(8,128)(2,1)} collective-permute-done((bf16[256,256]{1,0:T(8,128)(2,1)}, bf16[256,256]{1,0:T(8,128)(2,1)}, u32[]{:S(2)}, u32[]{:S(2)}) %collective-permute-start.3) | collective-permute-done | bytes 131104 | tf_op jit(solution)/shard_map/cond/branch_1_fun/ppermute | solution.py:471
  58.5 2.0 %shard_map.75.refs_0_ = bf16[256,1024]{1,0:T(8,128)(2,1)S(1)} custom-call(s32[2,4]{1,0:T(2,128)S(1)} %get-tuple-element.253.offset_ref, s32[2,4]{1,0:T(2,128)S(1)} %get-tuple-element.254.count_ref, bf16[128,1024]{1,0:T(8,128)(2,1)} %get-tuple-element.205.refs_0_, bf16[128,1024]{1,0:T(8,128)(2,1)S(1)} %collective-permute-done.14.refs_1_, ...), custom_call_target="tpu_custom_call" | custom-call | flops 1024 | bytes 1024 | tf_op jit(solution)/shard_map/pallas_call | solution.py:192
  61.2 3.1 %shard_map.76 = (bf16[128,1024]{1,0:T(8,128)(2,1)S(1)}, bf16[128,1024]{1,0:T(8,128)(2,1)}, bf16[128,1024]{1,0:T(8,128)(2,1)}, bf16[128,1024]{1,0:T(8,128)(2,1)}) custom-call(s32[2,4]{1,0:T(2,128)S(1)} %get-tuple-element.253.offset_ref, s32[2,4]{1,0:T(2,128)S(1)} %get-tuple-element.254.count_ref, f32[256,1024]{1,0:T(8,128)S(1)} %get-tuple-element.211.before_ref, ...), custom_call_target="tpu_custom_call" | custom-call | flops 1024 | bytes 1024 | tf_op jit(solution)/shard_map/pallas_call | solution.py:365
  64.3 2.4 %collective-permute-start.21 = (bf16[128,1024]{1,0:T(8,128)(2,1)}, bf16[128,1024]{1,0:T(8,128)(2,1)}, u32[]{:S(2)}, u32[]{:S(2)}) collective-permute-start(bf16[128,1024]{1,0:T(8,128)(2,1)} %get-tuple-element.216), channel_id=1, source_target_pairs={{0,12},{4,8},{8,4},{12,0},{1,13},{5,9},{9,5},{13,1},{2,14},{6,10},... | collective-permute-start | bytes 786440 | tf_op jit(solution)/shard_map/ppermute | solution.py:468
  66.7 2.0 %collective-permute-start.23 = (bf16[128,1024]{1,0:T(8,128)(2,1)}, bf16[128,1024]{1,0:T(8,128)(2,1)}, u32[]{:S(2)}, u32[]{:S(2)}) collective-permute-start(bf16[128,1024]{1,0:T(8,128)(2,1)} %get-tuple-element.218), channel_id=1, source_target_pairs={{0,4},{4,0},{8,12},{12,8},{1,5},{5,1},{9,13},{13,9},{2,6},{6,2},{1... | collective-permute-start | bytes 786440 | tf_op jit(solution)/shard_map/ppermute | solution.py:468
  71.0 1.8 %shard_map.77 = (f32[256,256]{1,0:T(8,128)S(1)}, f32[256,256]{1,0:T(8,128)S(1)}, bf16[2,1024,256]{2,1,0:T(8,128)(2,1)S(1)}, bf16[2,1024,256]{2,1,0:T(8,128)(2,1)S(1)}) custom-call(s32[4]{0:T(128)S(1)} %pad_add_fusion.order_ref, bf16[1,4096,256]{2,1,0:T(8,128)(2,1)S(1)} %copy-done, bf16[1,4096,256]{2,1,0:T(8,128)(2,1)S(1)} %copy-done.2, ...), custom_call_target="tpu_custom_call" | custom-call | flops 1024 | bytes 1024 | tf_op jit(solution)/shard_map/pallas_call | solution.py:240
  72.8 2.2 %collective-permute-done.19 = bf16[256,1024]{1,0:T(8,128)(2,1)} collective-permute-done((bf16[256,1024]{1,0:T(8,128)(2,1)S(1)}, bf16[256,1024]{1,0:T(8,128)(2,1)}, u32[]{:S(2)}, u32[]{:S(2)}) %collective-permute-start.19) | collective-permute-done | bytes 524320 | tf_op jit(solution)/shard_map/ppermute | solution.py:471
  75.0 10.3 %conditional.7 = (bf16[256,256]{1,0:T(8,128)(2,1)}, bf16[256,256]{1,0:T(8,128)(2,1)}, f32[256,1024]{1,0:T(8,128)S(1)}, bf16[2,256,1024]{2,1,0:T(8,128)(2,1)S(1)}) conditional(s32[]{:T(128)} %convert_element_type.17, () %tuple.51, (bf16[256,1024]{1,0:T(8,128)(2,1)}, f32[256,256]{1,0:T(8,128)S(1)}, f32[256,256]{1,0:T(8,128)S(1)}, ...), branch_computations={%region_10.11_spmd, %region_11.12_spmd} | conditional | flops 3072 | bytes 3673280 | solution.py:548
  80.6 3.1 %collective-permute-done.5 = bf16[256,256]{1,0:T(8,128)(2,1)} collective-permute-done((bf16[256,256]{1,0:T(8,128)(2,1)S(1)}, bf16[256,256]{1,0:T(8,128)(2,1)}, u32[]{:S(2)}, u32[]{:S(2)}) %collective-permute-start.5) | collective-permute-done | bytes 131104 | tf_op jit(solution)/shard_map/cond/branch_1_fun/ppermute | solution.py:471
  83.7 1.7 %collective-permute-done.7 = bf16[256,256]{1,0:T(8,128)(2,1)} collective-permute-done((bf16[256,256]{1,0:T(8,128)(2,1)}, bf16[256,256]{1,0:T(8,128)(2,1)}, u32[]{:S(2)}, u32[]{:S(2)}) %collective-permute-start.7) | collective-permute-done | bytes 131104 | tf_op jit(solution)/shard_map/cond/branch_1_fun/ppermute | solution.py:471
  85.4 2.4 %shard_map.78 = (bf16[128,1024]{1,0:T(8,128)(2,1)S(1)}, bf16[128,1024]{1,0:T(8,128)(2,1)S(1)}, bf16[128,1024]{1,0:T(8,128)(2,1)S(1)}, bf16[128,1024]{1,0:T(8,128)(2,1)S(1)}) custom-call(s32[2,4]{1,0:T(2,128)S(1)} %get-tuple-element.253.offset_ref, s32[2,4]{1,0:T(2,128)S(1)} %get-tuple-element.254.count_ref, f32[256,1024]{1,0:T(8,128)S(1)} %get-tuple-element.230.before_ref, ...), custom_call_target="tpu_custom_call" | custom-call | flops 1024 | bytes 1024 | tf_op jit(solution)/shard_map/pallas_call | solution.py:365
  91.2 2.4 %collective-permute-start.27 = (bf16[128,1024]{1,0:T(8,128)(2,1)S(1)}, bf16[128,1024]{1,0:T(8,128)(2,1)S(1)}, u32[]{:S(2)}, u32[]{:S(2)}) collective-permute-start(bf16[128,1024]{1,0:T(8,128)(2,1)S(1)} %get-tuple-element.248), channel_id=1, source_target_pairs={{0,4},{4,0},{8,12},{12,8},{1,5},{5,1},{9,13},{13,9},{2,6},{6,2},{1... | collective-permute-start | bytes 786440 | tf_op jit(solution)/shard_map/ppermute | solution.py:468
  94.7 1.9 %shard_map.80.refs_0_ = f32[512,1024]{1,0:T(8,128)S(1)} custom-call(s32[4,512]{1,0:T(4,128)S(1)} %get-tuple-element.175.code_ref, f32[4,512]{1,0:T(4,128)S(1)} %shard_map.79.weight_ref, bf16[128,1024]{1,0:T(8,128)(2,1)S(1)} %get-tuple-element.241.refs_0_, bf16[128,1024]{1,0:T(8,128)(2,1)} %collective-permute-done.21.refs_1_, ...), custom_call_target="tpu_custom_call" | custom-call | flops 1024 | bytes 1024 | tf_op jit(solution)/shard_map/pallas_call | solution.py:441
  96.6 3.7 %collective-permute-done.25.refs_2_ = bf16[128,1024]{1,0:T(8,128)(2,1)S(1)} collective-permute-done((bf16[128,1024]{1,0:T(8,128)(2,1)S(1)}, bf16[128,1024]{1,0:T(8,128)(2,1)S(1)}, u32[]{:S(2)}, u32[]{:S(2)}) %collective-permute-start.25) | collective-permute-done | bytes 262176 | tf_op jit(solution)/shard_map/ppermute | solution.py:468
  100.3 13.8 %collective-permute-done.26.refs_3_ = bf16[128,1024]{1,0:T(8,128)(2,1)S(1)} collective-permute-done((bf16[128,1024]{1,0:T(8,128)(2,1)S(1)}, bf16[128,1024]{1,0:T(8,128)(2,1)S(1)}, u32[]{:S(2)}, u32[]{:S(2)}) %collective-permute-start.26) | collective-permute-done | bytes 262176 | tf_op jit(solution)/shard_map/ppermute | solution.py:468
  114.1 1.9 %shard_map.81 = bf16[512,1024]{1,0:T(8,128)(2,1)} custom-call(s32[4,512]{1,0:T(4,128)S(1)} %get-tuple-element.175.code_ref, f32[4,512]{1,0:T(4,128)S(1)} %shard_map.79.weight_ref, f32[512,1024]{1,0:T(8,128)S(1)} %shard_map.80.refs_0_, bf16[128,1024]{1,0:T(8,128)(2,1)S(1)} %get-tuple-element.245.refs_1_, ...), custom_call_target="tpu_custom_call" | custom-call | flops 1024 | bytes 1024 | tf_op jit(solution)/shard_map/pallas_call | solution.py:441
  (67 shorter events, 31.1 us)
Async XLA Ops:
  2.6 23.1 %collective-permute-start.11 = (bf16[128,1024]{1,0:T(8,128)(2,1)}, bf16[128,1024]{1,0:T(8,128)(2,1)S(1)}, u32[]{:S(2)}, u32[]{:S(2)}) collective-permute-start(bf16[128,1024]{1,0:T(8,128)(2,1)} %get-tuple-element.182), channel_id=1, source_target_pairs={{0,12},{4,8},{8,4},{12,0},{1,13},{5,9},{9,5},{13,1},{2,14},{6,10},... | collective-permute-start | bytes 786440 | tf_op jit(solution)/shard_map/ppermute | solution.py:468
  7.7 22.5 %collective-permute-start.12 = (bf16[128,1024]{1,0:T(8,128)(2,1)}, bf16[128,1024]{1,0:T(8,128)(2,1)S(1)}, u32[]{:S(2)}, u32[]{:S(2)}) collective-permute-start(bf16[128,1024]{1,0:T(8,128)(2,1)} %get-tuple-element.183), channel_id=1, source_target_pairs={{0,8},{4,12},{8,0},{12,4},{1,9},{5,13},{9,1},{13,5},{2,10},{6,14},... | collective-permute-start | bytes 786440 | tf_op jit(solution)/shard_map/ppermute | solution.py:468
  7.7 22.5 %collective-permute-start.13 = (bf16[128,1024]{1,0:T(8,128)(2,1)}, bf16[128,1024]{1,0:T(8,128)(2,1)S(1)}, u32[]{:S(2)}, u32[]{:S(2)}) collective-permute-start(bf16[128,1024]{1,0:T(8,128)(2,1)} %get-tuple-element.184), channel_id=1, source_target_pairs={{0,4},{4,0},{8,12},{12,8},{1,5},{5,1},{9,13},{13,9},{2,6},{6,2},{1... | collective-permute-start | bytes 786440 | tf_op jit(solution)/shard_map/ppermute | solution.py:468
  11.2 27.1 %copy-start = (bf16[1,4096,256]{2,1,0:T(8,128)(2,1)S(1)}, bf16[1,4096,256]{2,1,0:T(8,128)(2,1)}, u32[]{:S(2)}) copy-start(bf16[1,4096,256]{2,1,0:T(8,128)(2,1)} %gate_ref.3) | copy-start | bytes 6291460
  13.0 3.7 %collective-permute-start.8 = (f32[4,512]{1,0:T(4,128)S(1)}, f32[4,512]{1,0:T(4,128)S(1)}, u32[]{:S(2)}, u32[]{:S(2)}) collective-permute-start(f32[4,512]{1,0:T(4,128)S(1)} %branch_1_fun.10), channel_id=1, source_target_pairs={{0,2},{1,3},{2,0},{3,1},{4,6},{5,7},{6,4},{7,5},{8,10},{9,11},{10,... | collective-permute-start | bytes 24584 | tf_op jit(solution)/shard_map/cond/branch_1_fun/ppermute | solution.py:471
  16.7 1.2 %collective-permute-start.9 = (f32[4,512]{1,0:T(4,128)S(1)}, f32[4,512]{1,0:T(4,128)S(1)}, u32[]{:S(2)}, u32[]{:S(2)}) collective-permute-start(f32[4,512]{1,0:T(4,128)S(1)} %add.24), channel_id=1, source_target_pairs={{0,1},{1,0},{2,3},{3,2},{4,5},{5,4},{6,7},{7,6},{8,9},{9,8},{10,11... | collective-permute-start | bytes 24584 | tf_op jit(solution)/shard_map/cond/branch_1_fun/ppermute | solution.py:471
  18.4 6.6 %collective-permute-start.10 = (f32[1,4,512]{2,1,0:T(4,128)}, f32[1,4,512]{2,1,0:T(4,128)S(1)}, u32[]{:S(2)}, u32[]{:S(2)}) collective-permute-start(f32[1,4,512]{2,1,0:T(4,128)} %bitcast), channel_id=1, source_target_pairs={{0,4},{4,0},{8,12},{12,8},{1,5},{5,1},{9,13},{13,9},{2,6},{6,2},{1... | collective-permute-start | bytes 24584 | tf_op jit(solution)/shard_map/cond/branch_1_fun/ppermute | solution.py:468
  32.2 6.1 %collective-permute-start.18 = (bf16[256,1024]{1,0:T(8,128)(2,1)}, bf16[256,1024]{1,0:T(8,128)(2,1)S(1)}, u32[]{:S(2)}, u32[]{:S(2)}) collective-permute-start(bf16[256,1024]{1,0:T(8,128)(2,1)} %get-tuple-element.287.refs_0_), channel_id=1, source_target_pairs={{0,1},{1,0},{2,3},{3,2},{4,5},{5,4},{6,7},{7,6},{8,9},{9,8},{10,11... | collective-permute-start | bytes 1572872 | tf_op jit(solution)/shard_map/ppermute | solution.py:471
  32.3 14.7 %collective-permute-start.17 = (bf16[256,1024]{1,0:T(8,128)(2,1)}, bf16[256,1024]{1,0:T(8,128)(2,1)}, u32[]{:S(2)}, u32[]{:S(2)}) collective-permute-start(bf16[256,1024]{1,0:T(8,128)(2,1)} %get-tuple-element.287.refs_0_), channel_id=1, source_target_pairs={{0,2},{1,3},{2,0},{3,1},{4,6},{5,7},{6,4},{7,5},{8,10},{9,11},{10,... | collective-permute-start | bytes 1572872 | tf_op jit(solution)/shard_map/ppermute | solution.py:471
  33.8 23.5 %collective-permute-start.14 = (bf16[128,1024]{1,0:T(8,128)(2,1)}, bf16[128,1024]{1,0:T(8,128)(2,1)S(1)}, u32[]{:S(2)}, u32[]{:S(2)}) collective-permute-start(bf16[128,1024]{1,0:T(8,128)(2,1)} %get-tuple-element.191), channel_id=1, source_target_pairs={{0,12},{4,8},{8,4},{12,0},{1,13},{5,9},{9,5},{13,1},{2,14},{6,10},... | collective-permute-start | bytes 786440 | tf_op jit(solution)/shard_map/ppermute | solution.py:468
  36.3 22.2 %collective-permute-start.15 = (bf16[128,1024]{1,0:T(8,128)(2,1)}, bf16[128,1024]{1,0:T(8,128)(2,1)S(1)}, u32[]{:S(2)}, u32[]{:S(2)}) collective-permute-start(bf16[128,1024]{1,0:T(8,128)(2,1)} %get-tuple-element.192), channel_id=1, source_target_pairs={{0,8},{4,12},{8,0},{12,4},{1,9},{5,13},{9,1},{13,5},{2,10},{6,14},... | collective-permute-start | bytes 786440 | tf_op jit(solution)/shard_map/ppermute | solution.py:468
  36.3 22.2 %collective-permute-start.16 = (bf16[128,1024]{1,0:T(8,128)(2,1)}, bf16[128,1024]{1,0:T(8,128)(2,1)S(1)}, u32[]{:S(2)}, u32[]{:S(2)}) collective-permute-start(bf16[128,1024]{1,0:T(8,128)(2,1)} %get-tuple-element.193), channel_id=1, source_target_pairs={{0,4},{4,0},{8,12},{12,8},{1,5},{5,1},{9,13},{13,9},{2,6},{6,2},{1... | collective-permute-start | bytes 786440 | tf_op jit(solution)/shard_map/ppermute | solution.py:468
  39.9 7.0 %copy-start.3 = (bf16[1,1024,1024]{2,1,0:T(8,128)(2,1)S(1)}, bf16[1,1024,1024]{2,1,0:T(8,128)(2,1)}, u32[]{:S(2)}) copy-start(bf16[1,1024,1024]{2,1,0:T(8,128)(2,1)} %param.19) | copy-start | bytes 6291460
  46.9 2.1 %collective-permute-start = (bf16[256,1024]{1,0:T(8,128)(2,1)}, bf16[256,1024]{1,0:T(8,128)(2,1)S(1)}, u32[]{:S(2)}, u32[]{:S(2)}) collective-permute-start(bf16[256,1024]{1,0:T(8,128)(2,1)} %get-tuple-element.67.refs_0_), channel_id=1, source_target_pairs={{0,1},{1,0},{2,3},{3,2},{4,5},{5,4},{6,7},{7,6},{8,9},{9,8},{10,11... | collective-permute-start | bytes 1572872 | tf_op jit(solution)/shard_map/cond/branch_1_fun/ppermute | solution.py:471
  49.5 1.7 %collective-permute-start.2 = (bf16[256,256]{1,0:T(8,128)(2,1)S(1)}, bf16[256,256]{1,0:T(8,128)(2,1)S(1)}, u32[]{:S(2)}, u32[]{:S(2)}) collective-permute-start(bf16[256,256]{1,0:T(8,128)(2,1)S(1)} %branch_1_fun.13.refs_0_), channel_id=1, source_target_pairs={{0,1},{1,0},{2,3},{3,2},{4,5},{5,4},{6,7},{7,6},{8,9},{9,8},{10,11... | collective-permute-start | bytes 393224 | tf_op jit(solution)/shard_map/cond/branch_1_fun/ppermute | solution.py:471
  49.7 5.9 %collective-permute-start.1 = (bf16[256,256]{1,0:T(8,128)(2,1)S(1)}, bf16[256,256]{1,0:T(8,128)(2,1)}, u32[]{:S(2)}, u32[]{:S(2)}) collective-permute-start(bf16[256,256]{1,0:T(8,128)(2,1)S(1)} %branch_1_fun.13.refs_0_), channel_id=1, source_target_pairs={{0,2},{1,3},{2,0},{3,1},{4,6},{5,7},{6,4},{7,5},{8,10},{9,11},{10,... | collective-permute-start | bytes 393224 | tf_op jit(solution)/shard_map/cond/branch_1_fun/ppermute | solution.py:471
  55.6 1.7 %collective-permute-start.3 = (bf16[256,256]{1,0:T(8,128)(2,1)}, bf16[256,256]{1,0:T(8,128)(2,1)}, u32[]{:S(2)}, u32[]{:S(2)}) collective-permute-start(bf16[256,256]{1,0:T(8,128)(2,1)} %collective-permute-done.1), channel_id=1, source_target_pairs={{0,1},{1,0},{2,3},{3,2},{4,5},{5,4},{6,7},{7,6},{8,9},{9,8},{10,11... | collective-permute-start | bytes 393224 | tf_op jit(solution)/shard_map/cond/branch_1_fun/ppermute | solution.py:471
  60.5 8.9 %collective-permute-start.20 = (bf16[256,1024]{1,0:T(8,128)(2,1)S(1)}, bf16[256,1024]{1,0:T(8,128)(2,1)S(1)}, u32[]{:S(2)}, u32[]{:S(2)}) collective-permute-start(bf16[256,1024]{1,0:T(8,128)(2,1)S(1)} %shard_map.75.refs_0_), channel_id=1, source_target_pairs={{0,1},{1,0},{2,3},{3,2},{4,5},{5,4},{6,7},{7,6},{8,9},{9,8},{10,11... | collective-permute-start | bytes 1572872 | tf_op jit(solution)/shard_map/ppermute | solution.py:471
  60.6 14.4 %collective-permute-start.19 = (bf16[256,1024]{1,0:T(8,128)(2,1)S(1)}, bf16[256,1024]{1,0:T(8,128)(2,1)}, u32[]{:S(2)}, u32[]{:S(2)}) collective-permute-start(bf16[256,1024]{1,0:T(8,128)(2,1)S(1)} %shard_map.75.refs_0_), channel_id=1, source_target_pairs={{0,2},{1,3},{2,0},{3,1},{4,6},{5,7},{6,4},{7,5},{8,10},{9,11},{10,... | collective-permute-start | bytes 1572872 | tf_op jit(solution)/shard_map/ppermute | solution.py:471
  64.3 23.5 %collective-permute-start.21 = (bf16[128,1024]{1,0:T(8,128)(2,1)}, bf16[128,1024]{1,0:T(8,128)(2,1)}, u32[]{:S(2)}, u32[]{:S(2)}) collective-permute-start(bf16[128,1024]{1,0:T(8,128)(2,1)} %get-tuple-element.216), channel_id=1, source_target_pairs={{0,12},{4,8},{8,4},{12,0},{1,13},{5,9},{9,5},{13,1},{2,14},{6,10},... | collective-permute-start | bytes 786440 | tf_op jit(solution)/shard_map/ppermute | solution.py:468
  66.7 22.5 %collective-permute-start.22 = (bf16[128,1024]{1,0:T(8,128)(2,1)}, bf16[128,1024]{1,0:T(8,128)(2,1)}, u32[]{:S(2)}, u32[]{:S(2)}) collective-permute-start(bf16[128,1024]{1,0:T(8,128)(2,1)} %get-tuple-element.217), channel_id=1, source_target_pairs={{0,8},{4,12},{8,0},{12,4},{1,9},{5,13},{9,1},{13,5},{2,10},{6,14},... | collective-permute-start | bytes 786440 | tf_op jit(solution)/shard_map/ppermute | solution.py:468
  66.7 22.5 %collective-permute-start.23 = (bf16[128,1024]{1,0:T(8,128)(2,1)}, bf16[128,1024]{1,0:T(8,128)(2,1)}, u32[]{:S(2)}, u32[]{:S(2)}) collective-permute-start(bf16[128,1024]{1,0:T(8,128)(2,1)} %get-tuple-element.218), channel_id=1, source_target_pairs={{0,4},{4,0},{8,12},{12,8},{1,5},{5,1},{9,13},{13,9},{2,6},{6,2},{1... | collective-permute-start | bytes 786440 | tf_op jit(solution)/shard_map/ppermute | solution.py:468
  69.4 1.6 %copy-start.2 = (bf16[1,4096,256]{2,1,0:T(8,128)(2,1)S(1)}, bf16[1,4096,256]{2,1,0:T(8,128)(2,1)}, u32[]{:S(2)}) copy-start(bf16[1,4096,256]{2,1,0:T(8,128)(2,1)} %up_ref.3) | copy-start | bytes 6291460
  71.0 4.1 %copy-start.4 = (bf16[1,1024,1024]{2,1,0:T(8,128)(2,1)S(1)}, bf16[1,1024,1024]{2,1,0:T(8,128)(2,1)}, u32[]{:S(2)}) copy-start(bf16[1,1024,1024]{2,1,0:T(8,128)(2,1)} %param.19) | copy-start | bytes 6291460
  75.0 2.1 %collective-permute-start.4 = (bf16[256,1024]{1,0:T(8,128)(2,1)}, bf16[256,1024]{1,0:T(8,128)(2,1)S(1)}, u32[]{:S(2)}, u32[]{:S(2)}) collective-permute-start(bf16[256,1024]{1,0:T(8,128)(2,1)} %get-tuple-element.84.refs_0_), channel_id=1, source_target_pairs={{0,1},{1,0},{2,3},{3,2},{4,5},{5,4},{6,7},{7,6},{8,9},{9,8},{10,11... | collective-permute-start | bytes 1572872 | tf_op jit(solution)/shard_map/cond/branch_1_fun/ppermute | solution.py:471
  77.6 1.4 %collective-permute-start.6 = (bf16[256,256]{1,0:T(8,128)(2,1)S(1)}, bf16[256,256]{1,0:T(8,128)(2,1)S(1)}, u32[]{:S(2)}, u32[]{:S(2)}) collective-permute-start(bf16[256,256]{1,0:T(8,128)(2,1)S(1)} %branch_1_fun.16.refs_0_), channel_id=1, source_target_pairs={{0,1},{1,0},{2,3},{3,2},{4,5},{5,4},{6,7},{7,6},{8,9},{9,8},{10,11... | collective-permute-start | bytes 393224 | tf_op jit(solution)/shard_map/cond/branch_1_fun/ppermute | solution.py:471
  77.8 5.9 %collective-permute-start.5 = (bf16[256,256]{1,0:T(8,128)(2,1)S(1)}, bf16[256,256]{1,0:T(8,128)(2,1)}, u32[]{:S(2)}, u32[]{:S(2)}) collective-permute-start(bf16[256,256]{1,0:T(8,128)(2,1)S(1)} %branch_1_fun.16.refs_0_), channel_id=1, source_target_pairs={{0,2},{1,3},{2,0},{3,1},{4,6},{5,7},{6,4},{7,5},{8,10},{9,11},{10,... | collective-permute-start | bytes 393224 | tf_op jit(solution)/shard_map/cond/branch_1_fun/ppermute | solution.py:471
  83.7 1.7 %collective-permute-start.7 = (bf16[256,256]{1,0:T(8,128)(2,1)}, bf16[256,256]{1,0:T(8,128)(2,1)}, u32[]{:S(2)}, u32[]{:S(2)}) collective-permute-start(bf16[256,256]{1,0:T(8,128)(2,1)} %collective-permute-done.5), channel_id=1, source_target_pairs={{0,1},{1,0},{2,3},{3,2},{4,5},{5,4},{6,7},{7,6},{8,9},{9,8},{10,11... | collective-permute-start | bytes 393224 | tf_op jit(solution)/shard_map/cond/branch_1_fun/ppermute | solution.py:471
  85.4 5.9 %collective-permute-start.24 = (f32[2,4,512]{2,1,0:T(4,128)S(1)}, f32[2,4,512]{2,1,0:T(4,128)S(1)}, u32[]{:S(2)}, u32[]{:S(2)}) collective-permute-start(f32[2,4,512]{2,1,0:T(4,128)S(1)} %get-tuple-element.239), channel_id=1, source_target_pairs={{0,8},{4,12},{8,0},{12,4},{1,9},{5,13},{9,1},{13,5},{2,10},{6,14},... | collective-permute-start | bytes 49160 | tf_op jit(solution)/shard_map/ppermute | solution.py:468
  89.2 11.1 %collective-permute-start.25 = (bf16[128,1024]{1,0:T(8,128)(2,1)S(1)}, bf16[128,1024]{1,0:T(8,128)(2,1)S(1)}, u32[]{:S(2)}, u32[]{:S(2)}) collective-permute-start(bf16[128,1024]{1,0:T(8,128)(2,1)S(1)} %get-tuple-element.246), channel_id=1, source_target_pairs={{0,12},{4,8},{8,4},{12,0},{1,13},{5,9},{9,5},{13,1},{2,14},{6,10},... | collective-permute-start | bytes 786440 | tf_op jit(solution)/shard_map/ppermute | solution.py:468
  90.6 23.5 %collective-permute-start.26 = (bf16[128,1024]{1,0:T(8,128)(2,1)S(1)}, bf16[128,1024]{1,0:T(8,128)(2,1)S(1)}, u32[]{:S(2)}, u32[]{:S(2)}) collective-permute-start(bf16[128,1024]{1,0:T(8,128)(2,1)S(1)} %get-tuple-element.247), channel_id=1, source_target_pairs={{0,8},{4,12},{8,0},{12,4},{1,9},{5,13},{9,1},{13,5},{2,10},{6,14},... | collective-permute-start | bytes 786440 | tf_op jit(solution)/shard_map/ppermute | solution.py:468
  91.2 22.9 %collective-permute-start.27 = (bf16[128,1024]{1,0:T(8,128)(2,1)S(1)}, bf16[128,1024]{1,0:T(8,128)(2,1)S(1)}, u32[]{:S(2)}, u32[]{:S(2)}) collective-permute-start(bf16[128,1024]{1,0:T(8,128)(2,1)S(1)} %get-tuple-element.248), channel_id=1, source_target_pairs={{0,4},{4,0},{8,12},{12,8},{1,5},{5,1},{9,13},{13,9},{2,6},{6,2},{1... | collective-permute-start | bytes 786440 | tf_op jit(solution)/shard_map/ppermute | solution.py:468
  (1 other events, 1.6 us)

commit v16 on v15

--- a/solution.py
+++ b/solution.py
@@ -326,6 +326,21 @@
     )(order, down_weight, *hs)
 
 
+def down_step_kernel(h_ref, before_ref, down_ref, out_ref):
+    out_ref[...] = before_ref[...] + dot(h_ref[...], down_ref[0])
+
+
+def down_step(h, before, down):
+    return pl.pallas_call(
+        down_step_kernel,
+        out_shape=jax.ShapeDtypeStruct(before.shape, F32),
+        in_specs=whole(3),
+        out_specs=whole(1)[0],
+        compiler_params=params(),
+        cost_estimate=COST,
+    )(h, before, down)
+
+
 def down_last_kernel(parts, experts, k, direct, offset_ref, count_ref, before_ref, down_ref, *refs):
     hs, outs = refs[:parts], refs[parts : parts + experts]
     h_held, sems, *staged = refs[parts + experts :]
@@ -341,7 +356,7 @@
     total = before_ref[...]
     for i in range(parts):
         loads[i].wait()
-        total = total + dot(h_held[i], down_ref[i])
+        total = total + dot(h_held[i], down_ref[i + 1])
     result = total.astype(BF16)
     if direct:
         for i in range(experts):
@@ -411,42 +426,41 @@
     )(place, own, logits, code)
 
 
-def combine_kernel(experts, k, code_ref, weight_ref, *refs):
-    before, refs = refs[: k > 0], refs[k > 0 :]
-    blocks, (out_ref, held, sems) = refs[:experts], refs[experts:]
+def combine_kernel(places, k, more, code_ref, weight_ref, *refs):
+    before, refs = refs[:more], refs[more:]
+    count = len(places)
+    blocks, (out_ref, held, sems) = refs[:count], refs[count:]
     depth = blocks[0].shape[0]
     rows = code_ref.shape[1]
-    targets = [held.at[pl.ds(i * depth, depth)] for i in range(experts)]
-    loads = start_all(blocks, targets, sems)
+    loads = start_all(blocks, [held.at[pl.ds(i * depth, depth)] for i in range(count)], sems)
     slot_ids = lax.broadcasted_iota(I32, (depth, rows), 0) + k * depth
     parts = [
         jnp.where(slot_ids == code_ref[pl.ds(i, 1), :], weight_ref[pl.ds(i, 1), :], 0.0).astype(BF16)
-        for i in range(experts)
+        for i in places
     ]
     spread = jnp.concatenate(parts, axis=0)
     for load in loads:
         load.wait()
     total = lax.dot_general(spread, held[...], (((0,), (0,)), ((), ())), preferred_element_type=F32)
-    if k > 0:
+    if more:
         total = total + before[0][...]
     out_ref[...] = total.astype(out_ref.dtype)
 
 
-def combine(code, weights, k, blocks, so_far):
-    experts = len(blocks)
+def combine(code, weights, k, places, blocks, so_far, last):
+    count = len(places)
     depth, width = blocks[0].shape
     rows = code.shape[1]
-    last = k == BATCHES - 1
     more = [] if so_far is None else [so_far]
     return pl.pallas_call(
-        functools.partial(combine_kernel, experts, k),
+        functools.partial(combine_kernel, places, k, len(more)),
         out_shape=jax.ShapeDtypeStruct((rows, width), BF16 if last else F32),
-        in_specs=whole(2 + len(more)) + apart(experts),
+        in_specs=whole(2 + len(more)) + apart(count),
         out_specs=whole(1)[0],
-        scratch_shapes=[pltpu.VMEM((experts * depth, width), BF16), pltpu.SemaphoreType.DMA((experts,))],
-        compiler_params=params(),
-        cost_estimate=COST,
-    )(code, weights, *more, *blocks)
+        scratch_shapes=[pltpu.VMEM((count * depth, width), BF16), pltpu.SemaphoreType.DMA((count,))],
+        compiler_params=params(),
+        cost_estimate=COST,
+    )(code, weights, *more, *[blocks[i] for i in places])
 
 
 def after(value, *first):
@@ -534,7 +548,10 @@
         far = swap(hidden, bits[0])
         partial = down_first(order, near_places, far_places, down_weight, spread(hidden))
         far, partial = lax.optimization_barrier((far, partial))
-        return spread(far), partial
+        far = spread(far)
+        total = down_step(far[0], *partial)
+        far, total = lax.optimization_barrier((far[1:], total))
+        return far, (total, partial[1])
 
     def settle(k, far, partial):
         return tuple(
@@ -581,9 +598,11 @@
     waiting.append(exchange(results))
     weights = slot_weights(place, logits, gathered, code)
     total = None
-    for k in range(BATCHES):
-        total = combine(code, weights, k, waiting[k], total)
-    return total
+    for k in range(BATCHES - 1):
+        total = combine(code, weights, k, range(experts), waiting[k], total, False)
+    early = range(experts // 2)
+    total = combine(code, weights, BATCHES - 1, early, waiting[-1], total, False)
+    return combine(code, weights, BATCHES - 1, range(experts // 2, experts), waiting[-1], total, True)
 
 
 def solution(mesh):

time: 117 us -> 117 us (level)
  waiting for transfers between devices: 48.2 us -> 41.9 us
  Pallas kernels: 32.7 us -> 38.9 us
    ppermute x14, waiting for transfers between devices: 21 us -> 15 us  [swap(): return lax.ppermute(x, 'dp', [(i, i ^ bit) for i in range(width_parts)])]
    pallas_call x2 -> x5, Pallas kernels: 3.83 us -> 7.07 us  [the longest x3 4.02 us: combine(): pl.pallas_call(functools.partial(combine_kernel, places, k, len(more)), o...]
    pallas_call x2, Pallas kernels: 3.16 us -> 5.09 us  [down_first(): pl.pallas_call(functools.partial(down_first_kernel, parts, near, far), ou...]
  transfers between devices with their start and end apart: 28 -> 28, of which waited for: 17 -> 15; matrix products, arithmetic and copies ran while one was open for 3% -> 3% of each run, Pallas kernels for 21% -> 26%
where the time goes in v16:
time: 117 us
  waiting for transfers between devices  41.9 us (36%)
  Pallas kernels  38.9 us (33%)
  starting transfers between devices  26.9 us (23%)
  local copies, waits for them, and re-layouts  3.89 us (3%)
  other arithmetic  2.99 us (3%)
  between operations  1.68 us (1%)
    ppermute x14, waiting for transfers between devices, along_expert(): return lax.ppermute(x, 'expert', [(i, i ^ shift) for i in range(experts)])  26.9 us
    ppermute x14, starting transfers between devices, along_expert(): return lax.ppermute(x, 'expert', [(i, i ^ shift) for i in range(experts)])  20.5 us
    ppermute x14, waiting for transfers between devices, swap(): return lax.ppermute(x, 'dp', [(i, i ^ bit) for i in range(width_parts)])  15 us
    pallas_call x2, Pallas kernels, down_last(): pl.pallas_call(functools.partial(down_last_kernel, parts, experts, k, dir...  6.46 us
    ppermute x14, starting transfers between devices, swap(): return lax.ppermute(x, 'dp', [(i, i ^ bit) for i in range(width_parts)])  6.43 us
    pallas_call x2, Pallas kernels, down_first(): pl.pallas_call(functools.partial(down_first_kernel, parts, near, far), ou...  5.09 us
    pallas_call x2, Pallas kernels, gate_up_near(): pl.pallas_call(functools.partial(gate_up_near_kernel, parts, near, far),...  4.4 us
    pallas_call x3, Pallas kernels, combine(): pl.pallas_call(functools.partial(combine_kernel, places, k, len(more)), o...  4.02 us
  transfers between devices with their start and end apart: 28, of which 15 were waited for; matrix products, arithmetic and copies ran while one was open for 3% of the time, Pallas kernels for 26%

profile of v16, /device:TPU:0, one launch (start us, length us, event | category | flops | bytes accessed | tf_op | source)
XLA Modules:
  0.0 116.6 jit_solution(6259505054116212855)
XLA Ops:
  0.0 2.6 %shard_map.73 = (s32[4,512]{1,0:T(4,128)S(1)}, bf16[128,1024]{1,0:T(8,128)(2,1)S(1)}, bf16[128,1024]{1,0:T(8,128)(2,1)}, bf16[128,1024]{1,0:T(8,128)(2,1)}, bf16[128,1024]{1,0:T(8,128)(2,1)}) custom-call(s32[1]{0:T(128)} %bitcast.1.place_ref, s32[4,512]{1,0:T(4,128)} %picks_in.1, bf16[512,1024]{1,0:T(8,128)(2,1)} %tokens_ref.1), custom_call_target="tpu_custom_call" | custom-call | flops 1024 | bytes 1024 | tf_op jit(solution)/shard_map/pallas_call | solution.py:108
  2.6 5.1 %collective-permute-start.11 = (bf16[128,1024]{1,0:T(8,128)(2,1)}, bf16[128,1024]{1,0:T(8,128)(2,1)S(1)}, u32[]{:S(2)}, u32[]{:S(2)}) collective-permute-start(bf16[128,1024]{1,0:T(8,128)(2,1)} %get-tuple-element.183), channel_id=1, source_target_pairs={{0,12},{4,8},{8,4},{12,0},{1,13},{5,9},{9,5},{13,1},{2,14},{6,10},... | collective-permute-start | bytes 786440 | tf_op jit(solution)/shard_map/ppermute | solution.py:482
  11.4 14.3 %conditional.4 = (bf16[128,1024]{1,0:T(8,128)(2,1)}, bf16[128,1024]{1,0:T(8,128)(2,1)}, bf16[128,1024]{1,0:T(8,128)(2,1)}, bf16[128,1024]{1,0:T(8,128)(2,1)}, f3...) conditional(s32[]{:T(128)} %convert_element_type.16, () %tuple.51, (s32[4,512]{1,0:T(4,128)S(1)}, ...), branch_computations={%region_3.4_spmd, %region_4.5_spmd} | conditional | flops 10240 | bytes 1073216 | solution.py:540
  11.4 1.8 %branch_1_fun.12 = f32[4,512]{1,0:T(4,128)S(1)} custom-call(bf16[4,1024]{1,0:T(4,128)(2,1)} %get-tuple-element.60.router_ref, bf16[512,1024]{1,0:T(8,128)(2,1)} %get-tuple-element.55.tokens_ref), custom_call_target="tpu_custom_call" | custom-call | flops 1024 | bytes 1024 | tf_op jit(solution)/shard_map/cond/branch_1_fun/pallas_call | solution.py:134
  14.8 2.0 %collective-permute-done.8 = f32[4,512]{1,0:T(4,128)S(1)} collective-permute-done((f32[4,512]{1,0:T(4,128)S(1)}, f32[4,512]{1,0:T(4,128)S(1)}, u32[]{:S(2)}, u32[]{:S(2)}) %collective-permute-start.8) | collective-permute-done | bytes 8224 | tf_op jit(solution)/shard_map/cond/branch_1_fun/ppermute | solution.py:485
  20.0 2.7 %branch_1_fun.11 = (bf16[128,1024]{1,0:T(8,128)(2,1)}, bf16[128,1024]{1,0:T(8,128)(2,1)}, bf16[128,1024]{1,0:T(8,128)(2,1)}, bf16[128,1024]{1,0:T(8,128)(2,1)}) custom-call(s32[4,512]{1,0:T(4,128)S(1)} %get-tuple-element.54.code_ref, bf16[512,1024]{1,0:T(8,128)(2,1)} %get-tuple-element.55.tokens_ref), custom_call_target="tpu_custom_call" | custom-call | flops 1024 | bytes 1024 | tf_op jit(solution)/shard_map/cond/branch_1_fun/pallas_call | solution.py:155
  22.7 2.3 %collective-permute-done.10 = f32[1,4,512]{2,1,0:T(4,128)S(1)} collective-permute-done((f32[1,4,512]{2,1,0:T(4,128)}, f32[1,4,512]{2,1,0:T(4,128)S(1)}, u32[]{:S(2)}, u32[]{:S(2)}) %collective-permute-start.10) | collective-permute-done | bytes 8224 | tf_op jit(solution)/shard_map/cond/branch_1_fun/ppermute | solution.py:482
  25.7 4.5 %collective-permute-done.12 = bf16[128,1024]{1,0:T(8,128)(2,1)S(1)} collective-permute-done((bf16[128,1024]{1,0:T(8,128)(2,1)}, bf16[128,1024]{1,0:T(8,128)(2,1)S(1)}, u32[]{:S(2)}, u32[]{:S(2)}) %collective-permute-start.12) | collective-permute-done | bytes 262176 | tf_op jit(solution)/shard_map/ppermute | solution.py:482
  30.2 1.9 %conditional.5 = (bf16[256,1024]{1,0:T(8,128)(2,1)}) conditional(s32[]{:T(128)} %convert_element_type.16, () %tuple.57, (s32[2,4]{1,0:T(2,128)S(1)}, s32[2,4]{1,0:T(2,128)S(1)}, bf16[128,1024]{1,0:T(8,128)(2,1)S(1)}, bf16[128,1024]{1,0:T(8,128)(2,1)S(1)}, bf16[128,1024]{1,0:T(8,128)(2,1)S(1)}, /*index=5*/bf16[128,1024]{1,0:T(8,128)(2,1)S(1)}) %tuple.58), branch_computations={%region_6.7_spmd, %region_7.8_spmd} | conditional | flops 1024 | bytes 524298 | solution.py:565
  30.2 1.9 %branch_1_fun.13 = bf16[256,1024]{1,0:T(8,128)(2,1)} custom-call(s32[2,4]{1,0:T(2,128)S(1)} %get-tuple-element.61.offset_ref, s32[2,4]{1,0:T(2,128)S(1)} %get-tuple-element.62.count_ref, bf16[128,1024]{1,0:T(8,128)(2,1)S(1)} %get-tuple-element.63.refs_0_, bf16[128,1024]{1,0:T(8,128)(2,1)S(1)} %get-tuple-element.64.refs_1_, ...), custom_call_target="tpu_custom_call" | custom-call | flops 1024 | bytes 1024 | tf_op jit(solution)/shard_map/cond/branch_1_fun/pallas_call | solution.py:192
  33.8 2.5 %collective-permute-start.14 = (bf16[128,1024]{1,0:T(8,128)(2,1)}, bf16[128,1024]{1,0:T(8,128)(2,1)S(1)}, u32[]{:S(2)}, u32[]{:S(2)}) collective-permute-start(bf16[128,1024]{1,0:T(8,128)(2,1)} %get-tuple-element.192), channel_id=1, source_target_pairs={{0,12},{4,8},{8,4},{12,0},{1,13},{5,9},{9,5},{13,1},{2,14},{6,10},... | collective-permute-start | bytes 786440 | tf_op jit(solution)/shard_map/ppermute | solution.py:482
  36.3 1.9 %collective-permute-start.16 = (bf16[128,1024]{1,0:T(8,128)(2,1)}, bf16[128,1024]{1,0:T(8,128)(2,1)S(1)}, u32[]{:S(2)}, u32[]{:S(2)}) collective-permute-start(bf16[128,1024]{1,0:T(8,128)(2,1)} %get-tuple-element.194), channel_id=1, source_target_pairs={{0,4},{4,0},{8,12},{12,8},{1,5},{5,1},{9,13},{13,9},{2,6},{6,2},{1... | collective-permute-start | bytes 786440 | tf_op jit(solution)/shard_map/ppermute | solution.py:482
  39.9 2.6 %shard_map.74 = (f32[256,256]{1,0:T(8,128)S(1)}, f32[256,256]{1,0:T(8,128)S(1)}, bf16[2,1024,256]{2,1,0:T(8,128)(2,1)S(1)}, bf16[2,1024,256]{2,1,0:T(8,128)(2,1)S(1)}) custom-call(s32[4]{0:T(128)S(1)} %pad_add_fusion.order_ref, bf16[1,4096,256]{2,1,0:T(8,128)(2,1)S(1)} %copy-done, bf16[1,4096,256]{2,1,0:T(8,128)(2,1)S(1)} %copy-done.1, ...), custom_call_target="tpu_custom_call" | custom-call | flops 1024 | bytes 1024 | tf_op jit(solution)/shard_map/pallas_call | solution.py:240
  42.5 4.4 %collective-permute-done.17 = bf16[256,1024]{1,0:T(8,128)(2,1)} collective-permute-done((bf16[256,1024]{1,0:T(8,128)(2,1)}, bf16[256,1024]{1,0:T(8,128)(2,1)}, u32[]{:S(2)}, u32[]{:S(2)}) %collective-permute-start.17) | collective-permute-done | bytes 524320 | tf_op jit(solution)/shard_map/ppermute | solution.py:485
  46.9 10.1 %conditional.6 = (bf16[256,256]{1,0:T(8,128)(2,1)}, f32[256,1024]{1,0:T(8,128)S(1)}, bf16[2,256,1024]{2,1,0:T(8,128)(2,1)}) conditional(s32[]{:T(128)} %convert_element_type.16, () %tuple.56, (bf16[256,1024]{1,0:T(8,128)(2,1)}, f32[256,256]{1,0:T(8,128)S(1)}, f32[256,256]{1,0:T(8,128)S(1)}, bf16[2,1024,256]{2,1,0:T(8,128)(2,1)S(1)}, ...), branch_computations={%region_8.9_spmd, %region_9.10_spmd} | conditional | flops 4096 | bytes 3674296 | solution.py:565
  51.2 2.5 %branch_1_fun.16 = (f32[256,1024]{1,0:T(8,128)S(1)}, bf16[2,256,1024]{2,1,0:T(8,128)(2,1)}) custom-call(s32[4]{0:T(128)S(1)} %get-tuple-element.77.order_ref, bf16[1,1024,1024]{2,1,0:T(8,128)(2,1)S(1)} %get-tuple-element.78.down_ref, bf16[256,256]{1,0:T(8,128)(2,1)S(1)} %branch_1_fun.15.refs_0_, bf16[256,256]{1,0:T(8,128)(2,1)S(1)} %collective-permute-done.2.refs_1_), custom_call_target="tpu_custom_call" | custom-call | flops 1024 | bytes 1024 | tf_op jit(solution)/shard_map/cond/branch_1_fun/pallas_call | solution.py:311
  53.8 1.7 %collective-permute-done.1.h_ref = bf16[256,256]{1,0:T(8,128)(2,1)S(1)} collective-permute-done((bf16[256,256]{1,0:T(8,128)(2,1)S(1)}, bf16[256,256]{1,0:T(8,128)(2,1)S(1)}, u32[]{:S(2)}, u32[]{:S(2)}) %collective-permute-start.1) | collective-permute-done | bytes 131104 | tf_op jit(solution)/shard_map/cond/branch_1_fun/ppermute | solution.py:485
  58.5 2.0 %shard_map.75.refs_0_ = bf16[256,1024]{1,0:T(8,128)(2,1)S(1)} custom-call(s32[2,4]{1,0:T(2,128)S(1)} %get-tuple-element.251.offset_ref, s32[2,4]{1,0:T(2,128)S(1)} %get-tuple-element.252.count_ref, bf16[128,1024]{1,0:T(8,128)(2,1)} %get-tuple-element.206.refs_0_, bf16[128,1024]{1,0:T(8,128)(2,1)S(1)} %collective-permute-done.14.refs_1_, ...), custom_call_target="tpu_custom_call" | custom-call | flops 1024 | bytes 1024 | tf_op jit(solution)/shard_map/pallas_call | solution.py:192
  61.2 3.6 %shard_map.76 = (bf16[128,1024]{1,0:T(8,128)(2,1)S(1)}, bf16[128,1024]{1,0:T(8,128)(2,1)}, bf16[128,1024]{1,0:T(8,128)(2,1)}, bf16[128,1024]{1,0:T(8,128)(2,1)}) custom-call(s32[2,4]{1,0:T(2,128)S(1)} %get-tuple-element.251.offset_ref, s32[2,4]{1,0:T(2,128)S(1)} %get-tuple-element.252.count_ref, f32[256,1024]{1,0:T(8,128)S(1)} %get-tuple-element.211.before_ref, ...), custom_call_target="tpu_custom_call" | custom-call | flops 1024 | bytes 1024 | tf_op jit(solution)/shard_map/pallas_call | solution.py:380
  64.8 2.5 %collective-permute-start.21 = (bf16[128,1024]{1,0:T(8,128)(2,1)}, bf16[128,1024]{1,0:T(8,128)(2,1)}, u32[]{:S(2)}, u32[]{:S(2)}) collective-permute-start(bf16[128,1024]{1,0:T(8,128)(2,1)} %get-tuple-element.215), channel_id=1, source_target_pairs={{0,12},{4,8},{8,4},{12,0},{1,13},{5,9},{9,5},{13,1},{2,14},{6,10},... | collective-permute-start | bytes 786440 | tf_op jit(solution)/shard_map/ppermute | solution.py:482
  67.3 1.9 %collective-permute-start.23 = (bf16[128,1024]{1,0:T(8,128)(2,1)}, bf16[128,1024]{1,0:T(8,128)(2,1)}, u32[]{:S(2)}, u32[]{:S(2)}) collective-permute-start(bf16[128,1024]{1,0:T(8,128)(2,1)} %get-tuple-element.217), channel_id=1, source_target_pairs={{0,4},{4,0},{8,12},{12,8},{1,5},{5,1},{9,13},{13,9},{2,6},{6,2},{1... | collective-permute-start | bytes 786440 | tf_op jit(solution)/shard_map/ppermute | solution.py:482
  71.5 1.8 %shard_map.77 = (f32[256,256]{1,0:T(8,128)S(1)}, f32[256,256]{1,0:T(8,128)S(1)}, bf16[2,1024,256]{2,1,0:T(8,128)(2,1)S(1)}, bf16[2,1024,256]{2,1,0:T(8,128)(2,1)S(1)}) custom-call(s32[4]{0:T(128)S(1)} %pad_add_fusion.order_ref, bf16[1,4096,256]{2,1,0:T(8,128)(2,1)S(1)} %copy-done, bf16[1,4096,256]{2,1,0:T(8,128)(2,1)S(1)} %copy-done.2, ...), custom_call_target="tpu_custom_call" | custom-call | flops 1024 | bytes 1024 | tf_op jit(solution)/shard_map/pallas_call | solution.py:240
  73.3 1.7 %collective-permute-done.19 = bf16[256,1024]{1,0:T(8,128)(2,1)} collective-permute-done((bf16[256,1024]{1,0:T(8,128)(2,1)S(1)}, bf16[256,1024]{1,0:T(8,128)(2,1)}, u32[]{:S(2)}, u32[]{:S(2)}) %collective-permute-start.19) | collective-permute-done | bytes 524320 | tf_op jit(solution)/shard_map/ppermute | solution.py:485
  75.0 10.3 %conditional.7 = (bf16[256,256]{1,0:T(8,128)(2,1)}, f32[256,1024]{1,0:T(8,128)S(1)}, bf16[2,256,1024]{2,1,0:T(8,128)(2,1)}) conditional(s32[]{:T(128)} %convert_element_type.17, () %tuple.53, (bf16[256,1024]{1,0:T(8,128)(2,1)}, f32[256,256]{1,0:T(8,128)S(1)}, f32[256,256]{1,0:T(8,128)S(1)}, bf16[2,1024,256]{2,1,0:T(8,128)(2,1)S(1)}, ...), branch_computations={%region_10.11_spmd, %region_11.12_spmd} | conditional | flops 4096 | bytes 3674296 | solution.py:565
  79.0 2.5 %branch_1_fun.20 = (f32[256,1024]{1,0:T(8,128)S(1)}, bf16[2,256,1024]{2,1,0:T(8,128)(2,1)}) custom-call(s32[4]{0:T(128)S(1)} %get-tuple-element.96.order_ref, bf16[1,1024,1024]{2,1,0:T(8,128)(2,1)S(1)} %get-tuple-element.97.down_ref, bf16[256,256]{1,0:T(8,128)(2,1)S(1)} %branch_1_fun.19.refs_0_, bf16[256,256]{1,0:T(8,128)(2,1)S(1)} %collective-permute-done.6.refs_1_), custom_call_target="tpu_custom_call" | custom-call | flops 1024 | bytes 1024 | tf_op jit(solution)/shard_map/cond/branch_1_fun/pallas_call | solution.py:311
  81.6 2.0 %collective-permute-done.5.h_ref = bf16[256,256]{1,0:T(8,128)(2,1)S(1)} collective-permute-done((bf16[256,256]{1,0:T(8,128)(2,1)S(1)}, bf16[256,256]{1,0:T(8,128)(2,1)S(1)}, u32[]{:S(2)}, u32[]{:S(2)}) %collective-permute-start.5) | collective-permute-done | bytes 131104 | tf_op jit(solution)/shard_map/cond/branch_1_fun/ppermute | solution.py:485
  85.4 2.9 %shard_map.78 = (bf16[128,1024]{1,0:T(8,128)(2,1)S(1)}, bf16[128,1024]{1,0:T(8,128)(2,1)S(1)}, bf16[128,1024]{1,0:T(8,128)(2,1)S(1)}, bf16[128,1024]{1,0:T(8,128)(2,1)S(1)}) custom-call(s32[2,4]{1,0:T(2,128)S(1)} %get-tuple-element.251.offset_ref, s32[2,4]{1,0:T(2,128)S(1)} %get-tuple-element.252.count_ref, f32[256,1024]{1,0:T(8,128)S(1)} %get-tuple-element.229.before_ref, ...), custom_call_target="tpu_custom_call" | custom-call | flops 1024 | bytes 1024 | tf_op jit(solution)/shard_map/pallas_call | solution.py:380
  89.5 1.9 %collective-permute-start.25 = (bf16[128,1024]{1,0:T(8,128)(2,1)S(1)}, bf16[128,1024]{1,0:T(8,128)(2,1)S(1)}, u32[]{:S(2)}, u32[]{:S(2)}) collective-permute-start(bf16[128,1024]{1,0:T(8,128)(2,1)S(1)} %get-tuple-element.244), channel_id=1, source_target_pairs={{0,12},{4,8},{8,4},{12,0},{1,13},{5,9},{9,5},{13,1},{2,14},{6,10},... | collective-permute-start | bytes 786440 | tf_op jit(solution)/shard_map/ppermute | solution.py:482
  91.7 2.3 %collective-permute-start.27 = (bf16[128,1024]{1,0:T(8,128)(2,1)S(1)}, bf16[128,1024]{1,0:T(8,128)(2,1)S(1)}, u32[]{:S(2)}, u32[]{:S(2)}) collective-permute-start(bf16[128,1024]{1,0:T(8,128)(2,1)S(1)} %get-tuple-element.246), channel_id=1, source_target_pairs={{0,4},{4,0},{8,12},{12,8},{1,5},{5,1},{9,13},{13,9},{2,6},{6,2},{1... | collective-permute-start | bytes 786440 | tf_op jit(solution)/shard_map/ppermute | solution.py:482
  95.1 1.9 %shard_map.80.refs_0_ = f32[512,1024]{1,0:T(8,128)S(1)} custom-call(s32[4,512]{1,0:T(4,128)S(1)} %get-tuple-element.176.code_ref, f32[4,512]{1,0:T(4,128)S(1)} %shard_map.79.weight_ref, bf16[128,1024]{1,0:T(8,128)(2,1)S(1)} %get-tuple-element.239.refs_0_, bf16[128,1024]{1,0:T(8,128)(2,1)} %collective-permute-done.21.refs_1_, ...), custom_call_target="tpu_custom_call" | custom-call | flops 1024 | bytes 1024 | tf_op jit(solution)/shard_map/pallas_call | solution.py:455
  97.0 3.7 %collective-permute-done.25.refs_2_ = bf16[128,1024]{1,0:T(8,128)(2,1)S(1)} collective-permute-done((bf16[128,1024]{1,0:T(8,128)(2,1)S(1)}, bf16[128,1024]{1,0:T(8,128)(2,1)S(1)}, u32[]{:S(2)}, u32[]{:S(2)}) %collective-permute-start.25) | collective-permute-done | bytes 262176 | tf_op jit(solution)/shard_map/ppermute | solution.py:482
  101.3 13.7 %collective-permute-done.26.refs_1_ = bf16[128,1024]{1,0:T(8,128)(2,1)S(1)} collective-permute-done((bf16[128,1024]{1,0:T(8,128)(2,1)S(1)}, bf16[128,1024]{1,0:T(8,128)(2,1)S(1)}, u32[]{:S(2)}, u32[]{:S(2)}) %collective-permute-start.26) | collective-permute-done | bytes 262176 | tf_op jit(solution)/shard_map/ppermute | solution.py:482
  (70 shorter events, 31.6 us)
Async XLA Ops:
  2.6 23.1 %collective-permute-start.11 = (bf16[128,1024]{1,0:T(8,128)(2,1)}, bf16[128,1024]{1,0:T(8,128)(2,1)S(1)}, u32[]{:S(2)}, u32[]{:S(2)}) collective-permute-start(bf16[128,1024]{1,0:T(8,128)(2,1)} %get-tuple-element.183), channel_id=1, source_target_pairs={{0,12},{4,8},{8,4},{12,0},{1,13},{5,9},{9,5},{13,1},{2,14},{6,10},... | collective-permute-start | bytes 786440 | tf_op jit(solution)/shard_map/ppermute | solution.py:482
  7.7 22.5 %collective-permute-start.12 = (bf16[128,1024]{1,0:T(8,128)(2,1)}, bf16[128,1024]{1,0:T(8,128)(2,1)S(1)}, u32[]{:S(2)}, u32[]{:S(2)}) collective-permute-start(bf16[128,1024]{1,0:T(8,128)(2,1)} %get-tuple-element.184), channel_id=1, source_target_pairs={{0,8},{4,12},{8,0},{12,4},{1,9},{5,13},{9,1},{13,5},{2,10},{6,14},... | collective-permute-start | bytes 786440 | tf_op jit(solution)/shard_map/ppermute | solution.py:482
  7.7 22.5 %collective-permute-start.13 = (bf16[128,1024]{1,0:T(8,128)(2,1)}, bf16[128,1024]{1,0:T(8,128)(2,1)S(1)}, u32[]{:S(2)}, u32[]{:S(2)}) collective-permute-start(bf16[128,1024]{1,0:T(8,128)(2,1)} %get-tuple-element.185), channel_id=1, source_target_pairs={{0,4},{4,0},{8,12},{12,8},{1,5},{5,1},{9,13},{13,9},{2,6},{6,2},{1... | collective-permute-start | bytes 786440 | tf_op jit(solution)/shard_map/ppermute | solution.py:482
  11.4 26.9 %copy-start = (bf16[1,4096,256]{2,1,0:T(8,128)(2,1)S(1)}, bf16[1,4096,256]{2,1,0:T(8,128)(2,1)}, u32[]{:S(2)}) copy-start(bf16[1,4096,256]{2,1,0:T(8,128)(2,1)} %gate_ref.3) | copy-start | bytes 6291460
  13.2 3.7 %collective-permute-start.8 = (f32[4,512]{1,0:T(4,128)S(1)}, f32[4,512]{1,0:T(4,128)S(1)}, u32[]{:S(2)}, u32[]{:S(2)}) collective-permute-start(f32[4,512]{1,0:T(4,128)S(1)} %branch_1_fun.12), channel_id=1, source_target_pairs={{0,2},{1,3},{2,0},{3,1},{4,6},{5,7},{6,4},{7,5},{8,10},{9,11},{10,... | collective-permute-start | bytes 24584 | tf_op jit(solution)/shard_map/cond/branch_1_fun/ppermute | solution.py:485
  16.8 1.2 %collective-permute-start.9 = (f32[4,512]{1,0:T(4,128)S(1)}, f32[4,512]{1,0:T(4,128)S(1)}, u32[]{:S(2)}, u32[]{:S(2)}) collective-permute-start(f32[4,512]{1,0:T(4,128)S(1)} %add.24), channel_id=1, source_target_pairs={{0,1},{1,0},{2,3},{3,2},{4,5},{5,4},{6,7},{7,6},{8,9},{9,8},{10,11... | collective-permute-start | bytes 24584 | tf_op jit(solution)/shard_map/cond/branch_1_fun/ppermute | solution.py:485
  18.6 6.4 %collective-permute-start.10 = (f32[1,4,512]{2,1,0:T(4,128)}, f32[1,4,512]{2,1,0:T(4,128)S(1)}, u32[]{:S(2)}, u32[]{:S(2)}) collective-permute-start(f32[1,4,512]{2,1,0:T(4,128)} %bitcast), channel_id=1, source_target_pairs={{0,4},{4,0},{8,12},{12,8},{1,5},{5,1},{9,13},{13,9},{2,6},{6,2},{1... | collective-permute-start | bytes 24584 | tf_op jit(solution)/shard_map/cond/branch_1_fun/ppermute | solution.py:482
  32.2 6.1 %collective-permute-start.18 = (bf16[256,1024]{1,0:T(8,128)(2,1)}, bf16[256,1024]{1,0:T(8,128)(2,1)S(1)}, u32[]{:S(2)}, u32[]{:S(2)}) collective-permute-start(bf16[256,1024]{1,0:T(8,128)(2,1)} %get-tuple-element.281.refs_0_), channel_id=1, source_target_pairs={{0,1},{1,0},{2,3},{3,2},{4,5},{5,4},{6,7},{7,6},{8,9},{9,8},{10,11... | collective-permute-start | bytes 1572872 | tf_op jit(solution)/shard_map/ppermute | solution.py:485
  32.3 14.7 %collective-permute-start.17 = (bf16[256,1024]{1,0:T(8,128)(2,1)}, bf16[256,1024]{1,0:T(8,128)(2,1)}, u32[]{:S(2)}, u32[]{:S(2)}) collective-permute-start(bf16[256,1024]{1,0:T(8,128)(2,1)} %get-tuple-element.281.refs_0_), channel_id=1, source_target_pairs={{0,2},{1,3},{2,0},{3,1},{4,6},{5,7},{6,4},{7,5},{8,10},{9,11},{10,... | collective-permute-start | bytes 1572872 | tf_op jit(solution)/shard_map/ppermute | solution.py:485
  33.8 23.2 %collective-permute-start.14 = (bf16[128,1024]{1,0:T(8,128)(2,1)}, bf16[128,1024]{1,0:T(8,128)(2,1)S(1)}, u32[]{:S(2)}, u32[]{:S(2)}) collective-permute-start(bf16[128,1024]{1,0:T(8,128)(2,1)} %get-tuple-element.192), channel_id=1, source_target_pairs={{0,12},{4,8},{8,4},{12,0},{1,13},{5,9},{9,5},{13,1},{2,14},{6,10},... | collective-permute-start | bytes 786440 | tf_op jit(solution)/shard_map/ppermute | solution.py:482
  36.3 22.2 %collective-permute-start.15 = (bf16[128,1024]{1,0:T(8,128)(2,1)}, bf16[128,1024]{1,0:T(8,128)(2,1)S(1)}, u32[]{:S(2)}, u32[]{:S(2)}) collective-permute-start(bf16[128,1024]{1,0:T(8,128)(2,1)} %get-tuple-element.193), channel_id=1, source_target_pairs={{0,8},{4,12},{8,0},{12,4},{1,9},{5,13},{9,1},{13,5},{2,10},{6,14},... | collective-permute-start | bytes 786440 | tf_op jit(solution)/shard_map/ppermute | solution.py:482
  36.3 22.2 %collective-permute-start.16 = (bf16[128,1024]{1,0:T(8,128)(2,1)}, bf16[128,1024]{1,0:T(8,128)(2,1)S(1)}, u32[]{:S(2)}, u32[]{:S(2)}) collective-permute-start(bf16[128,1024]{1,0:T(8,128)(2,1)} %get-tuple-element.194), channel_id=1, source_target_pairs={{0,4},{4,0},{8,12},{12,8},{1,5},{5,1},{9,13},{13,9},{2,6},{6,2},{1... | collective-permute-start | bytes 786440 | tf_op jit(solution)/shard_map/ppermute | solution.py:482
  39.9 7.0 %copy-start.3 = (bf16[1,1024,1024]{2,1,0:T(8,128)(2,1)S(1)}, bf16[1,1024,1024]{2,1,0:T(8,128)(2,1)}, u32[]{:S(2)}) copy-start(bf16[1,1024,1024]{2,1,0:T(8,128)(2,1)} %param.19) | copy-start | bytes 6291460
  46.9 2.1 %collective-permute-start = (bf16[256,1024]{1,0:T(8,128)(2,1)}, bf16[256,1024]{1,0:T(8,128)(2,1)S(1)}, u32[]{:S(2)}, u32[]{:S(2)}) collective-permute-start(bf16[256,1024]{1,0:T(8,128)(2,1)} %get-tuple-element.67.refs_0_), channel_id=1, source_target_pairs={{0,1},{1,0},{2,3},{3,2},{4,5},{5,4},{6,7},{7,6},{8,9},{9,8},{10,11... | collective-permute-start | bytes 1572872 | tf_op jit(solution)/shard_map/cond/branch_1_fun/ppermute | solution.py:485
  49.5 1.7 %collective-permute-start.2 = (bf16[256,256]{1,0:T(8,128)(2,1)S(1)}, bf16[256,256]{1,0:T(8,128)(2,1)S(1)}, u32[]{:S(2)}, u32[]{:S(2)}) collective-permute-start(bf16[256,256]{1,0:T(8,128)(2,1)S(1)} %branch_1_fun.15.refs_0_), channel_id=1, source_target_pairs={{0,1},{1,0},{2,3},{3,2},{4,5},{5,4},{6,7},{7,6},{8,9},{9,8},{10,11... | collective-permute-start | bytes 393224 | tf_op jit(solution)/shard_map/cond/branch_1_fun/ppermute | solution.py:485
  49.7 5.8 %collective-permute-start.1 = (bf16[256,256]{1,0:T(8,128)(2,1)S(1)}, bf16[256,256]{1,0:T(8,128)(2,1)S(1)}, u32[]{:S(2)}, u32[]{:S(2)}) collective-permute-start(bf16[256,256]{1,0:T(8,128)(2,1)S(1)} %branch_1_fun.15.refs_0_), channel_id=1, source_target_pairs={{0,2},{1,3},{2,0},{3,1},{4,6},{5,7},{6,4},{7,5},{8,10},{9,11},{10,... | collective-permute-start | bytes 393224 | tf_op jit(solution)/shard_map/cond/branch_1_fun/ppermute | solution.py:485
  55.5 1.5 %collective-permute-start.3 = (bf16[256,256]{1,0:T(8,128)(2,1)S(1)}, bf16[256,256]{1,0:T(8,128)(2,1)}, u32[]{:S(2)}, u32[]{:S(2)}) collective-permute-start(bf16[256,256]{1,0:T(8,128)(2,1)S(1)} %collective-permute-done.1.h_ref), channel_id=1, source_target_pairs={{0,1},{1,0},{2,3},{3,2},{4,5},{5,4},{6,7},{7,6},{8,9},{9,8},{10,11... | collective-permute-start | bytes 393224 | tf_op jit(solution)/shard_map/cond/branch_1_fun/ppermute | solution.py:485
  60.5 9.4 %collective-permute-start.20 = (bf16[256,1024]{1,0:T(8,128)(2,1)S(1)}, bf16[256,1024]{1,0:T(8,128)(2,1)S(1)}, u32[]{:S(2)}, u32[]{:S(2)}) collective-permute-start(bf16[256,1024]{1,0:T(8,128)(2,1)S(1)} %shard_map.75.refs_0_), channel_id=1, source_target_pairs={{0,1},{1,0},{2,3},{3,2},{4,5},{5,4},{6,7},{7,6},{8,9},{9,8},{10,11... | collective-permute-start | bytes 1572872 | tf_op jit(solution)/shard_map/ppermute | solution.py:485
  60.6 14.4 %collective-permute-start.19 = (bf16[256,1024]{1,0:T(8,128)(2,1)S(1)}, bf16[256,1024]{1,0:T(8,128)(2,1)}, u32[]{:S(2)}, u32[]{:S(2)}) collective-permute-start(bf16[256,1024]{1,0:T(8,128)(2,1)S(1)} %shard_map.75.refs_0_), channel_id=1, source_target_pairs={{0,2},{1,3},{2,0},{3,1},{4,6},{5,7},{6,4},{7,5},{8,10},{9,11},{10,... | collective-permute-start | bytes 1572872 | tf_op jit(solution)/shard_map/ppermute | solution.py:485
  64.8 23.5 %collective-permute-start.21 = (bf16[128,1024]{1,0:T(8,128)(2,1)}, bf16[128,1024]{1,0:T(8,128)(2,1)}, u32[]{:S(2)}, u32[]{:S(2)}) collective-permute-start(bf16[128,1024]{1,0:T(8,128)(2,1)} %get-tuple-element.215), channel_id=1, source_target_pairs={{0,12},{4,8},{8,4},{12,0},{1,13},{5,9},{9,5},{13,1},{2,14},{6,10},... | collective-permute-start | bytes 786440 | tf_op jit(solution)/shard_map/ppermute | solution.py:482
  67.3 22.3 %collective-permute-start.22 = (bf16[128,1024]{1,0:T(8,128)(2,1)}, bf16[128,1024]{1,0:T(8,128)(2,1)}, u32[]{:S(2)}, u32[]{:S(2)}) collective-permute-start(bf16[128,1024]{1,0:T(8,128)(2,1)} %get-tuple-element.216), channel_id=1, source_target_pairs={{0,8},{4,12},{8,0},{12,4},{1,9},{5,13},{9,1},{13,5},{2,10},{6,14},... | collective-permute-start | bytes 786440 | tf_op jit(solution)/shard_map/ppermute | solution.py:482
  67.3 22.3 %collective-permute-start.23 = (bf16[128,1024]{1,0:T(8,128)(2,1)}, bf16[128,1024]{1,0:T(8,128)(2,1)}, u32[]{:S(2)}, u32[]{:S(2)}) collective-permute-start(bf16[128,1024]{1,0:T(8,128)(2,1)} %get-tuple-element.217), channel_id=1, source_target_pairs={{0,4},{4,0},{8,12},{12,8},{1,5},{5,1},{9,13},{13,9},{2,6},{6,2},{1... | collective-permute-start | bytes 786440 | tf_op jit(solution)/shard_map/ppermute | solution.py:482
  69.9 1.6 %copy-start.2 = (bf16[1,4096,256]{2,1,0:T(8,128)(2,1)S(1)}, bf16[1,4096,256]{2,1,0:T(8,128)(2,1)}, u32[]{:S(2)}) copy-start(bf16[1,4096,256]{2,1,0:T(8,128)(2,1)} %up_ref.3) | copy-start | bytes 6291460
  71.5 3.6 %copy-start.4 = (bf16[1,1024,1024]{2,1,0:T(8,128)(2,1)S(1)}, bf16[1,1024,1024]{2,1,0:T(8,128)(2,1)}, u32[]{:S(2)}) copy-start(bf16[1,1024,1024]{2,1,0:T(8,128)(2,1)} %param.19) | copy-start | bytes 6291460
  75.0 2.1 %collective-permute-start.4 = (bf16[256,1024]{1,0:T(8,128)(2,1)}, bf16[256,1024]{1,0:T(8,128)(2,1)S(1)}, u32[]{:S(2)}, u32[]{:S(2)}) collective-permute-start(bf16[256,1024]{1,0:T(8,128)(2,1)} %get-tuple-element.86.refs_0_), channel_id=1, source_target_pairs={{0,1},{1,0},{2,3},{3,2},{4,5},{5,4},{6,7},{7,6},{8,9},{9,8},{10,11... | collective-permute-start | bytes 1572872 | tf_op jit(solution)/shard_map/cond/branch_1_fun/ppermute | solution.py:485
  77.6 1.4 %collective-permute-start.6 = (bf16[256,256]{1,0:T(8,128)(2,1)S(1)}, bf16[256,256]{1,0:T(8,128)(2,1)S(1)}, u32[]{:S(2)}, u32[]{:S(2)}) collective-permute-start(bf16[256,256]{1,0:T(8,128)(2,1)S(1)} %branch_1_fun.19.refs_0_), channel_id=1, source_target_pairs={{0,1},{1,0},{2,3},{3,2},{4,5},{5,4},{6,7},{7,6},{8,9},{9,8},{10,11... | collective-permute-start | bytes 393224 | tf_op jit(solution)/shard_map/cond/branch_1_fun/ppermute | solution.py:485
  77.8 5.8 %collective-permute-start.5 = (bf16[256,256]{1,0:T(8,128)(2,1)S(1)}, bf16[256,256]{1,0:T(8,128)(2,1)S(1)}, u32[]{:S(2)}, u32[]{:S(2)}) collective-permute-start(bf16[256,256]{1,0:T(8,128)(2,1)S(1)} %branch_1_fun.19.refs_0_), channel_id=1, source_target_pairs={{0,2},{1,3},{2,0},{3,1},{4,6},{5,7},{6,4},{7,5},{8,10},{9,11},{10,... | collective-permute-start | bytes 393224 | tf_op jit(solution)/shard_map/cond/branch_1_fun/ppermute | solution.py:485
  83.6 1.5 %collective-permute-start.7 = (bf16[256,256]{1,0:T(8,128)(2,1)S(1)}, bf16[256,256]{1,0:T(8,128)(2,1)}, u32[]{:S(2)}, u32[]{:S(2)}) collective-permute-start(bf16[256,256]{1,0:T(8,128)(2,1)S(1)} %collective-permute-done.5.h_ref), channel_id=1, source_target_pairs={{0,1},{1,0},{2,3},{3,2},{4,5},{5,4},{6,7},{7,6},{8,9},{9,8},{10,11... | collective-permute-start | bytes 393224 | tf_op jit(solution)/shard_map/cond/branch_1_fun/ppermute | solution.py:485
  85.3 6.4 %collective-permute-start.24 = (f32[2,4,512]{2,1,0:T(4,128)S(1)}, f32[2,4,512]{2,1,0:T(4,128)S(1)}, u32[]{:S(2)}, u32[]{:S(2)}) collective-permute-start(f32[2,4,512]{2,1,0:T(4,128)S(1)} %get-tuple-element.237), channel_id=1, source_target_pairs={{0,8},{4,12},{8,0},{12,4},{1,9},{5,13},{9,1},{13,5},{2,10},{6,14},... | collective-permute-start | bytes 49160 | tf_op jit(solution)/shard_map/ppermute | solution.py:482
  89.5 11.1 %collective-permute-start.25 = (bf16[128,1024]{1,0:T(8,128)(2,1)S(1)}, bf16[128,1024]{1,0:T(8,128)(2,1)S(1)}, u32[]{:S(2)}, u32[]{:S(2)}) collective-permute-start(bf16[128,1024]{1,0:T(8,128)(2,1)S(1)} %get-tuple-element.244), channel_id=1, source_target_pairs={{0,12},{4,8},{8,4},{12,0},{1,13},{5,9},{9,5},{13,1},{2,14},{6,10},... | collective-permute-start | bytes 786440 | tf_op jit(solution)/shard_map/ppermute | solution.py:482
  91.4 23.5 %collective-permute-start.26 = (bf16[128,1024]{1,0:T(8,128)(2,1)S(1)}, bf16[128,1024]{1,0:T(8,128)(2,1)S(1)}, u32[]{:S(2)}, u32[]{:S(2)}) collective-permute-start(bf16[128,1024]{1,0:T(8,128)(2,1)S(1)} %get-tuple-element.245), channel_id=1, source_target_pairs={{0,8},{4,12},{8,0},{12,4},{1,9},{5,13},{9,1},{13,5},{2,10},{6,14},... | collective-permute-start | bytes 786440 | tf_op jit(solution)/shard_map/ppermute | solution.py:482
  91.7 23.2 %collective-permute-start.27 = (bf16[128,1024]{1,0:T(8,128)(2,1)S(1)}, bf16[128,1024]{1,0:T(8,128)(2,1)S(1)}, u32[]{:S(2)}, u32[]{:S(2)}) collective-permute-start(bf16[128,1024]{1,0:T(8,128)(2,1)S(1)} %get-tuple-element.246), channel_id=1, source_target_pairs={{0,4},{4,0},{8,12},{12,8},{1,5},{5,1},{9,13},{13,9},{2,6},{6,2},{1... | collective-permute-start | bytes 786440 | tf_op jit(solution)/shard_map/ppermute | solution.py:482
  (1 other events, 1.6 us)

commit v17 on v16

--- a/solution.py
+++ b/solution.py
@@ -326,21 +326,6 @@
     )(order, down_weight, *hs)
 
 
-def down_step_kernel(h_ref, before_ref, down_ref, out_ref):
-    out_ref[...] = before_ref[...] + dot(h_ref[...], down_ref[0])
-
-
-def down_step(h, before, down):
-    return pl.pallas_call(
-        down_step_kernel,
-        out_shape=jax.ShapeDtypeStruct(before.shape, F32),
-        in_specs=whole(3),
-        out_specs=whole(1)[0],
-        compiler_params=params(),
-        cost_estimate=COST,
-    )(h, before, down)
-
-
 def down_last_kernel(parts, experts, k, direct, offset_ref, count_ref, before_ref, down_ref, *refs):
     hs, outs = refs[:parts], refs[parts : parts + experts]
     h_held, sems, *staged = refs[parts + experts :]
@@ -356,7 +341,7 @@
     total = before_ref[...]
     for i in range(parts):
         loads[i].wait()
-        total = total + dot(h_held[i], down_ref[i + 1])
+        total = total + dot(h_held[i], down_ref[i])
     result = total.astype(BF16)
     if direct:
         for i in range(experts):
@@ -548,10 +533,7 @@
         far = swap(hidden, bits[0])
         partial = down_first(order, near_places, far_places, down_weight, spread(hidden))
         far, partial = lax.optimization_barrier((far, partial))
-        far = spread(far)
-        total = down_step(far[0], *partial)
-        far, total = lax.optimization_barrier((far[1:], total))
-        return far, (total, partial[1])
+        return spread(far), partial
 
     def settle(k, far, partial):
         return tuple(

time: 117 us -> 116 us (level)
  Pallas kernels: 38.9 us -> 32.9 us
  waiting for transfers between devices: 41.9 us -> 47.6 us
    ppermute x14, waiting for transfers between devices: 15 us -> 21 us  [swap(): return lax.ppermute(x, 'dp', [(i, i ^ bit) for i in range(width_parts)])]
    pallas_call x2 -> x0, Pallas kernels: 3.05 us -> none  [down_step(): pl.pallas_call(down_step_kernel, out_shape=jax.ShapeDtypeStruct(before.sh...]
    pallas_call x2, Pallas kernels: 5.09 us -> 3.16 us  [down_first(): pl.pallas_call(functools.partial(down_first_kernel, parts, near, far), ou...]
  transfers between devices with their start and end apart: 28 -> 28, of which waited for: 15 -> 17; matrix products, arithmetic and copies ran while one was open for 3% -> 3% of each run, Pallas kernels for 26% -> 21%
where the time goes in v17:
time: 116 us
  waiting for transfers between devices  47.6 us (41%)
  Pallas kernels  32.9 us (28%)
  starting transfers between devices  26.9 us (23%)
  local copies, waits for them, and re-layouts  3.89 us (3%)
  other arithmetic  2.93 us (3%)
  between operations  1.54 us (1%)
    ppermute x14, waiting for transfers between devices, along_expert(): return lax.ppermute(x, 'expert', [(i, i ^ shift) for i in range(experts)])  26.6 us
    ppermute x14, waiting for transfers between devices, swap(): return lax.ppermute(x, 'dp', [(i, i ^ bit) for i in range(width_parts)])  21 us
    ppermute x14, starting transfers between devices, along_expert(): return lax.ppermute(x, 'expert', [(i, i ^ shift) for i in range(experts)])  20.4 us
    ppermute x14, starting transfers between devices, swap(): return lax.ppermute(x, 'dp', [(i, i ^ bit) for i in range(width_parts)])  6.43 us
    pallas_call x2, Pallas kernels, down_last(): pl.pallas_call(functools.partial(down_last_kernel, parts, experts, k, dir...  5.47 us
    pallas_call x2, Pallas kernels, gate_up_near(): pl.pallas_call(functools.partial(gate_up_near_kernel, parts, near, far),...  4.4 us
    pallas_call x3, Pallas kernels, combine(): pl.pallas_call(functools.partial(combine_kernel, places, k, len(more)), o...  4.02 us
    pallas_call x2, Pallas kernels, compact(): pl.pallas_call(functools.partial(compact_kernel, experts, k), out_shape=j...  3.94 us
  transfers between devices with their start and end apart: 28, of which 17 were waited for; matrix products, arithmetic and copies ran while one was open for 3% of the time, Pallas kernels for 21%

profile of v17, /device:TPU:0, one launch (start us, length us, event | category | flops | bytes accessed | tf_op | source)
XLA Modules:
  0.0 115.8 jit_solution(3414435541213404351)
XLA Ops:
  0.0 2.6 %shard_map.73 = (s32[4,512]{1,0:T(4,128)S(1)}, bf16[128,1024]{1,0:T(8,128)(2,1)S(1)}, bf16[128,1024]{1,0:T(8,128)(2,1)}, bf16[128,1024]{1,0:T(8,128)(2,1)}, bf16[128,1024]{1,0:T(8,128)(2,1)}) custom-call(s32[1]{0:T(128)} %bitcast.1.place_ref, s32[4,512]{1,0:T(4,128)} %picks_in.1, bf16[512,1024]{1,0:T(8,128)(2,1)} %tokens_ref.1), custom_call_target="tpu_custom_call" | custom-call | flops 1024 | bytes 1024 | tf_op jit(solution)/shard_map/pallas_call | solution.py:108
  2.6 5.1 %collective-permute-start.11 = (bf16[128,1024]{1,0:T(8,128)(2,1)}, bf16[128,1024]{1,0:T(8,128)(2,1)S(1)}, u32[]{:S(2)}, u32[]{:S(2)}) collective-permute-start(bf16[128,1024]{1,0:T(8,128)(2,1)} %get-tuple-element.182), channel_id=1, source_target_pairs={{0,12},{4,8},{8,4},{12,0},{1,13},{5,9},{9,5},{13,1},{2,14},{6,10},... | collective-permute-start | bytes 786440 | tf_op jit(solution)/shard_map/ppermute | solution.py:467
  11.2 14.5 %conditional.4 = (bf16[128,1024]{1,0:T(8,128)(2,1)}, bf16[128,1024]{1,0:T(8,128)(2,1)}, bf16[128,1024]{1,0:T(8,128)(2,1)}, bf16[128,1024]{1,0:T(8,128)(2,1)}, f3...) conditional(s32[]{:T(128)} %convert_element_type.16, () %tuple.49, (s32[4,512]{1,0:T(4,128)S(1)}, ...), branch_computations={%region_3.4_spmd, %region_4.5_spmd} | conditional | flops 10240 | bytes 1073216 | solution.py:525
  11.2 1.8 %branch_1_fun.10 = f32[4,512]{1,0:T(4,128)S(1)} custom-call(bf16[4,1024]{1,0:T(4,128)(2,1)} %get-tuple-element.60.router_ref, bf16[512,1024]{1,0:T(8,128)(2,1)} %get-tuple-element.55.tokens_ref), custom_call_target="tpu_custom_call" | custom-call | flops 1024 | bytes 1024 | tf_op jit(solution)/shard_map/cond/branch_1_fun/pallas_call | solution.py:134
  13.0 1.7 %collective-permute-start.8 = (f32[4,512]{1,0:T(4,128)S(1)}, f32[4,512]{1,0:T(4,128)S(1)}, u32[]{:S(2)}, u32[]{:S(2)}) collective-permute-start(f32[4,512]{1,0:T(4,128)S(1)} %branch_1_fun.10), channel_id=1, source_target_pairs={{0,2},{1,3},{2,0},{3,1},{4,6},{5,7},{6,4},{7,5},{8,10},{9,11},{10,... | collective-permute-start | bytes 24584 | tf_op jit(solution)/shard_map/cond/branch_1_fun/ppermute | solution.py:470
  14.6 2.0 %collective-permute-done.8 = f32[4,512]{1,0:T(4,128)S(1)} collective-permute-done((f32[4,512]{1,0:T(4,128)S(1)}, f32[4,512]{1,0:T(4,128)S(1)}, u32[]{:S(2)}, u32[]{:S(2)}) %collective-permute-start.8) | collective-permute-done | bytes 8224 | tf_op jit(solution)/shard_map/cond/branch_1_fun/ppermute | solution.py:470
  19.8 2.7 %branch_1_fun.9 = (bf16[128,1024]{1,0:T(8,128)(2,1)}, bf16[128,1024]{1,0:T(8,128)(2,1)}, bf16[128,1024]{1,0:T(8,128)(2,1)}, bf16[128,1024]{1,0:T(8,128)(2,1)}) custom-call(s32[4,512]{1,0:T(4,128)S(1)} %get-tuple-element.54.code_ref, bf16[512,1024]{1,0:T(8,128)(2,1)} %get-tuple-element.55.tokens_ref), custom_call_target="tpu_custom_call" | custom-call | flops 1024 | bytes 1024 | tf_op jit(solution)/shard_map/cond/branch_1_fun/pallas_call | solution.py:155
  22.5 2.5 %collective-permute-done.10 = f32[1,4,512]{2,1,0:T(4,128)S(1)} collective-permute-done((f32[1,4,512]{2,1,0:T(4,128)}, f32[1,4,512]{2,1,0:T(4,128)S(1)}, u32[]{:S(2)}, u32[]{:S(2)}) %collective-permute-start.10) | collective-permute-done | bytes 8224 | tf_op jit(solution)/shard_map/cond/branch_1_fun/ppermute | solution.py:467
  25.7 4.5 %collective-permute-done.12 = bf16[128,1024]{1,0:T(8,128)(2,1)S(1)} collective-permute-done((bf16[128,1024]{1,0:T(8,128)(2,1)}, bf16[128,1024]{1,0:T(8,128)(2,1)S(1)}, u32[]{:S(2)}, u32[]{:S(2)}) %collective-permute-start.12) | collective-permute-done | bytes 262176 | tf_op jit(solution)/shard_map/ppermute | solution.py:467
  30.2 1.9 %conditional.5 = (bf16[256,1024]{1,0:T(8,128)(2,1)}) conditional(s32[]{:T(128)} %convert_element_type.16, () %tuple.55, (s32[2,4]{1,0:T(2,128)S(1)}, s32[2,4]{1,0:T(2,128)S(1)}, bf16[128,1024]{1,0:T(8,128)(2,1)S(1)}, bf16[128,1024]{1,0:T(8,128)(2,1)S(1)}, bf16[128,1024]{1,0:T(8,128)(2,1)S(1)}, /*index=5*/bf16[128,1024]{1,0:T(8,128)(2,1)S(1)}) %tuple.56), branch_computations={%region_6.7_spmd, %region_7.8_spmd} | conditional | flops 1024 | bytes 524298 | solution.py:547
  30.2 1.9 %branch_1_fun.11 = bf16[256,1024]{1,0:T(8,128)(2,1)} custom-call(s32[2,4]{1,0:T(2,128)S(1)} %get-tuple-element.61.offset_ref, s32[2,4]{1,0:T(2,128)S(1)} %get-tuple-element.62.count_ref, bf16[128,1024]{1,0:T(8,128)(2,1)S(1)} %get-tuple-element.63.refs_0_, bf16[128,1024]{1,0:T(8,128)(2,1)S(1)} %get-tuple-element.64.refs_1_, ...), custom_call_target="tpu_custom_call" | custom-call | flops 1024 | bytes 1024 | tf_op jit(solution)/shard_map/cond/branch_1_fun/pallas_call | solution.py:192
  33.8 2.5 %collective-permute-start.14 = (bf16[128,1024]{1,0:T(8,128)(2,1)}, bf16[128,1024]{1,0:T(8,128)(2,1)S(1)}, u32[]{:S(2)}, u32[]{:S(2)}) collective-permute-start(bf16[128,1024]{1,0:T(8,128)(2,1)} %get-tuple-element.191), channel_id=1, source_target_pairs={{0,12},{4,8},{8,4},{12,0},{1,13},{5,9},{9,5},{13,1},{2,14},{6,10},... | collective-permute-start | bytes 786440 | tf_op jit(solution)/shard_map/ppermute | solution.py:467
  36.3 1.9 %collective-permute-start.16 = (bf16[128,1024]{1,0:T(8,128)(2,1)}, bf16[128,1024]{1,0:T(8,128)(2,1)S(1)}, u32[]{:S(2)}, u32[]{:S(2)}) collective-permute-start(bf16[128,1024]{1,0:T(8,128)(2,1)} %get-tuple-element.193), channel_id=1, source_target_pairs={{0,4},{4,0},{8,12},{12,8},{1,5},{5,1},{9,13},{13,9},{2,6},{6,2},{1... | collective-permute-start | bytes 786440 | tf_op jit(solution)/shard_map/ppermute | solution.py:467
  39.9 2.6 %shard_map.74 = (f32[256,256]{1,0:T(8,128)S(1)}, f32[256,256]{1,0:T(8,128)S(1)}, bf16[2,1024,256]{2,1,0:T(8,128)(2,1)S(1)}, bf16[2,1024,256]{2,1,0:T(8,128)(2,1)S(1)}) custom-call(s32[4]{0:T(128)S(1)} %pad_add_fusion.order_ref, bf16[1,4096,256]{2,1,0:T(8,128)(2,1)S(1)} %copy-done, bf16[1,4096,256]{2,1,0:T(8,128)(2,1)S(1)} %copy-done.1, ...), custom_call_target="tpu_custom_call" | custom-call | flops 1024 | bytes 1024 | tf_op jit(solution)/shard_map/pallas_call | solution.py:240
  42.5 4.4 %collective-permute-done.17 = bf16[256,1024]{1,0:T(8,128)(2,1)} collective-permute-done((bf16[256,1024]{1,0:T(8,128)(2,1)}, bf16[256,1024]{1,0:T(8,128)(2,1)}, u32[]{:S(2)}, u32[]{:S(2)}) %collective-permute-start.17) | collective-permute-done | bytes 524320 | tf_op jit(solution)/shard_map/ppermute | solution.py:470
  46.9 10.3 %conditional.6 = (bf16[256,256]{1,0:T(8,128)(2,1)}, bf16[256,256]{1,0:T(8,128)(2,1)}, f32[256,1024]{1,0:T(8,128)S(1)}, bf16[2,256,1024]{2,1,0:T(8,128)(2,1)S(1)}) conditional(s32[]{:T(128)} %convert_element_type.16, () %tuple.54, (bf16[256,1024]{1,0:T(8,128)(2,1)}, f32[256,256]{1,0:T(8,128)S(1)}, f32[256,256]{1,0:T(8,128)S(1)}, ...), branch_computations={%region_8.9_spmd, %region_9.10_spmd} | conditional | flops 3072 | bytes 3673280 | solution.py:547
  52.8 2.8 %collective-permute-done.1 = bf16[256,256]{1,0:T(8,128)(2,1)} collective-permute-done((bf16[256,256]{1,0:T(8,128)(2,1)S(1)}, bf16[256,256]{1,0:T(8,128)(2,1)}, u32[]{:S(2)}, u32[]{:S(2)}) %collective-permute-start.1) | collective-permute-done | bytes 131104 | tf_op jit(solution)/shard_map/cond/branch_1_fun/ppermute | solution.py:470
  55.6 1.7 %collective-permute-done.3 = bf16[256,256]{1,0:T(8,128)(2,1)} collective-permute-done((bf16[256,256]{1,0:T(8,128)(2,1)}, bf16[256,256]{1,0:T(8,128)(2,1)}, u32[]{:S(2)}, u32[]{:S(2)}) %collective-permute-start.3) | collective-permute-done | bytes 131104 | tf_op jit(solution)/shard_map/cond/branch_1_fun/ppermute | solution.py:470
  58.5 2.0 %shard_map.75.refs_0_ = bf16[256,1024]{1,0:T(8,128)(2,1)S(1)} custom-call(s32[2,4]{1,0:T(2,128)S(1)} %get-tuple-element.253.offset_ref, s32[2,4]{1,0:T(2,128)S(1)} %get-tuple-element.254.count_ref, bf16[128,1024]{1,0:T(8,128)(2,1)} %get-tuple-element.205.refs_0_, bf16[128,1024]{1,0:T(8,128)(2,1)S(1)} %collective-permute-done.14.refs_1_, ...), custom_call_target="tpu_custom_call" | custom-call | flops 1024 | bytes 1024 | tf_op jit(solution)/shard_map/pallas_call | solution.py:192
  61.2 3.1 %shard_map.76 = (bf16[128,1024]{1,0:T(8,128)(2,1)S(1)}, bf16[128,1024]{1,0:T(8,128)(2,1)}, bf16[128,1024]{1,0:T(8,128)(2,1)}, bf16[128,1024]{1,0:T(8,128)(2,1)}) custom-call(s32[2,4]{1,0:T(2,128)S(1)} %get-tuple-element.253.offset_ref, s32[2,4]{1,0:T(2,128)S(1)} %get-tuple-element.254.count_ref, f32[256,1024]{1,0:T(8,128)S(1)} %get-tuple-element.211.before_ref, ...), custom_call_target="tpu_custom_call" | custom-call | flops 1024 | bytes 1024 | tf_op jit(solution)/shard_map/pallas_call | solution.py:365
  64.3 2.4 %collective-permute-start.21 = (bf16[128,1024]{1,0:T(8,128)(2,1)}, bf16[128,1024]{1,0:T(8,128)(2,1)}, u32[]{:S(2)}, u32[]{:S(2)}) collective-permute-start(bf16[128,1024]{1,0:T(8,128)(2,1)} %get-tuple-element.216), channel_id=1, source_target_pairs={{0,12},{4,8},{8,4},{12,0},{1,13},{5,9},{9,5},{13,1},{2,14},{6,10},... | collective-permute-start | bytes 786440 | tf_op jit(solution)/shard_map/ppermute | solution.py:467
  66.7 2.0 %collective-permute-start.23 = (bf16[128,1024]{1,0:T(8,128)(2,1)}, bf16[128,1024]{1,0:T(8,128)(2,1)}, u32[]{:S(2)}, u32[]{:S(2)}) collective-permute-start(bf16[128,1024]{1,0:T(8,128)(2,1)} %get-tuple-element.218), channel_id=1, source_target_pairs={{0,4},{4,0},{8,12},{12,8},{1,5},{5,1},{9,13},{13,9},{2,6},{6,2},{1... | collective-permute-start | bytes 786440 | tf_op jit(solution)/shard_map/ppermute | solution.py:467
  71.0 1.8 %shard_map.77 = (f32[256,256]{1,0:T(8,128)S(1)}, f32[256,256]{1,0:T(8,128)S(1)}, bf16[2,1024,256]{2,1,0:T(8,128)(2,1)S(1)}, bf16[2,1024,256]{2,1,0:T(8,128)(2,1)S(1)}) custom-call(s32[4]{0:T(128)S(1)} %pad_add_fusion.order_ref, bf16[1,4096,256]{2,1,0:T(8,128)(2,1)S(1)} %copy-done, bf16[1,4096,256]{2,1,0:T(8,128)(2,1)S(1)} %copy-done.2, ...), custom_call_target="tpu_custom_call" | custom-call | flops 1024 | bytes 1024 | tf_op jit(solution)/shard_map/pallas_call | solution.py:240
  72.8 2.2 %collective-permute-done.19 = bf16[256,1024]{1,0:T(8,128)(2,1)} collective-permute-done((bf16[256,1024]{1,0:T(8,128)(2,1)S(1)}, bf16[256,1024]{1,0:T(8,128)(2,1)}, u32[]{:S(2)}, u32[]{:S(2)}) %collective-permute-start.19) | collective-permute-done | bytes 524320 | tf_op jit(solution)/shard_map/ppermute | solution.py:470
  75.0 10.3 %conditional.7 = (bf16[256,256]{1,0:T(8,128)(2,1)}, bf16[256,256]{1,0:T(8,128)(2,1)}, f32[256,1024]{1,0:T(8,128)S(1)}, bf16[2,256,1024]{2,1,0:T(8,128)(2,1)S(1)}) conditional(s32[]{:T(128)} %convert_element_type.17, () %tuple.51, (bf16[256,1024]{1,0:T(8,128)(2,1)}, f32[256,256]{1,0:T(8,128)S(1)}, f32[256,256]{1,0:T(8,128)S(1)}, ...), branch_computations={%region_10.11_spmd, %region_11.12_spmd} | conditional | flops 3072 | bytes 3673280 | solution.py:547
  80.6 3.1 %collective-permute-done.5 = bf16[256,256]{1,0:T(8,128)(2,1)} collective-permute-done((bf16[256,256]{1,0:T(8,128)(2,1)S(1)}, bf16[256,256]{1,0:T(8,128)(2,1)}, u32[]{:S(2)}, u32[]{:S(2)}) %collective-permute-start.5) | collective-permute-done | bytes 131104 | tf_op jit(solution)/shard_map/cond/branch_1_fun/ppermute | solution.py:470
  83.7 1.7 %collective-permute-done.7 = bf16[256,256]{1,0:T(8,128)(2,1)} collective-permute-done((bf16[256,256]{1,0:T(8,128)(2,1)}, bf16[256,256]{1,0:T(8,128)(2,1)}, u32[]{:S(2)}, u32[]{:S(2)}) %collective-permute-start.7) | collective-permute-done | bytes 131104 | tf_op jit(solution)/shard_map/cond/branch_1_fun/ppermute | solution.py:470
  85.4 2.4 %shard_map.78 = (bf16[128,1024]{1,0:T(8,128)(2,1)S(1)}, bf16[128,1024]{1,0:T(8,128)(2,1)S(1)}, bf16[128,1024]{1,0:T(8,128)(2,1)S(1)}, bf16[128,1024]{1,0:T(8,128)(2,1)S(1)}) custom-call(s32[2,4]{1,0:T(2,128)S(1)} %get-tuple-element.253.offset_ref, s32[2,4]{1,0:T(2,128)S(1)} %get-tuple-element.254.count_ref, f32[256,1024]{1,0:T(8,128)S(1)} %get-tuple-element.230.before_ref, ...), custom_call_target="tpu_custom_call" | custom-call | flops 1024 | bytes 1024 | tf_op jit(solution)/shard_map/pallas_call | solution.py:365
  91.2 2.4 %collective-permute-start.27 = (bf16[128,1024]{1,0:T(8,128)(2,1)S(1)}, bf16[128,1024]{1,0:T(8,128)(2,1)S(1)}, u32[]{:S(2)}, u32[]{:S(2)}) collective-permute-start(bf16[128,1024]{1,0:T(8,128)(2,1)S(1)} %get-tuple-element.248), channel_id=1, source_target_pairs={{0,4},{4,0},{8,12},{12,8},{1,5},{5,1},{9,13},{13,9},{2,6},{6,2},{1... | collective-permute-start | bytes 786440 | tf_op jit(solution)/shard_map/ppermute | solution.py:467
  94.7 1.9 %shard_map.80.refs_0_ = f32[512,1024]{1,0:T(8,128)S(1)} custom-call(s32[4,512]{1,0:T(4,128)S(1)} %get-tuple-element.175.code_ref, f32[4,512]{1,0:T(4,128)S(1)} %shard_map.79.weight_ref, bf16[128,1024]{1,0:T(8,128)(2,1)S(1)} %get-tuple-element.241.refs_0_, bf16[128,1024]{1,0:T(8,128)(2,1)} %collective-permute-done.21.refs_1_, ...), custom_call_target="tpu_custom_call" | custom-call | flops 1024 | bytes 1024 | tf_op jit(solution)/shard_map/pallas_call | solution.py:440
  96.6 3.7 %collective-permute-done.25.refs_2_ = bf16[128,1024]{1,0:T(8,128)(2,1)S(1)} collective-permute-done((bf16[128,1024]{1,0:T(8,128)(2,1)S(1)}, bf16[128,1024]{1,0:T(8,128)(2,1)S(1)}, u32[]{:S(2)}, u32[]{:S(2)}) %collective-permute-start.25) | collective-permute-done | bytes 262176 | tf_op jit(solution)/shard_map/ppermute | solution.py:467
  100.9 13.2 %collective-permute-done.26.refs_1_ = bf16[128,1024]{1,0:T(8,128)(2,1)S(1)} collective-permute-done((bf16[128,1024]{1,0:T(8,128)(2,1)S(1)}, bf16[128,1024]{1,0:T(8,128)(2,1)S(1)}, u32[]{:S(2)}, u32[]{:S(2)}) %collective-permute-start.26) | collective-permute-done | bytes 262176 | tf_op jit(solution)/shard_map/ppermute | solution.py:467
  (68 shorter events, 31.5 us)
Async XLA Ops:
  2.6 23.1 %collective-permute-start.11 = (bf16[128,1024]{1,0:T(8,128)(2,1)}, bf16[128,1024]{1,0:T(8,128)(2,1)S(1)}, u32[]{:S(2)}, u32[]{:S(2)}) collective-permute-start(bf16[128,1024]{1,0:T(8,128)(2,1)} %get-tuple-element.182), channel_id=1, source_target_pairs={{0,12},{4,8},{8,4},{12,0},{1,13},{5,9},{9,5},{13,1},{2,14},{6,10},... | collective-permute-start | bytes 786440 | tf_op jit(solution)/shard_map/ppermute | solution.py:467
  7.7 22.5 %collective-permute-start.12 = (bf16[128,1024]{1,0:T(8,128)(2,1)}, bf16[128,1024]{1,0:T(8,128)(2,1)S(1)}, u32[]{:S(2)}, u32[]{:S(2)}) collective-permute-start(bf16[128,1024]{1,0:T(8,128)(2,1)} %get-tuple-element.183), channel_id=1, source_target_pairs={{0,8},{4,12},{8,0},{12,4},{1,9},{5,13},{9,1},{13,5},{2,10},{6,14},... | collective-permute-start | bytes 786440 | tf_op jit(solution)/shard_map/ppermute | solution.py:467
  7.7 22.5 %collective-permute-start.13 = (bf16[128,1024]{1,0:T(8,128)(2,1)}, bf16[128,1024]{1,0:T(8,128)(2,1)S(1)}, u32[]{:S(2)}, u32[]{:S(2)}) collective-permute-start(bf16[128,1024]{1,0:T(8,128)(2,1)} %get-tuple-element.184), channel_id=1, source_target_pairs={{0,4},{4,0},{8,12},{12,8},{1,5},{5,1},{9,13},{13,9},{2,6},{6,2},{1... | collective-permute-start | bytes 786440 | tf_op jit(solution)/shard_map/ppermute | solution.py:467
  11.2 27.1 %copy-start = (bf16[1,4096,256]{2,1,0:T(8,128)(2,1)S(1)}, bf16[1,4096,256]{2,1,0:T(8,128)(2,1)}, u32[]{:S(2)}) copy-start(bf16[1,4096,256]{2,1,0:T(8,128)(2,1)} %gate_ref.3) | copy-start | bytes 6291460
  13.0 3.7 %collective-permute-start.8 = (f32[4,512]{1,0:T(4,128)S(1)}, f32[4,512]{1,0:T(4,128)S(1)}, u32[]{:S(2)}, u32[]{:S(2)}) collective-permute-start(f32[4,512]{1,0:T(4,128)S(1)} %branch_1_fun.10), channel_id=1, source_target_pairs={{0,2},{1,3},{2,0},{3,1},{4,6},{5,7},{6,4},{7,5},{8,10},{9,11},{10,... | collective-permute-start | bytes 24584 | tf_op jit(solution)/shard_map/cond/branch_1_fun/ppermute | solution.py:470
  16.7 1.2 %collective-permute-start.9 = (f32[4,512]{1,0:T(4,128)S(1)}, f32[4,512]{1,0:T(4,128)S(1)}, u32[]{:S(2)}, u32[]{:S(2)}) collective-permute-start(f32[4,512]{1,0:T(4,128)S(1)} %add.24), channel_id=1, source_target_pairs={{0,1},{1,0},{2,3},{3,2},{4,5},{5,4},{6,7},{7,6},{8,9},{9,8},{10,11... | collective-permute-start | bytes 24584 | tf_op jit(solution)/shard_map/cond/branch_1_fun/ppermute | solution.py:470
  18.4 6.6 %collective-permute-start.10 = (f32[1,4,512]{2,1,0:T(4,128)}, f32[1,4,512]{2,1,0:T(4,128)S(1)}, u32[]{:S(2)}, u32[]{:S(2)}) collective-permute-start(f32[1,4,512]{2,1,0:T(4,128)} %bitcast), channel_id=1, source_target_pairs={{0,4},{4,0},{8,12},{12,8},{1,5},{5,1},{9,13},{13,9},{2,6},{6,2},{1... | collective-permute-start | bytes 24584 | tf_op jit(solution)/shard_map/cond/branch_1_fun/ppermute | solution.py:467
  32.2 6.1 %collective-permute-start.18 = (bf16[256,1024]{1,0:T(8,128)(2,1)}, bf16[256,1024]{1,0:T(8,128)(2,1)S(1)}, u32[]{:S(2)}, u32[]{:S(2)}) collective-permute-start(bf16[256,1024]{1,0:T(8,128)(2,1)} %get-tuple-element.287.refs_0_), channel_id=1, source_target_pairs={{0,1},{1,0},{2,3},{3,2},{4,5},{5,4},{6,7},{7,6},{8,9},{9,8},{10,11... | collective-permute-start | bytes 1572872 | tf_op jit(solution)/shard_map/ppermute | solution.py:470
  32.3 14.7 %collective-permute-start.17 = (bf16[256,1024]{1,0:T(8,128)(2,1)}, bf16[256,1024]{1,0:T(8,128)(2,1)}, u32[]{:S(2)}, u32[]{:S(2)}) collective-permute-start(bf16[256,1024]{1,0:T(8,128)(2,1)} %get-tuple-element.287.refs_0_), channel_id=1, source_target_pairs={{0,2},{1,3},{2,0},{3,1},{4,6},{5,7},{6,4},{7,5},{8,10},{9,11},{10,... | collective-permute-start | bytes 1572872 | tf_op jit(solution)/shard_map/ppermute | solution.py:470
  33.8 23.5 %collective-permute-start.14 = (bf16[128,1024]{1,0:T(8,128)(2,1)}, bf16[128,1024]{1,0:T(8,128)(2,1)S(1)}, u32[]{:S(2)}, u32[]{:S(2)}) collective-permute-start(bf16[128,1024]{1,0:T(8,128)(2,1)} %get-tuple-element.191), channel_id=1, source_target_pairs={{0,12},{4,8},{8,4},{12,0},{1,13},{5,9},{9,5},{13,1},{2,14},{6,10},... | collective-permute-start | bytes 786440 | tf_op jit(solution)/shard_map/ppermute | solution.py:467
  36.3 22.2 %collective-permute-start.15 = (bf16[128,1024]{1,0:T(8,128)(2,1)}, bf16[128,1024]{1,0:T(8,128)(2,1)S(1)}, u32[]{:S(2)}, u32[]{:S(2)}) collective-permute-start(bf16[128,1024]{1,0:T(8,128)(2,1)} %get-tuple-element.192), channel_id=1, source_target_pairs={{0,8},{4,12},{8,0},{12,4},{1,9},{5,13},{9,1},{13,5},{2,10},{6,14},... | collective-permute-start | bytes 786440 | tf_op jit(solution)/shard_map/ppermute | solution.py:467
  36.3 22.2 %collective-permute-start.16 = (bf16[128,1024]{1,0:T(8,128)(2,1)}, bf16[128,1024]{1,0:T(8,128)(2,1)S(1)}, u32[]{:S(2)}, u32[]{:S(2)}) collective-permute-start(bf16[128,1024]{1,0:T(8,128)(2,1)} %get-tuple-element.193), channel_id=1, source_target_pairs={{0,4},{4,0},{8,12},{12,8},{1,5},{5,1},{9,13},{13,9},{2,6},{6,2},{1... | collective-permute-start | bytes 786440 | tf_op jit(solution)/shard_map/ppermute | solution.py:467
  38.3 1.6 %copy-start.1 = (bf16[1,4096,256]{2,1,0:T(8,128)(2,1)S(1)}, bf16[1,4096,256]{2,1,0:T(8,128)(2,1)}, u32[]{:S(2)}) copy-start(bf16[1,4096,256]{2,1,0:T(8,128)(2,1)} %up_ref.3) | copy-start | bytes 6291460
  39.9 7.0 %copy-start.3 = (bf16[1,1024,1024]{2,1,0:T(8,128)(2,1)S(1)}, bf16[1,1024,1024]{2,1,0:T(8,128)(2,1)}, u32[]{:S(2)}) copy-start(bf16[1,1024,1024]{2,1,0:T(8,128)(2,1)} %param.19) | copy-start | bytes 6291460
  46.9 2.1 %collective-permute-start = (bf16[256,1024]{1,0:T(8,128)(2,1)}, bf16[256,1024]{1,0:T(8,128)(2,1)S(1)}, u32[]{:S(2)}, u32[]{:S(2)}) collective-permute-start(bf16[256,1024]{1,0:T(8,128)(2,1)} %get-tuple-element.67.refs_0_), channel_id=1, source_target_pairs={{0,1},{1,0},{2,3},{3,2},{4,5},{5,4},{6,7},{7,6},{8,9},{9,8},{10,11... | collective-permute-start | bytes 1572872 | tf_op jit(solution)/shard_map/cond/branch_1_fun/ppermute | solution.py:470
  49.5 1.7 %collective-permute-start.2 = (bf16[256,256]{1,0:T(8,128)(2,1)S(1)}, bf16[256,256]{1,0:T(8,128)(2,1)S(1)}, u32[]{:S(2)}, u32[]{:S(2)}) collective-permute-start(bf16[256,256]{1,0:T(8,128)(2,1)S(1)} %branch_1_fun.13.refs_0_), channel_id=1, source_target_pairs={{0,1},{1,0},{2,3},{3,2},{4,5},{5,4},{6,7},{7,6},{8,9},{9,8},{10,11... | collective-permute-start | bytes 393224 | tf_op jit(solution)/shard_map/cond/branch_1_fun/ppermute | solution.py:470
  49.7 5.9 %collective-permute-start.1 = (bf16[256,256]{1,0:T(8,128)(2,1)S(1)}, bf16[256,256]{1,0:T(8,128)(2,1)}, u32[]{:S(2)}, u32[]{:S(2)}) collective-permute-start(bf16[256,256]{1,0:T(8,128)(2,1)S(1)} %branch_1_fun.13.refs_0_), channel_id=1, source_target_pairs={{0,2},{1,3},{2,0},{3,1},{4,6},{5,7},{6,4},{7,5},{8,10},{9,11},{10,... | collective-permute-start | bytes 393224 | tf_op jit(solution)/shard_map/cond/branch_1_fun/ppermute | solution.py:470
  55.6 1.7 %collective-permute-start.3 = (bf16[256,256]{1,0:T(8,128)(2,1)}, bf16[256,256]{1,0:T(8,128)(2,1)}, u32[]{:S(2)}, u32[]{:S(2)}) collective-permute-start(bf16[256,256]{1,0:T(8,128)(2,1)} %collective-permute-done.1), channel_id=1, source_target_pairs={{0,1},{1,0},{2,3},{3,2},{4,5},{5,4},{6,7},{7,6},{8,9},{9,8},{10,11... | collective-permute-start | bytes 393224 | tf_op jit(solution)/shard_map/cond/branch_1_fun/ppermute | solution.py:470
  60.5 8.9 %collective-permute-start.20 = (bf16[256,1024]{1,0:T(8,128)(2,1)S(1)}, bf16[256,1024]{1,0:T(8,128)(2,1)S(1)}, u32[]{:S(2)}, u32[]{:S(2)}) collective-permute-start(bf16[256,1024]{1,0:T(8,128)(2,1)S(1)} %shard_map.75.refs_0_), channel_id=1, source_target_pairs={{0,1},{1,0},{2,3},{3,2},{4,5},{5,4},{6,7},{7,6},{8,9},{9,8},{10,11... | collective-permute-start | bytes 1572872 | tf_op jit(solution)/shard_map/ppermute | solution.py:470
  60.6 14.4 %collective-permute-start.19 = (bf16[256,1024]{1,0:T(8,128)(2,1)S(1)}, bf16[256,1024]{1,0:T(8,128)(2,1)}, u32[]{:S(2)}, u32[]{:S(2)}) collective-permute-start(bf16[256,1024]{1,0:T(8,128)(2,1)S(1)} %shard_map.75.refs_0_), channel_id=1, source_target_pairs={{0,2},{1,3},{2,0},{3,1},{4,6},{5,7},{6,4},{7,5},{8,10},{9,11},{10,... | collective-permute-start | bytes 1572872 | tf_op jit(solution)/shard_map/ppermute | solution.py:470
  64.3 23.5 %collective-permute-start.21 = (bf16[128,1024]{1,0:T(8,128)(2,1)}, bf16[128,1024]{1,0:T(8,128)(2,1)}, u32[]{:S(2)}, u32[]{:S(2)}) collective-permute-start(bf16[128,1024]{1,0:T(8,128)(2,1)} %get-tuple-element.216), channel_id=1, source_target_pairs={{0,12},{4,8},{8,4},{12,0},{1,13},{5,9},{9,5},{13,1},{2,14},{6,10},... | collective-permute-start | bytes 786440 | tf_op jit(solution)/shard_map/ppermute | solution.py:467
  66.7 22.5 %collective-permute-start.22 = (bf16[128,1024]{1,0:T(8,128)(2,1)}, bf16[128,1024]{1,0:T(8,128)(2,1)}, u32[]{:S(2)}, u32[]{:S(2)}) collective-permute-start(bf16[128,1024]{1,0:T(8,128)(2,1)} %get-tuple-element.217), channel_id=1, source_target_pairs={{0,8},{4,12},{8,0},{12,4},{1,9},{5,13},{9,1},{13,5},{2,10},{6,14},... | collective-permute-start | bytes 786440 | tf_op jit(solution)/shard_map/ppermute | solution.py:467
  66.7 22.5 %collective-permute-start.23 = (bf16[128,1024]{1,0:T(8,128)(2,1)}, bf16[128,1024]{1,0:T(8,128)(2,1)}, u32[]{:S(2)}, u32[]{:S(2)}) collective-permute-start(bf16[128,1024]{1,0:T(8,128)(2,1)} %get-tuple-element.218), channel_id=1, source_target_pairs={{0,4},{4,0},{8,12},{12,8},{1,5},{5,1},{9,13},{13,9},{2,6},{6,2},{1... | collective-permute-start | bytes 786440 | tf_op jit(solution)/shard_map/ppermute | solution.py:467
  71.0 4.1 %copy-start.4 = (bf16[1,1024,1024]{2,1,0:T(8,128)(2,1)S(1)}, bf16[1,1024,1024]{2,1,0:T(8,128)(2,1)}, u32[]{:S(2)}) copy-start(bf16[1,1024,1024]{2,1,0:T(8,128)(2,1)} %param.19) | copy-start | bytes 6291460
  75.0 2.1 %collective-permute-start.4 = (bf16[256,1024]{1,0:T(8,128)(2,1)}, bf16[256,1024]{1,0:T(8,128)(2,1)S(1)}, u32[]{:S(2)}, u32[]{:S(2)}) collective-permute-start(bf16[256,1024]{1,0:T(8,128)(2,1)} %get-tuple-element.84.refs_0_), channel_id=1, source_target_pairs={{0,1},{1,0},{2,3},{3,2},{4,5},{5,4},{6,7},{7,6},{8,9},{9,8},{10,11... | collective-permute-start | bytes 1572872 | tf_op jit(solution)/shard_map/cond/branch_1_fun/ppermute | solution.py:470
  77.6 1.4 %collective-permute-start.6 = (bf16[256,256]{1,0:T(8,128)(2,1)S(1)}, bf16[256,256]{1,0:T(8,128)(2,1)S(1)}, u32[]{:S(2)}, u32[]{:S(2)}) collective-permute-start(bf16[256,256]{1,0:T(8,128)(2,1)S(1)} %branch_1_fun.16.refs_0_), channel_id=1, source_target_pairs={{0,1},{1,0},{2,3},{3,2},{4,5},{5,4},{6,7},{7,6},{8,9},{9,8},{10,11... | collective-permute-start | bytes 393224 | tf_op jit(solution)/shard_map/cond/branch_1_fun/ppermute | solution.py:470
  77.8 5.9 %collective-permute-start.5 = (bf16[256,256]{1,0:T(8,128)(2,1)S(1)}, bf16[256,256]{1,0:T(8,128)(2,1)}, u32[]{:S(2)}, u32[]{:S(2)}) collective-permute-start(bf16[256,256]{1,0:T(8,128)(2,1)S(1)} %branch_1_fun.16.refs_0_), channel_id=1, source_target_pairs={{0,2},{1,3},{2,0},{3,1},{4,6},{5,7},{6,4},{7,5},{8,10},{9,11},{10,... | collective-permute-start | bytes 393224 | tf_op jit(solution)/shard_map/cond/branch_1_fun/ppermute | solution.py:470
  83.7 1.7 %collective-permute-start.7 = (bf16[256,256]{1,0:T(8,128)(2,1)}, bf16[256,256]{1,0:T(8,128)(2,1)}, u32[]{:S(2)}, u32[]{:S(2)}) collective-permute-start(bf16[256,256]{1,0:T(8,128)(2,1)} %collective-permute-done.5), channel_id=1, source_target_pairs={{0,1},{1,0},{2,3},{3,2},{4,5},{5,4},{6,7},{7,6},{8,9},{9,8},{10,11... | collective-permute-start | bytes 393224 | tf_op jit(solution)/shard_map/cond/branch_1_fun/ppermute | solution.py:470
  85.4 5.9 %collective-permute-start.24 = (f32[2,4,512]{2,1,0:T(4,128)S(1)}, f32[2,4,512]{2,1,0:T(4,128)S(1)}, u32[]{:S(2)}, u32[]{:S(2)}) collective-permute-start(f32[2,4,512]{2,1,0:T(4,128)S(1)} %get-tuple-element.239), channel_id=1, source_target_pairs={{0,8},{4,12},{8,0},{12,4},{1,9},{5,13},{9,1},{13,5},{2,10},{6,14},... | collective-permute-start | bytes 49160 | tf_op jit(solution)/shard_map/ppermute | solution.py:467
  89.2 11.1 %collective-permute-start.25 = (bf16[128,1024]{1,0:T(8,128)(2,1)S(1)}, bf16[128,1024]{1,0:T(8,128)(2,1)S(1)}, u32[]{:S(2)}, u32[]{:S(2)}) collective-permute-start(bf16[128,1024]{1,0:T(8,128)(2,1)S(1)} %get-tuple-element.246), channel_id=1, source_target_pairs={{0,12},{4,8},{8,4},{12,0},{1,13},{5,9},{9,5},{13,1},{2,14},{6,10},... | collective-permute-start | bytes 786440 | tf_op jit(solution)/shard_map/ppermute | solution.py:467
  90.6 23.5 %collective-permute-start.26 = (bf16[128,1024]{1,0:T(8,128)(2,1)S(1)}, bf16[128,1024]{1,0:T(8,128)(2,1)S(1)}, u32[]{:S(2)}, u32[]{:S(2)}) collective-permute-start(bf16[128,1024]{1,0:T(8,128)(2,1)S(1)} %get-tuple-element.247), channel_id=1, source_target_pairs={{0,8},{4,12},{8,0},{12,4},{1,9},{5,13},{9,1},{13,5},{2,10},{6,14},... | collective-permute-start | bytes 786440 | tf_op jit(solution)/shard_map/ppermute | solution.py:467
  91.2 22.9 %collective-permute-start.27 = (bf16[128,1024]{1,0:T(8,128)(2,1)S(1)}, bf16[128,1024]{1,0:T(8,128)(2,1)S(1)}, u32[]{:S(2)}, u32[]{:S(2)}) collective-permute-start(bf16[128,1024]{1,0:T(8,128)(2,1)S(1)} %get-tuple-element.248), channel_id=1, source_target_pairs={{0,4},{4,0},{8,12},{12,8},{1,5},{5,1},{9,13},{13,9},{2,6},{6,2},{1... | collective-permute-start | bytes 786440 | tf_op jit(solution)/shard_map/ppermute | solution.py:467
  (1 other events, 1.6 us)

commit v18 on v17

--- a/solution.py
+++ b/solution.py
@@ -32,7 +32,7 @@
 
 
 def partner(place, experts):
-    return -place % experts
+    return -(3 - place if place in (1, 2) else place) % experts
 
 
 def dot(a, b):

time: 116 us -> 116 us (level)
  the two profiles are of different devices: /device:TPU:0 before, /device:TPU:16 now
where the time goes in v18:
time: 116 us; the launch traced here: 115 us
  waiting for transfers between devices  47 us (41%)
  Pallas kernels  33 us (28%)
  starting transfers between devices  26.7 us (23%)
  local copies, waits for them, and re-layouts  3.89 us (3%)
  other arithmetic  2.93 us (3%)
  between operations  1.54 us (1%)
    ppermute x14, waiting for transfers between devices, along_expert(): return lax.ppermute(x, 'expert', [(i, i ^ shift) for i in range(experts)])  27.8 us
    ppermute x14, waiting for transfers between devices, swap(): return lax.ppermute(x, 'dp', [(i, i ^ bit) for i in range(width_parts)])  19.2 us
    ppermute x14, starting transfers between devices, along_expert(): return lax.ppermute(x, 'expert', [(i, i ^ shift) for i in range(experts)])  18.4 us
    ppermute x14, starting transfers between devices, swap(): return lax.ppermute(x, 'dp', [(i, i ^ bit) for i in range(width_parts)])  8.27 us
    pallas_call x2, Pallas kernels, down_last(): pl.pallas_call(functools.partial(down_last_kernel, parts, experts, k, dir...  5.47 us
    pallas_call x2, Pallas kernels, gate_up_near(): pl.pallas_call(functools.partial(gate_up_near_kernel, parts, near, far),...  4.4 us
    pallas_call x3, Pallas kernels, combine(): pl.pallas_call(functools.partial(combine_kernel, places, k, len(more)), o...  4.02 us
    pallas_call x2, Pallas kernels, compact(): pl.pallas_call(functools.partial(compact_kernel, experts, k), out_shape=j...  3.94 us
  transfers between devices with their start and end apart: 28, of which 15 were waited for; matrix products, arithmetic and copies ran while one was open for 3% of the time, Pallas kernels for 22%

profile of v18, /device:TPU:16, one launch (start us, length us, event | category | flops | bytes accessed | tf_op | source)
XLA Modules:
  0.0 115.0 jit_solution(5917049062994832630)
XLA Ops:
  0.0 2.6 %shard_map.73 = (s32[4,512]{1,0:T(4,128)S(1)}, bf16[128,1024]{1,0:T(8,128)(2,1)S(1)}, bf16[128,1024]{1,0:T(8,128)(2,1)}, bf16[128,1024]{1,0:T(8,128)(2,1)}, bf16[128,1024]{1,0:T(8,128)(2,1)}) custom-call(s32[1]{0:T(128)} %bitcast.1.place_ref, s32[4,512]{1,0:T(4,128)} %picks_in.1, bf16[512,1024]{1,0:T(8,128)(2,1)} %tokens_ref.1), custom_call_target="tpu_custom_call" | custom-call | flops 1024 | bytes 1024 | tf_op jit(solution)/shard_map/pallas_call | solution.py:108
  2.7 3.0 %collective-permute-start.12 = (bf16[128,1024]{1,0:T(8,128)(2,1)}, bf16[128,1024]{1,0:T(8,128)(2,1)S(1)}, u32[]{:S(2)}, u32[]{:S(2)}) collective-permute-start(bf16[128,1024]{1,0:T(8,128)(2,1)} %get-tuple-element.183), channel_id=1, source_target_pairs={{0,12},{4,8},{8,4},{12,0},{1,13},{5,9},{9,5},{13,1},{2,14},{6,10},... | collective-permute-start | bytes 786440 | tf_op jit(solution)/shard_map/ppermute | solution.py:467
  9.9 14.4 %conditional.4 = (bf16[128,1024]{1,0:T(8,128)(2,1)}, bf16[128,1024]{1,0:T(8,128)(2,1)}, bf16[128,1024]{1,0:T(8,128)(2,1)}, bf16[128,1024]{1,0:T(8,128)(2,1)}, f3...) conditional(s32[]{:T(128)} %convert_element_type.16, () %tuple.49, (s32[4,512]{1,0:T(4,128)S(1)}, ...), branch_computations={%region_3.4_spmd, %region_4.5_spmd} | conditional | flops 10240 | bytes 1073216 | solution.py:525
  9.9 1.8 %branch_1_fun.10 = f32[4,512]{1,0:T(4,128)S(1)} custom-call(bf16[4,1024]{1,0:T(4,128)(2,1)} %get-tuple-element.60.router_ref, bf16[512,1024]{1,0:T(8,128)(2,1)} %get-tuple-element.55.tokens_ref), custom_call_target="tpu_custom_call" | custom-call | flops 1024 | bytes 1024 | tf_op jit(solution)/shard_map/cond/branch_1_fun/pallas_call | solution.py:134
  13.2 2.2 %collective-permute-done.8 = f32[4,512]{1,0:T(4,128)S(1)} collective-permute-done((f32[4,512]{1,0:T(4,128)S(1)}, f32[4,512]{1,0:T(4,128)S(1)}, u32[]{:S(2)}, u32[]{:S(2)}) %collective-permute-start.8) | collective-permute-done | bytes 8224 | tf_op jit(solution)/shard_map/cond/branch_1_fun/ppermute | solution.py:470
  17.8 2.7 %branch_1_fun.9 = (bf16[128,1024]{1,0:T(8,128)(2,1)}, bf16[128,1024]{1,0:T(8,128)(2,1)}, bf16[128,1024]{1,0:T(8,128)(2,1)}, bf16[128,1024]{1,0:T(8,128)(2,1)}) custom-call(s32[4,512]{1,0:T(4,128)S(1)} %get-tuple-element.54.code_ref, bf16[512,1024]{1,0:T(8,128)(2,1)} %get-tuple-element.55.tokens_ref), custom_call_target="tpu_custom_call" | custom-call | flops 1024 | bytes 1024 | tf_op jit(solution)/shard_map/cond/branch_1_fun/pallas_call | solution.py:155
  20.5 3.1 %collective-permute-done.10 = f32[1,4,512]{2,1,0:T(4,128)S(1)} collective-permute-done((f32[1,4,512]{2,1,0:T(4,128)}, f32[1,4,512]{2,1,0:T(4,128)S(1)}, u32[]{:S(2)}, u32[]{:S(2)}) %collective-permute-start.10) | collective-permute-done | bytes 8224 | tf_op jit(solution)/shard_map/cond/branch_1_fun/ppermute | solution.py:467
  24.3 4.4 %collective-permute-done.12 = bf16[128,1024]{1,0:T(8,128)(2,1)S(1)} collective-permute-done((bf16[128,1024]{1,0:T(8,128)(2,1)}, bf16[128,1024]{1,0:T(8,128)(2,1)S(1)}, u32[]{:S(2)}, u32[]{:S(2)}) %collective-permute-start.12) | collective-permute-done | bytes 262176 | tf_op jit(solution)/shard_map/ppermute | solution.py:467
  28.7 2.0 %conditional.5 = (bf16[256,1024]{1,0:T(8,128)(2,1)}) conditional(s32[]{:T(128)} %convert_element_type.16, () %tuple.55, (s32[2,4]{1,0:T(2,128)S(1)}, s32[2,4]{1,0:T(2,128)S(1)}, bf16[128,1024]{1,0:T(8,128)(2,1)S(1)}, bf16[128,1024]{1,0:T(8,128)(2,1)S(1)}, bf16[128,1024]{1,0:T(8,128)(2,1)S(1)}, /*index=5*/bf16[128,1024]{1,0:T(8,128)(2,1)S(1)}) %tuple.56), branch_computations={%region_6.7_spmd, %region_7.8_spmd} | conditional | flops 1024 | bytes 524298 | solution.py:547
  28.7 1.9 %branch_1_fun.11 = bf16[256,1024]{1,0:T(8,128)(2,1)} custom-call(s32[2,4]{1,0:T(2,128)S(1)} %get-tuple-element.61.offset_ref, s32[2,4]{1,0:T(2,128)S(1)} %get-tuple-element.62.count_ref, bf16[128,1024]{1,0:T(8,128)(2,1)S(1)} %get-tuple-element.63.refs_0_, bf16[128,1024]{1,0:T(8,128)(2,1)S(1)} %get-tuple-element.64.refs_1_, ...), custom_call_target="tpu_custom_call" | custom-call | flops 1024 | bytes 1024 | tf_op jit(solution)/shard_map/cond/branch_1_fun/pallas_call | solution.py:192
  32.3 4.4 %collective-permute-start.16 = (bf16[128,1024]{1,0:T(8,128)(2,1)}, bf16[128,1024]{1,0:T(8,128)(2,1)S(1)}, u32[]{:S(2)}, u32[]{:S(2)}) collective-permute-start(bf16[128,1024]{1,0:T(8,128)(2,1)} %get-tuple-element.193), channel_id=1, source_target_pairs={{0,4},{4,0},{8,12},{12,8},{1,5},{5,1},{9,13},{13,9},{2,6},{6,2},{1... | collective-permute-start | bytes 786440 | tf_op jit(solution)/shard_map/ppermute | solution.py:467
  36.8 1.6 %copy-done.1 = bf16[1,4096,256]{2,1,0:T(8,128)(2,1)S(1)} copy-done((bf16[1,4096,256]{2,1,0:T(8,128)(2,1)S(1)}, bf16[1,4096,256]{2,1,0:T(8,128)(2,1)}, u32[]{:S(2)}) %copy-start.1) | copy-done | bytes 2097176
  38.4 2.6 %shard_map.74 = (f32[256,256]{1,0:T(8,128)S(1)}, f32[256,256]{1,0:T(8,128)S(1)}, bf16[2,1024,256]{2,1,0:T(8,128)(2,1)S(1)}, bf16[2,1024,256]{2,1,0:T(8,128)(2,1)S(1)}) custom-call(s32[4]{0:T(128)S(1)} %pad_add_fusion.order_ref, bf16[1,4096,256]{2,1,0:T(8,128)(2,1)S(1)} %copy-done, bf16[1,4096,256]{2,1,0:T(8,128)(2,1)S(1)} %copy-done.1, ...), custom_call_target="tpu_custom_call" | custom-call | flops 1024 | bytes 1024 | tf_op jit(solution)/shard_map/pallas_call | solution.py:240
  41.0 4.4 %collective-permute-done.17 = bf16[256,1024]{1,0:T(8,128)(2,1)} collective-permute-done((bf16[256,1024]{1,0:T(8,128)(2,1)}, bf16[256,1024]{1,0:T(8,128)(2,1)}, u32[]{:S(2)}, u32[]{:S(2)}) %collective-permute-start.17) | collective-permute-done | bytes 524320 | tf_op jit(solution)/shard_map/ppermute | solution.py:470
  45.4 10.3 %conditional.6 = (bf16[256,256]{1,0:T(8,128)(2,1)}, bf16[256,256]{1,0:T(8,128)(2,1)}, f32[256,1024]{1,0:T(8,128)S(1)}, bf16[2,256,1024]{2,1,0:T(8,128)(2,1)S(1)}) conditional(s32[]{:T(128)} %convert_element_type.16, () %tuple.54, (bf16[256,1024]{1,0:T(8,128)(2,1)}, f32[256,256]{1,0:T(8,128)S(1)}, f32[256,256]{1,0:T(8,128)S(1)}, ...), branch_computations={%region_8.9_spmd, %region_9.10_spmd} | conditional | flops 3072 | bytes 3673280 | solution.py:547
  51.3 2.8 %collective-permute-done.1 = bf16[256,256]{1,0:T(8,128)(2,1)} collective-permute-done((bf16[256,256]{1,0:T(8,128)(2,1)S(1)}, bf16[256,256]{1,0:T(8,128)(2,1)}, u32[]{:S(2)}, u32[]{:S(2)}) %collective-permute-start.1) | collective-permute-done | bytes 131104 | tf_op jit(solution)/shard_map/cond/branch_1_fun/ppermute | solution.py:470
  54.1 1.7 %collective-permute-done.3 = bf16[256,256]{1,0:T(8,128)(2,1)} collective-permute-done((bf16[256,256]{1,0:T(8,128)(2,1)}, bf16[256,256]{1,0:T(8,128)(2,1)}, u32[]{:S(2)}, u32[]{:S(2)}) %collective-permute-start.3) | collective-permute-done | bytes 131104 | tf_op jit(solution)/shard_map/cond/branch_1_fun/ppermute | solution.py:470
  55.8 2.0 %shard_map.75.refs_0_ = bf16[256,1024]{1,0:T(8,128)(2,1)S(1)} custom-call(s32[2,4]{1,0:T(2,128)S(1)} %get-tuple-element.253.offset_ref, s32[2,4]{1,0:T(2,128)S(1)} %get-tuple-element.254.count_ref, bf16[128,1024]{1,0:T(8,128)(2,1)} %get-tuple-element.205.refs_0_, bf16[128,1024]{1,0:T(8,128)(2,1)S(1)} %collective-permute-done.14.refs_1_, ...), custom_call_target="tpu_custom_call" | custom-call | flops 1024 | bytes 1024 | tf_op jit(solution)/shard_map/pallas_call | solution.py:192
  59.5 3.1 %shard_map.76 = (bf16[128,1024]{1,0:T(8,128)(2,1)S(1)}, bf16[128,1024]{1,0:T(8,128)(2,1)}, bf16[128,1024]{1,0:T(8,128)(2,1)}, bf16[128,1024]{1,0:T(8,128)(2,1)}) custom-call(s32[2,4]{1,0:T(2,128)S(1)} %get-tuple-element.253.offset_ref, s32[2,4]{1,0:T(2,128)S(1)} %get-tuple-element.254.count_ref, f32[256,1024]{1,0:T(8,128)S(1)} %get-tuple-element.211.before_ref, ...), custom_call_target="tpu_custom_call" | custom-call | flops 1024 | bytes 1024 | tf_op jit(solution)/shard_map/pallas_call | solution.py:365
  64.0 3.0 %collective-permute-start.23 = (bf16[128,1024]{1,0:T(8,128)(2,1)}, bf16[128,1024]{1,0:T(8,128)(2,1)}, u32[]{:S(2)}, u32[]{:S(2)}) collective-permute-start(bf16[128,1024]{1,0:T(8,128)(2,1)} %get-tuple-element.218), channel_id=1, source_target_pairs={{0,4},{4,0},{8,12},{12,8},{1,5},{5,1},{9,13},{13,9},{2,6},{6,2},{1... | collective-permute-start | bytes 786440 | tf_op jit(solution)/shard_map/ppermute | solution.py:467
  67.7 1.6 %copy-done.2 = bf16[1,4096,256]{2,1,0:T(8,128)(2,1)S(1)} copy-done((bf16[1,4096,256]{2,1,0:T(8,128)(2,1)S(1)}, bf16[1,4096,256]{2,1,0:T(8,128)(2,1)}, u32[]{:S(2)}) %copy-start.2) | copy-done | bytes 2097176
  69.3 1.8 %shard_map.77 = (f32[256,256]{1,0:T(8,128)S(1)}, f32[256,256]{1,0:T(8,128)S(1)}, bf16[2,1024,256]{2,1,0:T(8,128)(2,1)S(1)}, bf16[2,1024,256]{2,1,0:T(8,128)(2,1)S(1)}) custom-call(s32[4]{0:T(128)S(1)} %pad_add_fusion.order_ref, bf16[1,4096,256]{2,1,0:T(8,128)(2,1)S(1)} %copy-done, bf16[1,4096,256]{2,1,0:T(8,128)(2,1)S(1)} %copy-done.2, ...), custom_call_target="tpu_custom_call" | custom-call | flops 1024 | bytes 1024 | tf_op jit(solution)/shard_map/pallas_call | solution.py:240
  72.3 10.3 %conditional.7 = (bf16[256,256]{1,0:T(8,128)(2,1)}, bf16[256,256]{1,0:T(8,128)(2,1)}, f32[256,1024]{1,0:T(8,128)S(1)}, bf16[2,256,1024]{2,1,0:T(8,128)(2,1)S(1)}) conditional(s32[]{:T(128)} %convert_element_type.17, () %tuple.51, (bf16[256,1024]{1,0:T(8,128)(2,1)}, f32[256,256]{1,0:T(8,128)S(1)}, f32[256,256]{1,0:T(8,128)S(1)}, ...), branch_computations={%region_10.11_spmd, %region_11.12_spmd} | conditional | flops 3072 | bytes 3673280 | solution.py:547
  78.2 2.8 %collective-permute-done.5 = bf16[256,256]{1,0:T(8,128)(2,1)} collective-permute-done((bf16[256,256]{1,0:T(8,128)(2,1)S(1)}, bf16[256,256]{1,0:T(8,128)(2,1)}, u32[]{:S(2)}, u32[]{:S(2)}) %collective-permute-start.5) | collective-permute-done | bytes 131104 | tf_op jit(solution)/shard_map/cond/branch_1_fun/ppermute | solution.py:470
  81.0 1.7 %collective-permute-done.7 = bf16[256,256]{1,0:T(8,128)(2,1)} collective-permute-done((bf16[256,256]{1,0:T(8,128)(2,1)}, bf16[256,256]{1,0:T(8,128)(2,1)}, u32[]{:S(2)}, u32[]{:S(2)}) %collective-permute-start.7) | collective-permute-done | bytes 131104 | tf_op jit(solution)/shard_map/cond/branch_1_fun/ppermute | solution.py:470
  82.7 2.4 %shard_map.78 = (bf16[128,1024]{1,0:T(8,128)(2,1)S(1)}, bf16[128,1024]{1,0:T(8,128)(2,1)S(1)}, bf16[128,1024]{1,0:T(8,128)(2,1)S(1)}, bf16[128,1024]{1,0:T(8,128)(2,1)S(1)}) custom-call(s32[2,4]{1,0:T(2,128)S(1)} %get-tuple-element.253.offset_ref, s32[2,4]{1,0:T(2,128)S(1)} %get-tuple-element.254.count_ref, f32[256,1024]{1,0:T(8,128)S(1)} %get-tuple-element.230.before_ref, ...), custom_call_target="tpu_custom_call" | custom-call | flops 1024 | bytes 1024 | tf_op jit(solution)/shard_map/pallas_call | solution.py:365
  85.1 3.3 %collective-permute-done.22.refs_2_ = bf16[128,1024]{1,0:T(8,128)(2,1)} collective-permute-done((bf16[128,1024]{1,0:T(8,128)(2,1)}, bf16[128,1024]{1,0:T(8,128)(2,1)}, u32[]{:S(2)}, u32[]{:S(2)}) %collective-permute-start.22) | collective-permute-done | bytes 262176 | tf_op jit(solution)/shard_map/ppermute | solution.py:467
  88.3 2.1 %collective-permute-start.26 = (bf16[128,1024]{1,0:T(8,128)(2,1)S(1)}, bf16[128,1024]{1,0:T(8,128)(2,1)S(1)}, u32[]{:S(2)}, u32[]{:S(2)}) collective-permute-start(bf16[128,1024]{1,0:T(8,128)(2,1)S(1)} %get-tuple-element.247), channel_id=1, source_target_pairs={{0,12},{4,8},{8,4},{12,0},{1,13},{5,9},{9,5},{13,1},{2,14},{6,10},... | collective-permute-start | bytes 786440 | tf_op jit(solution)/shard_map/ppermute | solution.py:467
  90.4 2.4 %collective-permute-start.27 = (bf16[128,1024]{1,0:T(8,128)(2,1)S(1)}, bf16[128,1024]{1,0:T(8,128)(2,1)S(1)}, u32[]{:S(2)}, u32[]{:S(2)}) collective-permute-start(bf16[128,1024]{1,0:T(8,128)(2,1)S(1)} %get-tuple-element.248), channel_id=1, source_target_pairs={{0,4},{4,0},{8,12},{12,8},{1,5},{5,1},{9,13},{13,9},{2,6},{6,2},{1... | collective-permute-start | bytes 786440 | tf_op jit(solution)/shard_map/ppermute | solution.py:467
  93.9 1.9 %shard_map.80.refs_0_ = f32[512,1024]{1,0:T(8,128)S(1)} custom-call(s32[4,512]{1,0:T(4,128)S(1)} %get-tuple-element.175.code_ref, f32[4,512]{1,0:T(4,128)S(1)} %shard_map.79.weight_ref, bf16[128,1024]{1,0:T(8,128)(2,1)S(1)} %get-tuple-element.241.refs_0_, bf16[128,1024]{1,0:T(8,128)(2,1)} %collective-permute-done.21.refs_1_, ...), custom_call_target="tpu_custom_call" | custom-call | flops 1024 | bytes 1024 | tf_op jit(solution)/shard_map/pallas_call | solution.py:440
  95.8 10.3 %collective-permute-done.25.refs_2_ = bf16[128,1024]{1,0:T(8,128)(2,1)S(1)} collective-permute-done((bf16[128,1024]{1,0:T(8,128)(2,1)S(1)}, bf16[128,1024]{1,0:T(8,128)(2,1)S(1)}, u32[]{:S(2)}, u32[]{:S(2)}) %collective-permute-start.25) | collective-permute-done | bytes 262176 | tf_op jit(solution)/shard_map/ppermute | solution.py:467
  106.6 6.7 %collective-permute-done.26.refs_1_ = bf16[128,1024]{1,0:T(8,128)(2,1)S(1)} collective-permute-done((bf16[128,1024]{1,0:T(8,128)(2,1)S(1)}, bf16[128,1024]{1,0:T(8,128)(2,1)S(1)}, u32[]{:S(2)}, u32[]{:S(2)}) %collective-permute-start.26) | collective-permute-done | bytes 262176 | tf_op jit(solution)/shard_map/ppermute | solution.py:467
  (68 shorter events, 29.2 us)
Async XLA Ops:
  2.6 21.7 %collective-permute-start.11 = (bf16[128,1024]{1,0:T(8,128)(2,1)}, bf16[128,1024]{1,0:T(8,128)(2,1)S(1)}, u32[]{:S(2)}, u32[]{:S(2)}) collective-permute-start(bf16[128,1024]{1,0:T(8,128)(2,1)} %get-tuple-element.182), channel_id=1, source_target_pairs={{0,8},{4,12},{8,0},{12,4},{1,9},{5,13},{9,1},{13,5},{2,10},{6,14},... | collective-permute-start | bytes 786440 | tf_op jit(solution)/shard_map/ppermute | solution.py:467
  2.7 26.0 %collective-permute-start.12 = (bf16[128,1024]{1,0:T(8,128)(2,1)}, bf16[128,1024]{1,0:T(8,128)(2,1)S(1)}, u32[]{:S(2)}, u32[]{:S(2)}) collective-permute-start(bf16[128,1024]{1,0:T(8,128)(2,1)} %get-tuple-element.183), channel_id=1, source_target_pairs={{0,12},{4,8},{8,4},{12,0},{1,13},{5,9},{9,5},{13,1},{2,14},{6,10},... | collective-permute-start | bytes 786440 | tf_op jit(solution)/shard_map/ppermute | solution.py:467
  5.7 23.0 %collective-permute-start.13 = (bf16[128,1024]{1,0:T(8,128)(2,1)}, bf16[128,1024]{1,0:T(8,128)(2,1)S(1)}, u32[]{:S(2)}, u32[]{:S(2)}) collective-permute-start(bf16[128,1024]{1,0:T(8,128)(2,1)} %get-tuple-element.184), channel_id=1, source_target_pairs={{0,4},{4,0},{8,12},{12,8},{1,5},{5,1},{9,13},{13,9},{2,6},{6,2},{1... | collective-permute-start | bytes 786440 | tf_op jit(solution)/shard_map/ppermute | solution.py:467
  9.9 26.9 %copy-start = (bf16[1,4096,256]{2,1,0:T(8,128)(2,1)S(1)}, bf16[1,4096,256]{2,1,0:T(8,128)(2,1)}, u32[]{:S(2)}) copy-start(bf16[1,4096,256]{2,1,0:T(8,128)(2,1)} %gate_ref.3) | copy-start | bytes 6291460
  11.7 3.7 %collective-permute-start.8 = (f32[4,512]{1,0:T(4,128)S(1)}, f32[4,512]{1,0:T(4,128)S(1)}, u32[]{:S(2)}, u32[]{:S(2)}) collective-permute-start(f32[4,512]{1,0:T(4,128)S(1)} %branch_1_fun.10), channel_id=1, source_target_pairs={{0,2},{1,3},{2,0},{3,1},{4,6},{5,7},{6,4},{7,5},{8,10},{9,11},{10,... | collective-permute-start | bytes 24584 | tf_op jit(solution)/shard_map/cond/branch_1_fun/ppermute | solution.py:470
  15.4 1.2 %collective-permute-start.9 = (f32[4,512]{1,0:T(4,128)S(1)}, f32[4,512]{1,0:T(4,128)S(1)}, u32[]{:S(2)}, u32[]{:S(2)}) collective-permute-start(f32[4,512]{1,0:T(4,128)S(1)} %add.24), channel_id=1, source_target_pairs={{0,1},{1,0},{2,3},{3,2},{4,5},{5,4},{6,7},{7,6},{8,9},{9,8},{10,11... | collective-permute-start | bytes 24584 | tf_op jit(solution)/shard_map/cond/branch_1_fun/ppermute | solution.py:470
  17.1 6.5 %collective-permute-start.10 = (f32[1,4,512]{2,1,0:T(4,128)}, f32[1,4,512]{2,1,0:T(4,128)S(1)}, u32[]{:S(2)}, u32[]{:S(2)}) collective-permute-start(f32[1,4,512]{2,1,0:T(4,128)} %bitcast), channel_id=1, source_target_pairs={{0,4},{4,0},{8,12},{12,8},{1,5},{5,1},{9,13},{13,9},{2,6},{6,2},{1... | collective-permute-start | bytes 24584 | tf_op jit(solution)/shard_map/cond/branch_1_fun/ppermute | solution.py:467
  30.7 6.1 %collective-permute-start.18 = (bf16[256,1024]{1,0:T(8,128)(2,1)}, bf16[256,1024]{1,0:T(8,128)(2,1)S(1)}, u32[]{:S(2)}, u32[]{:S(2)}) collective-permute-start(bf16[256,1024]{1,0:T(8,128)(2,1)} %get-tuple-element.287.refs_0_), channel_id=1, source_target_pairs={{0,1},{1,0},{2,3},{3,2},{4,5},{5,4},{6,7},{7,6},{8,9},{9,8},{10,11... | collective-permute-start | bytes 1572872 | tf_op jit(solution)/shard_map/ppermute | solution.py:470
  30.8 14.7 %collective-permute-start.17 = (bf16[256,1024]{1,0:T(8,128)(2,1)}, bf16[256,1024]{1,0:T(8,128)(2,1)}, u32[]{:S(2)}, u32[]{:S(2)}) collective-permute-start(bf16[256,1024]{1,0:T(8,128)(2,1)} %get-tuple-element.287.refs_0_), channel_id=1, source_target_pairs={{0,2},{1,3},{2,0},{3,1},{4,6},{5,7},{6,4},{7,5},{8,10},{9,11},{10,... | collective-permute-start | bytes 1572872 | tf_op jit(solution)/shard_map/ppermute | solution.py:470
  32.3 23.5 %collective-permute-start.14 = (bf16[128,1024]{1,0:T(8,128)(2,1)}, bf16[128,1024]{1,0:T(8,128)(2,1)S(1)}, u32[]{:S(2)}, u32[]{:S(2)}) collective-permute-start(bf16[128,1024]{1,0:T(8,128)(2,1)} %get-tuple-element.191), channel_id=1, source_target_pairs={{0,8},{4,12},{8,0},{12,4},{1,9},{5,13},{9,1},{13,5},{2,10},{6,14},... | collective-permute-start | bytes 786440 | tf_op jit(solution)/shard_map/ppermute | solution.py:467
  32.3 23.5 %collective-permute-start.15 = (bf16[128,1024]{1,0:T(8,128)(2,1)}, bf16[128,1024]{1,0:T(8,128)(2,1)S(1)}, u32[]{:S(2)}, u32[]{:S(2)}) collective-permute-start(bf16[128,1024]{1,0:T(8,128)(2,1)} %get-tuple-element.192), channel_id=1, source_target_pairs={{0,12},{4,8},{8,4},{12,0},{1,13},{5,9},{9,5},{13,1},{2,14},{6,10},... | collective-permute-start | bytes 786440 | tf_op jit(solution)/shard_map/ppermute | solution.py:467
  32.3 23.5 %collective-permute-start.16 = (bf16[128,1024]{1,0:T(8,128)(2,1)}, bf16[128,1024]{1,0:T(8,128)(2,1)S(1)}, u32[]{:S(2)}, u32[]{:S(2)}) collective-permute-start(bf16[128,1024]{1,0:T(8,128)(2,1)} %get-tuple-element.193), channel_id=1, source_target_pairs={{0,4},{4,0},{8,12},{12,8},{1,5},{5,1},{9,13},{13,9},{2,6},{6,2},{1... | collective-permute-start | bytes 786440 | tf_op jit(solution)/shard_map/ppermute | solution.py:467
  36.8 1.6 %copy-start.1 = (bf16[1,4096,256]{2,1,0:T(8,128)(2,1)S(1)}, bf16[1,4096,256]{2,1,0:T(8,128)(2,1)}, u32[]{:S(2)}) copy-start(bf16[1,4096,256]{2,1,0:T(8,128)(2,1)} %up_ref.3) | copy-start | bytes 6291460
  38.4 7.0 %copy-start.3 = (bf16[1,1024,1024]{2,1,0:T(8,128)(2,1)S(1)}, bf16[1,1024,1024]{2,1,0:T(8,128)(2,1)}, u32[]{:S(2)}) copy-start(bf16[1,1024,1024]{2,1,0:T(8,128)(2,1)} %param.19) | copy-start | bytes 6291460
  45.4 2.1 %collective-permute-start = (bf16[256,1024]{1,0:T(8,128)(2,1)}, bf16[256,1024]{1,0:T(8,128)(2,1)S(1)}, u32[]{:S(2)}, u32[]{:S(2)}) collective-permute-start(bf16[256,1024]{1,0:T(8,128)(2,1)} %get-tuple-element.67.refs_0_), channel_id=1, source_target_pairs={{0,1},{1,0},{2,3},{3,2},{4,5},{5,4},{6,7},{7,6},{8,9},{9,8},{10,11... | collective-permute-start | bytes 1572872 | tf_op jit(solution)/shard_map/cond/branch_1_fun/ppermute | solution.py:470
  48.0 1.7 %collective-permute-start.2 = (bf16[256,256]{1,0:T(8,128)(2,1)S(1)}, bf16[256,256]{1,0:T(8,128)(2,1)S(1)}, u32[]{:S(2)}, u32[]{:S(2)}) collective-permute-start(bf16[256,256]{1,0:T(8,128)(2,1)S(1)} %branch_1_fun.13.refs_0_), channel_id=1, source_target_pairs={{0,1},{1,0},{2,3},{3,2},{4,5},{5,4},{6,7},{7,6},{8,9},{9,8},{10,11... | collective-permute-start | bytes 393224 | tf_op jit(solution)/shard_map/cond/branch_1_fun/ppermute | solution.py:470
  48.2 5.9 %collective-permute-start.1 = (bf16[256,256]{1,0:T(8,128)(2,1)S(1)}, bf16[256,256]{1,0:T(8,128)(2,1)}, u32[]{:S(2)}, u32[]{:S(2)}) collective-permute-start(bf16[256,256]{1,0:T(8,128)(2,1)S(1)} %branch_1_fun.13.refs_0_), channel_id=1, source_target_pairs={{0,2},{1,3},{2,0},{3,1},{4,6},{5,7},{6,4},{7,5},{8,10},{9,11},{10,... | collective-permute-start | bytes 393224 | tf_op jit(solution)/shard_map/cond/branch_1_fun/ppermute | solution.py:470
  54.1 1.7 %collective-permute-start.3 = (bf16[256,256]{1,0:T(8,128)(2,1)}, bf16[256,256]{1,0:T(8,128)(2,1)}, u32[]{:S(2)}, u32[]{:S(2)}) collective-permute-start(bf16[256,256]{1,0:T(8,128)(2,1)} %collective-permute-done.1), channel_id=1, source_target_pairs={{0,1},{1,0},{2,3},{3,2},{4,5},{5,4},{6,7},{7,6},{8,9},{9,8},{10,11... | collective-permute-start | bytes 393224 | tf_op jit(solution)/shard_map/cond/branch_1_fun/ppermute | solution.py:470
  57.8 9.9 %collective-permute-start.20 = (bf16[256,1024]{1,0:T(8,128)(2,1)S(1)}, bf16[256,1024]{1,0:T(8,128)(2,1)S(1)}, u32[]{:S(2)}, u32[]{:S(2)}) collective-permute-start(bf16[256,1024]{1,0:T(8,128)(2,1)S(1)} %shard_map.75.refs_0_), channel_id=1, source_target_pairs={{0,1},{1,0},{2,3},{3,2},{4,5},{5,4},{6,7},{7,6},{8,9},{9,8},{10,11... | collective-permute-start | bytes 1572872 | tf_op jit(solution)/shard_map/ppermute | solution.py:470
  58.0 14.3 %collective-permute-start.19 = (bf16[256,1024]{1,0:T(8,128)(2,1)S(1)}, bf16[256,1024]{1,0:T(8,128)(2,1)}, u32[]{:S(2)}, u32[]{:S(2)}) collective-permute-start(bf16[256,1024]{1,0:T(8,128)(2,1)S(1)} %shard_map.75.refs_0_), channel_id=1, source_target_pairs={{0,2},{1,3},{2,0},{3,1},{4,6},{5,7},{6,4},{7,5},{8,10},{9,11},{10,... | collective-permute-start | bytes 1572872 | tf_op jit(solution)/shard_map/ppermute | solution.py:470
  62.6 22.4 %collective-permute-start.21 = (bf16[128,1024]{1,0:T(8,128)(2,1)}, bf16[128,1024]{1,0:T(8,128)(2,1)}, u32[]{:S(2)}, u32[]{:S(2)}) collective-permute-start(bf16[128,1024]{1,0:T(8,128)(2,1)} %get-tuple-element.216), channel_id=1, source_target_pairs={{0,8},{4,12},{8,0},{12,4},{1,9},{5,13},{9,1},{13,5},{2,10},{6,14},... | collective-permute-start | bytes 786440 | tf_op jit(solution)/shard_map/ppermute | solution.py:467
  62.7 25.6 %collective-permute-start.22 = (bf16[128,1024]{1,0:T(8,128)(2,1)}, bf16[128,1024]{1,0:T(8,128)(2,1)}, u32[]{:S(2)}, u32[]{:S(2)}) collective-permute-start(bf16[128,1024]{1,0:T(8,128)(2,1)} %get-tuple-element.217), channel_id=1, source_target_pairs={{0,12},{4,8},{8,4},{12,0},{1,13},{5,9},{9,5},{13,1},{2,14},{6,10},... | collective-permute-start | bytes 786440 | tf_op jit(solution)/shard_map/ppermute | solution.py:467
  64.0 24.3 %collective-permute-start.23 = (bf16[128,1024]{1,0:T(8,128)(2,1)}, bf16[128,1024]{1,0:T(8,128)(2,1)}, u32[]{:S(2)}, u32[]{:S(2)}) collective-permute-start(bf16[128,1024]{1,0:T(8,128)(2,1)} %get-tuple-element.218), channel_id=1, source_target_pairs={{0,4},{4,0},{8,12},{12,8},{1,5},{5,1},{9,13},{13,9},{2,6},{6,2},{1... | collective-permute-start | bytes 786440 | tf_op jit(solution)/shard_map/ppermute | solution.py:467
  69.3 3.0 %copy-start.4 = (bf16[1,1024,1024]{2,1,0:T(8,128)(2,1)S(1)}, bf16[1,1024,1024]{2,1,0:T(8,128)(2,1)}, u32[]{:S(2)}) copy-start(bf16[1,1024,1024]{2,1,0:T(8,128)(2,1)} %param.19) | copy-start | bytes 6291460
  72.3 2.1 %collective-permute-start.4 = (bf16[256,1024]{1,0:T(8,128)(2,1)}, bf16[256,1024]{1,0:T(8,128)(2,1)S(1)}, u32[]{:S(2)}, u32[]{:S(2)}) collective-permute-start(bf16[256,1024]{1,0:T(8,128)(2,1)} %get-tuple-element.84.refs_0_), channel_id=1, source_target_pairs={{0,1},{1,0},{2,3},{3,2},{4,5},{5,4},{6,7},{7,6},{8,9},{9,8},{10,11... | collective-permute-start | bytes 1572872 | tf_op jit(solution)/shard_map/cond/branch_1_fun/ppermute | solution.py:470
  74.9 1.7 %collective-permute-start.6 = (bf16[256,256]{1,0:T(8,128)(2,1)S(1)}, bf16[256,256]{1,0:T(8,128)(2,1)S(1)}, u32[]{:S(2)}, u32[]{:S(2)}) collective-permute-start(bf16[256,256]{1,0:T(8,128)(2,1)S(1)} %branch_1_fun.16.refs_0_), channel_id=1, source_target_pairs={{0,1},{1,0},{2,3},{3,2},{4,5},{5,4},{6,7},{7,6},{8,9},{9,8},{10,11... | collective-permute-start | bytes 393224 | tf_op jit(solution)/shard_map/cond/branch_1_fun/ppermute | solution.py:470
  75.1 5.9 %collective-permute-start.5 = (bf16[256,256]{1,0:T(8,128)(2,1)S(1)}, bf16[256,256]{1,0:T(8,128)(2,1)}, u32[]{:S(2)}, u32[]{:S(2)}) collective-permute-start(bf16[256,256]{1,0:T(8,128)(2,1)S(1)} %branch_1_fun.16.refs_0_), channel_id=1, source_target_pairs={{0,2},{1,3},{2,0},{3,1},{4,6},{5,7},{6,4},{7,5},{8,10},{9,11},{10,... | collective-permute-start | bytes 393224 | tf_op jit(solution)/shard_map/cond/branch_1_fun/ppermute | solution.py:470
  81.0 1.7 %collective-permute-start.7 = (bf16[256,256]{1,0:T(8,128)(2,1)}, bf16[256,256]{1,0:T(8,128)(2,1)}, u32[]{:S(2)}, u32[]{:S(2)}) collective-permute-start(bf16[256,256]{1,0:T(8,128)(2,1)} %collective-permute-done.5), channel_id=1, source_target_pairs={{0,1},{1,0},{2,3},{3,2},{4,5},{5,4},{6,7},{7,6},{8,9},{9,8},{10,11... | collective-permute-start | bytes 393224 | tf_op jit(solution)/shard_map/cond/branch_1_fun/ppermute | solution.py:470
  82.7 7.7 %collective-permute-start.24 = (f32[2,4,512]{2,1,0:T(4,128)S(1)}, f32[2,4,512]{2,1,0:T(4,128)S(1)}, u32[]{:S(2)}, u32[]{:S(2)}) collective-permute-start(f32[2,4,512]{2,1,0:T(4,128)S(1)} %get-tuple-element.239), channel_id=1, source_target_pairs={{0,8},{4,12},{8,0},{12,4},{1,9},{5,13},{9,1},{13,5},{2,10},{6,14},... | collective-permute-start | bytes 49160 | tf_op jit(solution)/shard_map/ppermute | solution.py:467
  88.3 17.7 %collective-permute-start.25 = (bf16[128,1024]{1,0:T(8,128)(2,1)S(1)}, bf16[128,1024]{1,0:T(8,128)(2,1)S(1)}, u32[]{:S(2)}, u32[]{:S(2)}) collective-permute-start(bf16[128,1024]{1,0:T(8,128)(2,1)S(1)} %get-tuple-element.246), channel_id=1, source_target_pairs={{0,8},{4,12},{8,0},{12,4},{1,9},{5,13},{9,1},{13,5},{2,10},{6,14},... | collective-permute-start | bytes 786440 | tf_op jit(solution)/shard_map/ppermute | solution.py:467
  88.3 25.0 %collective-permute-start.26 = (bf16[128,1024]{1,0:T(8,128)(2,1)S(1)}, bf16[128,1024]{1,0:T(8,128)(2,1)S(1)}, u32[]{:S(2)}, u32[]{:S(2)}) collective-permute-start(bf16[128,1024]{1,0:T(8,128)(2,1)S(1)} %get-tuple-element.247), channel_id=1, source_target_pairs={{0,12},{4,8},{8,4},{12,0},{1,13},{5,9},{9,5},{13,1},{2,14},{6,10},... | collective-permute-start | bytes 786440 | tf_op jit(solution)/shard_map/ppermute | solution.py:467
  90.4 22.9 %collective-permute-start.27 = (bf16[128,1024]{1,0:T(8,128)(2,1)S(1)}, bf16[128,1024]{1,0:T(8,128)(2,1)S(1)}, u32[]{:S(2)}, u32[]{:S(2)}) collective-permute-start(bf16[128,1024]{1,0:T(8,128)(2,1)S(1)} %get-tuple-element.248), channel_id=1, source_target_pairs={{0,4},{4,0},{8,12},{12,8},{1,5},{5,1},{9,13},{13,9},{2,6},{6,2},{1... | collective-permute-start | bytes 786440 | tf_op jit(solution)/shard_map/ppermute | solution.py:467
  (1 other events, 1.6 us)

commit v19 on v18

--- a/solution.py
+++ b/solution.py
@@ -582,9 +582,10 @@
     total = None
     for k in range(BATCHES - 1):
         total = combine(code, weights, k, range(experts), waiting[k], total, False)
-    early = range(experts // 2)
+    late = (min(2, experts - 1),)
+    early = [i for i in range(experts) if i not in late]
     total = combine(code, weights, BATCHES - 1, early, waiting[-1], total, False)
-    return combine(code, weights, BATCHES - 1, range(experts // 2, experts), waiting[-1], total, True)
+    return combine(code, weights, BATCHES - 1, late, waiting[-1], total, True)
 
 
 def solution(mesh):

time: 116 us -> 116 us (level)
  transfers between devices with their start and end apart: 28 -> 28, of which waited for: 15 -> 16; matrix products, arithmetic and copies ran while one was open for 3% -> 3% of each run, Pallas kernels for 22% -> 22%
where the time goes in v19:
time: 116 us; the launch traced here: 115 us
  waiting for transfers between devices  47.5 us (41%)
  Pallas kernels  33.2 us (29%)
  starting transfers between devices  25.8 us (22%)
  local copies, waits for them, and re-layouts  3.89 us (3%)
  other arithmetic  2.93 us (3%)
  between operations  1.55 us (1%)
    ppermute x14, waiting for transfers between devices, along_expert(): return lax.ppermute(x, 'expert', [(i, i ^ shift) for i in range(experts)])  28.3 us
    ppermute x14, waiting for transfers between devices, swap(): return lax.ppermute(x, 'dp', [(i, i ^ bit) for i in range(width_parts)])  19.2 us
    ppermute x14, starting transfers between devices, along_expert(): return lax.ppermute(x, 'expert', [(i, i ^ shift) for i in range(experts)])  17.5 us
    ppermute x14, starting transfers between devices, swap(): return lax.ppermute(x, 'dp', [(i, i ^ bit) for i in range(width_parts)])  8.27 us
    pallas_call x2, Pallas kernels, down_last(): pl.pallas_call(functools.partial(down_last_kernel, parts, experts, k, dir...  5.47 us
    pallas_call x2, Pallas kernels, gate_up_near(): pl.pallas_call(functools.partial(gate_up_near_kernel, parts, near, far),...  4.4 us
    pallas_call x3, Pallas kernels, combine(): pl.pallas_call(functools.partial(combine_kernel, places, k, len(more)), o...  4.29 us
    pallas_call x2, Pallas kernels, compact(): pl.pallas_call(functools.partial(compact_kernel, experts, k), out_shape=j...  3.94 us
  transfers between devices with their start and end apart: 28, of which 16 were waited for; matrix products, arithmetic and copies ran while one was open for 3% of the time, Pallas kernels for 22%

profile of v19, /device:TPU:16, one launch (start us, length us, event | category | flops | bytes accessed | tf_op | source)
XLA Modules:
  0.0 114.9 jit_solution(6285836051070490893)
XLA Ops:
  0.0 2.6 %shard_map.73 = (s32[4,512]{1,0:T(4,128)S(1)}, bf16[128,1024]{1,0:T(8,128)(2,1)S(1)}, bf16[128,1024]{1,0:T(8,128)(2,1)}, bf16[128,1024]{1,0:T(8,128)(2,1)}, bf16[128,1024]{1,0:T(8,128)(2,1)}) custom-call(s32[1]{0:T(128)} %bitcast.1.place_ref, s32[4,512]{1,0:T(4,128)} %picks_in.1, bf16[512,1024]{1,0:T(8,128)(2,1)} %tokens_ref.1), custom_call_target="tpu_custom_call" | custom-call | flops 1024 | bytes 1024 | tf_op jit(solution)/shard_map/pallas_call | solution.py:108
  2.7 3.0 %collective-permute-start.12 = (bf16[128,1024]{1,0:T(8,128)(2,1)}, bf16[128,1024]{1,0:T(8,128)(2,1)S(1)}, u32[]{:S(2)}, u32[]{:S(2)}) collective-permute-start(bf16[128,1024]{1,0:T(8,128)(2,1)} %get-tuple-element.183), channel_id=1, source_target_pairs={{0,12},{4,8},{8,4},{12,0},{1,13},{5,9},{9,5},{13,1},{2,14},{6,10},... | collective-permute-start | bytes 786440 | tf_op jit(solution)/shard_map/ppermute | solution.py:467
  9.9 14.4 %conditional.4 = (bf16[128,1024]{1,0:T(8,128)(2,1)}, bf16[128,1024]{1,0:T(8,128)(2,1)}, bf16[128,1024]{1,0:T(8,128)(2,1)}, bf16[128,1024]{1,0:T(8,128)(2,1)}, f3...) conditional(s32[]{:T(128)} %convert_element_type.16, () %tuple.49, (s32[4,512]{1,0:T(4,128)S(1)}, ...), branch_computations={%region_3.4_spmd, %region_4.5_spmd} | conditional | flops 10240 | bytes 1073216 | solution.py:525
  9.9 1.8 %branch_1_fun.10 = f32[4,512]{1,0:T(4,128)S(1)} custom-call(bf16[4,1024]{1,0:T(4,128)(2,1)} %get-tuple-element.60.router_ref, bf16[512,1024]{1,0:T(8,128)(2,1)} %get-tuple-element.55.tokens_ref), custom_call_target="tpu_custom_call" | custom-call | flops 1024 | bytes 1024 | tf_op jit(solution)/shard_map/cond/branch_1_fun/pallas_call | solution.py:134
  13.2 2.2 %collective-permute-done.8 = f32[4,512]{1,0:T(4,128)S(1)} collective-permute-done((f32[4,512]{1,0:T(4,128)S(1)}, f32[4,512]{1,0:T(4,128)S(1)}, u32[]{:S(2)}, u32[]{:S(2)}) %collective-permute-start.8) | collective-permute-done | bytes 8224 | tf_op jit(solution)/shard_map/cond/branch_1_fun/ppermute | solution.py:470
  17.8 2.7 %branch_1_fun.9 = (bf16[128,1024]{1,0:T(8,128)(2,1)}, bf16[128,1024]{1,0:T(8,128)(2,1)}, bf16[128,1024]{1,0:T(8,128)(2,1)}, bf16[128,1024]{1,0:T(8,128)(2,1)}) custom-call(s32[4,512]{1,0:T(4,128)S(1)} %get-tuple-element.54.code_ref, bf16[512,1024]{1,0:T(8,128)(2,1)} %get-tuple-element.55.tokens_ref), custom_call_target="tpu_custom_call" | custom-call | flops 1024 | bytes 1024 | tf_op jit(solution)/shard_map/cond/branch_1_fun/pallas_call | solution.py:155
  20.5 3.1 %collective-permute-done.10 = f32[1,4,512]{2,1,0:T(4,128)S(1)} collective-permute-done((f32[1,4,512]{2,1,0:T(4,128)}, f32[1,4,512]{2,1,0:T(4,128)S(1)}, u32[]{:S(2)}, u32[]{:S(2)}) %collective-permute-start.10) | collective-permute-done | bytes 8224 | tf_op jit(solution)/shard_map/cond/branch_1_fun/ppermute | solution.py:467
  24.3 4.4 %collective-permute-done.12 = bf16[128,1024]{1,0:T(8,128)(2,1)S(1)} collective-permute-done((bf16[128,1024]{1,0:T(8,128)(2,1)}, bf16[128,1024]{1,0:T(8,128)(2,1)S(1)}, u32[]{:S(2)}, u32[]{:S(2)}) %collective-permute-start.12) | collective-permute-done | bytes 262176 | tf_op jit(solution)/shard_map/ppermute | solution.py:467
  28.7 2.0 %conditional.5 = (bf16[256,1024]{1,0:T(8,128)(2,1)}) conditional(s32[]{:T(128)} %convert_element_type.16, () %tuple.55, (s32[2,4]{1,0:T(2,128)S(1)}, s32[2,4]{1,0:T(2,128)S(1)}, bf16[128,1024]{1,0:T(8,128)(2,1)S(1)}, bf16[128,1024]{1,0:T(8,128)(2,1)S(1)}, bf16[128,1024]{1,0:T(8,128)(2,1)S(1)}, /*index=5*/bf16[128,1024]{1,0:T(8,128)(2,1)S(1)}) %tuple.56), branch_computations={%region_6.7_spmd, %region_7.8_spmd} | conditional | flops 1024 | bytes 524298 | solution.py:547
  28.7 1.9 %branch_1_fun.11 = bf16[256,1024]{1,0:T(8,128)(2,1)} custom-call(s32[2,4]{1,0:T(2,128)S(1)} %get-tuple-element.61.offset_ref, s32[2,4]{1,0:T(2,128)S(1)} %get-tuple-element.62.count_ref, bf16[128,1024]{1,0:T(8,128)(2,1)S(1)} %get-tuple-element.63.refs_0_, bf16[128,1024]{1,0:T(8,128)(2,1)S(1)} %get-tuple-element.64.refs_1_, ...), custom_call_target="tpu_custom_call" | custom-call | flops 1024 | bytes 1024 | tf_op jit(solution)/shard_map/cond/branch_1_fun/pallas_call | solution.py:192
  32.3 4.4 %collective-permute-start.16 = (bf16[128,1024]{1,0:T(8,128)(2,1)}, bf16[128,1024]{1,0:T(8,128)(2,1)S(1)}, u32[]{:S(2)}, u32[]{:S(2)}) collective-permute-start(bf16[128,1024]{1,0:T(8,128)(2,1)} %get-tuple-element.193), channel_id=1, source_target_pairs={{0,4},{4,0},{8,12},{12,8},{1,5},{5,1},{9,13},{13,9},{2,6},{6,2},{1... | collective-permute-start | bytes 786440 | tf_op jit(solution)/shard_map/ppermute | solution.py:467
  36.8 1.6 %copy-done.1 = bf16[1,4096,256]{2,1,0:T(8,128)(2,1)S(1)} copy-done((bf16[1,4096,256]{2,1,0:T(8,128)(2,1)S(1)}, bf16[1,4096,256]{2,1,0:T(8,128)(2,1)}, u32[]{:S(2)}) %copy-start.1) | copy-done | bytes 2097176
  38.4 2.6 %shard_map.74 = (f32[256,256]{1,0:T(8,128)S(1)}, f32[256,256]{1,0:T(8,128)S(1)}, bf16[2,1024,256]{2,1,0:T(8,128)(2,1)S(1)}, bf16[2,1024,256]{2,1,0:T(8,128)(2,1)S(1)}) custom-call(s32[4]{0:T(128)S(1)} %pad_add_fusion.order_ref, bf16[1,4096,256]{2,1,0:T(8,128)(2,1)S(1)} %copy-done, bf16[1,4096,256]{2,1,0:T(8,128)(2,1)S(1)} %copy-done.1, ...), custom_call_target="tpu_custom_call" | custom-call | flops 1024 | bytes 1024 | tf_op jit(solution)/shard_map/pallas_call | solution.py:240
  41.0 4.4 %collective-permute-done.17 = bf16[256,1024]{1,0:T(8,128)(2,1)} collective-permute-done((bf16[256,1024]{1,0:T(8,128)(2,1)}, bf16[256,1024]{1,0:T(8,128)(2,1)}, u32[]{:S(2)}, u32[]{:S(2)}) %collective-permute-start.17) | collective-permute-done | bytes 524320 | tf_op jit(solution)/shard_map/ppermute | solution.py:470
  45.4 10.3 %conditional.6 = (bf16[256,256]{1,0:T(8,128)(2,1)}, bf16[256,256]{1,0:T(8,128)(2,1)}, f32[256,1024]{1,0:T(8,128)S(1)}, bf16[2,256,1024]{2,1,0:T(8,128)(2,1)S(1)}) conditional(s32[]{:T(128)} %convert_element_type.16, () %tuple.54, (bf16[256,1024]{1,0:T(8,128)(2,1)}, f32[256,256]{1,0:T(8,128)S(1)}, f32[256,256]{1,0:T(8,128)S(1)}, ...), branch_computations={%region_8.9_spmd, %region_9.10_spmd} | conditional | flops 3072 | bytes 3673280 | solution.py:547
  51.3 2.8 %collective-permute-done.1 = bf16[256,256]{1,0:T(8,128)(2,1)} collective-permute-done((bf16[256,256]{1,0:T(8,128)(2,1)S(1)}, bf16[256,256]{1,0:T(8,128)(2,1)}, u32[]{:S(2)}, u32[]{:S(2)}) %collective-permute-start.1) | collective-permute-done | bytes 131104 | tf_op jit(solution)/shard_map/cond/branch_1_fun/ppermute | solution.py:470
  54.1 1.7 %collective-permute-done.3 = bf16[256,256]{1,0:T(8,128)(2,1)} collective-permute-done((bf16[256,256]{1,0:T(8,128)(2,1)}, bf16[256,256]{1,0:T(8,128)(2,1)}, u32[]{:S(2)}, u32[]{:S(2)}) %collective-permute-start.3) | collective-permute-done | bytes 131104 | tf_op jit(solution)/shard_map/cond/branch_1_fun/ppermute | solution.py:470
  55.8 2.0 %shard_map.75.refs_0_ = bf16[256,1024]{1,0:T(8,128)(2,1)S(1)} custom-call(s32[2,4]{1,0:T(2,128)S(1)} %get-tuple-element.253.offset_ref, s32[2,4]{1,0:T(2,128)S(1)} %get-tuple-element.254.count_ref, bf16[128,1024]{1,0:T(8,128)(2,1)} %get-tuple-element.205.refs_0_, bf16[128,1024]{1,0:T(8,128)(2,1)S(1)} %collective-permute-done.14.refs_1_, ...), custom_call_target="tpu_custom_call" | custom-call | flops 1024 | bytes 1024 | tf_op jit(solution)/shard_map/pallas_call | solution.py:192
  59.5 3.1 %shard_map.76 = (bf16[128,1024]{1,0:T(8,128)(2,1)S(1)}, bf16[128,1024]{1,0:T(8,128)(2,1)}, bf16[128,1024]{1,0:T(8,128)(2,1)}, bf16[128,1024]{1,0:T(8,128)(2,1)}) custom-call(s32[2,4]{1,0:T(2,128)S(1)} %get-tuple-element.253.offset_ref, s32[2,4]{1,0:T(2,128)S(1)} %get-tuple-element.254.count_ref, f32[256,1024]{1,0:T(8,128)S(1)} %get-tuple-element.211.before_ref, ...), custom_call_target="tpu_custom_call" | custom-call | flops 1024 | bytes 1024 | tf_op jit(solution)/shard_map/pallas_call | solution.py:365
  64.0 3.0 %collective-permute-start.23 = (bf16[128,1024]{1,0:T(8,128)(2,1)}, bf16[128,1024]{1,0:T(8,128)(2,1)}, u32[]{:S(2)}, u32[]{:S(2)}) collective-permute-start(bf16[128,1024]{1,0:T(8,128)(2,1)} %get-tuple-element.218), channel_id=1, source_target_pairs={{0,4},{4,0},{8,12},{12,8},{1,5},{5,1},{9,13},{13,9},{2,6},{6,2},{1... | collective-permute-start | bytes 786440 | tf_op jit(solution)/shard_map/ppermute | solution.py:467
  67.7 1.6 %copy-done.2 = bf16[1,4096,256]{2,1,0:T(8,128)(2,1)S(1)} copy-done((bf16[1,4096,256]{2,1,0:T(8,128)(2,1)S(1)}, bf16[1,4096,256]{2,1,0:T(8,128)(2,1)}, u32[]{:S(2)}) %copy-start.2) | copy-done | bytes 2097176
  69.3 1.8 %shard_map.77 = (f32[256,256]{1,0:T(8,128)S(1)}, f32[256,256]{1,0:T(8,128)S(1)}, bf16[2,1024,256]{2,1,0:T(8,128)(2,1)S(1)}, bf16[2,1024,256]{2,1,0:T(8,128)(2,1)S(1)}) custom-call(s32[4]{0:T(128)S(1)} %pad_add_fusion.order_ref, bf16[1,4096,256]{2,1,0:T(8,128)(2,1)S(1)} %copy-done, bf16[1,4096,256]{2,1,0:T(8,128)(2,1)S(1)} %copy-done.2, ...), custom_call_target="tpu_custom_call" | custom-call | flops 1024 | bytes 1024 | tf_op jit(solution)/shard_map/pallas_call | solution.py:240
  72.3 10.3 %conditional.7 = (bf16[256,256]{1,0:T(8,128)(2,1)}, bf16[256,256]{1,0:T(8,128)(2,1)}, f32[256,1024]{1,0:T(8,128)S(1)}, bf16[2,256,1024]{2,1,0:T(8,128)(2,1)S(1)}) conditional(s32[]{:T(128)} %convert_element_type.17, () %tuple.51, (bf16[256,1024]{1,0:T(8,128)(2,1)}, f32[256,256]{1,0:T(8,128)S(1)}, f32[256,256]{1,0:T(8,128)S(1)}, ...), branch_computations={%region_10.11_spmd, %region_11.12_spmd} | conditional | flops 3072 | bytes 3673280 | solution.py:547
  78.2 2.8 %collective-permute-done.5 = bf16[256,256]{1,0:T(8,128)(2,1)} collective-permute-done((bf16[256,256]{1,0:T(8,128)(2,1)S(1)}, bf16[256,256]{1,0:T(8,128)(2,1)}, u32[]{:S(2)}, u32[]{:S(2)}) %collective-permute-start.5) | collective-permute-done | bytes 131104 | tf_op jit(solution)/shard_map/cond/branch_1_fun/ppermute | solution.py:470
  81.0 1.7 %collective-permute-done.7 = bf16[256,256]{1,0:T(8,128)(2,1)} collective-permute-done((bf16[256,256]{1,0:T(8,128)(2,1)}, bf16[256,256]{1,0:T(8,128)(2,1)}, u32[]{:S(2)}, u32[]{:S(2)}) %collective-permute-start.7) | collective-permute-done | bytes 131104 | tf_op jit(solution)/shard_map/cond/branch_1_fun/ppermute | solution.py:470
  82.7 2.4 %shard_map.78 = (bf16[128,1024]{1,0:T(8,128)(2,1)S(1)}, bf16[128,1024]{1,0:T(8,128)(2,1)S(1)}, bf16[128,1024]{1,0:T(8,128)(2,1)S(1)}, bf16[128,1024]{1,0:T(8,128)(2,1)S(1)}) custom-call(s32[2,4]{1,0:T(2,128)S(1)} %get-tuple-element.253.offset_ref, s32[2,4]{1,0:T(2,128)S(1)} %get-tuple-element.254.count_ref, f32[256,1024]{1,0:T(8,128)S(1)} %get-tuple-element.230.before_ref, ...), custom_call_target="tpu_custom_call" | custom-call | flops 1024 | bytes 1024 | tf_op jit(solution)/shard_map/pallas_call | solution.py:365
  85.1 3.3 %collective-permute-done.22.refs_2_ = bf16[128,1024]{1,0:T(8,128)(2,1)} collective-permute-done((bf16[128,1024]{1,0:T(8,128)(2,1)}, bf16[128,1024]{1,0:T(8,128)(2,1)}, u32[]{:S(2)}, u32[]{:S(2)}) %collective-permute-start.22) | collective-permute-done | bytes 262176 | tf_op jit(solution)/shard_map/ppermute | solution.py:467
  88.4 1.8 %collective-permute-start.26 = (bf16[128,1024]{1,0:T(8,128)(2,1)S(1)}, bf16[128,1024]{1,0:T(8,128)(2,1)S(1)}, u32[]{:S(2)}, u32[]{:S(2)}) collective-permute-start(bf16[128,1024]{1,0:T(8,128)(2,1)S(1)} %get-tuple-element.247), channel_id=1, source_target_pairs={{0,4},{4,0},{8,12},{12,8},{1,5},{5,1},{9,13},{13,9},{2,6},{6,2},{1... | collective-permute-start | bytes 786440 | tf_op jit(solution)/shard_map/ppermute | solution.py:467
  90.2 1.7 %collective-permute-start.27 = (bf16[128,1024]{1,0:T(8,128)(2,1)S(1)}, bf16[128,1024]{1,0:T(8,128)(2,1)S(1)}, u32[]{:S(2)}, u32[]{:S(2)}) collective-permute-start(bf16[128,1024]{1,0:T(8,128)(2,1)S(1)} %get-tuple-element.248), channel_id=1, source_target_pairs={{0,12},{4,8},{8,4},{12,0},{1,13},{5,9},{9,5},{13,1},{2,14},{6,10},... | collective-permute-start | bytes 786440 | tf_op jit(solution)/shard_map/ppermute | solution.py:467
  93.0 1.9 %shard_map.80.refs_0_ = f32[512,1024]{1,0:T(8,128)S(1)} custom-call(s32[4,512]{1,0:T(4,128)S(1)} %get-tuple-element.175.code_ref, f32[4,512]{1,0:T(4,128)S(1)} %shard_map.79.weight_ref, bf16[128,1024]{1,0:T(8,128)(2,1)S(1)} %get-tuple-element.241.refs_0_, bf16[128,1024]{1,0:T(8,128)(2,1)} %collective-permute-done.21.refs_1_, ...), custom_call_target="tpu_custom_call" | custom-call | flops 1024 | bytes 1024 | tf_op jit(solution)/shard_map/pallas_call | solution.py:440
  94.9 6.8 %collective-permute-done.25.refs_2_ = bf16[128,1024]{1,0:T(8,128)(2,1)S(1)} collective-permute-done((bf16[128,1024]{1,0:T(8,128)(2,1)S(1)}, bf16[128,1024]{1,0:T(8,128)(2,1)S(1)}, u32[]{:S(2)}, u32[]{:S(2)}) %collective-permute-start.25) | collective-permute-done | bytes 262176 | tf_op jit(solution)/shard_map/ppermute | solution.py:467
  103.8 9.4 %collective-permute-done.27.refs_1_ = bf16[128,1024]{1,0:T(8,128)(2,1)S(1)} collective-permute-done((bf16[128,1024]{1,0:T(8,128)(2,1)S(1)}, bf16[128,1024]{1,0:T(8,128)(2,1)S(1)}, u32[]{:S(2)}, u32[]{:S(2)}) %collective-permute-start.27) | collective-permute-done | bytes 262176 | tf_op jit(solution)/shard_map/ppermute | solution.py:467
  (68 shorter events, 30.8 us)
Async XLA Ops:
  2.6 21.7 %collective-permute-start.11 = (bf16[128,1024]{1,0:T(8,128)(2,1)}, bf16[128,1024]{1,0:T(8,128)(2,1)S(1)}, u32[]{:S(2)}, u32[]{:S(2)}) collective-permute-start(bf16[128,1024]{1,0:T(8,128)(2,1)} %get-tuple-element.182), channel_id=1, source_target_pairs={{0,8},{4,12},{8,0},{12,4},{1,9},{5,13},{9,1},{13,5},{2,10},{6,14},... | collective-permute-start | bytes 786440 | tf_op jit(solution)/shard_map/ppermute | solution.py:467
  2.7 26.0 %collective-permute-start.12 = (bf16[128,1024]{1,0:T(8,128)(2,1)}, bf16[128,1024]{1,0:T(8,128)(2,1)S(1)}, u32[]{:S(2)}, u32[]{:S(2)}) collective-permute-start(bf16[128,1024]{1,0:T(8,128)(2,1)} %get-tuple-element.183), channel_id=1, source_target_pairs={{0,12},{4,8},{8,4},{12,0},{1,13},{5,9},{9,5},{13,1},{2,14},{6,10},... | collective-permute-start | bytes 786440 | tf_op jit(solution)/shard_map/ppermute | solution.py:467
  5.7 23.0 %collective-permute-start.13 = (bf16[128,1024]{1,0:T(8,128)(2,1)}, bf16[128,1024]{1,0:T(8,128)(2,1)S(1)}, u32[]{:S(2)}, u32[]{:S(2)}) collective-permute-start(bf16[128,1024]{1,0:T(8,128)(2,1)} %get-tuple-element.184), channel_id=1, source_target_pairs={{0,4},{4,0},{8,12},{12,8},{1,5},{5,1},{9,13},{13,9},{2,6},{6,2},{1... | collective-permute-start | bytes 786440 | tf_op jit(solution)/shard_map/ppermute | solution.py:467
  9.9 26.9 %copy-start = (bf16[1,4096,256]{2,1,0:T(8,128)(2,1)S(1)}, bf16[1,4096,256]{2,1,0:T(8,128)(2,1)}, u32[]{:S(2)}) copy-start(bf16[1,4096,256]{2,1,0:T(8,128)(2,1)} %gate_ref.3) | copy-start | bytes 6291460
  11.7 3.7 %collective-permute-start.8 = (f32[4,512]{1,0:T(4,128)S(1)}, f32[4,512]{1,0:T(4,128)S(1)}, u32[]{:S(2)}, u32[]{:S(2)}) collective-permute-start(f32[4,512]{1,0:T(4,128)S(1)} %branch_1_fun.10), channel_id=1, source_target_pairs={{0,2},{1,3},{2,0},{3,1},{4,6},{5,7},{6,4},{7,5},{8,10},{9,11},{10,... | collective-permute-start | bytes 24584 | tf_op jit(solution)/shard_map/cond/branch_1_fun/ppermute | solution.py:470
  15.4 1.2 %collective-permute-start.9 = (f32[4,512]{1,0:T(4,128)S(1)}, f32[4,512]{1,0:T(4,128)S(1)}, u32[]{:S(2)}, u32[]{:S(2)}) collective-permute-start(f32[4,512]{1,0:T(4,128)S(1)} %add.24), channel_id=1, source_target_pairs={{0,1},{1,0},{2,3},{3,2},{4,5},{5,4},{6,7},{7,6},{8,9},{9,8},{10,11... | collective-permute-start | bytes 24584 | tf_op jit(solution)/shard_map/cond/branch_1_fun/ppermute | solution.py:470
  17.1 6.5 %collective-permute-start.10 = (f32[1,4,512]{2,1,0:T(4,128)}, f32[1,4,512]{2,1,0:T(4,128)S(1)}, u32[]{:S(2)}, u32[]{:S(2)}) collective-permute-start(f32[1,4,512]{2,1,0:T(4,128)} %bitcast), channel_id=1, source_target_pairs={{0,4},{4,0},{8,12},{12,8},{1,5},{5,1},{9,13},{13,9},{2,6},{6,2},{1... | collective-permute-start | bytes 24584 | tf_op jit(solution)/shard_map/cond/branch_1_fun/ppermute | solution.py:467
  30.7 6.1 %collective-permute-start.18 = (bf16[256,1024]{1,0:T(8,128)(2,1)}, bf16[256,1024]{1,0:T(8,128)(2,1)S(1)}, u32[]{:S(2)}, u32[]{:S(2)}) collective-permute-start(bf16[256,1024]{1,0:T(8,128)(2,1)} %get-tuple-element.287.refs_0_), channel_id=1, source_target_pairs={{0,1},{1,0},{2,3},{3,2},{4,5},{5,4},{6,7},{7,6},{8,9},{9,8},{10,11... | collective-permute-start | bytes 1572872 | tf_op jit(solution)/shard_map/ppermute | solution.py:470
  30.8 14.7 %collective-permute-start.17 = (bf16[256,1024]{1,0:T(8,128)(2,1)}, bf16[256,1024]{1,0:T(8,128)(2,1)}, u32[]{:S(2)}, u32[]{:S(2)}) collective-permute-start(bf16[256,1024]{1,0:T(8,128)(2,1)} %get-tuple-element.287.refs_0_), channel_id=1, source_target_pairs={{0,2},{1,3},{2,0},{3,1},{4,6},{5,7},{6,4},{7,5},{8,10},{9,11},{10,... | collective-permute-start | bytes 1572872 | tf_op jit(solution)/shard_map/ppermute | solution.py:470
  32.3 23.5 %collective-permute-start.14 = (bf16[128,1024]{1,0:T(8,128)(2,1)}, bf16[128,1024]{1,0:T(8,128)(2,1)S(1)}, u32[]{:S(2)}, u32[]{:S(2)}) collective-permute-start(bf16[128,1024]{1,0:T(8,128)(2,1)} %get-tuple-element.191), channel_id=1, source_target_pairs={{0,8},{4,12},{8,0},{12,4},{1,9},{5,13},{9,1},{13,5},{2,10},{6,14},... | collective-permute-start | bytes 786440 | tf_op jit(solution)/shard_map/ppermute | solution.py:467
  32.3 23.5 %collective-permute-start.15 = (bf16[128,1024]{1,0:T(8,128)(2,1)}, bf16[128,1024]{1,0:T(8,128)(2,1)S(1)}, u32[]{:S(2)}, u32[]{:S(2)}) collective-permute-start(bf16[128,1024]{1,0:T(8,128)(2,1)} %get-tuple-element.192), channel_id=1, source_target_pairs={{0,12},{4,8},{8,4},{12,0},{1,13},{5,9},{9,5},{13,1},{2,14},{6,10},... | collective-permute-start | bytes 786440 | tf_op jit(solution)/shard_map/ppermute | solution.py:467
  32.3 23.5 %collective-permute-start.16 = (bf16[128,1024]{1,0:T(8,128)(2,1)}, bf16[128,1024]{1,0:T(8,128)(2,1)S(1)}, u32[]{:S(2)}, u32[]{:S(2)}) collective-permute-start(bf16[128,1024]{1,0:T(8,128)(2,1)} %get-tuple-element.193), channel_id=1, source_target_pairs={{0,4},{4,0},{8,12},{12,8},{1,5},{5,1},{9,13},{13,9},{2,6},{6,2},{1... | collective-permute-start | bytes 786440 | tf_op jit(solution)/shard_map/ppermute | solution.py:467
  36.8 1.6 %copy-start.1 = (bf16[1,4096,256]{2,1,0:T(8,128)(2,1)S(1)}, bf16[1,4096,256]{2,1,0:T(8,128)(2,1)}, u32[]{:S(2)}) copy-start(bf16[1,4096,256]{2,1,0:T(8,128)(2,1)} %up_ref.3) | copy-start | bytes 6291460
  38.4 7.0 %copy-start.3 = (bf16[1,1024,1024]{2,1,0:T(8,128)(2,1)S(1)}, bf16[1,1024,1024]{2,1,0:T(8,128)(2,1)}, u32[]{:S(2)}) copy-start(bf16[1,1024,1024]{2,1,0:T(8,128)(2,1)} %param.19) | copy-start | bytes 6291460
  45.4 2.1 %collective-permute-start = (bf16[256,1024]{1,0:T(8,128)(2,1)}, bf16[256,1024]{1,0:T(8,128)(2,1)S(1)}, u32[]{:S(2)}, u32[]{:S(2)}) collective-permute-start(bf16[256,1024]{1,0:T(8,128)(2,1)} %get-tuple-element.67.refs_0_), channel_id=1, source_target_pairs={{0,1},{1,0},{2,3},{3,2},{4,5},{5,4},{6,7},{7,6},{8,9},{9,8},{10,11... | collective-permute-start | bytes 1572872 | tf_op jit(solution)/shard_map/cond/branch_1_fun/ppermute | solution.py:470
  48.0 1.7 %collective-permute-start.2 = (bf16[256,256]{1,0:T(8,128)(2,1)S(1)}, bf16[256,256]{1,0:T(8,128)(2,1)S(1)}, u32[]{:S(2)}, u32[]{:S(2)}) collective-permute-start(bf16[256,256]{1,0:T(8,128)(2,1)S(1)} %branch_1_fun.13.refs_0_), channel_id=1, source_target_pairs={{0,1},{1,0},{2,3},{3,2},{4,5},{5,4},{6,7},{7,6},{8,9},{9,8},{10,11... | collective-permute-start | bytes 393224 | tf_op jit(solution)/shard_map/cond/branch_1_fun/ppermute | solution.py:470
  48.2 5.9 %collective-permute-start.1 = (bf16[256,256]{1,0:T(8,128)(2,1)S(1)}, bf16[256,256]{1,0:T(8,128)(2,1)}, u32[]{:S(2)}, u32[]{:S(2)}) collective-permute-start(bf16[256,256]{1,0:T(8,128)(2,1)S(1)} %branch_1_fun.13.refs_0_), channel_id=1, source_target_pairs={{0,2},{1,3},{2,0},{3,1},{4,6},{5,7},{6,4},{7,5},{8,10},{9,11},{10,... | collective-permute-start | bytes 393224 | tf_op jit(solution)/shard_map/cond/branch_1_fun/ppermute | solution.py:470
  54.1 1.7 %collective-permute-start.3 = (bf16[256,256]{1,0:T(8,128)(2,1)}, bf16[256,256]{1,0:T(8,128)(2,1)}, u32[]{:S(2)}, u32[]{:S(2)}) collective-permute-start(bf16[256,256]{1,0:T(8,128)(2,1)} %collective-permute-done.1), channel_id=1, source_target_pairs={{0,1},{1,0},{2,3},{3,2},{4,5},{5,4},{6,7},{7,6},{8,9},{9,8},{10,11... | collective-permute-start | bytes 393224 | tf_op jit(solution)/shard_map/cond/branch_1_fun/ppermute | solution.py:470
  57.8 9.9 %collective-permute-start.20 = (bf16[256,1024]{1,0:T(8,128)(2,1)S(1)}, bf16[256,1024]{1,0:T(8,128)(2,1)S(1)}, u32[]{:S(2)}, u32[]{:S(2)}) collective-permute-start(bf16[256,1024]{1,0:T(8,128)(2,1)S(1)} %shard_map.75.refs_0_), channel_id=1, source_target_pairs={{0,1},{1,0},{2,3},{3,2},{4,5},{5,4},{6,7},{7,6},{8,9},{9,8},{10,11... | collective-permute-start | bytes 1572872 | tf_op jit(solution)/shard_map/ppermute | solution.py:470
  58.0 14.3 %collective-permute-start.19 = (bf16[256,1024]{1,0:T(8,128)(2,1)S(1)}, bf16[256,1024]{1,0:T(8,128)(2,1)}, u32[]{:S(2)}, u32[]{:S(2)}) collective-permute-start(bf16[256,1024]{1,0:T(8,128)(2,1)S(1)} %shard_map.75.refs_0_), channel_id=1, source_target_pairs={{0,2},{1,3},{2,0},{3,1},{4,6},{5,7},{6,4},{7,5},{8,10},{9,11},{10,... | collective-permute-start | bytes 1572872 | tf_op jit(solution)/shard_map/ppermute | solution.py:470
  62.6 22.4 %collective-permute-start.21 = (bf16[128,1024]{1,0:T(8,128)(2,1)}, bf16[128,1024]{1,0:T(8,128)(2,1)}, u32[]{:S(2)}, u32[]{:S(2)}) collective-permute-start(bf16[128,1024]{1,0:T(8,128)(2,1)} %get-tuple-element.216), channel_id=1, source_target_pairs={{0,8},{4,12},{8,0},{12,4},{1,9},{5,13},{9,1},{13,5},{2,10},{6,14},... | collective-permute-start | bytes 786440 | tf_op jit(solution)/shard_map/ppermute | solution.py:467
  62.7 25.6 %collective-permute-start.22 = (bf16[128,1024]{1,0:T(8,128)(2,1)}, bf16[128,1024]{1,0:T(8,128)(2,1)}, u32[]{:S(2)}, u32[]{:S(2)}) collective-permute-start(bf16[128,1024]{1,0:T(8,128)(2,1)} %get-tuple-element.217), channel_id=1, source_target_pairs={{0,12},{4,8},{8,4},{12,0},{1,13},{5,9},{9,5},{13,1},{2,14},{6,10},... | collective-permute-start | bytes 786440 | tf_op jit(solution)/shard_map/ppermute | solution.py:467
  64.0 24.3 %collective-permute-start.23 = (bf16[128,1024]{1,0:T(8,128)(2,1)}, bf16[128,1024]{1,0:T(8,128)(2,1)}, u32[]{:S(2)}, u32[]{:S(2)}) collective-permute-start(bf16[128,1024]{1,0:T(8,128)(2,1)} %get-tuple-element.218), channel_id=1, source_target_pairs={{0,4},{4,0},{8,12},{12,8},{1,5},{5,1},{9,13},{13,9},{2,6},{6,2},{1... | collective-permute-start | bytes 786440 | tf_op jit(solution)/shard_map/ppermute | solution.py:467
  69.3 3.0 %copy-start.4 = (bf16[1,1024,1024]{2,1,0:T(8,128)(2,1)S(1)}, bf16[1,1024,1024]{2,1,0:T(8,128)(2,1)}, u32[]{:S(2)}) copy-start(bf16[1,1024,1024]{2,1,0:T(8,128)(2,1)} %param.19) | copy-start | bytes 6291460
  72.3 2.1 %collective-permute-start.4 = (bf16[256,1024]{1,0:T(8,128)(2,1)}, bf16[256,1024]{1,0:T(8,128)(2,1)S(1)}, u32[]{:S(2)}, u32[]{:S(2)}) collective-permute-start(bf16[256,1024]{1,0:T(8,128)(2,1)} %get-tuple-element.84.refs_0_), channel_id=1, source_target_pairs={{0,1},{1,0},{2,3},{3,2},{4,5},{5,4},{6,7},{7,6},{8,9},{9,8},{10,11... | collective-permute-start | bytes 1572872 | tf_op jit(solution)/shard_map/cond/branch_1_fun/ppermute | solution.py:470
  74.9 1.7 %collective-permute-start.6 = (bf16[256,256]{1,0:T(8,128)(2,1)S(1)}, bf16[256,256]{1,0:T(8,128)(2,1)S(1)}, u32[]{:S(2)}, u32[]{:S(2)}) collective-permute-start(bf16[256,256]{1,0:T(8,128)(2,1)S(1)} %branch_1_fun.16.refs_0_), channel_id=1, source_target_pairs={{0,1},{1,0},{2,3},{3,2},{4,5},{5,4},{6,7},{7,6},{8,9},{9,8},{10,11... | collective-permute-start | bytes 393224 | tf_op jit(solution)/shard_map/cond/branch_1_fun/ppermute | solution.py:470
  75.1 5.9 %collective-permute-start.5 = (bf16[256,256]{1,0:T(8,128)(2,1)S(1)}, bf16[256,256]{1,0:T(8,128)(2,1)}, u32[]{:S(2)}, u32[]{:S(2)}) collective-permute-start(bf16[256,256]{1,0:T(8,128)(2,1)S(1)} %branch_1_fun.16.refs_0_), channel_id=1, source_target_pairs={{0,2},{1,3},{2,0},{3,1},{4,6},{5,7},{6,4},{7,5},{8,10},{9,11},{10,... | collective-permute-start | bytes 393224 | tf_op jit(solution)/shard_map/cond/branch_1_fun/ppermute | solution.py:470
  81.0 1.7 %collective-permute-start.7 = (bf16[256,256]{1,0:T(8,128)(2,1)}, bf16[256,256]{1,0:T(8,128)(2,1)}, u32[]{:S(2)}, u32[]{:S(2)}) collective-permute-start(bf16[256,256]{1,0:T(8,128)(2,1)} %collective-permute-done.5), channel_id=1, source_target_pairs={{0,1},{1,0},{2,3},{3,2},{4,5},{5,4},{6,7},{7,6},{8,9},{9,8},{10,11... | collective-permute-start | bytes 393224 | tf_op jit(solution)/shard_map/cond/branch_1_fun/ppermute | solution.py:470
  82.7 5.7 %collective-permute-start.24 = (f32[2,4,512]{2,1,0:T(4,128)S(1)}, f32[2,4,512]{2,1,0:T(4,128)S(1)}, u32[]{:S(2)}, u32[]{:S(2)}) collective-permute-start(f32[2,4,512]{2,1,0:T(4,128)S(1)} %get-tuple-element.239), channel_id=1, source_target_pairs={{0,8},{4,12},{8,0},{12,4},{1,9},{5,13},{9,1},{13,5},{2,10},{6,14},... | collective-permute-start | bytes 49160 | tf_op jit(solution)/shard_map/ppermute | solution.py:467
  88.3 13.3 %collective-permute-start.25 = (bf16[128,1024]{1,0:T(8,128)(2,1)S(1)}, bf16[128,1024]{1,0:T(8,128)(2,1)S(1)}, u32[]{:S(2)}, u32[]{:S(2)}) collective-permute-start(bf16[128,1024]{1,0:T(8,128)(2,1)S(1)} %get-tuple-element.246), channel_id=1, source_target_pairs={{0,8},{4,12},{8,0},{12,4},{1,9},{5,13},{9,1},{13,5},{2,10},{6,14},... | collective-permute-start | bytes 786440 | tf_op jit(solution)/shard_map/ppermute | solution.py:467
  88.4 14.6 %collective-permute-start.26 = (bf16[128,1024]{1,0:T(8,128)(2,1)S(1)}, bf16[128,1024]{1,0:T(8,128)(2,1)S(1)}, u32[]{:S(2)}, u32[]{:S(2)}) collective-permute-start(bf16[128,1024]{1,0:T(8,128)(2,1)S(1)} %get-tuple-element.247), channel_id=1, source_target_pairs={{0,4},{4,0},{8,12},{12,8},{1,5},{5,1},{9,13},{13,9},{2,6},{6,2},{1... | collective-permute-start | bytes 786440 | tf_op jit(solution)/shard_map/ppermute | solution.py:467
  90.2 23.1 %collective-permute-start.27 = (bf16[128,1024]{1,0:T(8,128)(2,1)S(1)}, bf16[128,1024]{1,0:T(8,128)(2,1)S(1)}, u32[]{:S(2)}, u32[]{:S(2)}) collective-permute-start(bf16[128,1024]{1,0:T(8,128)(2,1)S(1)} %get-tuple-element.248), channel_id=1, source_target_pairs={{0,12},{4,8},{8,4},{12,0},{1,13},{5,9},{9,5},{13,1},{2,14},{6,10},... | collective-permute-start | bytes 786440 | tf_op jit(solution)/shard_map/ppermute | solution.py:467
  (1 other events, 1.6 us)

commit v20 on v19

--- a/solution.py
+++ b/solution.py
@@ -581,8 +581,8 @@
     weights = slot_weights(place, logits, gathered, code)
     total = None
     for k in range(BATCHES - 1):
-        total = combine(code, weights, k, range(experts), waiting[k], total, False)
-    late = (min(2, experts - 1),)
+        total = combine(code, weights, k, sorted(range(experts), key=lambda i: (0, 2, 1)[i] if i < 3 else i), waiting[k], total, False)
+    late = (min(1, experts - 1),)
     early = [i for i in range(experts) if i not in late]
     total = combine(code, weights, BATCHES - 1, early, waiting[-1], total, False)
     return combine(code, weights, BATCHES - 1, late, waiting[-1], total, True)

time: 116 us -> 117 us (level)
  the two profiles are of different devices: /device:TPU:16 before, /device:TPU:0 now
where the time goes in v20:
time: 117 us
  waiting for transfers between devices  38.2 us (33%)
  starting transfers between devices  36.8 us (31%)
  Pallas kernels  33.2 us (28%)
  local copies, waits for them, and re-layouts  3.89 us (3%)
  other arithmetic  2.93 us (3%)
  between operations  1.58 us (1%)
    ppermute x14, starting transfers between devices, along_expert(): return lax.ppermute(x, 'expert', [(i, i ^ shift) for i in range(experts)])  29.4 us
    ppermute x14, waiting for transfers between devices, along_expert(): return lax.ppermute(x, 'expert', [(i, i ^ shift) for i in range(experts)])  22.5 us
    ppermute x14, waiting for transfers between devices, swap(): return lax.ppermute(x, 'dp', [(i, i ^ bit) for i in range(width_parts)])  15.8 us
    ppermute x14, starting transfers between devices, swap(): return lax.ppermute(x, 'dp', [(i, i ^ bit) for i in range(width_parts)])  7.4 us
    pallas_call x2, Pallas kernels, down_last(): pl.pallas_call(functools.partial(down_last_kernel, parts, experts, k, dir...  5.48 us
    pallas_call x2, Pallas kernels, gate_up_near(): pl.pallas_call(functools.partial(gate_up_near_kernel, parts, near, far),...  4.4 us
    pallas_call x3, Pallas kernels, combine(): pl.pallas_call(functools.partial(combine_kernel, places, k, len(more)), o...  4.29 us
    pallas_call x2, Pallas kernels, compact(): pl.pallas_call(functools.partial(compact_kernel, experts, k), out_shape=j...  3.94 us
  transfers between devices with their start and end apart: 28, of which 15 were waited for; matrix products, arithmetic and copies ran while one was open for 3% of the time, Pallas kernels for 22%

profile of v20, /device:TPU:0, one launch (start us, length us, event | category | flops | bytes accessed | tf_op | source)
XLA Modules:
  0.0 116.8 jit_solution(11334760233828273515)
XLA Ops:
  0.0 2.6 %shard_map.73 = (s32[4,512]{1,0:T(4,128)S(1)}, bf16[128,1024]{1,0:T(8,128)(2,1)S(1)}, bf16[128,1024]{1,0:T(8,128)(2,1)}, bf16[128,1024]{1,0:T(8,128)(2,1)}, bf16[128,1024]{1,0:T(8,128)(2,1)}) custom-call(s32[1]{0:T(128)} %bitcast.1.place_ref, s32[4,512]{1,0:T(4,128)} %picks_in.1, bf16[512,1024]{1,0:T(8,128)(2,1)} %tokens_ref.1), custom_call_target="tpu_custom_call" | custom-call | flops 1024 | bytes 1024 | tf_op jit(solution)/shard_map/pallas_call | solution.py:108
  2.6 4.1 %collective-permute-start.11 = (bf16[128,1024]{1,0:T(8,128)(2,1)}, bf16[128,1024]{1,0:T(8,128)(2,1)S(1)}, u32[]{:S(2)}, u32[]{:S(2)}) collective-permute-start(bf16[128,1024]{1,0:T(8,128)(2,1)} %get-tuple-element.182), channel_id=1, source_target_pairs={{0,8},{4,12},{8,0},{12,4},{1,9},{5,13},{9,1},{13,5},{2,10},{6,14},... | collective-permute-start | bytes 786440 | tf_op jit(solution)/shard_map/ppermute | solution.py:467
  11.1 15.6 %conditional.4 = (bf16[128,1024]{1,0:T(8,128)(2,1)}, bf16[128,1024]{1,0:T(8,128)(2,1)}, bf16[128,1024]{1,0:T(8,128)(2,1)}, bf16[128,1024]{1,0:T(8,128)(2,1)}, f3...) conditional(s32[]{:T(128)} %convert_element_type.16, () %tuple.49, (s32[4,512]{1,0:T(4,128)S(1)}, ...), branch_computations={%region_3.4_spmd, %region_4.5_spmd} | conditional | flops 10240 | bytes 1073216 | solution.py:525
  11.2 1.8 %branch_1_fun.10 = f32[4,512]{1,0:T(4,128)S(1)} custom-call(bf16[4,1024]{1,0:T(4,128)(2,1)} %get-tuple-element.60.router_ref, bf16[512,1024]{1,0:T(8,128)(2,1)} %get-tuple-element.55.tokens_ref), custom_call_target="tpu_custom_call" | custom-call | flops 1024 | bytes 1024 | tf_op jit(solution)/shard_map/cond/branch_1_fun/pallas_call | solution.py:134
  14.4 2.2 %collective-permute-done.8 = f32[4,512]{1,0:T(4,128)S(1)} collective-permute-done((f32[4,512]{1,0:T(4,128)S(1)}, f32[4,512]{1,0:T(4,128)S(1)}, u32[]{:S(2)}, u32[]{:S(2)}) %collective-permute-start.8) | collective-permute-done | bytes 8224 | tf_op jit(solution)/shard_map/cond/branch_1_fun/ppermute | solution.py:470
  18.4 1.8 %collective-permute-start.10 = (f32[1,4,512]{2,1,0:T(4,128)}, f32[1,4,512]{2,1,0:T(4,128)S(1)}, u32[]{:S(2)}, u32[]{:S(2)}) collective-permute-start(f32[1,4,512]{2,1,0:T(4,128)} %bitcast), channel_id=1, source_target_pairs={{0,4},{4,0},{8,12},{12,8},{1,5},{5,1},{9,13},{13,9},{2,6},{6,2},{1... | collective-permute-start | bytes 24584 | tf_op jit(solution)/shard_map/cond/branch_1_fun/ppermute | solution.py:467
  20.1 2.7 %branch_1_fun.9 = (bf16[128,1024]{1,0:T(8,128)(2,1)}, bf16[128,1024]{1,0:T(8,128)(2,1)}, bf16[128,1024]{1,0:T(8,128)(2,1)}, bf16[128,1024]{1,0:T(8,128)(2,1)}) custom-call(s32[4,512]{1,0:T(4,128)S(1)} %get-tuple-element.54.code_ref, bf16[512,1024]{1,0:T(8,128)(2,1)} %get-tuple-element.55.tokens_ref), custom_call_target="tpu_custom_call" | custom-call | flops 1024 | bytes 1024 | tf_op jit(solution)/shard_map/cond/branch_1_fun/pallas_call | solution.py:155
  22.9 3.2 %collective-permute-done.10 = f32[1,4,512]{2,1,0:T(4,128)S(1)} collective-permute-done((f32[1,4,512]{2,1,0:T(4,128)}, f32[1,4,512]{2,1,0:T(4,128)S(1)}, u32[]{:S(2)}, u32[]{:S(2)}) %collective-permute-start.10) | collective-permute-done | bytes 8224 | tf_op jit(solution)/shard_map/cond/branch_1_fun/ppermute | solution.py:467
  26.8 2.0 %conditional.5 = (bf16[256,1024]{1,0:T(8,128)(2,1)}) conditional(s32[]{:T(128)} %convert_element_type.16, () %tuple.55, (s32[2,4]{1,0:T(2,128)S(1)}, s32[2,4]{1,0:T(2,128)S(1)}, bf16[128,1024]{1,0:T(8,128)(2,1)S(1)}, bf16[128,1024]{1,0:T(8,128)(2,1)S(1)}, bf16[128,1024]{1,0:T(8,128)(2,1)S(1)}, /*index=5*/bf16[128,1024]{1,0:T(8,128)(2,1)S(1)}) %tuple.56), branch_computations={%region_6.7_spmd, %region_7.8_spmd} | conditional | flops 1024 | bytes 524298 | solution.py:547
  26.8 1.9 %branch_1_fun.11 = bf16[256,1024]{1,0:T(8,128)(2,1)} custom-call(s32[2,4]{1,0:T(2,128)S(1)} %get-tuple-element.61.offset_ref, s32[2,4]{1,0:T(2,128)S(1)} %get-tuple-element.62.count_ref, bf16[128,1024]{1,0:T(8,128)(2,1)S(1)} %get-tuple-element.63.refs_0_, bf16[128,1024]{1,0:T(8,128)(2,1)S(1)} %get-tuple-element.64.refs_1_, ...), custom_call_target="tpu_custom_call" | custom-call | flops 1024 | bytes 1024 | tf_op jit(solution)/shard_map/cond/branch_1_fun/pallas_call | solution.py:192
  28.8 1.6 %collective-permute-start.17 = (bf16[256,1024]{1,0:T(8,128)(2,1)}, bf16[256,1024]{1,0:T(8,128)(2,1)}, u32[]{:S(2)}, u32[]{:S(2)}) collective-permute-start(bf16[256,1024]{1,0:T(8,128)(2,1)} %get-tuple-element.287.refs_0_), channel_id=1, source_target_pairs={{0,2},{1,3},{2,0},{3,1},{4,6},{5,7},{6,4},{7,5},{8,10},{9,11},{10,... | collective-permute-start | bytes 1572872 | tf_op jit(solution)/shard_map/ppermute | solution.py:470
  30.4 5.9 %collective-permute-start.14 = (bf16[128,1024]{1,0:T(8,128)(2,1)}, bf16[128,1024]{1,0:T(8,128)(2,1)S(1)}, u32[]{:S(2)}, u32[]{:S(2)}) collective-permute-start(bf16[128,1024]{1,0:T(8,128)(2,1)} %get-tuple-element.191), channel_id=1, source_target_pairs={{0,8},{4,12},{8,0},{12,4},{1,9},{5,13},{9,1},{13,5},{2,10},{6,14},... | collective-permute-start | bytes 786440 | tf_op jit(solution)/shard_map/ppermute | solution.py:467
  38.6 2.6 %shard_map.74 = (f32[256,256]{1,0:T(8,128)S(1)}, f32[256,256]{1,0:T(8,128)S(1)}, bf16[2,1024,256]{2,1,0:T(8,128)(2,1)S(1)}, bf16[2,1024,256]{2,1,0:T(8,128)(2,1)S(1)}) custom-call(s32[4]{0:T(128)S(1)} %pad_add_fusion.order_ref, bf16[1,4096,256]{2,1,0:T(8,128)(2,1)S(1)} %copy-done, bf16[1,4096,256]{2,1,0:T(8,128)(2,1)S(1)} %copy-done.1, ...), custom_call_target="tpu_custom_call" | custom-call | flops 1024 | bytes 1024 | tf_op jit(solution)/shard_map/pallas_call | solution.py:240
  41.2 2.3 %collective-permute-done.17 = bf16[256,1024]{1,0:T(8,128)(2,1)} collective-permute-done((bf16[256,1024]{1,0:T(8,128)(2,1)}, bf16[256,1024]{1,0:T(8,128)(2,1)}, u32[]{:S(2)}, u32[]{:S(2)}) %collective-permute-start.17) | collective-permute-done | bytes 524320 | tf_op jit(solution)/shard_map/ppermute | solution.py:470
  43.5 10.3 %conditional.6 = (bf16[256,256]{1,0:T(8,128)(2,1)}, bf16[256,256]{1,0:T(8,128)(2,1)}, f32[256,1024]{1,0:T(8,128)S(1)}, bf16[2,256,1024]{2,1,0:T(8,128)(2,1)S(1)}) conditional(s32[]{:T(128)} %convert_element_type.16, () %tuple.54, (bf16[256,1024]{1,0:T(8,128)(2,1)}, f32[256,256]{1,0:T(8,128)S(1)}, f32[256,256]{1,0:T(8,128)S(1)}, ...), branch_computations={%region_8.9_spmd, %region_9.10_spmd} | conditional | flops 3072 | bytes 3673280 | solution.py:547
  49.4 2.7 %collective-permute-done.1 = bf16[256,256]{1,0:T(8,128)(2,1)} collective-permute-done((bf16[256,256]{1,0:T(8,128)(2,1)S(1)}, bf16[256,256]{1,0:T(8,128)(2,1)}, u32[]{:S(2)}, u32[]{:S(2)}) %collective-permute-start.1) | collective-permute-done | bytes 131104 | tf_op jit(solution)/shard_map/cond/branch_1_fun/ppermute | solution.py:470
  52.1 1.7 %collective-permute-done.3 = bf16[256,256]{1,0:T(8,128)(2,1)} collective-permute-done((bf16[256,256]{1,0:T(8,128)(2,1)}, bf16[256,256]{1,0:T(8,128)(2,1)}, u32[]{:S(2)}, u32[]{:S(2)}) %collective-permute-start.3) | collective-permute-done | bytes 131104 | tf_op jit(solution)/shard_map/cond/branch_1_fun/ppermute | solution.py:470
  55.8 2.0 %shard_map.75.refs_0_ = bf16[256,1024]{1,0:T(8,128)(2,1)S(1)} custom-call(s32[2,4]{1,0:T(2,128)S(1)} %get-tuple-element.253.offset_ref, s32[2,4]{1,0:T(2,128)S(1)} %get-tuple-element.254.count_ref, bf16[128,1024]{1,0:T(8,128)(2,1)} %get-tuple-element.205.refs_0_, bf16[128,1024]{1,0:T(8,128)(2,1)S(1)} %collective-permute-done.14.refs_1_, ...), custom_call_target="tpu_custom_call" | custom-call | flops 1024 | bytes 1024 | tf_op jit(solution)/shard_map/pallas_call | solution.py:192
  58.5 3.1 %shard_map.76 = (bf16[128,1024]{1,0:T(8,128)(2,1)S(1)}, bf16[128,1024]{1,0:T(8,128)(2,1)}, bf16[128,1024]{1,0:T(8,128)(2,1)}, bf16[128,1024]{1,0:T(8,128)(2,1)}) custom-call(s32[2,4]{1,0:T(2,128)S(1)} %get-tuple-element.253.offset_ref, s32[2,4]{1,0:T(2,128)S(1)} %get-tuple-element.254.count_ref, f32[256,1024]{1,0:T(8,128)S(1)} %get-tuple-element.211.before_ref, ...), custom_call_target="tpu_custom_call" | custom-call | flops 1024 | bytes 1024 | tf_op jit(solution)/shard_map/pallas_call | solution.py:365
  61.6 5.1 %collective-permute-start.21 = (bf16[128,1024]{1,0:T(8,128)(2,1)}, bf16[128,1024]{1,0:T(8,128)(2,1)}, u32[]{:S(2)}, u32[]{:S(2)}) collective-permute-start(bf16[128,1024]{1,0:T(8,128)(2,1)} %get-tuple-element.216), channel_id=1, source_target_pairs={{0,8},{4,12},{8,0},{12,4},{1,9},{5,13},{9,1},{13,5},{2,10},{6,14},... | collective-permute-start | bytes 786440 | tf_op jit(solution)/shard_map/ppermute | solution.py:467
  66.7 2.2 %collective-permute-start.22 = (bf16[128,1024]{1,0:T(8,128)(2,1)}, bf16[128,1024]{1,0:T(8,128)(2,1)}, u32[]{:S(2)}, u32[]{:S(2)}) collective-permute-start(bf16[128,1024]{1,0:T(8,128)(2,1)} %get-tuple-element.217), channel_id=1, source_target_pairs={{0,12},{4,8},{8,4},{12,0},{1,13},{5,9},{9,5},{13,1},{2,14},{6,10},... | collective-permute-start | bytes 786440 | tf_op jit(solution)/shard_map/ppermute | solution.py:467
  71.1 1.8 %shard_map.77 = (f32[256,256]{1,0:T(8,128)S(1)}, f32[256,256]{1,0:T(8,128)S(1)}, bf16[2,1024,256]{2,1,0:T(8,128)(2,1)S(1)}, bf16[2,1024,256]{2,1,0:T(8,128)(2,1)S(1)}) custom-call(s32[4]{0:T(128)S(1)} %pad_add_fusion.order_ref, bf16[1,4096,256]{2,1,0:T(8,128)(2,1)S(1)} %copy-done, bf16[1,4096,256]{2,1,0:T(8,128)(2,1)S(1)} %copy-done.2, ...), custom_call_target="tpu_custom_call" | custom-call | flops 1024 | bytes 1024 | tf_op jit(solution)/shard_map/pallas_call | solution.py:240
  73.0 10.4 %conditional.7 = (bf16[256,256]{1,0:T(8,128)(2,1)}, bf16[256,256]{1,0:T(8,128)(2,1)}, f32[256,1024]{1,0:T(8,128)S(1)}, bf16[2,256,1024]{2,1,0:T(8,128)(2,1)S(1)}) conditional(s32[]{:T(128)} %convert_element_type.17, () %tuple.51, (bf16[256,1024]{1,0:T(8,128)(2,1)}, f32[256,256]{1,0:T(8,128)S(1)}, f32[256,256]{1,0:T(8,128)S(1)}, ...), branch_computations={%region_10.11_spmd, %region_11.12_spmd} | conditional | flops 3072 | bytes 3673280 | solution.py:547
  78.9 2.8 %collective-permute-done.5 = bf16[256,256]{1,0:T(8,128)(2,1)} collective-permute-done((bf16[256,256]{1,0:T(8,128)(2,1)S(1)}, bf16[256,256]{1,0:T(8,128)(2,1)}, u32[]{:S(2)}, u32[]{:S(2)}) %collective-permute-start.5) | collective-permute-done | bytes 131104 | tf_op jit(solution)/shard_map/cond/branch_1_fun/ppermute | solution.py:470
  81.7 1.7 %collective-permute-done.7 = bf16[256,256]{1,0:T(8,128)(2,1)} collective-permute-done((bf16[256,256]{1,0:T(8,128)(2,1)}, bf16[256,256]{1,0:T(8,128)(2,1)}, u32[]{:S(2)}, u32[]{:S(2)}) %collective-permute-start.7) | collective-permute-done | bytes 131104 | tf_op jit(solution)/shard_map/cond/branch_1_fun/ppermute | solution.py:470
  83.4 3.3 %collective-permute-start.24 = (f32[2,4,512]{2,1,0:T(4,128)S(1)}, f32[2,4,512]{2,1,0:T(4,128)S(1)}, u32[]{:S(2)}, u32[]{:S(2)}) collective-permute-start(f32[2,4,512]{2,1,0:T(4,128)S(1)} %get-tuple-element.239), channel_id=1, source_target_pairs={{0,8},{4,12},{8,0},{12,4},{1,9},{5,13},{9,1},{13,5},{2,10},{6,14},... | collective-permute-start | bytes 49160 | tf_op jit(solution)/shard_map/ppermute | solution.py:467
  86.7 2.4 %shard_map.78 = (bf16[128,1024]{1,0:T(8,128)(2,1)S(1)}, bf16[128,1024]{1,0:T(8,128)(2,1)S(1)}, bf16[128,1024]{1,0:T(8,128)(2,1)S(1)}, bf16[128,1024]{1,0:T(8,128)(2,1)S(1)}) custom-call(s32[2,4]{1,0:T(2,128)S(1)} %get-tuple-element.253.offset_ref, s32[2,4]{1,0:T(2,128)S(1)} %get-tuple-element.254.count_ref, f32[256,1024]{1,0:T(8,128)S(1)} %get-tuple-element.230.before_ref, ...), custom_call_target="tpu_custom_call" | custom-call | flops 1024 | bytes 1024 | tf_op jit(solution)/shard_map/pallas_call | solution.py:365
  89.1 3.3 %collective-permute-start.25 = (bf16[128,1024]{1,0:T(8,128)(2,1)S(1)}, bf16[128,1024]{1,0:T(8,128)(2,1)S(1)}, u32[]{:S(2)}, u32[]{:S(2)}) collective-permute-start(bf16[128,1024]{1,0:T(8,128)(2,1)S(1)} %get-tuple-element.246), channel_id=1, source_target_pairs={{0,12},{4,8},{8,4},{12,0},{1,13},{5,9},{9,5},{13,1},{2,14},{6,10},... | collective-permute-start | bytes 786440 | tf_op jit(solution)/shard_map/ppermute | solution.py:467
  95.0 1.9 %shard_map.80.refs_0_ = f32[512,1024]{1,0:T(8,128)S(1)} custom-call(s32[4,512]{1,0:T(4,128)S(1)} %get-tuple-element.175.code_ref, f32[4,512]{1,0:T(4,128)S(1)} %shard_map.79.weight_ref, bf16[128,1024]{1,0:T(8,128)(2,1)S(1)} %get-tuple-element.241.refs_0_, bf16[128,1024]{1,0:T(8,128)(2,1)} %collective-permute-done.22.refs_1_, ...), custom_call_target="tpu_custom_call" | custom-call | flops 1024 | bytes 1024 | tf_op jit(solution)/shard_map/pallas_call | solution.py:440
  96.9 3.3 %collective-permute-done.25.refs_2_ = bf16[128,1024]{1,0:T(8,128)(2,1)S(1)} collective-permute-done((bf16[128,1024]{1,0:T(8,128)(2,1)S(1)}, bf16[128,1024]{1,0:T(8,128)(2,1)S(1)}, u32[]{:S(2)}, u32[]{:S(2)}) %collective-permute-start.25) | collective-permute-done | bytes 262176 | tf_op jit(solution)/shard_map/ppermute | solution.py:467
  100.2 5.4 %collective-permute-done.26.refs_3_ = bf16[128,1024]{1,0:T(8,128)(2,1)S(1)} collective-permute-done((bf16[128,1024]{1,0:T(8,128)(2,1)S(1)}, bf16[128,1024]{1,0:T(8,128)(2,1)S(1)}, u32[]{:S(2)}, u32[]{:S(2)}) %collective-permute-start.26) | collective-permute-done | bytes 262176 | tf_op jit(solution)/shard_map/ppermute | solution.py:467
  106.5 8.7 %collective-permute-done.27.refs_1_ = bf16[128,1024]{1,0:T(8,128)(2,1)S(1)} collective-permute-done((bf16[128,1024]{1,0:T(8,128)(2,1)S(1)}, bf16[128,1024]{1,0:T(8,128)(2,1)S(1)}, u32[]{:S(2)}, u32[]{:S(2)}) %collective-permute-start.27) | collective-permute-done | bytes 262176 | tf_op jit(solution)/shard_map/ppermute | solution.py:467
  (68 shorter events, 31.2 us)
Async XLA Ops:
  2.6 24.1 %collective-permute-start.11 = (bf16[128,1024]{1,0:T(8,128)(2,1)}, bf16[128,1024]{1,0:T(8,128)(2,1)S(1)}, u32[]{:S(2)}, u32[]{:S(2)}) collective-permute-start(bf16[128,1024]{1,0:T(8,128)(2,1)} %get-tuple-element.182), channel_id=1, source_target_pairs={{0,8},{4,12},{8,0},{12,4},{1,9},{5,13},{9,1},{13,5},{2,10},{6,14},... | collective-permute-start | bytes 786440 | tf_op jit(solution)/shard_map/ppermute | solution.py:467
  6.7 20.0 %collective-permute-start.12 = (bf16[128,1024]{1,0:T(8,128)(2,1)}, bf16[128,1024]{1,0:T(8,128)(2,1)S(1)}, u32[]{:S(2)}, u32[]{:S(2)}) collective-permute-start(bf16[128,1024]{1,0:T(8,128)(2,1)} %get-tuple-element.183), channel_id=1, source_target_pairs={{0,12},{4,8},{8,4},{12,0},{1,13},{5,9},{9,5},{13,1},{2,14},{6,10},... | collective-permute-start | bytes 786440 | tf_op jit(solution)/shard_map/ppermute | solution.py:467
  8.1 18.7 %collective-permute-start.13 = (bf16[128,1024]{1,0:T(8,128)(2,1)}, bf16[128,1024]{1,0:T(8,128)(2,1)S(1)}, u32[]{:S(2)}, u32[]{:S(2)}) collective-permute-start(bf16[128,1024]{1,0:T(8,128)(2,1)} %get-tuple-element.184), channel_id=1, source_target_pairs={{0,4},{4,0},{8,12},{12,8},{1,5},{5,1},{9,13},{13,9},{2,6},{6,2},{1... | collective-permute-start | bytes 786440 | tf_op jit(solution)/shard_map/ppermute | solution.py:467
  11.1 25.9 %copy-start = (bf16[1,4096,256]{2,1,0:T(8,128)(2,1)S(1)}, bf16[1,4096,256]{2,1,0:T(8,128)(2,1)}, u32[]{:S(2)}) copy-start(bf16[1,4096,256]{2,1,0:T(8,128)(2,1)} %gate_ref.3) | copy-start | bytes 6291460
  12.9 3.7 %collective-permute-start.8 = (f32[4,512]{1,0:T(4,128)S(1)}, f32[4,512]{1,0:T(4,128)S(1)}, u32[]{:S(2)}, u32[]{:S(2)}) collective-permute-start(f32[4,512]{1,0:T(4,128)S(1)} %branch_1_fun.10), channel_id=1, source_target_pairs={{0,2},{1,3},{2,0},{3,1},{4,6},{5,7},{6,4},{7,5},{8,10},{9,11},{10,... | collective-permute-start | bytes 24584 | tf_op jit(solution)/shard_map/cond/branch_1_fun/ppermute | solution.py:470
  16.6 1.2 %collective-permute-start.9 = (f32[4,512]{1,0:T(4,128)S(1)}, f32[4,512]{1,0:T(4,128)S(1)}, u32[]{:S(2)}, u32[]{:S(2)}) collective-permute-start(f32[4,512]{1,0:T(4,128)S(1)} %add.24), channel_id=1, source_target_pairs={{0,1},{1,0},{2,3},{3,2},{4,5},{5,4},{6,7},{7,6},{8,9},{9,8},{10,11... | collective-permute-start | bytes 24584 | tf_op jit(solution)/shard_map/cond/branch_1_fun/ppermute | solution.py:470
  18.4 7.7 %collective-permute-start.10 = (f32[1,4,512]{2,1,0:T(4,128)}, f32[1,4,512]{2,1,0:T(4,128)S(1)}, u32[]{:S(2)}, u32[]{:S(2)}) collective-permute-start(f32[1,4,512]{2,1,0:T(4,128)} %bitcast), channel_id=1, source_target_pairs={{0,4},{4,0},{8,12},{12,8},{1,5},{5,1},{9,13},{13,9},{2,6},{6,2},{1... | collective-permute-start | bytes 24584 | tf_op jit(solution)/shard_map/cond/branch_1_fun/ppermute | solution.py:467
  28.7 8.3 %collective-permute-start.18 = (bf16[256,1024]{1,0:T(8,128)(2,1)}, bf16[256,1024]{1,0:T(8,128)(2,1)S(1)}, u32[]{:S(2)}, u32[]{:S(2)}) collective-permute-start(bf16[256,1024]{1,0:T(8,128)(2,1)} %get-tuple-element.287.refs_0_), channel_id=1, source_target_pairs={{0,1},{1,0},{2,3},{3,2},{4,5},{5,4},{6,7},{7,6},{8,9},{9,8},{10,11... | collective-permute-start | bytes 1572872 | tf_op jit(solution)/shard_map/ppermute | solution.py:470
  28.8 14.7 %collective-permute-start.17 = (bf16[256,1024]{1,0:T(8,128)(2,1)}, bf16[256,1024]{1,0:T(8,128)(2,1)}, u32[]{:S(2)}, u32[]{:S(2)}) collective-permute-start(bf16[256,1024]{1,0:T(8,128)(2,1)} %get-tuple-element.287.refs_0_), channel_id=1, source_target_pairs={{0,2},{1,3},{2,0},{3,1},{4,6},{5,7},{6,4},{7,5},{8,10},{9,11},{10,... | collective-permute-start | bytes 1572872 | tf_op jit(solution)/shard_map/ppermute | solution.py:470
  30.4 24.4 %collective-permute-start.14 = (bf16[128,1024]{1,0:T(8,128)(2,1)}, bf16[128,1024]{1,0:T(8,128)(2,1)S(1)}, u32[]{:S(2)}, u32[]{:S(2)}) collective-permute-start(bf16[128,1024]{1,0:T(8,128)(2,1)} %get-tuple-element.191), channel_id=1, source_target_pairs={{0,8},{4,12},{8,0},{12,4},{1,9},{5,13},{9,1},{13,5},{2,10},{6,14},... | collective-permute-start | bytes 786440 | tf_op jit(solution)/shard_map/ppermute | solution.py:467
  36.4 18.4 %collective-permute-start.15 = (bf16[128,1024]{1,0:T(8,128)(2,1)}, bf16[128,1024]{1,0:T(8,128)(2,1)S(1)}, u32[]{:S(2)}, u32[]{:S(2)}) collective-permute-start(bf16[128,1024]{1,0:T(8,128)(2,1)} %get-tuple-element.192), channel_id=1, source_target_pairs={{0,12},{4,8},{8,4},{12,0},{1,13},{5,9},{9,5},{13,1},{2,14},{6,10},... | collective-permute-start | bytes 786440 | tf_op jit(solution)/shard_map/ppermute | solution.py:467
  36.9 18.9 %collective-permute-start.16 = (bf16[128,1024]{1,0:T(8,128)(2,1)}, bf16[128,1024]{1,0:T(8,128)(2,1)S(1)}, u32[]{:S(2)}, u32[]{:S(2)}) collective-permute-start(bf16[128,1024]{1,0:T(8,128)(2,1)} %get-tuple-element.193), channel_id=1, source_target_pairs={{0,4},{4,0},{8,12},{12,8},{1,5},{5,1},{9,13},{13,9},{2,6},{6,2},{1... | collective-permute-start | bytes 786440 | tf_op jit(solution)/shard_map/ppermute | solution.py:467
  38.6 4.9 %copy-start.3 = (bf16[1,1024,1024]{2,1,0:T(8,128)(2,1)S(1)}, bf16[1,1024,1024]{2,1,0:T(8,128)(2,1)}, u32[]{:S(2)}) copy-start(bf16[1,1024,1024]{2,1,0:T(8,128)(2,1)} %param.19) | copy-start | bytes 6291460
  43.5 2.1 %collective-permute-start = (bf16[256,1024]{1,0:T(8,128)(2,1)}, bf16[256,1024]{1,0:T(8,128)(2,1)S(1)}, u32[]{:S(2)}, u32[]{:S(2)}) collective-permute-start(bf16[256,1024]{1,0:T(8,128)(2,1)} %get-tuple-element.67.refs_0_), channel_id=1, source_target_pairs={{0,1},{1,0},{2,3},{3,2},{4,5},{5,4},{6,7},{7,6},{8,9},{9,8},{10,11... | collective-permute-start | bytes 1572872 | tf_op jit(solution)/shard_map/cond/branch_1_fun/ppermute | solution.py:470
  46.0 1.8 %collective-permute-start.2 = (bf16[256,256]{1,0:T(8,128)(2,1)S(1)}, bf16[256,256]{1,0:T(8,128)(2,1)S(1)}, u32[]{:S(2)}, u32[]{:S(2)}) collective-permute-start(bf16[256,256]{1,0:T(8,128)(2,1)S(1)} %branch_1_fun.13.refs_0_), channel_id=1, source_target_pairs={{0,1},{1,0},{2,3},{3,2},{4,5},{5,4},{6,7},{7,6},{8,9},{9,8},{10,11... | collective-permute-start | bytes 393224 | tf_op jit(solution)/shard_map/cond/branch_1_fun/ppermute | solution.py:470
  46.2 5.9 %collective-permute-start.1 = (bf16[256,256]{1,0:T(8,128)(2,1)S(1)}, bf16[256,256]{1,0:T(8,128)(2,1)}, u32[]{:S(2)}, u32[]{:S(2)}) collective-permute-start(bf16[256,256]{1,0:T(8,128)(2,1)S(1)} %branch_1_fun.13.refs_0_), channel_id=1, source_target_pairs={{0,2},{1,3},{2,0},{3,1},{4,6},{5,7},{6,4},{7,5},{8,10},{9,11},{10,... | collective-permute-start | bytes 393224 | tf_op jit(solution)/shard_map/cond/branch_1_fun/ppermute | solution.py:470
  52.1 1.7 %collective-permute-start.3 = (bf16[256,256]{1,0:T(8,128)(2,1)}, bf16[256,256]{1,0:T(8,128)(2,1)}, u32[]{:S(2)}, u32[]{:S(2)}) collective-permute-start(bf16[256,256]{1,0:T(8,128)(2,1)} %collective-permute-done.1), channel_id=1, source_target_pairs={{0,1},{1,0},{2,3},{3,2},{4,5},{5,4},{6,7},{7,6},{8,9},{9,8},{10,11... | collective-permute-start | bytes 393224 | tf_op jit(solution)/shard_map/cond/branch_1_fun/ppermute | solution.py:470
  57.8 11.7 %collective-permute-start.20 = (bf16[256,1024]{1,0:T(8,128)(2,1)S(1)}, bf16[256,1024]{1,0:T(8,128)(2,1)S(1)}, u32[]{:S(2)}, u32[]{:S(2)}) collective-permute-start(bf16[256,1024]{1,0:T(8,128)(2,1)S(1)} %shard_map.75.refs_0_), channel_id=1, source_target_pairs={{0,1},{1,0},{2,3},{3,2},{4,5},{5,4},{6,7},{7,6},{8,9},{9,8},{10,11... | collective-permute-start | bytes 1572872 | tf_op jit(solution)/shard_map/ppermute | solution.py:470
  57.9 15.1 %collective-permute-start.19 = (bf16[256,1024]{1,0:T(8,128)(2,1)S(1)}, bf16[256,1024]{1,0:T(8,128)(2,1)}, u32[]{:S(2)}, u32[]{:S(2)}) collective-permute-start(bf16[256,1024]{1,0:T(8,128)(2,1)S(1)} %shard_map.75.refs_0_), channel_id=1, source_target_pairs={{0,2},{1,3},{2,0},{3,1},{4,6},{5,7},{6,4},{7,5},{8,10},{9,11},{10,... | collective-permute-start | bytes 1572872 | tf_op jit(solution)/shard_map/ppermute | solution.py:470
  61.6 27.5 %collective-permute-start.21 = (bf16[128,1024]{1,0:T(8,128)(2,1)}, bf16[128,1024]{1,0:T(8,128)(2,1)}, u32[]{:S(2)}, u32[]{:S(2)}) collective-permute-start(bf16[128,1024]{1,0:T(8,128)(2,1)} %get-tuple-element.216), channel_id=1, source_target_pairs={{0,8},{4,12},{8,0},{12,4},{1,9},{5,13},{9,1},{13,5},{2,10},{6,14},... | collective-permute-start | bytes 786440 | tf_op jit(solution)/shard_map/ppermute | solution.py:467
  66.7 22.4 %collective-permute-start.22 = (bf16[128,1024]{1,0:T(8,128)(2,1)}, bf16[128,1024]{1,0:T(8,128)(2,1)}, u32[]{:S(2)}, u32[]{:S(2)}) collective-permute-start(bf16[128,1024]{1,0:T(8,128)(2,1)} %get-tuple-element.217), channel_id=1, source_target_pairs={{0,12},{4,8},{8,4},{12,0},{1,13},{5,9},{9,5},{13,1},{2,14},{6,10},... | collective-permute-start | bytes 786440 | tf_op jit(solution)/shard_map/ppermute | solution.py:467
  68.9 20.2 %collective-permute-start.23 = (bf16[128,1024]{1,0:T(8,128)(2,1)}, bf16[128,1024]{1,0:T(8,128)(2,1)}, u32[]{:S(2)}, u32[]{:S(2)}) collective-permute-start(bf16[128,1024]{1,0:T(8,128)(2,1)} %get-tuple-element.218), channel_id=1, source_target_pairs={{0,4},{4,0},{8,12},{12,8},{1,5},{5,1},{9,13},{13,9},{2,6},{6,2},{1... | collective-permute-start | bytes 786440 | tf_op jit(solution)/shard_map/ppermute | solution.py:467
  69.5 1.6 %copy-start.2 = (bf16[1,4096,256]{2,1,0:T(8,128)(2,1)S(1)}, bf16[1,4096,256]{2,1,0:T(8,128)(2,1)}, u32[]{:S(2)}) copy-start(bf16[1,4096,256]{2,1,0:T(8,128)(2,1)} %up_ref.3) | copy-start | bytes 6291460
  71.1 1.8 %copy-start.4 = (bf16[1,1024,1024]{2,1,0:T(8,128)(2,1)S(1)}, bf16[1,1024,1024]{2,1,0:T(8,128)(2,1)}, u32[]{:S(2)}) copy-start(bf16[1,1024,1024]{2,1,0:T(8,128)(2,1)} %param.19) | copy-start | bytes 6291460
  73.0 2.2 %collective-permute-start.4 = (bf16[256,1024]{1,0:T(8,128)(2,1)}, bf16[256,1024]{1,0:T(8,128)(2,1)S(1)}, u32[]{:S(2)}, u32[]{:S(2)}) collective-permute-start(bf16[256,1024]{1,0:T(8,128)(2,1)} %get-tuple-element.84.refs_0_), channel_id=1, source_target_pairs={{0,1},{1,0},{2,3},{3,2},{4,5},{5,4},{6,7},{7,6},{8,9},{9,8},{10,11... | collective-permute-start | bytes 1572872 | tf_op jit(solution)/shard_map/cond/branch_1_fun/ppermute | solution.py:470
  75.6 1.7 %collective-permute-start.6 = (bf16[256,256]{1,0:T(8,128)(2,1)S(1)}, bf16[256,256]{1,0:T(8,128)(2,1)S(1)}, u32[]{:S(2)}, u32[]{:S(2)}) collective-permute-start(bf16[256,256]{1,0:T(8,128)(2,1)S(1)} %branch_1_fun.16.refs_0_), channel_id=1, source_target_pairs={{0,1},{1,0},{2,3},{3,2},{4,5},{5,4},{6,7},{7,6},{8,9},{9,8},{10,11... | collective-permute-start | bytes 393224 | tf_op jit(solution)/shard_map/cond/branch_1_fun/ppermute | solution.py:470
  75.8 5.9 %collective-permute-start.5 = (bf16[256,256]{1,0:T(8,128)(2,1)S(1)}, bf16[256,256]{1,0:T(8,128)(2,1)}, u32[]{:S(2)}, u32[]{:S(2)}) collective-permute-start(bf16[256,256]{1,0:T(8,128)(2,1)S(1)} %branch_1_fun.16.refs_0_), channel_id=1, source_target_pairs={{0,2},{1,3},{2,0},{3,1},{4,6},{5,7},{6,4},{7,5},{8,10},{9,11},{10,... | collective-permute-start | bytes 393224 | tf_op jit(solution)/shard_map/cond/branch_1_fun/ppermute | solution.py:470
  81.7 1.7 %collective-permute-start.7 = (bf16[256,256]{1,0:T(8,128)(2,1)}, bf16[256,256]{1,0:T(8,128)(2,1)}, u32[]{:S(2)}, u32[]{:S(2)}) collective-permute-start(bf16[256,256]{1,0:T(8,128)(2,1)} %collective-permute-done.5), channel_id=1, source_target_pairs={{0,1},{1,0},{2,3},{3,2},{4,5},{5,4},{6,7},{7,6},{8,9},{9,8},{10,11... | collective-permute-start | bytes 393224 | tf_op jit(solution)/shard_map/cond/branch_1_fun/ppermute | solution.py:470
  83.4 9.0 %collective-permute-start.24 = (f32[2,4,512]{2,1,0:T(4,128)S(1)}, f32[2,4,512]{2,1,0:T(4,128)S(1)}, u32[]{:S(2)}, u32[]{:S(2)}) collective-permute-start(f32[2,4,512]{2,1,0:T(4,128)S(1)} %get-tuple-element.239), channel_id=1, source_target_pairs={{0,8},{4,12},{8,0},{12,4},{1,9},{5,13},{9,1},{13,5},{2,10},{6,14},... | collective-permute-start | bytes 49160 | tf_op jit(solution)/shard_map/ppermute | solution.py:467
  89.1 11.1 %collective-permute-start.25 = (bf16[128,1024]{1,0:T(8,128)(2,1)S(1)}, bf16[128,1024]{1,0:T(8,128)(2,1)S(1)}, u32[]{:S(2)}, u32[]{:S(2)}) collective-permute-start(bf16[128,1024]{1,0:T(8,128)(2,1)S(1)} %get-tuple-element.246), channel_id=1, source_target_pairs={{0,12},{4,8},{8,4},{12,0},{1,13},{5,9},{9,5},{13,1},{2,14},{6,10},... | collective-permute-start | bytes 786440 | tf_op jit(solution)/shard_map/ppermute | solution.py:467
  92.4 13.2 %collective-permute-start.26 = (bf16[128,1024]{1,0:T(8,128)(2,1)S(1)}, bf16[128,1024]{1,0:T(8,128)(2,1)S(1)}, u32[]{:S(2)}, u32[]{:S(2)}) collective-permute-start(bf16[128,1024]{1,0:T(8,128)(2,1)S(1)} %get-tuple-element.247), channel_id=1, source_target_pairs={{0,4},{4,0},{8,12},{12,8},{1,5},{5,1},{9,13},{13,9},{2,6},{6,2},{1... | collective-permute-start | bytes 786440 | tf_op jit(solution)/shard_map/ppermute | solution.py:467
  93.0 22.2 %collective-permute-start.27 = (bf16[128,1024]{1,0:T(8,128)(2,1)S(1)}, bf16[128,1024]{1,0:T(8,128)(2,1)S(1)}, u32[]{:S(2)}, u32[]{:S(2)}) collective-permute-start(bf16[128,1024]{1,0:T(8,128)(2,1)S(1)} %get-tuple-element.248), channel_id=1, source_target_pairs={{0,8},{4,12},{8,0},{12,4},{1,9},{5,13},{9,1},{13,5},{2,10},{6,14},... | collective-permute-start | bytes 786440 | tf_op jit(solution)/shard_map/ppermute | solution.py:467
  (1 other events, 1.6 us)
